TPU v7x, 32 devices: a whole 2x2x4 slice. The times are simulated.
32 devices in a mesh: row: 8 (over z, x), col: 4 (over y, core).
Axes of the slice: x: 2, y: 2, z: 4, core: 2. Of those that a mesh axis runs over, the one named last changes fastest.
Arguments:
- inverse_set: float32 [1, 8, 128, 2, 4, 128], P(None, 'row', None, None, 'col'), may hold values from -6 to 6
- presence: int32 [1, 8, 2, 4], P(None, 'row', None, 'col'), may hold values 0 or 1
- factor: float32 [1, 8, 128, 512], P(None, 'row'), may hold values from -0.1875 to 0.1875
- dinv: float32 [512, 512], P('row', 'col'), may hold values from -6 to 6
Outputs:
- off_diag: float32 [1, 8, 128, 512], P(None, 'row', 'col')
- diag_block: float32 [512, 512], P('row', 'col')
All inputs are finite; a program needn't handle non-finite values. No bound on the sum of `presence` on one device may be relied on, other than what follows from the above.
Results may differ from a plain program's by a relative error of at most 0.00007.
Values sent between devices are 32-bit elements; how exact they have to be, the bound alone decides.
No kernel may reach another device: no remote copies, remote signals or barrier semaphores. Data moves between devices by JAX's collectives and lax.ppermute only.
A program may use at most 64 MiB of HBM per device.

v0:
```python
import jax
import jax.numpy as jnp
from jax import lax
from jax.sharding import PartitionSpec as P


def spread(value, axis, root):
    mine = lax.axis_index(axis) == root
    return lax.psum(jnp.where(mine, value, jnp.zeros_like(value)), axis)


def local(inverse_set, presence, factor, dinv):
    groups_row = lax.axis_size("row")
    groups_col = lax.axis_size("col")
    group_ratio = groups_row // groups_col
    col_index = lax.axis_index("col")
    block_order = factor.shape[2]
    width = factor.shape[3]
    block_cols = inverse_set.shape[3]
    own_rows = factor[:, 0]
    masked = (
        inverse_set[:, 0, :, :, 0, :] * presence[:, 0, :, 0].astype(jnp.float32)[:, None, :, None]
    )
    pieces = []
    for level in range(group_ratio):
        pieces.append(spread(own_rows, "row", level * groups_col + col_index))
    columns = jnp.stack(pieces, axis=1).reshape(block_cols, block_order, width)
    partial_value = jnp.einsum("axbz,bzy->axy", masked, columns, precision=lax.Precision.HIGHEST)
    update = lax.psum_scatter(partial_value, "col", scatter_dimension=1, tiled=True)
    share = block_order // groups_col
    rows_mine = lax.dynamic_slice_in_dim(own_rows, col_index * share, share, 1)
    diag_part = jnp.einsum("axy,axw->yw", rows_mine, update, precision=lax.Precision.HIGHEST)
    diag_half = lax.psum_scatter(diag_part, "col", scatter_dimension=1, tiled=True)
    diag_sum = lax.psum_scatter(diag_half, "row", scatter_dimension=0, tiled=True)
    off_diag = (-update)[:, None, :, :]
    diag_block = dinv + diag_sum
    return (off_diag, diag_block)


def solution(mesh):
    in_specs = (
        P(None, "row", None, None, "col", None),
        P(None, "row", None, "col"),
        P(None, "row", None, None),
        P("row", "col"),
    )
    out_specs = (P(None, "row", "col", None), P("row", "col"))
    return jax.shard_map(local, mesh=mesh, in_specs=in_specs, out_specs=out_specs, check_vma=False)
```

profile of v0, /device:TPU:0, one launch (start us, length us, event | category | flops | bytes accessed | tf_op | source)
XLA Modules:
  0.0 209.3 jit_solution(8208552488240920290)
XLA Ops:
  7.2 0.0 all-reduce.3.cloned.1.call-start
  7.2 1.8 broadcast_select_fusion.1
  9.0 0.0 copy-start.3
  9.0 0.0 copy-start.1
  9.0 0.0 all-reduce.3.cloned.1.call-update
  9.1 0.0 reduce-scatter.4.cloned.1.call-start
  9.1 0.6 copy-done.3
  9.7 0.3 copy-done.1
  9.9 0.2 broadcast_multiply_fusion
  10.1 76.7 %all-reduce.3.cloned.1.call-done = (f32[1,1,128,512]{3,2,1,0:T(8,128)}, f32[1,1,128,512]{3,2,1,0:T(8,128)}) async-done(((f32[1,1,128,512]{3,2,1,0:T(8,128)}, f32[1,1,128,512]{3,2,1,0:T(8,128)}), (f32[1,1,128,512]{3,2,1,0:T(8,128)}, f32[1,1,128,512]{3,2,1,0:T(8,128)})) %all-reduce.3.cloned.1.call-update) | async-done | bytes 524304 | tf_op jit(solution)/shard_map/psum | solution.py:9
  86.8 2.1 %convolution_bitcast_fusion = f32[1,128,512]{2,1,0:T(8,128)} fusion(f32[1,1,128,512]{3,2,1,0:T(8,128)} %get-tuple-element.2, f32[1,1,128,512]{3,2,1,0:T(8,128)} %get-tuple-element.3, f32[128,2,128]{2,1,0:T(2,128)S(1)} %bitcast.17), kind=kOutput, calls=%fused_computation | convolution fusion | flops 201457664 | bytes 917504 | tf_op jit(solution)/shard_map/axbz,bzy->axy/dot_general | solution.py:28
  89.0 0.0 reduce-scatter.4.cloned.1.call-update
  89.0 0.0 reduce-scatter.6.cloned.1.call-start
  89.0 19.7 %reduce-scatter.4.cloned.1.call-done = f32[1,32,512]{2,1,0:T(8,128)} async-done(((f32[1,128,512]{2,1,0:T(8,128)}), f32[1,32,512]{2,1,0:T(8,128)}) %reduce-scatter.4.cloned.1.call-update) | async-done | bytes 65552 | tf_op jit(solution)/shard_map/reduce_scatter | solution.py:29
  108.7 2.9 %fusion.3 = f32[512,512]{1,0:T(8,128)} fusion(f32[1,32,512]{2,1,0:T(8,128)} %reduce-scatter.4.cloned.1.call-done, f32[1,1,128,512]{3,2,1,0:T(8,128)} %param.6, s32[]{:T(128)S(6)} %select_n.45), kind=kOutput, calls=%fused_computation.8 | convolution fusion | flops 100663296 | bytes 1179652 | tf_op jit(solution)/shard_map/axy,axw->yw/dot_general | solution.py:32
  111.6 0.0 reduce-scatter.6.cloned.1.call-update
  111.6 0.0 reduce-scatter.8.cloned.1.call-start
  111.7 25.0 %reduce-scatter.6.cloned.1.call-done = f32[512,128]{1,0:T(8,128)} async-done(((f32[512,512]{1,0:T(8,128)}), f32[512,128]{1,0:T(8,128)}) %reduce-scatter.6.cloned.1.call-update) | async-done | bytes 262160 | tf_op jit(solution)/shard_map/reduce_scatter | solution.py:33
  136.6 0.0 reduce-scatter.8.cloned.1.call-update
  136.6 0.8 copy-done
  137.5 0.6 negate_bitcast_fusion
  138.1 63.3 %reduce-scatter.8.cloned.1.call-done = f32[64,128]{1,0:T(8,128)} async-done(((f32[512,128]{1,0:T(8,128)}), f32[64,128]{1,0:T(8,128)}) %reduce-scatter.8.cloned.1.call-update) | async-done | bytes 32784 | tf_op jit(solution)/shard_map/reduce_scatter | solution.py:34
  201.4 0.0 copy-done.2
  201.4 1.4 add.17
  (3 shorter events, 0.0 us)
Async XLA Ops:
  7.2 79.7 %all-reduce.3.cloned.1.call-start = ((), (), s32[]{:S(2)}) async-start(), calls=%async_computation.6 | async-start | bytes 1048576 | tf_op jit(solution)/shard_map/psum | solution.py:9
  9.0 0.7 copy-start.3
  9.0 0.9 copy-start.1
  9.1 99.7 %reduce-scatter.4.cloned.1.call-start = ((), (), s32[]{:S(2)}) async-start(), calls=%async_computation.3 | async-start | bytes 327680 | tf_op jit(solution)/shard_map/reduce_scatter | solution.py:29
  89.0 47.6 %reduce-scatter.6.cloned.1.call-start = ((), (), s32[]{:S(2)}) async-start(), calls=%async_computation.4 | async-start | bytes 1310720 | tf_op jit(solution)/shard_map/reduce_scatter | solution.py:33
  111.6 89.8 %reduce-scatter.8.cloned.1.call-start = ((), (), s32[]{:S(2)}) async-start(), calls=%async_computation.5 | async-start | bytes 294912 | tf_op jit(solution)/shard_map/reduce_scatter | solution.py:34
  136.6 0.8 copy-start
  137.5 64.0 %copy-start.2 = (f32[64,128]{1,0:T(8,128)S(1)}, f32[64,128]{1,0:T(8,128)}, u32[]{:S(2)}) copy-start(f32[64,128]{1,0:T(8,128)} %param.7) | copy-start | bytes 98308
Sparse Core Ops, SparseCore 0:
  11.5 75.3 all-reduce.2
  89.4 19.2 reduce-scatter.3
  111.7 24.8 reduce-scatter.5
  140.2 61.2 reduce-scatter.7
where the time goes:
time: 210 us; the launch traced here: 209 us
  waiting for transfers between devices  185 us (88%)
  between operations  13.8 us (7%)
  matrix products  5.01 us (2%)
  other arithmetic  3.97 us (2%)
    psum x1, waiting for transfers between devices, spread(): return lax.psum(jnp.where(mine, value, jnp.zeros_like(value)), axis)  76.7 us
    reduce_scatter x1, waiting for transfers between devices, local(): lax.psum_scatter(diag_half, 'row', scatter_dimension=0, tiled=True)  63.3 us
    reduce_scatter x1, waiting for transfers between devices, local(): lax.psum_scatter(diag_part, 'col', scatter_dimension=1, tiled=True)  25 us
    reduce_scatter x1, waiting for transfers between devices, local(): lax.psum_scatter(partial_value, 'col', scatter_dimension=1, tiled=True)  19.7 us
  transfers between devices with their start and end apart: 4, of which 4 were waited for; matrix products, arithmetic and copies ran while one was open for 0% of the time, Pallas kernels for 0%

commit v1 on v0

v1 whole, which is shorter than its diff:
```python
import jax
import jax.numpy as jnp
from jax import lax
from jax.sharding import PartitionSpec as P

HI = lax.Precision.HIGHEST


def to_all(value, axis):
    copies = jnp.broadcast_to(value[None], (lax.axis_size(axis),) + value.shape)
    return lax.all_to_all(copies, axis, 0, 0)


def local(inverse_set, presence, factor, dinv):
    groups_row = lax.axis_size("row")
    groups_col = lax.axis_size("col")
    col_index = lax.axis_index("col")
    block_rows, _, order, width = factor.shape
    block_cols = inverse_set.shape[3]
    total = block_cols * groups_col * order
    span = width // groups_col
    share = order // groups_col
    rows = block_rows * order

    own = factor[:, 0]
    masked = (
        inverse_set[:, 0, :, :, 0, :] * presence[:, 0, :, 0].astype(jnp.float32)[:, None, :, None]
    )
    columns = to_all(lax.dynamic_slice_in_dim(own, col_index * span, span, 2), "row")
    columns = columns.transpose(1, 0, 2, 3).reshape(total, span)
    wide = to_all(masked, "col")
    wide = wide.transpose(1, 2, 3, 0, 4).reshape(rows, total)
    update = jnp.dot(wide, columns, precision=HI)

    parts = update.reshape(block_rows, groups_col, share, span).transpose(1, 0, 2, 3)
    parts = lax.all_to_all(-parts, "col", 0, 0)
    off_diag = parts.transpose(1, 2, 0, 3).reshape(block_rows, 1, share, width)

    terms = jnp.dot(own.reshape(rows, width).T, update, precision=HI)
    terms = terms.reshape(groups_row, width // groups_row, span)
    terms = lax.all_to_all(terms, "row", 0, 0)
    diag_block = dinv + terms.sum(axis=0)
    return (off_diag, diag_block)


def solution(mesh):
    in_specs = (
        P(None, "row", None, None, "col", None),
        P(None, "row", None, "col"),
        P(None, "row", None, None),
        P("row", "col"),
    )
    out_specs = (P(None, "row", "col", None), P("row", "col"))
    return jax.shard_map(local, mesh=mesh, in_specs=in_specs, out_specs=out_specs, check_vma=False)
```

time: 210 us -> 60.5 us (0.29)
  waiting for transfers between devices: 185 us -> 34 us
  starting transfers between devices: 0.16 us -> 17.6 us
  between operations: 13.8 us -> 0.69 us
  matrix products: 5.01 us -> 2.05 us
    reduce_scatter x3 -> x0, waiting for transfers between devices: 108 us -> none  [the longest x1 63.3 us: local(): lax.psum_scatter(diag_half, 'row', scatter_dimension=0, tiled=True)]
    psum x1 -> x0, waiting for transfers between devices: 76.7 us -> none  [spread(): return lax.psum(jnp.where(mine, value, jnp.zeros_like(value)), axis)]
    all_to_all x0 -> x4, waiting for transfers between devices: none -> 34 us  [the longest x2 23.1 us: to_all(): return lax.all_to_all(copies, axis, 0, 0)]
    all_to_all x0 -> x4, starting transfers between devices: none -> 17.6 us  [the longest x2 10.7 us: to_all(): return lax.all_to_all(copies, axis, 0, 0)]
    dot_general x2, matrix products: 5.01 us -> 2.05 us  [the longest x1 1.63 us: local(): update = jnp.dot(wide, columns, precision=HI)]
  transfers between devices with their start and end apart: 4 -> 4, of which waited for: 4 -> 4; matrix products, arithmetic and copies ran while one was open for 0% -> 3% of each run, Pallas kernels for 0% -> 0%
where the time goes in v1:
time: 60.5 us; the launch traced here: 60 us
  waiting for transfers between devices  34 us (56%)
  starting transfers between devices  17.6 us (29%)
  local copies, waits for them, and re-layouts  3.34 us (6%)
  other arithmetic  2.35 us (4%)
  matrix products  2.05 us (3%)
  between operations  0.69 us (1%)
    all_to_all x2, waiting for transfers between devices, to_all(): return lax.all_to_all(copies, axis, 0, 0)  23.1 us
    all_to_all x2, starting transfers between devices, to_all(): return lax.all_to_all(copies, axis, 0, 0)  10.7 us
    all_to_all x1, waiting for transfers between devices, local(): terms = lax.all_to_all(terms, 'row', 0, 0)  8.06 us
    all_to_all x1, starting transfers between devices, local(): terms = lax.all_to_all(terms, 'row', 0, 0)  3.61 us
    all_to_all x1, starting transfers between devices, local(): parts = lax.all_to_all(-parts, 'col', 0, 0)  3.28 us
    all_to_all x1, waiting for transfers between devices, local(): parts = lax.all_to_all(-parts, 'col', 0, 0)  2.83 us
    mul x2, other arithmetic, local(): inverse_set[:, 0, :, :, 0, :]  1.71 us
    broadcast_in_dim x3, local copies, waits for them, and re-layouts, to_all(): copies = jnp.broadcast_to(value[None], (lax.axis_size(axis),) + value.shape)  1.69 us
  transfers between devices with their start and end apart: 4, of which 4 were waited for; matrix products, arithmetic and copies ran while one was open for 3% of the time, Pallas kernels for 0%

profile of v1, /device:TPU:0, one launch (start us, length us, event | category | flops | bytes accessed | tf_op | source)
XLA Modules:
  0.0 60.0 jit_solution(17553121566976666813)
XLA Ops:
  0.6 0.0 copy-start
  0.6 0.7 %convert_bitcast_fusion = f32[2]{0:T(128)S(1)} fusion(s32[1,1,2,1]{2,3,1,0:T(1,128)} %param.5), kind=kLoop, calls=%fused_computation.4 | loop fusion | flops 2 | bytes 16 | tf_op jit(solution)/shard_map/mul | solution.py:27
  1.3 1.0 %broadcast_multiply_fusion = f32[128,2,128]{2,1,0:T(2,128)S(1)} fusion(f32[128,2,128]{2,1,0:T(2,128)} %bitcast.27, f32[2]{0:T(128)S(1)} %convert_bitcast_fusion), kind=kLoop, calls=%fused_computation.2 | loop fusion | flops 32768 | bytes 262152 | tf_op jit(solution)/shard_map/mul | solution.py:27
  2.4 0.1 copy.14
  2.5 0.8 %broadcast_in_dim.6 = f32[4,1,128,2,128]{2,4,3,1,0:T(8,128)} broadcast(f32[128,2,128]{0,2,1:T(8,128)S(1)} %copy.14), dimensions={2,3,4} | broadcast | bytes 655360 | tf_op jit(solution)/shard_map/broadcast_in_dim | solution.py:10
  3.3 4.2 %all-to-all-start = ((f32[4,1,128,2,128]{2,4,3,1,0:T(8,128)}), f32[4,1,128,2,128]{2,4,3,1,0:T(8,128)S(1)}, u32[]{:S(2)}, u32[]{:S(2)}) async-start(f32[4,1,128,2,128]{2,4,3,1,0:T(8,128)} %broadcast_in_dim.6), calls=%async_computation | async-start | bytes 1048576 | tf_op jit(solution)/shard_map/all_to_all | solution.py:11
  7.5 0.0 copy-done
  7.6 8.8 %all-to-all-done = f32[4,1,128,2,128]{2,4,3,1,0:T(8,128)S(1)} async-done(((f32[4,1,128,2,128]{2,4,3,1,0:T(8,128)}), f32[4,1,128,2,128]{2,4,3,1,0:T(8,128)S(1)}, u32[]{:S(2)}, u32[]{:S(2)}) %all-to-all-start) | async-done | bytes 524320 | tf_op jit(solution)/shard_map/all_to_all | solution.py:11
  16.4 0.8 %broadcast_in_dim.8 = f32[8,1,128,128]{3,2,1,0:T(8,128)} broadcast(f32[128,128]{1,0:T(8,128)S(1)} %dynamic-slice_bitcast_fusion), dimensions={2,3} | broadcast | bytes 589824 | tf_op jit(solution)/shard_map/broadcast_in_dim | solution.py:10
  17.2 6.5 %all-to-all-start.1 = ((f32[8,1,128,128]{3,2,1,0:T(8,128)}), f32[8,1,128,128]{3,2,1,0:T(8,128)S(1)}, u32[]{:S(2)}, u32[]{:S(2)}) async-start(f32[8,1,128,128]{3,2,1,0:T(8,128)} %broadcast_in_dim.8), calls=%async_computation.1 | async-start | bytes 1048576 | tf_op jit(solution)/shard_map/all_to_all | solution.py:11
  23.7 14.3 %all-to-all-done.1 = f32[8,1,128,128]{3,2,1,0:T(8,128)S(1)} async-done(((f32[8,1,128,128]{3,2,1,0:T(8,128)}), f32[8,1,128,128]{3,2,1,0:T(8,128)S(1)}, u32[]{:S(2)}, u32[]{:S(2)}) %all-to-all-start.1) | async-done | bytes 524320 | tf_op jit(solution)/shard_map/all_to_all | solution.py:11
  38.0 1.6 %fusion.1 = (f32[128,128]{1,0:T(8,128)}, f32[128,128]{1,0:T(8,128)S(1)}) fusion(f32[128,1024]{0,1:T(8,128)S(1)} %bitcast.24, f32[1024,128]{1,0:T(8,128)S(1)} %bitcast.23), kind=kOutput, calls=%fused_computation.5 | convolution fusion | flops 201342976 | bytes 1179648 | tf_op jit(solution)/shard_map/dot_general | solution.py:33
  39.6 3.3 %all-to-all-start.2 = ((f32[4,1,32,128]{3,2,1,0:T(8,128)}), f32[4,1,32,128]{3,2,1,0:T(8,128)S(1)}, u32[]{:S(2)}, u32[]{:S(2)}) async-start(f32[4,1,32,128]{3,2,1,0:T(8,128)} %bitcast.7), calls=%async_computation.2 | async-start | bytes 131072 | tf_op jit(solution)/shard_map/all_to_all | solution.py:36
  42.9 0.4 convolution_bitcast_fusion
  43.4 0.8 %copy.18 = f32[512,128]{1,0:T(8,128)} copy(f32[512,128]{0,1:T(8,128)S(1)} %convolution_bitcast_fusion) | data formatting | bytes 524288 | tf_op jit(solution)/shard_map/dot_general | solution.py:39
  44.2 2.8 %all-to-all-done.2 = f32[4,1,32,128]{3,2,1,0:T(8,128)S(1)} async-done(((f32[4,1,32,128]{3,2,1,0:T(8,128)}), f32[4,1,32,128]{3,2,1,0:T(8,128)S(1)}, u32[]{:S(2)}, u32[]{:S(2)}) %all-to-all-start.2) | async-done | bytes 65568 | tf_op jit(solution)/shard_map/all_to_all | solution.py:36
  47.0 3.6 %all-to-all-start.3 = ((f32[8,64,128]{2,1,0:T(8,128)}), f32[8,64,128]{2,1,0:T(8,128)S(1)}, u32[]{:S(2)}, u32[]{:S(2)}) async-start(f32[8,64,128]{2,1,0:T(8,128)} %bitcast.12), calls=%async_computation.3 | async-start | bytes 524288 | tf_op jit(solution)/shard_map/all_to_all | solution.py:41
  50.7 0.6 %copy.19 = f32[1,1,32,512]{3,2,1,0:T(8,128)} copy(f32[1,1,32,512]{3,0,2,1:T(1,128)S(1)} %bitcast.26) | data formatting | bytes 131072
  51.3 0.0 copy-start.1
  51.3 8.1 %all-to-all-done.3 = f32[8,64,128]{2,1,0:T(8,128)S(1)} async-done(((f32[8,64,128]{2,1,0:T(8,128)}), f32[8,64,128]{2,1,0:T(8,128)S(1)}, u32[]{:S(2)}, u32[]{:S(2)}) %all-to-all-start.3) | async-done | bytes 262176 | tf_op jit(solution)/shard_map/all_to_all | solution.py:41
  59.4 0.0 copy-done.1
  59.4 0.6 %add.7 = f32[64,128]{1,0:T(8,128)} add(f32[64,128]{1,0:T(8,128)S(1)} %copy-done.1, f32[64,128]{1,0:T(8,128)S(1)} %reduce_sum.9) | non-fusion elementwise | flops 8192 | bytes 98304 | tf_op jit(solution)/shard_map/add | solution.py:42
  (4 shorter events, 0.1 us)
Async XLA Ops:
  0.6 6.9 %copy-start = (f32[1,1,128,512]{3,2,1,0:T(8,128)S(1)}, f32[1,1,128,512]{3,2,1,0:T(8,128)}, u32[]{:S(2)}) copy-start(f32[1,1,128,512]{3,2,1,0:T(8,128)} %param.6) | copy-start | bytes 786436
  3.3 13.1 %all-to-all-start = ((f32[4,1,128,2,128]{2,4,3,1,0:T(8,128)}), f32[4,1,128,2,128]{2,4,3,1,0:T(8,128)S(1)}, u32[]{:S(2)}, u32[]{:S(2)}) async-start(f32[4,1,128,2,128]{2,4,3,1,0:T(8,128)} %broadcast_in_dim.6), calls=%async_computation | async-start | bytes 1048576 | tf_op jit(solution)/shard_map/all_to_all | solution.py:11
  17.2 20.8 %all-to-all-start.1 = ((f32[8,1,128,128]{3,2,1,0:T(8,128)}), f32[8,1,128,128]{3,2,1,0:T(8,128)S(1)}, u32[]{:S(2)}, u32[]{:S(2)}) async-start(f32[8,1,128,128]{3,2,1,0:T(8,128)} %broadcast_in_dim.8), calls=%async_computation.1 | async-start | bytes 1048576 | tf_op jit(solution)/shard_map/all_to_all | solution.py:11
  39.6 7.4 %all-to-all-start.2 = ((f32[4,1,32,128]{3,2,1,0:T(8,128)}), f32[4,1,32,128]{3,2,1,0:T(8,128)S(1)}, u32[]{:S(2)}, u32[]{:S(2)}) async-start(f32[4,1,32,128]{3,2,1,0:T(8,128)} %bitcast.7), calls=%async_computation.2 | async-start | bytes 131072 | tf_op jit(solution)/shard_map/all_to_all | solution.py:36
  47.0 12.4 %all-to-all-start.3 = ((f32[8,64,128]{2,1,0:T(8,128)}), f32[8,64,128]{2,1,0:T(8,128)S(1)}, u32[]{:S(2)}, u32[]{:S(2)}) async-start(f32[8,64,128]{2,1,0:T(8,128)} %bitcast.12), calls=%async_computation.3 | async-start | bytes 524288 | tf_op jit(solution)/shard_map/all_to_all | solution.py:41
  51.3 8.1 %copy-start.1 = (f32[64,128]{1,0:T(8,128)S(1)}, f32[64,128]{1,0:T(8,128)}, u32[]{:S(2)}) copy-start(f32[64,128]{1,0:T(8,128)} %param.7) | copy-start | bytes 98308

commit v2 on v1

v2 whole, which is shorter than its diff:
```python
import jax
import jax.numpy as jnp
from jax import lax
from jax.sharding import PartitionSpec as P

HI = lax.Precision.HIGHEST


def shifted(value, axis, step):
    size = lax.axis_size(axis)
    return lax.ppermute(value, axis, [(i, (i + step) % size) for i in range(size)])


def to_all(value, axis):
    size = lax.axis_size(axis)
    return jnp.stack([shifted(value, axis, step) for step in range(size - 1, 0, -1)] + [value])


def turned(values, axis_at, first, size):
    twice = jnp.concatenate([values, values], axis=axis_at)
    return lax.dynamic_slice_in_dim(twice, first, size, axis_at)


def swap(values, axis):
    size = lax.axis_size(axis)
    me = lax.axis_index(axis)
    pieces = []
    for step in range(size):
        piece = lax.dynamic_index_in_dim(values, (me + step) % size, 0, keepdims=False)
        pieces.append(shifted(piece, axis, step) if step else piece)
    return pieces


def local(inverse_set, presence, factor, dinv):
    groups_row = lax.axis_size("row")
    groups_col = lax.axis_size("col")
    row_index = lax.axis_index("row")
    col_index = lax.axis_index("col")
    block_rows, _, order, width = factor.shape
    block_cols = inverse_set.shape[3]
    total = block_cols * groups_col * order
    span = width // groups_col
    share = order // groups_col
    rows = block_rows * order

    own = factor[:, 0]
    columns = to_all(lax.dynamic_slice_in_dim(own, col_index * span, span, 2), "row")
    columns = columns.transpose(1, 0, 2, 3).reshape(total, span)
    masked = (
        inverse_set[:, 0, :, :, 0, :] * presence[:, 0, :, 0].astype(jnp.float32)[:, None, :, None]
    )
    wide = to_all(masked, "col")
    wide = turned(wide, 0, (groups_col - 1 - col_index) % groups_col, groups_col)
    wide = wide.transpose(1, 2, 3, 0, 4).reshape(rows, block_rows, groups_row, order)
    wide = turned(wide, 2, (row_index + 1) % groups_row, groups_row).reshape(rows, total)
    update = jnp.dot(wide, columns, precision=HI)

    parts = update.reshape(block_rows, groups_col, share, span).transpose(1, 0, 2, 3)
    parts = jnp.stack(swap(-parts, "col")[::-1])
    parts = turned(parts, 0, (groups_col - 1 - col_index) % groups_col, groups_col)
    off_diag = parts.transpose(1, 2, 0, 3).reshape(block_rows, 1, share, width)

    terms = jnp.dot(own.reshape(rows, width).T, update, precision=HI)
    terms = terms.reshape(groups_row, width // groups_row, span)
    diag_block = dinv + sum(swap(terms, "row"))
    return (off_diag, diag_block)


def solution(mesh):
    in_specs = (
        P(None, "row", None, None, "col", None),
        P(None, "row", None, "col"),
        P(None, "row", None, None),
        P("row", "col"),
    )
    out_specs = (P(None, "row", "col", None), P("row", "col"))
    return jax.shard_map(local, mesh=mesh, in_specs=in_specs, out_specs=out_specs, check_vma=False)
```

time: 60.5 us -> 53.1 us (0.88)
  waiting for transfers between devices: 34 us -> 24.8 us
  starting transfers between devices: 17.6 us -> 22.7 us
  other arithmetic: 2.35 us -> 0.99 us
  local copies, waits for them, and re-layouts: 3.34 us -> 2.17 us
  matrix products: 2.05 us -> 1.41 us
    all_to_all x4 -> x0, waiting for transfers between devices: 34 us -> none  [the longest x2 23.1 us: to_all(): return lax.all_to_all(copies, axis, 0, 0)]
    ppermute x0 -> x20, waiting for transfers between devices: none -> 24.8 us  [shifted(): lax.ppermute(value, axis, [(i, (i + step) % size) for i in range(size)])]
    ppermute x0 -> x20, starting transfers between devices: none -> 22.7 us  [shifted(): lax.ppermute(value, axis, [(i, (i + step) % size) for i in range(size)])]
    all_to_all x4 -> x0, starting transfers between devices: 17.6 us -> none  [the longest x2 10.7 us: to_all(): return lax.all_to_all(copies, axis, 0, 0)]
    broadcast_in_dim x3 -> x0, local copies, waits for them, and re-layouts: 1.69 us -> none  [to_all(): copies = jnp.broadcast_to(value[None], (lax.axis_size(axis),) + value.shape)]
    mul x2, other arithmetic: 1.71 us -> 0.08 us  [local(): inverse_set[:, 0, :, :, 0, :]]
    dynamic_slice x0 -> x3, local copies, waits for them, and re-layouts: none -> 1.12 us  [the longest x1 0.88 us: local(): lax.dynamic_slice_in_dim(own, col_index * span, span, 2)]
    dot_general x1, local copies, waits for them, and re-layouts: 0.83 us -> 0.12 us  [local(): terms = jnp.dot(own.reshape(rows, width).T, update, precision=HI)]
  transfers between devices with their start and end apart: 4 -> 20, of which waited for: 4 -> 10; matrix products, arithmetic and copies ran while one was open for 3% -> 2% of each run, Pallas kernels for 0% -> 0%
where the time goes in v2:
time: 53.1 us; the launch traced here: 52.9 us
  waiting for transfers between devices  24.8 us (47%)
  starting transfers between devices  22.7 us (43%)
  local copies, waits for them, and re-layouts  2.17 us (4%)
  matrix products  1.41 us (3%)
  other arithmetic  0.99 us (2%)
  between operations  0.91 us (2%)
    ppermute x20, waiting for transfers between devices, shifted(): lax.ppermute(value, axis, [(i, (i + step) % size) for i in range(size)])  24.8 us
    ppermute x20, starting transfers between devices, shifted(): lax.ppermute(value, axis, [(i, (i + step) % size) for i in range(size)])  22.7 us
  transfers between devices with their start and end apart: 20, of which 10 were waited for; matrix products, arithmetic and copies ran while one was open for 2% of the time, Pallas kernels for 0%

profile of v2, /device:TPU:0, one launch (start us, length us, event | category | flops | bytes accessed | tf_op | source)
XLA Modules:
  0.0 52.9 jit_solution(17604306873002055897)
XLA Ops:
  0.7 0.9 %dynamic-slice_bitcast_fusion.1 = f32[1,128,128]{2,1,0:T(8,128)S(1)} fusion(f32[1,1,128,512]{3,2,1,0:T(8,128)} %param.6, s32[]{:T(128)S(6)} %select_n.111), kind=kLoop, calls=%fused_computation.24 | loop fusion | bytes 131076 | tf_op jit(solution)/shard_map/dynamic_slice | solution.py:47
  1.5 6.0 %collective-permute-start.3 = (f32[1,128,128]{2,1,0:T(8,128)S(1)}, f32[1,128,128]{2,1,0:T(8,128)S(1)}, u32[]{:S(2)}, u32[]{:S(2)}) collective-permute-start(f32[1,128,128]{2,1,0:T(8,128)S(1)} %dynamic-slice_bitcast_fusion.1), channel_id=1, source_target_pairs={{0,28},{4,0},{8,4},{12,8},{16,12},{20,16},{24,20},{28,24},{1,29},{... | collective-permute-start | bytes 196616 | tf_op jit(solution)/shard_map/ppermute | solution.py:11
  7.6 0.7 %collective-permute-start = (f32[1,128,2,128]{3,1,2,0:T(8,128)S(1)}, f32[1,128,2,128]{3,1,2,0:T(8,128)S(1)}, u32[]{:S(2)}, u32[]{:S(2)}) collective-permute-start(f32[1,128,2,128]{3,1,2,0:T(8,128)S(1)} %bitcast_multiply_fusion.1), channel_id=1, source_target_pairs={{0,3},{1,0},{2,1},{3,2},{4,7},{5,4},{6,5},{7,6},{8,11},{9,8},{10,9... | collective-permute-start | bytes 393224 | tf_op jit(solution)/shard_map/ppermute | solution.py:11
  8.3 0.9 %collective-permute-start.1 = (f32[1,128,2,128]{3,1,2,0:T(8,128)S(1)}, f32[1,128,2,128]{3,1,2,0:T(8,128)S(1)}, u32[]{:S(2)}, u32[]{:S(2)}) collective-permute-start(f32[1,128,2,128]{3,1,2,0:T(8,128)S(1)} %bitcast_multiply_fusion.1), channel_id=1, source_target_pairs={{0,2},{1,3},{2,0},{3,1},{4,6},{5,7},{6,4},{7,5},{8,10},{9,11},{10,... | collective-permute-start | bytes 393224 | tf_op jit(solution)/shard_map/ppermute | solution.py:11
  9.4 0.5 collective-permute-start.4
  9.9 1.8 %collective-permute-start.5 = (f32[1,128,128]{2,1,0:T(8,128)S(1)}, f32[1,128,128]{2,1,0:T(8,128)S(1)}, u32[]{:S(2)}, u32[]{:S(2)}) collective-permute-start(f32[1,128,128]{2,1,0:T(8,128)S(1)} %dynamic-slice_bitcast_fusion.1), channel_id=1, source_target_pairs={{0,20},{4,24},{8,28},{12,0},{16,4},{20,8},{24,12},{28,16},{1,21},{... | collective-permute-start | bytes 196616 | tf_op jit(solution)/shard_map/ppermute | solution.py:11
  11.7 2.6 %collective-permute-done.4 = f32[1,128,128]{2,1,0:T(8,128)S(1)} collective-permute-done((f32[1,128,128]{2,1,0:T(8,128)S(1)}, f32[1,128,128]{2,1,0:T(8,128)S(1)}, u32[]{:S(2)}, u32[]{:S(2)}) %collective-permute-start.4) | collective-permute-done | bytes 65568 | tf_op jit(solution)/shard_map/ppermute | solution.py:11
  14.3 1.2 %collective-permute-done.5 = f32[1,128,128]{2,1,0:T(8,128)S(1)} collective-permute-done((f32[1,128,128]{2,1,0:T(8,128)S(1)}, f32[1,128,128]{2,1,0:T(8,128)S(1)}, u32[]{:S(2)}, u32[]{:S(2)}) %collective-permute-start.5) | collective-permute-done | bytes 65568 | tf_op jit(solution)/shard_map/ppermute | solution.py:11
  15.6 1.7 %collective-permute-start.7 = (f32[1,128,128]{2,1,0:T(8,128)S(1)}, f32[1,128,128]{2,1,0:T(8,128)S(1)}, u32[]{:S(2)}, u32[]{:S(2)}) collective-permute-start(f32[1,128,128]{2,1,0:T(8,128)S(1)} %dynamic-slice_bitcast_fusion.1), channel_id=1, source_target_pairs={{0,12},{4,16},{8,20},{12,24},{16,28},{20,0},{24,4},{28,8},{1,13},{... | collective-permute-start | bytes 196616 | tf_op jit(solution)/shard_map/ppermute | solution.py:11
  17.3 3.3 %collective-permute-done.6 = f32[1,128,128]{2,1,0:T(8,128)S(1)} collective-permute-done((f32[1,128,128]{2,1,0:T(8,128)S(1)}, f32[1,128,128]{2,1,0:T(8,128)S(1)}, u32[]{:S(2)}, u32[]{:S(2)}) %collective-permute-start.6) | collective-permute-done | bytes 65568 | tf_op jit(solution)/shard_map/ppermute | solution.py:11
  20.5 3.1 %collective-permute-done.7 = f32[1,128,128]{2,1,0:T(8,128)S(1)} collective-permute-done((f32[1,128,128]{2,1,0:T(8,128)S(1)}, f32[1,128,128]{2,1,0:T(8,128)S(1)}, u32[]{:S(2)}, u32[]{:S(2)}) %collective-permute-start.7) | collective-permute-done | bytes 65568 | tf_op jit(solution)/shard_map/ppermute | solution.py:11
  23.7 1.1 %collective-permute-start.9 = (f32[1,128,128]{2,1,0:T(8,128)S(1)}, f32[1,128,128]{2,1,0:T(8,128)S(1)}, u32[]{:S(2)}, u32[]{:S(2)}) collective-permute-start(f32[1,128,128]{2,1,0:T(8,128)S(1)} %dynamic-slice_bitcast_fusion.1), channel_id=1, source_target_pairs={{0,4},{4,8},{8,12},{12,16},{16,20},{20,24},{24,28},{28,0},{1,5},{5... | collective-permute-start | bytes 196616 | tf_op jit(solution)/shard_map/ppermute | solution.py:11
  24.8 1.8 %collective-permute-done.8 = f32[1,128,128]{2,1,0:T(8,128)S(1)} collective-permute-done((f32[1,128,128]{2,1,0:T(8,128)S(1)}, f32[1,128,128]{2,1,0:T(8,128)S(1)}, u32[]{:S(2)}, u32[]{:S(2)}) %collective-permute-start.8) | collective-permute-done | bytes 65568 | tf_op jit(solution)/shard_map/ppermute | solution.py:11
  26.6 4.0 %collective-permute-done.9 = f32[1,128,128]{2,1,0:T(8,128)S(1)} collective-permute-done((f32[1,128,128]{2,1,0:T(8,128)S(1)}, f32[1,128,128]{2,1,0:T(8,128)S(1)}, u32[]{:S(2)}, u32[]{:S(2)}) %collective-permute-start.9) | collective-permute-done | bytes 65568 | tf_op jit(solution)/shard_map/ppermute | solution.py:11
  31.4 1.0 %fusion.11 = (f32[128,128]{1,0:T(8,128)S(1)}, f32[128,128]{1,0:T(8,128)S(1)}) fusion(f32[128,1024]{0,1:T(8,128)S(1)} %bitcast.103, f32[1024,128]{1,0:T(8,128)S(1)} %bitcast.107), kind=kOutput, calls=%fused_computation.53 | convolution fusion | flops 201342976 | bytes 1179648 | tf_op jit(solution)/shard_map/dot_general | solution.py:56
  33.2 2.3 %collective-permute-start.15 = (f32[64,128]{1,0:T(8,128)S(1)}, f32[64,128]{1,0:T(8,128)S(1)}, u32[]{:S(2)}, u32[]{:S(2)}) collective-permute-start(f32[64,128]{1,0:T(8,128)S(1)} %get-tuple-element.7), channel_id=1, source_target_pairs={{0,12},{4,16},{8,20},{12,24},{16,28},{20,0},{24,4},{28,8},{1,13},{... | collective-permute-start | bytes 98312 | tf_op jit(solution)/shard_map/ppermute | solution.py:11
  35.5 2.9 %collective-permute-start.16 = (f32[64,128]{1,0:T(8,128)S(1)}, f32[64,128]{1,0:T(8,128)S(1)}, u32[]{:S(2)}, u32[]{:S(2)}) collective-permute-start(f32[64,128]{1,0:T(8,128)S(1)} %get-tuple-element.6), channel_id=1, source_target_pairs={{0,16},{4,20},{8,24},{12,28},{16,0},{20,4},{24,8},{28,12},{1,17},{... | collective-permute-start | bytes 98312 | tf_op jit(solution)/shard_map/ppermute | solution.py:11
  38.4 3.7 %collective-permute-done.11 = f32[1,32,128]{2,1,0:T(8,128)S(1)} collective-permute-done((f32[1,32,128]{2,1,0:T(8,128)S(1)}, f32[1,32,128]{2,1,0:T(8,128)S(1)}, u32[]{:S(2)}, u32[]{:S(2)}) %collective-permute-start.11) | collective-permute-done | bytes 16416 | tf_op jit(solution)/shard_map/ppermute | solution.py:11
  42.1 3.2 %collective-permute-done.12 = f32[1,32,128]{2,1,0:T(8,128)S(1)} collective-permute-done((f32[1,32,128]{2,1,0:T(8,128)S(1)}, f32[1,32,128]{2,1,0:T(8,128)S(1)}, u32[]{:S(2)}, u32[]{:S(2)}) %collective-permute-start.12) | collective-permute-done | bytes 16416 | tf_op jit(solution)/shard_map/ppermute | solution.py:11
  45.4 2.9 %collective-permute-start.18 = (f32[64,128]{1,0:T(8,128)S(1)}, f32[64,128]{1,0:T(8,128)S(1)}, u32[]{:S(2)}, u32[]{:S(2)}) collective-permute-start(f32[64,128]{1,0:T(8,128)S(1)} %get-tuple-element.4), channel_id=1, source_target_pairs={{0,24},{4,28},{8,0},{12,4},{16,8},{20,12},{24,16},{28,20},{1,25},{... | collective-permute-start | bytes 98312 | tf_op jit(solution)/shard_map/ppermute | solution.py:11
  48.4 1.4 %collective-permute-start.19 = (f32[64,128]{1,0:T(8,128)S(1)}, f32[64,128]{1,0:T(8,128)S(1)}, u32[]{:S(2)}, u32[]{:S(2)}) collective-permute-start(f32[64,128]{1,0:T(8,128)S(1)} %get-tuple-element.3), channel_id=1, source_target_pairs={{0,28},{4,0},{8,4},{12,8},{16,12},{20,16},{24,20},{28,24},{1,29},{... | collective-permute-start | bytes 98312 | tf_op jit(solution)/shard_map/ppermute | solution.py:11
  49.9 0.7 %reshape.60 = f32[1,1,32,512]{3,2,1,0:T(8,128)} reshape(f32[1,32,4,128]{3,2,1,0:T(4,128)S(1)} %copy.30) | data formatting | bytes 131072 | tf_op jit(solution)/shard_map/reshape | solution.py:61
  50.7 1.6 %collective-permute-done.19 = f32[64,128]{1,0:T(8,128)S(1)} collective-permute-done((f32[64,128]{1,0:T(8,128)S(1)}, f32[64,128]{1,0:T(8,128)S(1)}, u32[]{:S(2)}, u32[]{:S(2)}) %collective-permute-start.19) | collective-permute-done | bytes 32800 | tf_op jit(solution)/shard_map/ppermute | solution.py:11
  52.3 0.6 %fusion.10 = f32[64,128]{1,0:T(8,128)} fusion(f32[64,128]{1,0:T(8,128)S(1)} %copy-done.2, f32[64,128]{1,0:T(8,128)S(1)} %collective-permute-done.19, f32[64,128]{1,0:T(8,128)S(1)} %collective-permute-done.18, f32[64,128]{1,0:T(8,128)S(1)} %collective-permute-done.17, f32[64,128]{1,0:T(8,128)S(1)} %collective-permute-done.16, ...), kind=kLoop, calls=%fused_computation.40 | loop fusion | flops 65536 | bytes 327684 | tf_op jit(solution)/shard_map/add | solution.py:65
  (63 shorter events, 2.0 us)
Async XLA Ops:
  0.6 6.9 %copy-start = (f32[1,1,128,2,1,128]{5,4,3,2,1,0:T(1,128)S(1)}, f32[1,1,128,2,1,128]{5,4,3,2,1,0:T(1,128)}, u32[]{:S(2)}) copy-start(f32[1,1,128,2,1,128]{5,4,3,2,1,0:T(1,128)} %param.4) | copy-start | bytes 393220
  0.6 6.9 %copy-start.3 = (s32[1,1,2,1]{2,3,1,0:T(1,128)S(1)}, s32[1,1,2,1]{2,3,1,0:T(1,128)}, u32[]{:S(2)}) copy-start(s32[1,1,2,1]{2,3,1,0:T(1,128)} %param.5) | copy-start | bytes 28
  1.5 8.3 %collective-permute-start.3 = (f32[1,128,128]{2,1,0:T(8,128)S(1)}, f32[1,128,128]{2,1,0:T(8,128)S(1)}, u32[]{:S(2)}, u32[]{:S(2)}) collective-permute-start(f32[1,128,128]{2,1,0:T(8,128)S(1)} %dynamic-slice_bitcast_fusion.1), channel_id=1, source_target_pairs={{0,28},{4,0},{8,4},{12,8},{16,12},{20,16},{24,20},{28,24},{1,29},{... | collective-permute-start | bytes 196616 | tf_op jit(solution)/shard_map/ppermute | solution.py:11
  7.6 23.1 %collective-permute-start = (f32[1,128,2,128]{3,1,2,0:T(8,128)S(1)}, f32[1,128,2,128]{3,1,2,0:T(8,128)S(1)}, u32[]{:S(2)}, u32[]{:S(2)}) collective-permute-start(f32[1,128,2,128]{3,1,2,0:T(8,128)S(1)} %bitcast_multiply_fusion.1), channel_id=1, source_target_pairs={{0,3},{1,0},{2,1},{3,2},{4,7},{5,4},{6,5},{7,6},{8,11},{9,8},{10,9... | collective-permute-start | bytes 393224 | tf_op jit(solution)/shard_map/ppermute | solution.py:11
  8.3 22.4 %collective-permute-start.1 = (f32[1,128,2,128]{3,1,2,0:T(8,128)S(1)}, f32[1,128,2,128]{3,1,2,0:T(8,128)S(1)}, u32[]{:S(2)}, u32[]{:S(2)}) collective-permute-start(f32[1,128,2,128]{3,1,2,0:T(8,128)S(1)} %bitcast_multiply_fusion.1), channel_id=1, source_target_pairs={{0,2},{1,3},{2,0},{3,1},{4,6},{5,7},{6,4},{7,5},{8,10},{9,11},{10,... | collective-permute-start | bytes 393224 | tf_op jit(solution)/shard_map/ppermute | solution.py:11
  9.3 21.5 %collective-permute-start.2 = (f32[1,128,2,128]{3,1,2,0:T(8,128)S(1)}, f32[1,128,2,128]{3,1,2,0:T(8,128)S(1)}, u32[]{:S(2)}, u32[]{:S(2)}) collective-permute-start(f32[1,128,2,128]{3,1,2,0:T(8,128)S(1)} %bitcast_multiply_fusion.1), channel_id=1, source_target_pairs={{0,1},{1,2},{2,3},{3,0},{4,5},{5,6},{6,7},{7,4},{8,9},{9,10},{10,1... | collective-permute-start | bytes 393224 | tf_op jit(solution)/shard_map/ppermute | solution.py:11
  9.4 4.9 %collective-permute-start.4 = (f32[1,128,128]{2,1,0:T(8,128)S(1)}, f32[1,128,128]{2,1,0:T(8,128)S(1)}, u32[]{:S(2)}, u32[]{:S(2)}) collective-permute-start(f32[1,128,128]{2,1,0:T(8,128)S(1)} %dynamic-slice_bitcast_fusion.1), channel_id=1, source_target_pairs={{0,24},{4,28},{8,0},{12,4},{16,8},{20,12},{24,16},{28,20},{1,25},{... | collective-permute-start | bytes 196616 | tf_op jit(solution)/shard_map/ppermute | solution.py:11
  9.9 5.7 %collective-permute-start.5 = (f32[1,128,128]{2,1,0:T(8,128)S(1)}, f32[1,128,128]{2,1,0:T(8,128)S(1)}, u32[]{:S(2)}, u32[]{:S(2)}) collective-permute-start(f32[1,128,128]{2,1,0:T(8,128)S(1)} %dynamic-slice_bitcast_fusion.1), channel_id=1, source_target_pairs={{0,20},{4,24},{8,28},{12,0},{16,4},{20,8},{24,12},{28,16},{1,21},{... | collective-permute-start | bytes 196616 | tf_op jit(solution)/shard_map/ppermute | solution.py:11
  14.3 6.2 %collective-permute-start.6 = (f32[1,128,128]{2,1,0:T(8,128)S(1)}, f32[1,128,128]{2,1,0:T(8,128)S(1)}, u32[]{:S(2)}, u32[]{:S(2)}) collective-permute-start(f32[1,128,128]{2,1,0:T(8,128)S(1)} %dynamic-slice_bitcast_fusion.1), channel_id=1, source_target_pairs={{0,16},{4,20},{8,24},{12,28},{16,0},{20,4},{24,8},{28,12},{1,17},{... | collective-permute-start | bytes 196616 | tf_op jit(solution)/shard_map/ppermute | solution.py:11
  15.6 8.1 %collective-permute-start.7 = (f32[1,128,128]{2,1,0:T(8,128)S(1)}, f32[1,128,128]{2,1,0:T(8,128)S(1)}, u32[]{:S(2)}, u32[]{:S(2)}) collective-permute-start(f32[1,128,128]{2,1,0:T(8,128)S(1)} %dynamic-slice_bitcast_fusion.1), channel_id=1, source_target_pairs={{0,12},{4,16},{8,20},{12,24},{16,28},{20,0},{24,4},{28,8},{1,13},{... | collective-permute-start | bytes 196616 | tf_op jit(solution)/shard_map/ppermute | solution.py:11
  17.3 13.4 %copy-start.1 = (f32[1,1,128,512]{3,2,1,0:T(8,128)S(1)}, f32[1,1,128,512]{3,2,1,0:T(8,128)}, u32[]{:S(2)}) copy-start(f32[1,1,128,512]{3,2,1,0:T(8,128)} %param.6) | copy-start | bytes 786436
  20.5 6.1 %collective-permute-start.8 = (f32[1,128,128]{2,1,0:T(8,128)S(1)}, f32[1,128,128]{2,1,0:T(8,128)S(1)}, u32[]{:S(2)}, u32[]{:S(2)}) collective-permute-start(f32[1,128,128]{2,1,0:T(8,128)S(1)} %dynamic-slice_bitcast_fusion.1), channel_id=1, source_target_pairs={{0,8},{4,12},{8,16},{12,20},{16,24},{20,28},{24,0},{28,4},{1,9},{5... | collective-permute-start | bytes 196616 | tf_op jit(solution)/shard_map/ppermute | solution.py:11
  23.7 7.0 %collective-permute-start.9 = (f32[1,128,128]{2,1,0:T(8,128)S(1)}, f32[1,128,128]{2,1,0:T(8,128)S(1)}, u32[]{:S(2)}, u32[]{:S(2)}) collective-permute-start(f32[1,128,128]{2,1,0:T(8,128)S(1)} %dynamic-slice_bitcast_fusion.1), channel_id=1, source_target_pairs={{0,4},{4,8},{8,12},{12,16},{16,20},{20,24},{24,28},{28,0},{1,5},{5... | collective-permute-start | bytes 196616 | tf_op jit(solution)/shard_map/ppermute | solution.py:11
  33.0 5.5 %collective-permute-start.10 = (f32[1,32,128]{2,1,0:T(8,128)S(1)}, f32[1,32,128]{2,1,0:T(8,128)S(1)}, u32[]{:S(2)}, u32[]{:S(2)}) collective-permute-start(f32[1,32,128]{2,1,0:T(8,128)S(1)} %get-tuple-element.11), channel_id=1, source_target_pairs={{0,3},{1,0},{2,1},{3,2},{4,7},{5,4},{6,5},{7,6},{8,11},{9,8},{10,9... | collective-permute-start | bytes 49160 | tf_op jit(solution)/shard_map/ppermute | solution.py:11
  33.1 12.4 %collective-permute-start.13 = (f32[64,128]{1,0:T(8,128)S(1)}, f32[64,128]{1,0:T(8,128)S(1)}, u32[]{:S(2)}, u32[]{:S(2)}) collective-permute-start(f32[64,128]{1,0:T(8,128)S(1)} %get-tuple-element.2), channel_id=1, source_target_pairs={{0,4},{4,8},{8,12},{12,16},{16,20},{20,24},{24,28},{28,0},{1,5},{5... | collective-permute-start | bytes 98312 | tf_op jit(solution)/shard_map/ppermute | solution.py:11
  33.1 15.2 %collective-permute-start.14 = (f32[64,128]{1,0:T(8,128)S(1)}, f32[64,128]{1,0:T(8,128)S(1)}, u32[]{:S(2)}, u32[]{:S(2)}) collective-permute-start(f32[64,128]{1,0:T(8,128)S(1)} %get-tuple-element.8), channel_id=1, source_target_pairs={{0,8},{4,12},{8,16},{12,20},{16,24},{20,28},{24,0},{28,4},{1,9},{5... | collective-permute-start | bytes 98312 | tf_op jit(solution)/shard_map/ppermute | solution.py:11
  33.2 17.3 %collective-permute-start.15 = (f32[64,128]{1,0:T(8,128)S(1)}, f32[64,128]{1,0:T(8,128)S(1)}, u32[]{:S(2)}, u32[]{:S(2)}) collective-permute-start(f32[64,128]{1,0:T(8,128)S(1)} %get-tuple-element.7), channel_id=1, source_target_pairs={{0,12},{4,16},{8,20},{12,24},{16,28},{20,0},{24,4},{28,8},{1,13},{... | collective-permute-start | bytes 98312 | tf_op jit(solution)/shard_map/ppermute | solution.py:11
  35.5 15.1 %collective-permute-start.16 = (f32[64,128]{1,0:T(8,128)S(1)}, f32[64,128]{1,0:T(8,128)S(1)}, u32[]{:S(2)}, u32[]{:S(2)}) collective-permute-start(f32[64,128]{1,0:T(8,128)S(1)} %get-tuple-element.6), channel_id=1, source_target_pairs={{0,16},{4,20},{8,24},{12,28},{16,0},{20,4},{24,8},{28,12},{1,17},{... | collective-permute-start | bytes 98312 | tf_op jit(solution)/shard_map/ppermute | solution.py:11
  38.4 3.7 %collective-permute-start.11 = (f32[1,32,128]{2,1,0:T(8,128)S(1)}, f32[1,32,128]{2,1,0:T(8,128)S(1)}, u32[]{:S(2)}, u32[]{:S(2)}) collective-permute-start(f32[1,32,128]{2,1,0:T(8,128)S(1)} %get-tuple-element.10), channel_id=1, source_target_pairs={{0,2},{1,3},{2,0},{3,1},{4,6},{5,7},{6,4},{7,5},{8,10},{9,11},{10,... | collective-permute-start | bytes 49160 | tf_op jit(solution)/shard_map/ppermute | solution.py:11
  42.1 3.2 %collective-permute-start.12 = (f32[1,32,128]{2,1,0:T(8,128)S(1)}, f32[1,32,128]{2,1,0:T(8,128)S(1)}, u32[]{:S(2)}, u32[]{:S(2)}) collective-permute-start(f32[1,32,128]{2,1,0:T(8,128)S(1)} %get-tuple-element.9), channel_id=1, source_target_pairs={{0,1},{1,2},{2,3},{3,0},{4,5},{5,6},{6,7},{7,4},{8,9},{9,10},{10,1... | collective-permute-start | bytes 49160 | tf_op jit(solution)/shard_map/ppermute | solution.py:11
  45.3 5.2 %collective-permute-start.17 = (f32[64,128]{1,0:T(8,128)S(1)}, f32[64,128]{1,0:T(8,128)S(1)}, u32[]{:S(2)}, u32[]{:S(2)}) collective-permute-start(f32[64,128]{1,0:T(8,128)S(1)} %get-tuple-element.5), channel_id=1, source_target_pairs={{0,20},{4,24},{8,28},{12,0},{16,4},{20,8},{24,12},{28,16},{1,21},{... | collective-permute-start | bytes 98312 | tf_op jit(solution)/shard_map/ppermute | solution.py:11
  45.4 5.3 %collective-permute-start.18 = (f32[64,128]{1,0:T(8,128)S(1)}, f32[64,128]{1,0:T(8,128)S(1)}, u32[]{:S(2)}, u32[]{:S(2)}) collective-permute-start(f32[64,128]{1,0:T(8,128)S(1)} %get-tuple-element.4), channel_id=1, source_target_pairs={{0,24},{4,28},{8,0},{12,4},{16,8},{20,12},{24,16},{28,20},{1,25},{... | collective-permute-start | bytes 98312 | tf_op jit(solution)/shard_map/ppermute | solution.py:11
  48.4 3.9 %collective-permute-start.19 = (f32[64,128]{1,0:T(8,128)S(1)}, f32[64,128]{1,0:T(8,128)S(1)}, u32[]{:S(2)}, u32[]{:S(2)}) collective-permute-start(f32[64,128]{1,0:T(8,128)S(1)} %get-tuple-element.3), channel_id=1, source_target_pairs={{0,28},{4,0},{8,4},{12,8},{16,12},{20,16},{24,20},{28,24},{1,29},{... | collective-permute-start | bytes 98312 | tf_op jit(solution)/shard_map/ppermute | solution.py:11
  49.9 2.4 %copy-start.2 = (f32[64,128]{1,0:T(8,128)S(1)}, f32[64,128]{1,0:T(8,128)}, u32[]{:S(2)}) copy-start(f32[64,128]{1,0:T(8,128)} %param.7) | copy-start | bytes 98308

commit v3 on v1

--- a/solution.py
+++ b/solution.py
@@ -6,9 +6,44 @@
 HI = lax.Precision.HIGHEST
 
 
+def flipped(value, axis, flip):
+    return lax.ppermute(value, axis, [(i, i ^ flip) for i in range(lax.axis_size(axis))])
+
+
 def to_all(value, axis):
     copies = jnp.broadcast_to(value[None], (lax.axis_size(axis),) + value.shape)
     return lax.all_to_all(copies, axis, 0, 0)
+
+
+def doubled(value, axis):
+    me = lax.axis_index(axis)
+    held = value[None]
+    bit = 1
+    while bit < lax.axis_size(axis):
+        other = flipped(held, axis, bit)
+        upper = (me & bit) != 0
+        held = jnp.concatenate([jnp.where(upper, other, held), jnp.where(upper, held, other)])
+        bit *= 2
+    return held
+
+
+def swap(values, axis):
+    size = lax.axis_size(axis)
+    me = lax.axis_index(axis)
+    pieces = []
+    for flip in range(size):
+        piece = lax.dynamic_index_in_dim(values, me ^ flip, 0, keepdims=False)
+        pieces.append(flipped(piece, axis, flip) if flip else piece)
+    held = [piece[None] for piece in pieces]
+    bit = 1
+    while bit < size:
+        upper = (me & bit) != 0
+        held = [
+            jnp.concatenate([jnp.where(upper, b, a), jnp.where(upper, a, b)])
+            for a, b in zip(held[::2], held[1::2])
+        ]
+        bit *= 2
+    return held[0]
 
 
 def local(inverse_set, presence, factor, dinv):
@@ -23,23 +58,22 @@
     rows = block_rows * order
 
     own = factor[:, 0]
+    columns = to_all(lax.dynamic_slice_in_dim(own, col_index * span, span, 2), "row")
+    columns = columns.transpose(1, 0, 2, 3).reshape(total, span)
     masked = (
         inverse_set[:, 0, :, :, 0, :] * presence[:, 0, :, 0].astype(jnp.float32)[:, None, :, None]
     )
-    columns = to_all(lax.dynamic_slice_in_dim(own, col_index * span, span, 2), "row")
-    columns = columns.transpose(1, 0, 2, 3).reshape(total, span)
-    wide = to_all(masked, "col")
+    wide = doubled(masked, "col")
     wide = wide.transpose(1, 2, 3, 0, 4).reshape(rows, total)
     update = jnp.dot(wide, columns, precision=HI)
 
-    parts = update.reshape(block_rows, groups_col, share, span).transpose(1, 0, 2, 3)
-    parts = lax.all_to_all(-parts, "col", 0, 0)
-    off_diag = parts.transpose(1, 2, 0, 3).reshape(block_rows, 1, share, width)
-
     terms = jnp.dot(own.reshape(rows, width).T, update, precision=HI)
     terms = terms.reshape(groups_row, width // groups_row, span)
-    terms = lax.all_to_all(terms, "row", 0, 0)
-    diag_block = dinv + terms.sum(axis=0)
+    diag_block = dinv + lax.all_to_all(terms, "row", 0, 0).sum(axis=0)
+
+    parts = update.reshape(block_rows, groups_col, share, span).transpose(1, 0, 2, 3)
+    parts = swap(-parts, "col")
+    off_diag = parts.transpose(1, 2, 0, 3).reshape(block_rows, 1, share, width)
     return (off_diag, diag_block)
 
 

time: 60.5 us -> 44.3 us (0.73)
  waiting for transfers between devices: 34 us -> 22.9 us
  starting transfers between devices: 17.6 us -> 14.5 us
  other arithmetic: 2.35 us -> 0.94 us
  matrix products: 2.05 us -> 1.41 us
    all_to_all x2 -> x1, waiting for transfers between devices: 23.1 us -> 6.44 us  [to_all(): return lax.all_to_all(copies, axis, 0, 0)]
    ppermute x0 -> x5, waiting for transfers between devices: none -> 8.05 us  [flipped(): lax.ppermute(value, axis, [(i, i ^ flip) for i in range(lax.axis_size(axi...]
    ppermute x0 -> x5, starting transfers between devices: none -> 4.02 us  [flipped(): lax.ppermute(value, axis, [(i, i ^ flip) for i in range(lax.axis_size(axi...]
    all_to_all x2 -> x1, starting transfers between devices: 10.7 us -> 6.84 us  [to_all(): return lax.all_to_all(copies, axis, 0, 0)]
    all_to_all x2 -> x1, starting transfers between devices: 6.9 us -> 3.64 us  [local(): diag_block = dinv + lax.all_to_all(terms, 'row', 0, 0).sum(axis=0)]
    all_to_all x2 -> x1, waiting for transfers between devices: 10.9 us -> 8.39 us  [local(): diag_block = dinv + lax.all_to_all(terms, 'row', 0, 0).sum(axis=0)]
    mul x2, other arithmetic: 1.71 us -> 0.08 us  [local(): inverse_set[:, 0, :, :, 0, :]]
    broadcast_in_dim x3 -> x2, local copies, waits for them, and re-layouts: 1.69 us -> 0.83 us  [to_all(): copies = jnp.broadcast_to(value[None], (lax.axis_size(axis),) + value.shape)]
  transfers between devices with their start and end apart: 4 -> 7, of which waited for: 4 -> 4; matrix products, arithmetic and copies ran while one was open for 3% -> 7% of each run, Pallas kernels for 0% -> 0%
where the time goes in v3:
time: 44.3 us; the launch traced here: 44 us
  waiting for transfers between devices  22.9 us (52%)
  starting transfers between devices  14.5 us (33%)
  local copies, waits for them, and re-layouts  3.44 us (8%)
  matrix products  1.41 us (3%)
  other arithmetic  0.94 us (2%)
  between operations  0.81 us (2%)
    all_to_all x1, waiting for transfers between devices, local(): diag_block = dinv + lax.all_to_all(terms, 'row', 0, 0).sum(axis=0)  8.39 us
    ppermute x5, waiting for transfers between devices, flipped(): lax.ppermute(value, axis, [(i, i ^ flip) for i in range(lax.axis_size(axi...  8.05 us
    all_to_all x1, starting transfers between devices, to_all(): return lax.all_to_all(copies, axis, 0, 0)  6.84 us
    all_to_all x1, waiting for transfers between devices, to_all(): return lax.all_to_all(copies, axis, 0, 0)  6.44 us
    ppermute x5, starting transfers between devices, flipped(): lax.ppermute(value, axis, [(i, i ^ flip) for i in range(lax.axis_size(axi...  4.02 us
    all_to_all x1, starting transfers between devices, local(): diag_block = dinv + lax.all_to_all(terms, 'row', 0, 0).sum(axis=0)  3.64 us
    unnamed x7, local copies, waits for them, and re-layouts  1.06 us
    dot_general x1, matrix products, local(): update = jnp.dot(wide, columns, precision=HI)  1 us
  transfers between devices with their start and end apart: 7, of which 4 were waited for; matrix products, arithmetic and copies ran while one was open for 7% of the time, Pallas kernels for 0%

profile of v3, /device:TPU:0, one launch (start us, length us, event | category | flops | bytes accessed | tf_op | source)
XLA Modules:
  0.0 44.0 jit_solution(1510787598225228431)
XLA Ops:
  0.6 0.0 copy-start
  0.7 1.0 %copy.8 = f32[1,1,128,2,1,128]{2,5,3,4,1,0:T(8,128)S(1)} copy(f32[1,1,128,2,1,128]{5,4,3,2,1,0:T(1,128)} %param.4) | data formatting | bytes 262144 | tf_op args[0]
  1.7 0.1 bitcast_multiply_fusion
  1.8 0.5 %collective-permute-start = (f32[1,1,128,2,128]{2,4,0,3,1:T(8,128)S(1)}, f32[1,1,128,2,128]{2,4,0,3,1:T(8,128)S(1)}, u32[]{:S(2)}, u32[]{:S(2)}) collective-permute-start(f32[1,1,128,2,128]{2,4,0,3,1:T(8,128)S(1)} %bitcast_multiply_fusion), channel_id=1, source_target_pairs={{0,1},{1,0},{2,3},{3,2},{4,5},{5,4},{6,7},{7,6},{8,9},{9,8},{10,11... | collective-permute-start | bytes 393224 | tf_op jit(solution)/shard_map/ppermute | solution.py:10
  2.3 0.8 %broadcast_in_dim.7 = f32[8,1,128,128]{3,2,1,0:T(8,128)} broadcast(f32[128,128]{1,0:T(8,128)S(1)} %dynamic-slice_bitcast_fusion), dimensions={2,3} | broadcast | bytes 589824 | tf_op jit(solution)/shard_map/broadcast_in_dim | solution.py:14
  3.2 6.8 %all-to-all-start = ((f32[8,1,128,128]{3,2,1,0:T(8,128)}), f32[8,1,128,128]{3,2,1,0:T(8,128)S(1)}, u32[]{:S(2)}, u32[]{:S(2)}) async-start(f32[8,1,128,128]{3,2,1,0:T(8,128)} %broadcast_in_dim.7), calls=%async_computation | async-start | bytes 1048576 | tf_op jit(solution)/shard_map/all_to_all | solution.py:15
  10.0 0.0 collective-permute-done
  10.0 0.1 broadcast_select_fusion.3
  10.1 1.6 %collective-permute-start.1 = (f32[2,1,128,2,128]{2,4,0,3,1:T(8,128)S(1)}, f32[2,1,128,2,128]{2,4,0,3,1:T(8,128)S(1)}, u32[]{:S(2)}, u32[]{:S(2)}) collective-permute-start(f32[2,1,128,2,128]{2,4,0,3,1:T(8,128)S(1)} %pad_maximum_fusion.1), channel_id=1, source_target_pairs={{0,2},{1,3},{2,0},{3,1},{4,6},{5,7},{6,4},{7,5},{8,10},{9,11},{10,... | collective-permute-start | bytes 786440 | tf_op jit(solution)/shard_map/ppermute | solution.py:10
  11.7 6.9 %collective-permute-done.1 = f32[2,1,128,2,128]{2,4,0,3,1:T(8,128)S(1)} collective-permute-done((f32[2,1,128,2,128]{2,4,0,3,1:T(8,128)S(1)}, f32[2,1,128,2,128]{2,4,0,3,1:T(8,128)S(1)}, u32[]{:S(2)}, u32[]{:S(2)}) %collective-permute-start.1) | collective-permute-done | bytes 262176 | tf_op jit(solution)/shard_map/ppermute | solution.py:10
  18.7 6.4 %all-to-all-done = f32[8,1,128,128]{3,2,1,0:T(8,128)S(1)} async-done(((f32[8,1,128,128]{3,2,1,0:T(8,128)}), f32[8,1,128,128]{3,2,1,0:T(8,128)S(1)}, u32[]{:S(2)}, u32[]{:S(2)}) %all-to-all-start) | async-done | bytes 524320 | tf_op jit(solution)/shard_map/all_to_all | solution.py:15
  25.1 1.0 %fusion.3 = (f32[128,128]{1,0:T(8,128)S(1)}, f32[128,128]{1,0:T(8,128)S(1)}) fusion(f32[128,1024]{0,1:T(8,128)S(1)} %bitcast.40, f32[1024,128]{1,0:T(8,128)S(1)} %bitcast.39), kind=kOutput, calls=%fused_computation.23 | convolution fusion | flops 201342976 | bytes 1179648 | tf_op jit(solution)/shard_map/dot_general | solution.py:68
  26.1 0.1 collective-permute-start.4
  26.2 1.2 %collective-permute-done.4 = f32[1,32,128]{2,1,0:T(8,128)S(1)} collective-permute-done((f32[1,32,128]{2,1,0:T(8,128)S(1)}, f32[1,32,128]{2,1,0:T(8,128)S(1)}, u32[]{:S(2)}, u32[]{:S(2)}) %collective-permute-start.4) | collective-permute-done | bytes 16416 | tf_op jit(solution)/shard_map/ppermute | solution.py:10
  27.4 1.3 %collective-permute-start.2 = (f32[1,32,128]{2,1,0:T(8,128)S(1)}, f32[1,32,128]{2,1,0:T(8,128)S(1)}, u32[]{:S(2)}, u32[]{:S(2)}) collective-permute-start(f32[1,32,128]{2,1,0:T(8,128)S(1)} %get-tuple-element.10), channel_id=1, source_target_pairs={{0,3},{1,2},{2,1},{3,0},{4,7},{5,6},{6,5},{7,4},{8,11},{9,10},{10,... | collective-permute-start | bytes 49160 | tf_op jit(solution)/shard_map/ppermute | solution.py:10
  28.7 0.5 %collective-permute-start.3 = (f32[1,32,128]{2,1,0:T(8,128)S(1)}, f32[1,32,128]{2,1,0:T(8,128)S(1)}, u32[]{:S(2)}, u32[]{:S(2)}) collective-permute-start(f32[1,32,128]{2,1,0:T(8,128)S(1)} %get-tuple-element.11), channel_id=1, source_target_pairs={{0,2},{1,3},{2,0},{3,1},{4,6},{5,7},{6,4},{7,5},{8,10},{9,11},{10,... | collective-permute-start | bytes 49160 | tf_op jit(solution)/shard_map/ppermute | solution.py:10
  29.3 0.4 convolution_bitcast_fusion
  29.7 0.8 %copy.11 = f32[512,128]{1,0:T(8,128)} copy(f32[512,128]{0,1:T(8,128)S(1)} %convolution_bitcast_fusion) | data formatting | bytes 524288 | tf_op jit(solution)/shard_map/dot_general | solution.py:70
  30.5 3.6 %all-to-all-start.1 = ((f32[8,64,128]{2,1,0:T(8,128)}), f32[8,64,128]{2,1,0:T(8,128)S(1)}, u32[]{:S(2)}, u32[]{:S(2)}) async-start(f32[8,64,128]{2,1,0:T(8,128)} %bitcast.17), calls=%async_computation.1 | async-start | bytes 524288 | tf_op jit(solution)/shard_map/all_to_all | solution.py:72
  34.2 0.0 collective-permute-done.2
  34.2 0.0 collective-permute-done.3
  34.3 0.7 %reshape.171 = f32[1,1,32,512]{3,2,1,0:T(8,128)} reshape(f32[1,32,4,128]{3,2,1,0:T(4,128)S(1)} %copy.10) | data formatting | bytes 131072 | tf_op jit(solution)/shard_map/reshape | solution.py:76
  34.9 8.4 %all-to-all-done.1 = f32[8,64,128]{2,1,0:T(8,128)S(1)} async-done(((f32[8,64,128]{2,1,0:T(8,128)}), f32[8,64,128]{2,1,0:T(8,128)S(1)}, u32[]{:S(2)}, u32[]{:S(2)}) %all-to-all-start.1) | async-done | bytes 262176 | tf_op jit(solution)/shard_map/all_to_all | solution.py:72
  43.3 0.6 %add.24 = f32[64,128]{1,0:T(8,128)} add(f32[64,128]{1,0:T(8,128)S(1)} %copy-done.1, f32[64,128]{1,0:T(8,128)S(1)} %reduce_sum.9) | non-fusion elementwise | flops 8192 | bytes 98304 | tf_op jit(solution)/shard_map/add | solution.py:72
  (17 shorter events, 0.2 us)
Async XLA Ops:
  0.6 1.7 %copy-start = (f32[1,1,128,512]{3,2,1,0:T(8,128)S(1)}, f32[1,1,128,512]{3,2,1,0:T(8,128)}, u32[]{:S(2)}) copy-start(f32[1,1,128,512]{3,2,1,0:T(8,128)} %param.6) | copy-start | bytes 786436
  0.6 1.1 %copy-start.2 = (s32[1,1,2,1]{2,3,1,0:T(1,128)S(1)}, s32[1,1,2,1]{2,3,1,0:T(1,128)}, u32[]{:S(2)}) copy-start(s32[1,1,2,1]{2,3,1,0:T(1,128)} %param.5) | copy-start | bytes 28
  1.8 8.2 %collective-permute-start = (f32[1,1,128,2,128]{2,4,0,3,1:T(8,128)S(1)}, f32[1,1,128,2,128]{2,4,0,3,1:T(8,128)S(1)}, u32[]{:S(2)}, u32[]{:S(2)}) collective-permute-start(f32[1,1,128,2,128]{2,4,0,3,1:T(8,128)S(1)} %bitcast_multiply_fusion), channel_id=1, source_target_pairs={{0,1},{1,0},{2,3},{3,2},{4,5},{5,4},{6,7},{7,6},{8,9},{9,8},{10,11... | collective-permute-start | bytes 393224 | tf_op jit(solution)/shard_map/ppermute | solution.py:10
  3.2 22.0 %all-to-all-start = ((f32[8,1,128,128]{3,2,1,0:T(8,128)}), f32[8,1,128,128]{3,2,1,0:T(8,128)S(1)}, u32[]{:S(2)}, u32[]{:S(2)}) async-start(f32[8,1,128,128]{3,2,1,0:T(8,128)} %broadcast_in_dim.7), calls=%async_computation | async-start | bytes 1048576 | tf_op jit(solution)/shard_map/all_to_all | solution.py:15
  10.1 8.5 %collective-permute-start.1 = (f32[2,1,128,2,128]{2,4,0,3,1:T(8,128)S(1)}, f32[2,1,128,2,128]{2,4,0,3,1:T(8,128)S(1)}, u32[]{:S(2)}, u32[]{:S(2)}) collective-permute-start(f32[2,1,128,2,128]{2,4,0,3,1:T(8,128)S(1)} %pad_maximum_fusion.1), channel_id=1, source_target_pairs={{0,2},{1,3},{2,0},{3,1},{4,6},{5,7},{6,4},{7,5},{8,10},{9,11},{10,... | collective-permute-start | bytes 786440 | tf_op jit(solution)/shard_map/ppermute | solution.py:10
  26.1 1.2 %collective-permute-start.4 = (f32[1,32,128]{2,1,0:T(8,128)S(1)}, f32[1,32,128]{2,1,0:T(8,128)S(1)}, u32[]{:S(2)}, u32[]{:S(2)}) collective-permute-start(f32[1,32,128]{2,1,0:T(8,128)S(1)} %dynamic-slice_bitcast_fusion.1), channel_id=1, source_target_pairs={{0,1},{1,0},{2,3},{3,2},{4,5},{5,4},{6,7},{7,6},{8,9},{9,8},{10,11... | collective-permute-start | bytes 49160 | tf_op jit(solution)/shard_map/ppermute | solution.py:10
  27.4 6.7 %collective-permute-start.2 = (f32[1,32,128]{2,1,0:T(8,128)S(1)}, f32[1,32,128]{2,1,0:T(8,128)S(1)}, u32[]{:S(2)}, u32[]{:S(2)}) collective-permute-start(f32[1,32,128]{2,1,0:T(8,128)S(1)} %get-tuple-element.10), channel_id=1, source_target_pairs={{0,3},{1,2},{2,1},{3,0},{4,7},{5,6},{6,5},{7,4},{8,11},{9,10},{10,... | collective-permute-start | bytes 49160 | tf_op jit(solution)/shard_map/ppermute | solution.py:10
  28.7 5.4 %collective-permute-start.3 = (f32[1,32,128]{2,1,0:T(8,128)S(1)}, f32[1,32,128]{2,1,0:T(8,128)S(1)}, u32[]{:S(2)}, u32[]{:S(2)}) collective-permute-start(f32[1,32,128]{2,1,0:T(8,128)S(1)} %get-tuple-element.11), channel_id=1, source_target_pairs={{0,2},{1,3},{2,0},{3,1},{4,6},{5,7},{6,4},{7,5},{8,10},{9,11},{10,... | collective-permute-start | bytes 49160 | tf_op jit(solution)/shard_map/ppermute | solution.py:10
  30.5 12.8 %all-to-all-start.1 = ((f32[8,64,128]{2,1,0:T(8,128)}), f32[8,64,128]{2,1,0:T(8,128)S(1)}, u32[]{:S(2)}, u32[]{:S(2)}) async-start(f32[8,64,128]{2,1,0:T(8,128)} %bitcast.17), calls=%async_computation.1 | async-start | bytes 524288 | tf_op jit(solution)/shard_map/all_to_all | solution.py:72
  34.9 8.4 %copy-start.1 = (f32[64,128]{1,0:T(8,128)S(1)}, f32[64,128]{1,0:T(8,128)}, u32[]{:S(2)}) copy-start(f32[64,128]{1,0:T(8,128)} %param.7) | copy-start | bytes 98308

commit v4 on v3

v4 whole, which is shorter than its diff:
```python
import jax
import jax.numpy as jnp
from jax import lax
from jax.sharding import PartitionSpec as P

HI = lax.Precision.HIGHEST


def flipped(value, axis, flip):
    return lax.ppermute(value, axis, [(i, i ^ flip) for i in range(lax.axis_size(axis))])


def ordered(lower_first, first, second):
    return jnp.stack([jnp.where(lower_first, first, second), jnp.where(lower_first, second, first)])


def swap(values, axis):
    size = lax.axis_size(axis)
    me = lax.axis_index(axis)
    held = []
    for flip in range(size):
        piece = lax.dynamic_index_in_dim(values, me ^ flip, 0, keepdims=True)
        held.append(flipped(piece, axis, flip) if flip else piece)
    bit = 1
    while bit < size:
        lower = (me & bit) == 0
        held = [
            ordered(lower, a, b).reshape((2 * a.shape[0],) + a.shape[1:])
            for a, b in zip(held[::2], held[1::2])
        ]
        bit *= 2
    return held[0]


def pair_rows(masked):
    groups_row = lax.axis_size("row")
    groups_col = lax.axis_size("col")
    row_bit = lax.axis_index("row") & 1
    col_index = lax.axis_index("col")
    col_bit = col_index & 1
    cross = [
        (r * groups_col + c, (r ^ 1) * groups_col + (c ^ 1))
        for r in range(groups_row)
        for c in range(groups_col)
        if (r ^ c) & 1
    ]
    held = jnp.where(row_bit == col_bit, masked, lax.ppermute(masked, ("row", "col"), cross))[None]
    bit = 2
    while bit < groups_col:
        other = flipped(held, "col", bit)
        lower = (col_index & bit) == 0
        held = ordered(lower, held, other).reshape((2 * held.shape[0],) + held.shape[1:])
        bit *= 2
    return ordered(col_bit == 0, held, flipped(held, "col", 1))


def local(inverse_set, presence, factor, dinv):
    groups_row = lax.axis_size("row")
    groups_col = lax.axis_size("col")
    row_bit = lax.axis_index("row") & 1
    col_index = lax.axis_index("col")
    block_rows, _, order, width = factor.shape
    block_cols = inverse_set.shape[3]
    half = block_cols * (groups_col // 2) * order
    span = width // groups_col
    share = order // groups_col
    rows = block_rows * order

    own = factor[:, 0]
    mine = lax.dynamic_slice_in_dim(own, col_index * span, span, 2)
    lines = [list(range(bit, groups_row, 2)) for bit in range(2)]
    copies = jnp.broadcast_to(mine[None], (groups_row // 2,) + mine.shape)
    columns = lax.all_to_all(copies, "row", 0, 0, axis_index_groups=lines)
    columns = columns.transpose(1, 0, 2, 3).reshape(half, span)

    masked = (
        inverse_set[:, 0, :, :, 0, :] * presence[:, 0, :, 0].astype(jnp.float32)[:, None, :, None]
    )
    wide = pair_rows(masked).transpose(0, 2, 3, 4, 1, 5).reshape(2 * rows, half)
    pair_factor = ordered(row_bit == 0, own, flipped(own, "row", 1)).reshape(2 * rows, width)

    partial_pair = jnp.dot(wide, columns, precision=HI)
    terms = jnp.dot(pair_factor.T, partial_pair, precision=HI)
    terms = terms.reshape(groups_row, width // groups_row, span)
    diag_block = dinv + lax.all_to_all(terms, "row", 0, 0).sum(axis=0)

    partial_pair = -partial_pair.reshape(2, rows, span)
    kept = lax.dynamic_index_in_dim(partial_pair, row_bit, 0, keepdims=False)
    sent = lax.dynamic_index_in_dim(partial_pair, 1 - row_bit, 0, keepdims=False)
    parts = (kept + flipped(sent, "row", 1)).reshape(block_rows, groups_col, share, span)
    parts = swap(parts.transpose(1, 0, 2, 3), "col")
    off_diag = parts.transpose(1, 2, 0, 3).reshape(block_rows, 1, share, width)
    return (off_diag, diag_block)


def solution(mesh):
    in_specs = (
        P(None, "row", None, None, "col", None),
        P(None, "row", None, "col"),
        P(None, "row", None, None),
        P("row", "col"),
    )
    out_specs = (P(None, "row", "col", None), P("row", "col"))
    return jax.shard_map(local, mesh=mesh, in_specs=in_specs, out_specs=out_specs, check_vma=False)
```

time: 44.3 us -> 54.2 us (1.22)
  starting transfers between devices: 14.5 us -> 25.4 us
  waiting for transfers between devices: 22.9 us -> 19.9 us
  other arithmetic: 0.94 us -> 3.37 us
  local copies, waits for them, and re-layouts: 3.44 us -> 2.44 us
    ppermute x5 -> x7, starting transfers between devices: 4.02 us -> 15.7 us  [flipped(): lax.ppermute(value, axis, [(i, i ^ flip) for i in range(lax.axis_size(axi...]
    ppermute x5 -> x7, waiting for transfers between devices: 8.05 us -> 6.07 us  [flipped(): lax.ppermute(value, axis, [(i, i ^ flip) for i in range(lax.axis_size(axi...]
    all_to_all x1, starting transfers between devices: 6.84 us -> 4.87 us  [local(): columns = lax.all_to_all(copies, 'row', 0, 0, axis_index_groups=lines)]
    mul x2, other arithmetic: 0.08 us -> 1.74 us  [local(): inverse_set[:, 0, :, :, 0, :]]
    all_to_all x1, waiting for transfers between devices: 6.44 us -> 4.96 us  [local(): columns = lax.all_to_all(copies, 'row', 0, 0, axis_index_groups=lines)]
    unnamed x7 -> x6, local copies, waits for them, and re-layouts: 1.06 us -> 0.01 us
    dot_general x1 -> x0, local copies, waits for them, and re-layouts: 0.83 us -> none  [local(): terms = jnp.dot(own.reshape(rows, width).T, update, precision=HI)]
    ppermute x0 -> x1, starting transfers between devices: none -> 0.67 us  [pair_rows(): lax.ppermute(masked, ('row', 'col'), cross)]
  transfers between devices with their start and end apart: 7 -> 10, of which waited for: 4 -> 5; matrix products, arithmetic and copies ran while one was open for 7% -> 9% of each run, Pallas kernels for 0% -> 0%
where the time goes in v4:
time: 54.2 us; the launch traced here: 53.8 us
  starting transfers between devices  25.4 us (47%)
  waiting for transfers between devices  19.9 us (37%)
  other arithmetic  3.37 us (6%)
  local copies, waits for them, and re-layouts  2.44 us (5%)
  matrix products  1.85 us (3%)
  between operations  0.84 us (2%)
    ppermute x7, starting transfers between devices, flipped(): lax.ppermute(value, axis, [(i, i ^ flip) for i in range(lax.axis_size(axi...  15.7 us
    all_to_all x1, waiting for transfers between devices, local(): diag_block = dinv + lax.all_to_all(terms, 'row', 0, 0).sum(axis=0)  8.9 us
    ppermute x7, waiting for transfers between devices, flipped(): lax.ppermute(value, axis, [(i, i ^ flip) for i in range(lax.axis_size(axi...  6.07 us
    all_to_all x1, waiting for transfers between devices, local(): columns = lax.all_to_all(copies, 'row', 0, 0, axis_index_groups=lines)  4.96 us
    all_to_all x1, starting transfers between devices, local(): columns = lax.all_to_all(copies, 'row', 0, 0, axis_index_groups=lines)  4.87 us
    all_to_all x1, starting transfers between devices, local(): diag_block = dinv + lax.all_to_all(terms, 'row', 0, 0).sum(axis=0)  4.15 us
    mul x2, other arithmetic, local(): inverse_set[:, 0, :, :, 0, :]  1.74 us
    dot_general x1, matrix products, local(): terms = jnp.dot(pair_factor.T, partial_pair, precision=HI)  1.27 us
  transfers between devices with their start and end apart: 10, of which 5 were waited for; matrix products, arithmetic and copies ran while one was open for 9% of the time, Pallas kernels for 0%

profile of v4, /device:TPU:0, one launch (start us, length us, event | category | flops | bytes accessed | tf_op | source)
XLA Modules:
  0.0 53.8 jit_solution(14959936411262957451)
XLA Ops:
  0.6 0.7 %convert_bitcast_fusion = f32[2]{0:T(128)S(1)} fusion(s32[1,1,2,1]{2,3,1,0:T(1,128)} %param.5), kind=kLoop, calls=%fused_computation.28 | loop fusion | flops 2 | bytes 16 | tf_op jit(solution)/shard_map/mul | solution.py:77
  1.3 1.1 %broadcast_multiply_fusion = f32[1,128,2,128]{3,2,1,0:T(2,128)S(1)} fusion(f32[1,128,2,128]{3,2,1,0:T(2,128)} %bitcast.71, f32[2]{0:T(128)S(1)} %convert_bitcast_fusion), kind=kLoop, calls=%fused_computation.12 | loop fusion | flops 32768 | bytes 262152 | tf_op jit(solution)/shard_map/mul | solution.py:77
  2.4 0.7 %collective-permute-start = (f32[1,128,2,128]{3,2,1,0:T(2,128)S(1)}, f32[1,128,2,128]{3,2,1,0:T(2,128)S(1)}, u32[]{:S(2)}, u32[]{:S(2)}) collective-permute-start(f32[1,128,2,128]{3,2,1,0:T(2,128)S(1)} %broadcast_multiply_fusion), channel_id=1, source_target_pairs={{1,4},{3,6},{4,1},{6,3},{9,12},{11,14},{12,9},{14,11},{17,20},{19,... | collective-permute-start | bytes 393224 | tf_op jit(solution)/shard_map/ppermute | solution.py:47
  3.2 3.0 %collective-permute-start.1 = (f32[1,1,128,2,128]{4,3,2,1,0:T(2,128)S(1)}, f32[1,1,128,2,128]{4,3,2,1,0:T(2,128)S(1)}, u32[]{:S(2)}, u32[]{:S(2)}) collective-permute-start(f32[1,1,128,2,128]{4,3,2,1,0:T(2,128)S(1)} %select_bitcast_fusion.6), channel_id=1, source_target_pairs={{0,2},{1,3},{2,0},{3,1},{4,6},{5,7},{6,4},{7,5},{8,10},{9,11},{10,... | collective-permute-start | bytes 393224 | tf_op jit(solution)/shard_map/ppermute | solution.py:10
  6.3 2.9 %collective-permute-done.1 = f32[1,1,128,2,128]{4,3,2,1,0:T(2,128)S(1)} collective-permute-done((f32[1,1,128,2,128]{4,3,2,1,0:T(2,128)S(1)}, f32[1,1,128,2,128]{4,3,2,1,0:T(2,128)S(1)}, u32[]{:S(2)}, u32[]{:S(2)}) %collective-permute-start.1) | collective-permute-done | bytes 131104 | tf_op jit(solution)/shard_map/ppermute | solution.py:10
  9.4 4.9 %collective-permute-start.2 = (f32[2,1,128,2,128]{4,3,2,0,1:T(2,128)S(1)}, f32[2,1,128,2,128]{4,3,2,0,1:T(2,128)S(1)}, u32[]{:S(2)}, u32[]{:S(2)}) collective-permute-start(f32[2,1,128,2,128]{4,3,2,0,1:T(2,128)S(1)} %maximum_bitcast_fusion.1), channel_id=1, source_target_pairs={{0,1},{1,0},{2,3},{3,2},{4,5},{5,4},{6,7},{7,6},{8,9},{9,8},{10,11... | collective-permute-start | bytes 786440 | tf_op jit(solution)/shard_map/ppermute | solution.py:10
  14.3 0.7 %broadcast_in_dim.14 = f32[4,1,128,128]{3,2,1,0:T(8,128)} broadcast(f32[128,128]{1,0:T(8,128)S(1)} %dynamic-slice_bitcast_fusion.1), dimensions={2,3} | broadcast | bytes 327680 | tf_op jit(solution)/shard_map/broadcast_in_dim | solution.py:72
  15.0 4.9 %all-to-all-start = ((f32[4,1,128,128]{3,2,1,0:T(8,128)}), f32[4,1,128,128]{3,2,1,0:T(8,128)S(1)}, u32[]{:S(2)}, u32[]{:S(2)}) async-start(f32[4,1,128,128]{3,2,1,0:T(8,128)} %broadcast_in_dim.14), calls=%async_computation | async-start | bytes 524288 | tf_op jit(solution)/shard_map/all_to_all | solution.py:73
  19.9 3.5 %collective-permute-start.7 = (f32[1,128,512]{2,1,0:T(8,128)S(1)}, f32[1,128,512]{2,1,0:T(8,128)S(1)}, u32[]{:S(2)}, u32[]{:S(2)}) collective-permute-start(f32[1,128,512]{2,1,0:T(8,128)S(1)} %bitcast.75), channel_id=1, source_target_pairs={{0,4},{4,0},{8,12},{12,8},{16,20},{20,16},{24,28},{28,24},{1,5},{5... | collective-permute-start | bytes 786440 | tf_op jit(solution)/shard_map/ppermute | solution.py:10
  23.4 0.2 select_bitcast_fusion.3
  23.6 0.2 maximum_bitcast_fusion
  23.9 0.4 copy.11
  24.3 0.4 reshape.95
  24.7 5.0 %all-to-all-done = f32[4,1,128,128]{3,2,1,0:T(8,128)S(1)} async-done(((f32[4,1,128,128]{3,2,1,0:T(8,128)}), f32[4,1,128,128]{3,2,1,0:T(8,128)S(1)}, u32[]{:S(2)}, u32[]{:S(2)}) %all-to-all-start) | async-done | bytes 262176 | tf_op jit(solution)/shard_map/all_to_all | solution.py:73
  29.7 0.6 %fusion.2 = (f32[256,128]{1,0:T(8,128)S(1)}, f32[256,128]{1,0:T(8,128)S(1)}) fusion(f32[256,512]{1,0:T(8,128)S(1)} %reshape.95, f32[512,128]{1,0:T(8,128)S(1)} %bitcast.70), kind=kOutput, calls=%fused_computation.29 | convolution fusion | flops 201359360 | bytes 1048576 | tf_op jit(solution)/shard_map/dot_general | solution.py:82
  30.3 2.6 %collective-permute-start.3 = (f32[128,128]{1,0:T(8,128)S(1)}, f32[128,128]{1,0:T(8,128)S(1)}, u32[]{:S(2)}, u32[]{:S(2)}) collective-permute-start(f32[128,128]{1,0:T(8,128)S(1)} %dynamic-slice_bitcast_fusion), channel_id=1, source_target_pairs={{0,4},{4,0},{8,12},{12,8},{16,20},{20,16},{24,28},{28,24},{1,5},{5... | collective-permute-start | bytes 196616 | tf_op jit(solution)/shard_map/ppermute | solution.py:10
  33.0 2.2 %collective-permute-done.3 = f32[128,128]{1,0:T(8,128)S(1)} collective-permute-done((f32[128,128]{1,0:T(8,128)S(1)}, f32[128,128]{1,0:T(8,128)S(1)}, u32[]{:S(2)}, u32[]{:S(2)}) %collective-permute-start.3) | collective-permute-done | bytes 65568 | tf_op jit(solution)/shard_map/ppermute | solution.py:10
  35.5 0.9 %collective-permute-done.4 = f32[1,1,32,128]{3,2,1,0:T(8,128)S(1)} collective-permute-done((f32[1,1,32,128]{3,2,1,0:T(8,128)S(1)}, f32[1,1,32,128]{3,2,1,0:T(8,128)S(1)}, u32[]{:S(2)}, u32[]{:S(2)}) %collective-permute-start.4) | collective-permute-done | bytes 16416 | tf_op jit(solution)/shard_map/ppermute | solution.py:10
  36.5 1.6 %collective-permute-start.5 = (f32[1,1,32,128]{3,2,1,0:T(8,128)S(1)}, f32[1,1,32,128]{3,2,1,0:T(8,128)S(1)}, u32[]{:S(2)}, u32[]{:S(2)}) collective-permute-start(f32[1,1,32,128]{3,2,1,0:T(8,128)S(1)} %get-tuple-element.13), channel_id=1, source_target_pairs={{0,2},{1,3},{2,0},{3,1},{4,6},{5,7},{6,4},{7,5},{8,10},{9,11},{10,... | collective-permute-start | bytes 49160 | tf_op jit(solution)/shard_map/ppermute | solution.py:10
  38.1 1.3 %fusion = f32[8,64,128]{2,1,0:T(8,128)} fusion(f32[8,64,256]{2,1,0:T(8,128)S(1)} %bitcast.68, f32[256,128]{1,0:T(8,128)S(1)} %get-tuple-element.17), kind=kOutput, calls=%fused_computation.7 | convolution fusion | flops 201326592 | bytes 917504 | tf_op jit(solution)/shard_map/dot_general | solution.py:83
  39.3 4.1 %all-to-all-start.1 = ((f32[8,64,128]{2,1,0:T(8,128)}), f32[8,64,128]{2,1,0:T(8,128)S(1)}, u32[]{:S(2)}, u32[]{:S(2)}) async-start(f32[8,64,128]{2,1,0:T(8,128)} %fusion), calls=%async_computation.1 | async-start | bytes 524288 | tf_op jit(solution)/shard_map/all_to_all | solution.py:85
  43.6 0.7 %reshape.97 = f32[1,1,32,512]{3,2,1,0:T(8,128)} reshape(f32[1,32,4,128]{3,2,1,0:T(4,128)S(1)} %bitcast.78) | data formatting | bytes 131072 | tf_op jit(solution)/shard_map/reshape | solution.py:92
  44.3 8.9 %all-to-all-done.1 = f32[8,64,128]{2,1,0:T(8,128)S(1)} async-done(((f32[8,64,128]{2,1,0:T(8,128)}), f32[8,64,128]{2,1,0:T(8,128)S(1)}, u32[]{:S(2)}, u32[]{:S(2)}) %all-to-all-start.1) | async-done | bytes 262176 | tf_op jit(solution)/shard_map/all_to_all | solution.py:85
  53.2 0.6 %add.38 = f32[64,128]{1,0:T(8,128)} add(f32[64,128]{1,0:T(8,128)S(1)} %copy-done.2, f32[64,128]{1,0:T(8,128)S(1)} %reduce_sum.9) | non-fusion elementwise | flops 8192 | bytes 98304 | tf_op jit(solution)/shard_map/add | solution.py:85
  (28 shorter events, 0.9 us)
Async XLA Ops:
  1.3 1.8 %copy-start = (f32[1,1,128,2,1,128]{5,4,3,2,1,0:T(1,128)S(1)}, f32[1,1,128,2,1,128]{5,4,3,2,1,0:T(1,128)}, u32[]{:S(2)}) copy-start(f32[1,1,128,2,1,128]{5,4,3,2,1,0:T(1,128)} %param.4) | copy-start | bytes 393220
  2.4 0.7 %collective-permute-start = (f32[1,128,2,128]{3,2,1,0:T(2,128)S(1)}, f32[1,128,2,128]{3,2,1,0:T(2,128)S(1)}, u32[]{:S(2)}, u32[]{:S(2)}) collective-permute-start(f32[1,128,2,128]{3,2,1,0:T(2,128)S(1)} %broadcast_multiply_fusion), channel_id=1, source_target_pairs={{1,4},{3,6},{4,1},{6,3},{9,12},{11,14},{12,9},{14,11},{17,20},{19,... | collective-permute-start | bytes 393224 | tf_op jit(solution)/shard_map/ppermute | solution.py:47
  3.2 6.0 %collective-permute-start.1 = (f32[1,1,128,2,128]{4,3,2,1,0:T(2,128)S(1)}, f32[1,1,128,2,128]{4,3,2,1,0:T(2,128)S(1)}, u32[]{:S(2)}, u32[]{:S(2)}) collective-permute-start(f32[1,1,128,2,128]{4,3,2,1,0:T(2,128)S(1)} %select_bitcast_fusion.6), channel_id=1, source_target_pairs={{0,2},{1,3},{2,0},{3,1},{4,6},{5,7},{6,4},{7,5},{8,10},{9,11},{10,... | collective-permute-start | bytes 393224 | tf_op jit(solution)/shard_map/ppermute | solution.py:10
  9.3 5.0 %copy-start.1 = (f32[1,1,128,512]{3,2,1,0:T(8,128)S(1)}, f32[1,1,128,512]{3,2,1,0:T(8,128)}, u32[]{:S(2)}) copy-start(f32[1,1,128,512]{3,2,1,0:T(8,128)} %param.6) | copy-start | bytes 786436
  9.4 14.0 %collective-permute-start.2 = (f32[2,1,128,2,128]{4,3,2,0,1:T(2,128)S(1)}, f32[2,1,128,2,128]{4,3,2,0,1:T(2,128)S(1)}, u32[]{:S(2)}, u32[]{:S(2)}) collective-permute-start(f32[2,1,128,2,128]{4,3,2,0,1:T(2,128)S(1)} %maximum_bitcast_fusion.1), channel_id=1, source_target_pairs={{0,1},{1,0},{2,3},{3,2},{4,5},{5,4},{6,7},{7,6},{8,9},{9,8},{10,11... | collective-permute-start | bytes 786440 | tf_op jit(solution)/shard_map/ppermute | solution.py:10
  15.0 14.7 %all-to-all-start = ((f32[4,1,128,128]{3,2,1,0:T(8,128)}), f32[4,1,128,128]{3,2,1,0:T(8,128)S(1)}, u32[]{:S(2)}, u32[]{:S(2)}) async-start(f32[4,1,128,128]{3,2,1,0:T(8,128)} %broadcast_in_dim.14), calls=%async_computation | async-start | bytes 524288 | tf_op jit(solution)/shard_map/all_to_all | solution.py:73
  19.9 13.0 %collective-permute-start.7 = (f32[1,128,512]{2,1,0:T(8,128)S(1)}, f32[1,128,512]{2,1,0:T(8,128)S(1)}, u32[]{:S(2)}, u32[]{:S(2)}) collective-permute-start(f32[1,128,512]{2,1,0:T(8,128)S(1)} %bitcast.75), channel_id=1, source_target_pairs={{0,4},{4,0},{8,12},{12,8},{16,20},{20,16},{24,28},{28,24},{1,5},{5... | collective-permute-start | bytes 786440 | tf_op jit(solution)/shard_map/ppermute | solution.py:10
  30.3 4.9 %collective-permute-start.3 = (f32[128,128]{1,0:T(8,128)S(1)}, f32[128,128]{1,0:T(8,128)S(1)}, u32[]{:S(2)}, u32[]{:S(2)}) collective-permute-start(f32[128,128]{1,0:T(8,128)S(1)} %dynamic-slice_bitcast_fusion), channel_id=1, source_target_pairs={{0,4},{4,0},{8,12},{12,8},{16,20},{20,16},{24,28},{28,24},{1,5},{5... | collective-permute-start | bytes 196616 | tf_op jit(solution)/shard_map/ppermute | solution.py:10
  35.2 1.2 %collective-permute-start.4 = (f32[1,1,32,128]{3,2,1,0:T(8,128)S(1)}, f32[1,1,32,128]{3,2,1,0:T(8,128)S(1)}, u32[]{:S(2)}, u32[]{:S(2)}) collective-permute-start(f32[1,1,32,128]{3,2,1,0:T(8,128)S(1)} %constant_dynamic-slice_fusion.2), channel_id=1, source_target_pairs={{0,1},{1,0},{2,3},{3,2},{4,5},{5,4},{6,7},{7,6},{8,9},{9,8},{10,11... | collective-permute-start | bytes 49160 | tf_op jit(solution)/shard_map/ppermute | solution.py:10
  36.5 7.0 %collective-permute-start.5 = (f32[1,1,32,128]{3,2,1,0:T(8,128)S(1)}, f32[1,1,32,128]{3,2,1,0:T(8,128)S(1)}, u32[]{:S(2)}, u32[]{:S(2)}) collective-permute-start(f32[1,1,32,128]{3,2,1,0:T(8,128)S(1)} %get-tuple-element.13), channel_id=1, source_target_pairs={{0,2},{1,3},{2,0},{3,1},{4,6},{5,7},{6,4},{7,5},{8,10},{9,11},{10,... | collective-permute-start | bytes 49160 | tf_op jit(solution)/shard_map/ppermute | solution.py:10
  38.1 5.4 %collective-permute-start.6 = (f32[1,1,32,128]{3,2,1,0:T(8,128)S(1)}, f32[1,1,32,128]{3,2,1,0:T(8,128)S(1)}, u32[]{:S(2)}, u32[]{:S(2)}) collective-permute-start(f32[1,1,32,128]{3,2,1,0:T(8,128)S(1)} %get-tuple-element.12), channel_id=1, source_target_pairs={{0,3},{1,2},{2,1},{3,0},{4,7},{5,6},{6,5},{7,4},{8,11},{9,10},{10,... | collective-permute-start | bytes 49160 | tf_op jit(solution)/shard_map/ppermute | solution.py:10
  39.3 13.8 %all-to-all-start.1 = ((f32[8,64,128]{2,1,0:T(8,128)}), f32[8,64,128]{2,1,0:T(8,128)S(1)}, u32[]{:S(2)}, u32[]{:S(2)}) async-start(f32[8,64,128]{2,1,0:T(8,128)} %fusion), calls=%async_computation.1 | async-start | bytes 524288 | tf_op jit(solution)/shard_map/all_to_all | solution.py:85
  44.3 8.9 %copy-start.2 = (f32[64,128]{1,0:T(8,128)S(1)}, f32[64,128]{1,0:T(8,128)}, u32[]{:S(2)}) copy-start(f32[64,128]{1,0:T(8,128)} %param.7) | copy-start | bytes 98308

commit v5 on v1

v5 whole, which is shorter than its diff:
```python
import functools

import jax
import jax.numpy as jnp
from jax import lax
from jax.experimental import pallas as pl
from jax.experimental.pallas import tpu as pltpu
from jax.sharding import PartitionSpec as P

LANES = 128
WHOLE = pl.BlockSpec(memory_space=pltpu.VMEM)
LIGHT = pl.CostEstimate(flops=1000, bytes_accessed=1000, transcendentals=0)


def flipped(value, axis, flip):
    return lax.ppermute(value, axis, [(i, i ^ flip) for i in range(lax.axis_size(axis))])


def two_parts(value):
    high = value.astype(jnp.bfloat16)
    return high, (value - high.astype(jnp.float32)).astype(jnp.bfloat16)


def product(left, right, contract):
    left_high, left_low = two_parts(left)
    right_high, right_low = two_parts(right)

    def once(a, b):
        return lax.dot_general(a, b, (contract, ((), ())), preferred_element_type=jnp.float32)

    return once(left_high, right_high) + (once(left_high, right_low) + once(left_low, right_high))


def prepare_kernel(presence, blocks, factor, masked, copies, sems):
    count, rows, span = copies.shape
    first = pl.multiple_of(lax.axis_index("col") * span, LANES)
    sends = [
        pltpu.make_async_copy(factor.at[:, pl.ds(first, span)], copies.at[i], sems.at[i])
        for i in range(count)
    ]
    for send in sends:
        send.start()
    block_cols, _, order = masked.shape
    block_rows = rows // order
    for a in range(block_rows):
        for b in range(block_cols):
            weight = presence[a * block_cols + b].astype(jnp.float32)
            picked = blocks[pl.ds(a * order * block_cols + b, order, stride=block_cols), :]
            masked[b, pl.ds(a * order, order), :] = picked * weight
    for send in sends:
        send.wait()


def prepare(presence, blocks, own, receivers, span):
    rows, width = own.shape
    block_cols = blocks.shape[0] // rows
    order = blocks.shape[1]
    if span % LANES:
        first = lax.axis_index("col") * span
        mine = lax.dynamic_slice_in_dim(own, first, span, 1)
        weights = presence.reshape(-1, 1, block_cols, 1).astype(jnp.float32)
        picked = blocks.reshape(-1, order, block_cols, order) * weights
        masked = picked.transpose(2, 0, 1, 3).reshape(block_cols, rows, order)
        return masked, jnp.broadcast_to(mine[None], (receivers, rows, span))
    return pl.pallas_call(
        prepare_kernel,
        out_shape=(
            jax.ShapeDtypeStruct((block_cols, rows, order), jnp.float32),
            jax.ShapeDtypeStruct((receivers, rows, span), jnp.float32),
        ),
        in_specs=[pl.BlockSpec(memory_space=pltpu.SMEM), WHOLE, pl.BlockSpec(memory_space=pl.ANY)],
        out_specs=(WHOLE, pl.BlockSpec(memory_space=pl.ANY)),
        scratch_shapes=[pltpu.SemaphoreType.DMA((receivers,))],
        cost_estimate=LIGHT,
    )(presence, blocks, own)


def middle_kernel(count, *refs):
    pieces = refs[: 2 * count]
    columns, own, near, terms, kept, sent = refs[2 * count :]
    block_cols, rows, _ = pieces[0].shape
    col_index = lax.axis_index("col")
    left, right = [], []
    for t in range(count):
        for b in range(block_cols):
            left.append(jnp.concatenate([pieces[t][b], pieces[count + t][b]], axis=0))
            right.append(columns[b * count + ((col_index >> 1) ^ t)])
    both = product(jnp.concatenate(left, axis=1), jnp.concatenate(right, axis=0), ((1,), (0,)))
    first, second = both[:rows], both[rows:]
    same = (lax.axis_index("row") & 1) == (col_index & 1)
    mine = jnp.where(same, first, second)
    other = jnp.where(same, second, first)
    kept[...] = -mine
    sent[...] = -other
    factors = jnp.concatenate([own[...], near[...]], axis=0)
    terms[...] = product(factors, jnp.concatenate([mine, other], axis=0), ((0,), (0,)))


def middle(pieces, columns, own, near):
    rows, width = own.shape
    span = columns.shape[2]
    part = jax.ShapeDtypeStruct((rows, span), jnp.float32)
    return pl.pallas_call(
        functools.partial(middle_kernel, len(pieces) // 2),
        out_shape=(jax.ShapeDtypeStruct((width, span), jnp.float32), part, part),
        in_specs=[WHOLE] * (len(pieces) + 3),
        out_specs=(WHOLE,) * 3,
        cost_estimate=LIGHT,
        compiler_params=pltpu.CompilerParams(vmem_limit_bytes=32 * 1024 * 1024),
    )(*pieces, columns, own, near)


def collect_kernel(*refs):
    out = refs[-1]
    span = refs[0].shape[1]
    for flip, piece in enumerate(refs[:-1]):
        first = pl.multiple_of((lax.axis_index("col") ^ flip) * span, LANES)
        out[:, pl.ds(first, span)] = piece[...]


def collect(held):
    share, span = held[0].shape
    if span % LANES:
        me = lax.axis_index("col")
        stacked = jnp.stack(held)
        return jnp.concatenate(
            [lax.dynamic_index_in_dim(stacked, me ^ j, 0, keepdims=False) for j in range(len(held))],
            axis=1,
        )
    return pl.pallas_call(
        collect_kernel,
        out_shape=jax.ShapeDtypeStruct((share, span * len(held)), jnp.float32),
        in_specs=[WHOLE] * len(held),
        out_specs=WHOLE,
        cost_estimate=LIGHT,
    )(*held)


def pair_rows(masked):
    groups_row = lax.axis_size("row")
    groups_col = lax.axis_size("col")
    cross = []
    for r in range(groups_row):
        for c in range(groups_col):
            odd = (r ^ c) & 1
            cross.append((r * groups_col + c, (r ^ odd) * groups_col + (c ^ odd)))
    held = lax.ppermute(masked, ("row", "col"), cross)
    held = [held] + [flipped(held, "col", flip) for flip in range(2, groups_col, 2)]
    return held + [flipped(piece, "col", 1) for piece in held]


def local(inverse_set, presence, factor, dinv):
    groups_row = lax.axis_size("row")
    groups_col = lax.axis_size("col")
    col_index = lax.axis_index("col")
    block_rows, _, order, width = factor.shape
    block_cols = inverse_set.shape[3]
    span = width // groups_col
    rows = block_rows * order
    share = order // groups_col

    own = factor.reshape(rows, width)
    blocks = inverse_set.reshape(rows * block_cols, order)
    masked, copies = prepare(presence.reshape(-1), blocks, own, groups_row // 2, span)
    lines = [list(range(bit, groups_row, 2)) for bit in range(2)]
    columns = lax.all_to_all(copies, "row", 0, 0, axis_index_groups=lines)
    columns = columns.reshape(groups_row // 2, block_rows, order, span).transpose(1, 0, 2, 3)
    columns = columns.reshape(-1, order, span)
    pieces = pair_rows(masked)
    near = flipped(own, "row", 1)

    terms, kept, sent = middle(pieces, columns, own, near)
    terms = lax.all_to_all(terms.reshape(groups_row, width // groups_row, span), "row", 0, 0)
    diag_block = dinv + terms.sum(axis=0)

    update = (kept + flipped(sent, "row", 1)).reshape(block_rows, groups_col, share, span)
    held = []
    for flip in range(groups_col):
        piece = lax.dynamic_index_in_dim(update, col_index ^ flip, 1, keepdims=False)
        piece = piece.reshape(block_rows * share, span)
        held.append(flipped(piece, "col", flip) if flip else piece)
    off_diag = collect(held).reshape(block_rows, 1, share, width)
    return (off_diag, diag_block)


def solution(mesh):
    in_specs = (
        P(None, "row", None, None, "col", None),
        P(None, "row", None, "col"),
        P(None, "row", None, None),
        P("row", "col"),
    )
    out_specs = (P(None, "row", "col", None), P("row", "col"))
    return jax.shard_map(local, mesh=mesh, in_specs=in_specs, out_specs=out_specs, check_vma=False)
```

time: 60.5 us -> 50.4 us (0.83)
  waiting for transfers between devices: 34 us -> 12 us
  Pallas kernels: 0 us -> 13.6 us
  starting transfers between devices: 17.6 us -> 21.1 us
  matrix products: 2.05 us -> 0 us
  other arithmetic: 2.35 us -> 0.65 us
  local copies, waits for them, and re-layouts: 3.34 us -> 1.96 us
    all_to_all x4 -> x2, waiting for transfers between devices: 34 us -> 0.15 us  [the longest x1 0.15 us: local(): columns = lax.all_to_all(copies, 'row', 0, 0, axis_index_groups=lines)]
    pallas_call x0 -> x3, Pallas kernels: none -> 13.6 us  [the longest x1 10.6 us: prepare(): pl.pallas_call(prepare_kernel, out_shape=(jax.ShapeDtypeStruct((block_col...]
    ppermute x0 -> x9, waiting for transfers between devices: none -> 11.9 us  [the longest x8 11.9 us: flipped(): lax.ppermute(value, axis, [(i, i ^ flip) for i in range(lax.axis_size(axi...]
    ppermute x0 -> x9, starting transfers between devices: none -> 8.85 us  [the longest x8 7.29 us: flipped(): lax.ppermute(value, axis, [(i, i ^ flip) for i in range(lax.axis_size(axi...]
    all_to_all x4 -> x2, starting transfers between devices: 17.6 us -> 12.2 us  [the longest x1 6.45 us: local(): columns = lax.all_to_all(copies, 'row', 0, 0, axis_index_groups=lines)]
    dot_general x2 -> x0, matrix products: 2.05 us -> none  [the longest x1 1.63 us: local(): update = jnp.dot(wide, columns, precision=HI)]
    mul x2 -> x0, other arithmetic: 1.71 us -> none  [local(): inverse_set[:, 0, :, :, 0, :]]
    broadcast_in_dim x3 -> x0, local copies, waits for them, and re-layouts: 1.69 us -> none  [to_all(): copies = jnp.broadcast_to(value[None], (lax.axis_size(axis),) + value.shape)]
  transfers between devices with their start and end apart: 4 -> 11, of which waited for: 4 -> 6; matrix products, arithmetic and copies ran while one was open for 3% -> 1% of each run, Pallas kernels for 0% -> 3%
where the time goes in v5:
time: 50.4 us; the launch traced here: 49.9 us
  starting transfers between devices  21.1 us (42%)
  Pallas kernels  13.6 us (27%)
  waiting for transfers between devices  12 us (24%)
  local copies, waits for them, and re-layouts  1.96 us (4%)
  between operations  0.66 us (1%)
  other arithmetic  0.65 us (1%)
    ppermute x8, waiting for transfers between devices, flipped(): lax.ppermute(value, axis, [(i, i ^ flip) for i in range(lax.axis_size(axi...  11.9 us
    pallas_call x1, Pallas kernels, prepare(): pl.pallas_call(prepare_kernel, out_shape=(jax.ShapeDtypeStruct((block_col...  10.6 us
    ppermute x8, starting transfers between devices, flipped(): lax.ppermute(value, axis, [(i, i ^ flip) for i in range(lax.axis_size(axi...  7.29 us
    all_to_all x1, starting transfers between devices, local(): columns = lax.all_to_all(copies, 'row', 0, 0, axis_index_groups=lines)  6.45 us
    all_to_all x1, starting transfers between devices, local(): lax.all_to_all(terms.reshape(groups_row, width // groups_row, span), 'row...  5.78 us
    ppermute x1, starting transfers between devices, pair_rows(): held = lax.ppermute(masked, ('row', 'col'), cross)  1.56 us
    pallas_call x1, Pallas kernels, middle(): pl.pallas_call(functools.partial(middle_kernel, len(pieces) // 2), out_sh...  1.54 us
    pallas_call x1, Pallas kernels, collect(): pl.pallas_call(collect_kernel, out_shape=jax.ShapeDtypeStruct((share, spa...  1.4 us
  transfers between devices with their start and end apart: 11, of which 6 were waited for; matrix products, arithmetic and copies ran while one was open for 1% of the time, Pallas kernels for 3%

profile of v5, /device:TPU:0, one launch (start us, length us, event | category | flops | bytes accessed | tf_op | source)
XLA Modules:
  0.0 49.9 jit_solution(4791527287295626360)
XLA Ops:
  0.6 10.6 %shard_map.59 = (f32[2,128,128]{2,1,0:T(8,128)}, f32[4,128,128]{2,1,0:T(8,128)}) custom-call(s32[2]{0:T(128)} %bitcast.20, f32[256,128]{1,0:T(8,128)} %bitcast.18, f32[128,512]{1,0:T(8,128)} %bitcast.14), custom_call_target="tpu_custom_call" | custom-call | flops 1000 | bytes 1000 | tf_op jit(solution)/shard_map/pallas_call | solution.py:65
  11.3 1.6 %collective-permute-start = (f32[2,128,128]{2,1,0:T(8,128)}, f32[2,128,128]{2,1,0:T(8,128)S(1)}, u32[]{:S(2)}, u32[]{:S(2)}) collective-permute-start(f32[2,128,128]{2,1,0:T(8,128)} %get-tuple-element.7), channel_id=1, source_target_pairs={{0,0},{1,4},{2,2},{3,6},{4,1},{5,5},{6,3},{7,7},{8,8},{9,12},{10,1... | collective-permute-start | bytes 393224 | tf_op jit(solution)/shard_map/ppermute | solution.py:147
  12.8 6.4 %all-to-all-start = ((f32[4,128,128]{2,1,0:T(8,128)}), f32[4,128,128]{2,1,0:T(8,128)S(1)}, u32[]{:S(2)}, u32[]{:S(2)}) async-start(f32[4,128,128]{2,1,0:T(8,128)} %get-tuple-element.8), calls=%async_computation | async-start | bytes 524288 | tf_op jit(solution)/shard_map/all_to_all | solution.py:166
  19.3 1.9 %collective-permute-start.4 = (f32[128,512]{1,0:T(8,128)S(1)}, f32[128,512]{1,0:T(8,128)S(1)}, u32[]{:S(2)}, u32[]{:S(2)}) collective-permute-start(f32[128,512]{1,0:T(8,128)S(1)} %bitcast.15), channel_id=1, source_target_pairs={{0,4},{4,0},{8,12},{12,8},{16,20},{20,16},{24,28},{28,24},{1,5},{5... | collective-permute-start | bytes 786440 | tf_op jit(solution)/shard_map/ppermute | solution.py:16
  21.2 1.5 %collective-permute-start.1 = (f32[2,128,128]{2,1,0:T(8,128)S(1)}, f32[2,128,128]{2,1,0:T(8,128)S(1)}, u32[]{:S(2)}, u32[]{:S(2)}) collective-permute-start(f32[2,128,128]{2,1,0:T(8,128)S(1)} %collective-permute-done.refs_0_), channel_id=1, source_target_pairs={{0,2},{1,3},{2,0},{3,1},{4,6},{5,7},{6,4},{7,5},{8,10},{9,11},{10,... | collective-permute-start | bytes 393224 | tf_op jit(solution)/shard_map/ppermute | solution.py:16
  22.7 0.0 collective-permute-start.2
  22.7 3.8 %collective-permute-done.1.refs_1_ = f32[2,128,128]{2,1,0:T(8,128)S(1)} collective-permute-done((f32[2,128,128]{2,1,0:T(8,128)S(1)}, f32[2,128,128]{2,1,0:T(8,128)S(1)}, u32[]{:S(2)}, u32[]{:S(2)}) %collective-permute-start.1) | collective-permute-done | bytes 131104 | tf_op jit(solution)/shard_map/ppermute | solution.py:16
  26.5 1.3 %collective-permute-done.4.refs_6_ = f32[128,512]{1,0:T(8,128)S(1)} collective-permute-done((f32[128,512]{1,0:T(8,128)S(1)}, f32[128,512]{1,0:T(8,128)S(1)}, u32[]{:S(2)}, u32[]{:S(2)}) %collective-permute-start.4) | collective-permute-done | bytes 262176 | tf_op jit(solution)/shard_map/ppermute | solution.py:16
  27.8 0.0 collective-permute-done.3.refs_3_
  27.8 0.1 all-to-all-done.refs_4_
  28.0 1.5 %shard_map.60 = (f32[512,128]{1,0:T(8,128)}, f32[128,128]{1,0:T(8,128)S(1)}, f32[128,128]{1,0:T(8,128)S(1)}) custom-call(f32[2,128,128]{2,1,0:T(8,128)S(1)} %collective-permute-done.refs_0_, f32[2,128,128]{2,1,0:T(8,128)S(1)} %collective-permute-done.1.refs_1_, f32[2,128,128]{2,1,0:T(8,128)S(1)} %collective-permute-done.2.refs_2_, ...), custom_call_target="tpu_custom_call" | custom-call | flops 1000 | bytes 1000 | tf_op jit(solution)/shard_map/pallas_call | solution.py:103
  29.5 5.8 %all-to-all-start.1 = ((f32[8,64,128]{2,1,0:T(8,128)}), f32[8,64,128]{2,1,0:T(8,128)S(1)}, u32[]{:S(2)}, u32[]{:S(2)}) async-start(f32[8,64,128]{2,1,0:T(8,128)} %bitcast.9), calls=%async_computation.1 | async-start | bytes 524288 | tf_op jit(solution)/shard_map/all_to_all | solution.py:173
  35.3 2.0 %collective-permute-start.5 = (f32[128,128]{1,0:T(8,128)S(1)}, f32[128,128]{1,0:T(8,128)S(1)}, u32[]{:S(2)}, u32[]{:S(2)}) collective-permute-start(f32[128,128]{1,0:T(8,128)S(1)} %get-tuple-element.10), channel_id=1, source_target_pairs={{0,4},{4,0},{8,12},{12,8},{16,20},{20,16},{24,28},{28,24},{1,5},{5... | collective-permute-start | bytes 196616 | tf_op jit(solution)/shard_map/ppermute | solution.py:16
  37.3 3.9 %collective-permute-done.5 = f32[128,128]{1,0:T(8,128)S(1)} collective-permute-done((f32[128,128]{1,0:T(8,128)S(1)}, f32[128,128]{1,0:T(8,128)S(1)}, u32[]{:S(2)}, u32[]{:S(2)}) %collective-permute-start.5) | collective-permute-done | bytes 65568 | tf_op jit(solution)/shard_map/ppermute | solution.py:16
  41.2 0.6 %dynamic-slice_bitcast_fusion = (f32[32,128]{1,0:T(8,128)S(1)}, f32[32,128]{1,0:T(8,128)S(1)}, f32[32,128]{1,0:T(8,128)S(1)}, f32[32,128]{1,0:T(8,128)}) fusion(f32[1,4,32,128]{3,2,1,0:T(8,128)S(1)} %bitcast.17, s32[]{:T(128)S(6)} %select_n.16, s32[]{:T(128)S(6)} %select_n.15, s32[]{:T(128)S(6)} %select_n.14, s32[]{:T(128)S(6)} %select_n.13), kind=kLoop, calls=%fused_computation | loop fusion | bytes 131088 | tf_op jit(solution)/shard_map/reshape | solution.py:180
  41.9 1.5 %collective-permute-start.7 = (f32[32,128]{1,0:T(8,128)S(1)}, f32[32,128]{1,0:T(8,128)S(1)}, u32[]{:S(2)}, u32[]{:S(2)}) collective-permute-start(f32[32,128]{1,0:T(8,128)S(1)} %get-tuple-element.13), channel_id=1, source_target_pairs={{0,2},{1,3},{2,0},{3,1},{4,6},{5,7},{6,4},{7,5},{8,10},{9,11},{10,... | collective-permute-start | bytes 49160 | tf_op jit(solution)/shard_map/ppermute | solution.py:16
  43.4 0.3 collective-permute-start.8
  43.7 1.9 %collective-permute-done.7.refs_2_ = f32[32,128]{1,0:T(8,128)S(1)} collective-permute-done((f32[32,128]{1,0:T(8,128)S(1)}, f32[32,128]{1,0:T(8,128)S(1)}, u32[]{:S(2)}, u32[]{:S(2)}) %collective-permute-start.7) | collective-permute-done | bytes 16416 | tf_op jit(solution)/shard_map/ppermute | solution.py:16
  45.6 0.9 %collective-permute-done.8.refs_3_ = f32[32,128]{1,0:T(8,128)S(1)} collective-permute-done((f32[32,128]{1,0:T(8,128)S(1)}, f32[32,128]{1,0:T(8,128)S(1)}, u32[]{:S(2)}, u32[]{:S(2)}) %collective-permute-start.8) | collective-permute-done | bytes 16416 | tf_op jit(solution)/shard_map/ppermute | solution.py:16
  46.6 0.6 %copy-done.4 = f32[32,128]{1,0:T(8,128)} copy-done((f32[32,128]{1,0:T(8,128)}, f32[32,128]{1,0:T(8,128)S(1)}, u32[]{:S(2)}) %copy-start.4) | copy-done | bytes 16408
  47.1 1.4 %shard_map.61 = f32[32,512]{1,0:T(8,128)} custom-call(f32[32,128]{1,0:T(8,128)} %get-tuple-element.15.refs_0_, f32[32,128]{1,0:T(8,128)} %copy-done.2, f32[32,128]{1,0:T(8,128)} %copy-done.3, f32[32,128]{1,0:T(8,128)} %copy-done.4), custom_call_target="tpu_custom_call" | custom-call | flops 1000 | bytes 1000 | tf_op jit(solution)/shard_map/pallas_call | solution.py:130
  48.6 0.0 all-to-all-done.1
  48.6 0.7 %copy-done.1 = f32[64,128]{1,0:T(8,128)S(1)} copy-done((f32[64,128]{1,0:T(8,128)S(1)}, f32[64,128]{1,0:T(8,128)}, u32[]{:S(2)}) %copy-start.1) | copy-done | bytes 32792
  49.3 0.6 %add.24 = f32[64,128]{1,0:T(8,128)} add(f32[64,128]{1,0:T(8,128)S(1)} %copy-done.1, f32[64,128]{1,0:T(8,128)S(1)} %reduce_sum.9) | non-fusion elementwise | flops 8192 | bytes 98304 | tf_op jit(solution)/shard_map/add | solution.py:174
  (15 shorter events, 0.1 us)
Async XLA Ops:
  11.3 9.9 %collective-permute-start = (f32[2,128,128]{2,1,0:T(8,128)}, f32[2,128,128]{2,1,0:T(8,128)S(1)}, u32[]{:S(2)}, u32[]{:S(2)}) collective-permute-start(f32[2,128,128]{2,1,0:T(8,128)} %get-tuple-element.7), channel_id=1, source_target_pairs={{0,0},{1,4},{2,2},{3,6},{4,1},{5,5},{6,3},{7,7},{8,8},{9,12},{10,1... | collective-permute-start | bytes 393224 | tf_op jit(solution)/shard_map/ppermute | solution.py:147
  12.8 6.5 %copy-start = (f32[1,1,128,512]{3,2,1,0:T(8,128)S(1)}, f32[1,1,128,512]{3,2,1,0:T(8,128)}, u32[]{:S(2)}) copy-start(f32[1,1,128,512]{3,2,1,0:T(8,128)} %param.6) | copy-start | bytes 786436
  12.8 15.1 %all-to-all-start = ((f32[4,128,128]{2,1,0:T(8,128)}), f32[4,128,128]{2,1,0:T(8,128)S(1)}, u32[]{:S(2)}, u32[]{:S(2)}) async-start(f32[4,128,128]{2,1,0:T(8,128)} %get-tuple-element.8), calls=%async_computation | async-start | bytes 524288 | tf_op jit(solution)/shard_map/all_to_all | solution.py:166
  19.3 8.5 %collective-permute-start.4 = (f32[128,512]{1,0:T(8,128)S(1)}, f32[128,512]{1,0:T(8,128)S(1)}, u32[]{:S(2)}, u32[]{:S(2)}) collective-permute-start(f32[128,512]{1,0:T(8,128)S(1)} %bitcast.15), channel_id=1, source_target_pairs={{0,4},{4,0},{8,12},{12,8},{16,20},{20,16},{24,28},{28,24},{1,5},{5... | collective-permute-start | bytes 786440 | tf_op jit(solution)/shard_map/ppermute | solution.py:16
  21.2 5.3 %collective-permute-start.1 = (f32[2,128,128]{2,1,0:T(8,128)S(1)}, f32[2,128,128]{2,1,0:T(8,128)S(1)}, u32[]{:S(2)}, u32[]{:S(2)}) collective-permute-start(f32[2,128,128]{2,1,0:T(8,128)S(1)} %collective-permute-done.refs_0_), channel_id=1, source_target_pairs={{0,2},{1,3},{2,0},{3,1},{4,6},{5,7},{6,4},{7,5},{8,10},{9,11},{10,... | collective-permute-start | bytes 393224 | tf_op jit(solution)/shard_map/ppermute | solution.py:16
  22.7 3.8 %collective-permute-start.2 = (f32[2,128,128]{2,1,0:T(8,128)S(1)}, f32[2,128,128]{2,1,0:T(8,128)S(1)}, u32[]{:S(2)}, u32[]{:S(2)}) collective-permute-start(f32[2,128,128]{2,1,0:T(8,128)S(1)} %collective-permute-done.refs_0_), channel_id=1, source_target_pairs={{0,1},{1,0},{2,3},{3,2},{4,5},{5,4},{6,7},{7,6},{8,9},{9,8},{10,11... | collective-permute-start | bytes 393224 | tf_op jit(solution)/shard_map/ppermute | solution.py:16
  26.5 1.3 %collective-permute-start.3 = (f32[2,128,128]{2,1,0:T(8,128)S(1)}, f32[2,128,128]{2,1,0:T(8,128)S(1)}, u32[]{:S(2)}, u32[]{:S(2)}) collective-permute-start(f32[2,128,128]{2,1,0:T(8,128)S(1)} %collective-permute-done.1.refs_1_), channel_id=1, source_target_pairs={{0,1},{1,0},{2,3},{3,2},{4,5},{5,4},{6,7},{7,6},{8,9},{9,8},{10,11... | collective-permute-start | bytes 393224 | tf_op jit(solution)/shard_map/ppermute | solution.py:16
  29.5 19.0 %all-to-all-start.1 = ((f32[8,64,128]{2,1,0:T(8,128)}), f32[8,64,128]{2,1,0:T(8,128)S(1)}, u32[]{:S(2)}, u32[]{:S(2)}) async-start(f32[8,64,128]{2,1,0:T(8,128)} %bitcast.9), calls=%async_computation.1 | async-start | bytes 524288 | tf_op jit(solution)/shard_map/all_to_all | solution.py:173
  35.3 5.9 %collective-permute-start.5 = (f32[128,128]{1,0:T(8,128)S(1)}, f32[128,128]{1,0:T(8,128)S(1)}, u32[]{:S(2)}, u32[]{:S(2)}) collective-permute-start(f32[128,128]{1,0:T(8,128)S(1)} %get-tuple-element.10), channel_id=1, source_target_pairs={{0,4},{4,0},{8,12},{12,8},{16,20},{20,16},{24,28},{28,24},{1,5},{5... | collective-permute-start | bytes 196616 | tf_op jit(solution)/shard_map/ppermute | solution.py:16
  41.9 1.9 %collective-permute-start.6 = (f32[32,128]{1,0:T(8,128)S(1)}, f32[32,128]{1,0:T(8,128)S(1)}, u32[]{:S(2)}, u32[]{:S(2)}) collective-permute-start(f32[32,128]{1,0:T(8,128)S(1)} %get-tuple-element.14), channel_id=1, source_target_pairs={{0,1},{1,0},{2,3},{3,2},{4,5},{5,4},{6,7},{7,6},{8,9},{9,8},{10,11... | collective-permute-start | bytes 49160 | tf_op jit(solution)/shard_map/ppermute | solution.py:16
  41.9 3.7 %collective-permute-start.7 = (f32[32,128]{1,0:T(8,128)S(1)}, f32[32,128]{1,0:T(8,128)S(1)}, u32[]{:S(2)}, u32[]{:S(2)}) collective-permute-start(f32[32,128]{1,0:T(8,128)S(1)} %get-tuple-element.13), channel_id=1, source_target_pairs={{0,2},{1,3},{2,0},{3,1},{4,6},{5,7},{6,4},{7,5},{8,10},{9,11},{10,... | collective-permute-start | bytes 49160 | tf_op jit(solution)/shard_map/ppermute | solution.py:16
  43.4 3.2 %collective-permute-start.8 = (f32[32,128]{1,0:T(8,128)S(1)}, f32[32,128]{1,0:T(8,128)S(1)}, u32[]{:S(2)}, u32[]{:S(2)}) collective-permute-start(f32[32,128]{1,0:T(8,128)S(1)} %get-tuple-element.12), channel_id=1, source_target_pairs={{0,3},{1,2},{2,1},{3,0},{4,7},{5,6},{6,5},{7,4},{8,11},{9,10},{10,... | collective-permute-start | bytes 49160 | tf_op jit(solution)/shard_map/ppermute | solution.py:16
  43.7 2.8 %copy-start.2 = (f32[32,128]{1,0:T(8,128)}, f32[32,128]{1,0:T(8,128)S(1)}, u32[]{:S(2)}) copy-start(f32[32,128]{1,0:T(8,128)S(1)} %collective-permute-done.6.refs_1_) | copy-start | bytes 49156
  45.6 1.0 %copy-start.3 = (f32[32,128]{1,0:T(8,128)}, f32[32,128]{1,0:T(8,128)S(1)}, u32[]{:S(2)}) copy-start(f32[32,128]{1,0:T(8,128)S(1)} %collective-permute-done.7.refs_2_) | copy-start | bytes 49156
  46.5 0.6 %copy-start.4 = (f32[32,128]{1,0:T(8,128)}, f32[32,128]{1,0:T(8,128)S(1)}, u32[]{:S(2)}) copy-start(f32[32,128]{1,0:T(8,128)S(1)} %collective-permute-done.8.refs_3_) | copy-start | bytes 49156
  48.6 0.8 %copy-start.1 = (f32[64,128]{1,0:T(8,128)S(1)}, f32[64,128]{1,0:T(8,128)}, u32[]{:S(2)}) copy-start(f32[64,128]{1,0:T(8,128)} %param.7) | copy-start | bytes 98308

commit v6 on v5

--- a/solution.py
+++ b/solution.py
@@ -31,24 +31,18 @@
     return once(left_high, right_high) + (once(left_high, right_low) + once(left_low, right_high))
 
 
-def prepare_kernel(presence, blocks, factor, masked, copies, sems):
+def prepare_kernel(presence, blocks, factor, masked, copies):
     count, rows, span = copies.shape
     first = pl.multiple_of(lax.axis_index("col") * span, LANES)
-    sends = [
-        pltpu.make_async_copy(factor.at[:, pl.ds(first, span)], copies.at[i], sems.at[i])
-        for i in range(count)
-    ]
-    for send in sends:
-        send.start()
+    mine = factor[:, pl.ds(first, span)]
+    for i in range(count):
+        copies[i] = mine
     block_cols, _, order = masked.shape
-    block_rows = rows // order
-    for a in range(block_rows):
+    for a in range(rows // order):
         for b in range(block_cols):
             weight = presence[a * block_cols + b].astype(jnp.float32)
             picked = blocks[pl.ds(a * order * block_cols + b, order, stride=block_cols), :]
             masked[b, pl.ds(a * order, order), :] = picked * weight
-    for send in sends:
-        send.wait()
 
 
 def prepare(presence, blocks, own, receivers, span):
@@ -68,18 +62,19 @@
             jax.ShapeDtypeStruct((block_cols, rows, order), jnp.float32),
             jax.ShapeDtypeStruct((receivers, rows, span), jnp.float32),
         ),
-        in_specs=[pl.BlockSpec(memory_space=pltpu.SMEM), WHOLE, pl.BlockSpec(memory_space=pl.ANY)],
-        out_specs=(WHOLE, pl.BlockSpec(memory_space=pl.ANY)),
-        scratch_shapes=[pltpu.SemaphoreType.DMA((receivers,))],
+        in_specs=[pl.BlockSpec(memory_space=pltpu.SMEM), WHOLE, WHOLE],
+        out_specs=(WHOLE, WHOLE),
         cost_estimate=LIGHT,
     )(presence, blocks, own)
 
 
 def middle_kernel(count, *refs):
     pieces = refs[: 2 * count]
-    columns, own, near, terms, kept, sent = refs[2 * count :]
-    block_cols, rows, _ = pieces[0].shape
+    columns, own, near, dinv, terms = refs[2 * count : 2 * count + 5]
+    outward = refs[2 * count + 5 :]
+    block_cols, rows, order = pieces[0].shape
     col_index = lax.axis_index("col")
+    row_index = lax.axis_index("row")
     left, right = [], []
     for t in range(count):
         for b in range(block_cols):
@@ -87,53 +82,61 @@
             right.append(columns[b * count + ((col_index >> 1) ^ t)])
     both = product(jnp.concatenate(left, axis=1), jnp.concatenate(right, axis=0), ((1,), (0,)))
     first, second = both[:rows], both[rows:]
-    same = (lax.axis_index("row") & 1) == (col_index & 1)
+    same = (row_index & 1) == (col_index & 1)
     mine = jnp.where(same, first, second)
     other = jnp.where(same, second, first)
-    kept[...] = -mine
-    sent[...] = -other
     factors = jnp.concatenate([own[...], near[...]], axis=0)
     terms[...] = product(factors, jnp.concatenate([mine, other], axis=0), ((0,), (0,)))
+    tall = dinv.shape[0]
+    here = pl.ds(pl.multiple_of(row_index * tall, 8), tall)
+    terms[here, :] = terms[here, :] + dinv[...]
+
+    scratch = outward[-1]
+    flips = len(outward[:-1]) // 2
+    share = order // flips
+    for near_row, value in enumerate((mine, other)):
+        scratch[...] = -value
+        for flip in range(flips):
+            start = (col_index ^ flip) * share
+            for a in range(rows // order):
+                picked = scratch[pl.ds(pl.multiple_of(a * order + start, 8), share), :]
+                outward[near_row * flips + flip][pl.ds(a * share, share), :] = picked
 
 
-def middle(pieces, columns, own, near):
+def middle(pieces, columns, own, near, dinv, flips):
     rows, width = own.shape
     span = columns.shape[2]
-    part = jax.ShapeDtypeStruct((rows, span), jnp.float32)
+    part = jax.ShapeDtypeStruct((rows // flips, span), jnp.float32)
     return pl.pallas_call(
         functools.partial(middle_kernel, len(pieces) // 2),
-        out_shape=(jax.ShapeDtypeStruct((width, span), jnp.float32), part, part),
-        in_specs=[WHOLE] * (len(pieces) + 3),
-        out_specs=(WHOLE,) * 3,
+        out_shape=(jax.ShapeDtypeStruct((width, span), jnp.float32),) + (part,) * (2 * flips),
+        in_specs=[WHOLE] * (len(pieces) + 4),
+        out_specs=(WHOLE,) * (1 + 2 * flips),
+        scratch_shapes=[pltpu.VMEM((rows, span), jnp.float32)],
         cost_estimate=LIGHT,
         compiler_params=pltpu.CompilerParams(vmem_limit_bytes=32 * 1024 * 1024),
-    )(*pieces, columns, own, near)
+    )(*pieces, columns, own, near, dinv)
 
 
-def collect_kernel(*refs):
-    out = refs[-1]
-    span = refs[0].shape[1]
-    for flip, piece in enumerate(refs[:-1]):
-        first = pl.multiple_of((lax.axis_index("col") ^ flip) * span, LANES)
-        out[:, pl.ds(first, span)] = piece[...]
+def exchange(outward, flips):
+    groups_row = lax.axis_size("row")
+    groups_col = lax.axis_size("col")
+    arrived = []
+    for index, piece in enumerate(outward):
+        near_row, flip = divmod(index, flips)
+        pairs = [
+            (r * groups_col + c, (r ^ near_row) * groups_col + (c ^ flip))
+            for r in range(groups_row)
+            for c in range(groups_col)
+        ]
+        arrived.append(lax.ppermute(piece, ("row", "col"), pairs) if index else piece)
+    return [arrived[flip] + arrived[flips + flip] for flip in range(flips)]
 
 
-def collect(held):
-    share, span = held[0].shape
-    if span % LANES:
-        me = lax.axis_index("col")
-        stacked = jnp.stack(held)
-        return jnp.concatenate(
-            [lax.dynamic_index_in_dim(stacked, me ^ j, 0, keepdims=False) for j in range(len(held))],
-            axis=1,
-        )
-    return pl.pallas_call(
-        collect_kernel,
-        out_shape=jax.ShapeDtypeStruct((share, span * len(held)), jnp.float32),
-        in_specs=[WHOLE] * len(held),
-        out_specs=WHOLE,
-        cost_estimate=LIGHT,
-    )(*held)
+def side_by_side(held):
+    me = lax.axis_index("col")
+    size = len(held)
+    return jnp.concatenate([lax.select_n(me ^ j, *held) for j in range(size)], axis=1)
 
 
 def pair_rows(masked):
@@ -152,7 +155,6 @@
 def local(inverse_set, presence, factor, dinv):
     groups_row = lax.axis_size("row")
     groups_col = lax.axis_size("col")
-    col_index = lax.axis_index("col")
     block_rows, _, order, width = factor.shape
     block_cols = inverse_set.shape[3]
     span = width // groups_col
@@ -169,18 +171,12 @@
     pieces = pair_rows(masked)
     near = flipped(own, "row", 1)
 
-    terms, kept, sent = middle(pieces, columns, own, near)
+    terms, *outward = middle(pieces, columns, own, near, dinv, groups_col)
     terms = lax.all_to_all(terms.reshape(groups_row, width // groups_row, span), "row", 0, 0)
-    diag_block = dinv + terms.sum(axis=0)
+    diag_block = terms.sum(axis=0)
 
-    update = (kept + flipped(sent, "row", 1)).reshape(block_rows, groups_col, share, span)
-    held = []
-    for flip in range(groups_col):
-        piece = lax.dynamic_index_in_dim(update, col_index ^ flip, 1, keepdims=False)
-        piece = piece.reshape(block_rows * share, span)
-        held.append(flipped(piece, "col", flip) if flip else piece)
-    off_diag = collect(held).reshape(block_rows, 1, share, width)
-    return (off_diag, diag_block)
+    off_diag = side_by_side(exchange(outward, groups_col))
+    return (off_diag.reshape(block_rows, 1, share, width), diag_block)
 
 
 def solution(mesh):

time: 50.4 us -> 42.8 us (0.85)
  Pallas kernels: 13.6 us -> 3.32 us
  starting transfers between devices: 21.1 us -> 23.9 us
  local copies, waits for them, and re-layouts: 1.96 us -> 0.01 us
  waiting for transfers between devices: 12 us -> 13.2 us
  other arithmetic: 0.65 us -> 1.3 us
    pallas_call x1, Pallas kernels: 10.6 us -> 1.79 us  [prepare(): pl.pallas_call(prepare_kernel, out_shape=(jax.ShapeDtypeStruct((block_col...]
    all_to_all x1, waiting for transfers between devices: 0.01 us -> 7.86 us  [local(): lax.all_to_all(terms.reshape(groups_row, width // groups_row, span), 'row...]
    ppermute x0 -> x7, starting transfers between devices: none -> 7.54 us  [exchange(): lax.ppermute(piece, ('row', 'col'), pairs)]
    ppermute x8 -> x4, waiting for transfers between devices: 11.9 us -> 5.12 us  [flipped(): lax.ppermute(value, axis, [(i, i ^ flip) for i in range(lax.axis_size(axi...]
    ppermute x8 -> x4, starting transfers between devices: 7.29 us -> 3.41 us  [flipped(): lax.ppermute(value, axis, [(i, i ^ flip) for i in range(lax.axis_size(axi...]
    pallas_call x1 -> x0, Pallas kernels: 1.4 us -> none  [collect(): pl.pallas_call(collect_kernel, out_shape=jax.ShapeDtypeStruct((share, spa...]
    unnamed x10 -> x4, local copies, waits for them, and re-layouts: 1.34 us -> 0.01 us
    all_to_all x1, starting transfers between devices: 5.78 us -> 4.99 us  [local(): lax.all_to_all(terms.reshape(groups_row, width // groups_row, span), 'row...]
  transfers between devices with their start and end apart: 11 -> 14, of which waited for: 6 -> 6; matrix products, arithmetic and copies ran while one was open for 1% -> 2% of each run, Pallas kernels for 3% -> 0%
where the time goes in v6:
time: 42.8 us; the launch traced here: 42.5 us
  starting transfers between devices  23.9 us (56%)
  waiting for transfers between devices  13.2 us (31%)
  Pallas kernels  3.32 us (8%)
  other arithmetic  1.3 us (3%)
  between operations  0.7 us (2%)
    all_to_all x1, waiting for transfers between devices, local(): lax.all_to_all(terms.reshape(groups_row, width // groups_row, span), 'row...  7.86 us
    ppermute x7, starting transfers between devices, exchange(): lax.ppermute(piece, ('row', 'col'), pairs)  7.54 us
    all_to_all x1, starting transfers between devices, local(): columns = lax.all_to_all(copies, 'row', 0, 0, axis_index_groups=lines)  6.45 us
    ppermute x4, waiting for transfers between devices, flipped(): lax.ppermute(value, axis, [(i, i ^ flip) for i in range(lax.axis_size(axi...  5.12 us
    all_to_all x1, starting transfers between devices, local(): lax.all_to_all(terms.reshape(groups_row, width // groups_row, span), 'row...  4.99 us
    ppermute x4, starting transfers between devices, flipped(): lax.ppermute(value, axis, [(i, i ^ flip) for i in range(lax.axis_size(axi...  3.41 us
    pallas_call x1, Pallas kernels, prepare(): pl.pallas_call(prepare_kernel, out_shape=(jax.ShapeDtypeStruct((block_col...  1.79 us
    ppermute x1, starting transfers between devices, pair_rows(): held = lax.ppermute(masked, ('row', 'col'), cross)  1.55 us
  transfers between devices with their start and end apart: 14, of which 6 were waited for; matrix products, arithmetic and copies ran while one was open for 2% of the time, Pallas kernels for 0%

profile of v6, /device:TPU:0, one launch (start us, length us, event | category | flops | bytes accessed | tf_op | source)
XLA Modules:
  0.0 42.5 jit_solution(7374420458673942568)
XLA Ops:
  0.6 1.8 %shard_map.59 = (f32[2,128,128]{2,1,0:T(8,128)}, f32[4,128,128]{2,1,0:T(8,128)}) custom-call(s32[2]{0:T(128)} %bitcast.10, f32[256,128]{1,0:T(8,128)} %bitcast.9, f32[128,512]{1,0:T(8,128)} %bitcast.6), custom_call_target="tpu_custom_call" | custom-call | flops 1000 | bytes 1000 | tf_op jit(solution)/shard_map/pallas_call | solution.py:59
  2.4 1.6 %collective-permute-start = (f32[2,128,128]{2,1,0:T(8,128)}, f32[2,128,128]{2,1,0:T(8,128)S(1)}, u32[]{:S(2)}, u32[]{:S(2)}) collective-permute-start(f32[2,128,128]{2,1,0:T(8,128)} %get-tuple-element.13), channel_id=1, source_target_pairs={{0,0},{1,4},{2,2},{3,6},{4,1},{5,5},{6,3},{7,7},{8,8},{9,12},{10,1... | collective-permute-start | bytes 393224 | tf_op jit(solution)/shard_map/ppermute | solution.py:150
  4.0 6.4 %all-to-all-start = ((f32[4,128,128]{2,1,0:T(8,128)}), f32[4,128,128]{2,1,0:T(8,128)S(1)}, u32[]{:S(2)}, u32[]{:S(2)}) async-start(f32[4,128,128]{2,1,0:T(8,128)} %get-tuple-element.14), calls=%async_computation | async-start | bytes 524288 | tf_op jit(solution)/shard_map/all_to_all | solution.py:168
  10.4 1.9 %collective-permute-start.4 = (f32[128,512]{1,0:T(8,128)S(1)}, f32[128,512]{1,0:T(8,128)S(1)}, u32[]{:S(2)}, u32[]{:S(2)}) collective-permute-start(f32[128,512]{1,0:T(8,128)S(1)} %bitcast.7), channel_id=1, source_target_pairs={{0,4},{4,0},{8,12},{12,8},{16,20},{20,16},{24,28},{28,24},{1,5},{5... | collective-permute-start | bytes 786440 | tf_op jit(solution)/shard_map/ppermute | solution.py:16
  12.3 1.5 %collective-permute-start.1 = (f32[2,128,128]{2,1,0:T(8,128)S(1)}, f32[2,128,128]{2,1,0:T(8,128)S(1)}, u32[]{:S(2)}, u32[]{:S(2)}) collective-permute-start(f32[2,128,128]{2,1,0:T(8,128)S(1)} %collective-permute-done.refs_0_), channel_id=1, source_target_pairs={{0,2},{1,3},{2,0},{3,1},{4,6},{5,7},{6,4},{7,5},{8,10},{9,11},{10,... | collective-permute-start | bytes 393224 | tf_op jit(solution)/shard_map/ppermute | solution.py:16
  13.8 0.0 collective-permute-start.2
  13.8 3.8 %collective-permute-done.1.refs_1_ = f32[2,128,128]{2,1,0:T(8,128)S(1)} collective-permute-done((f32[2,128,128]{2,1,0:T(8,128)S(1)}, f32[2,128,128]{2,1,0:T(8,128)S(1)}, u32[]{:S(2)}, u32[]{:S(2)}) %collective-permute-start.1) | collective-permute-done | bytes 131104 | tf_op jit(solution)/shard_map/ppermute | solution.py:16
  17.6 1.3 %collective-permute-done.4.refs_6_ = f32[128,512]{1,0:T(8,128)S(1)} collective-permute-done((f32[128,512]{1,0:T(8,128)S(1)}, f32[128,512]{1,0:T(8,128)S(1)}, u32[]{:S(2)}, u32[]{:S(2)}) %collective-permute-start.4) | collective-permute-done | bytes 262176 | tf_op jit(solution)/shard_map/ppermute | solution.py:16
  18.9 0.1 collective-permute-done.3.refs_3_
  19.0 0.1 all-to-all-done.refs_4_
  19.1 1.5 %shard_map.60 = (f32[512,128]{1,0:T(8,128)}, f32[32,128]{1,0:T(8,128)S(1)}, f32[32,128]{1,0:T(8,128)S(1)}, f32[32,128]{1,0:T(8,128)S(1)}, f32[32,128]{1,0:T(8,12...) custom-call(f32[2,128,128]{2,1,0:T(8,128)S(1)} %collective-permute-done.r, ...), custom_call_target="tpu_custom_call" | custom-call | flops 1000 | bytes 1000 | tf_op jit(solution)/shard_map/pallas_call | solution.py:110
  20.6 2.6 %collective-permute-start.10 = (f32[32,128]{1,0:T(8,128)S(1)}, f32[32,128]{1,0:T(8,128)S(1)}, u32[]{:S(2)}, u32[]{:S(2)}) collective-permute-start(f32[32,128]{1,0:T(8,128)S(1)} %get-tuple-element.21), channel_id=1, source_target_pairs={{0,3},{1,2},{2,1},{3,0},{4,7},{5,6},{6,5},{7,4},{8,11},{9,10},{10,... | collective-permute-start | bytes 49160 | tf_op jit(solution)/shard_map/ppermute | solution.py:132
  23.2 0.3 collective-permute-start.11
  23.5 1.2 %collective-permute-start.5 = (f32[32,128]{1,0:T(8,128)S(1)}, f32[32,128]{1,0:T(8,128)S(1)}, u32[]{:S(2)}, u32[]{:S(2)}) collective-permute-start(f32[32,128]{1,0:T(8,128)S(1)} %get-tuple-element.16), channel_id=1, source_target_pairs={{0,4},{1,5},{2,6},{3,7},{4,0},{5,1},{6,2},{7,3},{8,12},{9,13},{10,... | collective-permute-start | bytes 49160 | tf_op jit(solution)/shard_map/ppermute | solution.py:132
  24.7 0.3 collective-permute-start.6
  25.0 0.6 %collective-permute-start.7 = (f32[32,128]{1,0:T(8,128)S(1)}, f32[32,128]{1,0:T(8,128)S(1)}, u32[]{:S(2)}, u32[]{:S(2)}) collective-permute-start(f32[32,128]{1,0:T(8,128)S(1)} %get-tuple-element.18), channel_id=1, source_target_pairs={{0,5},{1,4},{2,7},{3,6},{4,1},{5,0},{6,3},{7,2},{8,13},{9,12},{10,... | collective-permute-start | bytes 49160 | tf_op jit(solution)/shard_map/ppermute | solution.py:132
  25.6 0.0 collective-permute-done.10
  25.7 1.5 %collective-permute-start.8 = (f32[32,128]{1,0:T(8,128)S(1)}, f32[32,128]{1,0:T(8,128)S(1)}, u32[]{:S(2)}, u32[]{:S(2)}) collective-permute-start(f32[32,128]{1,0:T(8,128)S(1)} %get-tuple-element.19), channel_id=1, source_target_pairs={{0,2},{1,3},{2,0},{3,1},{4,6},{5,7},{6,4},{7,5},{8,10},{9,11},{10,... | collective-permute-start | bytes 49160 | tf_op jit(solution)/shard_map/ppermute | solution.py:132
  27.2 0.1 collective-permute-done.11
  27.3 1.0 %collective-permute-start.9 = (f32[32,128]{1,0:T(8,128)S(1)}, f32[32,128]{1,0:T(8,128)S(1)}, u32[]{:S(2)}, u32[]{:S(2)}) collective-permute-start(f32[32,128]{1,0:T(8,128)S(1)} %get-tuple-element.20), channel_id=1, source_target_pairs={{0,6},{1,7},{2,4},{3,5},{4,2},{5,3},{6,0},{7,1},{8,14},{9,15},{10,... | collective-permute-start | bytes 49160 | tf_op jit(solution)/shard_map/ppermute | solution.py:132
  28.3 5.0 %all-to-all-start.1 = ((f32[8,64,128]{2,1,0:T(8,128)}), f32[8,64,128]{2,1,0:T(8,128)S(1)}, u32[]{:S(2)}, u32[]{:S(2)}) async-start(f32[8,64,128]{2,1,0:T(8,128)} %bitcast.4), calls=%async_computation.1 | async-start | bytes 524288 | tf_op jit(solution)/shard_map/all_to_all | solution.py:175
  33.4 0.6 %maximum_bitcast_fusion = f32[1,1,32,512]{3,2,1,0:T(8,128)} fusion(f32[32,128]{1,0:T(8,128)S(1)} %get-tuple-element.31, f32[32,128]{1,0:T(8,128)S(1)} %get-tuple-element.30, f32[32,128]{1,0:T(8,128)S(1)} %get-tuple-element.29, f32[32,128]{1,0:T(8,128)S(1)} %get-tuple-element.24), kind=kLoop, calls=%fused_computation | loop fusion | flops 49152 | bytes 131072 | tf_op jit(solution)/shard_map/reshape | solution.py:179
  34.0 7.9 %all-to-all-done.1 = f32[8,64,128]{2,1,0:T(8,128)S(1)} async-done(((f32[8,64,128]{2,1,0:T(8,128)}), f32[8,64,128]{2,1,0:T(8,128)S(1)}, u32[]{:S(2)}, u32[]{:S(2)}) %all-to-all-start.1) | async-done | bytes 262176 | tf_op jit(solution)/shard_map/all_to_all | solution.py:175
  41.9 0.6 %reduce_sum.9 = f32[64,128]{1,0:T(8,128)} reduce(f32[8,64,128]{2,1,0:T(8,128)S(1)} %all-to-all-done.1, f32[]{:T(128)} %constant.4.clone.1), dimensions={0}, to_apply=%region_0.0 | reduce | flops 57344 | bytes 294916 | tf_op jit(solution)/shard_map/reduce_sum | solution.py:176
  (14 shorter events, 0.1 us)
Async XLA Ops:
  2.4 9.9 %collective-permute-start = (f32[2,128,128]{2,1,0:T(8,128)}, f32[2,128,128]{2,1,0:T(8,128)S(1)}, u32[]{:S(2)}, u32[]{:S(2)}) collective-permute-start(f32[2,128,128]{2,1,0:T(8,128)} %get-tuple-element.13), channel_id=1, source_target_pairs={{0,0},{1,4},{2,2},{3,6},{4,1},{5,5},{6,3},{7,7},{8,8},{9,12},{10,1... | collective-permute-start | bytes 393224 | tf_op jit(solution)/shard_map/ppermute | solution.py:150
  4.0 6.5 %copy-start = (f32[1,1,128,512]{3,2,1,0:T(8,128)S(1)}, f32[1,1,128,512]{3,2,1,0:T(8,128)}, u32[]{:S(2)}) copy-start(f32[1,1,128,512]{3,2,1,0:T(8,128)} %param.6) | copy-start | bytes 786436
  4.0 15.1 %copy-start.1 = (f32[64,128]{1,0:T(8,128)S(1)}, f32[64,128]{1,0:T(8,128)}, u32[]{:S(2)}) copy-start(f32[64,128]{1,0:T(8,128)} %refs_7_.1) | copy-start | bytes 98308
  4.0 15.1 %all-to-all-start = ((f32[4,128,128]{2,1,0:T(8,128)}), f32[4,128,128]{2,1,0:T(8,128)S(1)}, u32[]{:S(2)}, u32[]{:S(2)}) async-start(f32[4,128,128]{2,1,0:T(8,128)} %get-tuple-element.14), calls=%async_computation | async-start | bytes 524288 | tf_op jit(solution)/shard_map/all_to_all | solution.py:168
  10.4 8.5 %collective-permute-start.4 = (f32[128,512]{1,0:T(8,128)S(1)}, f32[128,512]{1,0:T(8,128)S(1)}, u32[]{:S(2)}, u32[]{:S(2)}) collective-permute-start(f32[128,512]{1,0:T(8,128)S(1)} %bitcast.7), channel_id=1, source_target_pairs={{0,4},{4,0},{8,12},{12,8},{16,20},{20,16},{24,28},{28,24},{1,5},{5... | collective-permute-start | bytes 786440 | tf_op jit(solution)/shard_map/ppermute | solution.py:16
  12.3 5.3 %collective-permute-start.1 = (f32[2,128,128]{2,1,0:T(8,128)S(1)}, f32[2,128,128]{2,1,0:T(8,128)S(1)}, u32[]{:S(2)}, u32[]{:S(2)}) collective-permute-start(f32[2,128,128]{2,1,0:T(8,128)S(1)} %collective-permute-done.refs_0_), channel_id=1, source_target_pairs={{0,2},{1,3},{2,0},{3,1},{4,6},{5,7},{6,4},{7,5},{8,10},{9,11},{10,... | collective-permute-start | bytes 393224 | tf_op jit(solution)/shard_map/ppermute | solution.py:16
  13.8 3.8 %collective-permute-start.2 = (f32[2,128,128]{2,1,0:T(8,128)S(1)}, f32[2,128,128]{2,1,0:T(8,128)S(1)}, u32[]{:S(2)}, u32[]{:S(2)}) collective-permute-start(f32[2,128,128]{2,1,0:T(8,128)S(1)} %collective-permute-done.refs_0_), channel_id=1, source_target_pairs={{0,1},{1,0},{2,3},{3,2},{4,5},{5,4},{6,7},{7,6},{8,9},{9,8},{10,11... | collective-permute-start | bytes 393224 | tf_op jit(solution)/shard_map/ppermute | solution.py:16
  17.6 1.3 %collective-permute-start.3 = (f32[2,128,128]{2,1,0:T(8,128)S(1)}, f32[2,128,128]{2,1,0:T(8,128)S(1)}, u32[]{:S(2)}, u32[]{:S(2)}) collective-permute-start(f32[2,128,128]{2,1,0:T(8,128)S(1)} %collective-permute-done.1.refs_1_), channel_id=1, source_target_pairs={{0,1},{1,0},{2,3},{3,2},{4,5},{5,4},{6,7},{7,6},{8,9},{9,8},{10,11... | collective-permute-start | bytes 393224 | tf_op jit(solution)/shard_map/ppermute | solution.py:16
  20.6 5.0 %collective-permute-start.10 = (f32[32,128]{1,0:T(8,128)S(1)}, f32[32,128]{1,0:T(8,128)S(1)}, u32[]{:S(2)}, u32[]{:S(2)}) collective-permute-start(f32[32,128]{1,0:T(8,128)S(1)} %get-tuple-element.21), channel_id=1, source_target_pairs={{0,3},{1,2},{2,1},{3,0},{4,7},{5,6},{6,5},{7,4},{8,11},{9,10},{10,... | collective-permute-start | bytes 49160 | tf_op jit(solution)/shard_map/ppermute | solution.py:132
  23.2 4.1 %collective-permute-start.11 = (f32[32,128]{1,0:T(8,128)S(1)}, f32[32,128]{1,0:T(8,128)S(1)}, u32[]{:S(2)}, u32[]{:S(2)}) collective-permute-start(f32[32,128]{1,0:T(8,128)S(1)} %get-tuple-element.22), channel_id=1, source_target_pairs={{0,7},{1,6},{2,5},{3,4},{4,3},{5,2},{6,1},{7,0},{8,15},{9,14},{10,... | collective-permute-start | bytes 49160 | tf_op jit(solution)/shard_map/ppermute | solution.py:132
  23.5 9.8 %collective-permute-start.5 = (f32[32,128]{1,0:T(8,128)S(1)}, f32[32,128]{1,0:T(8,128)S(1)}, u32[]{:S(2)}, u32[]{:S(2)}) collective-permute-start(f32[32,128]{1,0:T(8,128)S(1)} %get-tuple-element.16), channel_id=1, source_target_pairs={{0,4},{1,5},{2,6},{3,7},{4,0},{5,1},{6,2},{7,3},{8,12},{9,13},{10,... | collective-permute-start | bytes 49160 | tf_op jit(solution)/shard_map/ppermute | solution.py:132
  24.7 8.6 %collective-permute-start.6 = (f32[32,128]{1,0:T(8,128)S(1)}, f32[32,128]{1,0:T(8,128)S(1)}, u32[]{:S(2)}, u32[]{:S(2)}) collective-permute-start(f32[32,128]{1,0:T(8,128)S(1)} %get-tuple-element.17), channel_id=1, source_target_pairs={{0,1},{1,0},{2,3},{3,2},{4,5},{5,4},{6,7},{7,6},{8,9},{9,8},{10,11... | collective-permute-start | bytes 49160 | tf_op jit(solution)/shard_map/ppermute | solution.py:132
  25.0 8.3 %collective-permute-start.7 = (f32[32,128]{1,0:T(8,128)S(1)}, f32[32,128]{1,0:T(8,128)S(1)}, u32[]{:S(2)}, u32[]{:S(2)}) collective-permute-start(f32[32,128]{1,0:T(8,128)S(1)} %get-tuple-element.18), channel_id=1, source_target_pairs={{0,5},{1,4},{2,7},{3,6},{4,1},{5,0},{6,3},{7,2},{8,13},{9,12},{10,... | collective-permute-start | bytes 49160 | tf_op jit(solution)/shard_map/ppermute | solution.py:132
  25.7 7.6 %collective-permute-start.8 = (f32[32,128]{1,0:T(8,128)S(1)}, f32[32,128]{1,0:T(8,128)S(1)}, u32[]{:S(2)}, u32[]{:S(2)}) collective-permute-start(f32[32,128]{1,0:T(8,128)S(1)} %get-tuple-element.19), channel_id=1, source_target_pairs={{0,2},{1,3},{2,0},{3,1},{4,6},{5,7},{6,4},{7,5},{8,10},{9,11},{10,... | collective-permute-start | bytes 49160 | tf_op jit(solution)/shard_map/ppermute | solution.py:132
  27.3 6.0 %collective-permute-start.9 = (f32[32,128]{1,0:T(8,128)S(1)}, f32[32,128]{1,0:T(8,128)S(1)}, u32[]{:S(2)}, u32[]{:S(2)}) collective-permute-start(f32[32,128]{1,0:T(8,128)S(1)} %get-tuple-element.20), channel_id=1, source_target_pairs={{0,6},{1,7},{2,4},{3,5},{4,2},{5,3},{6,0},{7,1},{8,14},{9,15},{10,... | collective-permute-start | bytes 49160 | tf_op jit(solution)/shard_map/ppermute | solution.py:132
  28.3 13.6 %all-to-all-start.1 = ((f32[8,64,128]{2,1,0:T(8,128)}), f32[8,64,128]{2,1,0:T(8,128)S(1)}, u32[]{:S(2)}, u32[]{:S(2)}) async-start(f32[8,64,128]{2,1,0:T(8,128)} %bitcast.4), calls=%async_computation.1 | async-start | bytes 524288 | tf_op jit(solution)/shard_map/all_to_all | solution.py:175

commit v7 on v6

--- a/solution.py
+++ b/solution.py
@@ -130,13 +130,32 @@
             for c in range(groups_col)
         ]
         arrived.append(lax.ppermute(piece, ("row", "col"), pairs) if index else piece)
-    return [arrived[flip] + arrived[flips + flip] for flip in range(flips)]
-
-
-def side_by_side(held):
-    me = lax.axis_index("col")
-    size = len(held)
-    return jnp.concatenate([lax.select_n(me ^ j, *held) for j in range(size)], axis=1)
+    return arrived
+
+
+def collect_kernel(*refs):
+    out = refs[-1]
+    flips = len(refs) // 2
+    span = refs[0].shape[1]
+    for flip in range(flips):
+        first = pl.multiple_of((lax.axis_index("col") ^ flip) * span, LANES)
+        out[:, pl.ds(first, span)] = refs[flip][...] + refs[flips + flip][...]
+
+
+def collect(arrived):
+    flips = len(arrived) // 2
+    share, span = arrived[0].shape
+    if span % LANES:
+        me = lax.axis_index("col")
+        held = [arrived[flip] + arrived[flips + flip] for flip in range(flips)]
+        return jnp.concatenate([lax.select_n(me ^ j, *held) for j in range(flips)], axis=1)
+    return pl.pallas_call(
+        collect_kernel,
+        out_shape=jax.ShapeDtypeStruct((share, span * flips), jnp.float32),
+        in_specs=[WHOLE] * len(arrived),
+        out_specs=WHOLE,
+        cost_estimate=LIGHT,
+    )(*arrived)
 
 
 def pair_rows(masked):
@@ -175,7 +194,7 @@
     terms = lax.all_to_all(terms.reshape(groups_row, width // groups_row, span), "row", 0, 0)
     diag_block = terms.sum(axis=0)
 
-    off_diag = side_by_side(exchange(outward, groups_col))
+    off_diag = collect(exchange(outward, groups_col))
     return (off_diag.reshape(block_rows, 1, share, width), diag_block)
 
 

time: 42.8 us -> 40.8 us (0.953)
  waiting for transfers between devices: 13.2 us -> 9.11 us
  Pallas kernels: 3.32 us -> 4.83 us
  local copies, waits for them, and re-layouts: 0.01 us -> 1.19 us
  other arithmetic: 1.3 us -> 0.63 us
    all_to_all x1, waiting for transfers between devices: 7.86 us -> 0.01 us  [local(): lax.all_to_all(terms.reshape(groups_row, width // groups_row, span), 'row...]
    ppermute x7, waiting for transfers between devices: 0.1 us -> 3.85 us  [exchange(): lax.ppermute(piece, ('row', 'col'), pairs)]
    pallas_call x0 -> x1, Pallas kernels: none -> 1.48 us  [collect(): pl.pallas_call(collect_kernel, out_shape=jax.ShapeDtypeStruct((share, spa...]
    unnamed x4 -> x20, local copies, waits for them, and re-layouts: 0.01 us -> 1.19 us
    ppermute x7, starting transfers between devices: 7.54 us -> 6.66 us  [exchange(): lax.ppermute(piece, ('row', 'col'), pairs)]
    all_to_all x1, starting transfers between devices: 4.99 us -> 5.82 us  [local(): lax.all_to_all(terms.reshape(groups_row, width // groups_row, span), 'row...]
    reshape x1 -> x0, other arithmetic: 0.64 us -> none  [local(): return (off_diag.reshape(block_rows, 1, share, width), diag_block)]
  transfers between devices with their start and end apart: 14 -> 14, of which waited for: 6 -> 7; matrix products, arithmetic and copies ran while one was open for 2% -> 0% of each run, Pallas kernels for 0% -> 4%
where the time goes in v7:
time: 40.8 us; the launch traced here: 40.4 us
  starting transfers between devices  23.9 us (59%)
  waiting for transfers between devices  9.11 us (22%)
  Pallas kernels  4.83 us (12%)
  local copies, waits for them, and re-layouts  1.19 us (3%)
  between operations  0.7 us (2%)
  other arithmetic  0.63 us (2%)
    ppermute x7, starting transfers between devices, exchange(): lax.ppermute(piece, ('row', 'col'), pairs)  6.66 us
    all_to_all x1, starting transfers between devices, local(): columns = lax.all_to_all(copies, 'row', 0, 0, axis_index_groups=lines)  6.45 us
    all_to_all x1, starting transfers between devices, local(): lax.all_to_all(terms.reshape(groups_row, width // groups_row, span), 'row...  5.82 us
    ppermute x4, waiting for transfers between devices, flipped(): lax.ppermute(value, axis, [(i, i ^ flip) for i in range(lax.axis_size(axi...  5.12 us
    ppermute x7, waiting for transfers between devices, exchange(): lax.ppermute(piece, ('row', 'col'), pairs)  3.85 us
    ppermute x4, starting transfers between devices, flipped(): lax.ppermute(value, axis, [(i, i ^ flip) for i in range(lax.axis_size(axi...  3.41 us
    pallas_call x1, Pallas kernels, prepare(): pl.pallas_call(prepare_kernel, out_shape=(jax.ShapeDtypeStruct((block_col...  1.81 us
    ppermute x1, starting transfers between devices, pair_rows(): held = lax.ppermute(masked, ('row', 'col'), cross)  1.55 us
  transfers between devices with their start and end apart: 14, of which 7 were waited for; matrix products, arithmetic and copies ran while one was open for 0% of the time, Pallas kernels for 4%

profile of v7, /device:TPU:0, one launch (start us, length us, event | category | flops | bytes accessed | tf_op | source)
XLA Modules:
  0.0 40.4 jit_solution(1405938605499451051)
XLA Ops:
  0.6 1.8 %shard_map.59 = (f32[2,128,128]{2,1,0:T(8,128)}, f32[4,128,128]{2,1,0:T(8,128)}) custom-call(s32[2]{0:T(128)} %bitcast.10, f32[256,128]{1,0:T(8,128)} %bitcast.8, f32[128,512]{1,0:T(8,128)} %bitcast.5), custom_call_target="tpu_custom_call" | custom-call | flops 1000 | bytes 1000 | tf_op jit(solution)/shard_map/pallas_call | solution.py:59
  2.4 1.6 %collective-permute-start = (f32[2,128,128]{2,1,0:T(8,128)}, f32[2,128,128]{2,1,0:T(8,128)S(1)}, u32[]{:S(2)}, u32[]{:S(2)}) collective-permute-start(f32[2,128,128]{2,1,0:T(8,128)} %get-tuple-element.13), channel_id=1, source_target_pairs={{0,0},{1,4},{2,2},{3,6},{4,1},{5,5},{6,3},{7,7},{8,8},{9,12},{10,1... | collective-permute-start | bytes 393224 | tf_op jit(solution)/shard_map/ppermute | solution.py:169
  4.0 6.4 %all-to-all-start = ((f32[4,128,128]{2,1,0:T(8,128)}), f32[4,128,128]{2,1,0:T(8,128)S(1)}, u32[]{:S(2)}, u32[]{:S(2)}) async-start(f32[4,128,128]{2,1,0:T(8,128)} %get-tuple-element.14), calls=%async_computation | async-start | bytes 524288 | tf_op jit(solution)/shard_map/all_to_all | solution.py:187
  10.4 1.9 %collective-permute-start.4 = (f32[128,512]{1,0:T(8,128)S(1)}, f32[128,512]{1,0:T(8,128)S(1)}, u32[]{:S(2)}, u32[]{:S(2)}) collective-permute-start(f32[128,512]{1,0:T(8,128)S(1)} %bitcast.6), channel_id=1, source_target_pairs={{0,4},{4,0},{8,12},{12,8},{16,20},{20,16},{24,28},{28,24},{1,5},{5... | collective-permute-start | bytes 786440 | tf_op jit(solution)/shard_map/ppermute | solution.py:16
  12.3 0.0 collective-permute-done.refs_0_
  12.3 1.5 %collective-permute-start.1 = (f32[2,128,128]{2,1,0:T(8,128)S(1)}, f32[2,128,128]{2,1,0:T(8,128)S(1)}, u32[]{:S(2)}, u32[]{:S(2)}) collective-permute-start(f32[2,128,128]{2,1,0:T(8,128)S(1)} %collective-permute-done.refs_0_), channel_id=1, source_target_pairs={{0,2},{1,3},{2,0},{3,1},{4,6},{5,7},{6,4},{7,5},{8,10},{9,11},{10,... | collective-permute-start | bytes 393224 | tf_op jit(solution)/shard_map/ppermute | solution.py:16
  13.9 3.8 %collective-permute-done.1.refs_1_ = f32[2,128,128]{2,1,0:T(8,128)S(1)} collective-permute-done((f32[2,128,128]{2,1,0:T(8,128)S(1)}, f32[2,128,128]{2,1,0:T(8,128)S(1)}, u32[]{:S(2)}, u32[]{:S(2)}) %collective-permute-start.1) | collective-permute-done | bytes 131104 | tf_op jit(solution)/shard_map/ppermute | solution.py:16
  17.6 1.3 %collective-permute-done.4.refs_6_ = f32[128,512]{1,0:T(8,128)S(1)} collective-permute-done((f32[128,512]{1,0:T(8,128)S(1)}, f32[128,512]{1,0:T(8,128)S(1)}, u32[]{:S(2)}, u32[]{:S(2)}) %collective-permute-start.4) | collective-permute-done | bytes 262176 | tf_op jit(solution)/shard_map/ppermute | solution.py:16
  18.9 0.1 collective-permute-done.3.refs_3_
  19.0 0.1 all-to-all-done.refs_4_
  19.1 1.5 %shard_map.60 = (f32[512,128]{1,0:T(8,128)}, f32[32,128]{1,0:T(8,128)S(1)}, f32[32,128]{1,0:T(8,128)S(1)}, f32[32,128]{1,0:T(8,128)S(1)}, f32[32,128]{1,0:T(8,12...) custom-call(f32[2,128,128]{2,1,0:T(8,128)S(1)} %collective-permute-done.r, ...), custom_call_target="tpu_custom_call" | custom-call | flops 1000 | bytes 1000 | tf_op jit(solution)/shard_map/pallas_call | solution.py:110
  20.7 0.6 %copy-done.2 = f32[32,128]{1,0:T(8,128)} copy-done((f32[32,128]{1,0:T(8,128)}, f32[32,128]{1,0:T(8,128)S(1)}, u32[]{:S(2)}) %copy-start.2) | copy-done | bytes 16408
  21.3 5.8 %all-to-all-start.1 = ((f32[8,64,128]{2,1,0:T(8,128)}), f32[8,64,128]{2,1,0:T(8,128)S(1)}, u32[]{:S(2)}, u32[]{:S(2)}) async-start(f32[8,64,128]{2,1,0:T(8,128)} %bitcast.4), calls=%async_computation.1 | async-start | bytes 524288 | tf_op jit(solution)/shard_map/all_to_all | solution.py:194
  27.1 1.6 %collective-permute-start.6 = (f32[32,128]{1,0:T(8,128)S(1)}, f32[32,128]{1,0:T(8,128)S(1)}, u32[]{:S(2)}, u32[]{:S(2)}) collective-permute-start(f32[32,128]{1,0:T(8,128)S(1)} %get-tuple-element.17), channel_id=1, source_target_pairs={{0,2},{1,3},{2,0},{3,1},{4,6},{5,7},{6,4},{7,5},{8,10},{9,11},{10,... | collective-permute-start | bytes 49160 | tf_op jit(solution)/shard_map/ppermute | solution.py:132
  28.7 0.3 collective-permute-start.7
  29.0 2.0 %collective-permute-start.8 = (f32[32,128]{1,0:T(8,128)S(1)}, f32[32,128]{1,0:T(8,128)S(1)}, u32[]{:S(2)}, u32[]{:S(2)}) collective-permute-start(f32[32,128]{1,0:T(8,128)S(1)} %get-tuple-element.19), channel_id=1, source_target_pairs={{0,4},{1,5},{2,6},{3,7},{4,0},{5,1},{6,2},{7,3},{8,12},{9,13},{10,... | collective-permute-start | bytes 49160 | tf_op jit(solution)/shard_map/ppermute | solution.py:132
  31.0 2.6 %collective-permute-start.10 = (f32[32,128]{1,0:T(8,128)S(1)}, f32[32,128]{1,0:T(8,128)S(1)}, u32[]{:S(2)}, u32[]{:S(2)}) collective-permute-start(f32[32,128]{1,0:T(8,128)S(1)} %get-tuple-element.21), channel_id=1, source_target_pairs={{0,6},{1,7},{2,4},{3,5},{4,2},{5,3},{6,0},{7,1},{8,14},{9,15},{10,... | collective-permute-start | bytes 49160 | tf_op jit(solution)/shard_map/ppermute | solution.py:132
  33.6 0.2 collective-permute-start.11
  33.8 0.7 %collective-permute-done.9.refs_5_ = f32[32,128]{1,0:T(8,128)S(1)} collective-permute-done((f32[32,128]{1,0:T(8,128)S(1)}, f32[32,128]{1,0:T(8,128)S(1)}, u32[]{:S(2)}, u32[]{:S(2)}) %collective-permute-start.9) | collective-permute-done | bytes 16416 | tf_op jit(solution)/shard_map/ppermute | solution.py:132
  34.5 1.4 %collective-permute-done.10.refs_6_ = f32[32,128]{1,0:T(8,128)S(1)} collective-permute-done((f32[32,128]{1,0:T(8,128)S(1)}, f32[32,128]{1,0:T(8,128)S(1)}, u32[]{:S(2)}, u32[]{:S(2)}) %collective-permute-start.10) | collective-permute-done | bytes 16416 | tf_op jit(solution)/shard_map/ppermute | solution.py:132
  35.9 1.7 %collective-permute-done.11.refs_7_ = f32[32,128]{1,0:T(8,128)S(1)} collective-permute-done((f32[32,128]{1,0:T(8,128)S(1)}, f32[32,128]{1,0:T(8,128)S(1)}, u32[]{:S(2)}, u32[]{:S(2)}) %collective-permute-start.11) | collective-permute-done | bytes 16416 | tf_op jit(solution)/shard_map/ppermute | solution.py:132
  37.7 0.6 %copy-done.9 = f32[32,128]{1,0:T(8,128)} copy-done((f32[32,128]{1,0:T(8,128)}, f32[32,128]{1,0:T(8,128)S(1)}, u32[]{:S(2)}) %copy-start.9) | copy-done | bytes 16408
  38.2 1.5 %shard_map.61 = f32[32,512]{1,0:T(8,128)} custom-call(f32[32,128]{1,0:T(8,128)} %copy-done.2, f32[32,128]{1,0:T(8,128)} %copy-done.3, f32[32,128]{1,0:T(8,128)} %copy-done.4, f32[32,128]{1,0:T(8,128)} %copy-done.5, f32[32,128]{1,0:T(8,128)} %copy-done.6, f32[32,128]{1,0:T(8,128)} %copy-done.7, f32[32,128]{1,0:T(8,128)} %copy-done.8, f32[32,128]{1,0:T(8,128)} %copy-done.9), custom_call_target="tpu_custom_call" | custom-call | flops 1000 | bytes 1000 | tf_op jit(solution)/shard_map/pallas_call | solution.py:152
  39.7 0.6 %reduce_sum.9 = f32[64,128]{1,0:T(8,128)} reduce(f32[8,64,128]{2,1,0:T(8,128)S(1)} %all-to-all-done.1, f32[]{:T(128)} %constant.0.clone.1), dimensions={0}, to_apply=%region_0.0 | reduce | flops 57344 | bytes 294916 | tf_op jit(solution)/shard_map/reduce_sum | solution.py:195
  (28 shorter events, 0.1 us)
Async XLA Ops:
  2.4 9.9 %collective-permute-start = (f32[2,128,128]{2,1,0:T(8,128)}, f32[2,128,128]{2,1,0:T(8,128)S(1)}, u32[]{:S(2)}, u32[]{:S(2)}) collective-permute-start(f32[2,128,128]{2,1,0:T(8,128)} %get-tuple-element.13), channel_id=1, source_target_pairs={{0,0},{1,4},{2,2},{3,6},{4,1},{5,5},{6,3},{7,7},{8,8},{9,12},{10,1... | collective-permute-start | bytes 393224 | tf_op jit(solution)/shard_map/ppermute | solution.py:169
  4.0 6.5 %copy-start = (f32[1,1,128,512]{3,2,1,0:T(8,128)S(1)}, f32[1,1,128,512]{3,2,1,0:T(8,128)}, u32[]{:S(2)}) copy-start(f32[1,1,128,512]{3,2,1,0:T(8,128)} %param.6) | copy-start | bytes 786436
  4.0 15.1 %copy-start.1 = (f32[64,128]{1,0:T(8,128)S(1)}, f32[64,128]{1,0:T(8,128)}, u32[]{:S(2)}) copy-start(f32[64,128]{1,0:T(8,128)} %refs_7_.1) | copy-start | bytes 98308
  4.0 15.1 %all-to-all-start = ((f32[4,128,128]{2,1,0:T(8,128)}), f32[4,128,128]{2,1,0:T(8,128)S(1)}, u32[]{:S(2)}, u32[]{:S(2)}) async-start(f32[4,128,128]{2,1,0:T(8,128)} %get-tuple-element.14), calls=%async_computation | async-start | bytes 524288 | tf_op jit(solution)/shard_map/all_to_all | solution.py:187
  10.4 8.5 %collective-permute-start.4 = (f32[128,512]{1,0:T(8,128)S(1)}, f32[128,512]{1,0:T(8,128)S(1)}, u32[]{:S(2)}, u32[]{:S(2)}) collective-permute-start(f32[128,512]{1,0:T(8,128)S(1)} %bitcast.6), channel_id=1, source_target_pairs={{0,4},{4,0},{8,12},{12,8},{16,20},{20,16},{24,28},{28,24},{1,5},{5... | collective-permute-start | bytes 786440 | tf_op jit(solution)/shard_map/ppermute | solution.py:16
  12.3 5.3 %collective-permute-start.1 = (f32[2,128,128]{2,1,0:T(8,128)S(1)}, f32[2,128,128]{2,1,0:T(8,128)S(1)}, u32[]{:S(2)}, u32[]{:S(2)}) collective-permute-start(f32[2,128,128]{2,1,0:T(8,128)S(1)} %collective-permute-done.refs_0_), channel_id=1, source_target_pairs={{0,2},{1,3},{2,0},{3,1},{4,6},{5,7},{6,4},{7,5},{8,10},{9,11},{10,... | collective-permute-start | bytes 393224 | tf_op jit(solution)/shard_map/ppermute | solution.py:16
  13.9 5.1 %collective-permute-start.2 = (f32[2,128,128]{2,1,0:T(8,128)S(1)}, f32[2,128,128]{2,1,0:T(8,128)S(1)}, u32[]{:S(2)}, u32[]{:S(2)}) collective-permute-start(f32[2,128,128]{2,1,0:T(8,128)S(1)} %collective-permute-done.refs_0_), channel_id=1, source_target_pairs={{0,1},{1,0},{2,3},{3,2},{4,5},{5,4},{6,7},{7,6},{8,9},{9,8},{10,11... | collective-permute-start | bytes 393224 | tf_op jit(solution)/shard_map/ppermute | solution.py:16
  17.6 1.3 %collective-permute-start.3 = (f32[2,128,128]{2,1,0:T(8,128)S(1)}, f32[2,128,128]{2,1,0:T(8,128)S(1)}, u32[]{:S(2)}, u32[]{:S(2)}) collective-permute-start(f32[2,128,128]{2,1,0:T(8,128)S(1)} %collective-permute-done.1.refs_1_), channel_id=1, source_target_pairs={{0,1},{1,0},{2,3},{3,2},{4,5},{5,4},{6,7},{7,6},{8,9},{9,8},{10,11... | collective-permute-start | bytes 393224 | tf_op jit(solution)/shard_map/ppermute | solution.py:16
  20.7 0.6 %copy-start.2 = (f32[32,128]{1,0:T(8,128)}, f32[32,128]{1,0:T(8,128)S(1)}, u32[]{:S(2)}) copy-start(f32[32,128]{1,0:T(8,128)S(1)} %get-tuple-element.15.refs_0_) | copy-start | bytes 49156
  21.3 18.5 %all-to-all-start.1 = ((f32[8,64,128]{2,1,0:T(8,128)}), f32[8,64,128]{2,1,0:T(8,128)S(1)}, u32[]{:S(2)}, u32[]{:S(2)}) async-start(f32[8,64,128]{2,1,0:T(8,128)} %bitcast.4), calls=%async_computation.1 | async-start | bytes 524288 | tf_op jit(solution)/shard_map/all_to_all | solution.py:194
  27.1 3.9 %collective-permute-start.5 = (f32[32,128]{1,0:T(8,128)S(1)}, f32[32,128]{1,0:T(8,128)S(1)}, u32[]{:S(2)}, u32[]{:S(2)}) collective-permute-start(f32[32,128]{1,0:T(8,128)S(1)} %get-tuple-element.16), channel_id=1, source_target_pairs={{0,1},{1,0},{2,3},{3,2},{4,5},{5,4},{6,7},{7,6},{8,9},{9,8},{10,11... | collective-permute-start | bytes 49160 | tf_op jit(solution)/shard_map/ppermute | solution.py:132
  27.1 6.5 %collective-permute-start.6 = (f32[32,128]{1,0:T(8,128)S(1)}, f32[32,128]{1,0:T(8,128)S(1)}, u32[]{:S(2)}, u32[]{:S(2)}) collective-permute-start(f32[32,128]{1,0:T(8,128)S(1)} %get-tuple-element.17), channel_id=1, source_target_pairs={{0,2},{1,3},{2,0},{3,1},{4,6},{5,7},{6,4},{7,5},{8,10},{9,11},{10,... | collective-permute-start | bytes 49160 | tf_op jit(solution)/shard_map/ppermute | solution.py:132
  28.7 5.1 %collective-permute-start.7 = (f32[32,128]{1,0:T(8,128)S(1)}, f32[32,128]{1,0:T(8,128)S(1)}, u32[]{:S(2)}, u32[]{:S(2)}) collective-permute-start(f32[32,128]{1,0:T(8,128)S(1)} %get-tuple-element.18), channel_id=1, source_target_pairs={{0,3},{1,2},{2,1},{3,0},{4,7},{5,6},{6,5},{7,4},{8,11},{9,10},{10,... | collective-permute-start | bytes 49160 | tf_op jit(solution)/shard_map/ppermute | solution.py:132
  29.0 4.8 %collective-permute-start.8 = (f32[32,128]{1,0:T(8,128)S(1)}, f32[32,128]{1,0:T(8,128)S(1)}, u32[]{:S(2)}, u32[]{:S(2)}) collective-permute-start(f32[32,128]{1,0:T(8,128)S(1)} %get-tuple-element.19), channel_id=1, source_target_pairs={{0,4},{1,5},{2,6},{3,7},{4,0},{5,1},{6,2},{7,3},{8,12},{9,13},{10,... | collective-permute-start | bytes 49160 | tf_op jit(solution)/shard_map/ppermute | solution.py:132
  31.0 3.5 %collective-permute-start.9 = (f32[32,128]{1,0:T(8,128)S(1)}, f32[32,128]{1,0:T(8,128)S(1)}, u32[]{:S(2)}, u32[]{:S(2)}) collective-permute-start(f32[32,128]{1,0:T(8,128)S(1)} %get-tuple-element.20), channel_id=1, source_target_pairs={{0,5},{1,4},{2,7},{3,6},{4,1},{5,0},{6,3},{7,2},{8,13},{9,12},{10,... | collective-permute-start | bytes 49160 | tf_op jit(solution)/shard_map/ppermute | solution.py:132
  31.0 6.7 %copy-start.3 = (f32[32,128]{1,0:T(8,128)}, f32[32,128]{1,0:T(8,128)S(1)}, u32[]{:S(2)}) copy-start(f32[32,128]{1,0:T(8,128)S(1)} %collective-permute-done.5.refs_1_) | copy-start | bytes 49156
  31.0 4.9 %collective-permute-start.10 = (f32[32,128]{1,0:T(8,128)S(1)}, f32[32,128]{1,0:T(8,128)S(1)}, u32[]{:S(2)}, u32[]{:S(2)}) collective-permute-start(f32[32,128]{1,0:T(8,128)S(1)} %get-tuple-element.21), channel_id=1, source_target_pairs={{0,6},{1,7},{2,4},{3,5},{4,2},{5,3},{6,0},{7,1},{8,14},{9,15},{10,... | collective-permute-start | bytes 49160 | tf_op jit(solution)/shard_map/ppermute | solution.py:132
  33.6 4.1 %copy-start.4 = (f32[32,128]{1,0:T(8,128)}, f32[32,128]{1,0:T(8,128)S(1)}, u32[]{:S(2)}) copy-start(f32[32,128]{1,0:T(8,128)S(1)} %collective-permute-done.6.refs_2_) | copy-start | bytes 49156
  33.6 4.1 %collective-permute-start.11 = (f32[32,128]{1,0:T(8,128)S(1)}, f32[32,128]{1,0:T(8,128)S(1)}, u32[]{:S(2)}, u32[]{:S(2)}) collective-permute-start(f32[32,128]{1,0:T(8,128)S(1)} %get-tuple-element.22), channel_id=1, source_target_pairs={{0,7},{1,6},{2,5},{3,4},{4,3},{5,2},{6,1},{7,0},{8,15},{9,14},{10,... | collective-permute-start | bytes 49160 | tf_op jit(solution)/shard_map/ppermute | solution.py:132
  33.8 3.9 %copy-start.5 = (f32[32,128]{1,0:T(8,128)}, f32[32,128]{1,0:T(8,128)S(1)}, u32[]{:S(2)}) copy-start(f32[32,128]{1,0:T(8,128)S(1)} %collective-permute-done.7.refs_3_) | copy-start | bytes 49156
  33.8 3.9 %copy-start.6 = (f32[32,128]{1,0:T(8,128)}, f32[32,128]{1,0:T(8,128)S(1)}, u32[]{:S(2)}) copy-start(f32[32,128]{1,0:T(8,128)S(1)} %collective-permute-done.8.refs_4_) | copy-start | bytes 49156
  34.5 3.2 %copy-start.7 = (f32[32,128]{1,0:T(8,128)}, f32[32,128]{1,0:T(8,128)S(1)}, u32[]{:S(2)}) copy-start(f32[32,128]{1,0:T(8,128)S(1)} %collective-permute-done.9.refs_5_) | copy-start | bytes 49156
  35.9 1.8 %copy-start.8 = (f32[32,128]{1,0:T(8,128)}, f32[32,128]{1,0:T(8,128)S(1)}, u32[]{:S(2)}) copy-start(f32[32,128]{1,0:T(8,128)S(1)} %collective-permute-done.10.refs_6_) | copy-start | bytes 49156
  37.6 0.6 %copy-start.9 = (f32[32,128]{1,0:T(8,128)}, f32[32,128]{1,0:T(8,128)S(1)}, u32[]{:S(2)}) copy-start(f32[32,128]{1,0:T(8,128)S(1)} %collective-permute-done.11.refs_7_) | copy-start | bytes 49156

commit v8 on v7

--- a/solution.py
+++ b/solution.py
@@ -9,6 +9,7 @@
 
 LANES = 128
 WHOLE = pl.BlockSpec(memory_space=pltpu.VMEM)
+ROOM = pltpu.CompilerParams(vmem_limit_bytes=16 * 1024 * 1024)
 LIGHT = pl.CostEstimate(flops=1000, bytes_accessed=1000, transcendentals=0)
 
 
@@ -31,12 +32,9 @@
     return once(left_high, right_high) + (once(left_high, right_low) + once(left_low, right_high))
 
 
-def prepare_kernel(presence, blocks, factor, masked, copies):
-    count, rows, span = copies.shape
-    first = pl.multiple_of(lax.axis_index("col") * span, LANES)
-    mine = factor[:, pl.ds(first, span)]
-    for i in range(count):
-        copies[i] = mine
+def prepare_kernel(presence, blocks, factor, masked, mine):
+    rows, span = mine.shape
+    mine[...] = factor[:, pl.ds(pl.multiple_of(lax.axis_index("col") * span, LANES), span)]
     block_cols, _, order = masked.shape
     for a in range(rows // order):
         for b in range(block_cols):
@@ -45,7 +43,7 @@
             masked[b, pl.ds(a * order, order), :] = picked * weight
 
 
-def prepare(presence, blocks, own, receivers, span):
+def prepare(presence, blocks, own, span):
     rows, width = own.shape
     block_cols = blocks.shape[0] // rows
     order = blocks.shape[1]
@@ -54,27 +52,32 @@
         mine = lax.dynamic_slice_in_dim(own, first, span, 1)
         weights = presence.reshape(-1, 1, block_cols, 1).astype(jnp.float32)
         picked = blocks.reshape(-1, order, block_cols, order) * weights
-        masked = picked.transpose(2, 0, 1, 3).reshape(block_cols, rows, order)
-        return masked, jnp.broadcast_to(mine[None], (receivers, rows, span))
+        return picked.transpose(2, 0, 1, 3).reshape(block_cols, rows, order), mine
     return pl.pallas_call(
         prepare_kernel,
         out_shape=(
             jax.ShapeDtypeStruct((block_cols, rows, order), jnp.float32),
-            jax.ShapeDtypeStruct((receivers, rows, span), jnp.float32),
+            jax.ShapeDtypeStruct((rows, span), jnp.float32),
         ),
         in_specs=[pl.BlockSpec(memory_space=pltpu.SMEM), WHOLE, WHOLE],
         out_specs=(WHOLE, WHOLE),
         cost_estimate=LIGHT,
+        compiler_params=ROOM,
     )(presence, blocks, own)
 
 
-def middle_kernel(count, *refs):
-    pieces = refs[: 2 * count]
-    columns, own, near, dinv, terms = refs[2 * count : 2 * count + 5]
-    outward = refs[2 * count + 5 :]
+def middle_kernel(count, lines, *refs):
+    pieces, refs = refs[: 2 * count], refs[2 * count :]
+    strips, refs = refs[:lines], refs[lines:]
+    own, near, dinv, terms = refs[:4]
+    outward, columns, scratch = refs[4:-2], refs[-2], refs[-1]
     block_cols, rows, order = pieces[0].shape
     col_index = lax.axis_index("col")
     row_index = lax.axis_index("row")
+    for line in range(lines):
+        for a in range(rows // order):
+            at = a * lines + ((row_index >> 1) ^ line)
+            columns[at] = strips[line][pl.ds(a * order, order), :]
     left, right = [], []
     for t in range(count):
         for b in range(block_cols):
@@ -91,8 +94,7 @@
     here = pl.ds(pl.multiple_of(row_index * tall, 8), tall)
     terms[here, :] = terms[here, :] + dinv[...]
 
-    scratch = outward[-1]
-    flips = len(outward[:-1]) // 2
+    flips = len(outward) // 2
     share = order // flips
     for near_row, value in enumerate((mine, other)):
         scratch[...] = -value
@@ -103,19 +105,24 @@
                 outward[near_row * flips + flip][pl.ds(a * share, share), :] = picked
 
 
-def middle(pieces, columns, own, near, dinv, flips):
+def middle(pieces, strips, own, near, dinv, flips):
     rows, width = own.shape
-    span = columns.shape[2]
+    order = pieces[0].shape[2]
+    span = strips[0].shape[1]
+    operands = (*pieces, *strips, own, near, dinv)
     part = jax.ShapeDtypeStruct((rows // flips, span), jnp.float32)
     return pl.pallas_call(
-        functools.partial(middle_kernel, len(pieces) // 2),
+        functools.partial(middle_kernel, len(pieces) // 2, len(strips)),
         out_shape=(jax.ShapeDtypeStruct((width, span), jnp.float32),) + (part,) * (2 * flips),
-        in_specs=[WHOLE] * (len(pieces) + 4),
+        in_specs=[WHOLE] * len(operands),
         out_specs=(WHOLE,) * (1 + 2 * flips),
-        scratch_shapes=[pltpu.VMEM((rows, span), jnp.float32)],
+        scratch_shapes=[
+            pltpu.VMEM((rows // order * len(strips), order, span), jnp.float32),
+            pltpu.VMEM((rows, span), jnp.float32),
+        ],
         cost_estimate=LIGHT,
-        compiler_params=pltpu.CompilerParams(vmem_limit_bytes=32 * 1024 * 1024),
-    )(*pieces, columns, own, near, dinv)
+        compiler_params=ROOM,
+    )(*operands)
 
 
 def exchange(outward, flips):
@@ -155,6 +162,7 @@
         in_specs=[WHOLE] * len(arrived),
         out_specs=WHOLE,
         cost_estimate=LIGHT,
+        compiler_params=ROOM,
     )(*arrived)
 
 
@@ -182,15 +190,12 @@
 
     own = factor.reshape(rows, width)
     blocks = inverse_set.reshape(rows * block_cols, order)
-    masked, copies = prepare(presence.reshape(-1), blocks, own, groups_row // 2, span)
-    lines = [list(range(bit, groups_row, 2)) for bit in range(2)]
-    columns = lax.all_to_all(copies, "row", 0, 0, axis_index_groups=lines)
-    columns = columns.reshape(groups_row // 2, block_rows, order, span).transpose(1, 0, 2, 3)
-    columns = columns.reshape(-1, order, span)
+    masked, mine = prepare(presence.reshape(-1), blocks, own, span)
+    strips = [mine] + [flipped(mine, "row", flip) for flip in range(2, groups_row, 2)]
     pieces = pair_rows(masked)
     near = flipped(own, "row", 1)
 
-    terms, *outward = middle(pieces, columns, own, near, dinv, groups_col)
+    terms, *outward = middle(pieces, strips, own, near, dinv, groups_col)
     terms = lax.all_to_all(terms.reshape(groups_row, width // groups_row, span), "row", 0, 0)
     diag_block = terms.sum(axis=0)
 

time: 40.8 us -> 43.9 us (1.076)
  starting transfers between devices: 23.9 us -> 29.3 us
  Pallas kernels: 4.83 us -> 2.77 us
  waiting for transfers between devices: 9.11 us -> 7.68 us
  local copies, waits for them, and re-layouts: 1.19 us -> 2.51 us
    ppermute x4 -> x7, starting transfers between devices: 3.41 us -> 15.3 us  [flipped(): lax.ppermute(value, axis, [(i, i ^ flip) for i in range(lax.axis_size(axi...]
    all_to_all x1 -> x0, starting transfers between devices: 6.45 us -> none  [local(): columns = lax.all_to_all(copies, 'row', 0, 0, axis_index_groups=lines)]
    ppermute x4 -> x7, waiting for transfers between devices: 5.12 us -> 3.79 us  [flipped(): lax.ppermute(value, axis, [(i, i ^ flip) for i in range(lax.axis_size(axi...]
    unnamed x20 -> x10, local copies, waits for them, and re-layouts: 1.19 us -> 2.51 us
    pallas_call x1, Pallas kernels: 1.81 us -> 0.56 us  [prepare(): pl.pallas_call(prepare_kernel, out_shape=(jax.ShapeDtypeStruct((block_col...]
    all_to_all x1, starting transfers between devices: 5.82 us -> 6.9 us  [local(): lax.all_to_all(terms.reshape(groups_row, width // groups_row, span), 'row...]
    ppermute x1, starting transfers between devices: 1.55 us -> 0.67 us  [pair_rows(): held = lax.ppermute(masked, ('row', 'col'), cross)]
    pallas_call x1, Pallas kernels: 1.48 us -> 0.64 us  [collect(): pl.pallas_call(collect_kernel, out_shape=jax.ShapeDtypeStruct((share, spa...]
  transfers between devices with their start and end apart: 14 -> 16, of which waited for: 7 -> 5; matrix products, arithmetic and copies ran while one was open for 0% -> 0% of each run, Pallas kernels for 4% -> 1%
where the time goes in v8:
time: 43.9 us; the launch traced here: 43.6 us
  starting transfers between devices  29.3 us (67%)
  waiting for transfers between devices  7.68 us (17%)
  Pallas kernels  2.77 us (6%)
  local copies, waits for them, and re-layouts  2.51 us (6%)
  between operations  0.7 us (2%)
  other arithmetic  0.63 us (1%)
    ppermute x7, starting transfers between devices, flipped(): lax.ppermute(value, axis, [(i, i ^ flip) for i in range(lax.axis_size(axi...  15.3 us
    all_to_all x1, starting transfers between devices, local(): lax.all_to_all(terms.reshape(groups_row, width // groups_row, span), 'row...  6.9 us
    ppermute x7, starting transfers between devices, exchange(): lax.ppermute(piece, ('row', 'col'), pairs)  6.42 us
    ppermute x7, waiting for transfers between devices, exchange(): lax.ppermute(piece, ('row', 'col'), pairs)  3.88 us
    ppermute x7, waiting for transfers between devices, flipped(): lax.ppermute(value, axis, [(i, i ^ flip) for i in range(lax.axis_size(axi...  3.79 us
    unnamed x10, local copies, waits for them, and re-layouts  2.51 us
    pallas_call x1, Pallas kernels, middle(): pl.pallas_call(functools.partial(middle_kernel, len(pieces) // 2, len(str...  1.57 us
  transfers between devices with their start and end apart: 16, of which 5 were waited for; matrix products, arithmetic and copies ran while one was open for 0% of the time, Pallas kernels for 1%

profile of v8, /device:TPU:0, one launch (start us, length us, event | category | flops | bytes accessed | tf_op | source)
XLA Modules:
  0.0 43.6 jit_solution(14866660068239291383)
XLA Ops:
  0.6 0.6 %copy-done.4 = s32[1,1,2,1]{2,3,1,0:T(1,128)S(1)} copy-done((s32[1,1,2,1]{2,3,1,0:T(1,128)S(1)}, s32[1,1,2,1]{2,3,1,0:T(1,128)}, u32[]{:S(2)}) %copy-start.4) | copy-done | bytes 32
  1.3 0.9 %copy-done = f32[1,1,128,512]{3,2,1,0:T(8,128)S(1)} copy-done((f32[1,1,128,512]{3,2,1,0:T(8,128)S(1)}, f32[1,1,128,512]{3,2,1,0:T(8,128)}, u32[]{:S(2)}) %copy-start) | copy-done | bytes 262168
  2.2 0.9 %copy-done.2 = f32[1,1,128,2,1,128]{5,4,3,2,1,0:T(1,128)S(1)} copy-done((f32[1,1,128,2,1,128]{5,4,3,2,1,0:T(1,128)S(1)}, f32[1,1,128,2,1,128]{5,4,3,2,1,0:T(1,128)}, u32[]{:S(2)}) %copy-start.2) | copy-done | bytes 131096
  3.1 0.6 %shard_map.59 = (f32[2,128,128]{2,1,0:T(8,128)S(1)}, f32[128,128]{1,0:T(8,128)S(1)}) custom-call(s32[2]{0:T(128)S(1)} %bitcast.9, f32[256,128]{1,0:T(8,128)S(1)} %bitcast.8, f32[128,512]{1,0:T(8,128)S(1)} %bitcast.5), custom_call_target="tpu_custom_call" | custom-call | flops 1000 | bytes 1000 | tf_op jit(solution)/shard_map/pallas_call | solution.py:56
  3.7 0.7 %collective-permute-start = (f32[2,128,128]{2,1,0:T(8,128)S(1)}, f32[2,128,128]{2,1,0:T(8,128)S(1)}, u32[]{:S(2)}, u32[]{:S(2)}) collective-permute-start(f32[2,128,128]{2,1,0:T(8,128)S(1)} %get-tuple-element.13), channel_id=1, source_target_pairs={{0,0},{1,4},{2,2},{3,6},{4,1},{5,5},{6,3},{7,7},{8,8},{9,12},{10,1... | collective-permute-start | bytes 393224 | tf_op jit(solution)/shard_map/ppermute | solution.py:177
  4.4 4.3 %collective-permute-start.7 = (f32[128,512]{1,0:T(8,128)S(1)}, f32[128,512]{1,0:T(8,128)S(1)}, u32[]{:S(2)}, u32[]{:S(2)}) collective-permute-start(f32[128,512]{1,0:T(8,128)S(1)} %bitcast.6), channel_id=1, source_target_pairs={{0,4},{4,0},{8,12},{12,8},{16,20},{20,16},{24,28},{28,24},{1,5},{5... | collective-permute-start | bytes 786440 | tf_op jit(solution)/shard_map/ppermute | solution.py:17
  8.6 1.5 %collective-permute-start.1 = (f32[2,128,128]{2,1,0:T(8,128)S(1)}, f32[2,128,128]{2,1,0:T(8,128)S(1)}, u32[]{:S(2)}, u32[]{:S(2)}) collective-permute-start(f32[2,128,128]{2,1,0:T(8,128)S(1)} %collective-permute-done.refs_0_), channel_id=1, source_target_pairs={{0,2},{1,3},{2,0},{3,1},{4,6},{5,7},{6,4},{7,5},{8,10},{9,11},{10,... | collective-permute-start | bytes 393224 | tf_op jit(solution)/shard_map/ppermute | solution.py:17
  10.2 3.6 %collective-permute-start.6 = (f32[128,128]{1,0:T(8,128)S(1)}, f32[128,128]{1,0:T(8,128)S(1)}, u32[]{:S(2)}, u32[]{:S(2)}) collective-permute-start(f32[128,128]{1,0:T(8,128)S(1)} %get-tuple-element.14.refs_4_), channel_id=1, source_target_pairs={{0,24},{4,28},{8,16},{12,20},{16,8},{20,12},{24,0},{28,4},{1,25},{... | collective-permute-start | bytes 196616 | tf_op jit(solution)/shard_map/ppermute | solution.py:17
  13.8 2.2 %collective-permute-start.2 = (f32[2,128,128]{2,1,0:T(8,128)S(1)}, f32[2,128,128]{2,1,0:T(8,128)S(1)}, u32[]{:S(2)}, u32[]{:S(2)}) collective-permute-start(f32[2,128,128]{2,1,0:T(8,128)S(1)} %collective-permute-done.refs_0_), channel_id=1, source_target_pairs={{0,1},{1,0},{2,3},{3,2},{4,5},{5,4},{6,7},{7,6},{8,9},{9,8},{10,11... | collective-permute-start | bytes 393224 | tf_op jit(solution)/shard_map/ppermute | solution.py:17
  16.0 2.1 %collective-permute-start.5 = (f32[128,128]{1,0:T(8,128)S(1)}, f32[128,128]{1,0:T(8,128)S(1)}, u32[]{:S(2)}, u32[]{:S(2)}) collective-permute-start(f32[128,128]{1,0:T(8,128)S(1)} %get-tuple-element.14.refs_4_), channel_id=1, source_target_pairs={{0,16},{4,20},{8,24},{12,28},{16,0},{20,4},{24,8},{28,12},{1,17},{... | collective-permute-start | bytes 196616 | tf_op jit(solution)/shard_map/ppermute | solution.py:17
  18.1 1.6 %collective-permute-start.4 = (f32[128,128]{1,0:T(8,128)S(1)}, f32[128,128]{1,0:T(8,128)S(1)}, u32[]{:S(2)}, u32[]{:S(2)}) collective-permute-start(f32[128,128]{1,0:T(8,128)S(1)} %get-tuple-element.14.refs_4_), channel_id=1, source_target_pairs={{0,8},{4,12},{8,0},{12,4},{16,24},{20,28},{24,16},{28,20},{1,9},{5... | collective-permute-start | bytes 196616 | tf_op jit(solution)/shard_map/ppermute | solution.py:17
  19.7 3.2 %collective-permute-done.5.refs_6_ = f32[128,128]{1,0:T(8,128)S(1)} collective-permute-done((f32[128,128]{1,0:T(8,128)S(1)}, f32[128,128]{1,0:T(8,128)S(1)}, u32[]{:S(2)}, u32[]{:S(2)}) %collective-permute-start.5) | collective-permute-done | bytes 65568 | tf_op jit(solution)/shard_map/ppermute | solution.py:17
  22.9 0.6 %collective-permute-done.4.refs_5_ = f32[128,128]{1,0:T(8,128)S(1)} collective-permute-done((f32[128,128]{1,0:T(8,128)S(1)}, f32[128,128]{1,0:T(8,128)S(1)}, u32[]{:S(2)}, u32[]{:S(2)}) %collective-permute-start.4) | collective-permute-done | bytes 65568 | tf_op jit(solution)/shard_map/ppermute | solution.py:17
  23.5 1.6 %shard_map.60 = (f32[512,128]{1,0:T(8,128)}, f32[32,128]{1,0:T(8,128)S(1)}, f32[32,128]{1,0:T(8,128)S(1)}, f32[32,128]{1,0:T(8,128)S(1)}, f32[32,128]{1,0:T(8,12...) custom-call(f32[2,128,128]{2,1,0:T(8,128)S(1)} %collective-permute-done.r, ...), custom_call_target="tpu_custom_call" | custom-call | flops 1000 | bytes 1000 | tf_op jit(solution)/shard_map/pallas_call | solution.py:114
  25.1 6.9 %all-to-all-start = ((f32[8,64,128]{2,1,0:T(8,128)}), f32[8,64,128]{2,1,0:T(8,128)S(1)}, u32[]{:S(2)}, u32[]{:S(2)}) async-start(f32[8,64,128]{2,1,0:T(8,128)} %bitcast.4), calls=%async_computation | async-start | bytes 524288 | tf_op jit(solution)/shard_map/all_to_all | solution.py:199
  32.0 1.4 %collective-permute-start.9 = (f32[32,128]{1,0:T(8,128)S(1)}, f32[32,128]{1,0:T(8,128)S(1)}, u32[]{:S(2)}, u32[]{:S(2)}) collective-permute-start(f32[32,128]{1,0:T(8,128)S(1)} %get-tuple-element.17), channel_id=1, source_target_pairs={{0,2},{1,3},{2,0},{3,1},{4,6},{5,7},{6,4},{7,5},{8,10},{9,11},{10,... | collective-permute-start | bytes 49160 | tf_op jit(solution)/shard_map/ppermute | solution.py:139
  33.4 0.5 %collective-permute-start.10 = (f32[32,128]{1,0:T(8,128)S(1)}, f32[32,128]{1,0:T(8,128)S(1)}, u32[]{:S(2)}, u32[]{:S(2)}) collective-permute-start(f32[32,128]{1,0:T(8,128)S(1)} %get-tuple-element.18), channel_id=1, source_target_pairs={{0,3},{1,2},{2,1},{3,0},{4,7},{5,6},{6,5},{7,4},{8,11},{9,10},{10,... | collective-permute-start | bytes 49160 | tf_op jit(solution)/shard_map/ppermute | solution.py:139
  33.9 2.0 %collective-permute-start.11 = (f32[32,128]{1,0:T(8,128)S(1)}, f32[32,128]{1,0:T(8,128)S(1)}, u32[]{:S(2)}, u32[]{:S(2)}) collective-permute-start(f32[32,128]{1,0:T(8,128)S(1)} %get-tuple-element.19), channel_id=1, source_target_pairs={{0,4},{1,5},{2,6},{3,7},{4,0},{5,1},{6,2},{7,3},{8,12},{9,13},{10,... | collective-permute-start | bytes 49160 | tf_op jit(solution)/shard_map/ppermute | solution.py:139
  35.9 2.4 %collective-permute-start.13 = (f32[32,128]{1,0:T(8,128)S(1)}, f32[32,128]{1,0:T(8,128)S(1)}, u32[]{:S(2)}, u32[]{:S(2)}) collective-permute-start(f32[32,128]{1,0:T(8,128)S(1)} %get-tuple-element.21), channel_id=1, source_target_pairs={{0,6},{1,7},{2,4},{3,5},{4,2},{5,3},{6,0},{7,1},{8,14},{9,15},{10,... | collective-permute-start | bytes 49160 | tf_op jit(solution)/shard_map/ppermute | solution.py:139
  38.5 0.6 %collective-permute-done.12.refs_5_ = f32[32,128]{1,0:T(8,128)S(1)} collective-permute-done((f32[32,128]{1,0:T(8,128)S(1)}, f32[32,128]{1,0:T(8,128)S(1)}, u32[]{:S(2)}, u32[]{:S(2)}) %collective-permute-start.12) | collective-permute-done | bytes 16416 | tf_op jit(solution)/shard_map/ppermute | solution.py:139
  39.1 1.5 %collective-permute-done.13.refs_6_ = f32[32,128]{1,0:T(8,128)S(1)} collective-permute-done((f32[32,128]{1,0:T(8,128)S(1)}, f32[32,128]{1,0:T(8,128)S(1)}, u32[]{:S(2)}, u32[]{:S(2)}) %collective-permute-start.13) | collective-permute-done | bytes 16416 | tf_op jit(solution)/shard_map/ppermute | solution.py:139
  40.5 1.8 %collective-permute-done.14.refs_7_ = f32[32,128]{1,0:T(8,128)S(1)} collective-permute-done((f32[32,128]{1,0:T(8,128)S(1)}, f32[32,128]{1,0:T(8,128)S(1)}, u32[]{:S(2)}, u32[]{:S(2)}) %collective-permute-start.14) | collective-permute-done | bytes 16416 | tf_op jit(solution)/shard_map/ppermute | solution.py:139
  42.3 0.6 %shard_map.61 = f32[32,512]{1,0:T(8,128)} custom-call(f32[32,128]{1,0:T(8,128)S(1)} %get-tuple-element.15.refs_0_, f32[32,128]{1,0:T(8,128)S(1)} %collective-permute-done.8.refs_1_, f32[32,128]{1,0:T(8,128)S(1)} %collective-permute-done.9.refs_2_, f32[32,128]{1,0:T(8,128)S(1)} %collective-permute-done.10.refs_3_, ...), custom_call_target="tpu_custom_call" | custom-call | flops 1000 | bytes 1000 | tf_op jit(solution)/shard_map/pallas_call | solution.py:159
  43.0 0.6 %reduce_sum.9 = f32[64,128]{1,0:T(8,128)} reduce(f32[8,64,128]{2,1,0:T(8,128)S(1)} %all-to-all-done, f32[]{:T(128)} %constant.0.clone.1), dimensions={0}, to_apply=%region_0.0 | reduce | flops 57344 | bytes 294916 | tf_op jit(solution)/shard_map/reduce_sum | solution.py:200
  (22 shorter events, 0.2 us)
Async XLA Ops:
  0.6 0.7 %copy-start.4 = (s32[1,1,2,1]{2,3,1,0:T(1,128)S(1)}, s32[1,1,2,1]{2,3,1,0:T(1,128)}, u32[]{:S(2)}) copy-start(s32[1,1,2,1]{2,3,1,0:T(1,128)} %param.5) | copy-start | bytes 28
  1.3 0.9 %copy-start = (f32[1,1,128,512]{3,2,1,0:T(8,128)S(1)}, f32[1,1,128,512]{3,2,1,0:T(8,128)}, u32[]{:S(2)}) copy-start(f32[1,1,128,512]{3,2,1,0:T(8,128)} %param.6) | copy-start | bytes 786436
  2.2 0.9 %copy-start.2 = (f32[1,1,128,2,1,128]{5,4,3,2,1,0:T(1,128)S(1)}, f32[1,1,128,2,1,128]{5,4,3,2,1,0:T(1,128)}, u32[]{:S(2)}) copy-start(f32[1,1,128,2,1,128]{5,4,3,2,1,0:T(1,128)} %param.4) | copy-start | bytes 393220
  3.1 20.4 %copy-start.1 = (f32[1,1,128,512]{3,2,1,0:T(8,128)S(1)}, f32[1,1,128,512]{3,2,1,0:T(8,128)}, u32[]{:S(2)}) copy-start(f32[1,1,128,512]{3,2,1,0:T(8,128)} %param.6) | copy-start | bytes 786436
  3.1 20.4 %copy-start.3 = (f32[64,128]{1,0:T(8,128)S(1)}, f32[64,128]{1,0:T(8,128)}, u32[]{:S(2)}) copy-start(f32[64,128]{1,0:T(8,128)} %refs_10_.1) | copy-start | bytes 98308
  3.7 4.9 %collective-permute-start = (f32[2,128,128]{2,1,0:T(8,128)S(1)}, f32[2,128,128]{2,1,0:T(8,128)S(1)}, u32[]{:S(2)}, u32[]{:S(2)}) collective-permute-start(f32[2,128,128]{2,1,0:T(8,128)S(1)} %get-tuple-element.13), channel_id=1, source_target_pairs={{0,0},{1,4},{2,2},{3,6},{4,1},{5,5},{6,3},{7,7},{8,8},{9,12},{10,1... | collective-permute-start | bytes 393224 | tf_op jit(solution)/shard_map/ppermute | solution.py:177
  4.4 19.1 %collective-permute-start.7 = (f32[128,512]{1,0:T(8,128)S(1)}, f32[128,512]{1,0:T(8,128)S(1)}, u32[]{:S(2)}, u32[]{:S(2)}) collective-permute-start(f32[128,512]{1,0:T(8,128)S(1)} %bitcast.6), channel_id=1, source_target_pairs={{0,4},{4,0},{8,12},{12,8},{16,20},{20,16},{24,28},{28,24},{1,5},{5... | collective-permute-start | bytes 786440 | tf_op jit(solution)/shard_map/ppermute | solution.py:17
  8.6 7.4 %collective-permute-start.1 = (f32[2,128,128]{2,1,0:T(8,128)S(1)}, f32[2,128,128]{2,1,0:T(8,128)S(1)}, u32[]{:S(2)}, u32[]{:S(2)}) collective-permute-start(f32[2,128,128]{2,1,0:T(8,128)S(1)} %collective-permute-done.refs_0_), channel_id=1, source_target_pairs={{0,2},{1,3},{2,0},{3,1},{4,6},{5,7},{6,4},{7,5},{8,10},{9,11},{10,... | collective-permute-start | bytes 393224 | tf_op jit(solution)/shard_map/ppermute | solution.py:17
  10.2 8.0 %collective-permute-start.6 = (f32[128,128]{1,0:T(8,128)S(1)}, f32[128,128]{1,0:T(8,128)S(1)}, u32[]{:S(2)}, u32[]{:S(2)}) collective-permute-start(f32[128,128]{1,0:T(8,128)S(1)} %get-tuple-element.14.refs_4_), channel_id=1, source_target_pairs={{0,24},{4,28},{8,16},{12,20},{16,8},{20,12},{24,0},{28,4},{1,25},{... | collective-permute-start | bytes 196616 | tf_op jit(solution)/shard_map/ppermute | solution.py:17
  13.8 9.7 %collective-permute-start.2 = (f32[2,128,128]{2,1,0:T(8,128)S(1)}, f32[2,128,128]{2,1,0:T(8,128)S(1)}, u32[]{:S(2)}, u32[]{:S(2)}) collective-permute-start(f32[2,128,128]{2,1,0:T(8,128)S(1)} %collective-permute-done.refs_0_), channel_id=1, source_target_pairs={{0,1},{1,0},{2,3},{3,2},{4,5},{5,4},{6,7},{7,6},{8,9},{9,8},{10,11... | collective-permute-start | bytes 393224 | tf_op jit(solution)/shard_map/ppermute | solution.py:17
  16.0 7.5 %collective-permute-start.3 = (f32[2,128,128]{2,1,0:T(8,128)S(1)}, f32[2,128,128]{2,1,0:T(8,128)S(1)}, u32[]{:S(2)}, u32[]{:S(2)}) collective-permute-start(f32[2,128,128]{2,1,0:T(8,128)S(1)} %collective-permute-done.1.refs_1_), channel_id=1, source_target_pairs={{0,1},{1,0},{2,3},{3,2},{4,5},{5,4},{6,7},{7,6},{8,9},{9,8},{10,11... | collective-permute-start | bytes 393224 | tf_op jit(solution)/shard_map/ppermute | solution.py:17
  16.0 6.9 %collective-permute-start.5 = (f32[128,128]{1,0:T(8,128)S(1)}, f32[128,128]{1,0:T(8,128)S(1)}, u32[]{:S(2)}, u32[]{:S(2)}) collective-permute-start(f32[128,128]{1,0:T(8,128)S(1)} %get-tuple-element.14.refs_4_), channel_id=1, source_target_pairs={{0,16},{4,20},{8,24},{12,28},{16,0},{20,4},{24,8},{28,12},{1,17},{... | collective-permute-start | bytes 196616 | tf_op jit(solution)/shard_map/ppermute | solution.py:17
  18.1 5.4 %collective-permute-start.4 = (f32[128,128]{1,0:T(8,128)S(1)}, f32[128,128]{1,0:T(8,128)S(1)}, u32[]{:S(2)}, u32[]{:S(2)}) collective-permute-start(f32[128,128]{1,0:T(8,128)S(1)} %get-tuple-element.14.refs_4_), channel_id=1, source_target_pairs={{0,8},{4,12},{8,0},{12,4},{16,24},{20,28},{24,16},{28,20},{1,9},{5... | collective-permute-start | bytes 196616 | tf_op jit(solution)/shard_map/ppermute | solution.py:17
  25.1 17.9 %all-to-all-start = ((f32[8,64,128]{2,1,0:T(8,128)}), f32[8,64,128]{2,1,0:T(8,128)S(1)}, u32[]{:S(2)}, u32[]{:S(2)}) async-start(f32[8,64,128]{2,1,0:T(8,128)} %bitcast.4), calls=%async_computation | async-start | bytes 524288 | tf_op jit(solution)/shard_map/all_to_all | solution.py:199
  32.0 3.9 %collective-permute-start.8 = (f32[32,128]{1,0:T(8,128)S(1)}, f32[32,128]{1,0:T(8,128)S(1)}, u32[]{:S(2)}, u32[]{:S(2)}) collective-permute-start(f32[32,128]{1,0:T(8,128)S(1)} %get-tuple-element.16), channel_id=1, source_target_pairs={{0,1},{1,0},{2,3},{3,2},{4,5},{5,4},{6,7},{7,6},{8,9},{9,8},{10,11... | collective-permute-start | bytes 49160 | tf_op jit(solution)/shard_map/ppermute | solution.py:139
  32.0 6.2 %collective-permute-start.9 = (f32[32,128]{1,0:T(8,128)S(1)}, f32[32,128]{1,0:T(8,128)S(1)}, u32[]{:S(2)}, u32[]{:S(2)}) collective-permute-start(f32[32,128]{1,0:T(8,128)S(1)} %get-tuple-element.17), channel_id=1, source_target_pairs={{0,2},{1,3},{2,0},{3,1},{4,6},{5,7},{6,4},{7,5},{8,10},{9,11},{10,... | collective-permute-start | bytes 49160 | tf_op jit(solution)/shard_map/ppermute | solution.py:139
  33.4 5.1 %collective-permute-start.10 = (f32[32,128]{1,0:T(8,128)S(1)}, f32[32,128]{1,0:T(8,128)S(1)}, u32[]{:S(2)}, u32[]{:S(2)}) collective-permute-start(f32[32,128]{1,0:T(8,128)S(1)} %get-tuple-element.18), channel_id=1, source_target_pairs={{0,3},{1,2},{2,1},{3,0},{4,7},{5,6},{6,5},{7,4},{8,11},{9,10},{10,... | collective-permute-start | bytes 49160 | tf_op jit(solution)/shard_map/ppermute | solution.py:139
  33.9 4.6 %collective-permute-start.11 = (f32[32,128]{1,0:T(8,128)S(1)}, f32[32,128]{1,0:T(8,128)S(1)}, u32[]{:S(2)}, u32[]{:S(2)}) collective-permute-start(f32[32,128]{1,0:T(8,128)S(1)} %get-tuple-element.19), channel_id=1, source_target_pairs={{0,4},{1,5},{2,6},{3,7},{4,0},{5,1},{6,2},{7,3},{8,12},{9,13},{10,... | collective-permute-start | bytes 49160 | tf_op jit(solution)/shard_map/ppermute | solution.py:139
  35.9 3.2 %collective-permute-start.12 = (f32[32,128]{1,0:T(8,128)S(1)}, f32[32,128]{1,0:T(8,128)S(1)}, u32[]{:S(2)}, u32[]{:S(2)}) collective-permute-start(f32[32,128]{1,0:T(8,128)S(1)} %get-tuple-element.20), channel_id=1, source_target_pairs={{0,5},{1,4},{2,7},{3,6},{4,1},{5,0},{6,3},{7,2},{8,13},{9,12},{10,... | collective-permute-start | bytes 49160 | tf_op jit(solution)/shard_map/ppermute | solution.py:139
  35.9 4.6 %collective-permute-start.13 = (f32[32,128]{1,0:T(8,128)S(1)}, f32[32,128]{1,0:T(8,128)S(1)}, u32[]{:S(2)}, u32[]{:S(2)}) collective-permute-start(f32[32,128]{1,0:T(8,128)S(1)} %get-tuple-element.21), channel_id=1, source_target_pairs={{0,6},{1,7},{2,4},{3,5},{4,2},{5,3},{6,0},{7,1},{8,14},{9,15},{10,... | collective-permute-start | bytes 49160 | tf_op jit(solution)/shard_map/ppermute | solution.py:139
  38.3 4.1 %collective-permute-start.14 = (f32[32,128]{1,0:T(8,128)S(1)}, f32[32,128]{1,0:T(8,128)S(1)}, u32[]{:S(2)}, u32[]{:S(2)}) collective-permute-start(f32[32,128]{1,0:T(8,128)S(1)} %get-tuple-element.22), channel_id=1, source_target_pairs={{0,7},{1,6},{2,5},{3,4},{4,3},{5,2},{6,1},{7,0},{8,15},{9,14},{10,... | collective-permute-start | bytes 49160 | tf_op jit(solution)/shard_map/ppermute | solution.py:139

commit v9 on v7

--- a/solution.py
+++ b/solution.py
@@ -9,6 +9,7 @@
 
 LANES = 128
 WHOLE = pl.BlockSpec(memory_space=pltpu.VMEM)
+ROOM = pltpu.CompilerParams(vmem_limit_bytes=16 * 1024 * 1024)
 LIGHT = pl.CostEstimate(flops=1000, bytes_accessed=1000, transcendentals=0)
 
 
@@ -33,8 +34,7 @@
 
 def prepare_kernel(presence, blocks, factor, masked, copies):
     count, rows, span = copies.shape
-    first = pl.multiple_of(lax.axis_index("col") * span, LANES)
-    mine = factor[:, pl.ds(first, span)]
+    mine = factor[:, pl.ds(pl.multiple_of(lax.axis_index("col") * span, LANES), span)]
     for i in range(count):
         copies[i] = mine
     block_cols, _, order = masked.shape
@@ -68,13 +68,11 @@
     )(presence, blocks, own)
 
 
-def middle_kernel(count, *refs):
+def partials_kernel(count, *refs):
     pieces = refs[: 2 * count]
-    columns, own, near, dinv, terms = refs[2 * count : 2 * count + 5]
-    outward = refs[2 * count + 5 :]
-    block_cols, rows, order = pieces[0].shape
+    columns, kept, sent = refs[2 * count :]
+    block_cols, rows, _ = pieces[0].shape
     col_index = lax.axis_index("col")
-    row_index = lax.axis_index("row")
     left, right = [], []
     for t in range(count):
         for b in range(block_cols):
@@ -82,79 +80,75 @@
             right.append(columns[b * count + ((col_index >> 1) ^ t)])
     both = product(jnp.concatenate(left, axis=1), jnp.concatenate(right, axis=0), ((1,), (0,)))
     first, second = both[:rows], both[rows:]
-    same = (row_index & 1) == (col_index & 1)
-    mine = jnp.where(same, first, second)
-    other = jnp.where(same, second, first)
-    factors = jnp.concatenate([own[...], near[...]], axis=0)
-    terms[...] = product(factors, jnp.concatenate([mine, other], axis=0), ((0,), (0,)))
+    same = (lax.axis_index("row") & 1) == (col_index & 1)
+    kept[...] = jnp.where(same, first, second)
+    sent[...] = jnp.where(same, second, first)
+
+
+def partials(pieces, columns):
+    part = jax.ShapeDtypeStruct((pieces[0].shape[1], columns.shape[2]), jnp.float32)
+    return pl.pallas_call(
+        functools.partial(partials_kernel, len(pieces) // 2),
+        out_shape=(part, part),
+        in_specs=[WHOLE] * (len(pieces) + 1),
+        out_specs=(WHOLE, WHOLE),
+        cost_estimate=LIGHT,
+        compiler_params=ROOM,
+    )(*pieces, columns)
+
+
+def finish_kernel(order, kept, got, own, dinv, terms, *refs):
+    outward, update = refs[:-1], refs[-1]
+    rows = kept.shape[0]
+    update[...] = kept[...] + got[...]
+    terms[...] = product(own[...], update[...], ((0,), (0,)))
     tall = dinv.shape[0]
-    here = pl.ds(pl.multiple_of(row_index * tall, 8), tall)
+    here = pl.ds(pl.multiple_of(lax.axis_index("row") * tall, 8), tall)
     terms[here, :] = terms[here, :] + dinv[...]
-
-    scratch = outward[-1]
-    flips = len(outward[:-1]) // 2
-    share = order // flips
-    for near_row, value in enumerate((mine, other)):
-        scratch[...] = -value
-        for flip in range(flips):
-            start = (col_index ^ flip) * share
-            for a in range(rows // order):
-                picked = scratch[pl.ds(pl.multiple_of(a * order + start, 8), share), :]
-                outward[near_row * flips + flip][pl.ds(a * share, share), :] = picked
-
-
-def middle(pieces, columns, own, near, dinv, flips):
+    share = order // len(outward)
+    for flip, piece in enumerate(outward):
+        start = (lax.axis_index("col") ^ flip) * share
+        for a in range(rows // order):
+            picked = update[pl.ds(pl.multiple_of(a * order + start, 8), share), :]
+            piece[pl.ds(a * share, share), :] = -picked
+
+
+def finish(kept, got, own, dinv, order, flips):
     rows, width = own.shape
-    span = columns.shape[2]
+    span = kept.shape[1]
     part = jax.ShapeDtypeStruct((rows // flips, span), jnp.float32)
     return pl.pallas_call(
-        functools.partial(middle_kernel, len(pieces) // 2),
-        out_shape=(jax.ShapeDtypeStruct((width, span), jnp.float32),) + (part,) * (2 * flips),
-        in_specs=[WHOLE] * (len(pieces) + 4),
-        out_specs=(WHOLE,) * (1 + 2 * flips),
+        functools.partial(finish_kernel, order),
+        out_shape=(jax.ShapeDtypeStruct((width, span), jnp.float32),) + (part,) * flips,
+        in_specs=[WHOLE] * 4,
+        out_specs=(WHOLE,) * (1 + flips),
         scratch_shapes=[pltpu.VMEM((rows, span), jnp.float32)],
         cost_estimate=LIGHT,
-        compiler_params=pltpu.CompilerParams(vmem_limit_bytes=32 * 1024 * 1024),
-    )(*pieces, columns, own, near, dinv)
-
-
-def exchange(outward, flips):
-    groups_row = lax.axis_size("row")
-    groups_col = lax.axis_size("col")
-    arrived = []
-    for index, piece in enumerate(outward):
-        near_row, flip = divmod(index, flips)
-        pairs = [
-            (r * groups_col + c, (r ^ near_row) * groups_col + (c ^ flip))
-            for r in range(groups_row)
-            for c in range(groups_col)
-        ]
-        arrived.append(lax.ppermute(piece, ("row", "col"), pairs) if index else piece)
-    return arrived
+        compiler_params=ROOM,
+    )(kept, got, own, dinv)
 
 
 def collect_kernel(*refs):
     out = refs[-1]
-    flips = len(refs) // 2
     span = refs[0].shape[1]
-    for flip in range(flips):
+    for flip, piece in enumerate(refs[:-1]):
         first = pl.multiple_of((lax.axis_index("col") ^ flip) * span, LANES)
-        out[:, pl.ds(first, span)] = refs[flip][...] + refs[flips + flip][...]
+        out[:, pl.ds(first, span)] = piece[...]
 
 
 def collect(arrived):
-    flips = len(arrived) // 2
+    flips = len(arrived)
     share, span = arrived[0].shape
     if span % LANES:
         me = lax.axis_index("col")
-        held = [arrived[flip] + arrived[flips + flip] for flip in range(flips)]
-        return jnp.concatenate([lax.select_n(me ^ j, *held) for j in range(flips)], axis=1)
+        return jnp.concatenate([lax.select_n(me ^ j, *arrived) for j in range(flips)], axis=1)
     return pl.pallas_call(
         collect_kernel,
         out_shape=jax.ShapeDtypeStruct((share, span * flips), jnp.float32),
-        in_specs=[WHOLE] * len(arrived),
+        in_specs=[WHOLE] * flips,
         out_specs=WHOLE,
         cost_estimate=LIGHT,
+        compiler_params=ROOM,
     )(*arrived)
 
 
@@ -186,16 +180,16 @@
     lines = [list(range(bit, groups_row, 2)) for bit in range(2)]
     columns = lax.all_to_all(copies, "row", 0, 0, axis_index_groups=lines)
     columns = columns.reshape(groups_row // 2, block_rows, order, span).transpose(1, 0, 2, 3)
-    columns = columns.reshape(-1, order, span)
     pieces = pair_rows(masked)
-    near = flipped(own, "row", 1)
-
-    terms, *outward = middle(pieces, columns, own, near, dinv, groups_col)
+
+    kept, sent = partials(pieces, columns.reshape(-1, order, span))
+    got = flipped(sent, "row", 1)
+    terms, *outward = finish(kept, got, own, dinv, order, groups_col)
     terms = lax.all_to_all(terms.reshape(groups_row, width // groups_row, span), "row", 0, 0)
     diag_block = terms.sum(axis=0)
 
-    off_diag = collect(exchange(outward, groups_col))
-    return (off_diag.reshape(block_rows, 1, share, width), diag_block)
+    arrived = [outward[0]] + [flipped(outward[f], "col", f) for f in range(1, groups_col)]
+    return (collect(arrived).reshape(block_rows, 1, share, width), diag_block)
 
 
 def solution(mesh):

time: 40.8 us -> 38.9 us (0.953)
  waiting for transfers between devices: 9.11 us -> 14.5 us
  starting transfers between devices: 23.9 us -> 19 us
  local copies, waits for them, and re-layouts: 1.19 us -> 0.01 us
  Pallas kernels: 4.83 us -> 3.81 us
    ppermute x7 -> x0, starting transfers between devices: 6.66 us -> none  [exchange(): lax.ppermute(piece, ('row', 'col'), pairs)]
    ppermute x4 -> x7, waiting for transfers between devices: 5.12 us -> 9.59 us  [flipped(): lax.ppermute(value, axis, [(i, i ^ flip) for i in range(lax.axis_size(axi...]
    ppermute x4 -> x7, starting transfers between devices: 3.41 us -> 7.37 us  [flipped(): lax.ppermute(value, axis, [(i, i ^ flip) for i in range(lax.axis_size(axi...]
    ppermute x7 -> x0, waiting for transfers between devices: 3.85 us -> none  [exchange(): lax.ppermute(piece, ('row', 'col'), pairs)]
    all_to_all x1, waiting for transfers between devices: 0.01 us -> 3.74 us  [local(): lax.all_to_all(terms.reshape(groups_row, width // groups_row, span), 'row...]
    all_to_all x1, starting transfers between devices: 5.82 us -> 3.76 us  [local(): lax.all_to_all(terms.reshape(groups_row, width // groups_row, span), 'row...]
    unnamed x20 -> x4, local copies, waits for them, and re-layouts: 1.19 us -> 0.01 us
    all_to_all x1, waiting for transfers between devices: 0.13 us -> 1.15 us  [local(): columns = lax.all_to_all(copies, 'row', 0, 0, axis_index_groups=lines)]
  transfers between devices with their start and end apart: 14 -> 10, of which waited for: 7 -> 7; matrix products, arithmetic and copies ran while one was open for 0% -> 0% of each run, Pallas kernels for 4% -> 2%
where the time goes in v9:
time: 38.9 us; the launch traced here: 38.6 us
  starting transfers between devices  19 us (49%)
  waiting for transfers between devices  14.5 us (37%)
  Pallas kernels  3.81 us (10%)
  between operations  0.66 us (2%)
  other arithmetic  0.63 us (2%)
    ppermute x7, waiting for transfers between devices, flipped(): lax.ppermute(value, axis, [(i, i ^ flip) for i in range(lax.axis_size(axi...  9.59 us
    ppermute x7, starting transfers between devices, flipped(): lax.ppermute(value, axis, [(i, i ^ flip) for i in range(lax.axis_size(axi...  7.37 us
    all_to_all x1, starting transfers between devices, local(): columns = lax.all_to_all(copies, 'row', 0, 0, axis_index_groups=lines)  6.32 us
    all_to_all x1, starting transfers between devices, local(): lax.all_to_all(terms.reshape(groups_row, width // groups_row, span), 'row...  3.76 us
    all_to_all x1, waiting for transfers between devices, local(): lax.all_to_all(terms.reshape(groups_row, width // groups_row, span), 'row...  3.74 us
    pallas_call x1, Pallas kernels, prepare(): pl.pallas_call(prepare_kernel, out_shape=(jax.ShapeDtypeStruct((block_col...  1.8 us
    ppermute x1, starting transfers between devices, pair_rows(): held = lax.ppermute(masked, ('row', 'col'), cross)  1.55 us
    all_to_all x1, waiting for transfers between devices, local(): columns = lax.all_to_all(copies, 'row', 0, 0, axis_index_groups=lines)  1.15 us
  transfers between devices with their start and end apart: 10, of which 7 were waited for; matrix products, arithmetic and copies ran while one was open for 0% of the time, Pallas kernels for 2%

profile of v9, /device:TPU:0, one launch (start us, length us, event | category | flops | bytes accessed | tf_op | source)
XLA Modules:
  0.0 38.6 jit_solution(18200674752892342109)
XLA Ops:
  0.6 1.8 %shard_map.59 = (f32[2,128,128]{2,1,0:T(8,128)}, f32[4,128,128]{2,1,0:T(8,128)}) custom-call(s32[2]{0:T(128)} %bitcast.9, f32[256,128]{1,0:T(8,128)} %bitcast.7, f32[128,512]{1,0:T(8,128)} %bitcast.5), custom_call_target="tpu_custom_call" | custom-call | flops 1000 | bytes 1000 | tf_op jit(solution)/shard_map/pallas_call | solution.py:59
  2.4 1.6 %collective-permute-start = (f32[2,128,128]{2,1,0:T(8,128)}, f32[2,128,128]{2,1,0:T(8,128)S(1)}, u32[]{:S(2)}, u32[]{:S(2)}) collective-permute-start(f32[2,128,128]{2,1,0:T(8,128)} %get-tuple-element.11), channel_id=1, source_target_pairs={{0,0},{1,4},{2,2},{3,6},{4,1},{5,5},{6,3},{7,7},{8,8},{9,12},{10,1... | collective-permute-start | bytes 393224 | tf_op jit(solution)/shard_map/ppermute | solution.py:163
  4.0 6.3 %all-to-all-start = ((f32[4,128,128]{2,1,0:T(8,128)}), f32[4,128,128]{2,1,0:T(8,128)S(1)}, u32[]{:S(2)}, u32[]{:S(2)}) async-start(f32[4,128,128]{2,1,0:T(8,128)} %get-tuple-element.12), calls=%async_computation | async-start | bytes 524288 | tf_op jit(solution)/shard_map/all_to_all | solution.py:181
  10.3 0.0 collective-permute-done.refs_0_
  10.3 1.6 %collective-permute-start.1 = (f32[2,128,128]{2,1,0:T(8,128)S(1)}, f32[2,128,128]{2,1,0:T(8,128)S(1)}, u32[]{:S(2)}, u32[]{:S(2)}) collective-permute-start(f32[2,128,128]{2,1,0:T(8,128)S(1)} %collective-permute-done.refs_0_), channel_id=1, source_target_pairs={{0,2},{1,3},{2,0},{3,1},{4,6},{5,7},{6,4},{7,5},{8,10},{9,11},{10,... | collective-permute-start | bytes 393224 | tf_op jit(solution)/shard_map/ppermute | solution.py:17
  11.9 1.4 %collective-permute-start.2 = (f32[2,128,128]{2,1,0:T(8,128)S(1)}, f32[2,128,128]{2,1,0:T(8,128)S(1)}, u32[]{:S(2)}, u32[]{:S(2)}) collective-permute-start(f32[2,128,128]{2,1,0:T(8,128)S(1)} %collective-permute-done.refs_0_), channel_id=1, source_target_pairs={{0,1},{1,0},{2,3},{3,2},{4,5},{5,4},{6,7},{7,6},{8,9},{9,8},{10,11... | collective-permute-start | bytes 393224 | tf_op jit(solution)/shard_map/ppermute | solution.py:17
  13.3 2.8 %collective-permute-done.1.refs_1_ = f32[2,128,128]{2,1,0:T(8,128)S(1)} collective-permute-done((f32[2,128,128]{2,1,0:T(8,128)S(1)}, f32[2,128,128]{2,1,0:T(8,128)S(1)}, u32[]{:S(2)}, u32[]{:S(2)}) %collective-permute-start.1) | collective-permute-done | bytes 131104 | tf_op jit(solution)/shard_map/ppermute | solution.py:17
  16.1 0.8 %collective-permute-start.3 = (f32[2,128,128]{2,1,0:T(8,128)S(1)}, f32[2,128,128]{2,1,0:T(8,128)S(1)}, u32[]{:S(2)}, u32[]{:S(2)}) collective-permute-start(f32[2,128,128]{2,1,0:T(8,128)S(1)} %collective-permute-done.1.refs_1_), channel_id=1, source_target_pairs={{0,1},{1,0},{2,3},{3,2},{4,5},{5,4},{6,7},{7,6},{8,9},{9,8},{10,11... | collective-permute-start | bytes 393224 | tf_op jit(solution)/shard_map/ppermute | solution.py:17
  16.9 0.0 collective-permute-done.2.refs_2_
  16.9 1.0 %collective-permute-done.3.refs_3_ = f32[2,128,128]{2,1,0:T(8,128)S(1)} collective-permute-done((f32[2,128,128]{2,1,0:T(8,128)S(1)}, f32[2,128,128]{2,1,0:T(8,128)S(1)}, u32[]{:S(2)}, u32[]{:S(2)}) %collective-permute-start.3) | collective-permute-done | bytes 131104 | tf_op jit(solution)/shard_map/ppermute | solution.py:17
  17.9 1.2 %all-to-all-done.refs_4_ = f32[4,128,128]{2,1,0:T(8,128)S(1)} async-done(((f32[4,128,128]{2,1,0:T(8,128)}), f32[4,128,128]{2,1,0:T(8,128)S(1)}, u32[]{:S(2)}, u32[]{:S(2)}) %all-to-all-start) | async-done | bytes 262176 | tf_op jit(solution)/shard_map/all_to_all | solution.py:181
  19.0 0.4 shard_map.60
  19.4 1.7 %collective-permute-start.4 = (f32[128,128]{1,0:T(8,128)S(1)}, f32[128,128]{1,0:T(8,128)S(1)}, u32[]{:S(2)}, u32[]{:S(2)}) collective-permute-start(f32[128,128]{1,0:T(8,128)S(1)} %get-tuple-element.14), channel_id=1, source_target_pairs={{0,4},{4,0},{8,12},{12,8},{16,20},{20,16},{24,28},{28,24},{1,5},{5... | collective-permute-start | bytes 196616 | tf_op jit(solution)/shard_map/ppermute | solution.py:17
  21.1 2.9 %collective-permute-done.4.got = f32[128,128]{1,0:T(8,128)S(1)} collective-permute-done((f32[128,128]{1,0:T(8,128)S(1)}, f32[128,128]{1,0:T(8,128)S(1)}, u32[]{:S(2)}, u32[]{:S(2)}) %collective-permute-start.4) | collective-permute-done | bytes 65568 | tf_op jit(solution)/shard_map/ppermute | solution.py:17
  24.1 1.0 %shard_map.61 = (f32[512,128]{1,0:T(8,128)}, f32[32,128]{1,0:T(8,128)S(1)}, f32[32,128]{1,0:T(8,128)S(1)}, f32[32,128]{1,0:T(8,128)S(1)}, f32[32,128]{1,0:T(8,128)S(1)}) custom-call(f32[128,128]{1,0:T(8,128)S(1)} %get-tuple-element.13.kept, f32[128,128]{1,0:T(8,128)S(1)} %collective-permute-done.4.got, f32[128,512]{1,0:T(8,128)S(1)} %bitcast.6, ...), custom_call_target="tpu_custom_call" | custom-call | flops 1000 | bytes 1000 | tf_op jit(solution)/shard_map/pallas_call | solution.py:120
  25.1 3.8 %all-to-all-start.1 = ((f32[8,64,128]{2,1,0:T(8,128)}), f32[8,64,128]{2,1,0:T(8,128)S(1)}, u32[]{:S(2)}, u32[]{:S(2)}) async-start(f32[8,64,128]{2,1,0:T(8,128)} %bitcast.4), calls=%async_computation.1 | async-start | bytes 524288 | tf_op jit(solution)/shard_map/all_to_all | solution.py:188
  28.8 1.6 %collective-permute-start.6 = (f32[32,128]{1,0:T(8,128)S(1)}, f32[32,128]{1,0:T(8,128)S(1)}, u32[]{:S(2)}, u32[]{:S(2)}) collective-permute-start(f32[32,128]{1,0:T(8,128)S(1)} %get-tuple-element.17), channel_id=1, source_target_pairs={{0,2},{1,3},{2,0},{3,1},{4,6},{5,7},{6,4},{7,5},{8,10},{9,11},{10,... | collective-permute-start | bytes 49160 | tf_op jit(solution)/shard_map/ppermute | solution.py:17
  30.4 0.3 collective-permute-start.7
  30.7 0.0 collective-permute-done.5.refs_1_
  30.7 1.9 %collective-permute-done.6.refs_2_ = f32[32,128]{1,0:T(8,128)S(1)} collective-permute-done((f32[32,128]{1,0:T(8,128)S(1)}, f32[32,128]{1,0:T(8,128)S(1)}, u32[]{:S(2)}, u32[]{:S(2)}) %collective-permute-start.6) | collective-permute-done | bytes 16416 | tf_op jit(solution)/shard_map/ppermute | solution.py:17
  32.6 0.9 %collective-permute-done.7.refs_3_ = f32[32,128]{1,0:T(8,128)S(1)} collective-permute-done((f32[32,128]{1,0:T(8,128)S(1)}, f32[32,128]{1,0:T(8,128)S(1)}, u32[]{:S(2)}, u32[]{:S(2)}) %collective-permute-start.7) | collective-permute-done | bytes 16416 | tf_op jit(solution)/shard_map/ppermute | solution.py:17
  33.6 0.6 %shard_map.62 = f32[32,512]{1,0:T(8,128)} custom-call(f32[32,128]{1,0:T(8,128)S(1)} %get-tuple-element.15.refs_0_, f32[32,128]{1,0:T(8,128)S(1)} %collective-permute-done.5.refs_1_, f32[32,128]{1,0:T(8,128)S(1)} %collective-permute-done.6.refs_2_, f32[32,128]{1,0:T(8,128)S(1)} %collective-permute-done.7.refs_3_), custom_call_target="tpu_custom_call" | custom-call | flops 1000 | bytes 1000 | tf_op jit(solution)/shard_map/pallas_call | solution.py:145
  34.2 3.7 %all-to-all-done.1 = f32[8,64,128]{2,1,0:T(8,128)S(1)} async-done(((f32[8,64,128]{2,1,0:T(8,128)}), f32[8,64,128]{2,1,0:T(8,128)S(1)}, u32[]{:S(2)}, u32[]{:S(2)}) %all-to-all-start.1) | async-done | bytes 262176 | tf_op jit(solution)/shard_map/all_to_all | solution.py:188
  38.0 0.6 %reduce_sum.9 = f32[64,128]{1,0:T(8,128)} reduce(f32[8,64,128]{2,1,0:T(8,128)S(1)} %all-to-all-done.1, f32[]{:T(128)} %constant.0.clone.1), dimensions={0}, to_apply=%region_0.0 | reduce | flops 57344 | bytes 294916 | tf_op jit(solution)/shard_map/reduce_sum | solution.py:189
  (5 shorter events, 0.0 us)
Async XLA Ops:
  2.4 7.9 %collective-permute-start = (f32[2,128,128]{2,1,0:T(8,128)}, f32[2,128,128]{2,1,0:T(8,128)S(1)}, u32[]{:S(2)}, u32[]{:S(2)}) collective-permute-start(f32[2,128,128]{2,1,0:T(8,128)} %get-tuple-element.11), channel_id=1, source_target_pairs={{0,0},{1,4},{2,2},{3,6},{4,1},{5,5},{6,3},{7,7},{8,8},{9,12},{10,1... | collective-permute-start | bytes 393224 | tf_op jit(solution)/shard_map/ppermute | solution.py:163
  4.0 15.0 %all-to-all-start = ((f32[4,128,128]{2,1,0:T(8,128)}), f32[4,128,128]{2,1,0:T(8,128)S(1)}, u32[]{:S(2)}, u32[]{:S(2)}) async-start(f32[4,128,128]{2,1,0:T(8,128)} %get-tuple-element.12), calls=%async_computation | async-start | bytes 524288 | tf_op jit(solution)/shard_map/all_to_all | solution.py:181
  10.3 13.8 %copy-start = (f32[1,1,128,512]{3,2,1,0:T(8,128)S(1)}, f32[1,1,128,512]{3,2,1,0:T(8,128)}, u32[]{:S(2)}) copy-start(f32[1,1,128,512]{3,2,1,0:T(8,128)} %param.6) | copy-start | bytes 786436
  10.3 13.8 %copy-start.1 = (f32[64,128]{1,0:T(8,128)S(1)}, f32[64,128]{1,0:T(8,128)}, u32[]{:S(2)}) copy-start(f32[64,128]{1,0:T(8,128)} %dinv.1) | copy-start | bytes 98308
  10.3 5.8 %collective-permute-start.1 = (f32[2,128,128]{2,1,0:T(8,128)S(1)}, f32[2,128,128]{2,1,0:T(8,128)S(1)}, u32[]{:S(2)}, u32[]{:S(2)}) collective-permute-start(f32[2,128,128]{2,1,0:T(8,128)S(1)} %collective-permute-done.refs_0_), channel_id=1, source_target_pairs={{0,2},{1,3},{2,0},{3,1},{4,6},{5,7},{6,4},{7,5},{8,10},{9,11},{10,... | collective-permute-start | bytes 393224 | tf_op jit(solution)/shard_map/ppermute | solution.py:17
  11.9 5.0 %collective-permute-start.2 = (f32[2,128,128]{2,1,0:T(8,128)S(1)}, f32[2,128,128]{2,1,0:T(8,128)S(1)}, u32[]{:S(2)}, u32[]{:S(2)}) collective-permute-start(f32[2,128,128]{2,1,0:T(8,128)S(1)} %collective-permute-done.refs_0_), channel_id=1, source_target_pairs={{0,1},{1,0},{2,3},{3,2},{4,5},{5,4},{6,7},{7,6},{8,9},{9,8},{10,11... | collective-permute-start | bytes 393224 | tf_op jit(solution)/shard_map/ppermute | solution.py:17
  16.1 1.8 %collective-permute-start.3 = (f32[2,128,128]{2,1,0:T(8,128)S(1)}, f32[2,128,128]{2,1,0:T(8,128)S(1)}, u32[]{:S(2)}, u32[]{:S(2)}) collective-permute-start(f32[2,128,128]{2,1,0:T(8,128)S(1)} %collective-permute-done.1.refs_1_), channel_id=1, source_target_pairs={{0,1},{1,0},{2,3},{3,2},{4,5},{5,4},{6,7},{7,6},{8,9},{9,8},{10,11... | collective-permute-start | bytes 393224 | tf_op jit(solution)/shard_map/ppermute | solution.py:17
  19.4 4.7 %collective-permute-start.4 = (f32[128,128]{1,0:T(8,128)S(1)}, f32[128,128]{1,0:T(8,128)S(1)}, u32[]{:S(2)}, u32[]{:S(2)}) collective-permute-start(f32[128,128]{1,0:T(8,128)S(1)} %get-tuple-element.14), channel_id=1, source_target_pairs={{0,4},{4,0},{8,12},{12,8},{16,20},{20,16},{24,28},{28,24},{1,5},{5... | collective-permute-start | bytes 196616 | tf_op jit(solution)/shard_map/ppermute | solution.py:17
  25.1 12.9 %all-to-all-start.1 = ((f32[8,64,128]{2,1,0:T(8,128)}), f32[8,64,128]{2,1,0:T(8,128)S(1)}, u32[]{:S(2)}, u32[]{:S(2)}) async-start(f32[8,64,128]{2,1,0:T(8,128)} %bitcast.4), calls=%async_computation.1 | async-start | bytes 524288 | tf_op jit(solution)/shard_map/all_to_all | solution.py:188
  28.8 1.9 %collective-permute-start.5 = (f32[32,128]{1,0:T(8,128)S(1)}, f32[32,128]{1,0:T(8,128)S(1)}, u32[]{:S(2)}, u32[]{:S(2)}) collective-permute-start(f32[32,128]{1,0:T(8,128)S(1)} %get-tuple-element.16), channel_id=1, source_target_pairs={{0,1},{1,0},{2,3},{3,2},{4,5},{5,4},{6,7},{7,6},{8,9},{9,8},{10,11... | collective-permute-start | bytes 49160 | tf_op jit(solution)/shard_map/ppermute | solution.py:17
  28.8 3.8 %collective-permute-start.6 = (f32[32,128]{1,0:T(8,128)S(1)}, f32[32,128]{1,0:T(8,128)S(1)}, u32[]{:S(2)}, u32[]{:S(2)}) collective-permute-start(f32[32,128]{1,0:T(8,128)S(1)} %get-tuple-element.17), channel_id=1, source_target_pairs={{0,2},{1,3},{2,0},{3,1},{4,6},{5,7},{6,4},{7,5},{8,10},{9,11},{10,... | collective-permute-start | bytes 49160 | tf_op jit(solution)/shard_map/ppermute | solution.py:17
  30.4 3.2 %collective-permute-start.7 = (f32[32,128]{1,0:T(8,128)S(1)}, f32[32,128]{1,0:T(8,128)S(1)}, u32[]{:S(2)}, u32[]{:S(2)}) collective-permute-start(f32[32,128]{1,0:T(8,128)S(1)} %get-tuple-element.18), channel_id=1, source_target_pairs={{0,3},{1,2},{2,1},{3,0},{4,7},{5,6},{6,5},{7,4},{8,11},{9,10},{10,... | collective-permute-start | bytes 49160 | tf_op jit(solution)/shard_map/ppermute | solution.py:17

commit v10 on v9

--- a/solution.py
+++ b/solution.py
@@ -32,11 +32,9 @@
     return once(left_high, right_high) + (once(left_high, right_low) + once(left_low, right_high))
 
 
-def prepare_kernel(presence, blocks, factor, masked, copies):
-    count, rows, span = copies.shape
-    mine = factor[:, pl.ds(pl.multiple_of(lax.axis_index("col") * span, LANES), span)]
-    for i in range(count):
-        copies[i] = mine
+def prepare_kernel(presence, blocks, factor, masked, mine):
+    rows, span = mine.shape
+    mine[...] = factor[:, pl.ds(pl.multiple_of(lax.axis_index("col") * span, LANES), span)]
     block_cols, _, order = masked.shape
     for a in range(rows // order):
         for b in range(block_cols):
@@ -45,7 +43,7 @@
             masked[b, pl.ds(a * order, order), :] = picked * weight
 
 
-def prepare(presence, blocks, own, receivers, span):
+def prepare(presence, blocks, own, span):
     rows, width = own.shape
     block_cols = blocks.shape[0] // rows
     order = blocks.shape[1]
@@ -54,13 +52,12 @@
         mine = lax.dynamic_slice_in_dim(own, first, span, 1)
         weights = presence.reshape(-1, 1, block_cols, 1).astype(jnp.float32)
         picked = blocks.reshape(-1, order, block_cols, order) * weights
-        masked = picked.transpose(2, 0, 1, 3).reshape(block_cols, rows, order)
-        return masked, jnp.broadcast_to(mine[None], (receivers, rows, span))
+        return picked.transpose(2, 0, 1, 3).reshape(block_cols, rows, order), mine
     return pl.pallas_call(
         prepare_kernel,
         out_shape=(
             jax.ShapeDtypeStruct((block_cols, rows, order), jnp.float32),
-            jax.ShapeDtypeStruct((receivers, rows, span), jnp.float32),
+            jax.ShapeDtypeStruct((rows, span), jnp.float32),
         ),
         in_specs=[pl.BlockSpec(memory_space=pltpu.SMEM), WHOLE, WHOLE],
         out_specs=(WHOLE, WHOLE),
@@ -68,11 +65,17 @@
     )(presence, blocks, own)
 
 
-def partials_kernel(count, *refs):
-    pieces = refs[: 2 * count]
-    columns, kept, sent = refs[2 * count :]
-    block_cols, rows, _ = pieces[0].shape
+def partials_kernel(count, flips, *refs):
+    pieces, refs = refs[: 2 * count], refs[2 * count :]
+    strips = refs[: len(flips)]
+    kept, sent, columns = refs[len(flips) :]
+    block_cols, rows, order = pieces[0].shape
     col_index = lax.axis_index("col")
+    row_index = lax.axis_index("row")
+    for flip, strip in zip(flips, strips):
+        for a in range(rows // order):
+            at = a * len(flips) + ((row_index ^ flip) >> 1)
+            columns[at] = strip[pl.ds(a * order, order), :]
     left, right = [], []
     for t in range(count):
         for b in range(block_cols):
@@ -80,21 +83,24 @@
             right.append(columns[b * count + ((col_index >> 1) ^ t)])
     both = product(jnp.concatenate(left, axis=1), jnp.concatenate(right, axis=0), ((1,), (0,)))
     first, second = both[:rows], both[rows:]
-    same = (lax.axis_index("row") & 1) == (col_index & 1)
+    same = (row_index & 1) == (col_index & 1)
     kept[...] = jnp.where(same, first, second)
     sent[...] = jnp.where(same, second, first)
 
 
-def partials(pieces, columns):
-    part = jax.ShapeDtypeStruct((pieces[0].shape[1], columns.shape[2]), jnp.float32)
-    return pl.pallas_call(
-        functools.partial(partials_kernel, len(pieces) // 2),
+def partials(pieces, strips, flips):
+    _, rows, order = pieces[0].shape
+    span = strips[0].shape[1]
+    part = jax.ShapeDtypeStruct((rows, span), jnp.float32)
+    return pl.pallas_call(
+        functools.partial(partials_kernel, len(pieces) // 2, flips),
         out_shape=(part, part),
-        in_specs=[WHOLE] * (len(pieces) + 1),
+        in_specs=[WHOLE] * (len(pieces) + len(strips)),
         out_specs=(WHOLE, WHOLE),
+        scratch_shapes=[pltpu.VMEM((rows // order * len(strips), order, span), jnp.float32)],
         cost_estimate=LIGHT,
         compiler_params=ROOM,
-    )(*pieces, columns)
+    )(*pieces, *strips)
 
 
 def finish_kernel(order, kept, got, own, dinv, terms, *refs):
@@ -152,6 +158,16 @@
     )(*arrived)
 
 
+def along_line(mine):
+    strips, flips = [mine], [0]
+    bit = lax.axis_size("row") // 2
+    while bit > 1:
+        strips = strips + [flipped(strip, "row", bit) for strip in strips]
+        flips = flips + [flip ^ bit for flip in flips]
+        bit //= 2
+    return strips, tuple(flips)
+
+
 def pair_rows(masked):
     groups_row = lax.axis_size("row")
     groups_col = lax.axis_size("col")
@@ -176,13 +192,9 @@
 
     own = factor.reshape(rows, width)
     blocks = inverse_set.reshape(rows * block_cols, order)
-    masked, copies = prepare(presence.reshape(-1), blocks, own, groups_row // 2, span)
-    lines = [list(range(bit, groups_row, 2)) for bit in range(2)]
-    columns = lax.all_to_all(copies, "row", 0, 0, axis_index_groups=lines)
-    columns = columns.reshape(groups_row // 2, block_rows, order, span).transpose(1, 0, 2, 3)
-    pieces = pair_rows(masked)
-
-    kept, sent = partials(pieces, columns.reshape(-1, order, span))
+    masked, mine = prepare(presence.reshape(-1), blocks, own, span)
+    strips, flips = along_line(mine)
+    kept, sent = partials(pair_rows(masked), strips, flips)
     got = flipped(sent, "row", 1)
     terms, *outward = finish(kept, got, own, dinv, order, groups_col)
     terms = lax.all_to_all(terms.reshape(groups_row, width // groups_row, span), "row", 0, 0)

time: 38.9 us -> 43.6 us (1.12)
  starting transfers between devices: 19 us -> 25.4 us
  waiting for transfers between devices: 14.5 us -> 12 us
  local copies, waits for them, and re-layouts: 0.01 us -> 0.85 us
    ppermute x7 -> x10, starting transfers between devices: 7.37 us -> 16.9 us  [flipped(): lax.ppermute(value, axis, [(i, i ^ flip) for i in range(lax.axis_size(axi...]
    all_to_all x1 -> x0, starting transfers between devices: 6.32 us -> none  [local(): columns = lax.all_to_all(copies, 'row', 0, 0, axis_index_groups=lines)]
    all_to_all x1, starting transfers between devices: 3.76 us -> 6.93 us  [local(): lax.all_to_all(terms.reshape(groups_row, width // groups_row, span), 'row...]
    all_to_all x1 -> x0, waiting for transfers between devices: 1.15 us -> none  [local(): columns = lax.all_to_all(copies, 'row', 0, 0, axis_index_groups=lines)]
    ppermute x7 -> x10, waiting for transfers between devices: 9.59 us -> 8.52 us  [flipped(): lax.ppermute(value, axis, [(i, i ^ flip) for i in range(lax.axis_size(axi...]
    unnamed x4 -> x6, local copies, waits for them, and re-layouts: 0.01 us -> 0.85 us
  transfers between devices with their start and end apart: 10 -> 12, of which waited for: 7 -> 6; matrix products, arithmetic and copies ran while one was open for 0% -> 0% of each run, Pallas kernels for 2% -> 1%
where the time goes in v10:
time: 43.6 us; the launch traced here: 43.3 us
  starting transfers between devices  25.4 us (58%)
  waiting for transfers between devices  12 us (28%)
  Pallas kernels  3.74 us (9%)
  local copies, waits for them, and re-layouts  0.85 us (2%)
  between operations  0.67 us (2%)
  other arithmetic  0.63 us (1%)
    ppermute x10, starting transfers between devices, flipped(): lax.ppermute(value, axis, [(i, i ^ flip) for i in range(lax.axis_size(axi...  16.9 us
    ppermute x10, waiting for transfers between devices, flipped(): lax.ppermute(value, axis, [(i, i ^ flip) for i in range(lax.axis_size(axi...  8.52 us
    all_to_all x1, starting transfers between devices, local(): lax.all_to_all(terms.reshape(groups_row, width // groups_row, span), 'row...  6.93 us
    all_to_all x1, waiting for transfers between devices, local(): lax.all_to_all(terms.reshape(groups_row, width // groups_row, span), 'row...  3.49 us
    pallas_call x1, Pallas kernels, prepare(): pl.pallas_call(prepare_kernel, out_shape=(jax.ShapeDtypeStruct((block_col...  1.72 us
    ppermute x1, starting transfers between devices, pair_rows(): held = lax.ppermute(masked, ('row', 'col'), cross)  1.55 us
    pallas_call x1, Pallas kernels, finish(): pl.pallas_call(functools.partial(finish_kernel, order), out_shape=(jax.Sh...  1 us
  transfers between devices with their start and end apart: 12, of which 6 were waited for; matrix products, arithmetic and copies ran while one was open for 0% of the time, Pallas kernels for 1%

profile of v10, /device:TPU:0, one launch (start us, length us, event | category | flops | bytes accessed | tf_op | source)
XLA Modules:
  0.0 43.3 jit_solution(7072700489044591344)
XLA Ops:
  0.6 1.7 %shard_map.59 = (f32[2,128,128]{2,1,0:T(8,128)}, f32[128,128]{1,0:T(8,128)}) custom-call(s32[2]{0:T(128)} %bitcast.9, f32[256,128]{1,0:T(8,128)} %bitcast.7, f32[128,512]{1,0:T(8,128)} %bitcast.5), custom_call_target="tpu_custom_call" | custom-call | flops 1000 | bytes 1000 | tf_op jit(solution)/shard_map/pallas_call | solution.py:56
  2.4 1.6 %collective-permute-start = (f32[2,128,128]{2,1,0:T(8,128)}, f32[2,128,128]{2,1,0:T(8,128)S(1)}, u32[]{:S(2)}, u32[]{:S(2)}) collective-permute-start(f32[2,128,128]{2,1,0:T(8,128)} %get-tuple-element.11), channel_id=1, source_target_pairs={{0,0},{1,4},{2,2},{3,6},{4,1},{5,5},{6,3},{7,7},{8,8},{9,12},{10,1... | collective-permute-start | bytes 393224 | tf_op jit(solution)/shard_map/ppermute | solution.py:179
  3.9 0.0 collective-permute-done.refs_0_
  3.9 3.0 %collective-permute-start.1 = (f32[2,128,128]{2,1,0:T(8,128)S(1)}, f32[2,128,128]{2,1,0:T(8,128)S(1)}, u32[]{:S(2)}, u32[]{:S(2)}) collective-permute-start(f32[2,128,128]{2,1,0:T(8,128)S(1)} %collective-permute-done.refs_0_), channel_id=1, source_target_pairs={{0,2},{1,3},{2,0},{3,1},{4,6},{5,7},{6,4},{7,5},{8,10},{9,11},{10,... | collective-permute-start | bytes 393224 | tf_op jit(solution)/shard_map/ppermute | solution.py:17
  6.9 2.6 %collective-permute-start.4 = (f32[128,128]{1,0:T(8,128)}, f32[128,128]{1,0:T(8,128)S(1)}, u32[]{:S(2)}, u32[]{:S(2)}) collective-permute-start(f32[128,128]{1,0:T(8,128)} %get-tuple-element.12.refs_4_), channel_id=1, source_target_pairs={{0,16},{4,20},{8,24},{12,28},{16,0},{20,4},{24,8},{28,12},{1,17},{... | collective-permute-start | bytes 196616 | tf_op jit(solution)/shard_map/ppermute | solution.py:17
  9.5 4.5 %collective-permute-start.2 = (f32[2,128,128]{2,1,0:T(8,128)S(1)}, f32[2,128,128]{2,1,0:T(8,128)S(1)}, u32[]{:S(2)}, u32[]{:S(2)}) collective-permute-start(f32[2,128,128]{2,1,0:T(8,128)S(1)} %collective-permute-done.refs_0_), channel_id=1, source_target_pairs={{0,1},{1,0},{2,3},{3,2},{4,5},{5,4},{6,7},{7,6},{8,9},{9,8},{10,11... | collective-permute-start | bytes 393224 | tf_op jit(solution)/shard_map/ppermute | solution.py:17
  14.0 0.1 collective-permute-start.3
  14.1 1.8 %collective-permute-start.5 = (f32[128,128]{1,0:T(8,128)}, f32[128,128]{1,0:T(8,128)S(1)}, u32[]{:S(2)}, u32[]{:S(2)}) collective-permute-start(f32[128,128]{1,0:T(8,128)} %get-tuple-element.12.refs_4_), channel_id=1, source_target_pairs={{0,8},{4,12},{8,0},{12,4},{16,24},{20,28},{24,16},{28,20},{1,9},{5... | collective-permute-start | bytes 196616 | tf_op jit(solution)/shard_map/ppermute | solution.py:17
  15.8 0.2 collective-permute-start.6
  16.1 2.9 %collective-permute-done.5.refs_6_ = f32[128,128]{1,0:T(8,128)S(1)} collective-permute-done((f32[128,128]{1,0:T(8,128)}, f32[128,128]{1,0:T(8,128)S(1)}, u32[]{:S(2)}, u32[]{:S(2)}) %collective-permute-start.5) | collective-permute-done | bytes 65568 | tf_op jit(solution)/shard_map/ppermute | solution.py:17
  18.9 1.2 %collective-permute-done.6.refs_7_ = f32[128,128]{1,0:T(8,128)S(1)} collective-permute-done((f32[128,128]{1,0:T(8,128)S(1)}, f32[128,128]{1,0:T(8,128)S(1)}, u32[]{:S(2)}, u32[]{:S(2)}) %collective-permute-start.6) | collective-permute-done | bytes 65568 | tf_op jit(solution)/shard_map/ppermute | solution.py:17
  20.1 0.8 %copy-done.1 = f32[128,128]{1,0:T(8,128)S(1)} copy-done((f32[128,128]{1,0:T(8,128)S(1)}, f32[128,128]{1,0:T(8,128)}, u32[]{:S(2)}) %copy-start.1) | copy-done | bytes 65560
  21.0 0.4 shard_map.60
  21.4 2.9 %collective-permute-start.7 = (f32[128,128]{1,0:T(8,128)S(1)}, f32[128,128]{1,0:T(8,128)S(1)}, u32[]{:S(2)}, u32[]{:S(2)}) collective-permute-start(f32[128,128]{1,0:T(8,128)S(1)} %get-tuple-element.14), channel_id=1, source_target_pairs={{0,4},{4,0},{8,12},{12,8},{16,20},{20,16},{24,28},{28,24},{1,5},{5... | collective-permute-start | bytes 196616 | tf_op jit(solution)/shard_map/ppermute | solution.py:17
  24.3 2.2 %collective-permute-done.7.got = f32[128,128]{1,0:T(8,128)S(1)} collective-permute-done((f32[128,128]{1,0:T(8,128)S(1)}, f32[128,128]{1,0:T(8,128)S(1)}, u32[]{:S(2)}, u32[]{:S(2)}) %collective-permute-start.7) | collective-permute-done | bytes 65568 | tf_op jit(solution)/shard_map/ppermute | solution.py:17
  26.5 1.0 %shard_map.61 = (f32[512,128]{1,0:T(8,128)}, f32[32,128]{1,0:T(8,128)S(1)}, f32[32,128]{1,0:T(8,128)S(1)}, f32[32,128]{1,0:T(8,128)S(1)}, f32[32,128]{1,0:T(8,128)S(1)}) custom-call(f32[128,128]{1,0:T(8,128)S(1)} %get-tuple-element.13.kept, f32[128,128]{1,0:T(8,128)S(1)} %collective-permute-done.7.got, f32[128,512]{1,0:T(8,128)S(1)} %bitcast.6, ...), custom_call_target="tpu_custom_call" | custom-call | flops 1000 | bytes 1000 | tf_op jit(solution)/shard_map/pallas_call | solution.py:126
  27.5 6.9 %all-to-all-start = ((f32[8,64,128]{2,1,0:T(8,128)}), f32[8,64,128]{2,1,0:T(8,128)S(1)}, u32[]{:S(2)}, u32[]{:S(2)}) async-start(f32[8,64,128]{2,1,0:T(8,128)} %bitcast.4), calls=%async_computation | async-start | bytes 524288 | tf_op jit(solution)/shard_map/all_to_all | solution.py:200
  34.4 0.9 %collective-permute-start.9 = (f32[32,128]{1,0:T(8,128)S(1)}, f32[32,128]{1,0:T(8,128)S(1)}, u32[]{:S(2)}, u32[]{:S(2)}) collective-permute-start(f32[32,128]{1,0:T(8,128)S(1)} %get-tuple-element.17), channel_id=1, source_target_pairs={{0,2},{1,3},{2,0},{3,1},{4,6},{5,7},{6,4},{7,5},{8,10},{9,11},{10,... | collective-permute-start | bytes 49160 | tf_op jit(solution)/shard_map/ppermute | solution.py:17
  35.4 0.9 %collective-permute-start.10 = (f32[32,128]{1,0:T(8,128)S(1)}, f32[32,128]{1,0:T(8,128)S(1)}, u32[]{:S(2)}, u32[]{:S(2)}) collective-permute-start(f32[32,128]{1,0:T(8,128)S(1)} %get-tuple-element.18), channel_id=1, source_target_pairs={{0,3},{1,2},{2,1},{3,0},{4,7},{5,6},{6,5},{7,4},{8,11},{9,10},{10,... | collective-permute-start | bytes 49160 | tf_op jit(solution)/shard_map/ppermute | solution.py:17
  36.3 1.9 %collective-permute-done.9.refs_2_ = f32[32,128]{1,0:T(8,128)S(1)} collective-permute-done((f32[32,128]{1,0:T(8,128)S(1)}, f32[32,128]{1,0:T(8,128)S(1)}, u32[]{:S(2)}, u32[]{:S(2)}) %collective-permute-start.9) | collective-permute-done | bytes 16416 | tf_op jit(solution)/shard_map/ppermute | solution.py:17
  38.3 0.3 collective-permute-done.10.refs_3_
  38.5 0.6 %shard_map.62 = f32[32,512]{1,0:T(8,128)} custom-call(f32[32,128]{1,0:T(8,128)S(1)} %get-tuple-element.15.refs_0_, f32[32,128]{1,0:T(8,128)S(1)} %collective-permute-done.8.refs_1_, f32[32,128]{1,0:T(8,128)S(1)} %collective-permute-done.9.refs_2_, f32[32,128]{1,0:T(8,128)S(1)} %collective-permute-done.10.refs_3_), custom_call_target="tpu_custom_call" | custom-call | flops 1000 | bytes 1000 | tf_op jit(solution)/shard_map/pallas_call | solution.py:151
  39.2 3.5 %all-to-all-done = f32[8,64,128]{2,1,0:T(8,128)S(1)} async-done(((f32[8,64,128]{2,1,0:T(8,128)}), f32[8,64,128]{2,1,0:T(8,128)S(1)}, u32[]{:S(2)}, u32[]{:S(2)}) %all-to-all-start) | async-done | bytes 262176 | tf_op jit(solution)/shard_map/all_to_all | solution.py:200
  42.7 0.6 %reduce_sum.9 = f32[64,128]{1,0:T(8,128)} reduce(f32[8,64,128]{2,1,0:T(8,128)S(1)} %all-to-all-done, f32[]{:T(128)} %constant.0.clone.1), dimensions={0}, to_apply=%region_0.0 | reduce | flops 57344 | bytes 294916 | tf_op jit(solution)/shard_map/reduce_sum | solution.py:201
  (11 shorter events, 0.0 us)
Async XLA Ops:
  0.6 25.9 %copy-start.2 = (f32[64,128]{1,0:T(8,128)S(1)}, f32[64,128]{1,0:T(8,128)}, u32[]{:S(2)}) copy-start(f32[64,128]{1,0:T(8,128)} %dinv.1) | copy-start | bytes 98308
  2.4 1.6 %collective-permute-start = (f32[2,128,128]{2,1,0:T(8,128)}, f32[2,128,128]{2,1,0:T(8,128)S(1)}, u32[]{:S(2)}, u32[]{:S(2)}) collective-permute-start(f32[2,128,128]{2,1,0:T(8,128)} %get-tuple-element.11), channel_id=1, source_target_pairs={{0,0},{1,4},{2,2},{3,6},{4,1},{5,5},{6,3},{7,7},{8,8},{9,12},{10,1... | collective-permute-start | bytes 393224 | tf_op jit(solution)/shard_map/ppermute | solution.py:179
  3.9 10.1 %collective-permute-start.1 = (f32[2,128,128]{2,1,0:T(8,128)S(1)}, f32[2,128,128]{2,1,0:T(8,128)S(1)}, u32[]{:S(2)}, u32[]{:S(2)}) collective-permute-start(f32[2,128,128]{2,1,0:T(8,128)S(1)} %collective-permute-done.refs_0_), channel_id=1, source_target_pairs={{0,2},{1,3},{2,0},{3,1},{4,6},{5,7},{6,4},{7,5},{8,10},{9,11},{10,... | collective-permute-start | bytes 393224 | tf_op jit(solution)/shard_map/ppermute | solution.py:17
  6.9 19.6 %copy-start = (f32[1,1,128,512]{3,2,1,0:T(8,128)S(1)}, f32[1,1,128,512]{3,2,1,0:T(8,128)}, u32[]{:S(2)}) copy-start(f32[1,1,128,512]{3,2,1,0:T(8,128)} %param.6) | copy-start | bytes 786436
  6.9 9.0 %collective-permute-start.4 = (f32[128,128]{1,0:T(8,128)}, f32[128,128]{1,0:T(8,128)S(1)}, u32[]{:S(2)}, u32[]{:S(2)}) collective-permute-start(f32[128,128]{1,0:T(8,128)} %get-tuple-element.12.refs_4_), channel_id=1, source_target_pairs={{0,16},{4,20},{8,24},{12,28},{16,0},{20,4},{24,8},{28,12},{1,17},{... | collective-permute-start | bytes 196616 | tf_op jit(solution)/shard_map/ppermute | solution.py:17
  9.5 10.7 %collective-permute-start.2 = (f32[2,128,128]{2,1,0:T(8,128)S(1)}, f32[2,128,128]{2,1,0:T(8,128)S(1)}, u32[]{:S(2)}, u32[]{:S(2)}) collective-permute-start(f32[2,128,128]{2,1,0:T(8,128)S(1)} %collective-permute-done.refs_0_), channel_id=1, source_target_pairs={{0,1},{1,0},{2,3},{3,2},{4,5},{5,4},{6,7},{7,6},{8,9},{9,8},{10,11... | collective-permute-start | bytes 393224 | tf_op jit(solution)/shard_map/ppermute | solution.py:17
  14.0 6.1 %collective-permute-start.3 = (f32[2,128,128]{2,1,0:T(8,128)S(1)}, f32[2,128,128]{2,1,0:T(8,128)S(1)}, u32[]{:S(2)}, u32[]{:S(2)}) collective-permute-start(f32[2,128,128]{2,1,0:T(8,128)S(1)} %collective-permute-done.1.refs_1_), channel_id=1, source_target_pairs={{0,1},{1,0},{2,3},{3,2},{4,5},{5,4},{6,7},{7,6},{8,9},{9,8},{10,11... | collective-permute-start | bytes 393224 | tf_op jit(solution)/shard_map/ppermute | solution.py:17
  14.1 4.9 %collective-permute-start.5 = (f32[128,128]{1,0:T(8,128)}, f32[128,128]{1,0:T(8,128)S(1)}, u32[]{:S(2)}, u32[]{:S(2)}) collective-permute-start(f32[128,128]{1,0:T(8,128)} %get-tuple-element.12.refs_4_), channel_id=1, source_target_pairs={{0,8},{4,12},{8,0},{12,4},{16,24},{20,28},{24,16},{28,20},{1,9},{5... | collective-permute-start | bytes 196616 | tf_op jit(solution)/shard_map/ppermute | solution.py:17
  15.8 4.3 %collective-permute-start.6 = (f32[128,128]{1,0:T(8,128)S(1)}, f32[128,128]{1,0:T(8,128)S(1)}, u32[]{:S(2)}, u32[]{:S(2)}) collective-permute-start(f32[128,128]{1,0:T(8,128)S(1)} %collective-permute-done.4.refs_5_), channel_id=1, source_target_pairs={{0,8},{4,12},{8,0},{12,4},{16,24},{20,28},{24,16},{28,20},{1,9},{5... | collective-permute-start | bytes 196616 | tf_op jit(solution)/shard_map/ppermute | solution.py:17
  20.1 0.8 %copy-start.1 = (f32[128,128]{1,0:T(8,128)S(1)}, f32[128,128]{1,0:T(8,128)}, u32[]{:S(2)}) copy-start(f32[128,128]{1,0:T(8,128)} %get-tuple-element.12.refs_4_) | copy-start | bytes 196612
  21.4 5.1 %collective-permute-start.7 = (f32[128,128]{1,0:T(8,128)S(1)}, f32[128,128]{1,0:T(8,128)S(1)}, u32[]{:S(2)}, u32[]{:S(2)}) collective-permute-start(f32[128,128]{1,0:T(8,128)S(1)} %get-tuple-element.14), channel_id=1, source_target_pairs={{0,4},{4,0},{8,12},{12,8},{16,20},{20,16},{24,28},{28,24},{1,5},{5... | collective-permute-start | bytes 196616 | tf_op jit(solution)/shard_map/ppermute | solution.py:17
  27.5 15.2 %all-to-all-start = ((f32[8,64,128]{2,1,0:T(8,128)}), f32[8,64,128]{2,1,0:T(8,128)S(1)}, u32[]{:S(2)}, u32[]{:S(2)}) async-start(f32[8,64,128]{2,1,0:T(8,128)} %bitcast.4), calls=%async_computation | async-start | bytes 524288 | tf_op jit(solution)/shard_map/all_to_all | solution.py:200
  34.4 1.9 %collective-permute-start.8 = (f32[32,128]{1,0:T(8,128)S(1)}, f32[32,128]{1,0:T(8,128)S(1)}, u32[]{:S(2)}, u32[]{:S(2)}) collective-permute-start(f32[32,128]{1,0:T(8,128)S(1)} %get-tuple-element.16), channel_id=1, source_target_pairs={{0,1},{1,0},{2,3},{3,2},{4,5},{5,4},{6,7},{7,6},{8,9},{9,8},{10,11... | collective-permute-start | bytes 49160 | tf_op jit(solution)/shard_map/ppermute | solution.py:17
  34.4 3.8 %collective-permute-start.9 = (f32[32,128]{1,0:T(8,128)S(1)}, f32[32,128]{1,0:T(8,128)S(1)}, u32[]{:S(2)}, u32[]{:S(2)}) collective-permute-start(f32[32,128]{1,0:T(8,128)S(1)} %get-tuple-element.17), channel_id=1, source_target_pairs={{0,2},{1,3},{2,0},{3,1},{4,6},{5,7},{6,4},{7,5},{8,10},{9,11},{10,... | collective-permute-start | bytes 49160 | tf_op jit(solution)/shard_map/ppermute | solution.py:17
  35.4 3.2 %collective-permute-start.10 = (f32[32,128]{1,0:T(8,128)S(1)}, f32[32,128]{1,0:T(8,128)S(1)}, u32[]{:S(2)}, u32[]{:S(2)}) collective-permute-start(f32[32,128]{1,0:T(8,128)S(1)} %get-tuple-element.18), channel_id=1, source_target_pairs={{0,3},{1,2},{2,1},{3,0},{4,7},{5,6},{6,5},{7,4},{8,11},{9,10},{10,... | collective-permute-start | bytes 49160 | tf_op jit(solution)/shard_map/ppermute | solution.py:17

commit v11 on v9

--- a/solution.py
+++ b/solution.py
@@ -70,7 +70,7 @@
 
 def partials_kernel(count, *refs):
     pieces = refs[: 2 * count]
-    columns, kept, sent = refs[2 * count :]
+    columns, both = refs[2 * count :]
     block_cols, rows, _ = pieces[0].shape
     col_index = lax.axis_index("col")
     left, right = [], []
@@ -78,54 +78,89 @@
         for b in range(block_cols):
             left.append(jnp.concatenate([pieces[t][b], pieces[count + t][b]], axis=0))
             right.append(columns[b * count + ((col_index >> 1) ^ t)])
-    both = product(jnp.concatenate(left, axis=1), jnp.concatenate(right, axis=0), ((1,), (0,)))
-    first, second = both[:rows], both[rows:]
-    same = (lax.axis_index("row") & 1) == (col_index & 1)
-    kept[...] = jnp.where(same, first, second)
-    sent[...] = jnp.where(same, second, first)
+    summed = product(jnp.concatenate(left, axis=1), jnp.concatenate(right, axis=0), ((1,), (0,)))
+    here = (col_index & 1) * rows
+    both[pl.ds(pl.multiple_of(here, 8), rows), :] = summed[:rows]
+    both[pl.ds(pl.multiple_of(rows - here, 8), rows), :] = summed[rows:]
 
 
 def partials(pieces, columns):
-    part = jax.ShapeDtypeStruct((pieces[0].shape[1], columns.shape[2]), jnp.float32)
+    shape = (2 * pieces[0].shape[1], columns.shape[2])
     return pl.pallas_call(
         functools.partial(partials_kernel, len(pieces) // 2),
+        out_shape=jax.ShapeDtypeStruct(shape, jnp.float32),
+        in_specs=[WHOLE] * (len(pieces) + 1),
+        out_specs=WHOLE,
+        cost_estimate=LIGHT,
+        compiler_params=ROOM,
+    )(*pieces, columns)
+
+
+def halves_kernel(tall, own, held, stay, go):
+    even, odd = [
+        jnp.concatenate([own[:, i : i + tall] for i in range(first, own.shape[1], 2 * tall)], axis=1)
+        for first in (0, tall)
+    ]
+    upper = (lax.axis_index("row") & 1) == 1
+    stay[...] = jnp.where(upper, odd, even)
+    go[...] = jnp.where(upper, even, odd)
+
+
+def halves(own, held, tall):
+    rows, width = own.shape
+    part = jax.ShapeDtypeStruct((rows, width // 2), jnp.float32)
+    return pl.pallas_call(
+        functools.partial(halves_kernel, tall),
         out_shape=(part, part),
-        in_specs=[WHOLE] * (len(pieces) + 1),
+        in_specs=[WHOLE, pl.BlockSpec(memory_space=pl.ANY)],
         out_specs=(WHOLE, WHOLE),
         cost_estimate=LIGHT,
         compiler_params=ROOM,
-    )(*pieces, columns)
-
-
-def finish_kernel(order, kept, got, own, dinv, terms, *refs):
-    outward, update = refs[:-1], refs[-1]
-    rows = kept.shape[0]
-    update[...] = kept[...] + got[...]
-    terms[...] = product(own[...], update[...], ((0,), (0,)))
+    )(own, held)
+
+
+def finish_kernel(order, flips, both, got, stay, near, dinv, *refs):
+    update, terms = refs[-2:]
+    along, outward = refs[: len(flips)], refs[len(flips) : -2]
+    rows = stay.shape[0]
+    row_index = lax.axis_index("row")
+    here = (row_index & 1) * rows
+    update[...] = both[...] + got[...]
+    mine = update[pl.ds(pl.multiple_of(here, 8), rows), :]
+    other = update[pl.ds(pl.multiple_of(rows - here, 8), rows), :]
+    factors = jnp.concatenate([stay[...], near[...]], axis=0)
+    terms[...] = product(factors, jnp.concatenate([mine, other], axis=0), ((0,), (0,)))
     tall = dinv.shape[0]
-    here = pl.ds(pl.multiple_of(lax.axis_index("row") * tall, 8), tall)
-    terms[here, :] = terms[here, :] + dinv[...]
+    for flip, piece in zip(flips, along):
+        slot = ((row_index ^ flip) >> 1) * tall
+        piece[...] = terms[pl.ds(pl.multiple_of(slot, 8), tall), :]
+    along[0][...] = along[0][...] + dinv[...]
     share = order // len(outward)
     for flip, piece in enumerate(outward):
-        start = (lax.axis_index("col") ^ flip) * share
+        start = here + (lax.axis_index("col") ^ flip) * share
         for a in range(rows // order):
             picked = update[pl.ds(pl.multiple_of(a * order + start, 8), share), :]
             piece[pl.ds(a * share, share), :] = -picked
 
 
-def finish(kept, got, own, dinv, order, flips):
-    rows, width = own.shape
-    span = kept.shape[1]
-    part = jax.ShapeDtypeStruct((rows // flips, span), jnp.float32)
-    return pl.pallas_call(
-        functools.partial(finish_kernel, order),
-        out_shape=(jax.ShapeDtypeStruct((width, span), jnp.float32),) + (part,) * flips,
-        in_specs=[WHOLE] * 4,
-        out_specs=(WHOLE,) * (1 + flips),
-        scratch_shapes=[pltpu.VMEM((rows, span), jnp.float32)],
-        cost_estimate=LIGHT,
-        compiler_params=ROOM,
-    )(kept, got, own, dinv)
+def finish(both, got, stay, near, dinv, order, flips, receivers):
+    rows, half = stay.shape
+    span = both.shape[1]
+    along = (jax.ShapeDtypeStruct(dinv.shape, jnp.float32),) * len(flips)
+    outward = (jax.ShapeDtypeStruct((rows // receivers, span), jnp.float32),) * receivers
+    outs = pl.pallas_call(
+        functools.partial(finish_kernel, order, flips),
+        out_shape=along + outward,
+        in_specs=[WHOLE] * 5,
+        out_specs=(WHOLE,) * (len(flips) + receivers),
+        scratch_shapes=[
+            pltpu.VMEM((2 * rows, span), jnp.float32),
+            pltpu.VMEM((half, span), jnp.float32),
+        ],
+        cost_estimate=LIGHT,
+        compiler_params=ROOM,
+    )(both, got, stay, near, dinv)
+    return outs[: len(flips)], outs[len(flips) :]
 
 
 def collect_kernel(*refs):
@@ -181,12 +216,16 @@
     columns = lax.all_to_all(copies, "row", 0, 0, axis_index_groups=lines)
     columns = columns.reshape(groups_row // 2, block_rows, order, span).transpose(1, 0, 2, 3)
     pieces = pair_rows(masked)
-
-    kept, sent = partials(pieces, columns.reshape(-1, order, span))
-    got = flipped(sent, "row", 1)
-    terms, *outward = finish(kept, got, own, dinv, order, groups_col)
-    terms = lax.all_to_all(terms.reshape(groups_row, width // groups_row, span), "row", 0, 0)
-    diag_block = terms.sum(axis=0)
+    stay, go = halves(own, pieces[0], width // groups_row)
+    near = flipped(go, "row", 1)
+
+    both = partials(pieces, columns.reshape(-1, order, span))
+    got = flipped(both, "row", 1)
+    flips = tuple(range(0, groups_row, 2))
+    along, outward = finish(both, got, stay, near, dinv, order, flips, groups_col)
+    diag_block = along[0]
+    for flip, piece in zip(flips[1:], along[1:]):
+        diag_block = diag_block + flipped(piece, "row", flip)
 
     arrived = [outward[0]] + [flipped(outward[f], "col", f) for f in range(1, groups_col)]
     return (collect(arrived).reshape(block_rows, 1, share, width), diag_block)

time: 38.9 us -> 36.8 us (0.946)
  waiting for transfers between devices: 14.5 us -> 11.9 us
  starting transfers between devices: 19 us -> 20.1 us
  Pallas kernels: 3.81 us -> 3.26 us
    ppermute x7 -> x11, starting transfers between devices: 7.37 us -> 12.1 us  [flipped(): lax.ppermute(value, axis, [(i, i ^ flip) for i in range(lax.axis_size(axi...]
    all_to_all x1 -> x0, starting transfers between devices: 3.76 us -> none  [local(): lax.all_to_all(terms.reshape(groups_row, width // groups_row, span), 'row...]
    all_to_all x1 -> x0, waiting for transfers between devices: 3.74 us -> none  [local(): lax.all_to_all(terms.reshape(groups_row, width // groups_row, span), 'row...]
    ppermute x7 -> x11, waiting for transfers between devices: 9.59 us -> 10.7 us  [flipped(): lax.ppermute(value, axis, [(i, i ^ flip) for i in range(lax.axis_size(axi...]
    reduce_sum x1 -> x0, other arithmetic: 0.63 us -> none  [local(): diag_block = terms.sum(axis=0)]
    add x0 -> x1, other arithmetic: none -> 0.62 us  [local(): diag_block = diag_block + flipped(piece, 'row', flip)]
    pallas_call x1 -> x2, Pallas kernels: 1.01 us -> 0.45 us  [the longest x1 0.32 us: finish(): pl.pallas_call(functools.partial(finish_kernel, order, flips), out_shape=...]
  transfers between devices with their start and end apart: 10 -> 13, of which waited for: 7 -> 8; matrix products, arithmetic and copies ran while one was open for 0% -> 0% of each run, Pallas kernels for 2% -> 3%
where the time goes in v11:
time: 36.8 us; the launch traced here: 36.6 us
  starting transfers between devices  20.1 us (55%)
  waiting for transfers between devices  11.9 us (32%)
  Pallas kernels  3.26 us (9%)
  between operations  0.67 us (2%)
  other arithmetic  0.62 us (2%)
    ppermute x11, starting transfers between devices, flipped(): lax.ppermute(value, axis, [(i, i ^ flip) for i in range(lax.axis_size(axi...  12.1 us
    ppermute x11, waiting for transfers between devices, flipped(): lax.ppermute(value, axis, [(i, i ^ flip) for i in range(lax.axis_size(axi...  10.7 us
    all_to_all x1, starting transfers between devices, local(): columns = lax.all_to_all(copies, 'row', 0, 0, axis_index_groups=lines)  6.45 us
    pallas_call x1, Pallas kernels, prepare(): pl.pallas_call(prepare_kernel, out_shape=(jax.ShapeDtypeStruct((block_col...  1.8 us
    ppermute x1, starting transfers between devices, pair_rows(): held = lax.ppermute(masked, ('row', 'col'), cross)  1.55 us
    all_to_all x1, waiting for transfers between devices, local(): columns = lax.all_to_all(copies, 'row', 0, 0, axis_index_groups=lines)  1.21 us
  transfers between devices with their start and end apart: 13, of which 8 were waited for; matrix products, arithmetic and copies ran while one was open for 0% of the time, Pallas kernels for 3%

profile of v11, /device:TPU:0, one launch (start us, length us, event | category | flops | bytes accessed | tf_op | source)
XLA Modules:
  0.0 36.6 jit_solution(10712868628716359401)
XLA Ops:
  0.6 1.8 %shard_map.59 = (f32[2,128,128]{2,1,0:T(8,128)}, f32[4,128,128]{2,1,0:T(8,128)}) custom-call(s32[2]{0:T(128)} %bitcast.8, f32[256,128]{1,0:T(8,128)} %bitcast.6, f32[128,512]{1,0:T(8,128)} %bitcast.4), custom_call_target="tpu_custom_call" | custom-call | flops 1000 | bytes 1000 | tf_op jit(solution)/shard_map/pallas_call | solution.py:59
  2.4 1.6 %collective-permute-start = (f32[2,128,128]{2,1,0:T(8,128)}, f32[2,128,128]{2,1,0:T(8,128)S(1)}, u32[]{:S(2)}, u32[]{:S(2)}) collective-permute-start(f32[2,128,128]{2,1,0:T(8,128)} %get-tuple-element.14), channel_id=1, source_target_pairs={{0,0},{1,4},{2,2},{3,6},{4,1},{5,5},{6,3},{7,7},{8,8},{9,12},{10,1... | collective-permute-start | bytes 393224 | tf_op jit(solution)/shard_map/ppermute | solution.py:198
  4.0 6.4 %all-to-all-start = ((f32[4,128,128]{2,1,0:T(8,128)}), f32[4,128,128]{2,1,0:T(8,128)S(1)}, u32[]{:S(2)}, u32[]{:S(2)}) async-start(f32[4,128,128]{2,1,0:T(8,128)} %get-tuple-element.15), calls=%async_computation | async-start | bytes 524288 | tf_op jit(solution)/shard_map/all_to_all | solution.py:216
  10.4 1.5 %collective-permute-start.1 = (f32[2,128,128]{2,1,0:T(8,128)S(1)}, f32[2,128,128]{2,1,0:T(8,128)S(1)}, u32[]{:S(2)}, u32[]{:S(2)}) collective-permute-start(f32[2,128,128]{2,1,0:T(8,128)S(1)} %collective-permute-done.refs_0_.held), channel_id=1, source_target_pairs={{0,2},{1,3},{2,0},{3,1},{4,6},{5,7},{6,4},{7,5},{8,10},{9,11},{10,... | collective-permute-start | bytes 393224 | tf_op jit(solution)/shard_map/ppermute | solution.py:17
  12.0 1.4 %collective-permute-start.2 = (f32[2,128,128]{2,1,0:T(8,128)S(1)}, f32[2,128,128]{2,1,0:T(8,128)S(1)}, u32[]{:S(2)}, u32[]{:S(2)}) collective-permute-start(f32[2,128,128]{2,1,0:T(8,128)S(1)} %collective-permute-done.refs_0_.held), channel_id=1, source_target_pairs={{0,1},{1,0},{2,3},{3,2},{4,5},{5,4},{6,7},{7,6},{8,9},{9,8},{10,11... | collective-permute-start | bytes 393224 | tf_op jit(solution)/shard_map/ppermute | solution.py:17
  13.4 2.7 %collective-permute-done.1.refs_1_ = f32[2,128,128]{2,1,0:T(8,128)S(1)} collective-permute-done((f32[2,128,128]{2,1,0:T(8,128)S(1)}, f32[2,128,128]{2,1,0:T(8,128)S(1)}, u32[]{:S(2)}, u32[]{:S(2)}) %collective-permute-start.1) | collective-permute-done | bytes 131104 | tf_op jit(solution)/shard_map/ppermute | solution.py:17
  16.1 0.8 %collective-permute-start.3 = (f32[2,128,128]{2,1,0:T(8,128)S(1)}, f32[2,128,128]{2,1,0:T(8,128)S(1)}, u32[]{:S(2)}, u32[]{:S(2)}) collective-permute-start(f32[2,128,128]{2,1,0:T(8,128)S(1)} %collective-permute-done.1.refs_1_), channel_id=1, source_target_pairs={{0,1},{1,0},{2,3},{3,2},{4,5},{5,4},{6,7},{7,6},{8,9},{9,8},{10,11... | collective-permute-start | bytes 393224 | tf_op jit(solution)/shard_map/ppermute | solution.py:17
  17.1 0.4 %collective-permute-start.5 = (f32[128,256]{1,0:T(8,128)S(1)}, f32[128,256]{1,0:T(8,128)S(1)}, u32[]{:S(2)}, u32[]{:S(2)}) collective-permute-start(f32[128,256]{1,0:T(8,128)S(1)} %get-tuple-element.17), channel_id=1, source_target_pairs={{0,4},{4,0},{8,12},{12,8},{16,20},{20,16},{24,28},{28,24},{1,5},{5... | collective-permute-start | bytes 393224 | tf_op jit(solution)/shard_map/ppermute | solution.py:17
  17.5 0.4 %collective-permute-done.3.refs_3_ = f32[2,128,128]{2,1,0:T(8,128)S(1)} collective-permute-done((f32[2,128,128]{2,1,0:T(8,128)S(1)}, f32[2,128,128]{2,1,0:T(8,128)S(1)}, u32[]{:S(2)}, u32[]{:S(2)}) %collective-permute-start.3) | collective-permute-done | bytes 131104 | tf_op jit(solution)/shard_map/ppermute | solution.py:17
  17.9 1.2 %all-to-all-done.refs_4_ = f32[4,128,128]{2,1,0:T(8,128)S(1)} async-done(((f32[4,128,128]{2,1,0:T(8,128)}), f32[4,128,128]{2,1,0:T(8,128)S(1)}, u32[]{:S(2)}, u32[]{:S(2)}) %all-to-all-start) | async-done | bytes 262176 | tf_op jit(solution)/shard_map/all_to_all | solution.py:216
  19.1 0.4 %shard_map.60.both = f32[256,128]{1,0:T(8,128)S(1)} custom-call(f32[2,128,128]{2,1,0:T(8,128)S(1)} %collective-permute-done.refs_0_.held, f32[2,128,128]{2,1,0:T(8,128)S(1)} %collective-permute-done.1.refs_1_, f32[2,128,128]{2,1,0:T(8,128)S(1)} %collective-permute-done.2.refs_2_, f32[2,128,128]{2,1,0:T(8,128)S(1)} %collective-permute-done.3.refs_3_, ...), custom_call_target="tpu_custom_call" | custom-call | flops 1000 | bytes 1000 | tf_op jit(solution)/shard_map/pallas_call | solution.py:89
  19.5 1.7 %collective-permute-start.4 = (f32[256,128]{1,0:T(8,128)S(1)}, f32[256,128]{1,0:T(8,128)S(1)}, u32[]{:S(2)}, u32[]{:S(2)}) collective-permute-start(f32[256,128]{1,0:T(8,128)S(1)} %shard_map.60.both), channel_id=1, source_target_pairs={{0,4},{4,0},{8,12},{12,8},{16,20},{20,16},{24,28},{28,24},{1,5},{5... | collective-permute-start | bytes 393224 | tf_op jit(solution)/shard_map/ppermute | solution.py:17
  21.2 1.3 %collective-permute-done.5.near = f32[128,256]{1,0:T(8,128)S(1)} collective-permute-done((f32[128,256]{1,0:T(8,128)S(1)}, f32[128,256]{1,0:T(8,128)S(1)}, u32[]{:S(2)}, u32[]{:S(2)}) %collective-permute-start.5) | collective-permute-done | bytes 131104 | tf_op jit(solution)/shard_map/ppermute | solution.py:17
  22.6 3.0 %collective-permute-done.4.got = f32[256,128]{1,0:T(8,128)S(1)} collective-permute-done((f32[256,128]{1,0:T(8,128)S(1)}, f32[256,128]{1,0:T(8,128)S(1)}, u32[]{:S(2)}, u32[]{:S(2)}) %collective-permute-start.4) | collective-permute-done | bytes 131104 | tf_op jit(solution)/shard_map/ppermute | solution.py:17
  25.6 0.3 shard_map.62
  25.9 0.3 collective-permute-start.6
  26.1 1.7 %collective-permute-start.9 = (f32[64,128]{1,0:T(8,128)S(1)}, f32[64,128]{1,0:T(8,128)S(1)}, u32[]{:S(2)}, u32[]{:S(2)}) collective-permute-start(f32[64,128]{1,0:T(8,128)S(1)} %get-tuple-element.23), channel_id=1, source_target_pairs={{0,8},{4,12},{8,0},{12,4},{16,24},{20,28},{24,16},{28,20},{1,9},{5... | collective-permute-start | bytes 98312 | tf_op jit(solution)/shard_map/ppermute | solution.py:17
  27.9 2.4 %collective-permute-start.10 = (f32[64,128]{1,0:T(8,128)S(1)}, f32[64,128]{1,0:T(8,128)S(1)}, u32[]{:S(2)}, u32[]{:S(2)}) collective-permute-start(f32[64,128]{1,0:T(8,128)S(1)} %get-tuple-element.24), channel_id=1, source_target_pairs={{0,16},{4,20},{8,24},{12,28},{16,0},{20,4},{24,8},{28,12},{1,17},{... | collective-permute-start | bytes 98312 | tf_op jit(solution)/shard_map/ppermute | solution.py:17
  30.2 0.3 collective-permute-start.11
  30.5 1.5 %collective-permute-start.7 = (f32[32,128]{1,0:T(8,128)S(1)}, f32[32,128]{1,0:T(8,128)S(1)}, u32[]{:S(2)}, u32[]{:S(2)}) collective-permute-start(f32[32,128]{1,0:T(8,128)S(1)} %get-tuple-element.20), channel_id=1, source_target_pairs={{0,2},{1,3},{2,0},{3,1},{4,6},{5,7},{6,4},{7,5},{8,10},{9,11},{10,... | collective-permute-start | bytes 49160 | tf_op jit(solution)/shard_map/ppermute | solution.py:17
  32.1 2.2 %collective-permute-done.7.refs_2_ = f32[32,128]{1,0:T(8,128)S(1)} collective-permute-done((f32[32,128]{1,0:T(8,128)S(1)}, f32[32,128]{1,0:T(8,128)S(1)}, u32[]{:S(2)}, u32[]{:S(2)}) %collective-permute-start.7) | collective-permute-done | bytes 16416 | tf_op jit(solution)/shard_map/ppermute | solution.py:17
  34.3 0.9 %collective-permute-done.8.refs_3_ = f32[32,128]{1,0:T(8,128)S(1)} collective-permute-done((f32[32,128]{1,0:T(8,128)S(1)}, f32[32,128]{1,0:T(8,128)S(1)}, u32[]{:S(2)}, u32[]{:S(2)}) %collective-permute-start.8) | collective-permute-done | bytes 16416 | tf_op jit(solution)/shard_map/ppermute | solution.py:17
  35.2 0.6 %shard_map.63 = f32[32,512]{1,0:T(8,128)} custom-call(f32[32,128]{1,0:T(8,128)S(1)} %get-tuple-element.18.refs_0_, f32[32,128]{1,0:T(8,128)S(1)} %collective-permute-done.6.refs_1_, f32[32,128]{1,0:T(8,128)S(1)} %collective-permute-done.7.refs_2_, f32[32,128]{1,0:T(8,128)S(1)} %collective-permute-done.8.refs_3_), custom_call_target="tpu_custom_call" | custom-call | flops 1000 | bytes 1000 | tf_op jit(solution)/shard_map/pallas_call | solution.py:180
  35.9 0.6 %add_add_fusion = f32[64,128]{1,0:T(8,128)} fusion(f32[64,128]{1,0:T(8,128)S(1)} %collective-permute-done.11, f32[64,128]{1,0:T(8,128)S(1)} %collective-permute-done.10, f32[64,128]{1,0:T(8,128)S(1)} %get-tuple-element.22, f32[64,128]{1,0:T(8,128)S(1)} %collective-permute-done.9), kind=kLoop, calls=%fused_computation | loop fusion | flops 24576 | bytes 163840 | tf_op jit(solution)/shard_map/add | solution.py:228
  (12 shorter events, 0.2 us)
Async XLA Ops:
  2.4 8.0 %collective-permute-start = (f32[2,128,128]{2,1,0:T(8,128)}, f32[2,128,128]{2,1,0:T(8,128)S(1)}, u32[]{:S(2)}, u32[]{:S(2)}) collective-permute-start(f32[2,128,128]{2,1,0:T(8,128)} %get-tuple-element.14), channel_id=1, source_target_pairs={{0,0},{1,4},{2,2},{3,6},{4,1},{5,5},{6,3},{7,7},{8,8},{9,12},{10,1... | collective-permute-start | bytes 393224 | tf_op jit(solution)/shard_map/ppermute | solution.py:198
  4.0 12.9 %copy-start = (f32[1,1,128,512]{3,2,1,0:T(8,128)S(1)}, f32[1,1,128,512]{3,2,1,0:T(8,128)}, u32[]{:S(2)}) copy-start(f32[1,1,128,512]{3,2,1,0:T(8,128)} %param.6) | copy-start | bytes 786436
  4.0 15.1 %all-to-all-start = ((f32[4,128,128]{2,1,0:T(8,128)}), f32[4,128,128]{2,1,0:T(8,128)S(1)}, u32[]{:S(2)}, u32[]{:S(2)}) async-start(f32[4,128,128]{2,1,0:T(8,128)} %get-tuple-element.15), calls=%async_computation | async-start | bytes 524288 | tf_op jit(solution)/shard_map/all_to_all | solution.py:216
  10.4 5.7 %collective-permute-start.1 = (f32[2,128,128]{2,1,0:T(8,128)S(1)}, f32[2,128,128]{2,1,0:T(8,128)S(1)}, u32[]{:S(2)}, u32[]{:S(2)}) collective-permute-start(f32[2,128,128]{2,1,0:T(8,128)S(1)} %collective-permute-done.refs_0_.held), channel_id=1, source_target_pairs={{0,2},{1,3},{2,0},{3,1},{4,6},{5,7},{6,4},{7,5},{8,10},{9,11},{10,... | collective-permute-start | bytes 393224 | tf_op jit(solution)/shard_map/ppermute | solution.py:17
  12.0 5.6 %collective-permute-start.2 = (f32[2,128,128]{2,1,0:T(8,128)S(1)}, f32[2,128,128]{2,1,0:T(8,128)S(1)}, u32[]{:S(2)}, u32[]{:S(2)}) collective-permute-start(f32[2,128,128]{2,1,0:T(8,128)S(1)} %collective-permute-done.refs_0_.held), channel_id=1, source_target_pairs={{0,1},{1,0},{2,3},{3,2},{4,5},{5,4},{6,7},{7,6},{8,9},{9,8},{10,11... | collective-permute-start | bytes 393224 | tf_op jit(solution)/shard_map/ppermute | solution.py:17
  16.1 1.8 %collective-permute-start.3 = (f32[2,128,128]{2,1,0:T(8,128)S(1)}, f32[2,128,128]{2,1,0:T(8,128)S(1)}, u32[]{:S(2)}, u32[]{:S(2)}) collective-permute-start(f32[2,128,128]{2,1,0:T(8,128)S(1)} %collective-permute-done.1.refs_1_), channel_id=1, source_target_pairs={{0,1},{1,0},{2,3},{3,2},{4,5},{5,4},{6,7},{7,6},{8,9},{9,8},{10,11... | collective-permute-start | bytes 393224 | tf_op jit(solution)/shard_map/ppermute | solution.py:17
  17.1 8.5 %copy-start.1 = (f32[64,128]{1,0:T(8,128)S(1)}, f32[64,128]{1,0:T(8,128)}, u32[]{:S(2)}) copy-start(f32[64,128]{1,0:T(8,128)} %dinv.1) | copy-start | bytes 98308
  17.1 5.5 %collective-permute-start.5 = (f32[128,256]{1,0:T(8,128)S(1)}, f32[128,256]{1,0:T(8,128)S(1)}, u32[]{:S(2)}, u32[]{:S(2)}) collective-permute-start(f32[128,256]{1,0:T(8,128)S(1)} %get-tuple-element.17), channel_id=1, source_target_pairs={{0,4},{4,0},{8,12},{12,8},{16,20},{20,16},{24,28},{28,24},{1,5},{5... | collective-permute-start | bytes 393224 | tf_op jit(solution)/shard_map/ppermute | solution.py:17
  19.5 6.1 %collective-permute-start.4 = (f32[256,128]{1,0:T(8,128)S(1)}, f32[256,128]{1,0:T(8,128)S(1)}, u32[]{:S(2)}, u32[]{:S(2)}) collective-permute-start(f32[256,128]{1,0:T(8,128)S(1)} %shard_map.60.both), channel_id=1, source_target_pairs={{0,4},{4,0},{8,12},{12,8},{16,20},{20,16},{24,28},{28,24},{1,5},{5... | collective-permute-start | bytes 393224 | tf_op jit(solution)/shard_map/ppermute | solution.py:17
  25.9 6.2 %collective-permute-start.6 = (f32[32,128]{1,0:T(8,128)S(1)}, f32[32,128]{1,0:T(8,128)S(1)}, u32[]{:S(2)}, u32[]{:S(2)}) collective-permute-start(f32[32,128]{1,0:T(8,128)S(1)} %get-tuple-element.19), channel_id=1, source_target_pairs={{0,1},{1,0},{2,3},{3,2},{4,5},{5,4},{6,7},{7,6},{8,9},{9,8},{10,11... | collective-permute-start | bytes 49160 | tf_op jit(solution)/shard_map/ppermute | solution.py:17
  26.1 9.7 %collective-permute-start.9 = (f32[64,128]{1,0:T(8,128)S(1)}, f32[64,128]{1,0:T(8,128)S(1)}, u32[]{:S(2)}, u32[]{:S(2)}) collective-permute-start(f32[64,128]{1,0:T(8,128)S(1)} %get-tuple-element.23), channel_id=1, source_target_pairs={{0,8},{4,12},{8,0},{12,4},{16,24},{20,28},{24,16},{28,20},{1,9},{5... | collective-permute-start | bytes 98312 | tf_op jit(solution)/shard_map/ppermute | solution.py:17
  27.9 8.0 %collective-permute-start.10 = (f32[64,128]{1,0:T(8,128)S(1)}, f32[64,128]{1,0:T(8,128)S(1)}, u32[]{:S(2)}, u32[]{:S(2)}) collective-permute-start(f32[64,128]{1,0:T(8,128)S(1)} %get-tuple-element.24), channel_id=1, source_target_pairs={{0,16},{4,20},{8,24},{12,28},{16,0},{20,4},{24,8},{28,12},{1,17},{... | collective-permute-start | bytes 98312 | tf_op jit(solution)/shard_map/ppermute | solution.py:17
  30.2 5.7 %collective-permute-start.11 = (f32[64,128]{1,0:T(8,128)S(1)}, f32[64,128]{1,0:T(8,128)S(1)}, u32[]{:S(2)}, u32[]{:S(2)}) collective-permute-start(f32[64,128]{1,0:T(8,128)S(1)} %get-tuple-element.25), channel_id=1, source_target_pairs={{0,24},{4,28},{8,16},{12,20},{16,8},{20,12},{24,0},{28,4},{1,25},{... | collective-permute-start | bytes 98312 | tf_op jit(solution)/shard_map/ppermute | solution.py:17
  30.5 3.7 %collective-permute-start.7 = (f32[32,128]{1,0:T(8,128)S(1)}, f32[32,128]{1,0:T(8,128)S(1)}, u32[]{:S(2)}, u32[]{:S(2)}) collective-permute-start(f32[32,128]{1,0:T(8,128)S(1)} %get-tuple-element.20), channel_id=1, source_target_pairs={{0,2},{1,3},{2,0},{3,1},{4,6},{5,7},{6,4},{7,5},{8,10},{9,11},{10,... | collective-permute-start | bytes 49160 | tf_op jit(solution)/shard_map/ppermute | solution.py:17
  32.1 3.2 %collective-permute-start.8 = (f32[32,128]{1,0:T(8,128)S(1)}, f32[32,128]{1,0:T(8,128)S(1)}, u32[]{:S(2)}, u32[]{:S(2)}) collective-permute-start(f32[32,128]{1,0:T(8,128)S(1)} %get-tuple-element.21), channel_id=1, source_target_pairs={{0,3},{1,2},{2,1},{3,0},{4,7},{5,6},{6,5},{7,4},{8,11},{9,10},{10,... | collective-permute-start | bytes 49160 | tf_op jit(solution)/shard_map/ppermute | solution.py:17

commit v12 on v11

--- a/solution.py
+++ b/solution.py
@@ -70,7 +70,7 @@
 
 def partials_kernel(count, *refs):
     pieces = refs[: 2 * count]
-    columns, both = refs[2 * count :]
+    columns, _, both = refs[2 * count :]
     block_cols, rows, _ = pieces[0].shape
     col_index = lax.axis_index("col")
     left, right = [], []
@@ -84,16 +84,16 @@
     both[pl.ds(pl.multiple_of(rows - here, 8), rows), :] = summed[rows:]
 
 
-def partials(pieces, columns):
+def partials(pieces, columns, near):
     shape = (2 * pieces[0].shape[1], columns.shape[2])
     return pl.pallas_call(
         functools.partial(partials_kernel, len(pieces) // 2),
         out_shape=jax.ShapeDtypeStruct(shape, jnp.float32),
-        in_specs=[WHOLE] * (len(pieces) + 1),
+        in_specs=[WHOLE] * (len(pieces) + 1) + [pl.BlockSpec(memory_space=pl.ANY)],
         out_specs=WHOLE,
         cost_estimate=LIGHT,
         compiler_params=ROOM,
-    )(*pieces, columns)
+    )(*pieces, columns, near)
 
 
 def halves_kernel(tall, own, held, stay, go):
@@ -219,7 +219,7 @@
     stay, go = halves(own, pieces[0], width // groups_row)
     near = flipped(go, "row", 1)
 
-    both = partials(pieces, columns.reshape(-1, order, span))
+    both = partials(pieces, columns.reshape(-1, order, span), near)
     got = flipped(both, "row", 1)
     flips = tuple(range(0, groups_row, 2))
     along, outward = finish(both, got, stay, near, dinv, order, flips, groups_col)

time: 36.8 us -> 36.8 us (level)
  transfers between devices with their start and end apart: 13 -> 13, of which waited for: 8 -> 6; matrix products, arithmetic and copies ran while one was open for 0% -> 0% of each run, Pallas kernels for 3% -> 2%
where the time goes in v12:
time: 36.8 us; the launch traced here: 36.5 us
  starting transfers between devices  20.2 us (55%)
  waiting for transfers between devices  11.7 us (32%)
  Pallas kernels  3.26 us (9%)
  between operations  0.68 us (2%)
  other arithmetic  0.63 us (2%)
    ppermute x11, starting transfers between devices, flipped(): lax.ppermute(value, axis, [(i, i ^ flip) for i in range(lax.axis_size(axi...  12.2 us
    ppermute x11, waiting for transfers between devices, flipped(): lax.ppermute(value, axis, [(i, i ^ flip) for i in range(lax.axis_size(axi...  10.8 us
    all_to_all x1, starting transfers between devices, local(): columns = lax.all_to_all(copies, 'row', 0, 0, axis_index_groups=lines)  6.45 us
    pallas_call x1, Pallas kernels, prepare(): pl.pallas_call(prepare_kernel, out_shape=(jax.ShapeDtypeStruct((block_col...  1.8 us
    ppermute x1, starting transfers between devices, pair_rows(): held = lax.ppermute(masked, ('row', 'col'), cross)  1.55 us
    all_to_all x1, waiting for transfers between devices, local(): columns = lax.all_to_all(copies, 'row', 0, 0, axis_index_groups=lines)  0.94 us
  transfers between devices with their start and end apart: 13, of which 6 were waited for; matrix products, arithmetic and copies ran while one was open for 0% of the time, Pallas kernels for 2%

profile of v12, /device:TPU:0, one launch (start us, length us, event | category | flops | bytes accessed | tf_op | source)
XLA Modules:
  0.0 36.5 jit_solution(1195598873859531350)
XLA Ops:
  0.6 1.8 %shard_map.59 = (f32[2,128,128]{2,1,0:T(8,128)}, f32[4,128,128]{2,1,0:T(8,128)}) custom-call(s32[2]{0:T(128)} %bitcast.8, f32[256,128]{1,0:T(8,128)} %bitcast.6, f32[128,512]{1,0:T(8,128)} %bitcast.4), custom_call_target="tpu_custom_call" | custom-call | flops 1000 | bytes 1000 | tf_op jit(solution)/shard_map/pallas_call | solution.py:59
  2.4 1.6 %collective-permute-start = (f32[2,128,128]{2,1,0:T(8,128)}, f32[2,128,128]{2,1,0:T(8,128)S(1)}, u32[]{:S(2)}, u32[]{:S(2)}) collective-permute-start(f32[2,128,128]{2,1,0:T(8,128)} %get-tuple-element.14), channel_id=1, source_target_pairs={{0,0},{1,4},{2,2},{3,6},{4,1},{5,5},{6,3},{7,7},{8,8},{9,12},{10,1... | collective-permute-start | bytes 393224 | tf_op jit(solution)/shard_map/ppermute | solution.py:198
  4.0 6.4 %all-to-all-start = ((f32[4,128,128]{2,1,0:T(8,128)}), f32[4,128,128]{2,1,0:T(8,128)S(1)}, u32[]{:S(2)}, u32[]{:S(2)}) async-start(f32[4,128,128]{2,1,0:T(8,128)} %get-tuple-element.15), calls=%async_computation | async-start | bytes 524288 | tf_op jit(solution)/shard_map/all_to_all | solution.py:216
  10.4 1.5 %collective-permute-start.1 = (f32[2,128,128]{2,1,0:T(8,128)S(1)}, f32[2,128,128]{2,1,0:T(8,128)S(1)}, u32[]{:S(2)}, u32[]{:S(2)}) collective-permute-start(f32[2,128,128]{2,1,0:T(8,128)S(1)} %collective-permute-done.held.refs_0_), channel_id=1, source_target_pairs={{0,2},{1,3},{2,0},{3,1},{4,6},{5,7},{6,4},{7,5},{8,10},{9,11},{10,... | collective-permute-start | bytes 393224 | tf_op jit(solution)/shard_map/ppermute | solution.py:17
  12.0 0.1 shard_map.60
  12.1 0.0 copy-start.1
  12.1 1.9 %collective-permute-start.4 = (f32[128,256]{1,0:T(8,128)S(1)}, f32[128,256]{1,0:T(8,128)S(1)}, u32[]{:S(2)}, u32[]{:S(2)}) collective-permute-start(f32[128,256]{1,0:T(8,128)S(1)} %get-tuple-element.16), channel_id=1, source_target_pairs={{0,4},{4,0},{8,12},{12,8},{16,20},{20,16},{24,28},{28,24},{1,5},{5... | collective-permute-start | bytes 393224 | tf_op jit(solution)/shard_map/ppermute | solution.py:17
  14.1 2.1 %collective-permute-done.1.refs_1_ = f32[2,128,128]{2,1,0:T(8,128)S(1)} collective-permute-done((f32[2,128,128]{2,1,0:T(8,128)S(1)}, f32[2,128,128]{2,1,0:T(8,128)S(1)}, u32[]{:S(2)}, u32[]{:S(2)}) %collective-permute-start.1) | collective-permute-done | bytes 131104 | tf_op jit(solution)/shard_map/ppermute | solution.py:17
  16.1 0.8 %collective-permute-start.3 = (f32[2,128,128]{2,1,0:T(8,128)S(1)}, f32[2,128,128]{2,1,0:T(8,128)S(1)}, u32[]{:S(2)}, u32[]{:S(2)}) collective-permute-start(f32[2,128,128]{2,1,0:T(8,128)S(1)} %collective-permute-done.1.refs_1_), channel_id=1, source_target_pairs={{0,1},{1,0},{2,3},{3,2},{4,5},{5,4},{6,7},{7,6},{8,9},{9,8},{10,11... | collective-permute-start | bytes 393224 | tf_op jit(solution)/shard_map/ppermute | solution.py:17
  16.9 1.2 %collective-permute-done.4.refs_5_.near = f32[128,256]{1,0:T(8,128)S(1)} collective-permute-done((f32[128,256]{1,0:T(8,128)S(1)}, f32[128,256]{1,0:T(8,128)S(1)}, u32[]{:S(2)}, u32[]{:S(2)}) %collective-permute-start.4) | collective-permute-done | bytes 131104 | tf_op jit(solution)/shard_map/ppermute | solution.py:17
  18.2 0.9 %all-to-all-done.refs_4_ = f32[4,128,128]{2,1,0:T(8,128)S(1)} async-done(((f32[4,128,128]{2,1,0:T(8,128)}), f32[4,128,128]{2,1,0:T(8,128)S(1)}, u32[]{:S(2)}, u32[]{:S(2)}) %all-to-all-start) | async-done | bytes 262176 | tf_op jit(solution)/shard_map/all_to_all | solution.py:216
  19.1 0.4 %shard_map.61.both = f32[256,128]{1,0:T(8,128)S(1)} custom-call(f32[2,128,128]{2,1,0:T(8,128)S(1)} %collective-permute-done.held.refs_0_, f32[2,128,128]{2,1,0:T(8,128)S(1)} %collective-permute-done.1.refs_1_, f32[2,128,128]{2,1,0:T(8,128)S(1)} %collective-permute-done.2.refs_2_, f32[2,128,128]{2,1,0:T(8,128)S(1)} %collective-permute-done.3.refs_3_, ...), custom_call_target="tpu_custom_call" | custom-call | flops 1000 | bytes 1000 | tf_op jit(solution)/shard_map/pallas_call | solution.py:89
  19.5 1.7 %collective-permute-start.5 = (f32[256,128]{1,0:T(8,128)S(1)}, f32[256,128]{1,0:T(8,128)S(1)}, u32[]{:S(2)}, u32[]{:S(2)}) collective-permute-start(f32[256,128]{1,0:T(8,128)S(1)} %shard_map.61.both), channel_id=1, source_target_pairs={{0,4},{4,0},{8,12},{12,8},{16,20},{20,16},{24,28},{28,24},{1,5},{5... | collective-permute-start | bytes 393224 | tf_op jit(solution)/shard_map/ppermute | solution.py:17
  21.2 4.3 %collective-permute-done.5.got = f32[256,128]{1,0:T(8,128)S(1)} collective-permute-done((f32[256,128]{1,0:T(8,128)S(1)}, f32[256,128]{1,0:T(8,128)S(1)}, u32[]{:S(2)}, u32[]{:S(2)}) %collective-permute-start.5) | collective-permute-done | bytes 131104 | tf_op jit(solution)/shard_map/ppermute | solution.py:17
  25.6 0.3 shard_map.62
  25.9 0.3 collective-permute-start.6
  26.1 0.8 %collective-permute-start.9 = (f32[64,128]{1,0:T(8,128)S(1)}, f32[64,128]{1,0:T(8,128)S(1)}, u32[]{:S(2)}, u32[]{:S(2)}) collective-permute-start(f32[64,128]{1,0:T(8,128)S(1)} %get-tuple-element.23), channel_id=1, source_target_pairs={{0,8},{4,12},{8,0},{12,4},{16,24},{20,28},{24,16},{28,20},{1,9},{5... | collective-permute-start | bytes 98312 | tf_op jit(solution)/shard_map/ppermute | solution.py:17
  26.9 2.3 %collective-permute-start.10 = (f32[64,128]{1,0:T(8,128)S(1)}, f32[64,128]{1,0:T(8,128)S(1)}, u32[]{:S(2)}, u32[]{:S(2)}) collective-permute-start(f32[64,128]{1,0:T(8,128)S(1)} %get-tuple-element.24), channel_id=1, source_target_pairs={{0,16},{4,20},{8,24},{12,28},{16,0},{20,4},{24,8},{28,12},{1,17},{... | collective-permute-start | bytes 98312 | tf_op jit(solution)/shard_map/ppermute | solution.py:17
  29.2 1.3 %collective-permute-start.11 = (f32[64,128]{1,0:T(8,128)S(1)}, f32[64,128]{1,0:T(8,128)S(1)}, u32[]{:S(2)}, u32[]{:S(2)}) collective-permute-start(f32[64,128]{1,0:T(8,128)S(1)} %get-tuple-element.25), channel_id=1, source_target_pairs={{0,24},{4,28},{8,16},{12,20},{16,8},{20,12},{24,0},{28,4},{1,25},{... | collective-permute-start | bytes 98312 | tf_op jit(solution)/shard_map/ppermute | solution.py:17
  30.5 1.5 %collective-permute-start.7 = (f32[32,128]{1,0:T(8,128)S(1)}, f32[32,128]{1,0:T(8,128)S(1)}, u32[]{:S(2)}, u32[]{:S(2)}) collective-permute-start(f32[32,128]{1,0:T(8,128)S(1)} %get-tuple-element.20), channel_id=1, source_target_pairs={{0,2},{1,3},{2,0},{3,1},{4,6},{5,7},{6,4},{7,5},{8,10},{9,11},{10,... | collective-permute-start | bytes 49160 | tf_op jit(solution)/shard_map/ppermute | solution.py:17
  32.1 2.2 %collective-permute-done.7.refs_2_ = f32[32,128]{1,0:T(8,128)S(1)} collective-permute-done((f32[32,128]{1,0:T(8,128)S(1)}, f32[32,128]{1,0:T(8,128)S(1)}, u32[]{:S(2)}, u32[]{:S(2)}) %collective-permute-start.7) | collective-permute-done | bytes 16416 | tf_op jit(solution)/shard_map/ppermute | solution.py:17
  34.3 0.9 %collective-permute-done.8.refs_3_ = f32[32,128]{1,0:T(8,128)S(1)} collective-permute-done((f32[32,128]{1,0:T(8,128)S(1)}, f32[32,128]{1,0:T(8,128)S(1)}, u32[]{:S(2)}, u32[]{:S(2)}) %collective-permute-start.8) | collective-permute-done | bytes 16416 | tf_op jit(solution)/shard_map/ppermute | solution.py:17
  35.2 0.6 %shard_map.63 = f32[32,512]{1,0:T(8,128)} custom-call(f32[32,128]{1,0:T(8,128)S(1)} %get-tuple-element.18.refs_0_, f32[32,128]{1,0:T(8,128)S(1)} %collective-permute-done.6.refs_1_, f32[32,128]{1,0:T(8,128)S(1)} %collective-permute-done.7.refs_2_, f32[32,128]{1,0:T(8,128)S(1)} %collective-permute-done.8.refs_3_), custom_call_target="tpu_custom_call" | custom-call | flops 1000 | bytes 1000 | tf_op jit(solution)/shard_map/pallas_call | solution.py:180
  35.9 0.6 %add_add_fusion = f32[64,128]{1,0:T(8,128)} fusion(f32[64,128]{1,0:T(8,128)S(1)} %collective-permute-done.11, f32[64,128]{1,0:T(8,128)S(1)} %collective-permute-done.10, f32[64,128]{1,0:T(8,128)S(1)} %get-tuple-element.22, f32[64,128]{1,0:T(8,128)S(1)} %collective-permute-done.9), kind=kLoop, calls=%fused_computation | loop fusion | flops 24576 | bytes 163840 | tf_op jit(solution)/shard_map/add | solution.py:228
  (12 shorter events, 0.0 us)
Async XLA Ops:
  2.4 8.0 %collective-permute-start = (f32[2,128,128]{2,1,0:T(8,128)}, f32[2,128,128]{2,1,0:T(8,128)S(1)}, u32[]{:S(2)}, u32[]{:S(2)}) collective-permute-start(f32[2,128,128]{2,1,0:T(8,128)} %get-tuple-element.14), channel_id=1, source_target_pairs={{0,0},{1,4},{2,2},{3,6},{4,1},{5,5},{6,3},{7,7},{8,8},{9,12},{10,1... | collective-permute-start | bytes 393224 | tf_op jit(solution)/shard_map/ppermute | solution.py:198
  4.0 8.0 %copy-start = (f32[1,1,128,512]{3,2,1,0:T(8,128)S(1)}, f32[1,1,128,512]{3,2,1,0:T(8,128)}, u32[]{:S(2)}) copy-start(f32[1,1,128,512]{3,2,1,0:T(8,128)} %param.6) | copy-start | bytes 786436
  4.0 15.1 %all-to-all-start = ((f32[4,128,128]{2,1,0:T(8,128)}), f32[4,128,128]{2,1,0:T(8,128)S(1)}, u32[]{:S(2)}, u32[]{:S(2)}) async-start(f32[4,128,128]{2,1,0:T(8,128)} %get-tuple-element.15), calls=%async_computation | async-start | bytes 524288 | tf_op jit(solution)/shard_map/all_to_all | solution.py:216
  10.4 5.7 %collective-permute-start.1 = (f32[2,128,128]{2,1,0:T(8,128)S(1)}, f32[2,128,128]{2,1,0:T(8,128)S(1)}, u32[]{:S(2)}, u32[]{:S(2)}) collective-permute-start(f32[2,128,128]{2,1,0:T(8,128)S(1)} %collective-permute-done.held.refs_0_), channel_id=1, source_target_pairs={{0,2},{1,3},{2,0},{3,1},{4,6},{5,7},{6,4},{7,5},{8,10},{9,11},{10,... | collective-permute-start | bytes 393224 | tf_op jit(solution)/shard_map/ppermute | solution.py:17
  12.1 13.5 %copy-start.1 = (f32[64,128]{1,0:T(8,128)S(1)}, f32[64,128]{1,0:T(8,128)}, u32[]{:S(2)}) copy-start(f32[64,128]{1,0:T(8,128)} %dinv.1) | copy-start | bytes 98308
  12.1 6.1 %collective-permute-start.4 = (f32[128,256]{1,0:T(8,128)S(1)}, f32[128,256]{1,0:T(8,128)S(1)}, u32[]{:S(2)}, u32[]{:S(2)}) collective-permute-start(f32[128,256]{1,0:T(8,128)S(1)} %get-tuple-element.16), channel_id=1, source_target_pairs={{0,4},{4,0},{8,12},{12,8},{16,20},{20,16},{24,28},{28,24},{1,5},{5... | collective-permute-start | bytes 393224 | tf_op jit(solution)/shard_map/ppermute | solution.py:17
  14.1 2.9 %collective-permute-start.2 = (f32[2,128,128]{2,1,0:T(8,128)S(1)}, f32[2,128,128]{2,1,0:T(8,128)S(1)}, u32[]{:S(2)}, u32[]{:S(2)}) collective-permute-start(f32[2,128,128]{2,1,0:T(8,128)S(1)} %collective-permute-done.held.refs_0_), channel_id=1, source_target_pairs={{0,1},{1,0},{2,3},{3,2},{4,5},{5,4},{6,7},{7,6},{8,9},{9,8},{10,11... | collective-permute-start | bytes 393224 | tf_op jit(solution)/shard_map/ppermute | solution.py:17
  16.1 2.1 %collective-permute-start.3 = (f32[2,128,128]{2,1,0:T(8,128)S(1)}, f32[2,128,128]{2,1,0:T(8,128)S(1)}, u32[]{:S(2)}, u32[]{:S(2)}) collective-permute-start(f32[2,128,128]{2,1,0:T(8,128)S(1)} %collective-permute-done.1.refs_1_), channel_id=1, source_target_pairs={{0,1},{1,0},{2,3},{3,2},{4,5},{5,4},{6,7},{7,6},{8,9},{9,8},{10,11... | collective-permute-start | bytes 393224 | tf_op jit(solution)/shard_map/ppermute | solution.py:17
  19.5 6.1 %collective-permute-start.5 = (f32[256,128]{1,0:T(8,128)S(1)}, f32[256,128]{1,0:T(8,128)S(1)}, u32[]{:S(2)}, u32[]{:S(2)}) collective-permute-start(f32[256,128]{1,0:T(8,128)S(1)} %shard_map.61.both), channel_id=1, source_target_pairs={{0,4},{4,0},{8,12},{12,8},{16,20},{20,16},{24,28},{28,24},{1,5},{5... | collective-permute-start | bytes 393224 | tf_op jit(solution)/shard_map/ppermute | solution.py:17
  25.9 6.2 %collective-permute-start.6 = (f32[32,128]{1,0:T(8,128)S(1)}, f32[32,128]{1,0:T(8,128)S(1)}, u32[]{:S(2)}, u32[]{:S(2)}) collective-permute-start(f32[32,128]{1,0:T(8,128)S(1)} %get-tuple-element.19), channel_id=1, source_target_pairs={{0,1},{1,0},{2,3},{3,2},{4,5},{5,4},{6,7},{7,6},{8,9},{9,8},{10,11... | collective-permute-start | bytes 49160 | tf_op jit(solution)/shard_map/ppermute | solution.py:17
  26.1 9.7 %collective-permute-start.9 = (f32[64,128]{1,0:T(8,128)S(1)}, f32[64,128]{1,0:T(8,128)S(1)}, u32[]{:S(2)}, u32[]{:S(2)}) collective-permute-start(f32[64,128]{1,0:T(8,128)S(1)} %get-tuple-element.23), channel_id=1, source_target_pairs={{0,8},{4,12},{8,0},{12,4},{16,24},{20,28},{24,16},{28,20},{1,9},{5... | collective-permute-start | bytes 98312 | tf_op jit(solution)/shard_map/ppermute | solution.py:17
  26.9 9.0 %collective-permute-start.10 = (f32[64,128]{1,0:T(8,128)S(1)}, f32[64,128]{1,0:T(8,128)S(1)}, u32[]{:S(2)}, u32[]{:S(2)}) collective-permute-start(f32[64,128]{1,0:T(8,128)S(1)} %get-tuple-element.24), channel_id=1, source_target_pairs={{0,16},{4,20},{8,24},{12,28},{16,0},{20,4},{24,8},{28,12},{1,17},{... | collective-permute-start | bytes 98312 | tf_op jit(solution)/shard_map/ppermute | solution.py:17
  29.2 6.7 %collective-permute-start.11 = (f32[64,128]{1,0:T(8,128)S(1)}, f32[64,128]{1,0:T(8,128)S(1)}, u32[]{:S(2)}, u32[]{:S(2)}) collective-permute-start(f32[64,128]{1,0:T(8,128)S(1)} %get-tuple-element.25), channel_id=1, source_target_pairs={{0,24},{4,28},{8,16},{12,20},{16,8},{20,12},{24,0},{28,4},{1,25},{... | collective-permute-start | bytes 98312 | tf_op jit(solution)/shard_map/ppermute | solution.py:17
  30.5 3.7 %collective-permute-start.7 = (f32[32,128]{1,0:T(8,128)S(1)}, f32[32,128]{1,0:T(8,128)S(1)}, u32[]{:S(2)}, u32[]{:S(2)}) collective-permute-start(f32[32,128]{1,0:T(8,128)S(1)} %get-tuple-element.20), channel_id=1, source_target_pairs={{0,2},{1,3},{2,0},{3,1},{4,6},{5,7},{6,4},{7,5},{8,10},{9,11},{10,... | collective-permute-start | bytes 49160 | tf_op jit(solution)/shard_map/ppermute | solution.py:17
  32.1 3.2 %collective-permute-start.8 = (f32[32,128]{1,0:T(8,128)S(1)}, f32[32,128]{1,0:T(8,128)S(1)}, u32[]{:S(2)}, u32[]{:S(2)}) collective-permute-start(f32[32,128]{1,0:T(8,128)S(1)} %get-tuple-element.21), channel_id=1, source_target_pairs={{0,3},{1,2},{2,1},{3,0},{4,7},{5,6},{6,5},{7,4},{8,11},{9,10},{10,... | collective-permute-start | bytes 49160 | tf_op jit(solution)/shard_map/ppermute | solution.py:17

commit v13 on v12

--- a/solution.py
+++ b/solution.py
@@ -10,6 +10,7 @@
 LANES = 128
 WHOLE = pl.BlockSpec(memory_space=pltpu.VMEM)
 ROOM = pltpu.CompilerParams(vmem_limit_bytes=16 * 1024 * 1024)
+HEAVY = 10**11
 LIGHT = pl.CostEstimate(flops=1000, bytes_accessed=1000, transcendentals=0)
 
 
@@ -32,11 +33,9 @@
     return once(left_high, right_high) + (once(left_high, right_low) + once(left_low, right_high))
 
 
-def prepare_kernel(presence, blocks, factor, masked, copies):
-    count, rows, span = copies.shape
-    mine = factor[:, pl.ds(pl.multiple_of(lax.axis_index("col") * span, LANES), span)]
-    for i in range(count):
-        copies[i] = mine
+def prepare_kernel(presence, blocks, factor, masked, mine):
+    rows, span = mine.shape
+    mine[...] = factor[:, pl.ds(pl.multiple_of(lax.axis_index("col") * span, LANES), span)]
     block_cols, _, order = masked.shape
     for a in range(rows // order):
         for b in range(block_cols):
@@ -45,7 +44,7 @@
             masked[b, pl.ds(a * order, order), :] = picked * weight
 
 
-def prepare(presence, blocks, own, receivers, span):
+def prepare(presence, blocks, own, span):
     rows, width = own.shape
     block_cols = blocks.shape[0] // rows
     order = blocks.shape[1]
@@ -54,18 +53,36 @@
         mine = lax.dynamic_slice_in_dim(own, first, span, 1)
         weights = presence.reshape(-1, 1, block_cols, 1).astype(jnp.float32)
         picked = blocks.reshape(-1, order, block_cols, order) * weights
-        masked = picked.transpose(2, 0, 1, 3).reshape(block_cols, rows, order)
-        return masked, jnp.broadcast_to(mine[None], (receivers, rows, span))
+        return picked.transpose(2, 0, 1, 3).reshape(block_cols, rows, order), mine
     return pl.pallas_call(
         prepare_kernel,
         out_shape=(
             jax.ShapeDtypeStruct((block_cols, rows, order), jnp.float32),
-            jax.ShapeDtypeStruct((receivers, rows, span), jnp.float32),
+            jax.ShapeDtypeStruct((rows, span), jnp.float32),
         ),
         in_specs=[pl.BlockSpec(memory_space=pltpu.SMEM), WHOLE, WHOLE],
         out_specs=(WHOLE, WHOLE),
         cost_estimate=LIGHT,
     )(presence, blocks, own)
+
+
+def joined_kernel(bit, first, second, out):
+    here = jnp.where((lax.axis_index("row") & bit) == 0, 0, 1)
+    out[:, here] = first[...]
+    out[:, 1 - here] = second[...]
+
+
+def joined(first, second, bit):
+    count, rows, span = first.shape
+    both = pl.pallas_call(
+        functools.partial(joined_kernel, bit),
+        out_shape=jax.ShapeDtypeStruct((count, 2, rows, span), jnp.float32),
+        in_specs=[WHOLE, WHOLE],
+        out_specs=WHOLE,
+        cost_estimate=pl.CostEstimate(flops=HEAVY, bytes_accessed=1000, transcendentals=0),
+        compiler_params=ROOM,
+    )(first, second)
+    return both.reshape(2 * count, rows, span)
 
 
 def partials_kernel(count, *refs):
@@ -200,6 +217,15 @@
     return held + [flipped(piece, "col", 1) for piece in held]
 
 
+def along_line(mine):
+    strips = mine[None]
+    bit = lax.axis_size("row") // 2
+    while bit > 1:
+        strips = joined(strips, flipped(strips, "row", bit), bit)
+        bit //= 2
+    return strips
+
+
 def local(inverse_set, presence, factor, dinv):
     groups_row = lax.axis_size("row")
     groups_col = lax.axis_size("col")
@@ -211,15 +237,14 @@
 
     own = factor.reshape(rows, width)
     blocks = inverse_set.reshape(rows * block_cols, order)
-    masked, copies = prepare(presence.reshape(-1), blocks, own, groups_row // 2, span)
-    lines = [list(range(bit, groups_row, 2)) for bit in range(2)]
-    columns = lax.all_to_all(copies, "row", 0, 0, axis_index_groups=lines)
-    columns = columns.reshape(groups_row // 2, block_rows, order, span).transpose(1, 0, 2, 3)
+    masked, mine = prepare(presence.reshape(-1), blocks, own, span)
+    columns = along_line(mine).reshape(-1, block_rows, order, span).transpose(1, 0, 2, 3)
+    columns = columns.reshape(-1, order, span)
     pieces = pair_rows(masked)
     stay, go = halves(own, pieces[0], width // groups_row)
     near = flipped(go, "row", 1)
 
-    both = partials(pieces, columns.reshape(-1, order, span), near)
+    both = partials(pieces, columns, near)
     got = flipped(both, "row", 1)
     flips = tuple(range(0, groups_row, 2))
     along, outward = finish(both, got, stay, near, dinv, order, flips, groups_col)

time: 36.8 us -> 36.5 us (level)
  waiting for transfers between devices: 11.7 us -> 10.6 us
  local copies, waits for them, and re-layouts: 0.01 us -> 0.85 us
    ppermute x11 -> x13, starting transfers between devices: 12.2 us -> 18.6 us  [flipped(): lax.ppermute(value, axis, [(i, i ^ flip) for i in range(lax.axis_size(axi...]
    all_to_all x1 -> x0, starting transfers between devices: 6.45 us -> none  [local(): columns = lax.all_to_all(copies, 'row', 0, 0, axis_index_groups=lines)]
    all_to_all x1 -> x0, waiting for transfers between devices: 0.94 us -> none  [local(): columns = lax.all_to_all(copies, 'row', 0, 0, axis_index_groups=lines)]
    unnamed x4 -> x6, local copies, waits for them, and re-layouts: 0.01 us -> 0.85 us
    ppermute x11 -> x13, waiting for transfers between devices: 10.8 us -> 10.6 us  [flipped(): lax.ppermute(value, axis, [(i, i ^ flip) for i in range(lax.axis_size(axi...]
  transfers between devices with their start and end apart: 13 -> 14, of which waited for: 6 -> 5; matrix products, arithmetic and copies ran while one was open for 0% -> 0% of each run, Pallas kernels for 2% -> 2%
where the time goes in v13:
time: 36.5 us; the launch traced here: 36.3 us
  starting transfers between devices  20.3 us (56%)
  waiting for transfers between devices  10.6 us (29%)
  Pallas kernels  3.22 us (9%)
  local copies, waits for them, and re-layouts  0.85 us (2%)
  between operations  0.7 us (2%)
  other arithmetic  0.63 us (2%)
    ppermute x13, starting transfers between devices, flipped(): lax.ppermute(value, axis, [(i, i ^ flip) for i in range(lax.axis_size(axi...  18.6 us
    ppermute x13, waiting for transfers between devices, flipped(): lax.ppermute(value, axis, [(i, i ^ flip) for i in range(lax.axis_size(axi...  10.6 us
    pallas_call x1, Pallas kernels, prepare(): pl.pallas_call(prepare_kernel, out_shape=(jax.ShapeDtypeStruct((block_col...  1.72 us
    ppermute x1, starting transfers between devices, pair_rows(): held = lax.ppermute(masked, ('row', 'col'), cross)  1.68 us
    unnamed x6, local copies, waits for them, and re-layouts  0.85 us
  transfers between devices with their start and end apart: 14, of which 5 were waited for; matrix products, arithmetic and copies ran while one was open for 0% of the time, Pallas kernels for 2%

profile of v13, /device:TPU:0, one launch (start us, length us, event | category | flops | bytes accessed | tf_op | source)
XLA Modules:
  0.0 36.3 jit_solution(15664301888741793705)
XLA Ops:
  0.6 1.7 %shard_map.59 = (f32[2,128,128]{2,1,0:T(8,128)}, f32[128,128]{1,0:T(8,128)}) custom-call(s32[2]{0:T(128)} %bitcast.16, f32[256,128]{1,0:T(8,128)} %bitcast.14, f32[128,512]{1,0:T(8,128)} %bitcast.7), custom_call_target="tpu_custom_call" | custom-call | flops 1000 | bytes 1000 | tf_op jit(solution)/shard_map/pallas_call | solution.py:57
  2.4 4.0 %collective-permute-start.4 = (f32[1,128,128]{2,1,0:T(8,128)}, f32[1,128,128]{2,1,0:T(8,128)S(1)}, u32[]{:S(2)}, u32[]{:S(2)}) collective-permute-start(f32[1,128,128]{2,1,0:T(8,128)} %bitcast.12), channel_id=1, source_target_pairs={{0,16},{4,20},{8,24},{12,28},{16,0},{20,4},{24,8},{28,12},{1,17},{... | collective-permute-start | bytes 196616 | tf_op jit(solution)/shard_map/ppermute | solution.py:18
  6.4 1.7 %collective-permute-start = (f32[2,128,128]{2,1,0:T(8,128)}, f32[2,128,128]{2,1,0:T(8,128)S(1)}, u32[]{:S(2)}, u32[]{:S(2)}) collective-permute-start(f32[2,128,128]{2,1,0:T(8,128)} %get-tuple-element.14), channel_id=1, source_target_pairs={{0,0},{1,4},{2,2},{3,6},{4,1},{5,5},{6,3},{7,7},{8,8},{9,12},{10,1... | collective-permute-start | bytes 393224 | tf_op jit(solution)/shard_map/ppermute | solution.py:215
  8.1 2.2 %collective-permute-done.4.second = f32[1,128,128]{2,1,0:T(8,128)S(1)} collective-permute-done((f32[1,128,128]{2,1,0:T(8,128)}, f32[1,128,128]{2,1,0:T(8,128)S(1)}, u32[]{:S(2)}, u32[]{:S(2)}) %collective-permute-start.4) | collective-permute-done | bytes 65568 | tf_op jit(solution)/shard_map/ppermute | solution.py:18
  10.2 0.8 %copy-done.2 = f32[128,128]{1,0:T(8,128)S(1)} copy-done((f32[128,128]{1,0:T(8,128)S(1)}, f32[128,128]{1,0:T(8,128)}, u32[]{:S(2)}) %copy-start.2) | copy-done | bytes 65560
  11.1 1.8 %collective-permute-start.1 = (f32[2,128,128]{2,1,0:T(8,128)S(1)}, f32[2,128,128]{2,1,0:T(8,128)S(1)}, u32[]{:S(2)}, u32[]{:S(2)}) collective-permute-start(f32[2,128,128]{2,1,0:T(8,128)S(1)} %collective-permute-done.held.refs_0_), channel_id=1, source_target_pairs={{0,2},{1,3},{2,0},{3,1},{4,6},{5,7},{6,4},{7,5},{8,10},{9,11},{10,... | collective-permute-start | bytes 393224 | tf_op jit(solution)/shard_map/ppermute | solution.py:18
  12.9 0.5 %collective-permute-start.5 = (f32[2,128,128]{2,1,0:T(8,128)S(1)}, f32[2,128,128]{2,1,0:T(8,128)S(1)}, u32[]{:S(2)}, u32[]{:S(2)}) collective-permute-start(f32[2,128,128]{2,1,0:T(8,128)S(1)} %bitcast.10), channel_id=1, source_target_pairs={{0,8},{4,12},{8,0},{12,4},{16,24},{20,28},{24,16},{28,20},{1,9},{5... | collective-permute-start | bytes 393224 | tf_op jit(solution)/shard_map/ppermute | solution.py:18
  13.4 0.1 shard_map.62
  13.5 4.3 %collective-permute-start.6 = (f32[128,256]{1,0:T(8,128)S(1)}, f32[128,256]{1,0:T(8,128)S(1)}, u32[]{:S(2)}, u32[]{:S(2)}) collective-permute-start(f32[128,256]{1,0:T(8,128)S(1)} %get-tuple-element.16), channel_id=1, source_target_pairs={{0,4},{4,0},{8,12},{12,8},{16,20},{20,16},{24,28},{28,24},{1,5},{5... | collective-permute-start | bytes 393224 | tf_op jit(solution)/shard_map/ppermute | solution.py:18
  17.8 0.5 %collective-permute-start.3 = (f32[2,128,128]{2,1,0:T(8,128)S(1)}, f32[2,128,128]{2,1,0:T(8,128)S(1)}, u32[]{:S(2)}, u32[]{:S(2)}) collective-permute-start(f32[2,128,128]{2,1,0:T(8,128)S(1)} %collective-permute-done.1.refs_1_), channel_id=1, source_target_pairs={{0,1},{1,0},{2,3},{3,2},{4,5},{5,4},{6,7},{7,6},{8,9},{9,8},{10,11... | collective-permute-start | bytes 393224 | tf_op jit(solution)/shard_map/ppermute | solution.py:18
  18.3 0.7 %collective-permute-done.5.second = f32[2,128,128]{2,1,0:T(8,128)S(1)} collective-permute-done((f32[2,128,128]{2,1,0:T(8,128)S(1)}, f32[2,128,128]{2,1,0:T(8,128)S(1)}, u32[]{:S(2)}, u32[]{:S(2)}) %collective-permute-start.5) | collective-permute-done | bytes 131104 | tf_op jit(solution)/shard_map/ppermute | solution.py:18
  19.1 2.0 %collective-permute-done.6.refs_5_.near = f32[128,256]{1,0:T(8,128)S(1)} collective-permute-done((f32[128,256]{1,0:T(8,128)S(1)}, f32[128,256]{1,0:T(8,128)S(1)}, u32[]{:S(2)}, u32[]{:S(2)}) %collective-permute-start.6) | collective-permute-done | bytes 131104 | tf_op jit(solution)/shard_map/ppermute | solution.py:18
  21.0 0.4 %shard_map.63.both = f32[256,128]{1,0:T(8,128)S(1)} custom-call(f32[2,128,128]{2,1,0:T(8,128)S(1)} %collective-permute-done.held.refs_0_, f32[2,128,128]{2,1,0:T(8,128)S(1)} %collective-permute-done.1.refs_1_, f32[2,128,128]{2,1,0:T(8,128)S(1)} %collective-permute-done.2.refs_2_, f32[2,128,128]{2,1,0:T(8,128)S(1)} %collective-permute-done.3.refs_3_, ...), custom_call_target="tpu_custom_call" | custom-call | flops 1000 | bytes 1000 | tf_op jit(solution)/shard_map/pallas_call | solution.py:106
  21.4 1.8 %collective-permute-start.7 = (f32[256,128]{1,0:T(8,128)S(1)}, f32[256,128]{1,0:T(8,128)S(1)}, u32[]{:S(2)}, u32[]{:S(2)}) collective-permute-start(f32[256,128]{1,0:T(8,128)S(1)} %shard_map.63.both), channel_id=1, source_target_pairs={{0,4},{4,0},{8,12},{12,8},{16,20},{20,16},{24,28},{28,24},{1,5},{5... | collective-permute-start | bytes 393224 | tf_op jit(solution)/shard_map/ppermute | solution.py:18
  23.2 3.2 %collective-permute-done.7.got = f32[256,128]{1,0:T(8,128)S(1)} collective-permute-done((f32[256,128]{1,0:T(8,128)S(1)}, f32[256,128]{1,0:T(8,128)S(1)}, u32[]{:S(2)}, u32[]{:S(2)}) %collective-permute-start.7) | collective-permute-done | bytes 131104 | tf_op jit(solution)/shard_map/ppermute | solution.py:18
  26.5 0.3 shard_map.64
  26.8 0.1 collective-permute-start.10
  26.9 0.8 %collective-permute-start.11 = (f32[64,128]{1,0:T(8,128)S(1)}, f32[64,128]{1,0:T(8,128)S(1)}, u32[]{:S(2)}, u32[]{:S(2)}) collective-permute-start(f32[64,128]{1,0:T(8,128)S(1)} %get-tuple-element.23), channel_id=1, source_target_pairs={{0,8},{4,12},{8,0},{12,4},{16,24},{20,28},{24,16},{28,20},{1,9},{5... | collective-permute-start | bytes 98312 | tf_op jit(solution)/shard_map/ppermute | solution.py:18
  27.7 0.7 %collective-permute-start.12 = (f32[64,128]{1,0:T(8,128)S(1)}, f32[64,128]{1,0:T(8,128)S(1)}, u32[]{:S(2)}, u32[]{:S(2)}) collective-permute-start(f32[64,128]{1,0:T(8,128)S(1)} %get-tuple-element.24), channel_id=1, source_target_pairs={{0,16},{4,20},{8,24},{12,28},{16,0},{20,4},{24,8},{28,12},{1,17},{... | collective-permute-start | bytes 98312 | tf_op jit(solution)/shard_map/ppermute | solution.py:18
  28.4 2.9 %collective-permute-start.13 = (f32[64,128]{1,0:T(8,128)S(1)}, f32[64,128]{1,0:T(8,128)S(1)}, u32[]{:S(2)}, u32[]{:S(2)}) collective-permute-start(f32[64,128]{1,0:T(8,128)S(1)} %get-tuple-element.25), channel_id=1, source_target_pairs={{0,24},{4,28},{8,16},{12,20},{16,8},{20,12},{24,0},{28,4},{1,25},{... | collective-permute-start | bytes 98312 | tf_op jit(solution)/shard_map/ppermute | solution.py:18
  31.3 1.2 %collective-permute-start.9 = (f32[32,128]{1,0:T(8,128)S(1)}, f32[32,128]{1,0:T(8,128)S(1)}, u32[]{:S(2)}, u32[]{:S(2)}) collective-permute-start(f32[32,128]{1,0:T(8,128)S(1)} %get-tuple-element.20), channel_id=1, source_target_pairs={{0,2},{1,3},{2,0},{3,1},{4,6},{5,7},{6,4},{7,5},{8,10},{9,11},{10,... | collective-permute-start | bytes 49160 | tf_op jit(solution)/shard_map/ppermute | solution.py:18
  32.5 2.5 %collective-permute-done.9.refs_2_ = f32[32,128]{1,0:T(8,128)S(1)} collective-permute-done((f32[32,128]{1,0:T(8,128)S(1)}, f32[32,128]{1,0:T(8,128)S(1)}, u32[]{:S(2)}, u32[]{:S(2)}) %collective-permute-start.9) | collective-permute-done | bytes 16416 | tf_op jit(solution)/shard_map/ppermute | solution.py:18
  35.1 0.6 %shard_map.65 = f32[32,512]{1,0:T(8,128)} custom-call(f32[32,128]{1,0:T(8,128)S(1)} %get-tuple-element.18.refs_0_, f32[32,128]{1,0:T(8,128)S(1)} %collective-permute-done.8.refs_1_, f32[32,128]{1,0:T(8,128)S(1)} %collective-permute-done.9.refs_2_, f32[32,128]{1,0:T(8,128)S(1)} %collective-permute-done.10.refs_3_), custom_call_target="tpu_custom_call" | custom-call | flops 1000 | bytes 1000 | tf_op jit(solution)/shard_map/pallas_call | solution.py:197
  35.7 0.6 %add_add_fusion = f32[64,128]{1,0:T(8,128)} fusion(f32[64,128]{1,0:T(8,128)S(1)} %collective-permute-done.13, f32[64,128]{1,0:T(8,128)S(1)} %collective-permute-done.12, f32[64,128]{1,0:T(8,128)S(1)} %get-tuple-element.22, f32[64,128]{1,0:T(8,128)S(1)} %collective-permute-done.11), kind=kLoop, calls=%fused_computation | loop fusion | flops 24576 | bytes 163840 | tf_op jit(solution)/shard_map/add | solution.py:253
  (18 shorter events, 0.1 us)
Async XLA Ops:
  2.4 7.9 %collective-permute-start.4 = (f32[1,128,128]{2,1,0:T(8,128)}, f32[1,128,128]{2,1,0:T(8,128)S(1)}, u32[]{:S(2)}, u32[]{:S(2)}) collective-permute-start(f32[1,128,128]{2,1,0:T(8,128)} %bitcast.12), channel_id=1, source_target_pairs={{0,16},{4,20},{8,24},{12,28},{16,0},{20,4},{24,8},{28,12},{1,17},{... | collective-permute-start | bytes 196616 | tf_op jit(solution)/shard_map/ppermute | solution.py:18
  6.4 7.0 %copy-start = (f32[1,1,128,512]{3,2,1,0:T(8,128)S(1)}, f32[1,1,128,512]{3,2,1,0:T(8,128)}, u32[]{:S(2)}) copy-start(f32[1,1,128,512]{3,2,1,0:T(8,128)} %param.6) | copy-start | bytes 786436
  6.4 4.7 %collective-permute-start = (f32[2,128,128]{2,1,0:T(8,128)}, f32[2,128,128]{2,1,0:T(8,128)S(1)}, u32[]{:S(2)}, u32[]{:S(2)}) collective-permute-start(f32[2,128,128]{2,1,0:T(8,128)} %get-tuple-element.14), channel_id=1, source_target_pairs={{0,0},{1,4},{2,2},{3,6},{4,1},{5,5},{6,3},{7,7},{8,8},{9,12},{10,1... | collective-permute-start | bytes 393224 | tf_op jit(solution)/shard_map/ppermute | solution.py:215
  10.2 0.8 %copy-start.2 = (f32[128,128]{1,0:T(8,128)S(1)}, f32[128,128]{1,0:T(8,128)}, u32[]{:S(2)}) copy-start(f32[128,128]{1,0:T(8,128)} %get-tuple-element.15) | copy-start | bytes 196612
  11.1 6.7 %collective-permute-start.1 = (f32[2,128,128]{2,1,0:T(8,128)S(1)}, f32[2,128,128]{2,1,0:T(8,128)S(1)}, u32[]{:S(2)}, u32[]{:S(2)}) collective-permute-start(f32[2,128,128]{2,1,0:T(8,128)S(1)} %collective-permute-done.held.refs_0_), channel_id=1, source_target_pairs={{0,2},{1,3},{2,0},{3,1},{4,6},{5,7},{6,4},{7,5},{8,10},{9,11},{10,... | collective-permute-start | bytes 393224 | tf_op jit(solution)/shard_map/ppermute | solution.py:18
  12.9 6.1 %collective-permute-start.5 = (f32[2,128,128]{2,1,0:T(8,128)S(1)}, f32[2,128,128]{2,1,0:T(8,128)S(1)}, u32[]{:S(2)}, u32[]{:S(2)}) collective-permute-start(f32[2,128,128]{2,1,0:T(8,128)S(1)} %bitcast.10), channel_id=1, source_target_pairs={{0,8},{4,12},{8,0},{12,4},{16,24},{20,28},{24,16},{28,20},{1,9},{5... | collective-permute-start | bytes 393224 | tf_op jit(solution)/shard_map/ppermute | solution.py:18
  13.5 7.5 %collective-permute-start.6 = (f32[128,256]{1,0:T(8,128)S(1)}, f32[128,256]{1,0:T(8,128)S(1)}, u32[]{:S(2)}, u32[]{:S(2)}) collective-permute-start(f32[128,256]{1,0:T(8,128)S(1)} %get-tuple-element.16), channel_id=1, source_target_pairs={{0,4},{4,0},{8,12},{12,8},{16,20},{20,16},{24,28},{28,24},{1,5},{5... | collective-permute-start | bytes 393224 | tf_op jit(solution)/shard_map/ppermute | solution.py:18
  17.8 3.2 %collective-permute-start.2 = (f32[2,128,128]{2,1,0:T(8,128)S(1)}, f32[2,128,128]{2,1,0:T(8,128)S(1)}, u32[]{:S(2)}, u32[]{:S(2)}) collective-permute-start(f32[2,128,128]{2,1,0:T(8,128)S(1)} %collective-permute-done.held.refs_0_), channel_id=1, source_target_pairs={{0,1},{1,0},{2,3},{3,2},{4,5},{5,4},{6,7},{7,6},{8,9},{9,8},{10,11... | collective-permute-start | bytes 393224 | tf_op jit(solution)/shard_map/ppermute | solution.py:18
  17.8 3.2 %collective-permute-start.3 = (f32[2,128,128]{2,1,0:T(8,128)S(1)}, f32[2,128,128]{2,1,0:T(8,128)S(1)}, u32[]{:S(2)}, u32[]{:S(2)}) collective-permute-start(f32[2,128,128]{2,1,0:T(8,128)S(1)} %collective-permute-done.1.refs_1_), channel_id=1, source_target_pairs={{0,1},{1,0},{2,3},{3,2},{4,5},{5,4},{6,7},{7,6},{8,9},{9,8},{10,11... | collective-permute-start | bytes 393224 | tf_op jit(solution)/shard_map/ppermute | solution.py:18
  21.0 5.4 %copy-start.1 = (f32[64,128]{1,0:T(8,128)S(1)}, f32[64,128]{1,0:T(8,128)}, u32[]{:S(2)}) copy-start(f32[64,128]{1,0:T(8,128)} %dinv.1) | copy-start | bytes 98308
  21.4 5.0 %collective-permute-start.7 = (f32[256,128]{1,0:T(8,128)S(1)}, f32[256,128]{1,0:T(8,128)S(1)}, u32[]{:S(2)}, u32[]{:S(2)}) collective-permute-start(f32[256,128]{1,0:T(8,128)S(1)} %shard_map.63.both), channel_id=1, source_target_pairs={{0,4},{4,0},{8,12},{12,8},{16,20},{20,16},{24,28},{28,24},{1,5},{5... | collective-permute-start | bytes 393224 | tf_op jit(solution)/shard_map/ppermute | solution.py:18
  26.8 4.5 %collective-permute-start.10 = (f32[32,128]{1,0:T(8,128)S(1)}, f32[32,128]{1,0:T(8,128)S(1)}, u32[]{:S(2)}, u32[]{:S(2)}) collective-permute-start(f32[32,128]{1,0:T(8,128)S(1)} %get-tuple-element.21), channel_id=1, source_target_pairs={{0,3},{1,2},{2,1},{3,0},{4,7},{5,6},{6,5},{7,4},{8,11},{9,10},{10,... | collective-permute-start | bytes 49160 | tf_op jit(solution)/shard_map/ppermute | solution.py:18
  26.9 8.8 %collective-permute-start.11 = (f32[64,128]{1,0:T(8,128)S(1)}, f32[64,128]{1,0:T(8,128)S(1)}, u32[]{:S(2)}, u32[]{:S(2)}) collective-permute-start(f32[64,128]{1,0:T(8,128)S(1)} %get-tuple-element.23), channel_id=1, source_target_pairs={{0,8},{4,12},{8,0},{12,4},{16,24},{20,28},{24,16},{28,20},{1,9},{5... | collective-permute-start | bytes 98312 | tf_op jit(solution)/shard_map/ppermute | solution.py:18
  27.7 8.0 %collective-permute-start.12 = (f32[64,128]{1,0:T(8,128)S(1)}, f32[64,128]{1,0:T(8,128)S(1)}, u32[]{:S(2)}, u32[]{:S(2)}) collective-permute-start(f32[64,128]{1,0:T(8,128)S(1)} %get-tuple-element.24), channel_id=1, source_target_pairs={{0,16},{4,20},{8,24},{12,28},{16,0},{20,4},{24,8},{28,12},{1,17},{... | collective-permute-start | bytes 98312 | tf_op jit(solution)/shard_map/ppermute | solution.py:18
  28.4 7.3 %collective-permute-start.13 = (f32[64,128]{1,0:T(8,128)S(1)}, f32[64,128]{1,0:T(8,128)S(1)}, u32[]{:S(2)}, u32[]{:S(2)}) collective-permute-start(f32[64,128]{1,0:T(8,128)S(1)} %get-tuple-element.25), channel_id=1, source_target_pairs={{0,24},{4,28},{8,16},{12,20},{16,8},{20,12},{24,0},{28,4},{1,25},{... | collective-permute-start | bytes 98312 | tf_op jit(solution)/shard_map/ppermute | solution.py:18
  31.3 1.2 %collective-permute-start.8 = (f32[32,128]{1,0:T(8,128)S(1)}, f32[32,128]{1,0:T(8,128)S(1)}, u32[]{:S(2)}, u32[]{:S(2)}) collective-permute-start(f32[32,128]{1,0:T(8,128)S(1)} %get-tuple-element.19), channel_id=1, source_target_pairs={{0,1},{1,0},{2,3},{3,2},{4,5},{5,4},{6,7},{7,6},{8,9},{9,8},{10,11... | collective-permute-start | bytes 49160 | tf_op jit(solution)/shard_map/ppermute | solution.py:18
  31.3 3.7 %collective-permute-start.9 = (f32[32,128]{1,0:T(8,128)S(1)}, f32[32,128]{1,0:T(8,128)S(1)}, u32[]{:S(2)}, u32[]{:S(2)}) collective-permute-start(f32[32,128]{1,0:T(8,128)S(1)} %get-tuple-element.20), channel_id=1, source_target_pairs={{0,2},{1,3},{2,0},{3,1},{4,6},{5,7},{6,4},{7,5},{8,10},{9,11},{10,... | collective-permute-start | bytes 49160 | tf_op jit(solution)/shard_map/ppermute | solution.py:18

commit v14 on v13

--- a/solution.py
+++ b/solution.py
@@ -87,8 +87,8 @@
 
 def partials_kernel(count, *refs):
     pieces = refs[: 2 * count]
-    columns, _, both = refs[2 * count :]
-    block_cols, rows, _ = pieces[0].shape
+    columns, _, both, *outward = refs[2 * count :]
+    block_cols, rows, order = pieces[0].shape
     col_index = lax.axis_index("col")
     left, right = [], []
     for t in range(count):
@@ -99,18 +99,26 @@
     here = (col_index & 1) * rows
     both[pl.ds(pl.multiple_of(here, 8), rows), :] = summed[:rows]
     both[pl.ds(pl.multiple_of(rows - here, 8), rows), :] = summed[rows:]
-
-
-def partials(pieces, columns, near):
-    shape = (2 * pieces[0].shape[1], columns.shape[2])
-    return pl.pallas_call(
+    share = order // len(outward)
+    for flip, piece in enumerate(outward):
+        start = (col_index ^ flip) * share
+        for a in range(2 * rows // order):
+            picked = both[pl.ds(pl.multiple_of(a * order + start, 8), share), :]
+            piece[pl.ds(a * share, share), :] = -picked
+
+
+def partials(pieces, columns, near, receivers):
+    rows, span = 2 * pieces[0].shape[1], columns.shape[2]
+    outward = (jax.ShapeDtypeStruct((rows // receivers, span), jnp.float32),) * receivers
+    both, *outward = pl.pallas_call(
         functools.partial(partials_kernel, len(pieces) // 2),
-        out_shape=jax.ShapeDtypeStruct(shape, jnp.float32),
+        out_shape=(jax.ShapeDtypeStruct((rows, span), jnp.float32),) + outward,
         in_specs=[WHOLE] * (len(pieces) + 1) + [pl.BlockSpec(memory_space=pl.ANY)],
-        out_specs=WHOLE,
+        out_specs=(WHOLE,) * (1 + receivers),
         cost_estimate=LIGHT,
         compiler_params=ROOM,
     )(*pieces, columns, near)
+    return both, outward
 
 
 def halves_kernel(tall, own, held, stay, go):
@@ -136,9 +144,8 @@
     )(own, held)
 
 
-def finish_kernel(order, flips, both, got, stay, near, dinv, *refs):
-    update, terms = refs[-2:]
-    along, outward = refs[: len(flips)], refs[len(flips) : -2]
+def finish_kernel(flips, both, got, stay, near, dinv, *refs):
+    along, update, terms = refs[:-2], refs[-2], refs[-1]
     rows = stay.shape[0]
     row_index = lax.axis_index("row")
     here = (row_index & 1) * rows
@@ -152,24 +159,16 @@
         slot = ((row_index ^ flip) >> 1) * tall
         piece[...] = terms[pl.ds(pl.multiple_of(slot, 8), tall), :]
     along[0][...] = along[0][...] + dinv[...]
-    share = order // len(outward)
-    for flip, piece in enumerate(outward):
-        start = here + (lax.axis_index("col") ^ flip) * share
-        for a in range(rows // order):
-            picked = update[pl.ds(pl.multiple_of(a * order + start, 8), share), :]
-            piece[pl.ds(a * share, share), :] = -picked
-
-
-def finish(both, got, stay, near, dinv, order, flips, receivers):
+
+
+def finish(both, got, stay, near, dinv, flips):
     rows, half = stay.shape
     span = both.shape[1]
-    along = (jax.ShapeDtypeStruct(dinv.shape, jnp.float32),) * len(flips)
-    outward = (jax.ShapeDtypeStruct((rows // receivers, span), jnp.float32),) * receivers
-    outs = pl.pallas_call(
-        functools.partial(finish_kernel, order, flips),
-        out_shape=along + outward,
+    return pl.pallas_call(
+        functools.partial(finish_kernel, flips),
+        out_shape=(jax.ShapeDtypeStruct(dinv.shape, jnp.float32),) * len(flips),
         in_specs=[WHOLE] * 5,
-        out_specs=(WHOLE,) * (len(flips) + receivers),
+        out_specs=(WHOLE,) * len(flips),
         scratch_shapes=[
             pltpu.VMEM((2 * rows, span), jnp.float32),
             pltpu.VMEM((half, span), jnp.float32),
@@ -177,28 +176,34 @@
         cost_estimate=LIGHT,
         compiler_params=ROOM,
     )(both, got, stay, near, dinv)
-    return outs[: len(flips)], outs[len(flips) :]
 
 
 def collect_kernel(*refs):
-    out = refs[-1]
+    keep, send = refs[-2:]
+    share = keep.shape[0]
     span = refs[0].shape[1]
-    for flip, piece in enumerate(refs[:-1]):
-        first = pl.multiple_of((lax.axis_index("col") ^ flip) * span, LANES)
-        out[:, pl.ds(first, span)] = piece[...]
+    here = (lax.axis_index("row") & 1) * share
+    for flip, piece in enumerate(refs[:-2]):
+        spot = pl.ds(pl.multiple_of((lax.axis_index("col") ^ flip) * span, LANES), span)
+        keep[:, spot] = piece[pl.ds(pl.multiple_of(here, 8), share), :]
+        send[:, spot] = piece[pl.ds(pl.multiple_of(share - here, 8), share), :]
 
 
 def collect(arrived):
     flips = len(arrived)
-    share, span = arrived[0].shape
+    share, span = arrived[0].shape[0] // 2, arrived[0].shape[1]
     if span % LANES:
         me = lax.axis_index("col")
-        return jnp.concatenate([lax.select_n(me ^ j, *arrived) for j in range(flips)], axis=1)
+        row_bit = lax.axis_index("row") & 1
+        laid = jnp.concatenate([lax.select_n(me ^ j, *arrived) for j in range(flips)], axis=1)
+        laid = laid.reshape(2, share, span * flips)
+        return [lax.dynamic_index_in_dim(laid, row_bit ^ k, 0, keepdims=False) for k in range(2)]
+    part = jax.ShapeDtypeStruct((share, span * flips), jnp.float32)
     return pl.pallas_call(
         collect_kernel,
-        out_shape=jax.ShapeDtypeStruct((share, span * flips), jnp.float32),
+        out_shape=(part, part),
         in_specs=[WHOLE] * flips,
-        out_specs=WHOLE,
+        out_specs=(WHOLE, WHOLE),
         cost_estimate=LIGHT,
         compiler_params=ROOM,
     )(*arrived)
@@ -244,16 +249,18 @@
     stay, go = halves(own, pieces[0], width // groups_row)
     near = flipped(go, "row", 1)
 
-    both = partials(pieces, columns, near)
+    both, outward = partials(pieces, columns, near, groups_col)
     got = flipped(both, "row", 1)
+    arrived = [outward[0]] + [flipped(outward[f], "col", f) for f in range(1, groups_col)]
+    keep, send = collect(arrived)
+    off_diag = keep + flipped(send, "row", 1)
+
     flips = tuple(range(0, groups_row, 2))
-    along, outward = finish(both, got, stay, near, dinv, order, flips, groups_col)
+    along = finish(both, got, stay, near, dinv, flips)
     diag_block = along[0]
     for flip, piece in zip(flips[1:], along[1:]):
         diag_block = diag_block + flipped(piece, "row", flip)
-
-    arrived = [outward[0]] + [flipped(outward[f], "col", f) for f in range(1, groups_col)]
-    return (collect(arrived).reshape(block_rows, 1, share, width), diag_block)
+    return (off_diag.reshape(block_rows, 1, share, width), diag_block)
 
 
 def solution(mesh):

time: 36.5 us -> 36.2 us (level)
  waiting for transfers between devices: 10.6 us -> 8.86 us
  starting transfers between devices: 20.3 us -> 21.2 us
  other arithmetic: 0.63 us -> 1.26 us
  Pallas kernels: 3.22 us -> 2.61 us
  local copies, waits for them, and re-layouts: 0.85 us -> 1.23 us
    ppermute x13 -> x14, waiting for transfers between devices: 10.6 us -> 8.86 us  [flipped(): lax.ppermute(value, axis, [(i, i ^ flip) for i in range(lax.axis_size(axi...]
    ppermute x13 -> x14, starting transfers between devices: 18.6 us -> 19.6 us  [flipped(): lax.ppermute(value, axis, [(i, i ^ flip) for i in range(lax.axis_size(axi...]
    reshape x0 -> x1, other arithmetic: none -> 0.64 us  [local(): return (off_diag.reshape(block_rows, 1, share, width), diag_block)]
    pallas_call x2, Pallas kernels: 0.95 us -> 0.33 us  [the longest x1 0.32 us: finish(): pl.pallas_call(functools.partial(finish_kernel, flips), out_shape=(jax.Sh...]
    unnamed x6, local copies, waits for them, and re-layouts: 0.85 us -> 1.23 us
  transfers between devices with their start and end apart: 14 -> 15, of which waited for: 5 -> 7; matrix products, arithmetic and copies ran while one was open for 0% -> 2% of each run, Pallas kernels for 2% -> 1%
where the time goes in v14:
time: 36.2 us; the launch traced here: 35.9 us
  starting transfers between devices  21.2 us (59%)
  waiting for transfers between devices  8.86 us (24%)
  Pallas kernels  2.61 us (7%)
  other arithmetic  1.26 us (3%)
  local copies, waits for them, and re-layouts  1.23 us (3%)
  between operations  0.69 us (2%)
    ppermute x14, starting transfers between devices, flipped(): lax.ppermute(value, axis, [(i, i ^ flip) for i in range(lax.axis_size(axi...  19.6 us
    ppermute x14, waiting for transfers between devices, flipped(): lax.ppermute(value, axis, [(i, i ^ flip) for i in range(lax.axis_size(axi...  8.86 us
    pallas_call x1, Pallas kernels, prepare(): pl.pallas_call(prepare_kernel, out_shape=(jax.ShapeDtypeStruct((block_col...  1.72 us
    ppermute x1, starting transfers between devices, pair_rows(): held = lax.ppermute(masked, ('row', 'col'), cross)  1.68 us
    unnamed x6, local copies, waits for them, and re-layouts  1.23 us
  transfers between devices with their start and end apart: 15, of which 7 were waited for; matrix products, arithmetic and copies ran while one was open for 2% of the time, Pallas kernels for 1%

profile of v14, /device:TPU:0, one launch (start us, length us, event | category | flops | bytes accessed | tf_op | source)
XLA Modules:
  0.0 35.9 jit_solution(3143503034262340093)
XLA Ops:
  0.6 1.7 %shard_map.59 = (f32[2,128,128]{2,1,0:T(8,128)}, f32[128,128]{1,0:T(8,128)}) custom-call(s32[2]{0:T(128)} %bitcast.16, f32[256,128]{1,0:T(8,128)} %bitcast.15, f32[128,512]{1,0:T(8,128)} %bitcast.8), custom_call_target="tpu_custom_call" | custom-call | flops 1000 | bytes 1000 | tf_op jit(solution)/shard_map/pallas_call | solution.py:57
  2.4 4.0 %collective-permute-start.4 = (f32[1,128,128]{2,1,0:T(8,128)}, f32[1,128,128]{2,1,0:T(8,128)S(1)}, u32[]{:S(2)}, u32[]{:S(2)}) collective-permute-start(f32[1,128,128]{2,1,0:T(8,128)} %bitcast.13), channel_id=1, source_target_pairs={{0,16},{4,20},{8,24},{12,28},{16,0},{20,4},{24,8},{28,12},{1,17},{... | collective-permute-start | bytes 196616 | tf_op jit(solution)/shard_map/ppermute | solution.py:18
  6.4 1.7 %collective-permute-start = (f32[2,128,128]{2,1,0:T(8,128)}, f32[2,128,128]{2,1,0:T(8,128)S(1)}, u32[]{:S(2)}, u32[]{:S(2)}) collective-permute-start(f32[2,128,128]{2,1,0:T(8,128)} %get-tuple-element.17), channel_id=1, source_target_pairs={{0,0},{1,4},{2,2},{3,6},{4,1},{5,5},{6,3},{7,7},{8,8},{9,12},{10,1... | collective-permute-start | bytes 393224 | tf_op jit(solution)/shard_map/ppermute | solution.py:220
  8.1 2.2 %collective-permute-done.4.second = f32[1,128,128]{2,1,0:T(8,128)S(1)} collective-permute-done((f32[1,128,128]{2,1,0:T(8,128)}, f32[1,128,128]{2,1,0:T(8,128)S(1)}, u32[]{:S(2)}, u32[]{:S(2)}) %collective-permute-start.4) | collective-permute-done | bytes 65568 | tf_op jit(solution)/shard_map/ppermute | solution.py:18
  10.2 0.8 %copy-done.2 = f32[128,128]{1,0:T(8,128)S(1)} copy-done((f32[128,128]{1,0:T(8,128)S(1)}, f32[128,128]{1,0:T(8,128)}, u32[]{:S(2)}) %copy-start.2) | copy-done | bytes 65560
  11.1 1.8 %collective-permute-start.1 = (f32[2,128,128]{2,1,0:T(8,128)S(1)}, f32[2,128,128]{2,1,0:T(8,128)S(1)}, u32[]{:S(2)}, u32[]{:S(2)}) collective-permute-start(f32[2,128,128]{2,1,0:T(8,128)S(1)} %collective-permute-done.held.refs_0_), channel_id=1, source_target_pairs={{0,2},{1,3},{2,0},{3,1},{4,6},{5,7},{6,4},{7,5},{8,10},{9,11},{10,... | collective-permute-start | bytes 393224 | tf_op jit(solution)/shard_map/ppermute | solution.py:18
  12.9 0.5 %collective-permute-start.5 = (f32[2,128,128]{2,1,0:T(8,128)S(1)}, f32[2,128,128]{2,1,0:T(8,128)S(1)}, u32[]{:S(2)}, u32[]{:S(2)}) collective-permute-start(f32[2,128,128]{2,1,0:T(8,128)S(1)} %bitcast.11), channel_id=1, source_target_pairs={{0,8},{4,12},{8,0},{12,4},{16,24},{20,28},{24,16},{28,20},{1,9},{5... | collective-permute-start | bytes 393224 | tf_op jit(solution)/shard_map/ppermute | solution.py:18
  13.5 4.3 %collective-permute-start.6 = (f32[128,256]{1,0:T(8,128)S(1)}, f32[128,256]{1,0:T(8,128)S(1)}, u32[]{:S(2)}, u32[]{:S(2)}) collective-permute-start(f32[128,256]{1,0:T(8,128)S(1)} %get-tuple-element.19), channel_id=1, source_target_pairs={{0,4},{4,0},{8,12},{12,8},{16,20},{20,16},{24,28},{28,24},{1,5},{5... | collective-permute-start | bytes 393224 | tf_op jit(solution)/shard_map/ppermute | solution.py:18
  17.8 0.5 %collective-permute-start.3 = (f32[2,128,128]{2,1,0:T(8,128)S(1)}, f32[2,128,128]{2,1,0:T(8,128)S(1)}, u32[]{:S(2)}, u32[]{:S(2)}) collective-permute-start(f32[2,128,128]{2,1,0:T(8,128)S(1)} %collective-permute-done.1.refs_1_), channel_id=1, source_target_pairs={{0,1},{1,0},{2,3},{3,2},{4,5},{5,4},{6,7},{7,6},{8,9},{9,8},{10,11... | collective-permute-start | bytes 393224 | tf_op jit(solution)/shard_map/ppermute | solution.py:18
  18.3 0.7 %collective-permute-done.5.second = f32[2,128,128]{2,1,0:T(8,128)S(1)} collective-permute-done((f32[2,128,128]{2,1,0:T(8,128)S(1)}, f32[2,128,128]{2,1,0:T(8,128)S(1)}, u32[]{:S(2)}, u32[]{:S(2)}) %collective-permute-start.5) | collective-permute-done | bytes 131104 | tf_op jit(solution)/shard_map/ppermute | solution.py:18
  19.2 1.9 %collective-permute-done.6.refs_5_.near = f32[128,256]{1,0:T(8,128)S(1)} collective-permute-done((f32[128,256]{1,0:T(8,128)S(1)}, f32[128,256]{1,0:T(8,128)S(1)}, u32[]{:S(2)}, u32[]{:S(2)}) %collective-permute-start.6) | collective-permute-done | bytes 131104 | tf_op jit(solution)/shard_map/ppermute | solution.py:18
  21.0 0.4 %shard_map.63 = (f32[256,128]{1,0:T(8,128)S(1)}, f32[64,128]{1,0:T(8,128)S(1)}, f32[64,128]{1,0:T(8,128)S(1)}, f32[64,128]{1,0:T(8,128)S(1)}, f32[64,128]{1,0:T(8,128)S(1)}) custom-call(f32[2,128,128]{2,1,0:T(8,128)S(1)} %collective-permute-done.held.refs_0_, f32[2,128,128]{2,1,0:T(8,128)S(1)} %collective-permute-done.1.refs_1_, ...), custom_call_target="tpu_custom_call" | custom-call | flops 1000 | bytes 1000 | tf_op jit(solution)/shard_map/pallas_call | solution.py:113
  21.4 1.8 %collective-permute-start.11 = (f32[256,128]{1,0:T(8,128)S(1)}, f32[256,128]{1,0:T(8,128)S(1)}, u32[]{:S(2)}, u32[]{:S(2)}) collective-permute-start(f32[256,128]{1,0:T(8,128)S(1)} %get-tuple-element.26.both), channel_id=1, source_target_pairs={{0,4},{4,0},{8,12},{12,8},{16,20},{20,16},{24,28},{28,24},{1,5},{5... | collective-permute-start | bytes 393224 | tf_op jit(solution)/shard_map/ppermute | solution.py:18
  23.2 0.5 %collective-permute-start.8 = (f32[64,128]{1,0:T(8,128)S(1)}, f32[64,128]{1,0:T(8,128)S(1)}, u32[]{:S(2)}, u32[]{:S(2)}) collective-permute-start(f32[64,128]{1,0:T(8,128)S(1)} %get-tuple-element.22), channel_id=1, source_target_pairs={{0,2},{1,3},{2,0},{3,1},{4,6},{5,7},{6,4},{7,5},{8,10},{9,11},{10,... | collective-permute-start | bytes 98312 | tf_op jit(solution)/shard_map/ppermute | solution.py:18
  23.7 1.4 %collective-permute-start.9 = (f32[64,128]{1,0:T(8,128)S(1)}, f32[64,128]{1,0:T(8,128)S(1)}, u32[]{:S(2)}, u32[]{:S(2)}) collective-permute-start(f32[64,128]{1,0:T(8,128)S(1)} %get-tuple-element.23), channel_id=1, source_target_pairs={{0,3},{1,2},{2,1},{3,0},{4,7},{5,6},{6,5},{7,4},{8,11},{9,10},{10,... | collective-permute-start | bytes 98312 | tf_op jit(solution)/shard_map/ppermute | solution.py:18
  25.1 2.3 %collective-permute-done.8.refs_2_ = f32[64,128]{1,0:T(8,128)S(1)} collective-permute-done((f32[64,128]{1,0:T(8,128)S(1)}, f32[64,128]{1,0:T(8,128)S(1)}, u32[]{:S(2)}, u32[]{:S(2)}) %collective-permute-start.8) | collective-permute-done | bytes 32800 | tf_op jit(solution)/shard_map/ppermute | solution.py:18
  27.5 0.3 collective-permute-start.10
  27.8 0.4 %copy-done.1 = f32[64,128]{1,0:T(8,128)S(1)} copy-done((f32[64,128]{1,0:T(8,128)S(1)}, f32[64,128]{1,0:T(8,128)}, u32[]{:S(2)}) %copy-start.1) | copy-done | bytes 32792
  28.5 0.7 %collective-permute-start.12 = (f32[64,128]{1,0:T(8,128)S(1)}, f32[64,128]{1,0:T(8,128)S(1)}, u32[]{:S(2)}, u32[]{:S(2)}) collective-permute-start(f32[64,128]{1,0:T(8,128)S(1)} %get-tuple-element.29), channel_id=1, source_target_pairs={{0,8},{4,12},{8,0},{12,4},{16,24},{20,28},{24,16},{28,20},{1,9},{5... | collective-permute-start | bytes 98312 | tf_op jit(solution)/shard_map/ppermute | solution.py:18
  29.5 3.5 %collective-permute-start.14 = (f32[64,128]{1,0:T(8,128)S(1)}, f32[64,128]{1,0:T(8,128)S(1)}, u32[]{:S(2)}, u32[]{:S(2)}) collective-permute-start(f32[64,128]{1,0:T(8,128)S(1)} %get-tuple-element.31), channel_id=1, source_target_pairs={{0,24},{4,28},{8,16},{12,20},{16,8},{20,12},{24,0},{28,4},{1,25},{... | collective-permute-start | bytes 98312 | tf_op jit(solution)/shard_map/ppermute | solution.py:18
  33.0 0.6 %add_bitcast_fusion = f32[1,1,32,512]{3,2,1,0:T(8,128)} fusion(f32[32,512]{1,0:T(8,128)S(1)} %get-tuple-element.24, f32[32,512]{1,0:T(8,128)S(1)} %collective-permute-done.10), kind=kLoop, calls=%fused_computation | loop fusion | flops 16384 | bytes 196608 | tf_op jit(solution)/shard_map/reshape | solution.py:263
  33.6 0.9 %collective-permute-done.13 = f32[64,128]{1,0:T(8,128)S(1)} collective-permute-done((f32[64,128]{1,0:T(8,128)S(1)}, f32[64,128]{1,0:T(8,128)S(1)}, u32[]{:S(2)}, u32[]{:S(2)}) %collective-permute-start.13) | collective-permute-done | bytes 32800 | tf_op jit(solution)/shard_map/ppermute | solution.py:18
  34.5 0.8 %collective-permute-done.14 = f32[64,128]{1,0:T(8,128)S(1)} collective-permute-done((f32[64,128]{1,0:T(8,128)S(1)}, f32[64,128]{1,0:T(8,128)S(1)}, u32[]{:S(2)}, u32[]{:S(2)}) %collective-permute-start.14) | collective-permute-done | bytes 32800 | tf_op jit(solution)/shard_map/ppermute | solution.py:18
  35.3 0.6 %add_add_fusion = f32[64,128]{1,0:T(8,128)} fusion(f32[64,128]{1,0:T(8,128)S(1)} %collective-permute-done.14, f32[64,128]{1,0:T(8,128)S(1)} %collective-permute-done.13, f32[64,128]{1,0:T(8,128)S(1)} %get-tuple-element.28, f32[64,128]{1,0:T(8,128)S(1)} %collective-permute-done.12), kind=kLoop, calls=%fused_computation.1 | loop fusion | flops 24576 | bytes 163840 | tf_op jit(solution)/shard_map/add | solution.py:262
  (21 shorter events, 0.9 us)
Async XLA Ops:
  2.4 7.9 %collective-permute-start.4 = (f32[1,128,128]{2,1,0:T(8,128)}, f32[1,128,128]{2,1,0:T(8,128)S(1)}, u32[]{:S(2)}, u32[]{:S(2)}) collective-permute-start(f32[1,128,128]{2,1,0:T(8,128)} %bitcast.13), channel_id=1, source_target_pairs={{0,16},{4,20},{8,24},{12,28},{16,0},{20,4},{24,8},{28,12},{1,17},{... | collective-permute-start | bytes 196616 | tf_op jit(solution)/shard_map/ppermute | solution.py:18
  6.4 7.0 %copy-start = (f32[1,1,128,512]{3,2,1,0:T(8,128)S(1)}, f32[1,1,128,512]{3,2,1,0:T(8,128)}, u32[]{:S(2)}) copy-start(f32[1,1,128,512]{3,2,1,0:T(8,128)} %param.6) | copy-start | bytes 786436
  6.4 4.7 %collective-permute-start = (f32[2,128,128]{2,1,0:T(8,128)}, f32[2,128,128]{2,1,0:T(8,128)S(1)}, u32[]{:S(2)}, u32[]{:S(2)}) collective-permute-start(f32[2,128,128]{2,1,0:T(8,128)} %get-tuple-element.17), channel_id=1, source_target_pairs={{0,0},{1,4},{2,2},{3,6},{4,1},{5,5},{6,3},{7,7},{8,8},{9,12},{10,1... | collective-permute-start | bytes 393224 | tf_op jit(solution)/shard_map/ppermute | solution.py:220
  10.2 0.8 %copy-start.2 = (f32[128,128]{1,0:T(8,128)S(1)}, f32[128,128]{1,0:T(8,128)}, u32[]{:S(2)}) copy-start(f32[128,128]{1,0:T(8,128)} %get-tuple-element.18) | copy-start | bytes 196612
  11.1 6.7 %collective-permute-start.1 = (f32[2,128,128]{2,1,0:T(8,128)S(1)}, f32[2,128,128]{2,1,0:T(8,128)S(1)}, u32[]{:S(2)}, u32[]{:S(2)}) collective-permute-start(f32[2,128,128]{2,1,0:T(8,128)S(1)} %collective-permute-done.held.refs_0_), channel_id=1, source_target_pairs={{0,2},{1,3},{2,0},{3,1},{4,6},{5,7},{6,4},{7,5},{8,10},{9,11},{10,... | collective-permute-start | bytes 393224 | tf_op jit(solution)/shard_map/ppermute | solution.py:18
  12.9 6.1 %collective-permute-start.5 = (f32[2,128,128]{2,1,0:T(8,128)S(1)}, f32[2,128,128]{2,1,0:T(8,128)S(1)}, u32[]{:S(2)}, u32[]{:S(2)}) collective-permute-start(f32[2,128,128]{2,1,0:T(8,128)S(1)} %bitcast.11), channel_id=1, source_target_pairs={{0,8},{4,12},{8,0},{12,4},{16,24},{20,28},{24,16},{28,20},{1,9},{5... | collective-permute-start | bytes 393224 | tf_op jit(solution)/shard_map/ppermute | solution.py:18
  13.5 7.5 %collective-permute-start.6 = (f32[128,256]{1,0:T(8,128)S(1)}, f32[128,256]{1,0:T(8,128)S(1)}, u32[]{:S(2)}, u32[]{:S(2)}) collective-permute-start(f32[128,256]{1,0:T(8,128)S(1)} %get-tuple-element.19), channel_id=1, source_target_pairs={{0,4},{4,0},{8,12},{12,8},{16,20},{20,16},{24,28},{28,24},{1,5},{5... | collective-permute-start | bytes 393224 | tf_op jit(solution)/shard_map/ppermute | solution.py:18
  17.8 1.3 %collective-permute-start.2 = (f32[2,128,128]{2,1,0:T(8,128)S(1)}, f32[2,128,128]{2,1,0:T(8,128)S(1)}, u32[]{:S(2)}, u32[]{:S(2)}) collective-permute-start(f32[2,128,128]{2,1,0:T(8,128)S(1)} %collective-permute-done.held.refs_0_), channel_id=1, source_target_pairs={{0,1},{1,0},{2,3},{3,2},{4,5},{5,4},{6,7},{7,6},{8,9},{9,8},{10,11... | collective-permute-start | bytes 393224 | tf_op jit(solution)/shard_map/ppermute | solution.py:18
  17.8 3.2 %collective-permute-start.3 = (f32[2,128,128]{2,1,0:T(8,128)S(1)}, f32[2,128,128]{2,1,0:T(8,128)S(1)}, u32[]{:S(2)}, u32[]{:S(2)}) collective-permute-start(f32[2,128,128]{2,1,0:T(8,128)S(1)} %collective-permute-done.1.refs_1_), channel_id=1, source_target_pairs={{0,1},{1,0},{2,3},{3,2},{4,5},{5,4},{6,7},{7,6},{8,9},{9,8},{10,11... | collective-permute-start | bytes 393224 | tf_op jit(solution)/shard_map/ppermute | solution.py:18
  21.4 6.4 %collective-permute-start.11 = (f32[256,128]{1,0:T(8,128)S(1)}, f32[256,128]{1,0:T(8,128)S(1)}, u32[]{:S(2)}, u32[]{:S(2)}) collective-permute-start(f32[256,128]{1,0:T(8,128)S(1)} %get-tuple-element.26.both), channel_id=1, source_target_pairs={{0,4},{4,0},{8,12},{12,8},{16,20},{20,16},{24,28},{28,24},{1,5},{5... | collective-permute-start | bytes 393224 | tf_op jit(solution)/shard_map/ppermute | solution.py:18
  23.2 1.9 %collective-permute-start.7 = (f32[64,128]{1,0:T(8,128)S(1)}, f32[64,128]{1,0:T(8,128)S(1)}, u32[]{:S(2)}, u32[]{:S(2)}) collective-permute-start(f32[64,128]{1,0:T(8,128)S(1)} %get-tuple-element.21), channel_id=1, source_target_pairs={{0,1},{1,0},{2,3},{3,2},{4,5},{5,4},{6,7},{7,6},{8,9},{9,8},{10,11... | collective-permute-start | bytes 98312 | tf_op jit(solution)/shard_map/ppermute | solution.py:18
  23.2 4.2 %collective-permute-start.8 = (f32[64,128]{1,0:T(8,128)S(1)}, f32[64,128]{1,0:T(8,128)S(1)}, u32[]{:S(2)}, u32[]{:S(2)}) collective-permute-start(f32[64,128]{1,0:T(8,128)S(1)} %get-tuple-element.22), channel_id=1, source_target_pairs={{0,2},{1,3},{2,0},{3,1},{4,6},{5,7},{6,4},{7,5},{8,10},{9,11},{10,... | collective-permute-start | bytes 98312 | tf_op jit(solution)/shard_map/ppermute | solution.py:18
  23.7 3.7 %collective-permute-start.9 = (f32[64,128]{1,0:T(8,128)S(1)}, f32[64,128]{1,0:T(8,128)S(1)}, u32[]{:S(2)}, u32[]{:S(2)}) collective-permute-start(f32[64,128]{1,0:T(8,128)S(1)} %get-tuple-element.23), channel_id=1, source_target_pairs={{0,3},{1,2},{2,1},{3,0},{4,7},{5,6},{6,5},{7,4},{8,11},{9,10},{10,... | collective-permute-start | bytes 98312 | tf_op jit(solution)/shard_map/ppermute | solution.py:18
  27.4 0.8 %copy-start.1 = (f32[64,128]{1,0:T(8,128)S(1)}, f32[64,128]{1,0:T(8,128)}, u32[]{:S(2)}) copy-start(f32[64,128]{1,0:T(8,128)} %dinv.1) | copy-start | bytes 98308
  27.5 5.5 %collective-permute-start.10 = (f32[32,512]{1,0:T(8,128)S(1)}, f32[32,512]{1,0:T(8,128)S(1)}, u32[]{:S(2)}, u32[]{:S(2)}) collective-permute-start(f32[32,512]{1,0:T(8,128)S(1)} %get-tuple-element.25), channel_id=1, source_target_pairs={{0,4},{4,0},{8,12},{12,8},{16,20},{20,16},{24,28},{28,24},{1,5},{5... | collective-permute-start | bytes 196616 | tf_op jit(solution)/shard_map/ppermute | solution.py:18
  28.5 5.1 %collective-permute-start.12 = (f32[64,128]{1,0:T(8,128)S(1)}, f32[64,128]{1,0:T(8,128)S(1)}, u32[]{:S(2)}, u32[]{:S(2)}) collective-permute-start(f32[64,128]{1,0:T(8,128)S(1)} %get-tuple-element.29), channel_id=1, source_target_pairs={{0,8},{4,12},{8,0},{12,4},{16,24},{20,28},{24,16},{28,20},{1,9},{5... | collective-permute-start | bytes 98312 | tf_op jit(solution)/shard_map/ppermute | solution.py:18
  29.2 5.3 %collective-permute-start.13 = (f32[64,128]{1,0:T(8,128)S(1)}, f32[64,128]{1,0:T(8,128)S(1)}, u32[]{:S(2)}, u32[]{:S(2)}) collective-permute-start(f32[64,128]{1,0:T(8,128)S(1)} %get-tuple-element.30), channel_id=1, source_target_pairs={{0,16},{4,20},{8,24},{12,28},{16,0},{20,4},{24,8},{28,12},{1,17},{... | collective-permute-start | bytes 98312 | tf_op jit(solution)/shard_map/ppermute | solution.py:18
  29.5 5.8 %collective-permute-start.14 = (f32[64,128]{1,0:T(8,128)S(1)}, f32[64,128]{1,0:T(8,128)S(1)}, u32[]{:S(2)}, u32[]{:S(2)}) collective-permute-start(f32[64,128]{1,0:T(8,128)S(1)} %get-tuple-element.31), channel_id=1, source_target_pairs={{0,24},{4,28},{8,16},{12,20},{16,8},{20,12},{24,0},{28,4},{1,25},{... | collective-permute-start | bytes 98312 | tf_op jit(solution)/shard_map/ppermute | solution.py:18

commit v15 on v14

--- a/solution.py
+++ b/solution.py
@@ -10,7 +10,7 @@
 LANES = 128
 WHOLE = pl.BlockSpec(memory_space=pltpu.VMEM)
 ROOM = pltpu.CompilerParams(vmem_limit_bytes=16 * 1024 * 1024)
-HEAVY = 10**11
+HEAVY = 10**9
 LIGHT = pl.CostEstimate(flops=1000, bytes_accessed=1000, transcendentals=0)
 
 
@@ -68,12 +68,17 @@
 
 def joined_kernel(bit, first, second, out):
     here = jnp.where((lax.axis_index("row") & bit) == 0, 0, 1)
-    out[:, here] = first[...]
+    if first.ndim == 2:
+        span = out.shape[3]
+        spot = pl.ds(pl.multiple_of(lax.axis_index("col") * span, LANES), span)
+        out[0, here] = first[:, spot]
+    else:
+        out[:, here] = first[...]
     out[:, 1 - here] = second[...]
 
 
 def joined(first, second, bit):
-    count, rows, span = first.shape
+    count, rows, span = second.shape
     both = pl.pallas_call(
         functools.partial(joined_kernel, bit),
         out_shape=jax.ShapeDtypeStruct((count, 2, rows, span), jnp.float32),
@@ -179,17 +184,17 @@
 
 
 def collect_kernel(*refs):
-    keep, send = refs[-2:]
+    arrived, (_, keep, send) = refs[:-3], refs[-3:]
     share = keep.shape[0]
     span = refs[0].shape[1]
     here = (lax.axis_index("row") & 1) * share
-    for flip, piece in enumerate(refs[:-2]):
+    for flip, piece in enumerate(arrived):
         spot = pl.ds(pl.multiple_of((lax.axis_index("col") ^ flip) * span, LANES), span)
         keep[:, spot] = piece[pl.ds(pl.multiple_of(here, 8), share), :]
         send[:, spot] = piece[pl.ds(pl.multiple_of(share - here, 8), share), :]
 
 
-def collect(arrived):
+def collect(arrived, along):
     flips = len(arrived)
     share, span = arrived[0].shape[0] // 2, arrived[0].shape[1]
     if span % LANES:
@@ -202,11 +207,11 @@
     return pl.pallas_call(
         collect_kernel,
         out_shape=(part, part),
-        in_specs=[WHOLE] * flips,
+        in_specs=[WHOLE] * flips + [pl.BlockSpec(memory_space=pl.ANY)],
         out_specs=(WHOLE, WHOLE),
         cost_estimate=LIGHT,
         compiler_params=ROOM,
-    )(*arrived)
+    )(*arrived, along)
 
 
 def pair_rows(masked):
@@ -222,11 +227,12 @@
     return held + [flipped(piece, "col", 1) for piece in held]
 
 
-def along_line(mine):
+def along_line(mine, own):
     strips = mine[None]
     bit = lax.axis_size("row") // 2
     while bit > 1:
-        strips = joined(strips, flipped(strips, "row", bit), bit)
+        whole = strips.shape[0] == 1 and mine.shape[1] % LANES == 0
+        strips = joined(own if whole else strips, flipped(strips, "row", bit), bit)
         bit //= 2
     return strips
 
@@ -243,7 +249,7 @@
     own = factor.reshape(rows, width)
     blocks = inverse_set.reshape(rows * block_cols, order)
     masked, mine = prepare(presence.reshape(-1), blocks, own, span)
-    columns = along_line(mine).reshape(-1, block_rows, order, span).transpose(1, 0, 2, 3)
+    columns = along_line(mine, own).reshape(-1, block_rows, order, span).transpose(1, 0, 2, 3)
     columns = columns.reshape(-1, order, span)
     pieces = pair_rows(masked)
     stay, go = halves(own, pieces[0], width // groups_row)
@@ -252,11 +258,10 @@
     both, outward = partials(pieces, columns, near, groups_col)
     got = flipped(both, "row", 1)
     arrived = [outward[0]] + [flipped(outward[f], "col", f) for f in range(1, groups_col)]
-    keep, send = collect(arrived)
-    off_diag = keep + flipped(send, "row", 1)
-
     flips = tuple(range(0, groups_row, 2))
     along = finish(both, got, stay, near, dinv, flips)
+    keep, send = collect(arrived, along[0])
+    off_diag = keep + flipped(send, "row", 1)
     diag_block = along[0]
     for flip, piece in zip(flips[1:], along[1:]):
         diag_block = diag_block + flipped(piece, "row", flip)

time: 36.2 us -> 35.4 us (0.978)
  local copies, waits for them, and re-layouts: 1.23 us -> 0.01 us
  waiting for transfers between devices: 8.86 us -> 9.97 us
  starting transfers between devices: 21.2 us -> 20.7 us
    unnamed x6 -> x4, local copies, waits for them, and re-layouts: 1.23 us -> 0.01 us
    ppermute x14, waiting for transfers between devices: 8.86 us -> 9.97 us  [flipped(): lax.ppermute(value, axis, [(i, i ^ flip) for i in range(lax.axis_size(axi...]
    ppermute x14, starting transfers between devices: 19.6 us -> 19.1 us  [flipped(): lax.ppermute(value, axis, [(i, i ^ flip) for i in range(lax.axis_size(axi...]
  transfers between devices with their start and end apart: 15 -> 15, of which waited for: 7 -> 6; matrix products, arithmetic and copies ran while one was open for 2% -> 2% of each run, Pallas kernels for 1% -> 1%
where the time goes in v15:
time: 35.4 us; the launch traced here: 35.3 us
  starting transfers between devices  20.7 us (58%)
  waiting for transfers between devices  9.97 us (28%)
  Pallas kernels  2.65 us (7%)
  other arithmetic  1.26 us (4%)
  between operations  0.7 us (2%)
    ppermute x14, starting transfers between devices, flipped(): lax.ppermute(value, axis, [(i, i ^ flip) for i in range(lax.axis_size(axi...  19.1 us
    ppermute x14, waiting for transfers between devices, flipped(): lax.ppermute(value, axis, [(i, i ^ flip) for i in range(lax.axis_size(axi...  9.97 us
    pallas_call x1, Pallas kernels, prepare(): pl.pallas_call(prepare_kernel, out_shape=(jax.ShapeDtypeStruct((block_col...  1.75 us
    ppermute x1, starting transfers between devices, pair_rows(): held = lax.ppermute(masked, ('row', 'col'), cross)  1.55 us
  transfers between devices with their start and end apart: 15, of which 6 were waited for; matrix products, arithmetic and copies ran while one was open for 2% of the time, Pallas kernels for 1%

profile of v15, /device:TPU:0, one launch (start us, length us, event | category | flops | bytes accessed | tf_op | source)
XLA Modules:
  0.0 35.3 jit_solution(13913439367359402579)
XLA Ops:
  0.6 1.8 %shard_map.59 = (f32[2,128,128]{2,1,0:T(8,128)}, f32[128,128]{1,0:T(8,128)}) custom-call(s32[2]{0:T(128)} %bitcast.15, f32[256,128]{1,0:T(8,128)} %bitcast.14, f32[128,512]{1,0:T(8,128)} %bitcast.8), custom_call_target="tpu_custom_call" | custom-call | flops 1000 | bytes 1000 | tf_op jit(solution)/shard_map/pallas_call | solution.py:57
  2.4 1.6 %collective-permute-start = (f32[2,128,128]{2,1,0:T(8,128)}, f32[2,128,128]{2,1,0:T(8,128)S(1)}, u32[]{:S(2)}, u32[]{:S(2)}) collective-permute-start(f32[2,128,128]{2,1,0:T(8,128)} %get-tuple-element.17), channel_id=1, source_target_pairs={{0,0},{1,4},{2,2},{3,6},{4,1},{5,5},{6,3},{7,7},{8,8},{9,12},{10,1... | collective-permute-start | bytes 393224 | tf_op jit(solution)/shard_map/ppermute | solution.py:225
  3.9 4.0 %collective-permute-start.4 = (f32[1,128,128]{2,1,0:T(8,128)}, f32[1,128,128]{2,1,0:T(8,128)S(1)}, u32[]{:S(2)}, u32[]{:S(2)}) collective-permute-start(f32[1,128,128]{2,1,0:T(8,128)} %bitcast.16), channel_id=1, source_target_pairs={{0,16},{4,20},{8,24},{12,28},{16,0},{20,4},{24,8},{28,12},{1,17},{... | collective-permute-start | bytes 196616 | tf_op jit(solution)/shard_map/ppermute | solution.py:18
  8.0 1.5 %collective-permute-start.1 = (f32[2,128,128]{2,1,0:T(8,128)S(1)}, f32[2,128,128]{2,1,0:T(8,128)S(1)}, u32[]{:S(2)}, u32[]{:S(2)}) collective-permute-start(f32[2,128,128]{2,1,0:T(8,128)S(1)} %collective-permute-done.held.refs_0_), channel_id=1, source_target_pairs={{0,2},{1,3},{2,0},{3,1},{4,6},{5,7},{6,4},{7,5},{8,10},{9,11},{10,... | collective-permute-start | bytes 393224 | tf_op jit(solution)/shard_map/ppermute | solution.py:18
  9.5 0.9 %collective-permute-done.4.second = f32[1,128,128]{2,1,0:T(8,128)S(1)} collective-permute-done((f32[1,128,128]{2,1,0:T(8,128)}, f32[1,128,128]{2,1,0:T(8,128)S(1)}, u32[]{:S(2)}, u32[]{:S(2)}) %collective-permute-start.4) | collective-permute-done | bytes 65568 | tf_op jit(solution)/shard_map/ppermute | solution.py:18
  10.5 2.8 %collective-permute-start.5 = (f32[2,128,128]{2,1,0:T(8,128)S(1)}, f32[2,128,128]{2,1,0:T(8,128)S(1)}, u32[]{:S(2)}, u32[]{:S(2)}) collective-permute-start(f32[2,128,128]{2,1,0:T(8,128)S(1)} %bitcast.12), channel_id=1, source_target_pairs={{0,8},{4,12},{8,0},{12,4},{16,24},{20,28},{24,16},{28,20},{1,9},{5... | collective-permute-start | bytes 393224 | tf_op jit(solution)/shard_map/ppermute | solution.py:18
  13.4 1.8 %collective-permute-start.6 = (f32[128,256]{1,0:T(8,128)S(1)}, f32[128,256]{1,0:T(8,128)S(1)}, u32[]{:S(2)}, u32[]{:S(2)}) collective-permute-start(f32[128,256]{1,0:T(8,128)S(1)} %get-tuple-element.19), channel_id=1, source_target_pairs={{0,4},{4,0},{8,12},{12,8},{16,20},{20,16},{24,28},{28,24},{1,5},{5... | collective-permute-start | bytes 393224 | tf_op jit(solution)/shard_map/ppermute | solution.py:18
  15.2 0.5 %collective-permute-start.3 = (f32[2,128,128]{2,1,0:T(8,128)S(1)}, f32[2,128,128]{2,1,0:T(8,128)S(1)}, u32[]{:S(2)}, u32[]{:S(2)}) collective-permute-start(f32[2,128,128]{2,1,0:T(8,128)S(1)} %collective-permute-done.1.refs_1_), channel_id=1, source_target_pairs={{0,1},{1,0},{2,3},{3,2},{4,5},{5,4},{6,7},{7,6},{8,9},{9,8},{10,11... | collective-permute-start | bytes 393224 | tf_op jit(solution)/shard_map/ppermute | solution.py:18
  15.7 1.0 %collective-permute-done.5.second = f32[2,128,128]{2,1,0:T(8,128)S(1)} collective-permute-done((f32[2,128,128]{2,1,0:T(8,128)S(1)}, f32[2,128,128]{2,1,0:T(8,128)S(1)}, u32[]{:S(2)}, u32[]{:S(2)}) %collective-permute-start.5) | collective-permute-done | bytes 131104 | tf_op jit(solution)/shard_map/ppermute | solution.py:18
  16.8 2.4 %collective-permute-done.6.refs_5_.near = f32[128,256]{1,0:T(8,128)S(1)} collective-permute-done((f32[128,256]{1,0:T(8,128)S(1)}, f32[128,256]{1,0:T(8,128)S(1)}, u32[]{:S(2)}, u32[]{:S(2)}) %collective-permute-start.6) | collective-permute-done | bytes 131104 | tf_op jit(solution)/shard_map/ppermute | solution.py:18
  19.2 0.4 %shard_map.63 = (f32[256,128]{1,0:T(8,128)S(1)}, f32[64,128]{1,0:T(8,128)S(1)}, f32[64,128]{1,0:T(8,128)S(1)}, f32[64,128]{1,0:T(8,128)S(1)}, f32[64,128]{1,0:T(8,128)S(1)}) custom-call(f32[2,128,128]{2,1,0:T(8,128)S(1)} %collective-permute-done.held.refs_0_, f32[2,128,128]{2,1,0:T(8,128)S(1)} %collective-permute-done.1.refs_1_, ...), custom_call_target="tpu_custom_call" | custom-call | flops 1000 | bytes 1000 | tf_op jit(solution)/shard_map/pallas_call | solution.py:118
  19.6 1.1 %collective-permute-start.10 = (f32[256,128]{1,0:T(8,128)S(1)}, f32[256,128]{1,0:T(8,128)S(1)}, u32[]{:S(2)}, u32[]{:S(2)}) collective-permute-start(f32[256,128]{1,0:T(8,128)S(1)} %get-tuple-element.24.both), channel_id=1, source_target_pairs={{0,4},{4,0},{8,12},{12,8},{16,20},{20,16},{24,28},{28,24},{1,5},{5... | collective-permute-start | bytes 393224 | tf_op jit(solution)/shard_map/ppermute | solution.py:18
  20.7 0.9 %collective-permute-start.8 = (f32[64,128]{1,0:T(8,128)S(1)}, f32[64,128]{1,0:T(8,128)S(1)}, u32[]{:S(2)}, u32[]{:S(2)}) collective-permute-start(f32[64,128]{1,0:T(8,128)S(1)} %get-tuple-element.22), channel_id=1, source_target_pairs={{0,2},{1,3},{2,0},{3,1},{4,6},{5,7},{6,4},{7,5},{8,10},{9,11},{10,... | collective-permute-start | bytes 98312 | tf_op jit(solution)/shard_map/ppermute | solution.py:18
  21.5 1.0 %collective-permute-start.9 = (f32[64,128]{1,0:T(8,128)S(1)}, f32[64,128]{1,0:T(8,128)S(1)}, u32[]{:S(2)}, u32[]{:S(2)}) collective-permute-start(f32[64,128]{1,0:T(8,128)S(1)} %get-tuple-element.23), channel_id=1, source_target_pairs={{0,3},{1,2},{2,1},{3,0},{4,7},{5,6},{6,5},{7,4},{8,11},{9,10},{10,... | collective-permute-start | bytes 98312 | tf_op jit(solution)/shard_map/ppermute | solution.py:18
  22.5 2.1 %collective-permute-done.10.got = f32[256,128]{1,0:T(8,128)S(1)} collective-permute-done((f32[256,128]{1,0:T(8,128)S(1)}, f32[256,128]{1,0:T(8,128)S(1)}, u32[]{:S(2)}, u32[]{:S(2)}) %collective-permute-start.10) | collective-permute-done | bytes 131104 | tf_op jit(solution)/shard_map/ppermute | solution.py:18
  24.6 0.3 shard_map.64
  24.9 1.2 %collective-permute-start.12 = (f32[64,128]{1,0:T(8,128)S(1)}, f32[64,128]{1,0:T(8,128)S(1)}, u32[]{:S(2)}, u32[]{:S(2)}) collective-permute-start(f32[64,128]{1,0:T(8,128)S(1)} %get-tuple-element.29), channel_id=1, source_target_pairs={{0,8},{4,12},{8,0},{12,4},{16,24},{20,28},{24,16},{28,20},{1,9},{5... | collective-permute-start | bytes 98312 | tf_op jit(solution)/shard_map/ppermute | solution.py:18
  26.1 2.2 %collective-permute-start.13 = (f32[64,128]{1,0:T(8,128)S(1)}, f32[64,128]{1,0:T(8,128)S(1)}, u32[]{:S(2)}, u32[]{:S(2)}) collective-permute-start(f32[64,128]{1,0:T(8,128)S(1)} %get-tuple-element.30), channel_id=1, source_target_pairs={{0,16},{4,20},{8,24},{12,28},{16,0},{20,4},{24,8},{28,12},{1,17},{... | collective-permute-start | bytes 98312 | tf_op jit(solution)/shard_map/ppermute | solution.py:18
  28.3 1.2 %collective-permute-start.14 = (f32[64,128]{1,0:T(8,128)S(1)}, f32[64,128]{1,0:T(8,128)S(1)}, u32[]{:S(2)}, u32[]{:S(2)}) collective-permute-start(f32[64,128]{1,0:T(8,128)S(1)} %get-tuple-element.31), channel_id=1, source_target_pairs={{0,24},{4,28},{8,16},{12,20},{16,8},{20,12},{24,0},{28,4},{1,25},{... | collective-permute-start | bytes 98312 | tf_op jit(solution)/shard_map/ppermute | solution.py:18
  29.5 1.0 %collective-permute-start.11 = (f32[32,512]{1,0:T(8,128)S(1)}, f32[32,512]{1,0:T(8,128)S(1)}, u32[]{:S(2)}, u32[]{:S(2)}) collective-permute-start(f32[32,512]{1,0:T(8,128)S(1)} %get-tuple-element.28), channel_id=1, source_target_pairs={{0,4},{4,0},{8,12},{12,8},{16,20},{20,16},{24,28},{28,24},{1,5},{5... | collective-permute-start | bytes 196616 | tf_op jit(solution)/shard_map/ppermute | solution.py:18
  30.5 0.5 %collective-permute-done.13 = f32[64,128]{1,0:T(8,128)S(1)} collective-permute-done((f32[64,128]{1,0:T(8,128)S(1)}, f32[64,128]{1,0:T(8,128)S(1)}, u32[]{:S(2)}, u32[]{:S(2)}) %collective-permute-start.13) | collective-permute-done | bytes 32800 | tf_op jit(solution)/shard_map/ppermute | solution.py:18
  31.0 3.0 %collective-permute-done.14 = f32[64,128]{1,0:T(8,128)S(1)} collective-permute-done((f32[64,128]{1,0:T(8,128)S(1)}, f32[64,128]{1,0:T(8,128)S(1)}, u32[]{:S(2)}, u32[]{:S(2)}) %collective-permute-start.14) | collective-permute-done | bytes 32800 | tf_op jit(solution)/shard_map/ppermute | solution.py:18
  34.0 0.6 %add_add_fusion = f32[64,128]{1,0:T(8,128)} fusion(f32[64,128]{1,0:T(8,128)S(1)} %collective-permute-done.14, f32[64,128]{1,0:T(8,128)S(1)} %collective-permute-done.13, f32[64,128]{1,0:T(8,128)S(1)} %get-tuple-element.26.refs_4_, f32[64,128]{1,0:T(8,128)S(1)} %collective-permute-done.12), kind=kLoop, calls=%fused_computation.1 | loop fusion | flops 24576 | bytes 163840 | tf_op jit(solution)/shard_map/add | solution.py:267
  34.6 0.6 %add_bitcast_fusion = f32[1,1,32,512]{3,2,1,0:T(8,128)} fusion(f32[32,512]{1,0:T(8,128)S(1)} %get-tuple-element.27, f32[32,512]{1,0:T(8,128)S(1)} %collective-permute-done.11), kind=kLoop, calls=%fused_computation | loop fusion | flops 16384 | bytes 196608 | tf_op jit(solution)/shard_map/reshape | solution.py:268
  (19 shorter events, 0.2 us)
Async XLA Ops:
  0.6 9.8 %copy-start = (f32[1,1,128,512]{3,2,1,0:T(8,128)S(1)}, f32[1,1,128,512]{3,2,1,0:T(8,128)}, u32[]{:S(2)}) copy-start(f32[1,1,128,512]{3,2,1,0:T(8,128)} %param.6) | copy-start | bytes 786436
  2.4 5.6 %collective-permute-start = (f32[2,128,128]{2,1,0:T(8,128)}, f32[2,128,128]{2,1,0:T(8,128)S(1)}, u32[]{:S(2)}, u32[]{:S(2)}) collective-permute-start(f32[2,128,128]{2,1,0:T(8,128)} %get-tuple-element.17), channel_id=1, source_target_pairs={{0,0},{1,4},{2,2},{3,6},{4,1},{5,5},{6,3},{7,7},{8,8},{9,12},{10,1... | collective-permute-start | bytes 393224 | tf_op jit(solution)/shard_map/ppermute | solution.py:225
  3.9 6.5 %collective-permute-start.4 = (f32[1,128,128]{2,1,0:T(8,128)}, f32[1,128,128]{2,1,0:T(8,128)S(1)}, u32[]{:S(2)}, u32[]{:S(2)}) collective-permute-start(f32[1,128,128]{2,1,0:T(8,128)} %bitcast.16), channel_id=1, source_target_pairs={{0,16},{4,20},{8,24},{12,28},{16,0},{20,4},{24,8},{28,12},{1,17},{... | collective-permute-start | bytes 196616 | tf_op jit(solution)/shard_map/ppermute | solution.py:18
  8.0 7.2 %collective-permute-start.1 = (f32[2,128,128]{2,1,0:T(8,128)S(1)}, f32[2,128,128]{2,1,0:T(8,128)S(1)}, u32[]{:S(2)}, u32[]{:S(2)}) collective-permute-start(f32[2,128,128]{2,1,0:T(8,128)S(1)} %collective-permute-done.held.refs_0_), channel_id=1, source_target_pairs={{0,2},{1,3},{2,0},{3,1},{4,6},{5,7},{6,4},{7,5},{8,10},{9,11},{10,... | collective-permute-start | bytes 393224 | tf_op jit(solution)/shard_map/ppermute | solution.py:18
  10.5 6.3 %collective-permute-start.5 = (f32[2,128,128]{2,1,0:T(8,128)S(1)}, f32[2,128,128]{2,1,0:T(8,128)S(1)}, u32[]{:S(2)}, u32[]{:S(2)}) collective-permute-start(f32[2,128,128]{2,1,0:T(8,128)S(1)} %bitcast.12), channel_id=1, source_target_pairs={{0,8},{4,12},{8,0},{12,4},{16,24},{20,28},{24,16},{28,20},{1,9},{5... | collective-permute-start | bytes 393224 | tf_op jit(solution)/shard_map/ppermute | solution.py:18
  13.4 5.8 %collective-permute-start.6 = (f32[128,256]{1,0:T(8,128)S(1)}, f32[128,256]{1,0:T(8,128)S(1)}, u32[]{:S(2)}, u32[]{:S(2)}) collective-permute-start(f32[128,256]{1,0:T(8,128)S(1)} %get-tuple-element.19), channel_id=1, source_target_pairs={{0,4},{4,0},{8,12},{12,8},{16,20},{20,16},{24,28},{28,24},{1,5},{5... | collective-permute-start | bytes 393224 | tf_op jit(solution)/shard_map/ppermute | solution.py:18
  15.2 1.6 %collective-permute-start.2 = (f32[2,128,128]{2,1,0:T(8,128)S(1)}, f32[2,128,128]{2,1,0:T(8,128)S(1)}, u32[]{:S(2)}, u32[]{:S(2)}) collective-permute-start(f32[2,128,128]{2,1,0:T(8,128)S(1)} %collective-permute-done.held.refs_0_), channel_id=1, source_target_pairs={{0,1},{1,0},{2,3},{3,2},{4,5},{5,4},{6,7},{7,6},{8,9},{9,8},{10,11... | collective-permute-start | bytes 393224 | tf_op jit(solution)/shard_map/ppermute | solution.py:18
  15.2 4.0 %collective-permute-start.3 = (f32[2,128,128]{2,1,0:T(8,128)S(1)}, f32[2,128,128]{2,1,0:T(8,128)S(1)}, u32[]{:S(2)}, u32[]{:S(2)}) collective-permute-start(f32[2,128,128]{2,1,0:T(8,128)S(1)} %collective-permute-done.1.refs_1_), channel_id=1, source_target_pairs={{0,1},{1,0},{2,3},{3,2},{4,5},{5,4},{6,7},{7,6},{8,9},{9,8},{10,11... | collective-permute-start | bytes 393224 | tf_op jit(solution)/shard_map/ppermute | solution.py:18
  19.2 5.4 %copy-start.1 = (f32[64,128]{1,0:T(8,128)S(1)}, f32[64,128]{1,0:T(8,128)}, u32[]{:S(2)}) copy-start(f32[64,128]{1,0:T(8,128)} %dinv.1) | copy-start | bytes 98308
  19.6 5.0 %collective-permute-start.10 = (f32[256,128]{1,0:T(8,128)S(1)}, f32[256,128]{1,0:T(8,128)S(1)}, u32[]{:S(2)}, u32[]{:S(2)}) collective-permute-start(f32[256,128]{1,0:T(8,128)S(1)} %get-tuple-element.24.both), channel_id=1, source_target_pairs={{0,4},{4,0},{8,12},{12,8},{16,20},{20,16},{24,28},{28,24},{1,5},{5... | collective-permute-start | bytes 393224 | tf_op jit(solution)/shard_map/ppermute | solution.py:18
  20.6 7.6 %collective-permute-start.7 = (f32[64,128]{1,0:T(8,128)S(1)}, f32[64,128]{1,0:T(8,128)S(1)}, u32[]{:S(2)}, u32[]{:S(2)}) collective-permute-start(f32[64,128]{1,0:T(8,128)S(1)} %get-tuple-element.21), channel_id=1, source_target_pairs={{0,1},{1,0},{2,3},{3,2},{4,5},{5,4},{6,7},{7,6},{8,9},{9,8},{10,11... | collective-permute-start | bytes 98312 | tf_op jit(solution)/shard_map/ppermute | solution.py:18
  20.7 8.8 %collective-permute-start.8 = (f32[64,128]{1,0:T(8,128)S(1)}, f32[64,128]{1,0:T(8,128)S(1)}, u32[]{:S(2)}, u32[]{:S(2)}) collective-permute-start(f32[64,128]{1,0:T(8,128)S(1)} %get-tuple-element.22), channel_id=1, source_target_pairs={{0,2},{1,3},{2,0},{3,1},{4,6},{5,7},{6,4},{7,5},{8,10},{9,11},{10,... | collective-permute-start | bytes 98312 | tf_op jit(solution)/shard_map/ppermute | solution.py:18
  21.5 8.0 %collective-permute-start.9 = (f32[64,128]{1,0:T(8,128)S(1)}, f32[64,128]{1,0:T(8,128)S(1)}, u32[]{:S(2)}, u32[]{:S(2)}) collective-permute-start(f32[64,128]{1,0:T(8,128)S(1)} %get-tuple-element.23), channel_id=1, source_target_pairs={{0,3},{1,2},{2,1},{3,0},{4,7},{5,6},{6,5},{7,4},{8,11},{9,10},{10,... | collective-permute-start | bytes 98312 | tf_op jit(solution)/shard_map/ppermute | solution.py:18
  24.9 5.6 %collective-permute-start.12 = (f32[64,128]{1,0:T(8,128)S(1)}, f32[64,128]{1,0:T(8,128)S(1)}, u32[]{:S(2)}, u32[]{:S(2)}) collective-permute-start(f32[64,128]{1,0:T(8,128)S(1)} %get-tuple-element.29), channel_id=1, source_target_pairs={{0,8},{4,12},{8,0},{12,4},{16,24},{20,28},{24,16},{28,20},{1,9},{5... | collective-permute-start | bytes 98312 | tf_op jit(solution)/shard_map/ppermute | solution.py:18
  26.1 4.9 %collective-permute-start.13 = (f32[64,128]{1,0:T(8,128)S(1)}, f32[64,128]{1,0:T(8,128)S(1)}, u32[]{:S(2)}, u32[]{:S(2)}) collective-permute-start(f32[64,128]{1,0:T(8,128)S(1)} %get-tuple-element.30), channel_id=1, source_target_pairs={{0,16},{4,20},{8,24},{12,28},{16,0},{20,4},{24,8},{28,12},{1,17},{... | collective-permute-start | bytes 98312 | tf_op jit(solution)/shard_map/ppermute | solution.py:18
  28.3 5.7 %collective-permute-start.14 = (f32[64,128]{1,0:T(8,128)S(1)}, f32[64,128]{1,0:T(8,128)S(1)}, u32[]{:S(2)}, u32[]{:S(2)}) collective-permute-start(f32[64,128]{1,0:T(8,128)S(1)} %get-tuple-element.31), channel_id=1, source_target_pairs={{0,24},{4,28},{8,16},{12,20},{16,8},{20,12},{24,0},{28,4},{1,25},{... | collective-permute-start | bytes 98312 | tf_op jit(solution)/shard_map/ppermute | solution.py:18
  29.5 5.1 %collective-permute-start.11 = (f32[32,512]{1,0:T(8,128)S(1)}, f32[32,512]{1,0:T(8,128)S(1)}, u32[]{:S(2)}, u32[]{:S(2)}) collective-permute-start(f32[32,512]{1,0:T(8,128)S(1)} %get-tuple-element.28), channel_id=1, source_target_pairs={{0,4},{4,0},{8,12},{12,8},{16,20},{20,16},{24,28},{28,24},{1,5},{5... | collective-permute-start | bytes 196616 | tf_op jit(solution)/shard_map/ppermute | solution.py:18

commit v16 on v15

--- a/solution.py
+++ b/solution.py
@@ -66,7 +66,7 @@
     )(presence, blocks, own)
 
 
-def joined_kernel(bit, first, second, out):
+def joined_kernel(bit, first, second, near, out):
     here = jnp.where((lax.axis_index("row") & bit) == 0, 0, 1)
     if first.ndim == 2:
         span = out.shape[3]
@@ -77,22 +77,22 @@
     out[:, 1 - here] = second[...]
 
 
-def joined(first, second, bit):
+def joined(first, second, bit, near):
     count, rows, span = second.shape
     both = pl.pallas_call(
         functools.partial(joined_kernel, bit),
         out_shape=jax.ShapeDtypeStruct((count, 2, rows, span), jnp.float32),
-        in_specs=[WHOLE, WHOLE],
+        in_specs=[WHOLE, WHOLE, pl.BlockSpec(memory_space=pl.ANY)],
         out_specs=WHOLE,
         cost_estimate=pl.CostEstimate(flops=HEAVY, bytes_accessed=1000, transcendentals=0),
         compiler_params=ROOM,
-    )(first, second)
+    )(first, second, near)
     return both.reshape(2 * count, rows, span)
 
 
 def partials_kernel(count, *refs):
     pieces = refs[: 2 * count]
-    columns, _, both, *outward = refs[2 * count :]
+    columns, both, *outward = refs[2 * count :]
     block_cols, rows, order = pieces[0].shape
     col_index = lax.axis_index("col")
     left, right = [], []
@@ -112,21 +112,21 @@
             piece[pl.ds(a * share, share), :] = -picked
 
 
-def partials(pieces, columns, near, receivers):
+def partials(pieces, columns, receivers):
     rows, span = 2 * pieces[0].shape[1], columns.shape[2]
     outward = (jax.ShapeDtypeStruct((rows // receivers, span), jnp.float32),) * receivers
     both, *outward = pl.pallas_call(
         functools.partial(partials_kernel, len(pieces) // 2),
         out_shape=(jax.ShapeDtypeStruct((rows, span), jnp.float32),) + outward,
-        in_specs=[WHOLE] * (len(pieces) + 1) + [pl.BlockSpec(memory_space=pl.ANY)],
+        in_specs=[WHOLE] * (len(pieces) + 1),
         out_specs=(WHOLE,) * (1 + receivers),
         cost_estimate=LIGHT,
         compiler_params=ROOM,
-    )(*pieces, columns, near)
+    )(*pieces, columns)
     return both, outward
 
 
-def halves_kernel(tall, own, held, stay, go):
+def halves_kernel(tall, own, stay, go):
     even, odd = [
         jnp.concatenate([own[:, i : i + tall] for i in range(first, own.shape[1], 2 * tall)], axis=1)
         for first in (0, tall)
@@ -136,17 +136,17 @@
     go[...] = jnp.where(upper, even, odd)
 
 
-def halves(own, held, tall):
+def halves(own, tall):
     rows, width = own.shape
     part = jax.ShapeDtypeStruct((rows, width // 2), jnp.float32)
     return pl.pallas_call(
         functools.partial(halves_kernel, tall),
         out_shape=(part, part),
-        in_specs=[WHOLE, pl.BlockSpec(memory_space=pl.ANY)],
+        in_specs=[WHOLE],
         out_specs=(WHOLE, WHOLE),
         cost_estimate=LIGHT,
         compiler_params=ROOM,
-    )(own, held)
+    )(own)
 
 
 def finish_kernel(flips, both, got, stay, near, dinv, *refs):
@@ -227,12 +227,13 @@
     return held + [flipped(piece, "col", 1) for piece in held]
 
 
-def along_line(mine, own):
+def along_line(mine, own, near):
     strips = mine[None]
     bit = lax.axis_size("row") // 2
     while bit > 1:
         whole = strips.shape[0] == 1 and mine.shape[1] % LANES == 0
-        strips = joined(own if whole else strips, flipped(strips, "row", bit), bit)
+        first = own if whole else strips
+        strips = joined(first, flipped(strips, "row", bit), bit, near if bit == 2 else mine)
         bit //= 2
     return strips
 
@@ -249,16 +250,16 @@
     own = factor.reshape(rows, width)
     blocks = inverse_set.reshape(rows * block_cols, order)
     masked, mine = prepare(presence.reshape(-1), blocks, own, span)
-    columns = along_line(mine, own).reshape(-1, block_rows, order, span).transpose(1, 0, 2, 3)
+    stay, go = halves(own, width // groups_row)
+    near = flipped(go, "row", 1)
+    columns = along_line(mine, own, near).reshape(-1, block_rows, order, span).transpose(1, 0, 2, 3)
     columns = columns.reshape(-1, order, span)
     pieces = pair_rows(masked)
-    stay, go = halves(own, pieces[0], width // groups_row)
-    near = flipped(go, "row", 1)
-
-    both, outward = partials(pieces, columns, near, groups_col)
+
+    both, outward = partials(pieces, columns, groups_col)
     got = flipped(both, "row", 1)
     arrived = [outward[0]] + [flipped(outward[f], "col", f) for f in range(1, groups_col)]
-    flips = tuple(range(0, groups_row, 2))
+    flips = (0,) + tuple(range(groups_row - 2, 0, -2))
     along = finish(both, got, stay, near, dinv, flips)
     keep, send = collect(arrived, along[0])
     off_diag = keep + flipped(send, "row", 1)

time: 35.4 us -> 33.8 us (0.955)
  starting transfers between devices: 20.7 us -> 18.6 us
  waiting for transfers between devices: 9.97 us -> 10.4 us
    ppermute x14, starting transfers between devices: 19.1 us -> 17.1 us  [flipped(): lax.ppermute(value, axis, [(i, i ^ flip) for i in range(lax.axis_size(axi...]
    ppermute x14, waiting for transfers between devices: 9.97 us -> 10.4 us  [flipped(): lax.ppermute(value, axis, [(i, i ^ flip) for i in range(lax.axis_size(axi...]
  transfers between devices with their start and end apart: 15 -> 15, of which waited for: 6 -> 5; matrix products, arithmetic and copies ran while one was open for 2% -> 2% of each run, Pallas kernels for 1% -> 2%
where the time goes in v16:
time: 33.8 us; the launch traced here: 33.7 us
  starting transfers between devices  18.6 us (55%)
  waiting for transfers between devices  10.4 us (31%)
  Pallas kernels  2.66 us (8%)
  other arithmetic  1.26 us (4%)
  between operations  0.72 us (2%)
    ppermute x14, starting transfers between devices, flipped(): lax.ppermute(value, axis, [(i, i ^ flip) for i in range(lax.axis_size(axi...  17.1 us
    ppermute x14, waiting for transfers between devices, flipped(): lax.ppermute(value, axis, [(i, i ^ flip) for i in range(lax.axis_size(axi...  10.4 us
    pallas_call x1, Pallas kernels, prepare(): pl.pallas_call(prepare_kernel, out_shape=(jax.ShapeDtypeStruct((block_col...  1.75 us
    ppermute x1, starting transfers between devices, pair_rows(): held = lax.ppermute(masked, ('row', 'col'), cross)  1.55 us
  transfers between devices with their start and end apart: 15, of which 5 were waited for; matrix products, arithmetic and copies ran while one was open for 2% of the time, Pallas kernels for 2%

profile of v16, /device:TPU:0, one launch (start us, length us, event | category | flops | bytes accessed | tf_op | source)
XLA Modules:
  0.0 33.7 jit_solution(554171191357565339)
XLA Ops:
  0.6 1.8 %shard_map.59 = (f32[2,128,128]{2,1,0:T(8,128)}, f32[128,128]{1,0:T(8,128)}) custom-call(s32[2]{0:T(128)} %bitcast.16, f32[256,128]{1,0:T(8,128)} %bitcast.15, f32[128,512]{1,0:T(8,128)} %bitcast.8), custom_call_target="tpu_custom_call" | custom-call | flops 1000 | bytes 1000 | tf_op jit(solution)/shard_map/pallas_call | solution.py:57
  2.4 1.6 %collective-permute-start = (f32[2,128,128]{2,1,0:T(8,128)}, f32[2,128,128]{2,1,0:T(8,128)S(1)}, u32[]{:S(2)}, u32[]{:S(2)}) collective-permute-start(f32[2,128,128]{2,1,0:T(8,128)} %get-tuple-element.17), channel_id=1, source_target_pairs={{0,0},{1,4},{2,2},{3,6},{4,1},{5,5},{6,3},{7,7},{8,8},{9,12},{10,1... | collective-permute-start | bytes 393224 | tf_op jit(solution)/shard_map/ppermute | solution.py:225
  3.9 4.0 %collective-permute-start.4 = (f32[1,128,128]{2,1,0:T(8,128)}, f32[1,128,128]{2,1,0:T(8,128)S(1)}, u32[]{:S(2)}, u32[]{:S(2)}) collective-permute-start(f32[1,128,128]{2,1,0:T(8,128)} %bitcast.14), channel_id=1, source_target_pairs={{0,16},{4,20},{8,24},{12,28},{16,0},{20,4},{24,8},{28,12},{1,17},{... | collective-permute-start | bytes 196616 | tf_op jit(solution)/shard_map/ppermute | solution.py:18
  8.0 0.1 shard_map.61
  8.1 2.0 %collective-permute-start.6 = (f32[128,256]{1,0:T(8,128)S(1)}, f32[128,256]{1,0:T(8,128)S(1)}, u32[]{:S(2)}, u32[]{:S(2)}) collective-permute-start(f32[128,256]{1,0:T(8,128)S(1)} %get-tuple-element.19), channel_id=1, source_target_pairs={{0,4},{4,0},{8,12},{12,8},{16,20},{20,16},{24,28},{28,24},{1,5},{5... | collective-permute-start | bytes 393224 | tf_op jit(solution)/shard_map/ppermute | solution.py:18
  10.1 1.5 %collective-permute-start.1 = (f32[2,128,128]{2,1,0:T(8,128)S(1)}, f32[2,128,128]{2,1,0:T(8,128)S(1)}, u32[]{:S(2)}, u32[]{:S(2)}) collective-permute-start(f32[2,128,128]{2,1,0:T(8,128)S(1)} %collective-permute-done.refs_0_), channel_id=1, source_target_pairs={{0,2},{1,3},{2,0},{3,1},{4,6},{5,7},{6,4},{7,5},{8,10},{9,11},{10,... | collective-permute-start | bytes 393224 | tf_op jit(solution)/shard_map/ppermute | solution.py:18
  11.7 1.6 %collective-permute-start.5 = (f32[2,128,128]{2,1,0:T(8,128)S(1)}, f32[2,128,128]{2,1,0:T(8,128)S(1)}, u32[]{:S(2)}, u32[]{:S(2)}) collective-permute-start(f32[2,128,128]{2,1,0:T(8,128)S(1)} %bitcast.12), channel_id=1, source_target_pairs={{0,8},{4,12},{8,0},{12,4},{16,24},{20,28},{24,16},{28,20},{1,9},{5... | collective-permute-start | bytes 393224 | tf_op jit(solution)/shard_map/ppermute | solution.py:18
  13.3 0.2 collective-permute-start.2
  13.6 2.3 %collective-permute-done.1.refs_1_ = f32[2,128,128]{2,1,0:T(8,128)S(1)} collective-permute-done((f32[2,128,128]{2,1,0:T(8,128)S(1)}, f32[2,128,128]{2,1,0:T(8,128)S(1)}, u32[]{:S(2)}, u32[]{:S(2)}) %collective-permute-start.1) | collective-permute-done | bytes 131104 | tf_op jit(solution)/shard_map/ppermute | solution.py:18
  15.9 2.0 %collective-permute-done.5.second = f32[2,128,128]{2,1,0:T(8,128)S(1)} collective-permute-done((f32[2,128,128]{2,1,0:T(8,128)S(1)}, f32[2,128,128]{2,1,0:T(8,128)S(1)}, u32[]{:S(2)}, u32[]{:S(2)}) %collective-permute-start.5) | collective-permute-done | bytes 131104 | tf_op jit(solution)/shard_map/ppermute | solution.py:18
  17.9 0.4 %shard_map.63 = (f32[256,128]{1,0:T(8,128)S(1)}, f32[64,128]{1,0:T(8,128)S(1)}, f32[64,128]{1,0:T(8,128)S(1)}, f32[64,128]{1,0:T(8,128)S(1)}, f32[64,128]{1,0:T(8,128)S(1)}) custom-call(f32[2,128,128]{2,1,0:T(8,128)S(1)} %collective-permute-done.refs_0_, f32[2,128,128]{2,1,0:T(8,128)S(1)} %collective-permute-done.1.refs_1_, ...), custom_call_target="tpu_custom_call" | custom-call | flops 1000 | bytes 1000 | tf_op jit(solution)/shard_map/pallas_call | solution.py:118
  18.3 0.7 %collective-permute-start.10 = (f32[256,128]{1,0:T(8,128)S(1)}, f32[256,128]{1,0:T(8,128)S(1)}, u32[]{:S(2)}, u32[]{:S(2)}) collective-permute-start(f32[256,128]{1,0:T(8,128)S(1)} %get-tuple-element.24.both), channel_id=1, source_target_pairs={{0,4},{4,0},{8,12},{12,8},{16,20},{20,16},{24,28},{28,24},{1,5},{5... | collective-permute-start | bytes 393224 | tf_op jit(solution)/shard_map/ppermute | solution.py:18
  19.0 1.5 %collective-permute-start.8 = (f32[64,128]{1,0:T(8,128)S(1)}, f32[64,128]{1,0:T(8,128)S(1)}, u32[]{:S(2)}, u32[]{:S(2)}) collective-permute-start(f32[64,128]{1,0:T(8,128)S(1)} %get-tuple-element.22), channel_id=1, source_target_pairs={{0,2},{1,3},{2,0},{3,1},{4,6},{5,7},{6,4},{7,5},{8,10},{9,11},{10,... | collective-permute-start | bytes 98312 | tf_op jit(solution)/shard_map/ppermute | solution.py:18
  20.5 0.4 %collective-permute-start.9 = (f32[64,128]{1,0:T(8,128)S(1)}, f32[64,128]{1,0:T(8,128)S(1)}, u32[]{:S(2)}, u32[]{:S(2)}) collective-permute-start(f32[64,128]{1,0:T(8,128)S(1)} %get-tuple-element.23), channel_id=1, source_target_pairs={{0,3},{1,2},{2,1},{3,0},{4,7},{5,6},{6,5},{7,4},{8,11},{9,10},{10,... | collective-permute-start | bytes 98312 | tf_op jit(solution)/shard_map/ppermute | solution.py:18
  20.9 3.0 %collective-permute-done.10.got = f32[256,128]{1,0:T(8,128)S(1)} collective-permute-done((f32[256,128]{1,0:T(8,128)S(1)}, f32[256,128]{1,0:T(8,128)S(1)}, u32[]{:S(2)}, u32[]{:S(2)}) %collective-permute-start.10) | collective-permute-done | bytes 131104 | tf_op jit(solution)/shard_map/ppermute | solution.py:18
  23.9 0.3 shard_map.64
  24.2 3.3 %collective-permute-start.12 = (f32[64,128]{1,0:T(8,128)S(1)}, f32[64,128]{1,0:T(8,128)S(1)}, u32[]{:S(2)}, u32[]{:S(2)}) collective-permute-start(f32[64,128]{1,0:T(8,128)S(1)} %get-tuple-element.29), channel_id=1, source_target_pairs={{0,24},{4,28},{8,16},{12,20},{16,8},{20,12},{24,0},{28,4},{1,25},{... | collective-permute-start | bytes 98312 | tf_op jit(solution)/shard_map/ppermute | solution.py:18
  27.6 1.1 %collective-permute-start.14 = (f32[64,128]{1,0:T(8,128)S(1)}, f32[64,128]{1,0:T(8,128)S(1)}, u32[]{:S(2)}, u32[]{:S(2)}) collective-permute-start(f32[64,128]{1,0:T(8,128)S(1)} %get-tuple-element.31), channel_id=1, source_target_pairs={{0,8},{4,12},{8,0},{12,4},{16,24},{20,28},{24,16},{28,20},{1,9},{5... | collective-permute-start | bytes 98312 | tf_op jit(solution)/shard_map/ppermute | solution.py:18
  28.7 0.7 %collective-permute-start.11 = (f32[32,512]{1,0:T(8,128)S(1)}, f32[32,512]{1,0:T(8,128)S(1)}, u32[]{:S(2)}, u32[]{:S(2)}) collective-permute-start(f32[32,512]{1,0:T(8,128)S(1)} %get-tuple-element.28), channel_id=1, source_target_pairs={{0,4},{4,0},{8,12},{12,8},{16,20},{20,16},{24,28},{28,24},{1,5},{5... | collective-permute-start | bytes 196616 | tf_op jit(solution)/shard_map/ppermute | solution.py:18
  29.4 0.6 %collective-permute-done.12 = f32[64,128]{1,0:T(8,128)S(1)} collective-permute-done((f32[64,128]{1,0:T(8,128)S(1)}, f32[64,128]{1,0:T(8,128)S(1)}, u32[]{:S(2)}, u32[]{:S(2)}) %collective-permute-start.12) | collective-permute-done | bytes 32800 | tf_op jit(solution)/shard_map/ppermute | solution.py:18
  30.0 2.4 %collective-permute-done.13 = f32[64,128]{1,0:T(8,128)S(1)} collective-permute-done((f32[64,128]{1,0:T(8,128)S(1)}, f32[64,128]{1,0:T(8,128)S(1)}, u32[]{:S(2)}, u32[]{:S(2)}) %collective-permute-start.13) | collective-permute-done | bytes 32800 | tf_op jit(solution)/shard_map/ppermute | solution.py:18
  32.4 0.6 %add_add_fusion = f32[64,128]{1,0:T(8,128)} fusion(f32[64,128]{1,0:T(8,128)S(1)} %collective-permute-done.14, f32[64,128]{1,0:T(8,128)S(1)} %collective-permute-done.13, f32[64,128]{1,0:T(8,128)S(1)} %get-tuple-element.26.refs_4_, f32[64,128]{1,0:T(8,128)S(1)} %collective-permute-done.12), kind=kLoop, calls=%fused_computation.1 | loop fusion | flops 24576 | bytes 163840 | tf_op jit(solution)/shard_map/add | solution.py:268
  33.0 0.0 collective-permute-done.11
  33.0 0.6 %add_bitcast_fusion = f32[1,1,32,512]{3,2,1,0:T(8,128)} fusion(f32[32,512]{1,0:T(8,128)S(1)} %get-tuple-element.27, f32[32,512]{1,0:T(8,128)S(1)} %collective-permute-done.11), kind=kLoop, calls=%fused_computation | loop fusion | flops 16384 | bytes 196608 | tf_op jit(solution)/shard_map/reshape | solution.py:269
  (21 shorter events, 0.1 us)
Async XLA Ops:
  0.6 7.4 %copy-start = (f32[1,1,128,512]{3,2,1,0:T(8,128)S(1)}, f32[1,1,128,512]{3,2,1,0:T(8,128)}, u32[]{:S(2)}) copy-start(f32[1,1,128,512]{3,2,1,0:T(8,128)} %param.6) | copy-start | bytes 786436
  2.4 7.7 %collective-permute-start = (f32[2,128,128]{2,1,0:T(8,128)}, f32[2,128,128]{2,1,0:T(8,128)S(1)}, u32[]{:S(2)}, u32[]{:S(2)}) collective-permute-start(f32[2,128,128]{2,1,0:T(8,128)} %get-tuple-element.17), channel_id=1, source_target_pairs={{0,0},{1,4},{2,2},{3,6},{4,1},{5,5},{6,3},{7,7},{8,8},{9,12},{10,1... | collective-permute-start | bytes 393224 | tf_op jit(solution)/shard_map/ppermute | solution.py:225
  3.9 7.7 %copy-start.2 = (f32[128,128]{1,0:T(8,128)S(1)}, f32[128,128]{1,0:T(8,128)}, u32[]{:S(2)}) copy-start(f32[128,128]{1,0:T(8,128)} %get-tuple-element.18.near) | copy-start | bytes 196612
  3.9 7.7 %collective-permute-start.4 = (f32[1,128,128]{2,1,0:T(8,128)}, f32[1,128,128]{2,1,0:T(8,128)S(1)}, u32[]{:S(2)}, u32[]{:S(2)}) collective-permute-start(f32[1,128,128]{2,1,0:T(8,128)} %bitcast.14), channel_id=1, source_target_pairs={{0,16},{4,20},{8,24},{12,28},{16,0},{20,4},{24,8},{28,12},{1,17},{... | collective-permute-start | bytes 196616 | tf_op jit(solution)/shard_map/ppermute | solution.py:18
  8.1 7.8 %collective-permute-start.6 = (f32[128,256]{1,0:T(8,128)S(1)}, f32[128,256]{1,0:T(8,128)S(1)}, u32[]{:S(2)}, u32[]{:S(2)}) collective-permute-start(f32[128,256]{1,0:T(8,128)S(1)} %get-tuple-element.19), channel_id=1, source_target_pairs={{0,4},{4,0},{8,12},{12,8},{16,20},{20,16},{24,28},{28,24},{1,5},{5... | collective-permute-start | bytes 393224 | tf_op jit(solution)/shard_map/ppermute | solution.py:18
  10.1 5.8 %collective-permute-start.1 = (f32[2,128,128]{2,1,0:T(8,128)S(1)}, f32[2,128,128]{2,1,0:T(8,128)S(1)}, u32[]{:S(2)}, u32[]{:S(2)}) collective-permute-start(f32[2,128,128]{2,1,0:T(8,128)S(1)} %collective-permute-done.refs_0_), channel_id=1, source_target_pairs={{0,2},{1,3},{2,0},{3,1},{4,6},{5,7},{6,4},{7,5},{8,10},{9,11},{10,... | collective-permute-start | bytes 393224 | tf_op jit(solution)/shard_map/ppermute | solution.py:18
  11.7 6.2 %collective-permute-start.5 = (f32[2,128,128]{2,1,0:T(8,128)S(1)}, f32[2,128,128]{2,1,0:T(8,128)S(1)}, u32[]{:S(2)}, u32[]{:S(2)}) collective-permute-start(f32[2,128,128]{2,1,0:T(8,128)S(1)} %bitcast.12), channel_id=1, source_target_pairs={{0,8},{4,12},{8,0},{12,4},{16,24},{20,28},{24,16},{28,20},{1,9},{5... | collective-permute-start | bytes 393224 | tf_op jit(solution)/shard_map/ppermute | solution.py:18
  13.3 4.6 %collective-permute-start.2 = (f32[2,128,128]{2,1,0:T(8,128)S(1)}, f32[2,128,128]{2,1,0:T(8,128)S(1)}, u32[]{:S(2)}, u32[]{:S(2)}) collective-permute-start(f32[2,128,128]{2,1,0:T(8,128)S(1)} %collective-permute-done.refs_0_), channel_id=1, source_target_pairs={{0,1},{1,0},{2,3},{3,2},{4,5},{5,4},{6,7},{7,6},{8,9},{9,8},{10,11... | collective-permute-start | bytes 393224 | tf_op jit(solution)/shard_map/ppermute | solution.py:18
  15.9 2.0 %collective-permute-start.3 = (f32[2,128,128]{2,1,0:T(8,128)S(1)}, f32[2,128,128]{2,1,0:T(8,128)S(1)}, u32[]{:S(2)}, u32[]{:S(2)}) collective-permute-start(f32[2,128,128]{2,1,0:T(8,128)S(1)} %collective-permute-done.1.refs_1_), channel_id=1, source_target_pairs={{0,1},{1,0},{2,3},{3,2},{4,5},{5,4},{6,7},{7,6},{8,9},{9,8},{10,11... | collective-permute-start | bytes 393224 | tf_op jit(solution)/shard_map/ppermute | solution.py:18
  17.9 6.0 %copy-start.1 = (f32[64,128]{1,0:T(8,128)S(1)}, f32[64,128]{1,0:T(8,128)}, u32[]{:S(2)}) copy-start(f32[64,128]{1,0:T(8,128)} %dinv.1) | copy-start | bytes 98308
  18.3 5.6 %collective-permute-start.10 = (f32[256,128]{1,0:T(8,128)S(1)}, f32[256,128]{1,0:T(8,128)S(1)}, u32[]{:S(2)}, u32[]{:S(2)}) collective-permute-start(f32[256,128]{1,0:T(8,128)S(1)} %get-tuple-element.24.both), channel_id=1, source_target_pairs={{0,4},{4,0},{8,12},{12,8},{16,20},{20,16},{24,28},{28,24},{1,5},{5... | collective-permute-start | bytes 393224 | tf_op jit(solution)/shard_map/ppermute | solution.py:18
  19.0 8.6 %collective-permute-start.7 = (f32[64,128]{1,0:T(8,128)S(1)}, f32[64,128]{1,0:T(8,128)S(1)}, u32[]{:S(2)}, u32[]{:S(2)}) collective-permute-start(f32[64,128]{1,0:T(8,128)S(1)} %get-tuple-element.21), channel_id=1, source_target_pairs={{0,1},{1,0},{2,3},{3,2},{4,5},{5,4},{6,7},{7,6},{8,9},{9,8},{10,11... | collective-permute-start | bytes 98312 | tf_op jit(solution)/shard_map/ppermute | solution.py:18
  19.0 9.7 %collective-permute-start.8 = (f32[64,128]{1,0:T(8,128)S(1)}, f32[64,128]{1,0:T(8,128)S(1)}, u32[]{:S(2)}, u32[]{:S(2)}) collective-permute-start(f32[64,128]{1,0:T(8,128)S(1)} %get-tuple-element.22), channel_id=1, source_target_pairs={{0,2},{1,3},{2,0},{3,1},{4,6},{5,7},{6,4},{7,5},{8,10},{9,11},{10,... | collective-permute-start | bytes 98312 | tf_op jit(solution)/shard_map/ppermute | solution.py:18
  20.5 8.2 %collective-permute-start.9 = (f32[64,128]{1,0:T(8,128)S(1)}, f32[64,128]{1,0:T(8,128)S(1)}, u32[]{:S(2)}, u32[]{:S(2)}) collective-permute-start(f32[64,128]{1,0:T(8,128)S(1)} %get-tuple-element.23), channel_id=1, source_target_pairs={{0,3},{1,2},{2,1},{3,0},{4,7},{5,6},{6,5},{7,4},{8,11},{9,10},{10,... | collective-permute-start | bytes 98312 | tf_op jit(solution)/shard_map/ppermute | solution.py:18
  24.2 5.8 %collective-permute-start.12 = (f32[64,128]{1,0:T(8,128)S(1)}, f32[64,128]{1,0:T(8,128)S(1)}, u32[]{:S(2)}, u32[]{:S(2)}) collective-permute-start(f32[64,128]{1,0:T(8,128)S(1)} %get-tuple-element.29), channel_id=1, source_target_pairs={{0,24},{4,28},{8,16},{12,20},{16,8},{20,12},{24,0},{28,4},{1,25},{... | collective-permute-start | bytes 98312 | tf_op jit(solution)/shard_map/ppermute | solution.py:18
  27.6 4.8 %collective-permute-start.13 = (f32[64,128]{1,0:T(8,128)S(1)}, f32[64,128]{1,0:T(8,128)S(1)}, u32[]{:S(2)}, u32[]{:S(2)}) collective-permute-start(f32[64,128]{1,0:T(8,128)S(1)} %get-tuple-element.30), channel_id=1, source_target_pairs={{0,16},{4,20},{8,24},{12,28},{16,0},{20,4},{24,8},{28,12},{1,17},{... | collective-permute-start | bytes 98312 | tf_op jit(solution)/shard_map/ppermute | solution.py:18
  27.6 4.8 %collective-permute-start.14 = (f32[64,128]{1,0:T(8,128)S(1)}, f32[64,128]{1,0:T(8,128)S(1)}, u32[]{:S(2)}, u32[]{:S(2)}) collective-permute-start(f32[64,128]{1,0:T(8,128)S(1)} %get-tuple-element.31), channel_id=1, source_target_pairs={{0,8},{4,12},{8,0},{12,4},{16,24},{20,28},{24,16},{28,20},{1,9},{5... | collective-permute-start | bytes 98312 | tf_op jit(solution)/shard_map/ppermute | solution.py:18
  28.7 4.3 %collective-permute-start.11 = (f32[32,512]{1,0:T(8,128)S(1)}, f32[32,512]{1,0:T(8,128)S(1)}, u32[]{:S(2)}, u32[]{:S(2)}) collective-permute-start(f32[32,512]{1,0:T(8,128)S(1)} %get-tuple-element.28), channel_id=1, source_target_pairs={{0,4},{4,0},{8,12},{12,8},{16,20},{20,16},{24,28},{28,24},{1,5},{5... | collective-permute-start | bytes 196616 | tf_op jit(solution)/shard_map/ppermute | solution.py:18

commit v17 on v16

--- a/solution.py
+++ b/solution.py
@@ -184,7 +184,7 @@
 
 
 def collect_kernel(*refs):
-    arrived, (_, keep, send) = refs[:-3], refs[-3:]
+    arrived, (keep, send) = refs[:-2], refs[-2:]
     share = keep.shape[0]
     span = refs[0].shape[1]
     here = (lax.axis_index("row") & 1) * share
@@ -194,7 +194,7 @@
         send[:, spot] = piece[pl.ds(pl.multiple_of(share - here, 8), share), :]
 
 
-def collect(arrived, along):
+def collect(arrived):
     flips = len(arrived)
     share, span = arrived[0].shape[0] // 2, arrived[0].shape[1]
     if span % LANES:
@@ -207,22 +207,55 @@
     return pl.pallas_call(
         collect_kernel,
         out_shape=(part, part),
-        in_specs=[WHOLE] * flips + [pl.BlockSpec(memory_space=pl.ANY)],
+        in_specs=[WHOLE] * flips,
         out_specs=(WHOLE, WHOLE),
         cost_estimate=LIGHT,
         compiler_params=ROOM,
-    )(*arrived, along)
+    )(*arrived)
+
+
+def close_kernel(keep, came, *refs):
+    along, (off_diag, diag_block) = refs[:-2], refs[-2:]
+    off_diag[...] = keep[...] + came[...]
+    total = along[0][...]
+    for piece in along[1:]:
+        total = total + piece[...]
+    diag_block[...] = total
+
+
+def close(keep, came, along):
+    return pl.pallas_call(
+        close_kernel,
+        out_shape=[jax.ShapeDtypeStruct(x.shape, jnp.float32) for x in (keep, along[0])],
+        in_specs=[WHOLE] * (2 + len(along)),
+        out_specs=[WHOLE, WHOLE],
+        cost_estimate=LIGHT,
+        compiler_params=ROOM,
+    )(keep, came, *along)
+
+
+def pick_kernel(masked, swapped, held):
+    same = (lax.axis_index("row") & 1) == (lax.axis_index("col") & 1)
+    held[...] = jnp.where(same, masked[...], swapped[...])
 
 
 def pair_rows(masked):
     groups_row = lax.axis_size("row")
     groups_col = lax.axis_size("col")
-    cross = []
-    for r in range(groups_row):
-        for c in range(groups_col):
-            odd = (r ^ c) & 1
-            cross.append((r * groups_col + c, (r ^ odd) * groups_col + (c ^ odd)))
-    held = lax.ppermute(masked, ("row", "col"), cross)
+    cross = [
+        (r * groups_col + c, (r ^ 1) * groups_col + (c ^ 1))
+        for r in range(groups_row)
+        for c in range(groups_col)
+        if (r ^ c) & 1
+    ]
+    held = pl.pallas_call(
+        pick_kernel,
+        out_shape=jax.ShapeDtypeStruct(masked.shape, jnp.float32),
+        in_specs=[WHOLE, WHOLE],
+        out_specs=WHOLE,
+        cost_estimate=LIGHT,
+        compiler_params=ROOM,
+    )(masked, lax.ppermute(masked, ("row", "col"), cross))
     held = [held] + [flipped(held, "col", flip) for flip in range(2, groups_col, 2)]
     return held + [flipped(piece, "col", 1) for piece in held]
 
@@ -259,13 +292,13 @@
     both, outward = partials(pieces, columns, groups_col)
     got = flipped(both, "row", 1)
     arrived = [outward[0]] + [flipped(outward[f], "col", f) for f in range(1, groups_col)]
+    keep, send = collect(arrived)
+    came = flipped(send, "row", 1)
+
     flips = (0,) + tuple(range(groups_row - 2, 0, -2))
     along = finish(both, got, stay, near, dinv, flips)
-    keep, send = collect(arrived, along[0])
-    off_diag = keep + flipped(send, "row", 1)
-    diag_block = along[0]
-    for flip, piece in zip(flips[1:], along[1:]):
-        diag_block = diag_block + flipped(piece, "row", flip)
+    met = [flipped(piece, "row", flip) if flip else piece for flip, piece in zip(flips, along)]
+    off_diag, diag_block = close(keep, came, met)
     return (off_diag.reshape(block_rows, 1, share, width), diag_block)
 
 

time: 33.8 us -> 34.3 us (1.015)
  other arithmetic: 1.26 us -> 0 us
  starting transfers between devices: 18.6 us -> 19.3 us
  Pallas kernels: 2.66 us -> 3.33 us
  waiting for transfers between devices: 10.4 us -> 10.8 us
    ppermute x14, starting transfers between devices: 17.1 us -> 18.7 us  [flipped(): lax.ppermute(value, axis, [(i, i ^ flip) for i in range(lax.axis_size(axi...]
    ppermute x1, starting transfers between devices: 1.55 us -> 0.66 us  [pair_rows(): lax.ppermute(masked, ('row', 'col'), cross)]
    pallas_call x0 -> x2, Pallas kernels: none -> 0.67 us  [the longest x1 0.65 us: close(): pl.pallas_call(close_kernel, out_shape=[jax.ShapeDtypeStruct(x.shape, jnp...]
    reshape x1 -> x0, other arithmetic: 0.64 us -> none  [local(): return (off_diag.reshape(block_rows, 1, share, width), diag_block)]
    add x1 -> x0, other arithmetic: 0.63 us -> none  [local(): diag_block = diag_block + flipped(piece, 'row', flip)]
    ppermute x14, waiting for transfers between devices: 10.4 us -> 10.7 us  [flipped(): lax.ppermute(value, axis, [(i, i ^ flip) for i in range(lax.axis_size(axi...]
  transfers between devices with their start and end apart: 15 -> 15, of which waited for: 5 -> 6; matrix products, arithmetic and copies ran while one was open for 2% -> 0% of each run, Pallas kernels for 2% -> 2%
where the time goes in v17:
time: 34.3 us; the launch traced here: 34.1 us
  starting transfers between devices  19.3 us (56%)
  waiting for transfers between devices  10.8 us (31%)
  Pallas kernels  3.33 us (10%)
  between operations  0.74 us (2%)
    ppermute x14, starting transfers between devices, flipped(): lax.ppermute(value, axis, [(i, i ^ flip) for i in range(lax.axis_size(axi...  18.7 us
    ppermute x14, waiting for transfers between devices, flipped(): lax.ppermute(value, axis, [(i, i ^ flip) for i in range(lax.axis_size(axi...  10.7 us
    pallas_call x1, Pallas kernels, prepare(): pl.pallas_call(prepare_kernel, out_shape=(jax.ShapeDtypeStruct((block_col...  1.75 us
  transfers between devices with their start and end apart: 15, of which 6 were waited for; matrix products, arithmetic and copies ran while one was open for 0% of the time, Pallas kernels for 2%

profile of v17, /device:TPU:0, one launch (start us, length us, event | category | flops | bytes accessed | tf_op | source)
XLA Modules:
  0.0 34.1 jit_solution(8863779205538912941)
XLA Ops:
  0.6 1.8 %shard_map.59 = (f32[2,128,128]{2,1,0:T(8,128)}, f32[128,128]{1,0:T(8,128)}) custom-call(s32[2]{0:T(128)} %bitcast.15, f32[256,128]{1,0:T(8,128)} %bitcast.14, f32[128,512]{1,0:T(8,128)} %bitcast.7), custom_call_target="tpu_custom_call" | custom-call | flops 1000 | bytes 1000 | tf_op jit(solution)/shard_map/pallas_call | solution.py:57
  2.4 0.7 %collective-permute-start = (f32[2,128,128]{2,1,0:T(8,128)}, f32[2,128,128]{2,1,0:T(8,128)S(1)}, u32[]{:S(2)}, u32[]{:S(2)}) collective-permute-start(f32[2,128,128]{2,1,0:T(8,128)} %get-tuple-element.19.masked), channel_id=1, source_target_pairs={{1,4},{3,6},{4,1},{6,3},{9,12},{11,14},{12,9},{14,11},{17,20},{19,... | collective-permute-start | bytes 393224 | tf_op jit(solution)/shard_map/ppermute | solution.py:258
  3.1 4.1 %collective-permute-start.4 = (f32[1,128,128]{2,1,0:T(8,128)}, f32[1,128,128]{2,1,0:T(8,128)S(1)}, u32[]{:S(2)}, u32[]{:S(2)}) collective-permute-start(f32[1,128,128]{2,1,0:T(8,128)} %bitcast.13), channel_id=1, source_target_pairs={{0,16},{4,20},{8,24},{12,28},{16,0},{20,4},{24,8},{28,12},{1,17},{... | collective-permute-start | bytes 196616 | tf_op jit(solution)/shard_map/ppermute | solution.py:18
  7.2 0.1 shard_map.62
  7.3 0.0 copy-start.3
  7.3 2.8 %collective-permute-start.6 = (f32[128,256]{1,0:T(8,128)S(1)}, f32[128,256]{1,0:T(8,128)S(1)}, u32[]{:S(2)}, u32[]{:S(2)}) collective-permute-start(f32[128,256]{1,0:T(8,128)S(1)} %get-tuple-element.21), channel_id=1, source_target_pairs={{0,4},{4,0},{8,12},{12,8},{16,20},{20,16},{24,28},{28,24},{1,5},{5... | collective-permute-start | bytes 393224 | tf_op jit(solution)/shard_map/ppermute | solution.py:18
  10.1 0.0 collective-permute-done.swapped
  10.2 1.6 %collective-permute-start.1 = (f32[2,128,128]{2,1,0:T(8,128)S(1)}, f32[2,128,128]{2,1,0:T(8,128)S(1)}, u32[]{:S(2)}, u32[]{:S(2)}) collective-permute-start(f32[2,128,128]{2,1,0:T(8,128)S(1)} %shard_map.60.refs_0_), channel_id=1, source_target_pairs={{0,2},{1,3},{2,0},{3,1},{4,6},{5,7},{6,4},{7,5},{8,10},{9,11},{10,... | collective-permute-start | bytes 393224 | tf_op jit(solution)/shard_map/ppermute | solution.py:18
  11.8 1.6 %collective-permute-start.5 = (f32[2,128,128]{2,1,0:T(8,128)S(1)}, f32[2,128,128]{2,1,0:T(8,128)S(1)}, u32[]{:S(2)}, u32[]{:S(2)}) collective-permute-start(f32[2,128,128]{2,1,0:T(8,128)S(1)} %bitcast.11), channel_id=1, source_target_pairs={{0,8},{4,12},{8,0},{12,4},{16,24},{20,28},{24,16},{28,20},{1,9},{5... | collective-permute-start | bytes 393224 | tf_op jit(solution)/shard_map/ppermute | solution.py:18
  13.4 2.3 %collective-permute-done.1.refs_1_ = f32[2,128,128]{2,1,0:T(8,128)S(1)} collective-permute-done((f32[2,128,128]{2,1,0:T(8,128)S(1)}, f32[2,128,128]{2,1,0:T(8,128)S(1)}, u32[]{:S(2)}, u32[]{:S(2)}) %collective-permute-start.1) | collective-permute-done | bytes 131104 | tf_op jit(solution)/shard_map/ppermute | solution.py:18
  15.7 1.5 %collective-permute-done.5.second = f32[2,128,128]{2,1,0:T(8,128)S(1)} collective-permute-done((f32[2,128,128]{2,1,0:T(8,128)S(1)}, f32[2,128,128]{2,1,0:T(8,128)S(1)}, u32[]{:S(2)}, u32[]{:S(2)}) %collective-permute-start.5) | collective-permute-done | bytes 131104 | tf_op jit(solution)/shard_map/ppermute | solution.py:18
  17.2 0.4 %shard_map.64 = (f32[256,128]{1,0:T(8,128)S(1)}, f32[64,128]{1,0:T(8,128)S(1)}, f32[64,128]{1,0:T(8,128)S(1)}, f32[64,128]{1,0:T(8,128)S(1)}, f32[64,128]{1,0:T(8,128)S(1)}) custom-call(f32[2,128,128]{2,1,0:T(8,128)S(1)} %shard_map.60.refs_0_, f32[2,128,128]{2,1,0:T(8,128)S(1)} %collective-permute-done.1.refs_1_, ...), custom_call_target="tpu_custom_call" | custom-call | flops 1000 | bytes 1000 | tf_op jit(solution)/shard_map/pallas_call | solution.py:118
  17.6 1.4 %collective-permute-start.11 = (f32[256,128]{1,0:T(8,128)S(1)}, f32[256,128]{1,0:T(8,128)S(1)}, u32[]{:S(2)}, u32[]{:S(2)}) collective-permute-start(f32[256,128]{1,0:T(8,128)S(1)} %get-tuple-element.28.both), channel_id=1, source_target_pairs={{0,4},{4,0},{8,12},{12,8},{16,20},{20,16},{24,28},{28,24},{1,5},{5... | collective-permute-start | bytes 393224 | tf_op jit(solution)/shard_map/ppermute | solution.py:18
  19.1 1.5 %collective-permute-start.8 = (f32[64,128]{1,0:T(8,128)S(1)}, f32[64,128]{1,0:T(8,128)S(1)}, u32[]{:S(2)}, u32[]{:S(2)}) collective-permute-start(f32[64,128]{1,0:T(8,128)S(1)} %get-tuple-element.24), channel_id=1, source_target_pairs={{0,2},{1,3},{2,0},{3,1},{4,6},{5,7},{6,4},{7,5},{8,10},{9,11},{10,... | collective-permute-start | bytes 98312 | tf_op jit(solution)/shard_map/ppermute | solution.py:18
  20.5 0.4 %collective-permute-start.9 = (f32[64,128]{1,0:T(8,128)S(1)}, f32[64,128]{1,0:T(8,128)S(1)}, u32[]{:S(2)}, u32[]{:S(2)}) collective-permute-start(f32[64,128]{1,0:T(8,128)S(1)} %get-tuple-element.25), channel_id=1, source_target_pairs={{0,3},{1,2},{2,1},{3,0},{4,7},{5,6},{6,5},{7,4},{8,11},{9,10},{10,... | collective-permute-start | bytes 98312 | tf_op jit(solution)/shard_map/ppermute | solution.py:18
  20.9 2.1 %collective-permute-done.8.refs_2_ = f32[64,128]{1,0:T(8,128)S(1)} collective-permute-done((f32[64,128]{1,0:T(8,128)S(1)}, f32[64,128]{1,0:T(8,128)S(1)}, u32[]{:S(2)}, u32[]{:S(2)}) %collective-permute-start.8) | collective-permute-done | bytes 32800 | tf_op jit(solution)/shard_map/ppermute | solution.py:18
  23.0 0.9 %collective-permute-done.9.refs_3_ = f32[64,128]{1,0:T(8,128)S(1)} collective-permute-done((f32[64,128]{1,0:T(8,128)S(1)}, f32[64,128]{1,0:T(8,128)S(1)}, u32[]{:S(2)}, u32[]{:S(2)}) %collective-permute-start.9) | collective-permute-done | bytes 32800 | tf_op jit(solution)/shard_map/ppermute | solution.py:18
  23.9 0.8 %collective-permute-start.10 = (f32[32,512]{1,0:T(8,128)S(1)}, f32[32,512]{1,0:T(8,128)S(1)}, u32[]{:S(2)}, u32[]{:S(2)}) collective-permute-start(f32[32,512]{1,0:T(8,128)S(1)} %get-tuple-element.27), channel_id=1, source_target_pairs={{0,4},{4,0},{8,12},{12,8},{16,20},{20,16},{24,28},{28,24},{1,5},{5... | collective-permute-start | bytes 196616 | tf_op jit(solution)/shard_map/ppermute | solution.py:18
  24.7 0.3 shard_map.66
  25.0 3.7 %collective-permute-start.12 = (f32[64,128]{1,0:T(8,128)S(1)}, f32[64,128]{1,0:T(8,128)S(1)}, u32[]{:S(2)}, u32[]{:S(2)}) collective-permute-start(f32[64,128]{1,0:T(8,128)S(1)} %get-tuple-element.31), channel_id=1, source_target_pairs={{0,24},{4,28},{8,16},{12,20},{16,8},{20,12},{24,0},{28,4},{1,25},{... | collective-permute-start | bytes 98312 | tf_op jit(solution)/shard_map/ppermute | solution.py:18
  28.7 0.8 %collective-permute-start.14 = (f32[64,128]{1,0:T(8,128)S(1)}, f32[64,128]{1,0:T(8,128)S(1)}, u32[]{:S(2)}, u32[]{:S(2)}) collective-permute-start(f32[64,128]{1,0:T(8,128)S(1)} %get-tuple-element.33), channel_id=1, source_target_pairs={{0,8},{4,12},{8,0},{12,4},{16,24},{20,28},{24,16},{28,20},{1,9},{5... | collective-permute-start | bytes 98312 | tf_op jit(solution)/shard_map/ppermute | solution.py:18
  29.5 1.3 %collective-permute-done.12.refs_1_ = f32[64,128]{1,0:T(8,128)S(1)} collective-permute-done((f32[64,128]{1,0:T(8,128)S(1)}, f32[64,128]{1,0:T(8,128)S(1)}, u32[]{:S(2)}, u32[]{:S(2)}) %collective-permute-start.12) | collective-permute-done | bytes 32800 | tf_op jit(solution)/shard_map/ppermute | solution.py:18
  30.8 2.7 %collective-permute-done.13.refs_2_ = f32[64,128]{1,0:T(8,128)S(1)} collective-permute-done((f32[64,128]{1,0:T(8,128)S(1)}, f32[64,128]{1,0:T(8,128)S(1)}, u32[]{:S(2)}, u32[]{:S(2)}) %collective-permute-start.13) | collective-permute-done | bytes 32800 | tf_op jit(solution)/shard_map/ppermute | solution.py:18
  33.5 0.7 %shard_map.67 = (f32[32,512]{1,0:T(8,128)}, f32[64,128]{1,0:T(8,128)}) custom-call(f32[32,512]{1,0:T(8,128)S(1)} %get-tuple-element.26.keep, f32[32,512]{1,0:T(8,128)S(1)} %collective-permute-done.10.came, f32[64,128]{1,0:T(8,128)S(1)} %get-tuple-element.30.refs_0_, f32[64,128]{1,0:T(8,128)S(1)} %collective-permute-done.12.refs_1_, ...), custom_call_target="tpu_custom_call" | custom-call | flops 1000 | bytes 1000 | tf_op jit(solution)/shard_map/pallas_call | solution.py:227
  (23 shorter events, 0.1 us)
Async XLA Ops:
  0.6 6.5 %copy-start = (f32[1,1,128,512]{3,2,1,0:T(8,128)S(1)}, f32[1,1,128,512]{3,2,1,0:T(8,128)}, u32[]{:S(2)}) copy-start(f32[1,1,128,512]{3,2,1,0:T(8,128)} %param.6) | copy-start | bytes 786436
  2.4 7.7 %collective-permute-start = (f32[2,128,128]{2,1,0:T(8,128)}, f32[2,128,128]{2,1,0:T(8,128)S(1)}, u32[]{:S(2)}, u32[]{:S(2)}) collective-permute-start(f32[2,128,128]{2,1,0:T(8,128)} %get-tuple-element.19.masked), channel_id=1, source_target_pairs={{1,4},{3,6},{4,1},{6,3},{9,12},{11,14},{12,9},{14,11},{17,20},{19,... | collective-permute-start | bytes 393224 | tf_op jit(solution)/shard_map/ppermute | solution.py:258
  3.1 7.1 %copy-start.1 = (f32[2,128,128]{2,1,0:T(8,128)S(1)}, f32[2,128,128]{2,1,0:T(8,128)}, u32[]{:S(2)}) copy-start(f32[2,128,128]{2,1,0:T(8,128)} %get-tuple-element.19.masked) | copy-start | bytes 393220
  3.1 8.7 %collective-permute-start.4 = (f32[1,128,128]{2,1,0:T(8,128)}, f32[1,128,128]{2,1,0:T(8,128)S(1)}, u32[]{:S(2)}, u32[]{:S(2)}) collective-permute-start(f32[1,128,128]{2,1,0:T(8,128)} %bitcast.13), channel_id=1, source_target_pairs={{0,16},{4,20},{8,24},{12,28},{16,0},{20,4},{24,8},{28,12},{1,17},{... | collective-permute-start | bytes 196616 | tf_op jit(solution)/shard_map/ppermute | solution.py:18
  7.3 4.4 %copy-start.3 = (f32[128,128]{1,0:T(8,128)S(1)}, f32[128,128]{1,0:T(8,128)}, u32[]{:S(2)}) copy-start(f32[128,128]{1,0:T(8,128)} %get-tuple-element.20.near) | copy-start | bytes 196612
  7.3 8.4 %collective-permute-start.6 = (f32[128,256]{1,0:T(8,128)S(1)}, f32[128,256]{1,0:T(8,128)S(1)}, u32[]{:S(2)}, u32[]{:S(2)}) collective-permute-start(f32[128,256]{1,0:T(8,128)S(1)} %get-tuple-element.21), channel_id=1, source_target_pairs={{0,4},{4,0},{8,12},{12,8},{16,20},{20,16},{24,28},{28,24},{1,5},{5... | collective-permute-start | bytes 393224 | tf_op jit(solution)/shard_map/ppermute | solution.py:18
  10.2 5.5 %collective-permute-start.1 = (f32[2,128,128]{2,1,0:T(8,128)S(1)}, f32[2,128,128]{2,1,0:T(8,128)S(1)}, u32[]{:S(2)}, u32[]{:S(2)}) collective-permute-start(f32[2,128,128]{2,1,0:T(8,128)S(1)} %shard_map.60.refs_0_), channel_id=1, source_target_pairs={{0,2},{1,3},{2,0},{3,1},{4,6},{5,7},{6,4},{7,5},{8,10},{9,11},{10,... | collective-permute-start | bytes 393224 | tf_op jit(solution)/shard_map/ppermute | solution.py:18
  11.8 5.4 %collective-permute-start.5 = (f32[2,128,128]{2,1,0:T(8,128)S(1)}, f32[2,128,128]{2,1,0:T(8,128)S(1)}, u32[]{:S(2)}, u32[]{:S(2)}) collective-permute-start(f32[2,128,128]{2,1,0:T(8,128)S(1)} %bitcast.11), channel_id=1, source_target_pairs={{0,8},{4,12},{8,0},{12,4},{16,24},{20,28},{24,16},{28,20},{1,9},{5... | collective-permute-start | bytes 393224 | tf_op jit(solution)/shard_map/ppermute | solution.py:18
  13.4 3.8 %collective-permute-start.2 = (f32[2,128,128]{2,1,0:T(8,128)S(1)}, f32[2,128,128]{2,1,0:T(8,128)S(1)}, u32[]{:S(2)}, u32[]{:S(2)}) collective-permute-start(f32[2,128,128]{2,1,0:T(8,128)S(1)} %shard_map.60.refs_0_), channel_id=1, source_target_pairs={{0,1},{1,0},{2,3},{3,2},{4,5},{5,4},{6,7},{7,6},{8,9},{9,8},{10,11... | collective-permute-start | bytes 393224 | tf_op jit(solution)/shard_map/ppermute | solution.py:18
  15.7 1.5 %collective-permute-start.3 = (f32[2,128,128]{2,1,0:T(8,128)S(1)}, f32[2,128,128]{2,1,0:T(8,128)S(1)}, u32[]{:S(2)}, u32[]{:S(2)}) collective-permute-start(f32[2,128,128]{2,1,0:T(8,128)S(1)} %collective-permute-done.1.refs_1_), channel_id=1, source_target_pairs={{0,1},{1,0},{2,3},{3,2},{4,5},{5,4},{6,7},{7,6},{8,9},{9,8},{10,11... | collective-permute-start | bytes 393224 | tf_op jit(solution)/shard_map/ppermute | solution.py:18
  17.6 7.0 %collective-permute-start.11 = (f32[256,128]{1,0:T(8,128)S(1)}, f32[256,128]{1,0:T(8,128)S(1)}, u32[]{:S(2)}, u32[]{:S(2)}) collective-permute-start(f32[256,128]{1,0:T(8,128)S(1)} %get-tuple-element.28.both), channel_id=1, source_target_pairs={{0,4},{4,0},{8,12},{12,8},{16,20},{20,16},{24,28},{28,24},{1,5},{5... | collective-permute-start | bytes 393224 | tf_op jit(solution)/shard_map/ppermute | solution.py:18
  19.1 1.9 %collective-permute-start.7 = (f32[64,128]{1,0:T(8,128)S(1)}, f32[64,128]{1,0:T(8,128)S(1)}, u32[]{:S(2)}, u32[]{:S(2)}) collective-permute-start(f32[64,128]{1,0:T(8,128)S(1)} %get-tuple-element.23), channel_id=1, source_target_pairs={{0,1},{1,0},{2,3},{3,2},{4,5},{5,4},{6,7},{7,6},{8,9},{9,8},{10,11... | collective-permute-start | bytes 98312 | tf_op jit(solution)/shard_map/ppermute | solution.py:18
  19.1 3.9 %collective-permute-start.8 = (f32[64,128]{1,0:T(8,128)S(1)}, f32[64,128]{1,0:T(8,128)S(1)}, u32[]{:S(2)}, u32[]{:S(2)}) collective-permute-start(f32[64,128]{1,0:T(8,128)S(1)} %get-tuple-element.24), channel_id=1, source_target_pairs={{0,2},{1,3},{2,0},{3,1},{4,6},{5,7},{6,4},{7,5},{8,10},{9,11},{10,... | collective-permute-start | bytes 98312 | tf_op jit(solution)/shard_map/ppermute | solution.py:18
  20.5 3.3 %collective-permute-start.9 = (f32[64,128]{1,0:T(8,128)S(1)}, f32[64,128]{1,0:T(8,128)S(1)}, u32[]{:S(2)}, u32[]{:S(2)}) collective-permute-start(f32[64,128]{1,0:T(8,128)S(1)} %get-tuple-element.25), channel_id=1, source_target_pairs={{0,3},{1,2},{2,1},{3,0},{4,7},{5,6},{6,5},{7,4},{8,11},{9,10},{10,... | collective-permute-start | bytes 98312 | tf_op jit(solution)/shard_map/ppermute | solution.py:18
  23.9 0.8 %copy-start.2 = (f32[64,128]{1,0:T(8,128)S(1)}, f32[64,128]{1,0:T(8,128)}, u32[]{:S(2)}) copy-start(f32[64,128]{1,0:T(8,128)} %dinv.1) | copy-start | bytes 98308
  23.9 5.6 %collective-permute-start.10 = (f32[32,512]{1,0:T(8,128)S(1)}, f32[32,512]{1,0:T(8,128)S(1)}, u32[]{:S(2)}, u32[]{:S(2)}) collective-permute-start(f32[32,512]{1,0:T(8,128)S(1)} %get-tuple-element.27), channel_id=1, source_target_pairs={{0,4},{4,0},{8,12},{12,8},{16,20},{20,16},{24,28},{28,24},{1,5},{5... | collective-permute-start | bytes 196616 | tf_op jit(solution)/shard_map/ppermute | solution.py:18
  25.0 5.8 %collective-permute-start.12 = (f32[64,128]{1,0:T(8,128)S(1)}, f32[64,128]{1,0:T(8,128)S(1)}, u32[]{:S(2)}, u32[]{:S(2)}) collective-permute-start(f32[64,128]{1,0:T(8,128)S(1)} %get-tuple-element.31), channel_id=1, source_target_pairs={{0,24},{4,28},{8,16},{12,20},{16,8},{20,12},{24,0},{28,4},{1,25},{... | collective-permute-start | bytes 98312 | tf_op jit(solution)/shard_map/ppermute | solution.py:18
  28.7 4.8 %collective-permute-start.13 = (f32[64,128]{1,0:T(8,128)S(1)}, f32[64,128]{1,0:T(8,128)S(1)}, u32[]{:S(2)}, u32[]{:S(2)}) collective-permute-start(f32[64,128]{1,0:T(8,128)S(1)} %get-tuple-element.32), channel_id=1, source_target_pairs={{0,16},{4,20},{8,24},{12,28},{16,0},{20,4},{24,8},{28,12},{1,17},{... | collective-permute-start | bytes 98312 | tf_op jit(solution)/shard_map/ppermute | solution.py:18
  28.7 4.8 %collective-permute-start.14 = (f32[64,128]{1,0:T(8,128)S(1)}, f32[64,128]{1,0:T(8,128)S(1)}, u32[]{:S(2)}, u32[]{:S(2)}) collective-permute-start(f32[64,128]{1,0:T(8,128)S(1)} %get-tuple-element.33), channel_id=1, source_target_pairs={{0,8},{4,12},{8,0},{12,4},{16,24},{20,28},{24,16},{28,20},{1,9},{5... | collective-permute-start | bytes 98312 | tf_op jit(solution)/shard_map/ppermute | solution.py:18

commit v18 on v17

--- a/solution.py
+++ b/solution.py
@@ -33,40 +33,67 @@
     return once(left_high, right_high) + (once(left_high, right_low) + once(left_low, right_high))
 
 
-def prepare_kernel(presence, blocks, factor, masked, mine):
+def parity_half(factor, tall, parity):
+    even, odd = [
+        jnp.concatenate(
+            [factor[:, i : i + tall] for i in range(first, factor.shape[1], 2 * tall)], axis=1
+        )
+        for first in (0, tall)
+    ]
+    return jnp.where(parity == 1, odd, even)
+
+
+def prepare_kernel(tall, presence, blocks, factor, masked, swap, mine):
     rows, span = mine.shape
     mine[...] = factor[:, pl.ds(pl.multiple_of(lax.axis_index("col") * span, LANES), span)]
+    row_bit = lax.axis_index("row") & 1
+    same = row_bit == (lax.axis_index("col") & 1)
     block_cols, _, order = masked.shape
     for a in range(rows // order):
         for b in range(block_cols):
             weight = presence[a * block_cols + b].astype(jnp.float32)
             picked = blocks[pl.ds(a * order * block_cols + b, order, stride=block_cols), :]
             masked[b, pl.ds(a * order, order), :] = picked * weight
-
-
-def prepare(presence, blocks, own, span):
+    half = parity_half(factor[...], tall, 1 - row_bit)
+    for b in range(swap.shape[0]):
+        part = half[:, b * order : (b + 1) * order]
+        if part.shape[1] and b < block_cols:
+            swap[b] = jnp.where(same, part, masked[b])
+        else:
+            swap[b] = part if part.shape[1] else masked[b]
+
+
+def prepare(presence, blocks, own, span, tall):
     rows, width = own.shape
     block_cols = blocks.shape[0] // rows
     order = blocks.shape[1]
+    depth = max(block_cols, width // 2 // order)
     if span % LANES:
         first = lax.axis_index("col") * span
+        row_bit = lax.axis_index("row") & 1
+        same = row_bit == (lax.axis_index("col") & 1)
         mine = lax.dynamic_slice_in_dim(own, first, span, 1)
         weights = presence.reshape(-1, 1, block_cols, 1).astype(jnp.float32)
         picked = blocks.reshape(-1, order, block_cols, order) * weights
-        return picked.transpose(2, 0, 1, 3).reshape(block_cols, rows, order), mine
-    return pl.pallas_call(
-        prepare_kernel,
+        masked = picked.transpose(2, 0, 1, 3).reshape(block_cols, rows, order)
+        half = parity_half(own, tall, 1 - row_bit).reshape(rows, -1, order).transpose(1, 0, 2)
+        half = jnp.pad(half, ((0, depth - half.shape[0]), (0, 0), (0, 0)))
+        padded = jnp.pad(masked, ((0, depth - block_cols), (0, 0), (0, 0)))
+        return masked, jnp.where(same, half, padded), mine
+    return pl.pallas_call(
+        functools.partial(prepare_kernel, tall),
         out_shape=(
             jax.ShapeDtypeStruct((block_cols, rows, order), jnp.float32),
+            jax.ShapeDtypeStruct((depth, rows, order), jnp.float32),
             jax.ShapeDtypeStruct((rows, span), jnp.float32),
         ),
         in_specs=[pl.BlockSpec(memory_space=pltpu.SMEM), WHOLE, WHOLE],
-        out_specs=(WHOLE, WHOLE),
+        out_specs=(WHOLE,) * 3,
         cost_estimate=LIGHT,
     )(presence, blocks, own)
 
 
-def joined_kernel(bit, first, second, near, out):
+def joined_kernel(bit, first, second, out):
     here = jnp.where((lax.axis_index("row") & bit) == 0, 0, 1)
     if first.ndim == 2:
         span = out.shape[3]
@@ -77,31 +104,41 @@
     out[:, 1 - here] = second[...]
 
 
-def joined(first, second, bit, near):
+def joined(first, second, bit):
     count, rows, span = second.shape
     both = pl.pallas_call(
         functools.partial(joined_kernel, bit),
         out_shape=jax.ShapeDtypeStruct((count, 2, rows, span), jnp.float32),
-        in_specs=[WHOLE, WHOLE, pl.BlockSpec(memory_space=pl.ANY)],
+        in_specs=[WHOLE, WHOLE],
         out_specs=WHOLE,
         cost_estimate=pl.CostEstimate(flops=HEAVY, bytes_accessed=1000, transcendentals=0),
         compiler_params=ROOM,
-    )(first, second, near)
+    )(first, second)
     return both.reshape(2 * count, rows, span)
 
 
 def partials_kernel(count, *refs):
-    pieces = refs[: 2 * count]
-    columns, both, *outward = refs[2 * count :]
-    block_cols, rows, order = pieces[0].shape
+    masked, mate, swapped, mate_swapped = refs[:4]
+    pieces, refs = refs[4 : 2 * count + 2], refs[2 * count + 2 :]
+    columns, both, *outward = refs
+    block_cols, rows, order = masked.shape
     col_index = lax.axis_index("col")
+    row_bit = lax.axis_index("row") & 1
+    same = row_bit == (col_index & 1)
     left, right = [], []
     for t in range(count):
         for b in range(block_cols):
-            left.append(jnp.concatenate([pieces[t][b], pieces[count + t][b]], axis=0))
+            if t:
+                ours, theirs = pieces[t - 1][b], pieces[count + t - 2][b]
+                mine = jnp.where(same, ours, theirs)
+                other = jnp.where(same, theirs, ours)
+            else:
+                mine = jnp.where(same, masked[b], mate[b])
+                other = jnp.where(same, mate_swapped[b], swapped[b])
+            left.append(jnp.concatenate([mine, other], axis=0))
             right.append(columns[b * count + ((col_index >> 1) ^ t)])
     summed = product(jnp.concatenate(left, axis=1), jnp.concatenate(right, axis=0), ((1,), (0,)))
-    here = (col_index & 1) * rows
+    here = row_bit * rows
     both[pl.ds(pl.multiple_of(here, 8), rows), :] = summed[:rows]
     both[pl.ds(pl.multiple_of(rows - here, 8), rows), :] = summed[rows:]
     share = order // len(outward)
@@ -116,7 +153,7 @@
     rows, span = 2 * pieces[0].shape[1], columns.shape[2]
     outward = (jax.ShapeDtypeStruct((rows // receivers, span), jnp.float32),) * receivers
     both, *outward = pl.pallas_call(
-        functools.partial(partials_kernel, len(pieces) // 2),
+        functools.partial(partials_kernel, len(pieces) // 2 - 1),
         out_shape=(jax.ShapeDtypeStruct((rows, span), jnp.float32),) + outward,
         in_specs=[WHOLE] * (len(pieces) + 1),
         out_specs=(WHOLE,) * (1 + receivers),
@@ -126,30 +163,23 @@
     return both, outward
 
 
-def halves_kernel(tall, own, stay, go):
-    even, odd = [
-        jnp.concatenate([own[:, i : i + tall] for i in range(first, own.shape[1], 2 * tall)], axis=1)
-        for first in (0, tall)
-    ]
-    upper = (lax.axis_index("row") & 1) == 1
-    stay[...] = jnp.where(upper, odd, even)
-    go[...] = jnp.where(upper, even, odd)
-
-
-def halves(own, tall):
+def stay_kernel(tall, own, stay):
+    stay[...] = parity_half(own[...], tall, lax.axis_index("row") & 1)
+
+
+def stay_half(own, tall):
     rows, width = own.shape
-    part = jax.ShapeDtypeStruct((rows, width // 2), jnp.float32)
-    return pl.pallas_call(
-        functools.partial(halves_kernel, tall),
-        out_shape=(part, part),
+    return pl.pallas_call(
+        functools.partial(stay_kernel, tall),
+        out_shape=jax.ShapeDtypeStruct((rows, width // 2), jnp.float32),
         in_specs=[WHOLE],
-        out_specs=(WHOLE, WHOLE),
+        out_specs=WHOLE,
         cost_estimate=LIGHT,
         compiler_params=ROOM,
     )(own)
 
 
-def finish_kernel(flips, both, got, stay, near, dinv, *refs):
+def finish_kernel(flips, both, got, stay, swapped, mate_swapped, dinv, *refs):
     along, update, terms = refs[:-2], refs[-2], refs[-1]
     rows = stay.shape[0]
     row_index = lax.axis_index("row")
@@ -157,7 +187,10 @@
     update[...] = both[...] + got[...]
     mine = update[pl.ds(pl.multiple_of(here, 8), rows), :]
     other = update[pl.ds(pl.multiple_of(rows - here, 8), rows), :]
-    factors = jnp.concatenate([stay[...], near[...]], axis=0)
+    same = (row_index & 1) == (lax.axis_index("col") & 1)
+    depth = stay.shape[1] // swapped.shape[2]
+    near = [jnp.where(same, swapped[j], mate_swapped[j]) for j in range(depth)]
+    factors = jnp.concatenate([stay[...], jnp.concatenate(near, axis=1)], axis=0)
     terms[...] = product(factors, jnp.concatenate([mine, other], axis=0), ((0,), (0,)))
     tall = dinv.shape[0]
     for flip, piece in zip(flips, along):
@@ -166,13 +199,13 @@
     along[0][...] = along[0][...] + dinv[...]
 
 
-def finish(both, got, stay, near, dinv, flips):
+def finish(both, got, stay, swapped, mate_swapped, dinv, flips):
     rows, half = stay.shape
     span = both.shape[1]
     return pl.pallas_call(
         functools.partial(finish_kernel, flips),
         out_shape=(jax.ShapeDtypeStruct(dinv.shape, jnp.float32),) * len(flips),
-        in_specs=[WHOLE] * 5,
+        in_specs=[WHOLE] * 6,
         out_specs=(WHOLE,) * len(flips),
         scratch_shapes=[
             pltpu.VMEM((2 * rows, span), jnp.float32),
@@ -180,7 +213,7 @@
         ],
         cost_estimate=LIGHT,
         compiler_params=ROOM,
-    )(both, got, stay, near, dinv)
+    )(both, got, stay, swapped, mate_swapped, dinv)
 
 
 def collect_kernel(*refs):
@@ -236,18 +269,19 @@
 
 def pick_kernel(masked, swapped, held):
     same = (lax.axis_index("row") & 1) == (lax.axis_index("col") & 1)
-    held[...] = jnp.where(same, masked[...], swapped[...])
-
-
-def pair_rows(masked):
+    for b in range(held.shape[0]):
+        held[b] = jnp.where(same, masked[b], swapped[b])
+
+
+def pair_rows(masked, swap):
     groups_row = lax.axis_size("row")
     groups_col = lax.axis_size("col")
     cross = [
         (r * groups_col + c, (r ^ 1) * groups_col + (c ^ 1))
         for r in range(groups_row)
         for c in range(groups_col)
-        if (r ^ c) & 1
     ]
+    swapped = lax.ppermute(swap, ("row", "col"), cross)
     held = pl.pallas_call(
         pick_kernel,
         out_shape=jax.ShapeDtypeStruct(masked.shape, jnp.float32),
@@ -255,18 +289,20 @@
         out_specs=WHOLE,
         cost_estimate=LIGHT,
         compiler_params=ROOM,
-    )(masked, lax.ppermute(masked, ("row", "col"), cross))
-    held = [held] + [flipped(held, "col", flip) for flip in range(2, groups_col, 2)]
-    return held + [flipped(piece, "col", 1) for piece in held]
-
-
-def along_line(mine, own, near):
+    )(masked, swapped)
+    ours = [flipped(held, "col", flip) for flip in range(2, groups_col, 2)]
+    theirs = [flipped(piece, "col", 1) for piece in ours]
+    mates = [flipped(masked, "col", 1), flipped(swapped, "col", 1)]
+    return [masked, mates[0], swapped, mates[1]] + ours + theirs
+
+
+def along_line(mine, own):
     strips = mine[None]
     bit = lax.axis_size("row") // 2
     while bit > 1:
         whole = strips.shape[0] == 1 and mine.shape[1] % LANES == 0
         first = own if whole else strips
-        strips = joined(first, flipped(strips, "row", bit), bit, near if bit == 2 else mine)
+        strips = joined(first, flipped(strips, "row", bit), bit)
         bit //= 2
     return strips
 
@@ -282,12 +318,12 @@
 
     own = factor.reshape(rows, width)
     blocks = inverse_set.reshape(rows * block_cols, order)
-    masked, mine = prepare(presence.reshape(-1), blocks, own, span)
-    stay, go = halves(own, width // groups_row)
-    near = flipped(go, "row", 1)
-    columns = along_line(mine, own, near).reshape(-1, block_rows, order, span).transpose(1, 0, 2, 3)
+    tall = width // groups_row
+    masked, swap, mine = prepare(presence.reshape(-1), blocks, own, span, tall)
+    stay = stay_half(own, tall)
+    columns = along_line(mine, own).reshape(-1, block_rows, order, span).transpose(1, 0, 2, 3)
     columns = columns.reshape(-1, order, span)
-    pieces = pair_rows(masked)
+    pieces = pair_rows(masked, swap)
 
     both, outward = partials(pieces, columns, groups_col)
     got = flipped(both, "row", 1)
@@ -296,7 +332,7 @@
     came = flipped(send, "row", 1)
 
     flips = (0,) + tuple(range(groups_row - 2, 0, -2))
-    along = finish(both, got, stay, near, dinv, flips)
+    along = finish(both, got, stay, pieces[2], pieces[3], dinv, flips)
     met = [flipped(piece, "row", flip) if flip else piece for flip, piece in zip(flips, along)]
     off_diag, diag_block = close(keep, came, met)
     return (off_diag.reshape(block_rows, 1, share, width), diag_block)

time: 34.3 us -> 36 us (1.050)
  Pallas kernels: 3.33 us -> 5.24 us
  starting transfers between devices: 19.3 us -> 18 us
  waiting for transfers between devices: 10.8 us -> 11.8 us
    ppermute x14, starting transfers between devices: 18.7 us -> 15.6 us  [flipped(): lax.ppermute(value, axis, [(i, i ^ flip) for i in range(lax.axis_size(axi...]
    ppermute x1, starting transfers between devices: 0.66 us -> 2.38 us  [pair_rows(): swapped = lax.ppermute(swap, ('row', 'col'), cross)]
    ppermute x1, waiting for transfers between devices: 0.01 us -> 1.6 us  [pair_rows(): swapped = lax.ppermute(swap, ('row', 'col'), cross)]
    pallas_call x3, Pallas kernels: 2.27 us -> 3.26 us  [the longest x1 1.84 us: prepare(): pl.pallas_call(functools.partial(prepare_kernel, tall), out_shape=(jax.Sh...]
    pallas_call x1, Pallas kernels: 0.02 us -> 0.92 us  [pair_rows(): pl.pallas_call(pick_kernel, out_shape=jax.ShapeDtypeStruct(masked.shape,...]
    ppermute x14, waiting for transfers between devices: 10.7 us -> 10.2 us  [flipped(): lax.ppermute(value, axis, [(i, i ^ flip) for i in range(lax.axis_size(axi...]
  transfers between devices with their start and end apart: 15 -> 15, of which waited for: 6 -> 7; matrix products, arithmetic and copies ran while one was open for 0% -> 0% of each run, Pallas kernels for 2% -> 4%
where the time goes in v18:
time: 36 us; the launch traced here: 35.8 us
  starting transfers between devices  18 us (50%)
  waiting for transfers between devices  11.8 us (33%)
  Pallas kernels  5.24 us (15%)
  between operations  0.74 us (2%)
    ppermute x14, starting transfers between devices, flipped(): lax.ppermute(value, axis, [(i, i ^ flip) for i in range(lax.axis_size(axi...  15.6 us
    ppermute x14, waiting for transfers between devices, flipped(): lax.ppermute(value, axis, [(i, i ^ flip) for i in range(lax.axis_size(axi...  10.2 us
    ppermute x1, starting transfers between devices, pair_rows(): swapped = lax.ppermute(swap, ('row', 'col'), cross)  2.38 us
    pallas_call x1, Pallas kernels, prepare(): pl.pallas_call(functools.partial(prepare_kernel, tall), out_shape=(jax.Sh...  1.84 us
    ppermute x1, waiting for transfers between devices, pair_rows(): swapped = lax.ppermute(swap, ('row', 'col'), cross)  1.6 us
    pallas_call x1, Pallas kernels, partials(): pl.pallas_call(functools.partial(partials_kernel, len(pieces) // 2 - 1),...  1.29 us
    pallas_call x1, Pallas kernels, pair_rows(): pl.pallas_call(pick_kernel, out_shape=jax.ShapeDtypeStruct(masked.shape,...  0.92 us
  transfers between devices with their start and end apart: 15, of which 7 were waited for; matrix products, arithmetic and copies ran while one was open for 0% of the time, Pallas kernels for 4%

profile of v18, /device:TPU:0, one launch (start us, length us, event | category | flops | bytes accessed | tf_op | source)
XLA Modules:
  0.0 35.8 jit_solution(12771928756251374062)
XLA Ops:
  0.6 1.8 %shard_map.59 = (f32[2,128,128]{2,1,0:T(8,128)}, f32[2,128,128]{2,1,0:T(8,128)}, f32[128,128]{1,0:T(8,128)}) custom-call(s32[2]{0:T(128)} %bitcast.14, f32[256,128]{1,0:T(8,128)} %bitcast.13, f32[128,512]{1,0:T(8,128)} %bitcast.7), custom_call_target="tpu_custom_call" | custom-call | flops 1000 | bytes 1000 | tf_op jit(solution)/shard_map/pallas_call | solution.py:83
  2.5 2.4 %collective-permute-start.1 = (f32[2,128,128]{2,1,0:T(8,128)}, f32[2,128,128]{2,1,0:T(8,128)S(1)}, u32[]{:S(2)}, u32[]{:S(2)}) collective-permute-start(f32[2,128,128]{2,1,0:T(8,128)} %get-tuple-element.19), channel_id=1, source_target_pairs={{0,5},{1,4},{2,7},{3,6},{4,1},{5,0},{6,3},{7,2},{8,13},{9,12},{10,... | collective-permute-start | bytes 393224 | tf_op jit(solution)/shard_map/ppermute | solution.py:284
  4.9 2.6 %collective-permute-start.5 = (f32[1,128,128]{2,1,0:T(8,128)}, f32[1,128,128]{2,1,0:T(8,128)S(1)}, u32[]{:S(2)}, u32[]{:S(2)}) collective-permute-start(f32[1,128,128]{2,1,0:T(8,128)} %bitcast.15), channel_id=1, source_target_pairs={{0,16},{4,20},{8,24},{12,28},{16,0},{20,4},{24,8},{28,12},{1,17},{... | collective-permute-start | bytes 196616 | tf_op jit(solution)/shard_map/ppermute | solution.py:18
  7.4 1.6 %collective-permute-done.1.swapped.refs_2_ = f32[2,128,128]{2,1,0:T(8,128)S(1)} collective-permute-done((f32[2,128,128]{2,1,0:T(8,128)}, f32[2,128,128]{2,1,0:T(8,128)S(1)}, u32[]{:S(2)}, u32[]{:S(2)}) %collective-permute-start.1) | collective-permute-done | bytes 131104 | tf_op jit(solution)/shard_map/ppermute | solution.py:284
  9.0 0.9 %shard_map.60 = f32[2,128,128]{2,1,0:T(8,128)S(1)} custom-call(f32[2,128,128]{2,1,0:T(8,128)} %get-tuple-element.18.masked.refs_0_, f32[2,128,128]{2,1,0:T(8,128)S(1)} %collective-permute-done.1.swapped.refs_2_), custom_call_target="tpu_custom_call" | custom-call | flops 1000 | bytes 1000 | tf_op jit(solution)/shard_map/pallas_call | solution.py:285
  10.0 2.4 %collective-permute-start.3 = (f32[2,128,128]{2,1,0:T(8,128)S(1)}, f32[2,128,128]{2,1,0:T(8,128)S(1)}, u32[]{:S(2)}, u32[]{:S(2)}) collective-permute-start(f32[2,128,128]{2,1,0:T(8,128)S(1)} %shard_map.60), channel_id=1, source_target_pairs={{0,2},{1,3},{2,0},{3,1},{4,6},{5,7},{6,4},{7,5},{8,10},{9,11},{10,... | collective-permute-start | bytes 393224 | tf_op jit(solution)/shard_map/ppermute | solution.py:18
  12.4 1.6 %collective-permute-start.6 = (f32[2,128,128]{2,1,0:T(8,128)S(1)}, f32[2,128,128]{2,1,0:T(8,128)S(1)}, u32[]{:S(2)}, u32[]{:S(2)}) collective-permute-start(f32[2,128,128]{2,1,0:T(8,128)S(1)} %bitcast.11), channel_id=1, source_target_pairs={{0,8},{4,12},{8,0},{12,4},{16,24},{20,28},{24,16},{28,20},{1,9},{5... | collective-permute-start | bytes 393224 | tf_op jit(solution)/shard_map/ppermute | solution.py:18
  14.1 0.5 %collective-permute-start.2 = (f32[2,128,128]{2,1,0:T(8,128)S(1)}, f32[2,128,128]{2,1,0:T(8,128)S(1)}, u32[]{:S(2)}, u32[]{:S(2)}) collective-permute-start(f32[2,128,128]{2,1,0:T(8,128)S(1)} %collective-permute-done.1.swapped.refs_2_), channel_id=1, source_target_pairs={{0,1},{1,0},{2,3},{3,2},{4,5},{5,4},{6,7},{7,6},{8,9},{9,8},{10,11... | collective-permute-start | bytes 393224 | tf_op jit(solution)/shard_map/ppermute | solution.py:18
  14.6 1.6 %collective-permute-done.3.refs_4_ = f32[2,128,128]{2,1,0:T(8,128)S(1)} collective-permute-done((f32[2,128,128]{2,1,0:T(8,128)S(1)}, f32[2,128,128]{2,1,0:T(8,128)S(1)}, u32[]{:S(2)}, u32[]{:S(2)}) %collective-permute-start.3) | collective-permute-done | bytes 131104 | tf_op jit(solution)/shard_map/ppermute | solution.py:18
  16.2 1.6 %collective-permute-done.6.second = f32[2,128,128]{2,1,0:T(8,128)S(1)} collective-permute-done((f32[2,128,128]{2,1,0:T(8,128)S(1)}, f32[2,128,128]{2,1,0:T(8,128)S(1)}, u32[]{:S(2)}, u32[]{:S(2)}) %collective-permute-start.6) | collective-permute-done | bytes 131104 | tf_op jit(solution)/shard_map/ppermute | solution.py:18
  17.8 1.3 %shard_map.63 = (f32[256,128]{1,0:T(8,128)S(1)}, f32[64,128]{1,0:T(8,128)S(1)}, f32[64,128]{1,0:T(8,128)S(1)}, f32[64,128]{1,0:T(8,128)S(1)}, f32[64,128]{1,0:T(8,128)S(1)}) custom-call(f32[2,128,128]{2,1,0:T(8,128)} %get-tuple-element.18.masked.refs_0_, f32[2,128,128]{2,1,0:T(8,128)S(1)} %collective-permute-done.refs_1_, ...), custom_call_target="tpu_custom_call" | custom-call | flops 1000 | bytes 1000 | tf_op jit(solution)/shard_map/pallas_call | solution.py:155
  19.1 1.6 %collective-permute-start.11 = (f32[256,128]{1,0:T(8,128)S(1)}, f32[256,128]{1,0:T(8,128)S(1)}, u32[]{:S(2)}, u32[]{:S(2)}) collective-permute-start(f32[256,128]{1,0:T(8,128)S(1)} %get-tuple-element.27.both), channel_id=1, source_target_pairs={{0,4},{4,0},{8,12},{12,8},{16,20},{20,16},{24,28},{28,24},{1,5},{5... | collective-permute-start | bytes 393224 | tf_op jit(solution)/shard_map/ppermute | solution.py:18
  20.7 1.5 %collective-permute-start.8 = (f32[64,128]{1,0:T(8,128)S(1)}, f32[64,128]{1,0:T(8,128)S(1)}, u32[]{:S(2)}, u32[]{:S(2)}) collective-permute-start(f32[64,128]{1,0:T(8,128)S(1)} %get-tuple-element.23), channel_id=1, source_target_pairs={{0,2},{1,3},{2,0},{3,1},{4,6},{5,7},{6,4},{7,5},{8,10},{9,11},{10,... | collective-permute-start | bytes 98312 | tf_op jit(solution)/shard_map/ppermute | solution.py:18
  22.2 0.4 %collective-permute-start.9 = (f32[64,128]{1,0:T(8,128)S(1)}, f32[64,128]{1,0:T(8,128)S(1)}, u32[]{:S(2)}, u32[]{:S(2)}) collective-permute-start(f32[64,128]{1,0:T(8,128)S(1)} %get-tuple-element.24), channel_id=1, source_target_pairs={{0,3},{1,2},{2,1},{3,0},{4,7},{5,6},{6,5},{7,4},{8,11},{9,10},{10,... | collective-permute-start | bytes 98312 | tf_op jit(solution)/shard_map/ppermute | solution.py:18
  22.6 2.1 %collective-permute-done.8.refs_2_ = f32[64,128]{1,0:T(8,128)S(1)} collective-permute-done((f32[64,128]{1,0:T(8,128)S(1)}, f32[64,128]{1,0:T(8,128)S(1)}, u32[]{:S(2)}, u32[]{:S(2)}) %collective-permute-start.8) | collective-permute-done | bytes 32800 | tf_op jit(solution)/shard_map/ppermute | solution.py:18
  24.6 0.9 %collective-permute-done.9.refs_3_ = f32[64,128]{1,0:T(8,128)S(1)} collective-permute-done((f32[64,128]{1,0:T(8,128)S(1)}, f32[64,128]{1,0:T(8,128)S(1)}, u32[]{:S(2)}, u32[]{:S(2)}) %collective-permute-start.9) | collective-permute-done | bytes 32800 | tf_op jit(solution)/shard_map/ppermute | solution.py:18
  25.5 0.6 %collective-permute-start.10 = (f32[32,512]{1,0:T(8,128)S(1)}, f32[32,512]{1,0:T(8,128)S(1)}, u32[]{:S(2)}, u32[]{:S(2)}) collective-permute-start(f32[32,512]{1,0:T(8,128)S(1)} %get-tuple-element.26), channel_id=1, source_target_pairs={{0,4},{4,0},{8,12},{12,8},{16,20},{20,16},{24,28},{28,24},{1,5},{5... | collective-permute-start | bytes 196616 | tf_op jit(solution)/shard_map/ppermute | solution.py:18
  26.1 0.1 shard_map.65.stay
  26.3 0.3 shard_map.66
  26.6 3.7 %collective-permute-start.12 = (f32[64,128]{1,0:T(8,128)S(1)}, f32[64,128]{1,0:T(8,128)S(1)}, u32[]{:S(2)}, u32[]{:S(2)}) collective-permute-start(f32[64,128]{1,0:T(8,128)S(1)} %get-tuple-element.29), channel_id=1, source_target_pairs={{0,24},{4,28},{8,16},{12,20},{16,8},{20,12},{24,0},{28,4},{1,25},{... | collective-permute-start | bytes 98312 | tf_op jit(solution)/shard_map/ppermute | solution.py:18
  30.3 0.8 %collective-permute-start.14 = (f32[64,128]{1,0:T(8,128)S(1)}, f32[64,128]{1,0:T(8,128)S(1)}, u32[]{:S(2)}, u32[]{:S(2)}) collective-permute-start(f32[64,128]{1,0:T(8,128)S(1)} %get-tuple-element.31), channel_id=1, source_target_pairs={{0,8},{4,12},{8,0},{12,4},{16,24},{20,28},{24,16},{28,20},{1,9},{5... | collective-permute-start | bytes 98312 | tf_op jit(solution)/shard_map/ppermute | solution.py:18
  31.1 1.3 %collective-permute-done.12.refs_1_ = f32[64,128]{1,0:T(8,128)S(1)} collective-permute-done((f32[64,128]{1,0:T(8,128)S(1)}, f32[64,128]{1,0:T(8,128)S(1)}, u32[]{:S(2)}, u32[]{:S(2)}) %collective-permute-start.12) | collective-permute-done | bytes 32800 | tf_op jit(solution)/shard_map/ppermute | solution.py:18
  32.4 2.7 %collective-permute-done.13.refs_2_ = f32[64,128]{1,0:T(8,128)S(1)} collective-permute-done((f32[64,128]{1,0:T(8,128)S(1)}, f32[64,128]{1,0:T(8,128)S(1)}, u32[]{:S(2)}, u32[]{:S(2)}) %collective-permute-start.13) | collective-permute-done | bytes 32800 | tf_op jit(solution)/shard_map/ppermute | solution.py:18
  35.1 0.7 %shard_map.67 = (f32[32,512]{1,0:T(8,128)}, f32[64,128]{1,0:T(8,128)}) custom-call(f32[32,512]{1,0:T(8,128)S(1)} %get-tuple-element.25.keep, f32[32,512]{1,0:T(8,128)S(1)} %collective-permute-done.10.came, f32[64,128]{1,0:T(8,128)S(1)} %get-tuple-element.28.refs_0_, f32[64,128]{1,0:T(8,128)S(1)} %collective-permute-done.12.refs_1_, ...), custom_call_target="tpu_custom_call" | custom-call | flops 1000 | bytes 1000 | tf_op jit(solution)/shard_map/pallas_call | solution.py:260
  (19 shorter events, 0.1 us)
Async XLA Ops:
  2.5 9.9 %copy-start = (f32[1,1,128,512]{3,2,1,0:T(8,128)S(1)}, f32[1,1,128,512]{3,2,1,0:T(8,128)}, u32[]{:S(2)}) copy-start(f32[1,1,128,512]{3,2,1,0:T(8,128)} %param.6) | copy-start | bytes 786436
  2.5 6.6 %collective-permute-start.1 = (f32[2,128,128]{2,1,0:T(8,128)}, f32[2,128,128]{2,1,0:T(8,128)S(1)}, u32[]{:S(2)}, u32[]{:S(2)}) collective-permute-start(f32[2,128,128]{2,1,0:T(8,128)} %get-tuple-element.19), channel_id=1, source_target_pairs={{0,5},{1,4},{2,7},{3,6},{4,1},{5,0},{6,3},{7,2},{8,13},{9,12},{10,... | collective-permute-start | bytes 393224 | tf_op jit(solution)/shard_map/ppermute | solution.py:284
  4.9 7.6 %collective-permute-start.5 = (f32[1,128,128]{2,1,0:T(8,128)}, f32[1,128,128]{2,1,0:T(8,128)S(1)}, u32[]{:S(2)}, u32[]{:S(2)}) collective-permute-start(f32[1,128,128]{2,1,0:T(8,128)} %bitcast.15), channel_id=1, source_target_pairs={{0,16},{4,20},{8,24},{12,28},{16,0},{20,4},{24,8},{28,12},{1,17},{... | collective-permute-start | bytes 196616 | tf_op jit(solution)/shard_map/ppermute | solution.py:18
  10.0 6.2 %collective-permute-start.3 = (f32[2,128,128]{2,1,0:T(8,128)S(1)}, f32[2,128,128]{2,1,0:T(8,128)S(1)}, u32[]{:S(2)}, u32[]{:S(2)}) collective-permute-start(f32[2,128,128]{2,1,0:T(8,128)S(1)} %shard_map.60), channel_id=1, source_target_pairs={{0,2},{1,3},{2,0},{3,1},{4,6},{5,7},{6,4},{7,5},{8,10},{9,11},{10,... | collective-permute-start | bytes 393224 | tf_op jit(solution)/shard_map/ppermute | solution.py:18
  12.4 5.3 %collective-permute-start.6 = (f32[2,128,128]{2,1,0:T(8,128)S(1)}, f32[2,128,128]{2,1,0:T(8,128)S(1)}, u32[]{:S(2)}, u32[]{:S(2)}) collective-permute-start(f32[2,128,128]{2,1,0:T(8,128)S(1)} %bitcast.11), channel_id=1, source_target_pairs={{0,8},{4,12},{8,0},{12,4},{16,24},{20,28},{24,16},{28,20},{1,9},{5... | collective-permute-start | bytes 393224 | tf_op jit(solution)/shard_map/ppermute | solution.py:18
  14.1 3.7 %collective-permute-start = (f32[2,128,128]{2,1,0:T(8,128)}, f32[2,128,128]{2,1,0:T(8,128)S(1)}, u32[]{:S(2)}, u32[]{:S(2)}) collective-permute-start(f32[2,128,128]{2,1,0:T(8,128)} %get-tuple-element.18.masked.refs_0_), channel_id=1, source_target_pairs={{0,1},{1,0},{2,3},{3,2},{4,5},{5,4},{6,7},{7,6},{8,9},{9,8},{10,11... | collective-permute-start | bytes 393224 | tf_op jit(solution)/shard_map/ppermute | solution.py:18
  14.1 3.7 %collective-permute-start.2 = (f32[2,128,128]{2,1,0:T(8,128)S(1)}, f32[2,128,128]{2,1,0:T(8,128)S(1)}, u32[]{:S(2)}, u32[]{:S(2)}) collective-permute-start(f32[2,128,128]{2,1,0:T(8,128)S(1)} %collective-permute-done.1.swapped.refs_2_), channel_id=1, source_target_pairs={{0,1},{1,0},{2,3},{3,2},{4,5},{5,4},{6,7},{7,6},{8,9},{9,8},{10,11... | collective-permute-start | bytes 393224 | tf_op jit(solution)/shard_map/ppermute | solution.py:18
  16.2 1.6 %collective-permute-start.4 = (f32[2,128,128]{2,1,0:T(8,128)S(1)}, f32[2,128,128]{2,1,0:T(8,128)S(1)}, u32[]{:S(2)}, u32[]{:S(2)}) collective-permute-start(f32[2,128,128]{2,1,0:T(8,128)S(1)} %collective-permute-done.3.refs_4_), channel_id=1, source_target_pairs={{0,1},{1,0},{2,3},{3,2},{4,5},{5,4},{6,7},{7,6},{8,9},{9,8},{10,11... | collective-permute-start | bytes 393224 | tf_op jit(solution)/shard_map/ppermute | solution.py:18
  19.1 7.1 %collective-permute-start.11 = (f32[256,128]{1,0:T(8,128)S(1)}, f32[256,128]{1,0:T(8,128)S(1)}, u32[]{:S(2)}, u32[]{:S(2)}) collective-permute-start(f32[256,128]{1,0:T(8,128)S(1)} %get-tuple-element.27.both), channel_id=1, source_target_pairs={{0,4},{4,0},{8,12},{12,8},{16,20},{20,16},{24,28},{28,24},{1,5},{5... | collective-permute-start | bytes 393224 | tf_op jit(solution)/shard_map/ppermute | solution.py:18
  20.7 1.9 %collective-permute-start.7 = (f32[64,128]{1,0:T(8,128)S(1)}, f32[64,128]{1,0:T(8,128)S(1)}, u32[]{:S(2)}, u32[]{:S(2)}) collective-permute-start(f32[64,128]{1,0:T(8,128)S(1)} %get-tuple-element.22), channel_id=1, source_target_pairs={{0,1},{1,0},{2,3},{3,2},{4,5},{5,4},{6,7},{7,6},{8,9},{9,8},{10,11... | collective-permute-start | bytes 98312 | tf_op jit(solution)/shard_map/ppermute | solution.py:18
  20.7 3.9 %collective-permute-start.8 = (f32[64,128]{1,0:T(8,128)S(1)}, f32[64,128]{1,0:T(8,128)S(1)}, u32[]{:S(2)}, u32[]{:S(2)}) collective-permute-start(f32[64,128]{1,0:T(8,128)S(1)} %get-tuple-element.23), channel_id=1, source_target_pairs={{0,2},{1,3},{2,0},{3,1},{4,6},{5,7},{6,4},{7,5},{8,10},{9,11},{10,... | collective-permute-start | bytes 98312 | tf_op jit(solution)/shard_map/ppermute | solution.py:18
  22.2 3.3 %collective-permute-start.9 = (f32[64,128]{1,0:T(8,128)S(1)}, f32[64,128]{1,0:T(8,128)S(1)}, u32[]{:S(2)}, u32[]{:S(2)}) collective-permute-start(f32[64,128]{1,0:T(8,128)S(1)} %get-tuple-element.24), channel_id=1, source_target_pairs={{0,3},{1,2},{2,1},{3,0},{4,7},{5,6},{6,5},{7,4},{8,11},{9,10},{10,... | collective-permute-start | bytes 98312 | tf_op jit(solution)/shard_map/ppermute | solution.py:18
  25.5 0.8 %copy-start.1 = (f32[64,128]{1,0:T(8,128)S(1)}, f32[64,128]{1,0:T(8,128)}, u32[]{:S(2)}) copy-start(f32[64,128]{1,0:T(8,128)} %dinv.1) | copy-start | bytes 98308
  25.5 5.6 %collective-permute-start.10 = (f32[32,512]{1,0:T(8,128)S(1)}, f32[32,512]{1,0:T(8,128)S(1)}, u32[]{:S(2)}, u32[]{:S(2)}) collective-permute-start(f32[32,512]{1,0:T(8,128)S(1)} %get-tuple-element.26), channel_id=1, source_target_pairs={{0,4},{4,0},{8,12},{12,8},{16,20},{20,16},{24,28},{28,24},{1,5},{5... | collective-permute-start | bytes 196616 | tf_op jit(solution)/shard_map/ppermute | solution.py:18
  26.6 5.8 %collective-permute-start.12 = (f32[64,128]{1,0:T(8,128)S(1)}, f32[64,128]{1,0:T(8,128)S(1)}, u32[]{:S(2)}, u32[]{:S(2)}) collective-permute-start(f32[64,128]{1,0:T(8,128)S(1)} %get-tuple-element.29), channel_id=1, source_target_pairs={{0,24},{4,28},{8,16},{12,20},{16,8},{20,12},{24,0},{28,4},{1,25},{... | collective-permute-start | bytes 98312 | tf_op jit(solution)/shard_map/ppermute | solution.py:18
  30.3 4.8 %collective-permute-start.13 = (f32[64,128]{1,0:T(8,128)S(1)}, f32[64,128]{1,0:T(8,128)S(1)}, u32[]{:S(2)}, u32[]{:S(2)}) collective-permute-start(f32[64,128]{1,0:T(8,128)S(1)} %get-tuple-element.30), channel_id=1, source_target_pairs={{0,16},{4,20},{8,24},{12,28},{16,0},{20,4},{24,8},{28,12},{1,17},{... | collective-permute-start | bytes 98312 | tf_op jit(solution)/shard_map/ppermute | solution.py:18
  30.3 4.8 %collective-permute-start.14 = (f32[64,128]{1,0:T(8,128)S(1)}, f32[64,128]{1,0:T(8,128)S(1)}, u32[]{:S(2)}, u32[]{:S(2)}) collective-permute-start(f32[64,128]{1,0:T(8,128)S(1)} %get-tuple-element.31), channel_id=1, source_target_pairs={{0,8},{4,12},{8,0},{12,4},{16,24},{20,28},{24,16},{28,20},{1,9},{5... | collective-permute-start | bytes 98312 | tf_op jit(solution)/shard_map/ppermute | solution.py:18

commit v19 on v18

--- a/solution.py
+++ b/solution.py
@@ -43,24 +43,29 @@
     return jnp.where(parity == 1, odd, even)
 
 
-def prepare_kernel(tall, presence, blocks, factor, masked, swap, mine):
+def masked_block(presence, blocks, block_cols, a, b):
+    order = blocks.shape[1]
+    weight = presence[a * block_cols + b].astype(jnp.float32)
+    return blocks[pl.ds(a * order * block_cols + b, order, stride=block_cols), :] * weight
+
+
+def prepare_kernel(tall, presence, blocks, factor, swap, mine):
     rows, span = mine.shape
     mine[...] = factor[:, pl.ds(pl.multiple_of(lax.axis_index("col") * span, LANES), span)]
     row_bit = lax.axis_index("row") & 1
     same = row_bit == (lax.axis_index("col") & 1)
-    block_cols, _, order = masked.shape
-    for a in range(rows // order):
-        for b in range(block_cols):
-            weight = presence[a * block_cols + b].astype(jnp.float32)
-            picked = blocks[pl.ds(a * order * block_cols + b, order, stride=block_cols), :]
-            masked[b, pl.ds(a * order, order), :] = picked * weight
+    order = swap.shape[2]
+    block_cols = blocks.shape[0] // rows
     half = parity_half(factor[...], tall, 1 - row_bit)
     for b in range(swap.shape[0]):
-        part = half[:, b * order : (b + 1) * order]
-        if part.shape[1] and b < block_cols:
-            swap[b] = jnp.where(same, part, masked[b])
-        else:
-            swap[b] = part if part.shape[1] else masked[b]
+        for a in range(rows // order):
+            here = pl.ds(a * order, order)
+            part = half[a * order : (a + 1) * order, b * order : (b + 1) * order]
+            if b >= block_cols:
+                swap[b, here, :] = part
+                continue
+            block = masked_block(presence, blocks, block_cols, a, b)
+            swap[b, here, :] = jnp.where(same, part, block) if part.shape[1] else block
 
 
 def prepare(presence, blocks, own, span, tall):
@@ -79,16 +84,15 @@
         half = parity_half(own, tall, 1 - row_bit).reshape(rows, -1, order).transpose(1, 0, 2)
         half = jnp.pad(half, ((0, depth - half.shape[0]), (0, 0), (0, 0)))
         padded = jnp.pad(masked, ((0, depth - block_cols), (0, 0), (0, 0)))
-        return masked, jnp.where(same, half, padded), mine
+        return jnp.where(same, half, padded), mine
     return pl.pallas_call(
         functools.partial(prepare_kernel, tall),
         out_shape=(
-            jax.ShapeDtypeStruct((block_cols, rows, order), jnp.float32),
             jax.ShapeDtypeStruct((depth, rows, order), jnp.float32),
             jax.ShapeDtypeStruct((rows, span), jnp.float32),
         ),
         in_specs=[pl.BlockSpec(memory_space=pltpu.SMEM), WHOLE, WHOLE],
-        out_specs=(WHOLE,) * 3,
+        out_specs=(WHOLE, WHOLE),
         cost_estimate=LIGHT,
     )(presence, blocks, own)
 
@@ -118,27 +122,17 @@
 
 
 def partials_kernel(count, *refs):
-    masked, mate, swapped, mate_swapped = refs[:4]
-    pieces, refs = refs[4 : 2 * count + 2], refs[2 * count + 2 :]
-    columns, both, *outward = refs
-    block_cols, rows, order = masked.shape
+    pieces = refs[: 2 * count]
+    columns, both, *outward = refs[2 * count :]
+    block_cols, rows, order = pieces[0].shape
     col_index = lax.axis_index("col")
-    row_bit = lax.axis_index("row") & 1
-    same = row_bit == (col_index & 1)
     left, right = [], []
     for t in range(count):
         for b in range(block_cols):
-            if t:
-                ours, theirs = pieces[t - 1][b], pieces[count + t - 2][b]
-                mine = jnp.where(same, ours, theirs)
-                other = jnp.where(same, theirs, ours)
-            else:
-                mine = jnp.where(same, masked[b], mate[b])
-                other = jnp.where(same, mate_swapped[b], swapped[b])
-            left.append(jnp.concatenate([mine, other], axis=0))
+            left.append(jnp.concatenate([pieces[t][b], pieces[count + t][b]], axis=0))
             right.append(columns[b * count + ((col_index >> 1) ^ t)])
     summed = product(jnp.concatenate(left, axis=1), jnp.concatenate(right, axis=0), ((1,), (0,)))
-    here = row_bit * rows
+    here = (col_index & 1) * rows
     both[pl.ds(pl.multiple_of(here, 8), rows), :] = summed[:rows]
     both[pl.ds(pl.multiple_of(rows - here, 8), rows), :] = summed[rows:]
     share = order // len(outward)
@@ -153,7 +147,7 @@
     rows, span = 2 * pieces[0].shape[1], columns.shape[2]
     outward = (jax.ShapeDtypeStruct((rows // receivers, span), jnp.float32),) * receivers
     both, *outward = pl.pallas_call(
-        functools.partial(partials_kernel, len(pieces) // 2 - 1),
+        functools.partial(partials_kernel, len(pieces) // 2),
         out_shape=(jax.ShapeDtypeStruct((rows, span), jnp.float32),) + outward,
         in_specs=[WHOLE] * (len(pieces) + 1),
         out_specs=(WHOLE,) * (1 + receivers),
@@ -217,7 +211,7 @@
 
 
 def collect_kernel(*refs):
-    arrived, (keep, send) = refs[:-2], refs[-2:]
+    arrived, (_, keep, send) = refs[:-3], refs[-3:]
     share = keep.shape[0]
     span = refs[0].shape[1]
     here = (lax.axis_index("row") & 1) * share
@@ -227,7 +221,7 @@
         send[:, spot] = piece[pl.ds(pl.multiple_of(share - here, 8), share), :]
 
 
-def collect(arrived):
+def collect(arrived, along):
     flips = len(arrived)
     share, span = arrived[0].shape[0] // 2, arrived[0].shape[1]
     if span % LANES:
@@ -240,40 +234,52 @@
     return pl.pallas_call(
         collect_kernel,
         out_shape=(part, part),
-        in_specs=[WHOLE] * flips,
+        in_specs=[WHOLE] * flips + [pl.BlockSpec(memory_space=pl.ANY)],
         out_specs=(WHOLE, WHOLE),
         cost_estimate=LIGHT,
         compiler_params=ROOM,
-    )(*arrived)
-
-
-def close_kernel(keep, came, *refs):
-    along, (off_diag, diag_block) = refs[:-2], refs[-2:]
+    )(*arrived, along)
+
+
+def close_kernel(keep, came, total, off_diag, diag_block):
     off_diag[...] = keep[...] + came[...]
-    total = along[0][...]
-    for piece in along[1:]:
-        total = total + piece[...]
-    diag_block[...] = total
-
-
-def close(keep, came, along):
+    diag_block[...] = total[...]
+
+
+def close(keep, came, total):
     return pl.pallas_call(
         close_kernel,
-        out_shape=[jax.ShapeDtypeStruct(x.shape, jnp.float32) for x in (keep, along[0])],
-        in_specs=[WHOLE] * (2 + len(along)),
+        out_shape=[jax.ShapeDtypeStruct(x.shape, jnp.float32) for x in (keep, total)],
+        in_specs=[WHOLE] * 3,
         out_specs=[WHOLE, WHOLE],
         cost_estimate=LIGHT,
         compiler_params=ROOM,
-    )(keep, came, *along)
-
-
-def pick_kernel(masked, swapped, held):
+    )(keep, came, total)
+
+
+def pick_kernel(presence, blocks, swapped, held):
     same = (lax.axis_index("row") & 1) == (lax.axis_index("col") & 1)
-    for b in range(held.shape[0]):
-        held[b] = jnp.where(same, masked[b], swapped[b])
-
-
-def pair_rows(masked, swap):
+    block_cols, rows, order = held.shape
+    for b in range(block_cols):
+        for a in range(rows // order):
+            here = pl.ds(a * order, order)
+            block = masked_block(presence, blocks, block_cols, a, b)
+            held[b, here, :] = jnp.where(same, block, swapped[b, here, :])
+
+
+def pick(presence, blocks, swapped):
+    rows, order = swapped.shape[1:]
+    return pl.pallas_call(
+        pick_kernel,
+        out_shape=jax.ShapeDtypeStruct((blocks.shape[0] // rows, rows, order), jnp.float32),
+        in_specs=[pl.BlockSpec(memory_space=pltpu.SMEM), WHOLE, WHOLE],
+        out_specs=WHOLE,
+        cost_estimate=LIGHT,
+        compiler_params=ROOM,
+    )(presence, blocks, swapped)
+
+
+def crossed(swap):
     groups_row = lax.axis_size("row")
     groups_col = lax.axis_size("col")
     cross = [
@@ -281,19 +287,12 @@
         for r in range(groups_row)
         for c in range(groups_col)
     ]
-    swapped = lax.ppermute(swap, ("row", "col"), cross)
-    held = pl.pallas_call(
-        pick_kernel,
-        out_shape=jax.ShapeDtypeStruct(masked.shape, jnp.float32),
-        in_specs=[WHOLE, WHOLE],
-        out_specs=WHOLE,
-        cost_estimate=LIGHT,
-        compiler_params=ROOM,
-    )(masked, swapped)
-    ours = [flipped(held, "col", flip) for flip in range(2, groups_col, 2)]
-    theirs = [flipped(piece, "col", 1) for piece in ours]
-    mates = [flipped(masked, "col", 1), flipped(swapped, "col", 1)]
-    return [masked, mates[0], swapped, mates[1]] + ours + theirs
+    return lax.ppermute(swap, ("row", "col"), cross)
+
+
+def pair_rows(held):
+    held = [held] + [flipped(held, "col", flip) for flip in range(2, lax.axis_size("col"), 2)]
+    return held + [flipped(piece, "col", 1) for piece in held]
 
 
 def along_line(mine, own):
@@ -318,23 +317,25 @@
 
     own = factor.reshape(rows, width)
     blocks = inverse_set.reshape(rows * block_cols, order)
+    marks = presence.reshape(-1)
     tall = width // groups_row
-    masked, swap, mine = prepare(presence.reshape(-1), blocks, own, span, tall)
+    swap, mine = prepare(marks, blocks, own, span, tall)
+    swapped = crossed(swap)
     stay = stay_half(own, tall)
     columns = along_line(mine, own).reshape(-1, block_rows, order, span).transpose(1, 0, 2, 3)
     columns = columns.reshape(-1, order, span)
-    pieces = pair_rows(masked, swap)
+    pieces = pair_rows(pick(marks, blocks, swapped))
+    mate_swapped = flipped(swapped, "col", 1)
 
     both, outward = partials(pieces, columns, groups_col)
     got = flipped(both, "row", 1)
     arrived = [outward[0]] + [flipped(outward[f], "col", f) for f in range(1, groups_col)]
-    keep, send = collect(arrived)
+    flips = (0,) + tuple(range(groups_row - 2, 0, -2))
+    along = finish(both, got, stay, swapped, mate_swapped, dinv, flips)
+    keep, send = collect(arrived, along[0])
     came = flipped(send, "row", 1)
-
-    flips = (0,) + tuple(range(groups_row - 2, 0, -2))
-    along = finish(both, got, stay, pieces[2], pieces[3], dinv, flips)
     met = [flipped(piece, "row", flip) if flip else piece for flip, piece in zip(flips, along)]
-    off_diag, diag_block = close(keep, came, met)
+    off_diag, diag_block = close(keep, came, sum(met[1:], met[0]))
     return (off_diag.reshape(block_rows, 1, share, width), diag_block)
 
 

time: 36 us -> 33.3 us (0.925)
  waiting for transfers between devices: 11.8 us -> 9.15 us
  starting transfers between devices: 18 us -> 19.3 us
  Pallas kernels: 5.24 us -> 3.97 us
    ppermute x14, waiting for transfers between devices: 10.2 us -> 7.55 us  [flipped(): lax.ppermute(value, axis, [(i, i ^ flip) for i in range(lax.axis_size(axi...]
    pallas_call x2, Pallas kernels: 2.22 us -> 0.95 us  [the longest x1 0.56 us: pick(): pl.pallas_call(pick_kernel, out_shape=jax.ShapeDtypeStruct((blocks.shape[...]
    ppermute x14, starting transfers between devices: 15.6 us -> 16.9 us  [flipped(): lax.ppermute(value, axis, [(i, i ^ flip) for i in range(lax.axis_size(axi...]
  transfers between devices with their start and end apart: 15 -> 15, of which waited for: 7 -> 6; matrix products, arithmetic and copies ran while one was open for 0% -> 0% of each run, Pallas kernels for 4% -> 4%
where the time goes in v19:
time: 33.3 us; the launch traced here: 33.1 us
  starting transfers between devices  19.3 us (58%)
  waiting for transfers between devices  9.15 us (27%)
  Pallas kernels  3.97 us (12%)
  between operations  0.73 us (2%)
    ppermute x14, starting transfers between devices, flipped(): lax.ppermute(value, axis, [(i, i ^ flip) for i in range(lax.axis_size(axi...  16.9 us
    ppermute x14, waiting for transfers between devices, flipped(): lax.ppermute(value, axis, [(i, i ^ flip) for i in range(lax.axis_size(axi...  7.55 us
    ppermute x1, starting transfers between devices, crossed(): return lax.ppermute(swap, ('row', 'col'), cross)  2.38 us
    pallas_call x1, Pallas kernels, prepare(): pl.pallas_call(functools.partial(prepare_kernel, tall), out_shape=(jax.Sh...  1.85 us
    ppermute x1, waiting for transfers between devices, crossed(): return lax.ppermute(swap, ('row', 'col'), cross)  1.6 us
  transfers between devices with their start and end apart: 15, of which 6 were waited for; matrix products, arithmetic and copies ran while one was open for 0% of the time, Pallas kernels for 4%

profile of v19, /device:TPU:0, one launch (start us, length us, event | category | flops | bytes accessed | tf_op | source)
XLA Modules:
  0.0 33.1 jit_solution(5572517920152010272)
XLA Ops:
  0.6 1.8 %shard_map.59 = (f32[2,128,128]{2,1,0:T(8,128)}, f32[128,128]{1,0:T(8,128)}) custom-call(s32[2]{0:T(128)} %bitcast.13, f32[256,128]{1,0:T(8,128)} %bitcast.10, f32[128,512]{1,0:T(8,128)} %bitcast.7), custom_call_target="tpu_custom_call" | custom-call | flops 1000 | bytes 1000 | tf_op jit(solution)/shard_map/pallas_call | solution.py:88
  2.5 2.4 %collective-permute-start = (f32[2,128,128]{2,1,0:T(8,128)}, f32[2,128,128]{2,1,0:T(8,128)S(1)}, u32[]{:S(2)}, u32[]{:S(2)}) collective-permute-start(f32[2,128,128]{2,1,0:T(8,128)} %get-tuple-element.17), channel_id=1, source_target_pairs={{0,5},{1,4},{2,7},{3,6},{4,1},{5,0},{6,3},{7,2},{8,13},{9,12},{10,... | collective-permute-start | bytes 393224 | tf_op jit(solution)/shard_map/ppermute | solution.py:290
  4.9 2.6 %collective-permute-start.4 = (f32[1,128,128]{2,1,0:T(8,128)}, f32[1,128,128]{2,1,0:T(8,128)S(1)}, u32[]{:S(2)}, u32[]{:S(2)}) collective-permute-start(f32[1,128,128]{2,1,0:T(8,128)} %bitcast.17), channel_id=1, source_target_pairs={{0,16},{4,20},{8,24},{12,28},{16,0},{20,4},{24,8},{28,12},{1,17},{... | collective-permute-start | bytes 196616 | tf_op jit(solution)/shard_map/ppermute | solution.py:18
  7.5 1.6 %collective-permute-done.swapped = f32[2,128,128]{2,1,0:T(8,128)S(1)} collective-permute-done((f32[2,128,128]{2,1,0:T(8,128)}, f32[2,128,128]{2,1,0:T(8,128)S(1)}, u32[]{:S(2)}, u32[]{:S(2)}) %collective-permute-start) | collective-permute-done | bytes 131104 | tf_op jit(solution)/shard_map/ppermute | solution.py:290
  9.1 0.6 %shard_map.60.refs_0_ = f32[2,128,128]{2,1,0:T(8,128)S(1)} custom-call(s32[2]{0:T(128)S(1)} %bitcast.14, f32[256,128]{1,0:T(8,128)S(1)} %bitcast.11, f32[2,128,128]{2,1,0:T(8,128)S(1)} %collective-permute-done.swapped), custom_call_target="tpu_custom_call" | custom-call | flops 1000 | bytes 1000 | tf_op jit(solution)/shard_map/pallas_call | solution.py:272
  9.6 2.4 %collective-permute-start.1 = (f32[2,128,128]{2,1,0:T(8,128)S(1)}, f32[2,128,128]{2,1,0:T(8,128)S(1)}, u32[]{:S(2)}, u32[]{:S(2)}) collective-permute-start(f32[2,128,128]{2,1,0:T(8,128)S(1)} %shard_map.60.refs_0_), channel_id=1, source_target_pairs={{0,2},{1,3},{2,0},{3,1},{4,6},{5,7},{6,4},{7,5},{8,10},{9,11},{10,... | collective-permute-start | bytes 393224 | tf_op jit(solution)/shard_map/ppermute | solution.py:18
  12.1 0.0 collective-permute-done.4.second
  12.1 1.6 %collective-permute-start.5 = (f32[2,128,128]{2,1,0:T(8,128)S(1)}, f32[2,128,128]{2,1,0:T(8,128)S(1)}, u32[]{:S(2)}, u32[]{:S(2)}) collective-permute-start(f32[2,128,128]{2,1,0:T(8,128)S(1)} %bitcast.15), channel_id=1, source_target_pairs={{0,8},{4,12},{8,0},{12,4},{16,24},{20,28},{24,16},{28,20},{1,9},{5... | collective-permute-start | bytes 393224 | tf_op jit(solution)/shard_map/ppermute | solution.py:18
  13.7 2.1 %collective-permute-done.1.refs_1_ = f32[2,128,128]{2,1,0:T(8,128)S(1)} collective-permute-done((f32[2,128,128]{2,1,0:T(8,128)S(1)}, f32[2,128,128]{2,1,0:T(8,128)S(1)}, u32[]{:S(2)}, u32[]{:S(2)}) %collective-permute-start.1) | collective-permute-done | bytes 131104 | tf_op jit(solution)/shard_map/ppermute | solution.py:18
  15.9 0.5 %collective-permute-start.10 = (f32[2,128,128]{2,1,0:T(8,128)S(1)}, f32[2,128,128]{2,1,0:T(8,128)S(1)}, u32[]{:S(2)}, u32[]{:S(2)}) collective-permute-start(f32[2,128,128]{2,1,0:T(8,128)S(1)} %collective-permute-done.swapped), channel_id=1, source_target_pairs={{0,1},{1,0},{2,3},{3,2},{4,5},{5,4},{6,7},{7,6},{8,9},{9,8},{10,11... | collective-permute-start | bytes 393224 | tf_op jit(solution)/shard_map/ppermute | solution.py:18
  16.4 1.0 %collective-permute-done.5.second = f32[2,128,128]{2,1,0:T(8,128)S(1)} collective-permute-done((f32[2,128,128]{2,1,0:T(8,128)S(1)}, f32[2,128,128]{2,1,0:T(8,128)S(1)}, u32[]{:S(2)}, u32[]{:S(2)}) %collective-permute-start.5) | collective-permute-done | bytes 131104 | tf_op jit(solution)/shard_map/ppermute | solution.py:18
  17.5 0.4 %shard_map.63 = (f32[256,128]{1,0:T(8,128)S(1)}, f32[64,128]{1,0:T(8,128)S(1)}, f32[64,128]{1,0:T(8,128)S(1)}, f32[64,128]{1,0:T(8,128)S(1)}, f32[64,128]{1,0:T(8,128)S(1)}) custom-call(f32[2,128,128]{2,1,0:T(8,128)S(1)} %shard_map.60.refs_0_, f32[2,128,128]{2,1,0:T(8,128)S(1)} %collective-permute-done.1.refs_1_, ...), custom_call_target="tpu_custom_call" | custom-call | flops 1000 | bytes 1000 | tf_op jit(solution)/shard_map/pallas_call | solution.py:149
  17.9 1.6 %collective-permute-start.9 = (f32[256,128]{1,0:T(8,128)S(1)}, f32[256,128]{1,0:T(8,128)S(1)}, u32[]{:S(2)}, u32[]{:S(2)}) collective-permute-start(f32[256,128]{1,0:T(8,128)S(1)} %get-tuple-element.23.both), channel_id=1, source_target_pairs={{0,4},{4,0},{8,12},{12,8},{16,20},{20,16},{24,28},{28,24},{1,5},{5... | collective-permute-start | bytes 393224 | tf_op jit(solution)/shard_map/ppermute | solution.py:18
  19.5 0.1 shard_map.64.stay
  19.6 1.5 %collective-permute-start.7 = (f32[64,128]{1,0:T(8,128)S(1)}, f32[64,128]{1,0:T(8,128)S(1)}, u32[]{:S(2)}, u32[]{:S(2)}) collective-permute-start(f32[64,128]{1,0:T(8,128)S(1)} %get-tuple-element.21), channel_id=1, source_target_pairs={{0,2},{1,3},{2,0},{3,1},{4,6},{5,7},{6,4},{7,5},{8,10},{9,11},{10,... | collective-permute-start | bytes 98312 | tf_op jit(solution)/shard_map/ppermute | solution.py:18
  21.1 0.4 %collective-permute-start.8 = (f32[64,128]{1,0:T(8,128)S(1)}, f32[64,128]{1,0:T(8,128)S(1)}, u32[]{:S(2)}, u32[]{:S(2)}) collective-permute-start(f32[64,128]{1,0:T(8,128)S(1)} %get-tuple-element.22), channel_id=1, source_target_pairs={{0,3},{1,2},{2,1},{3,0},{4,7},{5,6},{6,5},{7,4},{8,11},{9,10},{10,... | collective-permute-start | bytes 98312 | tf_op jit(solution)/shard_map/ppermute | solution.py:18
  21.5 1.7 %collective-permute-done.9.got = f32[256,128]{1,0:T(8,128)S(1)} collective-permute-done((f32[256,128]{1,0:T(8,128)S(1)}, f32[256,128]{1,0:T(8,128)S(1)}, u32[]{:S(2)}, u32[]{:S(2)}) %collective-permute-start.9) | collective-permute-done | bytes 131104 | tf_op jit(solution)/shard_map/ppermute | solution.py:18
  23.3 0.3 %shard_map.65 = (f32[64,128]{1,0:T(8,128)S(1)}, f32[64,128]{1,0:T(8,128)S(1)}, f32[64,128]{1,0:T(8,128)S(1)}, f32[64,128]{1,0:T(8,128)S(1)}) custom-call(f32[256,128]{1,0:T(8,128)S(1)} %get-tuple-element.23.both, f32[256,128]{1,0:T(8,128)S(1)} %collective-permute-done.9.got, f32[128,256]{1,0:T(8,128)S(1)} %shard_map.64.stay, ...), custom_call_target="tpu_custom_call" | custom-call | flops 1000 | bytes 1000 | tf_op jit(solution)/shard_map/pallas_call | solution.py:199
  23.6 3.9 %collective-permute-start.12 = (f32[64,128]{1,0:T(8,128)S(1)}, f32[64,128]{1,0:T(8,128)S(1)}, u32[]{:S(2)}, u32[]{:S(2)}) collective-permute-start(f32[64,128]{1,0:T(8,128)S(1)} %get-tuple-element.27), channel_id=1, source_target_pairs={{0,24},{4,28},{8,16},{12,20},{16,8},{20,12},{24,0},{28,4},{1,25},{... | collective-permute-start | bytes 98312 | tf_op jit(solution)/shard_map/ppermute | solution.py:18
  27.5 0.6 %collective-permute-start.14 = (f32[64,128]{1,0:T(8,128)S(1)}, f32[64,128]{1,0:T(8,128)S(1)}, u32[]{:S(2)}, u32[]{:S(2)}) collective-permute-start(f32[64,128]{1,0:T(8,128)S(1)} %get-tuple-element.29), channel_id=1, source_target_pairs={{0,8},{4,12},{8,0},{12,4},{16,24},{20,28},{24,16},{28,20},{1,9},{5... | collective-permute-start | bytes 98312 | tf_op jit(solution)/shard_map/ppermute | solution.py:18
  28.2 1.7 %collective-permute-start.11 = (f32[32,512]{1,0:T(8,128)S(1)}, f32[32,512]{1,0:T(8,128)S(1)}, u32[]{:S(2)}, u32[]{:S(2)}) collective-permute-start(f32[32,512]{1,0:T(8,128)S(1)} %get-tuple-element.26), channel_id=1, source_target_pairs={{0,4},{4,0},{8,12},{12,8},{16,20},{20,16},{24,28},{28,24},{1,5},{5... | collective-permute-start | bytes 196616 | tf_op jit(solution)/shard_map/ppermute | solution.py:18
  29.9 2.4 %collective-permute-done.13 = f32[64,128]{1,0:T(8,128)S(1)} collective-permute-done((f32[64,128]{1,0:T(8,128)S(1)}, f32[64,128]{1,0:T(8,128)S(1)}, u32[]{:S(2)}, u32[]{:S(2)}) %collective-permute-start.13) | collective-permute-done | bytes 32800 | tf_op jit(solution)/shard_map/ppermute | solution.py:18
  32.3 0.2 collective-permute-done.11.came
  32.5 0.6 %shard_map.67 = (f32[32,512]{1,0:T(8,128)}, f32[64,128]{1,0:T(8,128)}) custom-call(f32[32,512]{1,0:T(8,128)S(1)} %get-tuple-element.25.keep, f32[32,512]{1,0:T(8,128)S(1)} %collective-permute-done.11.came, f32[64,128]{1,0:T(8,128)S(1)} %add_add_fusion.total), custom_call_target="tpu_custom_call" | custom-call | flops 1000 | bytes 1000 | tf_op jit(solution)/shard_map/pallas_call | solution.py:250
  (24 shorter events, 0.1 us)
Async XLA Ops:
  0.6 8.4 %copy-start.1 = (f32[1,1,128,2,1,128]{5,4,3,2,1,0:T(1,128)S(1)}, f32[1,1,128,2,1,128]{5,4,3,2,1,0:T(1,128)}, u32[]{:S(2)}) copy-start(f32[1,1,128,2,1,128]{5,4,3,2,1,0:T(1,128)} %param.4) | copy-start | bytes 393220
  0.6 8.4 %copy-start.3 = (s32[1,1,2,1]{2,3,1,0:T(1,128)S(1)}, s32[1,1,2,1]{2,3,1,0:T(1,128)}, u32[]{:S(2)}) copy-start(s32[1,1,2,1]{2,3,1,0:T(1,128)} %param.5) | copy-start | bytes 28
  2.5 9.6 %copy-start = (f32[1,1,128,512]{3,2,1,0:T(8,128)S(1)}, f32[1,1,128,512]{3,2,1,0:T(8,128)}, u32[]{:S(2)}) copy-start(f32[1,1,128,512]{3,2,1,0:T(8,128)} %param.6) | copy-start | bytes 786436
  2.5 6.6 %collective-permute-start = (f32[2,128,128]{2,1,0:T(8,128)}, f32[2,128,128]{2,1,0:T(8,128)S(1)}, u32[]{:S(2)}, u32[]{:S(2)}) collective-permute-start(f32[2,128,128]{2,1,0:T(8,128)} %get-tuple-element.17), channel_id=1, source_target_pairs={{0,5},{1,4},{2,7},{3,6},{4,1},{5,0},{6,3},{7,2},{8,13},{9,12},{10,... | collective-permute-start | bytes 393224 | tf_op jit(solution)/shard_map/ppermute | solution.py:290
  4.9 7.2 %collective-permute-start.4 = (f32[1,128,128]{2,1,0:T(8,128)}, f32[1,128,128]{2,1,0:T(8,128)S(1)}, u32[]{:S(2)}, u32[]{:S(2)}) collective-permute-start(f32[1,128,128]{2,1,0:T(8,128)} %bitcast.17), channel_id=1, source_target_pairs={{0,16},{4,20},{8,24},{12,28},{16,0},{20,4},{24,8},{28,12},{1,17},{... | collective-permute-start | bytes 196616 | tf_op jit(solution)/shard_map/ppermute | solution.py:18
  9.6 6.2 %collective-permute-start.1 = (f32[2,128,128]{2,1,0:T(8,128)S(1)}, f32[2,128,128]{2,1,0:T(8,128)S(1)}, u32[]{:S(2)}, u32[]{:S(2)}) collective-permute-start(f32[2,128,128]{2,1,0:T(8,128)S(1)} %shard_map.60.refs_0_), channel_id=1, source_target_pairs={{0,2},{1,3},{2,0},{3,1},{4,6},{5,7},{6,4},{7,5},{8,10},{9,11},{10,... | collective-permute-start | bytes 393224 | tf_op jit(solution)/shard_map/ppermute | solution.py:18
  12.1 5.3 %collective-permute-start.5 = (f32[2,128,128]{2,1,0:T(8,128)S(1)}, f32[2,128,128]{2,1,0:T(8,128)S(1)}, u32[]{:S(2)}, u32[]{:S(2)}) collective-permute-start(f32[2,128,128]{2,1,0:T(8,128)S(1)} %bitcast.15), channel_id=1, source_target_pairs={{0,8},{4,12},{8,0},{12,4},{16,24},{20,28},{24,16},{28,20},{1,9},{5... | collective-permute-start | bytes 393224 | tf_op jit(solution)/shard_map/ppermute | solution.py:18
  13.7 3.7 %collective-permute-start.2 = (f32[2,128,128]{2,1,0:T(8,128)S(1)}, f32[2,128,128]{2,1,0:T(8,128)S(1)}, u32[]{:S(2)}, u32[]{:S(2)}) collective-permute-start(f32[2,128,128]{2,1,0:T(8,128)S(1)} %shard_map.60.refs_0_), channel_id=1, source_target_pairs={{0,1},{1,0},{2,3},{3,2},{4,5},{5,4},{6,7},{7,6},{8,9},{9,8},{10,11... | collective-permute-start | bytes 393224 | tf_op jit(solution)/shard_map/ppermute | solution.py:18
  15.9 1.6 %collective-permute-start.3 = (f32[2,128,128]{2,1,0:T(8,128)S(1)}, f32[2,128,128]{2,1,0:T(8,128)S(1)}, u32[]{:S(2)}, u32[]{:S(2)}) collective-permute-start(f32[2,128,128]{2,1,0:T(8,128)S(1)} %collective-permute-done.1.refs_1_), channel_id=1, source_target_pairs={{0,1},{1,0},{2,3},{3,2},{4,5},{5,4},{6,7},{7,6},{8,9},{9,8},{10,11... | collective-permute-start | bytes 393224 | tf_op jit(solution)/shard_map/ppermute | solution.py:18
  15.9 5.6 %collective-permute-start.10 = (f32[2,128,128]{2,1,0:T(8,128)S(1)}, f32[2,128,128]{2,1,0:T(8,128)S(1)}, u32[]{:S(2)}, u32[]{:S(2)}) collective-permute-start(f32[2,128,128]{2,1,0:T(8,128)S(1)} %collective-permute-done.swapped), channel_id=1, source_target_pairs={{0,1},{1,0},{2,3},{3,2},{4,5},{5,4},{6,7},{7,6},{8,9},{9,8},{10,11... | collective-permute-start | bytes 393224 | tf_op jit(solution)/shard_map/ppermute | solution.py:18
  17.9 5.3 %collective-permute-start.9 = (f32[256,128]{1,0:T(8,128)S(1)}, f32[256,128]{1,0:T(8,128)S(1)}, u32[]{:S(2)}, u32[]{:S(2)}) collective-permute-start(f32[256,128]{1,0:T(8,128)S(1)} %get-tuple-element.23.both), channel_id=1, source_target_pairs={{0,4},{4,0},{8,12},{12,8},{16,20},{20,16},{24,28},{28,24},{1,5},{5... | collective-permute-start | bytes 393224 | tf_op jit(solution)/shard_map/ppermute | solution.py:18
  19.5 3.8 %copy-start.2 = (f32[64,128]{1,0:T(8,128)S(1)}, f32[64,128]{1,0:T(8,128)}, u32[]{:S(2)}) copy-start(f32[64,128]{1,0:T(8,128)} %dinv.1) | copy-start | bytes 98308
  19.5 8.0 %collective-permute-start.6 = (f32[64,128]{1,0:T(8,128)S(1)}, f32[64,128]{1,0:T(8,128)S(1)}, u32[]{:S(2)}, u32[]{:S(2)}) collective-permute-start(f32[64,128]{1,0:T(8,128)S(1)} %get-tuple-element.20), channel_id=1, source_target_pairs={{0,1},{1,0},{2,3},{3,2},{4,5},{5,4},{6,7},{7,6},{8,9},{9,8},{10,11... | collective-permute-start | bytes 98312 | tf_op jit(solution)/shard_map/ppermute | solution.py:18
  19.6 8.5 %collective-permute-start.7 = (f32[64,128]{1,0:T(8,128)S(1)}, f32[64,128]{1,0:T(8,128)S(1)}, u32[]{:S(2)}, u32[]{:S(2)}) collective-permute-start(f32[64,128]{1,0:T(8,128)S(1)} %get-tuple-element.21), channel_id=1, source_target_pairs={{0,2},{1,3},{2,0},{3,1},{4,6},{5,7},{6,4},{7,5},{8,10},{9,11},{10,... | collective-permute-start | bytes 98312 | tf_op jit(solution)/shard_map/ppermute | solution.py:18
  21.1 7.0 %collective-permute-start.8 = (f32[64,128]{1,0:T(8,128)S(1)}, f32[64,128]{1,0:T(8,128)S(1)}, u32[]{:S(2)}, u32[]{:S(2)}) collective-permute-start(f32[64,128]{1,0:T(8,128)S(1)} %get-tuple-element.22), channel_id=1, source_target_pairs={{0,3},{1,2},{2,1},{3,0},{4,7},{5,6},{6,5},{7,4},{8,11},{9,10},{10,... | collective-permute-start | bytes 98312 | tf_op jit(solution)/shard_map/ppermute | solution.py:18
  23.6 6.3 %collective-permute-start.12 = (f32[64,128]{1,0:T(8,128)S(1)}, f32[64,128]{1,0:T(8,128)S(1)}, u32[]{:S(2)}, u32[]{:S(2)}) collective-permute-start(f32[64,128]{1,0:T(8,128)S(1)} %get-tuple-element.27), channel_id=1, source_target_pairs={{0,24},{4,28},{8,16},{12,20},{16,8},{20,12},{24,0},{28,4},{1,25},{... | collective-permute-start | bytes 98312 | tf_op jit(solution)/shard_map/ppermute | solution.py:18
  27.5 4.8 %collective-permute-start.13 = (f32[64,128]{1,0:T(8,128)S(1)}, f32[64,128]{1,0:T(8,128)S(1)}, u32[]{:S(2)}, u32[]{:S(2)}) collective-permute-start(f32[64,128]{1,0:T(8,128)S(1)} %get-tuple-element.28), channel_id=1, source_target_pairs={{0,16},{4,20},{8,24},{12,28},{16,0},{20,4},{24,8},{28,12},{1,17},{... | collective-permute-start | bytes 98312 | tf_op jit(solution)/shard_map/ppermute | solution.py:18
  27.5 4.8 %collective-permute-start.14 = (f32[64,128]{1,0:T(8,128)S(1)}, f32[64,128]{1,0:T(8,128)S(1)}, u32[]{:S(2)}, u32[]{:S(2)}) collective-permute-start(f32[64,128]{1,0:T(8,128)S(1)} %get-tuple-element.29), channel_id=1, source_target_pairs={{0,8},{4,12},{8,0},{12,4},{16,24},{20,28},{24,16},{28,20},{1,9},{5... | collective-permute-start | bytes 98312 | tf_op jit(solution)/shard_map/ppermute | solution.py:18
  28.2 4.3 %collective-permute-start.11 = (f32[32,512]{1,0:T(8,128)S(1)}, f32[32,512]{1,0:T(8,128)S(1)}, u32[]{:S(2)}, u32[]{:S(2)}) collective-permute-start(f32[32,512]{1,0:T(8,128)S(1)} %get-tuple-element.26), channel_id=1, source_target_pairs={{0,4},{4,0},{8,12},{12,8},{16,20},{20,16},{24,28},{28,24},{1,5},{5... | collective-permute-start | bytes 196616 | tf_op jit(solution)/shard_map/ppermute | solution.py:18

commit v20 on v19

--- a/solution.py
+++ b/solution.py
@@ -45,7 +45,8 @@
 
 def masked_block(presence, blocks, block_cols, a, b):
     order = blocks.shape[1]
-    weight = presence[a * block_cols + b].astype(jnp.float32)
+    at = a * block_cols + b
+    weight = presence[:, at : at + 1].astype(jnp.float32)
     return blocks[pl.ds(a * order * block_cols + b, order, stride=block_cols), :] * weight
 
 
@@ -91,7 +92,7 @@
             jax.ShapeDtypeStruct((depth, rows, order), jnp.float32),
             jax.ShapeDtypeStruct((rows, span), jnp.float32),
         ),
-        in_specs=[pl.BlockSpec(memory_space=pltpu.SMEM), WHOLE, WHOLE],
+        in_specs=[WHOLE] * 3,
         out_specs=(WHOLE, WHOLE),
         cost_estimate=LIGHT,
     )(presence, blocks, own)
@@ -241,20 +242,21 @@
     )(*arrived, along)
 
 
-def close_kernel(keep, came, total, off_diag, diag_block):
+def close_kernel(keep, came, *refs):
+    met, (off_diag, diag_block) = refs[:-2], refs[-2:]
     off_diag[...] = keep[...] + came[...]
-    diag_block[...] = total[...]
-
-
-def close(keep, came, total):
+    diag_block[...] = sum([piece[...] for piece in met[1:]], met[0][...])
+
+
+def close(keep, came, met):
     return pl.pallas_call(
         close_kernel,
-        out_shape=[jax.ShapeDtypeStruct(x.shape, jnp.float32) for x in (keep, total)],
-        in_specs=[WHOLE] * 3,
+        out_shape=[jax.ShapeDtypeStruct(x.shape, jnp.float32) for x in (keep, met[0])],
+        in_specs=[WHOLE] * (2 + len(met)),
         out_specs=[WHOLE, WHOLE],
         cost_estimate=LIGHT,
         compiler_params=ROOM,
-    )(keep, came, total)
+    )(keep, came, *met)
 
 
 def pick_kernel(presence, blocks, swapped, held):
@@ -272,7 +274,7 @@
     return pl.pallas_call(
         pick_kernel,
         out_shape=jax.ShapeDtypeStruct((blocks.shape[0] // rows, rows, order), jnp.float32),
-        in_specs=[pl.BlockSpec(memory_space=pltpu.SMEM), WHOLE, WHOLE],
+        in_specs=[WHOLE] * 3,
         out_specs=WHOLE,
         cost_estimate=LIGHT,
         compiler_params=ROOM,
@@ -317,7 +319,7 @@
 
     own = factor.reshape(rows, width)
     blocks = inverse_set.reshape(rows * block_cols, order)
-    marks = presence.reshape(-1)
+    marks = presence.reshape(1, -1)
     tall = width // groups_row
     swap, mine = prepare(marks, blocks, own, span, tall)
     swapped = crossed(swap)
@@ -335,7 +337,7 @@
     keep, send = collect(arrived, along[0])
     came = flipped(send, "row", 1)
     met = [flipped(piece, "row", flip) if flip else piece for flip, piece in zip(flips, along)]
-    off_diag, diag_block = close(keep, came, sum(met[1:], met[0]))
+    off_diag, diag_block = close(keep, came, met)
     return (off_diag.reshape(block_rows, 1, share, width), diag_block)
 
 

time: 33.3 us -> 34.3 us (1.030)
  waiting for transfers between devices: 9.15 us -> 12 us
  starting transfers between devices: 19.3 us -> 17.9 us
  Pallas kernels: 3.97 us -> 3.51 us
    ppermute x14, waiting for transfers between devices: 7.55 us -> 10.4 us  [flipped(): lax.ppermute(value, axis, [(i, i ^ flip) for i in range(lax.axis_size(axi...]
    ppermute x14, starting transfers between devices: 16.9 us -> 15.5 us  [flipped(): lax.ppermute(value, axis, [(i, i ^ flip) for i in range(lax.axis_size(axi...]
    pallas_call x1, Pallas kernels: 0.56 us -> 0.08 us  [pick(): pl.pallas_call(pick_kernel, out_shape=jax.ShapeDtypeStruct((blocks.shape[...]
  transfers between devices with their start and end apart: 15 -> 15, of which waited for: 6 -> 8; matrix products, arithmetic and copies ran while one was open for 0% -> 0% of each run, Pallas kernels for 4% -> 3%
where the time goes in v20:
time: 34.3 us; the launch traced here: 34.1 us
  starting transfers between devices  17.9 us (52%)
  waiting for transfers between devices  12 us (35%)
  Pallas kernels  3.51 us (10%)
  between operations  0.74 us (2%)
    ppermute x14, starting transfers between devices, flipped(): lax.ppermute(value, axis, [(i, i ^ flip) for i in range(lax.axis_size(axi...  15.5 us
    ppermute x14, waiting for transfers between devices, flipped(): lax.ppermute(value, axis, [(i, i ^ flip) for i in range(lax.axis_size(axi...  10.4 us
    ppermute x1, starting transfers between devices, crossed(): return lax.ppermute(swap, ('row', 'col'), cross)  2.38 us
    pallas_call x1, Pallas kernels, prepare(): pl.pallas_call(functools.partial(prepare_kernel, tall), out_shape=(jax.Sh...  1.87 us
    ppermute x1, waiting for transfers between devices, crossed(): return lax.ppermute(swap, ('row', 'col'), cross)  1.6 us
  transfers between devices with their start and end apart: 15, of which 8 were waited for; matrix products, arithmetic and copies ran while one was open for 0% of the time, Pallas kernels for 3%

profile of v20, /device:TPU:0, one launch (start us, length us, event | category | flops | bytes accessed | tf_op | source)
XLA Modules:
  0.0 34.1 jit_solution(7500291721419626771)
XLA Ops:
  0.6 1.9 %shard_map.59 = (f32[2,128,128]{2,1,0:T(8,128)}, f32[128,128]{1,0:T(8,128)}) custom-call(s32[1,2]{1,0:T(1,128)} %bitcast.13, f32[256,128]{1,0:T(8,128)} %bitcast.10, f32[128,512]{1,0:T(8,128)} %bitcast.7), custom_call_target="tpu_custom_call" | custom-call | flops 1000 | bytes 1000 | tf_op jit(solution)/shard_map/pallas_call | solution.py:89
  2.5 2.4 %collective-permute-start = (f32[2,128,128]{2,1,0:T(8,128)}, f32[2,128,128]{2,1,0:T(8,128)S(1)}, u32[]{:S(2)}, u32[]{:S(2)}) collective-permute-start(f32[2,128,128]{2,1,0:T(8,128)} %get-tuple-element.17), channel_id=1, source_target_pairs={{0,5},{1,4},{2,7},{3,6},{4,1},{5,0},{6,3},{7,2},{8,13},{9,12},{10,... | collective-permute-start | bytes 393224 | tf_op jit(solution)/shard_map/ppermute | solution.py:292
  4.9 2.6 %collective-permute-start.4 = (f32[1,128,128]{2,1,0:T(8,128)}, f32[1,128,128]{2,1,0:T(8,128)S(1)}, u32[]{:S(2)}, u32[]{:S(2)}) collective-permute-start(f32[1,128,128]{2,1,0:T(8,128)} %bitcast.17), channel_id=1, source_target_pairs={{0,16},{4,20},{8,24},{12,28},{16,0},{20,4},{24,8},{28,12},{1,17},{... | collective-permute-start | bytes 196616 | tf_op jit(solution)/shard_map/ppermute | solution.py:18
  7.5 1.6 %collective-permute-done.swapped = f32[2,128,128]{2,1,0:T(8,128)S(1)} collective-permute-done((f32[2,128,128]{2,1,0:T(8,128)}, f32[2,128,128]{2,1,0:T(8,128)S(1)}, u32[]{:S(2)}, u32[]{:S(2)}) %collective-permute-start) | collective-permute-done | bytes 131104 | tf_op jit(solution)/shard_map/ppermute | solution.py:292
  9.2 2.4 %collective-permute-start.1 = (f32[2,128,128]{2,1,0:T(8,128)S(1)}, f32[2,128,128]{2,1,0:T(8,128)S(1)}, u32[]{:S(2)}, u32[]{:S(2)}) collective-permute-start(f32[2,128,128]{2,1,0:T(8,128)S(1)} %shard_map.60.refs_0_), channel_id=1, source_target_pairs={{0,2},{1,3},{2,0},{3,1},{4,6},{5,7},{6,4},{7,5},{8,10},{9,11},{10,... | collective-permute-start | bytes 393224 | tf_op jit(solution)/shard_map/ppermute | solution.py:18
  11.6 0.5 %collective-permute-done.4.second = f32[1,128,128]{2,1,0:T(8,128)S(1)} collective-permute-done((f32[1,128,128]{2,1,0:T(8,128)}, f32[1,128,128]{2,1,0:T(8,128)S(1)}, u32[]{:S(2)}, u32[]{:S(2)}) %collective-permute-start.4) | collective-permute-done | bytes 65568 | tf_op jit(solution)/shard_map/ppermute | solution.py:18
  12.1 1.2 %collective-permute-start.5 = (f32[2,128,128]{2,1,0:T(8,128)S(1)}, f32[2,128,128]{2,1,0:T(8,128)S(1)}, u32[]{:S(2)}, u32[]{:S(2)}) collective-permute-start(f32[2,128,128]{2,1,0:T(8,128)S(1)} %bitcast.15), channel_id=1, source_target_pairs={{0,8},{4,12},{8,0},{12,4},{16,24},{20,28},{24,16},{28,20},{1,9},{5... | collective-permute-start | bytes 393224 | tf_op jit(solution)/shard_map/ppermute | solution.py:18
  13.3 2.1 %collective-permute-done.1.refs_1_ = f32[2,128,128]{2,1,0:T(8,128)S(1)} collective-permute-done((f32[2,128,128]{2,1,0:T(8,128)S(1)}, f32[2,128,128]{2,1,0:T(8,128)S(1)}, u32[]{:S(2)}, u32[]{:S(2)}) %collective-permute-start.1) | collective-permute-done | bytes 131104 | tf_op jit(solution)/shard_map/ppermute | solution.py:18
  15.4 0.5 %collective-permute-start.10 = (f32[2,128,128]{2,1,0:T(8,128)S(1)}, f32[2,128,128]{2,1,0:T(8,128)S(1)}, u32[]{:S(2)}, u32[]{:S(2)}) collective-permute-start(f32[2,128,128]{2,1,0:T(8,128)S(1)} %collective-permute-done.swapped), channel_id=1, source_target_pairs={{0,1},{1,0},{2,3},{3,2},{4,5},{5,4},{6,7},{7,6},{8,9},{9,8},{10,11... | collective-permute-start | bytes 393224 | tf_op jit(solution)/shard_map/ppermute | solution.py:18
  15.9 1.2 %collective-permute-done.5.second = f32[2,128,128]{2,1,0:T(8,128)S(1)} collective-permute-done((f32[2,128,128]{2,1,0:T(8,128)S(1)}, f32[2,128,128]{2,1,0:T(8,128)S(1)}, u32[]{:S(2)}, u32[]{:S(2)}) %collective-permute-start.5) | collective-permute-done | bytes 131104 | tf_op jit(solution)/shard_map/ppermute | solution.py:18
  17.2 0.4 %shard_map.63 = (f32[256,128]{1,0:T(8,128)S(1)}, f32[64,128]{1,0:T(8,128)S(1)}, f32[64,128]{1,0:T(8,128)S(1)}, f32[64,128]{1,0:T(8,128)S(1)}, f32[64,128]{1,0:T(8,128)S(1)}) custom-call(f32[2,128,128]{2,1,0:T(8,128)S(1)} %shard_map.60.refs_0_, f32[2,128,128]{2,1,0:T(8,128)S(1)} %collective-permute-done.1.refs_1_, ...), custom_call_target="tpu_custom_call" | custom-call | flops 1000 | bytes 1000 | tf_op jit(solution)/shard_map/pallas_call | solution.py:150
  17.6 1.4 %collective-permute-start.9 = (f32[256,128]{1,0:T(8,128)S(1)}, f32[256,128]{1,0:T(8,128)S(1)}, u32[]{:S(2)}, u32[]{:S(2)}) collective-permute-start(f32[256,128]{1,0:T(8,128)S(1)} %get-tuple-element.23.both), channel_id=1, source_target_pairs={{0,4},{4,0},{8,12},{12,8},{16,20},{20,16},{24,28},{28,24},{1,5},{5... | collective-permute-start | bytes 393224 | tf_op jit(solution)/shard_map/ppermute | solution.py:18
  19.0 1.5 %collective-permute-start.7 = (f32[64,128]{1,0:T(8,128)S(1)}, f32[64,128]{1,0:T(8,128)S(1)}, u32[]{:S(2)}, u32[]{:S(2)}) collective-permute-start(f32[64,128]{1,0:T(8,128)S(1)} %get-tuple-element.21), channel_id=1, source_target_pairs={{0,2},{1,3},{2,0},{3,1},{4,6},{5,7},{6,4},{7,5},{8,10},{9,11},{10,... | collective-permute-start | bytes 98312 | tf_op jit(solution)/shard_map/ppermute | solution.py:18
  20.5 0.4 %collective-permute-start.8 = (f32[64,128]{1,0:T(8,128)S(1)}, f32[64,128]{1,0:T(8,128)S(1)}, u32[]{:S(2)}, u32[]{:S(2)}) collective-permute-start(f32[64,128]{1,0:T(8,128)S(1)} %get-tuple-element.22), channel_id=1, source_target_pairs={{0,3},{1,2},{2,1},{3,0},{4,7},{5,6},{6,5},{7,4},{8,11},{9,10},{10,... | collective-permute-start | bytes 98312 | tf_op jit(solution)/shard_map/ppermute | solution.py:18
  20.9 0.1 shard_map.64.stay
  21.0 1.8 %collective-permute-done.9.got = f32[256,128]{1,0:T(8,128)S(1)} collective-permute-done((f32[256,128]{1,0:T(8,128)S(1)}, f32[256,128]{1,0:T(8,128)S(1)}, u32[]{:S(2)}, u32[]{:S(2)}) %collective-permute-start.9) | collective-permute-done | bytes 131104 | tf_op jit(solution)/shard_map/ppermute | solution.py:18
  22.8 0.3 shard_map.65
  23.2 0.7 %collective-permute-done.8.refs_3_ = f32[64,128]{1,0:T(8,128)S(1)} collective-permute-done((f32[64,128]{1,0:T(8,128)S(1)}, f32[64,128]{1,0:T(8,128)S(1)}, u32[]{:S(2)}, u32[]{:S(2)}) %collective-permute-start.8) | collective-permute-done | bytes 32800 | tf_op jit(solution)/shard_map/ppermute | solution.py:18
  23.8 1.1 %collective-permute-start.11 = (f32[32,512]{1,0:T(8,128)S(1)}, f32[32,512]{1,0:T(8,128)S(1)}, u32[]{:S(2)}, u32[]{:S(2)}) collective-permute-start(f32[32,512]{1,0:T(8,128)S(1)} %get-tuple-element.26), channel_id=1, source_target_pairs={{0,4},{4,0},{8,12},{12,8},{16,20},{20,16},{24,28},{28,24},{1,5},{5... | collective-permute-start | bytes 196616 | tf_op jit(solution)/shard_map/ppermute | solution.py:18
  25.0 3.7 %collective-permute-start.12 = (f32[64,128]{1,0:T(8,128)S(1)}, f32[64,128]{1,0:T(8,128)S(1)}, u32[]{:S(2)}, u32[]{:S(2)}) collective-permute-start(f32[64,128]{1,0:T(8,128)S(1)} %get-tuple-element.27), channel_id=1, source_target_pairs={{0,24},{4,28},{8,16},{12,20},{16,8},{20,12},{24,0},{28,4},{1,25},{... | collective-permute-start | bytes 98312 | tf_op jit(solution)/shard_map/ppermute | solution.py:18
  28.6 0.7 %collective-permute-start.14 = (f32[64,128]{1,0:T(8,128)S(1)}, f32[64,128]{1,0:T(8,128)S(1)}, u32[]{:S(2)}, u32[]{:S(2)}) collective-permute-start(f32[64,128]{1,0:T(8,128)S(1)} %get-tuple-element.29), channel_id=1, source_target_pairs={{0,8},{4,12},{8,0},{12,4},{16,24},{20,28},{24,16},{28,20},{1,9},{5... | collective-permute-start | bytes 98312 | tf_op jit(solution)/shard_map/ppermute | solution.py:18
  29.4 1.4 %collective-permute-done.12.refs_1_ = f32[64,128]{1,0:T(8,128)S(1)} collective-permute-done((f32[64,128]{1,0:T(8,128)S(1)}, f32[64,128]{1,0:T(8,128)S(1)}, u32[]{:S(2)}, u32[]{:S(2)}) %collective-permute-start.12) | collective-permute-done | bytes 32800 | tf_op jit(solution)/shard_map/ppermute | solution.py:18
  30.7 2.7 %collective-permute-done.13.refs_2_ = f32[64,128]{1,0:T(8,128)S(1)} collective-permute-done((f32[64,128]{1,0:T(8,128)S(1)}, f32[64,128]{1,0:T(8,128)S(1)}, u32[]{:S(2)}, u32[]{:S(2)}) %collective-permute-start.13) | collective-permute-done | bytes 32800 | tf_op jit(solution)/shard_map/ppermute | solution.py:18
  33.5 0.7 %shard_map.67 = (f32[32,512]{1,0:T(8,128)}, f32[64,128]{1,0:T(8,128)}) custom-call(f32[32,512]{1,0:T(8,128)S(1)} %get-tuple-element.25.keep, f32[32,512]{1,0:T(8,128)S(1)} %collective-permute-done.11.came, f32[64,128]{1,0:T(8,128)S(1)} %get-tuple-element.24.refs_4_.refs_0_, f32[64,128]{1,0:T(8,128)S(1)} %collective-permute-done.12.refs_1_, ...), custom_call_target="tpu_custom_call" | custom-call | flops 1000 | bytes 1000 | tf_op jit(solution)/shard_map/pallas_call | solution.py:252
  (23 shorter events, 0.2 us)
Async XLA Ops:
  0.6 8.5 %copy-start.1 = (f32[1,1,128,2,1,128]{5,4,3,2,1,0:T(1,128)S(1)}, f32[1,1,128,2,1,128]{5,4,3,2,1,0:T(1,128)}, u32[]{:S(2)}) copy-start(f32[1,1,128,2,1,128]{5,4,3,2,1,0:T(1,128)} %param.4) | copy-start | bytes 393220
  0.6 8.5 %copy-start.3 = (s32[1,1,2,1]{2,3,1,0:T(1,128)S(1)}, s32[1,1,2,1]{2,3,1,0:T(1,128)}, u32[]{:S(2)}) copy-start(s32[1,1,2,1]{2,3,1,0:T(1,128)} %param.5) | copy-start | bytes 28
  2.5 9.6 %copy-start = (f32[1,1,128,512]{3,2,1,0:T(8,128)S(1)}, f32[1,1,128,512]{3,2,1,0:T(8,128)}, u32[]{:S(2)}) copy-start(f32[1,1,128,512]{3,2,1,0:T(8,128)} %param.6) | copy-start | bytes 786436
  2.5 6.6 %collective-permute-start = (f32[2,128,128]{2,1,0:T(8,128)}, f32[2,128,128]{2,1,0:T(8,128)S(1)}, u32[]{:S(2)}, u32[]{:S(2)}) collective-permute-start(f32[2,128,128]{2,1,0:T(8,128)} %get-tuple-element.17), channel_id=1, source_target_pairs={{0,5},{1,4},{2,7},{3,6},{4,1},{5,0},{6,3},{7,2},{8,13},{9,12},{10,... | collective-permute-start | bytes 393224 | tf_op jit(solution)/shard_map/ppermute | solution.py:292
  4.9 7.2 %collective-permute-start.4 = (f32[1,128,128]{2,1,0:T(8,128)}, f32[1,128,128]{2,1,0:T(8,128)S(1)}, u32[]{:S(2)}, u32[]{:S(2)}) collective-permute-start(f32[1,128,128]{2,1,0:T(8,128)} %bitcast.17), channel_id=1, source_target_pairs={{0,16},{4,20},{8,24},{12,28},{16,0},{20,4},{24,8},{28,12},{1,17},{... | collective-permute-start | bytes 196616 | tf_op jit(solution)/shard_map/ppermute | solution.py:18
  9.2 6.2 %collective-permute-start.1 = (f32[2,128,128]{2,1,0:T(8,128)S(1)}, f32[2,128,128]{2,1,0:T(8,128)S(1)}, u32[]{:S(2)}, u32[]{:S(2)}) collective-permute-start(f32[2,128,128]{2,1,0:T(8,128)S(1)} %shard_map.60.refs_0_), channel_id=1, source_target_pairs={{0,2},{1,3},{2,0},{3,1},{4,6},{5,7},{6,4},{7,5},{8,10},{9,11},{10,... | collective-permute-start | bytes 393224 | tf_op jit(solution)/shard_map/ppermute | solution.py:18
  12.1 5.0 %collective-permute-start.5 = (f32[2,128,128]{2,1,0:T(8,128)S(1)}, f32[2,128,128]{2,1,0:T(8,128)S(1)}, u32[]{:S(2)}, u32[]{:S(2)}) collective-permute-start(f32[2,128,128]{2,1,0:T(8,128)S(1)} %bitcast.15), channel_id=1, source_target_pairs={{0,8},{4,12},{8,0},{12,4},{16,24},{20,28},{24,16},{28,20},{1,9},{5... | collective-permute-start | bytes 393224 | tf_op jit(solution)/shard_map/ppermute | solution.py:18
  13.3 3.9 %collective-permute-start.2 = (f32[2,128,128]{2,1,0:T(8,128)S(1)}, f32[2,128,128]{2,1,0:T(8,128)S(1)}, u32[]{:S(2)}, u32[]{:S(2)}) collective-permute-start(f32[2,128,128]{2,1,0:T(8,128)S(1)} %shard_map.60.refs_0_), channel_id=1, source_target_pairs={{0,1},{1,0},{2,3},{3,2},{4,5},{5,4},{6,7},{7,6},{8,9},{9,8},{10,11... | collective-permute-start | bytes 393224 | tf_op jit(solution)/shard_map/ppermute | solution.py:18
  15.4 1.8 %collective-permute-start.3 = (f32[2,128,128]{2,1,0:T(8,128)S(1)}, f32[2,128,128]{2,1,0:T(8,128)S(1)}, u32[]{:S(2)}, u32[]{:S(2)}) collective-permute-start(f32[2,128,128]{2,1,0:T(8,128)S(1)} %collective-permute-done.1.refs_1_), channel_id=1, source_target_pairs={{0,1},{1,0},{2,3},{3,2},{4,5},{5,4},{6,7},{7,6},{8,9},{9,8},{10,11... | collective-permute-start | bytes 393224 | tf_op jit(solution)/shard_map/ppermute | solution.py:18
  15.4 5.6 %collective-permute-start.10 = (f32[2,128,128]{2,1,0:T(8,128)S(1)}, f32[2,128,128]{2,1,0:T(8,128)S(1)}, u32[]{:S(2)}, u32[]{:S(2)}) collective-permute-start(f32[2,128,128]{2,1,0:T(8,128)S(1)} %collective-permute-done.swapped), channel_id=1, source_target_pairs={{0,1},{1,0},{2,3},{3,2},{4,5},{5,4},{6,7},{7,6},{8,9},{9,8},{10,11... | collective-permute-start | bytes 393224 | tf_op jit(solution)/shard_map/ppermute | solution.py:18
  17.6 5.2 %collective-permute-start.9 = (f32[256,128]{1,0:T(8,128)S(1)}, f32[256,128]{1,0:T(8,128)S(1)}, u32[]{:S(2)}, u32[]{:S(2)}) collective-permute-start(f32[256,128]{1,0:T(8,128)S(1)} %get-tuple-element.23.both), channel_id=1, source_target_pairs={{0,4},{4,0},{8,12},{12,8},{16,20},{20,16},{24,28},{28,24},{1,5},{5... | collective-permute-start | bytes 393224 | tf_op jit(solution)/shard_map/ppermute | solution.py:18
  19.0 4.1 %collective-permute-start.6 = (f32[64,128]{1,0:T(8,128)S(1)}, f32[64,128]{1,0:T(8,128)S(1)}, u32[]{:S(2)}, u32[]{:S(2)}) collective-permute-start(f32[64,128]{1,0:T(8,128)S(1)} %get-tuple-element.20), channel_id=1, source_target_pairs={{0,1},{1,0},{2,3},{3,2},{4,5},{5,4},{6,7},{7,6},{8,9},{9,8},{10,11... | collective-permute-start | bytes 98312 | tf_op jit(solution)/shard_map/ppermute | solution.py:18
  19.0 4.1 %collective-permute-start.7 = (f32[64,128]{1,0:T(8,128)S(1)}, f32[64,128]{1,0:T(8,128)S(1)}, u32[]{:S(2)}, u32[]{:S(2)}) collective-permute-start(f32[64,128]{1,0:T(8,128)S(1)} %get-tuple-element.21), channel_id=1, source_target_pairs={{0,2},{1,3},{2,0},{3,1},{4,6},{5,7},{6,4},{7,5},{8,10},{9,11},{10,... | collective-permute-start | bytes 98312 | tf_op jit(solution)/shard_map/ppermute | solution.py:18
  20.5 2.3 %copy-start.2 = (f32[64,128]{1,0:T(8,128)S(1)}, f32[64,128]{1,0:T(8,128)}, u32[]{:S(2)}) copy-start(f32[64,128]{1,0:T(8,128)} %dinv.1) | copy-start | bytes 98308
  20.5 3.3 %collective-permute-start.8 = (f32[64,128]{1,0:T(8,128)S(1)}, f32[64,128]{1,0:T(8,128)S(1)}, u32[]{:S(2)}, u32[]{:S(2)}) collective-permute-start(f32[64,128]{1,0:T(8,128)S(1)} %get-tuple-element.22), channel_id=1, source_target_pairs={{0,3},{1,2},{2,1},{3,0},{4,7},{5,6},{6,5},{7,4},{8,11},{9,10},{10,... | collective-permute-start | bytes 98312 | tf_op jit(solution)/shard_map/ppermute | solution.py:18
  23.8 9.6 %collective-permute-start.11 = (f32[32,512]{1,0:T(8,128)S(1)}, f32[32,512]{1,0:T(8,128)S(1)}, u32[]{:S(2)}, u32[]{:S(2)}) collective-permute-start(f32[32,512]{1,0:T(8,128)S(1)} %get-tuple-element.26), channel_id=1, source_target_pairs={{0,4},{4,0},{8,12},{12,8},{16,20},{20,16},{24,28},{28,24},{1,5},{5... | collective-permute-start | bytes 196616 | tf_op jit(solution)/shard_map/ppermute | solution.py:18
  25.0 5.8 %collective-permute-start.12 = (f32[64,128]{1,0:T(8,128)S(1)}, f32[64,128]{1,0:T(8,128)S(1)}, u32[]{:S(2)}, u32[]{:S(2)}) collective-permute-start(f32[64,128]{1,0:T(8,128)S(1)} %get-tuple-element.27), channel_id=1, source_target_pairs={{0,24},{4,28},{8,16},{12,20},{16,8},{20,12},{24,0},{28,4},{1,25},{... | collective-permute-start | bytes 98312 | tf_op jit(solution)/shard_map/ppermute | solution.py:18
  28.6 4.8 %collective-permute-start.13 = (f32[64,128]{1,0:T(8,128)S(1)}, f32[64,128]{1,0:T(8,128)S(1)}, u32[]{:S(2)}, u32[]{:S(2)}) collective-permute-start(f32[64,128]{1,0:T(8,128)S(1)} %get-tuple-element.28), channel_id=1, source_target_pairs={{0,16},{4,20},{8,24},{12,28},{16,0},{20,4},{24,8},{28,12},{1,17},{... | collective-permute-start | bytes 98312 | tf_op jit(solution)/shard_map/ppermute | solution.py:18
  28.6 4.8 %collective-permute-start.14 = (f32[64,128]{1,0:T(8,128)S(1)}, f32[64,128]{1,0:T(8,128)S(1)}, u32[]{:S(2)}, u32[]{:S(2)}) collective-permute-start(f32[64,128]{1,0:T(8,128)S(1)} %get-tuple-element.29), channel_id=1, source_target_pairs={{0,8},{4,12},{8,0},{12,4},{16,24},{20,28},{24,16},{28,20},{1,9},{5... | collective-permute-start | bytes 98312 | tf_op jit(solution)/shard_map/ppermute | solution.py:18

commit v21 on v19

--- a/solution.py
+++ b/solution.py
@@ -45,7 +45,8 @@
 
 def masked_block(presence, blocks, block_cols, a, b):
     order = blocks.shape[1]
-    weight = presence[a * block_cols + b].astype(jnp.float32)
+    at = a * block_cols + b
+    weight = presence[:, at : at + 1].astype(jnp.float32)
     return blocks[pl.ds(a * order * block_cols + b, order, stride=block_cols), :] * weight
 
 
@@ -91,7 +92,7 @@
             jax.ShapeDtypeStruct((depth, rows, order), jnp.float32),
             jax.ShapeDtypeStruct((rows, span), jnp.float32),
         ),
-        in_specs=[pl.BlockSpec(memory_space=pltpu.SMEM), WHOLE, WHOLE],
+        in_specs=[WHOLE] * 3,
         out_specs=(WHOLE, WHOLE),
         cost_estimate=LIGHT,
     )(presence, blocks, own)
@@ -272,7 +273,7 @@
     return pl.pallas_call(
         pick_kernel,
         out_shape=jax.ShapeDtypeStruct((blocks.shape[0] // rows, rows, order), jnp.float32),
-        in_specs=[pl.BlockSpec(memory_space=pltpu.SMEM), WHOLE, WHOLE],
+        in_specs=[WHOLE] * 3,
         out_specs=WHOLE,
         cost_estimate=LIGHT,
         compiler_params=ROOM,
@@ -317,7 +318,7 @@
 
     own = factor.reshape(rows, width)
     blocks = inverse_set.reshape(rows * block_cols, order)
-    marks = presence.reshape(-1)
+    marks = presence.reshape(1, -1)
     tall = width // groups_row
     swap, mine = prepare(marks, blocks, own, span, tall)
     swapped = crossed(swap)

time: 33.3 us -> 32.8 us (0.985)
  starting transfers between devices: 19.3 us -> 18.6 us
  waiting for transfers between devices: 9.15 us -> 9.8 us
  Pallas kernels: 3.97 us -> 3.51 us
    ppermute x14, waiting for transfers between devices: 7.55 us -> 8.2 us  [flipped(): lax.ppermute(value, axis, [(i, i ^ flip) for i in range(lax.axis_size(axi...]
    ppermute x14, starting transfers between devices: 16.9 us -> 16.3 us  [flipped(): lax.ppermute(value, axis, [(i, i ^ flip) for i in range(lax.axis_size(axi...]
    pallas_call x1, Pallas kernels: 0.56 us -> 0.08 us  [pick(): pl.pallas_call(pick_kernel, out_shape=jax.ShapeDtypeStruct((blocks.shape[...]
  transfers between devices with their start and end apart: 15 -> 15, of which waited for: 6 -> 7; matrix products, arithmetic and copies ran while one was open for 0% -> 0% of each run, Pallas kernels for 4% -> 3%
where the time goes in v21:
time: 32.8 us; the launch traced here: 32.7 us
  starting transfers between devices  18.6 us (57%)
  waiting for transfers between devices  9.8 us (30%)
  Pallas kernels  3.51 us (11%)
  between operations  0.72 us (2%)
    ppermute x14, starting transfers between devices, flipped(): lax.ppermute(value, axis, [(i, i ^ flip) for i in range(lax.axis_size(axi...  16.3 us
    ppermute x14, waiting for transfers between devices, flipped(): lax.ppermute(value, axis, [(i, i ^ flip) for i in range(lax.axis_size(axi...  8.2 us
    ppermute x1, starting transfers between devices, crossed(): return lax.ppermute(swap, ('row', 'col'), cross)  2.38 us
    pallas_call x1, Pallas kernels, prepare(): pl.pallas_call(functools.partial(prepare_kernel, tall), out_shape=(jax.Sh...  1.87 us
    ppermute x1, waiting for transfers between devices, crossed(): return lax.ppermute(swap, ('row', 'col'), cross)  1.6 us
  transfers between devices with their start and end apart: 15, of which 7 were waited for; matrix products, arithmetic and copies ran while one was open for 0% of the time, Pallas kernels for 3%

profile of v21, /device:TPU:0, one launch (start us, length us, event | category | flops | bytes accessed | tf_op | source)
XLA Modules:
  0.0 32.7 jit_solution(5013706775367623886)
XLA Ops:
  0.6 1.9 %shard_map.59 = (f32[2,128,128]{2,1,0:T(8,128)}, f32[128,128]{1,0:T(8,128)}) custom-call(s32[1,2]{1,0:T(1,128)} %bitcast.13, f32[256,128]{1,0:T(8,128)} %bitcast.10, f32[128,512]{1,0:T(8,128)} %bitcast.7), custom_call_target="tpu_custom_call" | custom-call | flops 1000 | bytes 1000 | tf_op jit(solution)/shard_map/pallas_call | solution.py:89
  2.5 2.4 %collective-permute-start = (f32[2,128,128]{2,1,0:T(8,128)}, f32[2,128,128]{2,1,0:T(8,128)S(1)}, u32[]{:S(2)}, u32[]{:S(2)}) collective-permute-start(f32[2,128,128]{2,1,0:T(8,128)} %get-tuple-element.17), channel_id=1, source_target_pairs={{0,5},{1,4},{2,7},{3,6},{4,1},{5,0},{6,3},{7,2},{8,13},{9,12},{10,... | collective-permute-start | bytes 393224 | tf_op jit(solution)/shard_map/ppermute | solution.py:291
  4.9 2.6 %collective-permute-start.4 = (f32[1,128,128]{2,1,0:T(8,128)}, f32[1,128,128]{2,1,0:T(8,128)S(1)}, u32[]{:S(2)}, u32[]{:S(2)}) collective-permute-start(f32[1,128,128]{2,1,0:T(8,128)} %bitcast.17), channel_id=1, source_target_pairs={{0,16},{4,20},{8,24},{12,28},{16,0},{20,4},{24,8},{28,12},{1,17},{... | collective-permute-start | bytes 196616 | tf_op jit(solution)/shard_map/ppermute | solution.py:18
  7.5 1.6 %collective-permute-done.swapped = f32[2,128,128]{2,1,0:T(8,128)S(1)} collective-permute-done((f32[2,128,128]{2,1,0:T(8,128)}, f32[2,128,128]{2,1,0:T(8,128)S(1)}, u32[]{:S(2)}, u32[]{:S(2)}) %collective-permute-start) | collective-permute-done | bytes 131104 | tf_op jit(solution)/shard_map/ppermute | solution.py:291
  9.1 0.1 shard_map.60.refs_0_
  9.2 2.4 %collective-permute-start.1 = (f32[2,128,128]{2,1,0:T(8,128)S(1)}, f32[2,128,128]{2,1,0:T(8,128)S(1)}, u32[]{:S(2)}, u32[]{:S(2)}) collective-permute-start(f32[2,128,128]{2,1,0:T(8,128)S(1)} %shard_map.60.refs_0_), channel_id=1, source_target_pairs={{0,2},{1,3},{2,0},{3,1},{4,6},{5,7},{6,4},{7,5},{8,10},{9,11},{10,... | collective-permute-start | bytes 393224 | tf_op jit(solution)/shard_map/ppermute | solution.py:18
  11.6 0.5 %collective-permute-done.4.second = f32[1,128,128]{2,1,0:T(8,128)S(1)} collective-permute-done((f32[1,128,128]{2,1,0:T(8,128)}, f32[1,128,128]{2,1,0:T(8,128)S(1)}, u32[]{:S(2)}, u32[]{:S(2)}) %collective-permute-start.4) | collective-permute-done | bytes 65568 | tf_op jit(solution)/shard_map/ppermute | solution.py:18
  12.1 1.2 %collective-permute-start.5 = (f32[2,128,128]{2,1,0:T(8,128)S(1)}, f32[2,128,128]{2,1,0:T(8,128)S(1)}, u32[]{:S(2)}, u32[]{:S(2)}) collective-permute-start(f32[2,128,128]{2,1,0:T(8,128)S(1)} %bitcast.15), channel_id=1, source_target_pairs={{0,8},{4,12},{8,0},{12,4},{16,24},{20,28},{24,16},{28,20},{1,9},{5... | collective-permute-start | bytes 393224 | tf_op jit(solution)/shard_map/ppermute | solution.py:18
  13.3 2.1 %collective-permute-done.1.refs_1_ = f32[2,128,128]{2,1,0:T(8,128)S(1)} collective-permute-done((f32[2,128,128]{2,1,0:T(8,128)S(1)}, f32[2,128,128]{2,1,0:T(8,128)S(1)}, u32[]{:S(2)}, u32[]{:S(2)}) %collective-permute-start.1) | collective-permute-done | bytes 131104 | tf_op jit(solution)/shard_map/ppermute | solution.py:18
  15.4 0.5 %collective-permute-start.10 = (f32[2,128,128]{2,1,0:T(8,128)S(1)}, f32[2,128,128]{2,1,0:T(8,128)S(1)}, u32[]{:S(2)}, u32[]{:S(2)}) collective-permute-start(f32[2,128,128]{2,1,0:T(8,128)S(1)} %collective-permute-done.swapped), channel_id=1, source_target_pairs={{0,1},{1,0},{2,3},{3,2},{4,5},{5,4},{6,7},{7,6},{8,9},{9,8},{10,11... | collective-permute-start | bytes 393224 | tf_op jit(solution)/shard_map/ppermute | solution.py:18
  15.9 1.2 %collective-permute-done.5.second = f32[2,128,128]{2,1,0:T(8,128)S(1)} collective-permute-done((f32[2,128,128]{2,1,0:T(8,128)S(1)}, f32[2,128,128]{2,1,0:T(8,128)S(1)}, u32[]{:S(2)}, u32[]{:S(2)}) %collective-permute-start.5) | collective-permute-done | bytes 131104 | tf_op jit(solution)/shard_map/ppermute | solution.py:18
  17.2 0.4 %shard_map.63 = (f32[256,128]{1,0:T(8,128)S(1)}, f32[64,128]{1,0:T(8,128)S(1)}, f32[64,128]{1,0:T(8,128)S(1)}, f32[64,128]{1,0:T(8,128)S(1)}, f32[64,128]{1,0:T(8,128)S(1)}) custom-call(f32[2,128,128]{2,1,0:T(8,128)S(1)} %shard_map.60.refs_0_, f32[2,128,128]{2,1,0:T(8,128)S(1)} %collective-permute-done.1.refs_1_, ...), custom_call_target="tpu_custom_call" | custom-call | flops 1000 | bytes 1000 | tf_op jit(solution)/shard_map/pallas_call | solution.py:150
  17.6 1.4 %collective-permute-start.9 = (f32[256,128]{1,0:T(8,128)S(1)}, f32[256,128]{1,0:T(8,128)S(1)}, u32[]{:S(2)}, u32[]{:S(2)}) collective-permute-start(f32[256,128]{1,0:T(8,128)S(1)} %get-tuple-element.23.both), channel_id=1, source_target_pairs={{0,4},{4,0},{8,12},{12,8},{16,20},{20,16},{24,28},{28,24},{1,5},{5... | collective-permute-start | bytes 393224 | tf_op jit(solution)/shard_map/ppermute | solution.py:18
  19.0 0.1 shard_map.64.stay
  19.1 1.5 %collective-permute-start.7 = (f32[64,128]{1,0:T(8,128)S(1)}, f32[64,128]{1,0:T(8,128)S(1)}, u32[]{:S(2)}, u32[]{:S(2)}) collective-permute-start(f32[64,128]{1,0:T(8,128)S(1)} %get-tuple-element.21), channel_id=1, source_target_pairs={{0,2},{1,3},{2,0},{3,1},{4,6},{5,7},{6,4},{7,5},{8,10},{9,11},{10,... | collective-permute-start | bytes 98312 | tf_op jit(solution)/shard_map/ppermute | solution.py:18
  20.7 0.4 %collective-permute-start.8 = (f32[64,128]{1,0:T(8,128)S(1)}, f32[64,128]{1,0:T(8,128)S(1)}, u32[]{:S(2)}, u32[]{:S(2)}) collective-permute-start(f32[64,128]{1,0:T(8,128)S(1)} %get-tuple-element.22), channel_id=1, source_target_pairs={{0,3},{1,2},{2,1},{3,0},{4,7},{5,6},{6,5},{7,4},{8,11},{9,10},{10,... | collective-permute-start | bytes 98312 | tf_op jit(solution)/shard_map/ppermute | solution.py:18
  21.1 1.7 %collective-permute-done.9.got = f32[256,128]{1,0:T(8,128)S(1)} collective-permute-done((f32[256,128]{1,0:T(8,128)S(1)}, f32[256,128]{1,0:T(8,128)S(1)}, u32[]{:S(2)}, u32[]{:S(2)}) %collective-permute-start.9) | collective-permute-done | bytes 131104 | tf_op jit(solution)/shard_map/ppermute | solution.py:18
  22.8 0.3 %shard_map.65 = (f32[64,128]{1,0:T(8,128)S(1)}, f32[64,128]{1,0:T(8,128)S(1)}, f32[64,128]{1,0:T(8,128)S(1)}, f32[64,128]{1,0:T(8,128)S(1)}) custom-call(f32[256,128]{1,0:T(8,128)S(1)} %get-tuple-element.23.both, f32[256,128]{1,0:T(8,128)S(1)} %collective-permute-done.9.got, f32[128,256]{1,0:T(8,128)S(1)} %shard_map.64.stay, ...), custom_call_target="tpu_custom_call" | custom-call | flops 1000 | bytes 1000 | tf_op jit(solution)/shard_map/pallas_call | solution.py:200
  23.1 3.9 %collective-permute-start.12 = (f32[64,128]{1,0:T(8,128)S(1)}, f32[64,128]{1,0:T(8,128)S(1)}, u32[]{:S(2)}, u32[]{:S(2)}) collective-permute-start(f32[64,128]{1,0:T(8,128)S(1)} %get-tuple-element.27), channel_id=1, source_target_pairs={{0,24},{4,28},{8,16},{12,20},{16,8},{20,12},{24,0},{28,4},{1,25},{... | collective-permute-start | bytes 98312 | tf_op jit(solution)/shard_map/ppermute | solution.py:18
  27.1 0.6 %collective-permute-start.14 = (f32[64,128]{1,0:T(8,128)S(1)}, f32[64,128]{1,0:T(8,128)S(1)}, u32[]{:S(2)}, u32[]{:S(2)}) collective-permute-start(f32[64,128]{1,0:T(8,128)S(1)} %get-tuple-element.29), channel_id=1, source_target_pairs={{0,8},{4,12},{8,0},{12,4},{16,24},{20,28},{24,16},{28,20},{1,9},{5... | collective-permute-start | bytes 98312 | tf_op jit(solution)/shard_map/ppermute | solution.py:18
  27.7 1.7 %collective-permute-start.11 = (f32[32,512]{1,0:T(8,128)S(1)}, f32[32,512]{1,0:T(8,128)S(1)}, u32[]{:S(2)}, u32[]{:S(2)}) collective-permute-start(f32[32,512]{1,0:T(8,128)S(1)} %get-tuple-element.26), channel_id=1, source_target_pairs={{0,4},{4,0},{8,12},{12,8},{16,20},{20,16},{24,28},{28,24},{1,5},{5... | collective-permute-start | bytes 196616 | tf_op jit(solution)/shard_map/ppermute | solution.py:18
  29.4 2.5 %collective-permute-done.13 = f32[64,128]{1,0:T(8,128)S(1)} collective-permute-done((f32[64,128]{1,0:T(8,128)S(1)}, f32[64,128]{1,0:T(8,128)S(1)}, u32[]{:S(2)}, u32[]{:S(2)}) %collective-permute-start.13) | collective-permute-done | bytes 32800 | tf_op jit(solution)/shard_map/ppermute | solution.py:18
  31.9 0.2 collective-permute-done.11.came
  32.1 0.6 %shard_map.67 = (f32[32,512]{1,0:T(8,128)}, f32[64,128]{1,0:T(8,128)}) custom-call(f32[32,512]{1,0:T(8,128)S(1)} %get-tuple-element.25.keep, f32[32,512]{1,0:T(8,128)S(1)} %collective-permute-done.11.came, f32[64,128]{1,0:T(8,128)S(1)} %add_add_fusion.total), custom_call_target="tpu_custom_call" | custom-call | flops 1000 | bytes 1000 | tf_op jit(solution)/shard_map/pallas_call | solution.py:251
  (24 shorter events, 0.1 us)
Async XLA Ops:
  0.6 8.5 %copy-start.1 = (f32[1,1,128,2,1,128]{5,4,3,2,1,0:T(1,128)S(1)}, f32[1,1,128,2,1,128]{5,4,3,2,1,0:T(1,128)}, u32[]{:S(2)}) copy-start(f32[1,1,128,2,1,128]{5,4,3,2,1,0:T(1,128)} %param.4) | copy-start | bytes 393220
  0.6 8.5 %copy-start.3 = (s32[1,1,2,1]{2,3,1,0:T(1,128)S(1)}, s32[1,1,2,1]{2,3,1,0:T(1,128)}, u32[]{:S(2)}) copy-start(s32[1,1,2,1]{2,3,1,0:T(1,128)} %param.5) | copy-start | bytes 28
  2.5 9.6 %copy-start = (f32[1,1,128,512]{3,2,1,0:T(8,128)S(1)}, f32[1,1,128,512]{3,2,1,0:T(8,128)}, u32[]{:S(2)}) copy-start(f32[1,1,128,512]{3,2,1,0:T(8,128)} %param.6) | copy-start | bytes 786436
  2.5 6.6 %collective-permute-start = (f32[2,128,128]{2,1,0:T(8,128)}, f32[2,128,128]{2,1,0:T(8,128)S(1)}, u32[]{:S(2)}, u32[]{:S(2)}) collective-permute-start(f32[2,128,128]{2,1,0:T(8,128)} %get-tuple-element.17), channel_id=1, source_target_pairs={{0,5},{1,4},{2,7},{3,6},{4,1},{5,0},{6,3},{7,2},{8,13},{9,12},{10,... | collective-permute-start | bytes 393224 | tf_op jit(solution)/shard_map/ppermute | solution.py:291
  4.9 7.2 %collective-permute-start.4 = (f32[1,128,128]{2,1,0:T(8,128)}, f32[1,128,128]{2,1,0:T(8,128)S(1)}, u32[]{:S(2)}, u32[]{:S(2)}) collective-permute-start(f32[1,128,128]{2,1,0:T(8,128)} %bitcast.17), channel_id=1, source_target_pairs={{0,16},{4,20},{8,24},{12,28},{16,0},{20,4},{24,8},{28,12},{1,17},{... | collective-permute-start | bytes 196616 | tf_op jit(solution)/shard_map/ppermute | solution.py:18
  9.2 6.2 %collective-permute-start.1 = (f32[2,128,128]{2,1,0:T(8,128)S(1)}, f32[2,128,128]{2,1,0:T(8,128)S(1)}, u32[]{:S(2)}, u32[]{:S(2)}) collective-permute-start(f32[2,128,128]{2,1,0:T(8,128)S(1)} %shard_map.60.refs_0_), channel_id=1, source_target_pairs={{0,2},{1,3},{2,0},{3,1},{4,6},{5,7},{6,4},{7,5},{8,10},{9,11},{10,... | collective-permute-start | bytes 393224 | tf_op jit(solution)/shard_map/ppermute | solution.py:18
  12.1 5.0 %collective-permute-start.5 = (f32[2,128,128]{2,1,0:T(8,128)S(1)}, f32[2,128,128]{2,1,0:T(8,128)S(1)}, u32[]{:S(2)}, u32[]{:S(2)}) collective-permute-start(f32[2,128,128]{2,1,0:T(8,128)S(1)} %bitcast.15), channel_id=1, source_target_pairs={{0,8},{4,12},{8,0},{12,4},{16,24},{20,28},{24,16},{28,20},{1,9},{5... | collective-permute-start | bytes 393224 | tf_op jit(solution)/shard_map/ppermute | solution.py:18
  13.3 3.9 %collective-permute-start.2 = (f32[2,128,128]{2,1,0:T(8,128)S(1)}, f32[2,128,128]{2,1,0:T(8,128)S(1)}, u32[]{:S(2)}, u32[]{:S(2)}) collective-permute-start(f32[2,128,128]{2,1,0:T(8,128)S(1)} %shard_map.60.refs_0_), channel_id=1, source_target_pairs={{0,1},{1,0},{2,3},{3,2},{4,5},{5,4},{6,7},{7,6},{8,9},{9,8},{10,11... | collective-permute-start | bytes 393224 | tf_op jit(solution)/shard_map/ppermute | solution.py:18
  15.4 1.8 %collective-permute-start.3 = (f32[2,128,128]{2,1,0:T(8,128)S(1)}, f32[2,128,128]{2,1,0:T(8,128)S(1)}, u32[]{:S(2)}, u32[]{:S(2)}) collective-permute-start(f32[2,128,128]{2,1,0:T(8,128)S(1)} %collective-permute-done.1.refs_1_), channel_id=1, source_target_pairs={{0,1},{1,0},{2,3},{3,2},{4,5},{5,4},{6,7},{7,6},{8,9},{9,8},{10,11... | collective-permute-start | bytes 393224 | tf_op jit(solution)/shard_map/ppermute | solution.py:18
  15.4 5.6 %collective-permute-start.10 = (f32[2,128,128]{2,1,0:T(8,128)S(1)}, f32[2,128,128]{2,1,0:T(8,128)S(1)}, u32[]{:S(2)}, u32[]{:S(2)}) collective-permute-start(f32[2,128,128]{2,1,0:T(8,128)S(1)} %collective-permute-done.swapped), channel_id=1, source_target_pairs={{0,1},{1,0},{2,3},{3,2},{4,5},{5,4},{6,7},{7,6},{8,9},{9,8},{10,11... | collective-permute-start | bytes 393224 | tf_op jit(solution)/shard_map/ppermute | solution.py:18
  17.6 5.2 %collective-permute-start.9 = (f32[256,128]{1,0:T(8,128)S(1)}, f32[256,128]{1,0:T(8,128)S(1)}, u32[]{:S(2)}, u32[]{:S(2)}) collective-permute-start(f32[256,128]{1,0:T(8,128)S(1)} %get-tuple-element.23.both), channel_id=1, source_target_pairs={{0,4},{4,0},{8,12},{12,8},{16,20},{20,16},{24,28},{28,24},{1,5},{5... | collective-permute-start | bytes 393224 | tf_op jit(solution)/shard_map/ppermute | solution.py:18
  19.0 3.8 %copy-start.2 = (f32[64,128]{1,0:T(8,128)S(1)}, f32[64,128]{1,0:T(8,128)}, u32[]{:S(2)}) copy-start(f32[64,128]{1,0:T(8,128)} %dinv.1) | copy-start | bytes 98308
  19.0 8.1 %collective-permute-start.6 = (f32[64,128]{1,0:T(8,128)S(1)}, f32[64,128]{1,0:T(8,128)S(1)}, u32[]{:S(2)}, u32[]{:S(2)}) collective-permute-start(f32[64,128]{1,0:T(8,128)S(1)} %get-tuple-element.20), channel_id=1, source_target_pairs={{0,1},{1,0},{2,3},{3,2},{4,5},{5,4},{6,7},{7,6},{8,9},{9,8},{10,11... | collective-permute-start | bytes 98312 | tf_op jit(solution)/shard_map/ppermute | solution.py:18
  19.1 8.6 %collective-permute-start.7 = (f32[64,128]{1,0:T(8,128)S(1)}, f32[64,128]{1,0:T(8,128)S(1)}, u32[]{:S(2)}, u32[]{:S(2)}) collective-permute-start(f32[64,128]{1,0:T(8,128)S(1)} %get-tuple-element.21), channel_id=1, source_target_pairs={{0,2},{1,3},{2,0},{3,1},{4,6},{5,7},{6,4},{7,5},{8,10},{9,11},{10,... | collective-permute-start | bytes 98312 | tf_op jit(solution)/shard_map/ppermute | solution.py:18
  20.7 7.0 %collective-permute-start.8 = (f32[64,128]{1,0:T(8,128)S(1)}, f32[64,128]{1,0:T(8,128)S(1)}, u32[]{:S(2)}, u32[]{:S(2)}) collective-permute-start(f32[64,128]{1,0:T(8,128)S(1)} %get-tuple-element.22), channel_id=1, source_target_pairs={{0,3},{1,2},{2,1},{3,0},{4,7},{5,6},{6,5},{7,4},{8,11},{9,10},{10,... | collective-permute-start | bytes 98312 | tf_op jit(solution)/shard_map/ppermute | solution.py:18
  23.1 6.3 %collective-permute-start.12 = (f32[64,128]{1,0:T(8,128)S(1)}, f32[64,128]{1,0:T(8,128)S(1)}, u32[]{:S(2)}, u32[]{:S(2)}) collective-permute-start(f32[64,128]{1,0:T(8,128)S(1)} %get-tuple-element.27), channel_id=1, source_target_pairs={{0,24},{4,28},{8,16},{12,20},{16,8},{20,12},{24,0},{28,4},{1,25},{... | collective-permute-start | bytes 98312 | tf_op jit(solution)/shard_map/ppermute | solution.py:18
  27.0 4.8 %collective-permute-start.13 = (f32[64,128]{1,0:T(8,128)S(1)}, f32[64,128]{1,0:T(8,128)S(1)}, u32[]{:S(2)}, u32[]{:S(2)}) collective-permute-start(f32[64,128]{1,0:T(8,128)S(1)} %get-tuple-element.28), channel_id=1, source_target_pairs={{0,16},{4,20},{8,24},{12,28},{16,0},{20,4},{24,8},{28,12},{1,17},{... | collective-permute-start | bytes 98312 | tf_op jit(solution)/shard_map/ppermute | solution.py:18
  27.1 4.8 %collective-permute-start.14 = (f32[64,128]{1,0:T(8,128)S(1)}, f32[64,128]{1,0:T(8,128)S(1)}, u32[]{:S(2)}, u32[]{:S(2)}) collective-permute-start(f32[64,128]{1,0:T(8,128)S(1)} %get-tuple-element.29), channel_id=1, source_target_pairs={{0,8},{4,12},{8,0},{12,4},{16,24},{20,28},{24,16},{28,20},{1,9},{5... | collective-permute-start | bytes 98312 | tf_op jit(solution)/shard_map/ppermute | solution.py:18
  27.7 4.3 %collective-permute-start.11 = (f32[32,512]{1,0:T(8,128)S(1)}, f32[32,512]{1,0:T(8,128)S(1)}, u32[]{:S(2)}, u32[]{:S(2)}) collective-permute-start(f32[32,512]{1,0:T(8,128)S(1)} %get-tuple-element.26), channel_id=1, source_target_pairs={{0,4},{4,0},{8,12},{12,8},{16,20},{20,16},{24,28},{28,24},{1,5},{5... | collective-permute-start | bytes 196616 | tf_op jit(solution)/shard_map/ppermute | solution.py:18

commit v22 on v21

--- a/solution.py
+++ b/solution.py
@@ -50,23 +50,23 @@
     return blocks[pl.ds(a * order * block_cols + b, order, stride=block_cols), :] * weight
 
 
-def prepare_kernel(tall, presence, blocks, factor, swap, mine):
+def prepare_kernel(tall, presence, blocks, factor, mine, *swaps):
     rows, span = mine.shape
     mine[...] = factor[:, pl.ds(pl.multiple_of(lax.axis_index("col") * span, LANES), span)]
     row_bit = lax.axis_index("row") & 1
     same = row_bit == (lax.axis_index("col") & 1)
-    order = swap.shape[2]
+    order = blocks.shape[1]
     block_cols = blocks.shape[0] // rows
     half = parity_half(factor[...], tall, 1 - row_bit)
-    for b in range(swap.shape[0]):
+    for b, swap in enumerate(swaps):
         for a in range(rows // order):
             here = pl.ds(a * order, order)
             part = half[a * order : (a + 1) * order, b * order : (b + 1) * order]
             if b >= block_cols:
-                swap[b, here, :] = part
+                swap[here, :] = part
                 continue
             block = masked_block(presence, blocks, block_cols, a, b)
-            swap[b, here, :] = jnp.where(same, part, block) if part.shape[1] else block
+            swap[here, :] = jnp.where(same, part, block) if part.shape[1] else block
 
 
 def prepare(presence, blocks, own, span, tall):
@@ -85,52 +85,55 @@
         half = parity_half(own, tall, 1 - row_bit).reshape(rows, -1, order).transpose(1, 0, 2)
         half = jnp.pad(half, ((0, depth - half.shape[0]), (0, 0), (0, 0)))
         padded = jnp.pad(masked, ((0, depth - block_cols), (0, 0), (0, 0)))
-        return jnp.where(same, half, padded), mine
-    return pl.pallas_call(
+        return mine, list(jnp.where(same, half, padded))
+    mine, *swaps = pl.pallas_call(
         functools.partial(prepare_kernel, tall),
-        out_shape=(
-            jax.ShapeDtypeStruct((depth, rows, order), jnp.float32),
-            jax.ShapeDtypeStruct((rows, span), jnp.float32),
-        ),
+        out_shape=(jax.ShapeDtypeStruct((rows, span), jnp.float32),)
+        + (jax.ShapeDtypeStruct((rows, order), jnp.float32),) * depth,
         in_specs=[WHOLE] * 3,
-        out_specs=(WHOLE, WHOLE),
+        out_specs=(WHOLE,) * (1 + depth),
         cost_estimate=LIGHT,
     )(presence, blocks, own)
-
-
-def joined_kernel(bit, first, second, out):
-    here = jnp.where((lax.axis_index("row") & bit) == 0, 0, 1)
-    if first.ndim == 2:
-        span = out.shape[3]
-        spot = pl.ds(pl.multiple_of(lax.axis_index("col") * span, LANES), span)
-        out[0, here] = first[:, spot]
-    else:
-        out[:, here] = first[...]
-    out[:, 1 - here] = second[...]
-
-
-def joined(first, second, bit):
-    count, rows, span = second.shape
-    both = pl.pallas_call(
-        functools.partial(joined_kernel, bit),
-        out_shape=jax.ShapeDtypeStruct((count, 2, rows, span), jnp.float32),
-        in_specs=[WHOLE, WHOLE],
+    return mine, swaps
+
+
+def ordered_kernel(flips, *refs):
+    columns = refs[-1]
+    _, order, _ = columns.shape
+    for flip, strip in zip(flips, refs[:-1]):
+        at = (lax.axis_index("row") ^ flip) >> 1
+        for a in range(strip.shape[0] // order):
+            columns[a * len(flips) + at] = strip[pl.ds(a * order, order), :]
+
+
+def ordered(strips, flips, order):
+    rows, span = strips[0].shape
+    return pl.pallas_call(
+        functools.partial(ordered_kernel, flips),
+        out_shape=jax.ShapeDtypeStruct((rows // order * len(strips), order, span), jnp.float32),
+        in_specs=[WHOLE] * len(strips),
         out_specs=WHOLE,
         cost_estimate=pl.CostEstimate(flops=HEAVY, bytes_accessed=1000, transcendentals=0),
         compiler_params=ROOM,
-    )(first, second)
-    return both.reshape(2 * count, rows, span)
+    )(*strips)
 
 
 def partials_kernel(count, *refs):
-    pieces = refs[: 2 * count]
-    columns, both, *outward = refs[2 * count :]
-    block_cols, rows, order = pieces[0].shape
+    held, mate = refs[:2]
+    block_cols, rows, order = held.shape
+    far = (count - 1) * block_cols
+    ours, theirs, refs = refs[2 : 2 + far], refs[2 + far : 2 + 2 * far], refs[2 + 2 * far :]
+    columns, both, *outward = refs
     col_index = lax.axis_index("col")
     left, right = [], []
     for t in range(count):
         for b in range(block_cols):
-            left.append(jnp.concatenate([pieces[t][b], pieces[count + t][b]], axis=0))
+            if t:
+                at = (t - 1) * block_cols + b
+                pair = [ours[at][...], theirs[at][...]]
+            else:
+                pair = [held[b], mate[b]]
+            left.append(jnp.concatenate(pair, axis=0))
             right.append(columns[b * count + ((col_index >> 1) ^ t)])
     summed = product(jnp.concatenate(left, axis=1), jnp.concatenate(right, axis=0), ((1,), (0,)))
     here = (col_index & 1) * rows
@@ -144,17 +147,19 @@
             piece[pl.ds(a * share, share), :] = -picked
 
 
-def partials(pieces, columns, receivers):
-    rows, span = 2 * pieces[0].shape[1], columns.shape[2]
+def partials(held, mate, ours, theirs, columns, receivers):
+    block_cols, rows, _ = held.shape
+    rows, span = 2 * rows, columns.shape[2]
+    operands = (held, mate, *ours, *theirs, columns)
     outward = (jax.ShapeDtypeStruct((rows // receivers, span), jnp.float32),) * receivers
     both, *outward = pl.pallas_call(
-        functools.partial(partials_kernel, len(pieces) // 2),
+        functools.partial(partials_kernel, 1 + len(ours) // block_cols),
         out_shape=(jax.ShapeDtypeStruct((rows, span), jnp.float32),) + outward,
-        in_specs=[WHOLE] * (len(pieces) + 1),
+        in_specs=[WHOLE] * len(operands),
         out_specs=(WHOLE,) * (1 + receivers),
         cost_estimate=LIGHT,
         compiler_params=ROOM,
-    )(*pieces, columns)
+    )(*operands)
     return both, outward
 
 
@@ -258,26 +263,40 @@
     )(keep, came, total)
 
 
-def pick_kernel(presence, blocks, swapped, held):
+def pick_kernel(block_cols, b, presence, blocks, swapped, held):
     same = (lax.axis_index("row") & 1) == (lax.axis_index("col") & 1)
-    block_cols, rows, order = held.shape
-    for b in range(block_cols):
-        for a in range(rows // order):
-            here = pl.ds(a * order, order)
-            block = masked_block(presence, blocks, block_cols, a, b)
-            held[b, here, :] = jnp.where(same, block, swapped[b, here, :])
-
-
-def pick(presence, blocks, swapped):
-    rows, order = swapped.shape[1:]
-    return pl.pallas_call(
-        pick_kernel,
-        out_shape=jax.ShapeDtypeStruct((blocks.shape[0] // rows, rows, order), jnp.float32),
+    rows, order = held.shape
+    for a in range(rows // order):
+        here = pl.ds(a * order, order)
+        block = masked_block(presence, blocks, block_cols, a, b)
+        held[here, :] = jnp.where(same, block, swapped[here, :])
+
+
+def pick(presence, blocks, swapped, b):
+    return pl.pallas_call(
+        functools.partial(pick_kernel, blocks.shape[0] // swapped.shape[0], b),
+        out_shape=jax.ShapeDtypeStruct(swapped.shape, jnp.float32),
         in_specs=[WHOLE] * 3,
         out_specs=WHOLE,
         cost_estimate=LIGHT,
         compiler_params=ROOM,
     )(presence, blocks, swapped)
+
+
+def stacked_kernel(*refs):
+    for at, piece in enumerate(refs[:-1]):
+        refs[-1][at] = piece[...]
+
+
+def stacked(pieces):
+    return pl.pallas_call(
+        stacked_kernel,
+        out_shape=jax.ShapeDtypeStruct((len(pieces),) + pieces[0].shape, jnp.float32),
+        in_specs=[WHOLE] * len(pieces),
+        out_specs=WHOLE,
+        cost_estimate=LIGHT,
+        compiler_params=ROOM,
+    )(*pieces)
 
 
 def crossed(swap):
@@ -291,20 +310,14 @@
     return lax.ppermute(swap, ("row", "col"), cross)
 
 
-def pair_rows(held):
-    held = [held] + [flipped(held, "col", flip) for flip in range(2, lax.axis_size("col"), 2)]
-    return held + [flipped(piece, "col", 1) for piece in held]
-
-
-def along_line(mine, own):
-    strips = mine[None]
+def along_line(mine, order):
+    strips, flips = [mine], [0]
     bit = lax.axis_size("row") // 2
     while bit > 1:
-        whole = strips.shape[0] == 1 and mine.shape[1] % LANES == 0
-        first = own if whole else strips
-        strips = joined(first, flipped(strips, "row", bit), bit)
+        strips = strips + [flipped(strip, "row", bit) for strip in strips]
+        flips = flips + [flip ^ bit for flip in flips]
         bit //= 2
-    return strips
+    return ordered(strips, tuple(flips), order)
 
 
 def local(inverse_set, presence, factor, dinv):
@@ -320,15 +333,18 @@
     blocks = inverse_set.reshape(rows * block_cols, order)
     marks = presence.reshape(1, -1)
     tall = width // groups_row
-    swap, mine = prepare(marks, blocks, own, span, tall)
-    swapped = crossed(swap)
+    mine, swaps = prepare(marks, blocks, own, span, tall)
+    swapped = [crossed(swap) for swap in swaps]
     stay = stay_half(own, tall)
-    columns = along_line(mine, own).reshape(-1, block_rows, order, span).transpose(1, 0, 2, 3)
-    columns = columns.reshape(-1, order, span)
-    pieces = pair_rows(pick(marks, blocks, swapped))
-    mate_swapped = flipped(swapped, "col", 1)
-
-    both, outward = partials(pieces, columns, groups_col)
+    columns = along_line(mine, order)
+    held = [pick(marks, blocks, swapped[b], b) for b in range(block_cols)]
+    far = [(flip, piece) for flip in range(2, groups_col, 2) for piece in held]
+    ours = [flipped(piece, "col", flip) for flip, piece in far]
+    theirs = [flipped(piece, "col", 1) for piece in ours]
+    held, swapped = stacked(held), stacked(swapped)
+    mate, mate_swapped = flipped(held, "col", 1), flipped(swapped, "col", 1)
+
+    both, outward = partials(held, mate, ours, theirs, columns, groups_col)
     got = flipped(both, "row", 1)
     arrived = [outward[0]] + [flipped(outward[f], "col", f) for f in range(1, groups_col)]
     flips = (0,) + tuple(range(groups_row - 2, 0, -2))

time: 32.8 us -> 33.1 us (level)
  starting transfers between devices: 18.6 us -> 20.4 us
  waiting for transfers between devices: 9.8 us -> 8.16 us
    ppermute x14 -> x17, starting transfers between devices: 16.3 us -> 18 us  [flipped(): lax.ppermute(value, axis, [(i, i ^ flip) for i in range(lax.axis_size(axi...]
    ppermute x1 -> x2, waiting for transfers between devices: 1.6 us -> 0.01 us  [crossed(): return lax.ppermute(swap, ('row', 'col'), cross)]
    ppermute x14 -> x17, waiting for transfers between devices: 8.2 us -> 8.15 us  [flipped(): lax.ppermute(value, axis, [(i, i ^ flip) for i in range(lax.axis_size(axi...]
    ppermute x1 -> x2, starting transfers between devices: 2.38 us -> 2.41 us  [crossed(): return lax.ppermute(swap, ('row', 'col'), cross)]
  transfers between devices with their start and end apart: 15 -> 19, of which waited for: 7 -> 7; matrix products, arithmetic and copies ran while one was open for 0% -> 0% of each run, Pallas kernels for 3% -> 3%
where the time goes in v22:
time: 33.1 us; the launch traced here: 32.9 us
  starting transfers between devices  20.4 us (62%)
  waiting for transfers between devices  8.16 us (25%)
  Pallas kernels  3.57 us (11%)
  between operations  0.76 us (2%)
    ppermute x17, starting transfers between devices, flipped(): lax.ppermute(value, axis, [(i, i ^ flip) for i in range(lax.axis_size(axi...  18 us
    ppermute x17, waiting for transfers between devices, flipped(): lax.ppermute(value, axis, [(i, i ^ flip) for i in range(lax.axis_size(axi...  8.15 us
    ppermute x2, starting transfers between devices, crossed(): return lax.ppermute(swap, ('row', 'col'), cross)  2.41 us
    pallas_call x1, Pallas kernels, prepare(): pl.pallas_call(functools.partial(prepare_kernel, tall), out_shape=(jax.Sh...  1.85 us
  transfers between devices with their start and end apart: 19, of which 7 were waited for; matrix products, arithmetic and copies ran while one was open for 0% of the time, Pallas kernels for 3%

profile of v22, /device:TPU:0, one launch (start us, length us, event | category | flops | bytes accessed | tf_op | source)
XLA Modules:
  0.0 32.9 jit_solution(3216621872555350388)
XLA Ops:
  0.6 1.9 %shard_map.59 = (f32[128,128]{1,0:T(8,128)}, f32[128,128]{1,0:T(8,128)}, f32[128,128]{1,0:T(8,128)}) custom-call(s32[1,2]{1,0:T(1,128)} %bitcast.9, f32[256,128]{1,0:T(8,128)} %bitcast.4, f32[128,512]{1,0:T(8,128)} %bitcast.7), custom_call_target="tpu_custom_call" | custom-call | flops 1000 | bytes 1000 | tf_op jit(solution)/shard_map/pallas_call | solution.py:89
  2.5 2.4 %collective-permute-start = (f32[128,128]{1,0:T(8,128)}, f32[128,128]{1,0:T(8,128)S(1)}, u32[]{:S(2)}, u32[]{:S(2)}) collective-permute-start(f32[128,128]{1,0:T(8,128)} %get-tuple-element.18), channel_id=1, source_target_pairs={{0,5},{1,4},{2,7},{3,6},{4,1},{5,0},{6,3},{7,2},{8,13},{9,12},{10,... | collective-permute-start | bytes 196616 | tf_op jit(solution)/shard_map/ppermute | solution.py:310
  4.9 3.4 %collective-permute-start.7 = (f32[128,128]{1,0:T(8,128)}, f32[128,128]{1,0:T(8,128)S(1)}, u32[]{:S(2)}, u32[]{:S(2)}) collective-permute-start(f32[128,128]{1,0:T(8,128)} %get-tuple-element.20.refs_0_), channel_id=1, source_target_pairs={{0,16},{4,20},{8,24},{12,28},{16,0},{20,4},{24,8},{28,12},{1,17},{... | collective-permute-start | bytes 196616 | tf_op jit(solution)/shard_map/ppermute | solution.py:18
  8.3 1.6 %collective-permute-start.8 = (f32[128,128]{1,0:T(8,128)}, f32[128,128]{1,0:T(8,128)S(1)}, u32[]{:S(2)}, u32[]{:S(2)}) collective-permute-start(f32[128,128]{1,0:T(8,128)} %get-tuple-element.20.refs_0_), channel_id=1, source_target_pairs={{0,8},{4,12},{8,0},{12,4},{16,24},{20,28},{24,16},{28,20},{1,9},{5... | collective-permute-start | bytes 196616 | tf_op jit(solution)/shard_map/ppermute | solution.py:18
  9.9 1.5 %collective-permute-start.3 = (f32[128,128]{1,0:T(8,128)S(1)}, f32[128,128]{1,0:T(8,128)S(1)}, u32[]{:S(2)}, u32[]{:S(2)}) collective-permute-start(f32[128,128]{1,0:T(8,128)S(1)} %shard_map.60.refs_0_), channel_id=1, source_target_pairs={{0,2},{1,3},{2,0},{3,1},{4,6},{5,7},{6,4},{7,5},{8,10},{9,11},{10,... | collective-permute-start | bytes 196616 | tf_op jit(solution)/shard_map/ppermute | solution.py:18
  11.6 0.5 %collective-permute-start.4 = (f32[128,128]{1,0:T(8,128)S(1)}, f32[128,128]{1,0:T(8,128)S(1)}, u32[]{:S(2)}, u32[]{:S(2)}) collective-permute-start(f32[128,128]{1,0:T(8,128)S(1)} %shard_map.61.refs_1_), channel_id=1, source_target_pairs={{0,2},{1,3},{2,0},{3,1},{4,6},{5,7},{6,4},{7,5},{8,10},{9,11},{10,... | collective-permute-start | bytes 196616 | tf_op jit(solution)/shard_map/ppermute | solution.py:18
  12.1 0.9 %collective-permute-start.9 = (f32[128,128]{1,0:T(8,128)S(1)}, f32[128,128]{1,0:T(8,128)S(1)}, u32[]{:S(2)}, u32[]{:S(2)}) collective-permute-start(f32[128,128]{1,0:T(8,128)S(1)} %collective-permute-done.7.refs_1_), channel_id=1, source_target_pairs={{0,8},{4,12},{8,0},{12,4},{16,24},{20,28},{24,16},{28,20},{1,9},{5... | collective-permute-start | bytes 196616 | tf_op jit(solution)/shard_map/ppermute | solution.py:18
  13.1 0.6 %collective-permute-start.14 = (f32[2,128,128]{2,1,0:T(8,128)S(1)}, f32[2,128,128]{2,1,0:T(8,128)S(1)}, u32[]{:S(2)}, u32[]{:S(2)}) collective-permute-start(f32[2,128,128]{2,1,0:T(8,128)S(1)} %shard_map.66.swapped), channel_id=1, source_target_pairs={{0,1},{1,0},{2,3},{3,2},{4,5},{5,4},{6,7},{7,6},{8,9},{9,8},{10,11... | collective-permute-start | bytes 393224 | tf_op jit(solution)/shard_map/ppermute | solution.py:18
  13.7 1.0 %collective-permute-done.3.refs_2_ = f32[128,128]{1,0:T(8,128)S(1)} collective-permute-done((f32[128,128]{1,0:T(8,128)S(1)}, f32[128,128]{1,0:T(8,128)S(1)}, u32[]{:S(2)}, u32[]{:S(2)}) %collective-permute-start.3) | collective-permute-done | bytes 65568 | tf_op jit(solution)/shard_map/ppermute | solution.py:18
  14.7 1.2 %collective-permute-done.4.refs_3_ = f32[128,128]{1,0:T(8,128)S(1)} collective-permute-done((f32[128,128]{1,0:T(8,128)S(1)}, f32[128,128]{1,0:T(8,128)S(1)}, u32[]{:S(2)}, u32[]{:S(2)}) %collective-permute-start.4) | collective-permute-done | bytes 65568 | tf_op jit(solution)/shard_map/ppermute | solution.py:18
  15.9 0.5 %collective-permute-done.9.refs_3_ = f32[128,128]{1,0:T(8,128)S(1)} collective-permute-done((f32[128,128]{1,0:T(8,128)S(1)}, f32[128,128]{1,0:T(8,128)S(1)}, u32[]{:S(2)}, u32[]{:S(2)}) %collective-permute-start.9) | collective-permute-done | bytes 65568 | tf_op jit(solution)/shard_map/ppermute | solution.py:18
  16.4 0.7 %collective-permute-done.6.refs_5_ = f32[128,128]{1,0:T(8,128)S(1)} collective-permute-done((f32[128,128]{1,0:T(8,128)S(1)}, f32[128,128]{1,0:T(8,128)S(1)}, u32[]{:S(2)}, u32[]{:S(2)}) %collective-permute-start.6) | collective-permute-done | bytes 65568 | tf_op jit(solution)/shard_map/ppermute | solution.py:18
  17.1 0.4 %shard_map.64 = (f32[256,128]{1,0:T(8,128)S(1)}, f32[64,128]{1,0:T(8,128)S(1)}, f32[64,128]{1,0:T(8,128)S(1)}, f32[64,128]{1,0:T(8,128)S(1)}, f32[64,128]{1,0:T(8,128)S(1)}) custom-call(f32[2,128,128]{2,1,0:T(8,128)S(1)} %shard_map.62.refs_0_, f32[2,128,128]{2,1,0:T(8,128)S(1)} %collective-permute-done.2.refs_1_, ...), custom_call_target="tpu_custom_call" | custom-call | flops 1000 | bytes 1000 | tf_op jit(solution)/shard_map/pallas_call | solution.py:155
  17.5 1.6 %collective-permute-start.13 = (f32[256,128]{1,0:T(8,128)S(1)}, f32[256,128]{1,0:T(8,128)S(1)}, u32[]{:S(2)}, u32[]{:S(2)}) collective-permute-start(f32[256,128]{1,0:T(8,128)S(1)} %get-tuple-element.25.both), channel_id=1, source_target_pairs={{0,4},{4,0},{8,12},{12,8},{16,20},{20,16},{24,28},{28,24},{1,5},{5... | collective-permute-start | bytes 393224 | tf_op jit(solution)/shard_map/ppermute | solution.py:18
  19.2 0.9 %collective-permute-start.11 = (f32[64,128]{1,0:T(8,128)S(1)}, f32[64,128]{1,0:T(8,128)S(1)}, u32[]{:S(2)}, u32[]{:S(2)}) collective-permute-start(f32[64,128]{1,0:T(8,128)S(1)} %get-tuple-element.23), channel_id=1, source_target_pairs={{0,2},{1,3},{2,0},{3,1},{4,6},{5,7},{6,4},{7,5},{8,10},{9,11},{10,... | collective-permute-start | bytes 98312 | tf_op jit(solution)/shard_map/ppermute | solution.py:18
  20.1 1.0 %collective-permute-start.12 = (f32[64,128]{1,0:T(8,128)S(1)}, f32[64,128]{1,0:T(8,128)S(1)}, u32[]{:S(2)}, u32[]{:S(2)}) collective-permute-start(f32[64,128]{1,0:T(8,128)S(1)} %get-tuple-element.24), channel_id=1, source_target_pairs={{0,3},{1,2},{2,1},{3,0},{4,7},{5,6},{6,5},{7,4},{8,11},{9,10},{10,... | collective-permute-start | bytes 98312 | tf_op jit(solution)/shard_map/ppermute | solution.py:18
  21.1 2.0 %collective-permute-done.13.got = f32[256,128]{1,0:T(8,128)S(1)} collective-permute-done((f32[256,128]{1,0:T(8,128)S(1)}, f32[256,128]{1,0:T(8,128)S(1)}, u32[]{:S(2)}, u32[]{:S(2)}) %collective-permute-start.13) | collective-permute-done | bytes 131104 | tf_op jit(solution)/shard_map/ppermute | solution.py:18
  23.1 0.3 %shard_map.67 = (f32[64,128]{1,0:T(8,128)S(1)}, f32[64,128]{1,0:T(8,128)S(1)}, f32[64,128]{1,0:T(8,128)S(1)}, f32[64,128]{1,0:T(8,128)S(1)}) custom-call(f32[256,128]{1,0:T(8,128)S(1)} %get-tuple-element.25.both, f32[256,128]{1,0:T(8,128)S(1)} %collective-permute-done.13.got, f32[128,256]{1,0:T(8,128)S(1)} %shard_map.65.stay, ...), custom_call_target="tpu_custom_call" | custom-call | flops 1000 | bytes 1000 | tf_op jit(solution)/shard_map/pallas_call | solution.py:205
  23.5 2.3 %collective-permute-start.16 = (f32[64,128]{1,0:T(8,128)S(1)}, f32[64,128]{1,0:T(8,128)S(1)}, u32[]{:S(2)}, u32[]{:S(2)}) collective-permute-start(f32[64,128]{1,0:T(8,128)S(1)} %get-tuple-element.29), channel_id=1, source_target_pairs={{0,24},{4,28},{8,16},{12,20},{16,8},{20,12},{24,0},{28,4},{1,25},{... | collective-permute-start | bytes 98312 | tf_op jit(solution)/shard_map/ppermute | solution.py:18
  25.8 2.1 %collective-permute-start.18 = (f32[64,128]{1,0:T(8,128)S(1)}, f32[64,128]{1,0:T(8,128)S(1)}, u32[]{:S(2)}, u32[]{:S(2)}) collective-permute-start(f32[64,128]{1,0:T(8,128)S(1)} %get-tuple-element.31), channel_id=1, source_target_pairs={{0,8},{4,12},{8,0},{12,4},{16,24},{20,28},{24,16},{28,20},{1,9},{5... | collective-permute-start | bytes 98312 | tf_op jit(solution)/shard_map/ppermute | solution.py:18
  28.0 1.6 %collective-permute-start.15 = (f32[32,512]{1,0:T(8,128)S(1)}, f32[32,512]{1,0:T(8,128)S(1)}, u32[]{:S(2)}, u32[]{:S(2)}) collective-permute-start(f32[32,512]{1,0:T(8,128)S(1)} %get-tuple-element.28), channel_id=1, source_target_pairs={{0,4},{4,0},{8,12},{12,8},{16,20},{20,16},{24,28},{28,24},{1,5},{5... | collective-permute-start | bytes 196616 | tf_op jit(solution)/shard_map/ppermute | solution.py:18
  29.5 1.1 %collective-permute-done.17 = f32[64,128]{1,0:T(8,128)S(1)} collective-permute-done((f32[64,128]{1,0:T(8,128)S(1)}, f32[64,128]{1,0:T(8,128)S(1)}, u32[]{:S(2)}, u32[]{:S(2)}) %collective-permute-start.17) | collective-permute-done | bytes 32800 | tf_op jit(solution)/shard_map/ppermute | solution.py:18
  30.6 1.7 %collective-permute-done.15.came = f32[32,512]{1,0:T(8,128)S(1)} collective-permute-done((f32[32,512]{1,0:T(8,128)S(1)}, f32[32,512]{1,0:T(8,128)S(1)}, u32[]{:S(2)}, u32[]{:S(2)}) %collective-permute-start.15) | collective-permute-done | bytes 65568 | tf_op jit(solution)/shard_map/ppermute | solution.py:18
  32.3 0.6 %shard_map.69 = (f32[32,512]{1,0:T(8,128)}, f32[64,128]{1,0:T(8,128)}) custom-call(f32[32,512]{1,0:T(8,128)S(1)} %get-tuple-element.27.keep, f32[32,512]{1,0:T(8,128)S(1)} %collective-permute-done.15.came, f32[64,128]{1,0:T(8,128)S(1)} %add_add_fusion.total), custom_call_target="tpu_custom_call" | custom-call | flops 1000 | bytes 1000 | tf_op jit(solution)/shard_map/pallas_call | solution.py:256
  (36 shorter events, 0.5 us)
Async XLA Ops:
  0.6 9.2 %copy-start = (f32[1,1,128,2,1,128]{5,4,3,2,1,0:T(1,128)S(1)}, f32[1,1,128,2,1,128]{5,4,3,2,1,0:T(1,128)}, u32[]{:S(2)}) copy-start(f32[1,1,128,2,1,128]{5,4,3,2,1,0:T(1,128)} %param.4) | copy-start | bytes 393220
  2.5 7.4 %collective-permute-start = (f32[128,128]{1,0:T(8,128)}, f32[128,128]{1,0:T(8,128)S(1)}, u32[]{:S(2)}, u32[]{:S(2)}) collective-permute-start(f32[128,128]{1,0:T(8,128)} %get-tuple-element.18), channel_id=1, source_target_pairs={{0,5},{1,4},{2,7},{3,6},{4,1},{5,0},{6,3},{7,2},{8,13},{9,12},{10,... | collective-permute-start | bytes 196616 | tf_op jit(solution)/shard_map/ppermute | solution.py:310
  4.9 5.0 %copy-start.3 = (s32[1,1,2,1]{2,3,1,0:T(1,128)S(1)}, s32[1,1,2,1]{2,3,1,0:T(1,128)}, u32[]{:S(2)}) copy-start(s32[1,1,2,1]{2,3,1,0:T(1,128)} %param.5) | copy-start | bytes 28
  4.9 6.6 %collective-permute-start.1 = (f32[128,128]{1,0:T(8,128)}, f32[128,128]{1,0:T(8,128)S(1)}, u32[]{:S(2)}, u32[]{:S(2)}) collective-permute-start(f32[128,128]{1,0:T(8,128)} %get-tuple-element.19), channel_id=1, source_target_pairs={{0,5},{1,4},{2,7},{3,6},{4,1},{5,0},{6,3},{7,2},{8,13},{9,12},{10,... | collective-permute-start | bytes 196616 | tf_op jit(solution)/shard_map/ppermute | solution.py:310
  4.9 7.2 %collective-permute-start.7 = (f32[128,128]{1,0:T(8,128)}, f32[128,128]{1,0:T(8,128)S(1)}, u32[]{:S(2)}, u32[]{:S(2)}) collective-permute-start(f32[128,128]{1,0:T(8,128)} %get-tuple-element.20.refs_0_), channel_id=1, source_target_pairs={{0,16},{4,20},{8,24},{12,28},{16,0},{20,4},{24,8},{28,12},{1,17},{... | collective-permute-start | bytes 196616 | tf_op jit(solution)/shard_map/ppermute | solution.py:18
  8.3 4.8 %collective-permute-start.8 = (f32[128,128]{1,0:T(8,128)}, f32[128,128]{1,0:T(8,128)S(1)}, u32[]{:S(2)}, u32[]{:S(2)}) collective-permute-start(f32[128,128]{1,0:T(8,128)} %get-tuple-element.20.refs_0_), channel_id=1, source_target_pairs={{0,8},{4,12},{8,0},{12,4},{16,24},{20,28},{24,16},{28,20},{1,9},{5... | collective-permute-start | bytes 196616 | tf_op jit(solution)/shard_map/ppermute | solution.py:18
  9.9 4.7 %collective-permute-start.3 = (f32[128,128]{1,0:T(8,128)S(1)}, f32[128,128]{1,0:T(8,128)S(1)}, u32[]{:S(2)}, u32[]{:S(2)}) collective-permute-start(f32[128,128]{1,0:T(8,128)S(1)} %shard_map.60.refs_0_), channel_id=1, source_target_pairs={{0,2},{1,3},{2,0},{3,1},{4,6},{5,7},{6,4},{7,5},{8,10},{9,11},{10,... | collective-permute-start | bytes 196616 | tf_op jit(solution)/shard_map/ppermute | solution.py:18
  11.6 4.3 %collective-permute-start.4 = (f32[128,128]{1,0:T(8,128)S(1)}, f32[128,128]{1,0:T(8,128)S(1)}, u32[]{:S(2)}, u32[]{:S(2)}) collective-permute-start(f32[128,128]{1,0:T(8,128)S(1)} %shard_map.61.refs_1_), channel_id=1, source_target_pairs={{0,2},{1,3},{2,0},{3,1},{4,6},{5,7},{6,4},{7,5},{8,10},{9,11},{10,... | collective-permute-start | bytes 196616 | tf_op jit(solution)/shard_map/ppermute | solution.py:18
  12.1 4.3 %collective-permute-start.9 = (f32[128,128]{1,0:T(8,128)S(1)}, f32[128,128]{1,0:T(8,128)S(1)}, u32[]{:S(2)}, u32[]{:S(2)}) collective-permute-start(f32[128,128]{1,0:T(8,128)S(1)} %collective-permute-done.7.refs_1_), channel_id=1, source_target_pairs={{0,8},{4,12},{8,0},{12,4},{16,24},{20,28},{24,16},{28,20},{1,9},{5... | collective-permute-start | bytes 196616 | tf_op jit(solution)/shard_map/ppermute | solution.py:18
  13.0 3.4 %copy-start.4 = (f32[128,128]{1,0:T(8,128)S(1)}, f32[128,128]{1,0:T(8,128)}, u32[]{:S(2)}) copy-start(f32[128,128]{1,0:T(8,128)} %get-tuple-element.20.refs_0_) | copy-start | bytes 196612
  13.0 3.4 %collective-permute-start.2 = (f32[2,128,128]{2,1,0:T(8,128)S(1)}, f32[2,128,128]{2,1,0:T(8,128)S(1)}, u32[]{:S(2)}, u32[]{:S(2)}) collective-permute-start(f32[2,128,128]{2,1,0:T(8,128)S(1)} %shard_map.62.refs_0_), channel_id=1, source_target_pairs={{0,1},{1,0},{2,3},{3,2},{4,5},{5,4},{6,7},{7,6},{8,9},{9,8},{10,11... | collective-permute-start | bytes 393224 | tf_op jit(solution)/shard_map/ppermute | solution.py:18
  13.1 8.0 %collective-permute-start.14 = (f32[2,128,128]{2,1,0:T(8,128)S(1)}, f32[2,128,128]{2,1,0:T(8,128)S(1)}, u32[]{:S(2)}, u32[]{:S(2)}) collective-permute-start(f32[2,128,128]{2,1,0:T(8,128)S(1)} %shard_map.66.swapped), channel_id=1, source_target_pairs={{0,1},{1,0},{2,3},{3,2},{4,5},{5,4},{6,7},{7,6},{8,9},{9,8},{10,11... | collective-permute-start | bytes 393224 | tf_op jit(solution)/shard_map/ppermute | solution.py:18
  14.7 1.8 %collective-permute-start.5 = (f32[128,128]{1,0:T(8,128)S(1)}, f32[128,128]{1,0:T(8,128)S(1)}, u32[]{:S(2)}, u32[]{:S(2)}) collective-permute-start(f32[128,128]{1,0:T(8,128)S(1)} %collective-permute-done.3.refs_2_), channel_id=1, source_target_pairs={{0,1},{1,0},{2,3},{3,2},{4,5},{5,4},{6,7},{7,6},{8,9},{9,8},{10,11... | collective-permute-start | bytes 196616 | tf_op jit(solution)/shard_map/ppermute | solution.py:18
  15.9 1.3 %collective-permute-start.6 = (f32[128,128]{1,0:T(8,128)S(1)}, f32[128,128]{1,0:T(8,128)S(1)}, u32[]{:S(2)}, u32[]{:S(2)}) collective-permute-start(f32[128,128]{1,0:T(8,128)S(1)} %collective-permute-done.4.refs_3_), channel_id=1, source_target_pairs={{0,1},{1,0},{2,3},{3,2},{4,5},{5,4},{6,7},{7,6},{8,9},{9,8},{10,11... | collective-permute-start | bytes 196616 | tf_op jit(solution)/shard_map/ppermute | solution.py:18
  16.4 2.7 %copy-start.1 = (f32[1,1,128,512]{3,2,1,0:T(8,128)S(1)}, f32[1,1,128,512]{3,2,1,0:T(8,128)}, u32[]{:S(2)}) copy-start(f32[1,1,128,512]{3,2,1,0:T(8,128)} %param.6) | copy-start | bytes 786436
  17.5 5.6 %collective-permute-start.13 = (f32[256,128]{1,0:T(8,128)S(1)}, f32[256,128]{1,0:T(8,128)S(1)}, u32[]{:S(2)}, u32[]{:S(2)}) collective-permute-start(f32[256,128]{1,0:T(8,128)S(1)} %get-tuple-element.25.both), channel_id=1, source_target_pairs={{0,4},{4,0},{8,12},{12,8},{16,20},{20,16},{24,28},{28,24},{1,5},{5... | collective-permute-start | bytes 393224 | tf_op jit(solution)/shard_map/ppermute | solution.py:18
  19.1 4.1 %copy-start.2 = (f32[64,128]{1,0:T(8,128)S(1)}, f32[64,128]{1,0:T(8,128)}, u32[]{:S(2)}) copy-start(f32[64,128]{1,0:T(8,128)} %dinv.1) | copy-start | bytes 98308
  19.1 6.7 %collective-permute-start.10 = (f32[64,128]{1,0:T(8,128)S(1)}, f32[64,128]{1,0:T(8,128)S(1)}, u32[]{:S(2)}, u32[]{:S(2)}) collective-permute-start(f32[64,128]{1,0:T(8,128)S(1)} %get-tuple-element.22), channel_id=1, source_target_pairs={{0,1},{1,0},{2,3},{3,2},{4,5},{5,4},{6,7},{7,6},{8,9},{9,8},{10,11... | collective-permute-start | bytes 98312 | tf_op jit(solution)/shard_map/ppermute | solution.py:18
  19.2 8.7 %collective-permute-start.11 = (f32[64,128]{1,0:T(8,128)S(1)}, f32[64,128]{1,0:T(8,128)S(1)}, u32[]{:S(2)}, u32[]{:S(2)}) collective-permute-start(f32[64,128]{1,0:T(8,128)S(1)} %get-tuple-element.23), channel_id=1, source_target_pairs={{0,2},{1,3},{2,0},{3,1},{4,6},{5,7},{6,4},{7,5},{8,10},{9,11},{10,... | collective-permute-start | bytes 98312 | tf_op jit(solution)/shard_map/ppermute | solution.py:18
  20.1 7.8 %collective-permute-start.12 = (f32[64,128]{1,0:T(8,128)S(1)}, f32[64,128]{1,0:T(8,128)S(1)}, u32[]{:S(2)}, u32[]{:S(2)}) collective-permute-start(f32[64,128]{1,0:T(8,128)S(1)} %get-tuple-element.24), channel_id=1, source_target_pairs={{0,3},{1,2},{2,1},{3,0},{4,7},{5,6},{6,5},{7,4},{8,11},{9,10},{10,... | collective-permute-start | bytes 98312 | tf_op jit(solution)/shard_map/ppermute | solution.py:18
  23.5 6.0 %collective-permute-start.16 = (f32[64,128]{1,0:T(8,128)S(1)}, f32[64,128]{1,0:T(8,128)S(1)}, u32[]{:S(2)}, u32[]{:S(2)}) collective-permute-start(f32[64,128]{1,0:T(8,128)S(1)} %get-tuple-element.29), channel_id=1, source_target_pairs={{0,24},{4,28},{8,16},{12,20},{16,8},{20,12},{24,0},{28,4},{1,25},{... | collective-permute-start | bytes 98312 | tf_op jit(solution)/shard_map/ppermute | solution.py:18
  25.8 4.8 %collective-permute-start.17 = (f32[64,128]{1,0:T(8,128)S(1)}, f32[64,128]{1,0:T(8,128)S(1)}, u32[]{:S(2)}, u32[]{:S(2)}) collective-permute-start(f32[64,128]{1,0:T(8,128)S(1)} %get-tuple-element.30), channel_id=1, source_target_pairs={{0,16},{4,20},{8,24},{12,28},{16,0},{20,4},{24,8},{28,12},{1,17},{... | collective-permute-start | bytes 98312 | tf_op jit(solution)/shard_map/ppermute | solution.py:18
  25.8 4.8 %collective-permute-start.18 = (f32[64,128]{1,0:T(8,128)S(1)}, f32[64,128]{1,0:T(8,128)S(1)}, u32[]{:S(2)}, u32[]{:S(2)}) collective-permute-start(f32[64,128]{1,0:T(8,128)S(1)} %get-tuple-element.31), channel_id=1, source_target_pairs={{0,8},{4,12},{8,0},{12,4},{16,24},{20,28},{24,16},{28,20},{1,9},{5... | collective-permute-start | bytes 98312 | tf_op jit(solution)/shard_map/ppermute | solution.py:18
  28.0 4.3 %collective-permute-start.15 = (f32[32,512]{1,0:T(8,128)S(1)}, f32[32,512]{1,0:T(8,128)S(1)}, u32[]{:S(2)}, u32[]{:S(2)}) collective-permute-start(f32[32,512]{1,0:T(8,128)S(1)} %get-tuple-element.28), channel_id=1, source_target_pairs={{0,4},{4,0},{8,12},{12,8},{16,20},{20,16},{24,28},{28,24},{1,5},{5... | collective-permute-start | bytes 196616 | tf_op jit(solution)/shard_map/ppermute | solution.py:18

commit v23 on v22

--- a/solution.py
+++ b/solution.py
@@ -216,51 +216,55 @@
     )(both, got, stay, swapped, mate_swapped, dinv)
 
 
-def collect_kernel(*refs):
-    arrived, (_, keep, send) = refs[:-3], refs[-3:]
+def collect_kernel(flips, *refs):
+    arrived, (keep, send) = refs[:-2], refs[-2:]
     share = keep.shape[0]
     span = refs[0].shape[1]
     here = (lax.axis_index("row") & 1) * share
-    for flip, piece in enumerate(arrived):
+    for flip, piece in zip(flips, arrived):
         spot = pl.ds(pl.multiple_of((lax.axis_index("col") ^ flip) * span, LANES), span)
         keep[:, spot] = piece[pl.ds(pl.multiple_of(here, 8), share), :]
         send[:, spot] = piece[pl.ds(pl.multiple_of(share - here, 8), share), :]
 
 
-def collect(arrived, along):
-    flips = len(arrived)
+def collect(arrived, flips):
     share, span = arrived[0].shape[0] // 2, arrived[0].shape[1]
     if span % LANES:
         me = lax.axis_index("col")
+        by_flip = [arrived[flips.index(flip)] for flip in range(len(flips))]
         row_bit = lax.axis_index("row") & 1
-        laid = jnp.concatenate([lax.select_n(me ^ j, *arrived) for j in range(flips)], axis=1)
-        laid = laid.reshape(2, share, span * flips)
+        laid = jnp.concatenate([lax.select_n(me ^ j, *by_flip) for j in range(len(flips))], axis=1)
+        laid = laid.reshape(2, share, span * len(flips))
         return [lax.dynamic_index_in_dim(laid, row_bit ^ k, 0, keepdims=False) for k in range(2)]
-    part = jax.ShapeDtypeStruct((share, span * flips), jnp.float32)
-    return pl.pallas_call(
-        collect_kernel,
+    part = jax.ShapeDtypeStruct((share, span * len(flips)), jnp.float32)
+    return pl.pallas_call(
+        functools.partial(collect_kernel, flips),
         out_shape=(part, part),
-        in_specs=[WHOLE] * flips + [pl.BlockSpec(memory_space=pl.ANY)],
+        in_specs=[WHOLE] * len(flips),
         out_specs=(WHOLE, WHOLE),
         cost_estimate=LIGHT,
         compiler_params=ROOM,
-    )(*arrived, along)
-
-
-def close_kernel(keep, came, total, off_diag, diag_block):
+    )(*arrived)
+
+
+def close_kernel(keep, came, *refs):
+    along, (off_diag, diag_block) = refs[:-2], refs[-2:]
     off_diag[...] = keep[...] + came[...]
-    diag_block[...] = total[...]
-
-
-def close(keep, came, total):
+    total = along[0][...]
+    for piece in along[1:]:
+        total = total + piece[...]
+    diag_block[...] = total
+
+
+def close(keep, came, along):
     return pl.pallas_call(
         close_kernel,
-        out_shape=[jax.ShapeDtypeStruct(x.shape, jnp.float32) for x in (keep, total)],
-        in_specs=[WHOLE] * 3,
+        out_shape=[jax.ShapeDtypeStruct(x.shape, jnp.float32) for x in (keep, along[0])],
+        in_specs=[WHOLE] * (2 + len(along)),
         out_specs=[WHOLE, WHOLE],
         cost_estimate=LIGHT,
         compiler_params=ROOM,
-    )(keep, came, total)
+    )(keep, came, *along)
 
 
 def pick_kernel(block_cols, b, presence, blocks, swapped, held):
@@ -346,13 +350,14 @@
 
     both, outward = partials(held, mate, ours, theirs, columns, groups_col)
     got = flipped(both, "row", 1)
-    arrived = [outward[0]] + [flipped(outward[f], "col", f) for f in range(1, groups_col)]
+    far_first = (0, *range(groups_col - 1, 0, -1))
+    arrived = [flipped(outward[f], "col", f) if f else outward[f] for f in far_first]
+    keep, send = collect(arrived, far_first)
+    came = flipped(send, "row", 1)
     flips = (0,) + tuple(range(groups_row - 2, 0, -2))
     along = finish(both, got, stay, swapped, mate_swapped, dinv, flips)
-    keep, send = collect(arrived, along[0])
-    came = flipped(send, "row", 1)
     met = [flipped(piece, "row", flip) if flip else piece for flip, piece in zip(flips, along)]
-    off_diag, diag_block = close(keep, came, sum(met[1:], met[0]))
+    off_diag, diag_block = close(keep, came, met)
     return (off_diag.reshape(block_rows, 1, share, width), diag_block)
 
 

time: 33.1 us -> 32.9 us (level)
  starting transfers between devices: 20.4 us -> 19.4 us
  waiting for transfers between devices: 8.16 us -> 8.92 us
    ppermute x17, starting transfers between devices: 18 us -> 17 us  [flipped(): lax.ppermute(value, axis, [(i, i ^ flip) for i in range(lax.axis_size(axi...]
    ppermute x17, waiting for transfers between devices: 8.15 us -> 8.91 us  [flipped(): lax.ppermute(value, axis, [(i, i ^ flip) for i in range(lax.axis_size(axi...]
  transfers between devices with their start and end apart: 19 -> 19, of which waited for: 7 -> 8; matrix products, arithmetic and copies ran while one was open for 0% -> 0% of each run, Pallas kernels for 3% -> 3%
where the time goes in v23:
time: 32.9 us; the launch traced here: 32.7 us
  starting transfers between devices  19.4 us (59%)
  waiting for transfers between devices  8.92 us (27%)
  Pallas kernels  3.58 us (11%)
  between operations  0.77 us (2%)
    ppermute x17, starting transfers between devices, flipped(): lax.ppermute(value, axis, [(i, i ^ flip) for i in range(lax.axis_size(axi...  17 us
    ppermute x17, waiting for transfers between devices, flipped(): lax.ppermute(value, axis, [(i, i ^ flip) for i in range(lax.axis_size(axi...  8.91 us
    ppermute x2, starting transfers between devices, crossed(): return lax.ppermute(swap, ('row', 'col'), cross)  2.41 us
    pallas_call x1, Pallas kernels, prepare(): pl.pallas_call(functools.partial(prepare_kernel, tall), out_shape=(jax.Sh...  1.85 us
  transfers between devices with their start and end apart: 19, of which 8 were waited for; matrix products, arithmetic and copies ran while one was open for 0% of the time, Pallas kernels for 3%

profile of v23, /device:TPU:0, one launch (start us, length us, event | category | flops | bytes accessed | tf_op | source)
XLA Modules:
  0.0 32.7 jit_solution(2484982117003934265)
XLA Ops:
  0.6 1.9 %shard_map.59 = (f32[128,128]{1,0:T(8,128)}, f32[128,128]{1,0:T(8,128)}, f32[128,128]{1,0:T(8,128)}) custom-call(s32[1,2]{1,0:T(1,128)} %bitcast.9, f32[256,128]{1,0:T(8,128)} %bitcast.4, f32[128,512]{1,0:T(8,128)} %bitcast.7), custom_call_target="tpu_custom_call" | custom-call | flops 1000 | bytes 1000 | tf_op jit(solution)/shard_map/pallas_call | solution.py:89
  2.5 2.4 %collective-permute-start = (f32[128,128]{1,0:T(8,128)}, f32[128,128]{1,0:T(8,128)S(1)}, u32[]{:S(2)}, u32[]{:S(2)}) collective-permute-start(f32[128,128]{1,0:T(8,128)} %get-tuple-element.18), channel_id=1, source_target_pairs={{0,5},{1,4},{2,7},{3,6},{4,1},{5,0},{6,3},{7,2},{8,13},{9,12},{10,... | collective-permute-start | bytes 196616 | tf_op jit(solution)/shard_map/ppermute | solution.py:314
  4.9 3.4 %collective-permute-start.7 = (f32[128,128]{1,0:T(8,128)}, f32[128,128]{1,0:T(8,128)S(1)}, u32[]{:S(2)}, u32[]{:S(2)}) collective-permute-start(f32[128,128]{1,0:T(8,128)} %get-tuple-element.20.refs_0_), channel_id=1, source_target_pairs={{0,16},{4,20},{8,24},{12,28},{16,0},{20,4},{24,8},{28,12},{1,17},{... | collective-permute-start | bytes 196616 | tf_op jit(solution)/shard_map/ppermute | solution.py:18
  8.3 1.6 %collective-permute-start.8 = (f32[128,128]{1,0:T(8,128)}, f32[128,128]{1,0:T(8,128)S(1)}, u32[]{:S(2)}, u32[]{:S(2)}) collective-permute-start(f32[128,128]{1,0:T(8,128)} %get-tuple-element.20.refs_0_), channel_id=1, source_target_pairs={{0,8},{4,12},{8,0},{12,4},{16,24},{20,28},{24,16},{28,20},{1,9},{5... | collective-permute-start | bytes 196616 | tf_op jit(solution)/shard_map/ppermute | solution.py:18
  9.9 1.5 %collective-permute-start.3 = (f32[128,128]{1,0:T(8,128)S(1)}, f32[128,128]{1,0:T(8,128)S(1)}, u32[]{:S(2)}, u32[]{:S(2)}) collective-permute-start(f32[128,128]{1,0:T(8,128)S(1)} %shard_map.60.refs_0_), channel_id=1, source_target_pairs={{0,2},{1,3},{2,0},{3,1},{4,6},{5,7},{6,4},{7,5},{8,10},{9,11},{10,... | collective-permute-start | bytes 196616 | tf_op jit(solution)/shard_map/ppermute | solution.py:18
  11.6 0.5 %collective-permute-start.4 = (f32[128,128]{1,0:T(8,128)S(1)}, f32[128,128]{1,0:T(8,128)S(1)}, u32[]{:S(2)}, u32[]{:S(2)}) collective-permute-start(f32[128,128]{1,0:T(8,128)S(1)} %shard_map.61.refs_1_), channel_id=1, source_target_pairs={{0,2},{1,3},{2,0},{3,1},{4,6},{5,7},{6,4},{7,5},{8,10},{9,11},{10,... | collective-permute-start | bytes 196616 | tf_op jit(solution)/shard_map/ppermute | solution.py:18
  12.1 0.9 %collective-permute-start.9 = (f32[128,128]{1,0:T(8,128)S(1)}, f32[128,128]{1,0:T(8,128)S(1)}, u32[]{:S(2)}, u32[]{:S(2)}) collective-permute-start(f32[128,128]{1,0:T(8,128)S(1)} %collective-permute-done.7.refs_1_), channel_id=1, source_target_pairs={{0,8},{4,12},{8,0},{12,4},{16,24},{20,28},{24,16},{28,20},{1,9},{5... | collective-permute-start | bytes 196616 | tf_op jit(solution)/shard_map/ppermute | solution.py:18
  13.1 0.6 %collective-permute-start.15 = (f32[2,128,128]{2,1,0:T(8,128)S(1)}, f32[2,128,128]{2,1,0:T(8,128)S(1)}, u32[]{:S(2)}, u32[]{:S(2)}) collective-permute-start(f32[2,128,128]{2,1,0:T(8,128)S(1)} %shard_map.67.swapped), channel_id=1, source_target_pairs={{0,1},{1,0},{2,3},{3,2},{4,5},{5,4},{6,7},{7,6},{8,9},{9,8},{10,11... | collective-permute-start | bytes 393224 | tf_op jit(solution)/shard_map/ppermute | solution.py:18
  13.7 1.0 %collective-permute-done.3.refs_2_ = f32[128,128]{1,0:T(8,128)S(1)} collective-permute-done((f32[128,128]{1,0:T(8,128)S(1)}, f32[128,128]{1,0:T(8,128)S(1)}, u32[]{:S(2)}, u32[]{:S(2)}) %collective-permute-start.3) | collective-permute-done | bytes 65568 | tf_op jit(solution)/shard_map/ppermute | solution.py:18
  14.7 1.2 %collective-permute-done.4.refs_3_ = f32[128,128]{1,0:T(8,128)S(1)} collective-permute-done((f32[128,128]{1,0:T(8,128)S(1)}, f32[128,128]{1,0:T(8,128)S(1)}, u32[]{:S(2)}, u32[]{:S(2)}) %collective-permute-start.4) | collective-permute-done | bytes 65568 | tf_op jit(solution)/shard_map/ppermute | solution.py:18
  15.9 0.5 %collective-permute-done.9.refs_3_ = f32[128,128]{1,0:T(8,128)S(1)} collective-permute-done((f32[128,128]{1,0:T(8,128)S(1)}, f32[128,128]{1,0:T(8,128)S(1)}, u32[]{:S(2)}, u32[]{:S(2)}) %collective-permute-start.9) | collective-permute-done | bytes 65568 | tf_op jit(solution)/shard_map/ppermute | solution.py:18
  16.4 0.7 %collective-permute-done.6.refs_5_ = f32[128,128]{1,0:T(8,128)S(1)} collective-permute-done((f32[128,128]{1,0:T(8,128)S(1)}, f32[128,128]{1,0:T(8,128)S(1)}, u32[]{:S(2)}, u32[]{:S(2)}) %collective-permute-start.6) | collective-permute-done | bytes 65568 | tf_op jit(solution)/shard_map/ppermute | solution.py:18
  17.1 0.4 %shard_map.64 = (f32[256,128]{1,0:T(8,128)S(1)}, f32[64,128]{1,0:T(8,128)S(1)}, f32[64,128]{1,0:T(8,128)S(1)}, f32[64,128]{1,0:T(8,128)S(1)}, f32[64,128]{1,0:T(8,128)S(1)}) custom-call(f32[2,128,128]{2,1,0:T(8,128)S(1)} %shard_map.62.refs_0_, f32[2,128,128]{2,1,0:T(8,128)S(1)} %collective-permute-done.2.refs_1_, ...), custom_call_target="tpu_custom_call" | custom-call | flops 1000 | bytes 1000 | tf_op jit(solution)/shard_map/pallas_call | solution.py:155
  17.5 1.6 %collective-permute-start.14 = (f32[256,128]{1,0:T(8,128)S(1)}, f32[256,128]{1,0:T(8,128)S(1)}, u32[]{:S(2)}, u32[]{:S(2)}) collective-permute-start(f32[256,128]{1,0:T(8,128)S(1)} %get-tuple-element.27.both), channel_id=1, source_target_pairs={{0,4},{4,0},{8,12},{12,8},{16,20},{20,16},{24,28},{28,24},{1,5},{5... | collective-permute-start | bytes 393224 | tf_op jit(solution)/shard_map/ppermute | solution.py:18
  19.1 1.4 %collective-permute-start.11 = (f32[64,128]{1,0:T(8,128)S(1)}, f32[64,128]{1,0:T(8,128)S(1)}, u32[]{:S(2)}, u32[]{:S(2)}) collective-permute-start(f32[64,128]{1,0:T(8,128)S(1)} %get-tuple-element.23), channel_id=1, source_target_pairs={{0,2},{1,3},{2,0},{3,1},{4,6},{5,7},{6,4},{7,5},{8,10},{9,11},{10,... | collective-permute-start | bytes 98312 | tf_op jit(solution)/shard_map/ppermute | solution.py:18
  20.6 0.4 %collective-permute-start.12 = (f32[64,128]{1,0:T(8,128)S(1)}, f32[64,128]{1,0:T(8,128)S(1)}, u32[]{:S(2)}, u32[]{:S(2)}) collective-permute-start(f32[64,128]{1,0:T(8,128)S(1)} %get-tuple-element.24), channel_id=1, source_target_pairs={{0,1},{1,0},{2,3},{3,2},{4,5},{5,4},{6,7},{7,6},{8,9},{9,8},{10,11... | collective-permute-start | bytes 98312 | tf_op jit(solution)/shard_map/ppermute | solution.py:18
  20.9 1.8 %collective-permute-done.10.refs_1_ = f32[64,128]{1,0:T(8,128)S(1)} collective-permute-done((f32[64,128]{1,0:T(8,128)S(1)}, f32[64,128]{1,0:T(8,128)S(1)}, u32[]{:S(2)}, u32[]{:S(2)}) %collective-permute-start.10) | collective-permute-done | bytes 32800 | tf_op jit(solution)/shard_map/ppermute | solution.py:18
  22.7 0.8 %collective-permute-done.11.refs_2_ = f32[64,128]{1,0:T(8,128)S(1)} collective-permute-done((f32[64,128]{1,0:T(8,128)S(1)}, f32[64,128]{1,0:T(8,128)S(1)}, u32[]{:S(2)}, u32[]{:S(2)}) %collective-permute-start.11) | collective-permute-done | bytes 32800 | tf_op jit(solution)/shard_map/ppermute | solution.py:18
  23.5 0.6 %collective-permute-start.13 = (f32[32,512]{1,0:T(8,128)S(1)}, f32[32,512]{1,0:T(8,128)S(1)}, u32[]{:S(2)}, u32[]{:S(2)}) collective-permute-start(f32[32,512]{1,0:T(8,128)S(1)} %get-tuple-element.26), channel_id=1, source_target_pairs={{0,4},{4,0},{8,12},{12,8},{16,20},{20,16},{24,28},{28,24},{1,5},{5... | collective-permute-start | bytes 196616 | tf_op jit(solution)/shard_map/ppermute | solution.py:18
  24.6 2.6 %collective-permute-start.16 = (f32[64,128]{1,0:T(8,128)S(1)}, f32[64,128]{1,0:T(8,128)S(1)}, u32[]{:S(2)}, u32[]{:S(2)}) collective-permute-start(f32[64,128]{1,0:T(8,128)S(1)} %get-tuple-element.29), channel_id=1, source_target_pairs={{0,24},{4,28},{8,16},{12,20},{16,8},{20,12},{24,0},{28,4},{1,25},{... | collective-permute-start | bytes 98312 | tf_op jit(solution)/shard_map/ppermute | solution.py:18
  27.2 1.8 %collective-permute-start.18 = (f32[64,128]{1,0:T(8,128)S(1)}, f32[64,128]{1,0:T(8,128)S(1)}, u32[]{:S(2)}, u32[]{:S(2)}) collective-permute-start(f32[64,128]{1,0:T(8,128)S(1)} %get-tuple-element.31), channel_id=1, source_target_pairs={{0,8},{4,12},{8,0},{12,4},{16,24},{20,28},{24,16},{28,20},{1,9},{5... | collective-permute-start | bytes 98312 | tf_op jit(solution)/shard_map/ppermute | solution.py:18
  29.1 1.4 %collective-permute-done.16.refs_1_ = f32[64,128]{1,0:T(8,128)S(1)} collective-permute-done((f32[64,128]{1,0:T(8,128)S(1)}, f32[64,128]{1,0:T(8,128)S(1)}, u32[]{:S(2)}, u32[]{:S(2)}) %collective-permute-start.16) | collective-permute-done | bytes 32800 | tf_op jit(solution)/shard_map/ppermute | solution.py:18
  30.4 1.6 %collective-permute-done.17.refs_2_ = f32[64,128]{1,0:T(8,128)S(1)} collective-permute-done((f32[64,128]{1,0:T(8,128)S(1)}, f32[64,128]{1,0:T(8,128)S(1)}, u32[]{:S(2)}, u32[]{:S(2)}) %collective-permute-start.17) | collective-permute-done | bytes 32800 | tf_op jit(solution)/shard_map/ppermute | solution.py:18
  32.0 0.7 %shard_map.69 = (f32[32,512]{1,0:T(8,128)}, f32[64,128]{1,0:T(8,128)}) custom-call(f32[32,512]{1,0:T(8,128)S(1)} %get-tuple-element.25.keep, f32[32,512]{1,0:T(8,128)S(1)} %collective-permute-done.13.came, f32[64,128]{1,0:T(8,128)S(1)} %get-tuple-element.28.refs_0_, f32[64,128]{1,0:T(8,128)S(1)} %collective-permute-done.16.refs_1_, ...), custom_call_target="tpu_custom_call" | custom-call | flops 1000 | bytes 1000 | tf_op jit(solution)/shard_map/pallas_call | solution.py:260
  (35 shorter events, 0.9 us)
Async XLA Ops:
  0.6 9.2 %copy-start = (f32[1,1,128,2,1,128]{5,4,3,2,1,0:T(1,128)S(1)}, f32[1,1,128,2,1,128]{5,4,3,2,1,0:T(1,128)}, u32[]{:S(2)}) copy-start(f32[1,1,128,2,1,128]{5,4,3,2,1,0:T(1,128)} %param.4) | copy-start | bytes 393220
  2.5 7.4 %collective-permute-start = (f32[128,128]{1,0:T(8,128)}, f32[128,128]{1,0:T(8,128)S(1)}, u32[]{:S(2)}, u32[]{:S(2)}) collective-permute-start(f32[128,128]{1,0:T(8,128)} %get-tuple-element.18), channel_id=1, source_target_pairs={{0,5},{1,4},{2,7},{3,6},{4,1},{5,0},{6,3},{7,2},{8,13},{9,12},{10,... | collective-permute-start | bytes 196616 | tf_op jit(solution)/shard_map/ppermute | solution.py:314
  4.9 5.0 %copy-start.3 = (s32[1,1,2,1]{2,3,1,0:T(1,128)S(1)}, s32[1,1,2,1]{2,3,1,0:T(1,128)}, u32[]{:S(2)}) copy-start(s32[1,1,2,1]{2,3,1,0:T(1,128)} %param.5) | copy-start | bytes 28
  4.9 6.6 %collective-permute-start.1 = (f32[128,128]{1,0:T(8,128)}, f32[128,128]{1,0:T(8,128)S(1)}, u32[]{:S(2)}, u32[]{:S(2)}) collective-permute-start(f32[128,128]{1,0:T(8,128)} %get-tuple-element.19), channel_id=1, source_target_pairs={{0,5},{1,4},{2,7},{3,6},{4,1},{5,0},{6,3},{7,2},{8,13},{9,12},{10,... | collective-permute-start | bytes 196616 | tf_op jit(solution)/shard_map/ppermute | solution.py:314
  4.9 7.2 %collective-permute-start.7 = (f32[128,128]{1,0:T(8,128)}, f32[128,128]{1,0:T(8,128)S(1)}, u32[]{:S(2)}, u32[]{:S(2)}) collective-permute-start(f32[128,128]{1,0:T(8,128)} %get-tuple-element.20.refs_0_), channel_id=1, source_target_pairs={{0,16},{4,20},{8,24},{12,28},{16,0},{20,4},{24,8},{28,12},{1,17},{... | collective-permute-start | bytes 196616 | tf_op jit(solution)/shard_map/ppermute | solution.py:18
  8.3 4.8 %collective-permute-start.8 = (f32[128,128]{1,0:T(8,128)}, f32[128,128]{1,0:T(8,128)S(1)}, u32[]{:S(2)}, u32[]{:S(2)}) collective-permute-start(f32[128,128]{1,0:T(8,128)} %get-tuple-element.20.refs_0_), channel_id=1, source_target_pairs={{0,8},{4,12},{8,0},{12,4},{16,24},{20,28},{24,16},{28,20},{1,9},{5... | collective-permute-start | bytes 196616 | tf_op jit(solution)/shard_map/ppermute | solution.py:18
  9.9 4.7 %collective-permute-start.3 = (f32[128,128]{1,0:T(8,128)S(1)}, f32[128,128]{1,0:T(8,128)S(1)}, u32[]{:S(2)}, u32[]{:S(2)}) collective-permute-start(f32[128,128]{1,0:T(8,128)S(1)} %shard_map.60.refs_0_), channel_id=1, source_target_pairs={{0,2},{1,3},{2,0},{3,1},{4,6},{5,7},{6,4},{7,5},{8,10},{9,11},{10,... | collective-permute-start | bytes 196616 | tf_op jit(solution)/shard_map/ppermute | solution.py:18
  11.6 4.3 %collective-permute-start.4 = (f32[128,128]{1,0:T(8,128)S(1)}, f32[128,128]{1,0:T(8,128)S(1)}, u32[]{:S(2)}, u32[]{:S(2)}) collective-permute-start(f32[128,128]{1,0:T(8,128)S(1)} %shard_map.61.refs_1_), channel_id=1, source_target_pairs={{0,2},{1,3},{2,0},{3,1},{4,6},{5,7},{6,4},{7,5},{8,10},{9,11},{10,... | collective-permute-start | bytes 196616 | tf_op jit(solution)/shard_map/ppermute | solution.py:18
  12.1 4.3 %collective-permute-start.9 = (f32[128,128]{1,0:T(8,128)S(1)}, f32[128,128]{1,0:T(8,128)S(1)}, u32[]{:S(2)}, u32[]{:S(2)}) collective-permute-start(f32[128,128]{1,0:T(8,128)S(1)} %collective-permute-done.7.refs_1_), channel_id=1, source_target_pairs={{0,8},{4,12},{8,0},{12,4},{16,24},{20,28},{24,16},{28,20},{1,9},{5... | collective-permute-start | bytes 196616 | tf_op jit(solution)/shard_map/ppermute | solution.py:18
  13.0 3.4 %copy-start.4 = (f32[128,128]{1,0:T(8,128)S(1)}, f32[128,128]{1,0:T(8,128)}, u32[]{:S(2)}) copy-start(f32[128,128]{1,0:T(8,128)} %get-tuple-element.20.refs_0_) | copy-start | bytes 196612
  13.0 3.4 %collective-permute-start.2 = (f32[2,128,128]{2,1,0:T(8,128)S(1)}, f32[2,128,128]{2,1,0:T(8,128)S(1)}, u32[]{:S(2)}, u32[]{:S(2)}) collective-permute-start(f32[2,128,128]{2,1,0:T(8,128)S(1)} %shard_map.62.refs_0_), channel_id=1, source_target_pairs={{0,1},{1,0},{2,3},{3,2},{4,5},{5,4},{6,7},{7,6},{8,9},{9,8},{10,11... | collective-permute-start | bytes 393224 | tf_op jit(solution)/shard_map/ppermute | solution.py:18
  13.1 11.1 %collective-permute-start.15 = (f32[2,128,128]{2,1,0:T(8,128)S(1)}, f32[2,128,128]{2,1,0:T(8,128)S(1)}, u32[]{:S(2)}, u32[]{:S(2)}) collective-permute-start(f32[2,128,128]{2,1,0:T(8,128)S(1)} %shard_map.67.swapped), channel_id=1, source_target_pairs={{0,1},{1,0},{2,3},{3,2},{4,5},{5,4},{6,7},{7,6},{8,9},{9,8},{10,11... | collective-permute-start | bytes 393224 | tf_op jit(solution)/shard_map/ppermute | solution.py:18
  14.7 1.8 %collective-permute-start.5 = (f32[128,128]{1,0:T(8,128)S(1)}, f32[128,128]{1,0:T(8,128)S(1)}, u32[]{:S(2)}, u32[]{:S(2)}) collective-permute-start(f32[128,128]{1,0:T(8,128)S(1)} %collective-permute-done.3.refs_2_), channel_id=1, source_target_pairs={{0,1},{1,0},{2,3},{3,2},{4,5},{5,4},{6,7},{7,6},{8,9},{9,8},{10,11... | collective-permute-start | bytes 196616 | tf_op jit(solution)/shard_map/ppermute | solution.py:18
  15.9 1.3 %collective-permute-start.6 = (f32[128,128]{1,0:T(8,128)S(1)}, f32[128,128]{1,0:T(8,128)S(1)}, u32[]{:S(2)}, u32[]{:S(2)}) collective-permute-start(f32[128,128]{1,0:T(8,128)S(1)} %collective-permute-done.4.refs_3_), channel_id=1, source_target_pairs={{0,1},{1,0},{2,3},{3,2},{4,5},{5,4},{6,7},{7,6},{8,9},{9,8},{10,11... | collective-permute-start | bytes 196616 | tf_op jit(solution)/shard_map/ppermute | solution.py:18
  17.1 7.0 %copy-start.1 = (f32[1,1,128,512]{3,2,1,0:T(8,128)S(1)}, f32[1,1,128,512]{3,2,1,0:T(8,128)}, u32[]{:S(2)}) copy-start(f32[1,1,128,512]{3,2,1,0:T(8,128)} %param.6) | copy-start | bytes 786436
  17.5 6.7 %collective-permute-start.14 = (f32[256,128]{1,0:T(8,128)S(1)}, f32[256,128]{1,0:T(8,128)S(1)}, u32[]{:S(2)}, u32[]{:S(2)}) collective-permute-start(f32[256,128]{1,0:T(8,128)S(1)} %get-tuple-element.27.both), channel_id=1, source_target_pairs={{0,4},{4,0},{8,12},{12,8},{16,20},{20,16},{24,28},{28,24},{1,5},{5... | collective-permute-start | bytes 393224 | tf_op jit(solution)/shard_map/ppermute | solution.py:18
  19.1 3.6 %collective-permute-start.10 = (f32[64,128]{1,0:T(8,128)S(1)}, f32[64,128]{1,0:T(8,128)S(1)}, u32[]{:S(2)}, u32[]{:S(2)}) collective-permute-start(f32[64,128]{1,0:T(8,128)S(1)} %get-tuple-element.22), channel_id=1, source_target_pairs={{0,3},{1,2},{2,1},{3,0},{4,7},{5,6},{6,5},{7,4},{8,11},{9,10},{10,... | collective-permute-start | bytes 98312 | tf_op jit(solution)/shard_map/ppermute | solution.py:18
  19.1 4.3 %collective-permute-start.11 = (f32[64,128]{1,0:T(8,128)S(1)}, f32[64,128]{1,0:T(8,128)S(1)}, u32[]{:S(2)}, u32[]{:S(2)}) collective-permute-start(f32[64,128]{1,0:T(8,128)S(1)} %get-tuple-element.23), channel_id=1, source_target_pairs={{0,2},{1,3},{2,0},{3,1},{4,6},{5,7},{6,4},{7,5},{8,10},{9,11},{10,... | collective-permute-start | bytes 98312 | tf_op jit(solution)/shard_map/ppermute | solution.py:18
  20.6 2.9 %collective-permute-start.12 = (f32[64,128]{1,0:T(8,128)S(1)}, f32[64,128]{1,0:T(8,128)S(1)}, u32[]{:S(2)}, u32[]{:S(2)}) collective-permute-start(f32[64,128]{1,0:T(8,128)S(1)} %get-tuple-element.24), channel_id=1, source_target_pairs={{0,1},{1,0},{2,3},{3,2},{4,5},{5,4},{6,7},{7,6},{8,9},{9,8},{10,11... | collective-permute-start | bytes 98312 | tf_op jit(solution)/shard_map/ppermute | solution.py:18
  23.5 0.8 %copy-start.2 = (f32[64,128]{1,0:T(8,128)S(1)}, f32[64,128]{1,0:T(8,128)}, u32[]{:S(2)}) copy-start(f32[64,128]{1,0:T(8,128)} %dinv.1) | copy-start | bytes 98308
  23.5 5.6 %collective-permute-start.13 = (f32[32,512]{1,0:T(8,128)S(1)}, f32[32,512]{1,0:T(8,128)S(1)}, u32[]{:S(2)}, u32[]{:S(2)}) collective-permute-start(f32[32,512]{1,0:T(8,128)S(1)} %get-tuple-element.26), channel_id=1, source_target_pairs={{0,4},{4,0},{8,12},{12,8},{16,20},{20,16},{24,28},{28,24},{1,5},{5... | collective-permute-start | bytes 196616 | tf_op jit(solution)/shard_map/ppermute | solution.py:18
  24.6 5.8 %collective-permute-start.16 = (f32[64,128]{1,0:T(8,128)S(1)}, f32[64,128]{1,0:T(8,128)S(1)}, u32[]{:S(2)}, u32[]{:S(2)}) collective-permute-start(f32[64,128]{1,0:T(8,128)S(1)} %get-tuple-element.29), channel_id=1, source_target_pairs={{0,24},{4,28},{8,16},{12,20},{16,8},{20,12},{24,0},{28,4},{1,25},{... | collective-permute-start | bytes 98312 | tf_op jit(solution)/shard_map/ppermute | solution.py:18
  27.2 4.8 %collective-permute-start.17 = (f32[64,128]{1,0:T(8,128)S(1)}, f32[64,128]{1,0:T(8,128)S(1)}, u32[]{:S(2)}, u32[]{:S(2)}) collective-permute-start(f32[64,128]{1,0:T(8,128)S(1)} %get-tuple-element.30), channel_id=1, source_target_pairs={{0,16},{4,20},{8,24},{12,28},{16,0},{20,4},{24,8},{28,12},{1,17},{... | collective-permute-start | bytes 98312 | tf_op jit(solution)/shard_map/ppermute | solution.py:18
  27.2 4.8 %collective-permute-start.18 = (f32[64,128]{1,0:T(8,128)S(1)}, f32[64,128]{1,0:T(8,128)S(1)}, u32[]{:S(2)}, u32[]{:S(2)}) collective-permute-start(f32[64,128]{1,0:T(8,128)S(1)} %get-tuple-element.31), channel_id=1, source_target_pairs={{0,8},{4,12},{8,0},{12,4},{16,24},{20,28},{24,16},{28,20},{1,9},{5... | collective-permute-start | bytes 98312 | tf_op jit(solution)/shard_map/ppermute | solution.py:18

commit v24 on v22

--- a/solution.py
+++ b/solution.py
@@ -123,7 +123,7 @@
     block_cols, rows, order = held.shape
     far = (count - 1) * block_cols
     ours, theirs, refs = refs[2 : 2 + far], refs[2 + far : 2 + 2 * far], refs[2 + 2 * far :]
-    columns, both, *outward = refs
+    columns, both = refs
     col_index = lax.axis_index("col")
     left, right = [], []
     for t in range(count):
@@ -139,28 +139,19 @@
     here = (col_index & 1) * rows
     both[pl.ds(pl.multiple_of(here, 8), rows), :] = summed[:rows]
     both[pl.ds(pl.multiple_of(rows - here, 8), rows), :] = summed[rows:]
-    share = order // len(outward)
-    for flip, piece in enumerate(outward):
-        start = (col_index ^ flip) * share
-        for a in range(2 * rows // order):
-            picked = both[pl.ds(pl.multiple_of(a * order + start, 8), share), :]
-            piece[pl.ds(a * share, share), :] = -picked
-
-
-def partials(held, mate, ours, theirs, columns, receivers):
+
+
+def partials(held, mate, ours, theirs, columns):
     block_cols, rows, _ = held.shape
-    rows, span = 2 * rows, columns.shape[2]
     operands = (held, mate, *ours, *theirs, columns)
-    outward = (jax.ShapeDtypeStruct((rows // receivers, span), jnp.float32),) * receivers
-    both, *outward = pl.pallas_call(
+    return pl.pallas_call(
         functools.partial(partials_kernel, 1 + len(ours) // block_cols),
-        out_shape=(jax.ShapeDtypeStruct((rows, span), jnp.float32),) + outward,
+        out_shape=jax.ShapeDtypeStruct((2 * rows, columns.shape[2]), jnp.float32),
         in_specs=[WHOLE] * len(operands),
-        out_specs=(WHOLE,) * (1 + receivers),
+        out_specs=WHOLE,
         cost_estimate=LIGHT,
         compiler_params=ROOM,
     )(*operands)
-    return both, outward
 
 
 def stay_kernel(tall, own, stay):
@@ -179,15 +170,17 @@
     )(own)
 
 
-def finish_kernel(flips, both, got, stay, swapped, mate_swapped, dinv, *refs):
-    along, update, terms = refs[:-2], refs[-2], refs[-1]
+def finish_kernel(order, flips, both, got, stay, swapped, mate_swapped, dinv, *refs):
+    update, terms = refs[-2:]
+    along, outward = refs[: len(flips)], refs[len(flips) : -2]
     rows = stay.shape[0]
     row_index = lax.axis_index("row")
+    col_index = lax.axis_index("col")
     here = (row_index & 1) * rows
     update[...] = both[...] + got[...]
     mine = update[pl.ds(pl.multiple_of(here, 8), rows), :]
     other = update[pl.ds(pl.multiple_of(rows - here, 8), rows), :]
-    same = (row_index & 1) == (lax.axis_index("col") & 1)
+    same = (row_index & 1) == (col_index & 1)
     depth = stay.shape[1] // swapped.shape[2]
     near = [jnp.where(same, swapped[j], mate_swapped[j]) for j in range(depth)]
     factors = jnp.concatenate([stay[...], jnp.concatenate(near, axis=1)], axis=0)
@@ -197,16 +190,24 @@
         slot = ((row_index ^ flip) >> 1) * tall
         piece[...] = terms[pl.ds(pl.multiple_of(slot, 8), tall), :]
     along[0][...] = along[0][...] + dinv[...]
-
-
-def finish(both, got, stay, swapped, mate_swapped, dinv, flips):
+    share = order // len(outward)
+    for flip, piece in enumerate(outward):
+        start = here + (col_index ^ flip) * share
+        for a in range(rows // order):
+            picked = update[pl.ds(pl.multiple_of(a * order + start, 8), share), :]
+            piece[pl.ds(a * share, share), :] = -picked
+
+
+def finish(both, got, stay, swapped, mate_swapped, dinv, order, flips, receivers):
     rows, half = stay.shape
     span = both.shape[1]
-    return pl.pallas_call(
-        functools.partial(finish_kernel, flips),
-        out_shape=(jax.ShapeDtypeStruct(dinv.shape, jnp.float32),) * len(flips),
+    along = (jax.ShapeDtypeStruct(dinv.shape, jnp.float32),) * len(flips)
+    outward = (jax.ShapeDtypeStruct((rows // receivers, span), jnp.float32),) * receivers
+    outs = pl.pallas_call(
+        functools.partial(finish_kernel, order, flips),
+        out_shape=along + outward,
         in_specs=[WHOLE] * 6,
-        out_specs=(WHOLE,) * len(flips),
+        out_specs=(WHOLE,) * (len(flips) + receivers),
         scratch_shapes=[
             pltpu.VMEM((2 * rows, span), jnp.float32),
             pltpu.VMEM((half, span), jnp.float32),
@@ -214,53 +215,36 @@
         cost_estimate=LIGHT,
         compiler_params=ROOM,
     )(both, got, stay, swapped, mate_swapped, dinv)
-
-
-def collect_kernel(*refs):
-    arrived, (_, keep, send) = refs[:-3], refs[-3:]
-    share = keep.shape[0]
-    span = refs[0].shape[1]
-    here = (lax.axis_index("row") & 1) * share
+    return outs[: len(flips)], outs[len(flips) :]
+
+
+def close_kernel(count, *refs):
+    met, arrived = refs[:count], refs[count:-2]
+    off_diag, diag_block = refs[-2:]
+    span = arrived[0].shape[1]
     for flip, piece in enumerate(arrived):
-        spot = pl.ds(pl.multiple_of((lax.axis_index("col") ^ flip) * span, LANES), span)
-        keep[:, spot] = piece[pl.ds(pl.multiple_of(here, 8), share), :]
-        send[:, spot] = piece[pl.ds(pl.multiple_of(share - here, 8), share), :]
-
-
-def collect(arrived, along):
-    flips = len(arrived)
-    share, span = arrived[0].shape[0] // 2, arrived[0].shape[1]
+        first = pl.multiple_of((lax.axis_index("col") ^ flip) * span, LANES)
+        off_diag[:, pl.ds(first, span)] = piece[...]
+    diag_block[...] = sum([piece[...] for piece in met[1:]], met[0][...])
+
+
+def close(arrived, met):
+    share, span = arrived[0].shape
     if span % LANES:
         me = lax.axis_index("col")
-        row_bit = lax.axis_index("row") & 1
-        laid = jnp.concatenate([lax.select_n(me ^ j, *arrived) for j in range(flips)], axis=1)
-        laid = laid.reshape(2, share, span * flips)
-        return [lax.dynamic_index_in_dim(laid, row_bit ^ k, 0, keepdims=False) for k in range(2)]
-    part = jax.ShapeDtypeStruct((share, span * flips), jnp.float32)
-    return pl.pallas_call(
-        collect_kernel,
-        out_shape=(part, part),
-        in_specs=[WHOLE] * flips + [pl.BlockSpec(memory_space=pl.ANY)],
+        laid = [lax.select_n(me ^ j, *arrived) for j in range(len(arrived))]
+        return jnp.concatenate(laid, axis=1), sum(met[1:], met[0])
+    return pl.pallas_call(
+        functools.partial(close_kernel, len(met)),
+        out_shape=(
+            jax.ShapeDtypeStruct((share, span * len(arrived)), jnp.float32),
+            jax.ShapeDtypeStruct(met[0].shape, jnp.float32),
+        ),
+        in_specs=[WHOLE] * (len(arrived) + len(met)),
         out_specs=(WHOLE, WHOLE),
         cost_estimate=LIGHT,
         compiler_params=ROOM,
-    )(*arrived, along)
-
-
-def close_kernel(keep, came, total, off_diag, diag_block):
-    off_diag[...] = keep[...] + came[...]
-    diag_block[...] = total[...]
-
-
-def close(keep, came, total):
-    return pl.pallas_call(
-        close_kernel,
-        out_shape=[jax.ShapeDtypeStruct(x.shape, jnp.float32) for x in (keep, total)],
-        in_specs=[WHOLE] * 3,
-        out_specs=[WHOLE, WHOLE],
-        cost_estimate=LIGHT,
-        compiler_params=ROOM,
-    )(keep, came, total)
+    )(*met, *arrived)
 
 
 def pick_kernel(block_cols, b, presence, blocks, swapped, held):
@@ -344,15 +328,15 @@
     held, swapped = stacked(held), stacked(swapped)
     mate, mate_swapped = flipped(held, "col", 1), flipped(swapped, "col", 1)
 
-    both, outward = partials(held, mate, ours, theirs, columns, groups_col)
+    both = partials(held, mate, ours, theirs, columns)
     got = flipped(both, "row", 1)
-    arrived = [outward[0]] + [flipped(outward[f], "col", f) for f in range(1, groups_col)]
-    flips = (0,) + tuple(range(groups_row - 2, 0, -2))
-    along = finish(both, got, stay, swapped, mate_swapped, dinv, flips)
-    keep, send = collect(arrived, along[0])
-    came = flipped(send, "row", 1)
+    flips = (0, *range(groups_row - 2, 0, -2))
+    along, outward = finish(
+        both, got, stay, swapped, mate_swapped, dinv, order, flips, groups_col
+    )
     met = [flipped(piece, "row", flip) if flip else piece for flip, piece in zip(flips, along)]
-    off_diag, diag_block = close(keep, came, sum(met[1:], met[0]))
+    arrived = [flipped(piece, "col", f) if f else piece for f, piece in enumerate(outward)]
+    off_diag, diag_block = close(arrived, met)
     return (off_diag.reshape(block_rows, 1, share, width), diag_block)
 
 

time: 33.1 us -> 32.7 us (0.988)
  starting transfers between devices: 20.4 us -> 18 us
  waiting for transfers between devices: 8.16 us -> 10.3 us
    ppermute x17 -> x16, starting transfers between devices: 18 us -> 15.6 us  [flipped(): lax.ppermute(value, axis, [(i, i ^ flip) for i in range(lax.axis_size(axi...]
    ppermute x17 -> x16, waiting for transfers between devices: 8.15 us -> 10.3 us  [flipped(): lax.ppermute(value, axis, [(i, i ^ flip) for i in range(lax.axis_size(axi...]
    pallas_call x3 -> x2, Pallas kernels: 1 us -> 0.99 us  [the longest x1 0.66 us: close(): pl.pallas_call(functools.partial(close_kernel, len(met)), out_shape=(jax....]
  transfers between devices with their start and end apart: 19 -> 18, of which waited for: 7 -> 6; matrix products, arithmetic and copies ran while one was open for 0% -> 0% of each run, Pallas kernels for 3% -> 2%
where the time goes in v24:
time: 32.7 us; the launch traced here: 32.6 us
  starting transfers between devices  18 us (55%)
  waiting for transfers between devices  10.3 us (31%)
  Pallas kernels  3.53 us (11%)
  between operations  0.77 us (2%)
    ppermute x16, starting transfers between devices, flipped(): lax.ppermute(value, axis, [(i, i ^ flip) for i in range(lax.axis_size(axi...  15.6 us
    ppermute x16, waiting for transfers between devices, flipped(): lax.ppermute(value, axis, [(i, i ^ flip) for i in range(lax.axis_size(axi...  10.3 us
    ppermute x2, starting transfers between devices, crossed(): return lax.ppermute(swap, ('row', 'col'), cross)  2.43 us
    pallas_call x1, Pallas kernels, prepare(): pl.pallas_call(functools.partial(prepare_kernel, tall), out_shape=(jax.Sh...  1.83 us
    pallas_call x1, Pallas kernels, close(): pl.pallas_call(functools.partial(close_kernel, len(met)), out_shape=(jax....  0.66 us
  transfers between devices with their start and end apart: 18, of which 6 were waited for; matrix products, arithmetic and copies ran while one was open for 0% of the time, Pallas kernels for 2%

profile of v24, /device:TPU:0, one launch (start us, length us, event | category | flops | bytes accessed | tf_op | source)
XLA Modules:
  0.0 32.6 jit_solution(18257217539963641629)
XLA Ops:
  0.6 1.8 %shard_map.59 = (f32[128,128]{1,0:T(8,128)}, f32[128,128]{1,0:T(8,128)}, f32[128,128]{1,0:T(8,128)}) custom-call(s32[1,2]{1,0:T(1,128)} %bitcast.9, f32[256,128]{1,0:T(8,128)} %bitcast.4, f32[128,512]{1,0:T(8,128)} %bitcast.7), custom_call_target="tpu_custom_call" | custom-call | flops 1000 | bytes 1000 | tf_op jit(solution)/shard_map/pallas_call | solution.py:89
  2.5 2.4 %collective-permute-start = (f32[128,128]{1,0:T(8,128)}, f32[128,128]{1,0:T(8,128)S(1)}, u32[]{:S(2)}, u32[]{:S(2)}) collective-permute-start(f32[128,128]{1,0:T(8,128)} %get-tuple-element.15), channel_id=1, source_target_pairs={{0,5},{1,4},{2,7},{3,6},{4,1},{5,0},{6,3},{7,2},{8,13},{9,12},{10,... | collective-permute-start | bytes 196616 | tf_op jit(solution)/shard_map/ppermute | solution.py:294
  4.9 3.4 %collective-permute-start.7 = (f32[128,128]{1,0:T(8,128)}, f32[128,128]{1,0:T(8,128)S(1)}, u32[]{:S(2)}, u32[]{:S(2)}) collective-permute-start(f32[128,128]{1,0:T(8,128)} %get-tuple-element.17.refs_0_), channel_id=1, source_target_pairs={{0,16},{4,20},{8,24},{12,28},{16,0},{20,4},{24,8},{28,12},{1,17},{... | collective-permute-start | bytes 196616 | tf_op jit(solution)/shard_map/ppermute | solution.py:18
  8.3 1.6 %collective-permute-start.8 = (f32[128,128]{1,0:T(8,128)}, f32[128,128]{1,0:T(8,128)S(1)}, u32[]{:S(2)}, u32[]{:S(2)}) collective-permute-start(f32[128,128]{1,0:T(8,128)} %get-tuple-element.17.refs_0_), channel_id=1, source_target_pairs={{0,8},{4,12},{8,0},{12,4},{16,24},{20,28},{24,16},{28,20},{1,9},{5... | collective-permute-start | bytes 196616 | tf_op jit(solution)/shard_map/ppermute | solution.py:18
  9.8 0.1 shard_map.60.refs_0_
  9.9 1.5 %collective-permute-start.3 = (f32[128,128]{1,0:T(8,128)S(1)}, f32[128,128]{1,0:T(8,128)S(1)}, u32[]{:S(2)}, u32[]{:S(2)}) collective-permute-start(f32[128,128]{1,0:T(8,128)S(1)} %shard_map.60.refs_0_), channel_id=1, source_target_pairs={{0,2},{1,3},{2,0},{3,1},{4,6},{5,7},{6,4},{7,5},{8,10},{9,11},{10,... | collective-permute-start | bytes 196616 | tf_op jit(solution)/shard_map/ppermute | solution.py:18
  11.6 0.5 %collective-permute-start.4 = (f32[128,128]{1,0:T(8,128)S(1)}, f32[128,128]{1,0:T(8,128)S(1)}, u32[]{:S(2)}, u32[]{:S(2)}) collective-permute-start(f32[128,128]{1,0:T(8,128)S(1)} %shard_map.61.refs_1_), channel_id=1, source_target_pairs={{0,2},{1,3},{2,0},{3,1},{4,6},{5,7},{6,4},{7,5},{8,10},{9,11},{10,... | collective-permute-start | bytes 196616 | tf_op jit(solution)/shard_map/ppermute | solution.py:18
  12.1 0.9 %collective-permute-start.9 = (f32[128,128]{1,0:T(8,128)S(1)}, f32[128,128]{1,0:T(8,128)S(1)}, u32[]{:S(2)}, u32[]{:S(2)}) collective-permute-start(f32[128,128]{1,0:T(8,128)S(1)} %collective-permute-done.7.refs_1_), channel_id=1, source_target_pairs={{0,8},{4,12},{8,0},{12,4},{16,24},{20,28},{24,16},{28,20},{1,9},{5... | collective-permute-start | bytes 196616 | tf_op jit(solution)/shard_map/ppermute | solution.py:18
  13.1 0.6 %collective-permute-start.11 = (f32[2,128,128]{2,1,0:T(8,128)S(1)}, f32[2,128,128]{2,1,0:T(8,128)S(1)}, u32[]{:S(2)}, u32[]{:S(2)}) collective-permute-start(f32[2,128,128]{2,1,0:T(8,128)S(1)} %shard_map.66.swapped), channel_id=1, source_target_pairs={{0,1},{1,0},{2,3},{3,2},{4,5},{5,4},{6,7},{7,6},{8,9},{9,8},{10,11... | collective-permute-start | bytes 393224 | tf_op jit(solution)/shard_map/ppermute | solution.py:18
  13.7 1.0 %collective-permute-done.3.refs_2_ = f32[128,128]{1,0:T(8,128)S(1)} collective-permute-done((f32[128,128]{1,0:T(8,128)S(1)}, f32[128,128]{1,0:T(8,128)S(1)}, u32[]{:S(2)}, u32[]{:S(2)}) %collective-permute-start.3) | collective-permute-done | bytes 65568 | tf_op jit(solution)/shard_map/ppermute | solution.py:18
  14.6 1.2 %collective-permute-done.4.refs_3_ = f32[128,128]{1,0:T(8,128)S(1)} collective-permute-done((f32[128,128]{1,0:T(8,128)S(1)}, f32[128,128]{1,0:T(8,128)S(1)}, u32[]{:S(2)}, u32[]{:S(2)}) %collective-permute-start.4) | collective-permute-done | bytes 65568 | tf_op jit(solution)/shard_map/ppermute | solution.py:18
  15.8 0.5 %collective-permute-done.9.refs_3_ = f32[128,128]{1,0:T(8,128)S(1)} collective-permute-done((f32[128,128]{1,0:T(8,128)S(1)}, f32[128,128]{1,0:T(8,128)S(1)}, u32[]{:S(2)}, u32[]{:S(2)}) %collective-permute-start.9) | collective-permute-done | bytes 65568 | tf_op jit(solution)/shard_map/ppermute | solution.py:18
  16.4 0.7 %collective-permute-done.6.refs_5_ = f32[128,128]{1,0:T(8,128)S(1)} collective-permute-done((f32[128,128]{1,0:T(8,128)S(1)}, f32[128,128]{1,0:T(8,128)S(1)}, u32[]{:S(2)}, u32[]{:S(2)}) %collective-permute-start.6) | collective-permute-done | bytes 65568 | tf_op jit(solution)/shard_map/ppermute | solution.py:18
  17.1 0.4 %shard_map.64.both = f32[256,128]{1,0:T(8,128)S(1)} custom-call(f32[2,128,128]{2,1,0:T(8,128)S(1)} %shard_map.62.refs_0_, f32[2,128,128]{2,1,0:T(8,128)S(1)} %collective-permute-done.2.refs_1_, f32[128,128]{1,0:T(8,128)S(1)} %collective-permute-done.3.refs_2_, f32[128,128]{1,0:T(8,128)S(1)} %collective-permute-done.4.refs_3_, ...), custom_call_target="tpu_custom_call" | custom-call | flops 1000 | bytes 1000 | tf_op jit(solution)/shard_map/pallas_call | solution.py:147
  17.5 1.6 %collective-permute-start.10 = (f32[256,128]{1,0:T(8,128)S(1)}, f32[256,128]{1,0:T(8,128)S(1)}, u32[]{:S(2)}, u32[]{:S(2)}) collective-permute-start(f32[256,128]{1,0:T(8,128)S(1)} %shard_map.64.both), channel_id=1, source_target_pairs={{0,4},{4,0},{8,12},{12,8},{16,20},{20,16},{24,28},{28,24},{1,5},{5... | collective-permute-start | bytes 393224 | tf_op jit(solution)/shard_map/ppermute | solution.py:18
  19.0 0.1 shard_map.65.stay
  19.2 3.9 %collective-permute-done.10.got = f32[256,128]{1,0:T(8,128)S(1)} collective-permute-done((f32[256,128]{1,0:T(8,128)S(1)}, f32[256,128]{1,0:T(8,128)S(1)}, u32[]{:S(2)}, u32[]{:S(2)}) %collective-permute-start.10) | collective-permute-done | bytes 131104 | tf_op jit(solution)/shard_map/ppermute | solution.py:18
  23.1 0.3 %shard_map.67 = (f32[64,128]{1,0:T(8,128)S(1)}, f32[64,128]{1,0:T(8,128)S(1)}, f32[64,128]{1,0:T(8,128)S(1)}, f32[64,128]{1,0:T(8,128)S(1)}, f32[32,128]{1,0:T(8...) custom-call(f32[256,128]{1,0:T(8,128)S(1)} %shard_map.64.both, ...), custom_call_target="tpu_custom_call" | custom-call | flops 1000 | bytes 1000 | tf_op jit(solution)/shard_map/pallas_call | solution.py:206
  23.5 2.3 %collective-permute-start.12 = (f32[64,128]{1,0:T(8,128)S(1)}, f32[64,128]{1,0:T(8,128)S(1)}, u32[]{:S(2)}, u32[]{:S(2)}) collective-permute-start(f32[64,128]{1,0:T(8,128)S(1)} %get-tuple-element.19), channel_id=1, source_target_pairs={{0,24},{4,28},{8,16},{12,20},{16,8},{20,12},{24,0},{28,4},{1,25},{... | collective-permute-start | bytes 98312 | tf_op jit(solution)/shard_map/ppermute | solution.py:18
  25.8 2.1 %collective-permute-start.14 = (f32[64,128]{1,0:T(8,128)S(1)}, f32[64,128]{1,0:T(8,128)S(1)}, u32[]{:S(2)}, u32[]{:S(2)}) collective-permute-start(f32[64,128]{1,0:T(8,128)S(1)} %get-tuple-element.21), channel_id=1, source_target_pairs={{0,8},{4,12},{8,0},{12,4},{16,24},{20,28},{24,16},{28,20},{1,9},{5... | collective-permute-start | bytes 98312 | tf_op jit(solution)/shard_map/ppermute | solution.py:18
  28.0 0.6 %collective-permute-start.16 = (f32[32,128]{1,0:T(8,128)S(1)}, f32[32,128]{1,0:T(8,128)S(1)}, u32[]{:S(2)}, u32[]{:S(2)}) collective-permute-start(f32[32,128]{1,0:T(8,128)S(1)} %get-tuple-element.24), channel_id=1, source_target_pairs={{0,2},{1,3},{2,0},{3,1},{4,6},{5,7},{6,4},{7,5},{8,10},{9,11},{10,... | collective-permute-start | bytes 49160 | tf_op jit(solution)/shard_map/ppermute | solution.py:18
  28.6 0.4 %collective-permute-start.17 = (f32[32,128]{1,0:T(8,128)S(1)}, f32[32,128]{1,0:T(8,128)S(1)}, u32[]{:S(2)}, u32[]{:S(2)}) collective-permute-start(f32[32,128]{1,0:T(8,128)S(1)} %get-tuple-element.25), channel_id=1, source_target_pairs={{0,3},{1,2},{2,1},{3,0},{4,7},{5,6},{6,5},{7,4},{8,11},{9,10},{10,... | collective-permute-start | bytes 49160 | tf_op jit(solution)/shard_map/ppermute | solution.py:18
  28.9 2.9 %collective-permute-done.16.refs_6_ = f32[32,128]{1,0:T(8,128)S(1)} collective-permute-done((f32[32,128]{1,0:T(8,128)S(1)}, f32[32,128]{1,0:T(8,128)S(1)}, u32[]{:S(2)}, u32[]{:S(2)}) %collective-permute-start.16) | collective-permute-done | bytes 16416 | tf_op jit(solution)/shard_map/ppermute | solution.py:18
  31.9 0.7 %shard_map.68 = (f32[32,512]{1,0:T(8,128)}, f32[64,128]{1,0:T(8,128)}) custom-call(f32[64,128]{1,0:T(8,128)S(1)} %get-tuple-element.18.refs_0_, f32[64,128]{1,0:T(8,128)S(1)} %collective-permute-done.12.refs_1_, f32[64,128]{1,0:T(8,128)S(1)} %collective-permute-done.13.refs_2_, f32[64,128]{1,0:T(8,128)S(1)} %collective-permute-done.14.refs_3_, ...), custom_call_target="tpu_custom_call" | custom-call | flops 1000 | bytes 1000 | tf_op jit(solution)/shard_map/pallas_call | solution.py:237
  (32 shorter events, 0.4 us)
Async XLA Ops:
  0.6 9.2 %copy-start = (f32[1,1,128,2,1,128]{5,4,3,2,1,0:T(1,128)S(1)}, f32[1,1,128,2,1,128]{5,4,3,2,1,0:T(1,128)}, u32[]{:S(2)}) copy-start(f32[1,1,128,2,1,128]{5,4,3,2,1,0:T(1,128)} %param.4) | copy-start | bytes 393220
  2.5 7.4 %collective-permute-start = (f32[128,128]{1,0:T(8,128)}, f32[128,128]{1,0:T(8,128)S(1)}, u32[]{:S(2)}, u32[]{:S(2)}) collective-permute-start(f32[128,128]{1,0:T(8,128)} %get-tuple-element.15), channel_id=1, source_target_pairs={{0,5},{1,4},{2,7},{3,6},{4,1},{5,0},{6,3},{7,2},{8,13},{9,12},{10,... | collective-permute-start | bytes 196616 | tf_op jit(solution)/shard_map/ppermute | solution.py:294
  4.8 5.0 %copy-start.3 = (s32[1,1,2,1]{2,3,1,0:T(1,128)S(1)}, s32[1,1,2,1]{2,3,1,0:T(1,128)}, u32[]{:S(2)}) copy-start(s32[1,1,2,1]{2,3,1,0:T(1,128)} %param.5) | copy-start | bytes 28
  4.8 6.6 %collective-permute-start.1 = (f32[128,128]{1,0:T(8,128)}, f32[128,128]{1,0:T(8,128)S(1)}, u32[]{:S(2)}, u32[]{:S(2)}) collective-permute-start(f32[128,128]{1,0:T(8,128)} %get-tuple-element.16), channel_id=1, source_target_pairs={{0,5},{1,4},{2,7},{3,6},{4,1},{5,0},{6,3},{7,2},{8,13},{9,12},{10,... | collective-permute-start | bytes 196616 | tf_op jit(solution)/shard_map/ppermute | solution.py:294
  4.9 7.2 %collective-permute-start.7 = (f32[128,128]{1,0:T(8,128)}, f32[128,128]{1,0:T(8,128)S(1)}, u32[]{:S(2)}, u32[]{:S(2)}) collective-permute-start(f32[128,128]{1,0:T(8,128)} %get-tuple-element.17.refs_0_), channel_id=1, source_target_pairs={{0,16},{4,20},{8,24},{12,28},{16,0},{20,4},{24,8},{28,12},{1,17},{... | collective-permute-start | bytes 196616 | tf_op jit(solution)/shard_map/ppermute | solution.py:18
  8.3 4.8 %collective-permute-start.8 = (f32[128,128]{1,0:T(8,128)}, f32[128,128]{1,0:T(8,128)S(1)}, u32[]{:S(2)}, u32[]{:S(2)}) collective-permute-start(f32[128,128]{1,0:T(8,128)} %get-tuple-element.17.refs_0_), channel_id=1, source_target_pairs={{0,8},{4,12},{8,0},{12,4},{16,24},{20,28},{24,16},{28,20},{1,9},{5... | collective-permute-start | bytes 196616 | tf_op jit(solution)/shard_map/ppermute | solution.py:18
  9.9 4.7 %collective-permute-start.3 = (f32[128,128]{1,0:T(8,128)S(1)}, f32[128,128]{1,0:T(8,128)S(1)}, u32[]{:S(2)}, u32[]{:S(2)}) collective-permute-start(f32[128,128]{1,0:T(8,128)S(1)} %shard_map.60.refs_0_), channel_id=1, source_target_pairs={{0,2},{1,3},{2,0},{3,1},{4,6},{5,7},{6,4},{7,5},{8,10},{9,11},{10,... | collective-permute-start | bytes 196616 | tf_op jit(solution)/shard_map/ppermute | solution.py:18
  11.6 4.3 %collective-permute-start.4 = (f32[128,128]{1,0:T(8,128)S(1)}, f32[128,128]{1,0:T(8,128)S(1)}, u32[]{:S(2)}, u32[]{:S(2)}) collective-permute-start(f32[128,128]{1,0:T(8,128)S(1)} %shard_map.61.refs_1_), channel_id=1, source_target_pairs={{0,2},{1,3},{2,0},{3,1},{4,6},{5,7},{6,4},{7,5},{8,10},{9,11},{10,... | collective-permute-start | bytes 196616 | tf_op jit(solution)/shard_map/ppermute | solution.py:18
  12.1 4.3 %collective-permute-start.9 = (f32[128,128]{1,0:T(8,128)S(1)}, f32[128,128]{1,0:T(8,128)S(1)}, u32[]{:S(2)}, u32[]{:S(2)}) collective-permute-start(f32[128,128]{1,0:T(8,128)S(1)} %collective-permute-done.7.refs_1_), channel_id=1, source_target_pairs={{0,8},{4,12},{8,0},{12,4},{16,24},{20,28},{24,16},{28,20},{1,9},{5... | collective-permute-start | bytes 196616 | tf_op jit(solution)/shard_map/ppermute | solution.py:18
  13.0 3.4 %copy-start.4 = (f32[128,128]{1,0:T(8,128)S(1)}, f32[128,128]{1,0:T(8,128)}, u32[]{:S(2)}) copy-start(f32[128,128]{1,0:T(8,128)} %get-tuple-element.17.refs_0_) | copy-start | bytes 196612
  13.0 3.4 %collective-permute-start.2 = (f32[2,128,128]{2,1,0:T(8,128)S(1)}, f32[2,128,128]{2,1,0:T(8,128)S(1)}, u32[]{:S(2)}, u32[]{:S(2)}) collective-permute-start(f32[2,128,128]{2,1,0:T(8,128)S(1)} %shard_map.62.refs_0_), channel_id=1, source_target_pairs={{0,1},{1,0},{2,3},{3,2},{4,5},{5,4},{6,7},{7,6},{8,9},{9,8},{10,11... | collective-permute-start | bytes 393224 | tf_op jit(solution)/shard_map/ppermute | solution.py:18
  13.1 6.1 %collective-permute-start.11 = (f32[2,128,128]{2,1,0:T(8,128)S(1)}, f32[2,128,128]{2,1,0:T(8,128)S(1)}, u32[]{:S(2)}, u32[]{:S(2)}) collective-permute-start(f32[2,128,128]{2,1,0:T(8,128)S(1)} %shard_map.66.swapped), channel_id=1, source_target_pairs={{0,1},{1,0},{2,3},{3,2},{4,5},{5,4},{6,7},{7,6},{8,9},{9,8},{10,11... | collective-permute-start | bytes 393224 | tf_op jit(solution)/shard_map/ppermute | solution.py:18
  14.6 1.8 %collective-permute-start.5 = (f32[128,128]{1,0:T(8,128)S(1)}, f32[128,128]{1,0:T(8,128)S(1)}, u32[]{:S(2)}, u32[]{:S(2)}) collective-permute-start(f32[128,128]{1,0:T(8,128)S(1)} %collective-permute-done.3.refs_2_), channel_id=1, source_target_pairs={{0,1},{1,0},{2,3},{3,2},{4,5},{5,4},{6,7},{7,6},{8,9},{9,8},{10,11... | collective-permute-start | bytes 196616 | tf_op jit(solution)/shard_map/ppermute | solution.py:18
  15.8 1.3 %collective-permute-start.6 = (f32[128,128]{1,0:T(8,128)S(1)}, f32[128,128]{1,0:T(8,128)S(1)}, u32[]{:S(2)}, u32[]{:S(2)}) collective-permute-start(f32[128,128]{1,0:T(8,128)S(1)} %collective-permute-done.4.refs_3_), channel_id=1, source_target_pairs={{0,1},{1,0},{2,3},{3,2},{4,5},{5,4},{6,7},{7,6},{8,9},{9,8},{10,11... | collective-permute-start | bytes 196616 | tf_op jit(solution)/shard_map/ppermute | solution.py:18
  16.4 2.7 %copy-start.1 = (f32[1,1,128,512]{3,2,1,0:T(8,128)S(1)}, f32[1,1,128,512]{3,2,1,0:T(8,128)}, u32[]{:S(2)}) copy-start(f32[1,1,128,512]{3,2,1,0:T(8,128)} %param.6) | copy-start | bytes 786436
  17.5 5.6 %copy-start.2 = (f32[64,128]{1,0:T(8,128)S(1)}, f32[64,128]{1,0:T(8,128)}, u32[]{:S(2)}) copy-start(f32[64,128]{1,0:T(8,128)} %dinv.1) | copy-start | bytes 98308
  17.5 5.6 %collective-permute-start.10 = (f32[256,128]{1,0:T(8,128)S(1)}, f32[256,128]{1,0:T(8,128)S(1)}, u32[]{:S(2)}, u32[]{:S(2)}) collective-permute-start(f32[256,128]{1,0:T(8,128)S(1)} %shard_map.64.both), channel_id=1, source_target_pairs={{0,4},{4,0},{8,12},{12,8},{16,20},{20,16},{24,28},{28,24},{1,5},{5... | collective-permute-start | bytes 393224 | tf_op jit(solution)/shard_map/ppermute | solution.py:18
  23.5 5.1 %collective-permute-start.15 = (f32[32,128]{1,0:T(8,128)S(1)}, f32[32,128]{1,0:T(8,128)S(1)}, u32[]{:S(2)}, u32[]{:S(2)}) collective-permute-start(f32[32,128]{1,0:T(8,128)S(1)} %get-tuple-element.23), channel_id=1, source_target_pairs={{0,1},{1,0},{2,3},{3,2},{4,5},{5,4},{6,7},{7,6},{8,9},{9,8},{10,11... | collective-permute-start | bytes 49160 | tf_op jit(solution)/shard_map/ppermute | solution.py:18
  23.5 8.4 %collective-permute-start.12 = (f32[64,128]{1,0:T(8,128)S(1)}, f32[64,128]{1,0:T(8,128)S(1)}, u32[]{:S(2)}, u32[]{:S(2)}) collective-permute-start(f32[64,128]{1,0:T(8,128)S(1)} %get-tuple-element.19), channel_id=1, source_target_pairs={{0,24},{4,28},{8,16},{12,20},{16,8},{20,12},{24,0},{28,4},{1,25},{... | collective-permute-start | bytes 98312 | tf_op jit(solution)/shard_map/ppermute | solution.py:18
  25.8 6.1 %collective-permute-start.13 = (f32[64,128]{1,0:T(8,128)S(1)}, f32[64,128]{1,0:T(8,128)S(1)}, u32[]{:S(2)}, u32[]{:S(2)}) collective-permute-start(f32[64,128]{1,0:T(8,128)S(1)} %get-tuple-element.20), channel_id=1, source_target_pairs={{0,16},{4,20},{8,24},{12,28},{16,0},{20,4},{24,8},{28,12},{1,17},{... | collective-permute-start | bytes 98312 | tf_op jit(solution)/shard_map/ppermute | solution.py:18
  25.8 6.1 %collective-permute-start.14 = (f32[64,128]{1,0:T(8,128)S(1)}, f32[64,128]{1,0:T(8,128)S(1)}, u32[]{:S(2)}, u32[]{:S(2)}) collective-permute-start(f32[64,128]{1,0:T(8,128)S(1)} %get-tuple-element.21), channel_id=1, source_target_pairs={{0,8},{4,12},{8,0},{12,4},{16,24},{20,28},{24,16},{28,20},{1,9},{5... | collective-permute-start | bytes 98312 | tf_op jit(solution)/shard_map/ppermute | solution.py:18
  28.0 3.9 %collective-permute-start.16 = (f32[32,128]{1,0:T(8,128)S(1)}, f32[32,128]{1,0:T(8,128)S(1)}, u32[]{:S(2)}, u32[]{:S(2)}) collective-permute-start(f32[32,128]{1,0:T(8,128)S(1)} %get-tuple-element.24), channel_id=1, source_target_pairs={{0,2},{1,3},{2,0},{3,1},{4,6},{5,7},{6,4},{7,5},{8,10},{9,11},{10,... | collective-permute-start | bytes 49160 | tf_op jit(solution)/shard_map/ppermute | solution.py:18
  28.6 3.3 %collective-permute-start.17 = (f32[32,128]{1,0:T(8,128)S(1)}, f32[32,128]{1,0:T(8,128)S(1)}, u32[]{:S(2)}, u32[]{:S(2)}) collective-permute-start(f32[32,128]{1,0:T(8,128)S(1)} %get-tuple-element.25), channel_id=1, source_target_pairs={{0,3},{1,2},{2,1},{3,0},{4,7},{5,6},{6,5},{7,4},{8,11},{9,10},{10,... | collective-permute-start | bytes 49160 | tf_op jit(solution)/shard_map/ppermute | solution.py:18

commit v25 on v24

--- a/solution.py
+++ b/solution.py
@@ -123,7 +123,7 @@
     block_cols, rows, order = held.shape
     far = (count - 1) * block_cols
     ours, theirs, refs = refs[2 : 2 + far], refs[2 + far : 2 + 2 * far], refs[2 + 2 * far :]
-    columns, both = refs
+    columns, kept, sent = refs
     col_index = lax.axis_index("col")
     left, right = [], []
     for t in range(count):
@@ -136,96 +136,113 @@
             left.append(jnp.concatenate(pair, axis=0))
             right.append(columns[b * count + ((col_index >> 1) ^ t)])
     summed = product(jnp.concatenate(left, axis=1), jnp.concatenate(right, axis=0), ((1,), (0,)))
-    here = (col_index & 1) * rows
-    both[pl.ds(pl.multiple_of(here, 8), rows), :] = summed[:rows]
-    both[pl.ds(pl.multiple_of(rows - here, 8), rows), :] = summed[rows:]
+    same = (lax.axis_index("row") & 1) == (col_index & 1)
+    kept[...] = jnp.where(same, summed[:rows], summed[rows:])
+    sent[...] = jnp.where(same, summed[rows:], summed[:rows])
 
 
 def partials(held, mate, ours, theirs, columns):
     block_cols, rows, _ = held.shape
     operands = (held, mate, *ours, *theirs, columns)
+    part = jax.ShapeDtypeStruct((rows, columns.shape[2]), jnp.float32)
     return pl.pallas_call(
         functools.partial(partials_kernel, 1 + len(ours) // block_cols),
-        out_shape=jax.ShapeDtypeStruct((2 * rows, columns.shape[2]), jnp.float32),
+        out_shape=(part, part),
+        in_specs=[WHOLE] * len(operands),
+        out_specs=(WHOLE, WHOLE),
+        cost_estimate=LIGHT,
+        compiler_params=ROOM,
+    )(*operands)
+
+
+def halves_kernel(tall, own, stay, away, part):
+    row_bit = lax.axis_index("row") & 1
+    stay[...] = parity_half(own[...], tall, row_bit)
+    away[...] = parity_half(own[...], tall, 1 - row_bit)
+    share = part.shape[1]
+    upper = (lax.axis_index("col") & 1) == 1
+    part[...] = jnp.where(upper, stay[:, share:], stay[:, :share])
+
+
+def halves(own, tall):
+    rows, width = own.shape
+    half = jax.ShapeDtypeStruct((rows, width // 2), jnp.float32)
+    return pl.pallas_call(
+        functools.partial(halves_kernel, tall),
+        out_shape=(half, half, jax.ShapeDtypeStruct((rows, width // 4), jnp.float32)),
+        in_specs=[WHOLE],
+        out_specs=(WHOLE,) * 3,
+        cost_estimate=LIGHT,
+        compiler_params=ROOM,
+    )(own)
+
+
+def terms_kernel(kept, sent, stay, away, swapped, mate_swapped, part, mate_part, dinv, terms):
+    row_index = lax.axis_index("row")
+    row_bit = row_index & 1
+    col_bit = lax.axis_index("col") & 1
+    depth = stay.shape[1] // swapped.shape[2]
+    near = [
+        jnp.where(row_bit == col_bit, swapped[j], mate_swapped[j]) for j in range(depth)
+    ]
+    far = [
+        jnp.where(col_bit == 0, part[...], mate_part[...]),
+        jnp.where(col_bit == 0, mate_part[...], part[...]),
+    ]
+    partial_pair = jnp.concatenate([kept[...], sent[...]], axis=0)
+    shape = (terms.shape[0],) + terms.shape[2:]
+    for slot, own, other in ((row_bit, stay, near), (1 - row_bit, away, far)):
+        factors = jnp.concatenate([own[...], jnp.concatenate(other, axis=1)], axis=0)
+        terms[:, slot] = product(factors, partial_pair, ((0,), (0,))).reshape(shape)
+    line = row_index >> 1
+    terms[line, row_bit] = terms[line, row_bit] + dinv[...]
+
+
+def diagonal_terms(kept, sent, stay, away, swapped, mate_swapped, part, mate_part, dinv):
+    tall, span = dinv.shape[0], kept.shape[1]
+    operands = (kept, sent, stay, away, swapped, mate_swapped, part, mate_part, dinv)
+    return pl.pallas_call(
+        terms_kernel,
+        out_shape=jax.ShapeDtypeStruct((stay.shape[1] // tall, 2, tall, span), jnp.float32),
         in_specs=[WHOLE] * len(operands),
         out_specs=WHOLE,
-        cost_estimate=LIGHT,
+        cost_estimate=pl.CostEstimate(flops=HEAVY, bytes_accessed=1000, transcendentals=0),
         compiler_params=ROOM,
     )(*operands)
 
 
-def stay_kernel(tall, own, stay):
-    stay[...] = parity_half(own[...], tall, lax.axis_index("row") & 1)
-
-
-def stay_half(own, tall):
-    rows, width = own.shape
-    return pl.pallas_call(
-        functools.partial(stay_kernel, tall),
-        out_shape=jax.ShapeDtypeStruct((rows, width // 2), jnp.float32),
-        in_specs=[WHOLE],
-        out_specs=WHOLE,
-        cost_estimate=LIGHT,
-        compiler_params=ROOM,
-    )(own)
-
-
-def finish_kernel(order, flips, both, got, stay, swapped, mate_swapped, dinv, *refs):
-    update, terms = refs[-2:]
-    along, outward = refs[: len(flips)], refs[len(flips) : -2]
-    rows = stay.shape[0]
-    row_index = lax.axis_index("row")
-    col_index = lax.axis_index("col")
-    here = (row_index & 1) * rows
-    update[...] = both[...] + got[...]
-    mine = update[pl.ds(pl.multiple_of(here, 8), rows), :]
-    other = update[pl.ds(pl.multiple_of(rows - here, 8), rows), :]
-    same = (row_index & 1) == (col_index & 1)
-    depth = stay.shape[1] // swapped.shape[2]
-    near = [jnp.where(same, swapped[j], mate_swapped[j]) for j in range(depth)]
-    factors = jnp.concatenate([stay[...], jnp.concatenate(near, axis=1)], axis=0)
-    terms[...] = product(factors, jnp.concatenate([mine, other], axis=0), ((0,), (0,)))
-    tall = dinv.shape[0]
-    for flip, piece in zip(flips, along):
-        slot = ((row_index ^ flip) >> 1) * tall
-        piece[...] = terms[pl.ds(pl.multiple_of(slot, 8), tall), :]
-    along[0][...] = along[0][...] + dinv[...]
+def outward_kernel(order, kept, got, *refs):
+    outward, update = refs[:-1], refs[-1]
+    rows = kept.shape[0]
+    update[...] = kept[...] + got[...]
     share = order // len(outward)
     for flip, piece in enumerate(outward):
-        start = here + (col_index ^ flip) * share
+        start = (lax.axis_index("col") ^ flip) * share
         for a in range(rows // order):
             picked = update[pl.ds(pl.multiple_of(a * order + start, 8), share), :]
             piece[pl.ds(a * share, share), :] = -picked
 
 
-def finish(both, got, stay, swapped, mate_swapped, dinv, order, flips, receivers):
-    rows, half = stay.shape
-    span = both.shape[1]
-    along = (jax.ShapeDtypeStruct(dinv.shape, jnp.float32),) * len(flips)
-    outward = (jax.ShapeDtypeStruct((rows // receivers, span), jnp.float32),) * receivers
-    outs = pl.pallas_call(
-        functools.partial(finish_kernel, order, flips),
-        out_shape=along + outward,
-        in_specs=[WHOLE] * 6,
-        out_specs=(WHOLE,) * (len(flips) + receivers),
-        scratch_shapes=[
-            pltpu.VMEM((2 * rows, span), jnp.float32),
-            pltpu.VMEM((half, span), jnp.float32),
-        ],
-        cost_estimate=LIGHT,
-        compiler_params=ROOM,
-    )(both, got, stay, swapped, mate_swapped, dinv)
-    return outs[: len(flips)], outs[len(flips) :]
-
-
-def close_kernel(count, *refs):
-    met, arrived = refs[:count], refs[count:-2]
-    off_diag, diag_block = refs[-2:]
+def outward_pieces(kept, got, order, receivers):
+    rows, span = kept.shape
+    return pl.pallas_call(
+        functools.partial(outward_kernel, order),
+        out_shape=(jax.ShapeDtypeStruct((rows // receivers, span), jnp.float32),) * receivers,
+        in_specs=[WHOLE] * 2,
+        out_specs=(WHOLE,) * receivers,
+        scratch_shapes=[pltpu.VMEM((rows, span), jnp.float32)],
+        cost_estimate=LIGHT,
+        compiler_params=ROOM,
+    )(kept, got)
+
+
+def close_kernel(met, *refs):
+    arrived, off_diag, diag_block = refs[:-2], refs[-2], refs[-1]
     span = arrived[0].shape[1]
     for flip, piece in enumerate(arrived):
         first = pl.multiple_of((lax.axis_index("col") ^ flip) * span, LANES)
         off_diag[:, pl.ds(first, span)] = piece[...]
-    diag_block[...] = sum([piece[...] for piece in met[1:]], met[0][...])
+    diag_block[...] = jnp.sum(met[...], axis=0)
 
 
 def close(arrived, met):
@@ -233,18 +250,18 @@
     if span % LANES:
         me = lax.axis_index("col")
         laid = [lax.select_n(me ^ j, *arrived) for j in range(len(arrived))]
-        return jnp.concatenate(laid, axis=1), sum(met[1:], met[0])
-    return pl.pallas_call(
-        functools.partial(close_kernel, len(met)),
+        return jnp.concatenate(laid, axis=1), met.sum(axis=0)
+    return pl.pallas_call(
+        close_kernel,
         out_shape=(
             jax.ShapeDtypeStruct((share, span * len(arrived)), jnp.float32),
-            jax.ShapeDtypeStruct(met[0].shape, jnp.float32),
+            jax.ShapeDtypeStruct(met.shape[1:], jnp.float32),
         ),
-        in_specs=[WHOLE] * (len(arrived) + len(met)),
+        in_specs=[WHOLE] * (1 + len(arrived)),
         out_specs=(WHOLE, WHOLE),
         cost_estimate=LIGHT,
         compiler_params=ROOM,
-    )(*met, *arrived)
+    )(met, *arrived)
 
 
 def pick_kernel(block_cols, b, presence, blocks, swapped, held):
@@ -319,7 +336,9 @@
     tall = width // groups_row
     mine, swaps = prepare(marks, blocks, own, span, tall)
     swapped = [crossed(swap) for swap in swaps]
-    stay = stay_half(own, tall)
+    stay, away, part = halves(own, tall)
+    part = flipped(part, "row", 1)
+    mate_part = flipped(part, "col", 1)
     columns = along_line(mine, order)
     held = [pick(marks, blocks, swapped[b], b) for b in range(block_cols)]
     far = [(flip, piece) for flip in range(2, groups_col, 2) for piece in held]
@@ -328,13 +347,13 @@
     held, swapped = stacked(held), stacked(swapped)
     mate, mate_swapped = flipped(held, "col", 1), flipped(swapped, "col", 1)
 
-    both = partials(held, mate, ours, theirs, columns)
-    got = flipped(both, "row", 1)
-    flips = (0, *range(groups_row - 2, 0, -2))
-    along, outward = finish(
-        both, got, stay, swapped, mate_swapped, dinv, order, flips, groups_col
+    kept, sent = partials(held, mate, ours, theirs, columns)
+    got = flipped(sent, "row", 1)
+    terms = diagonal_terms(
+        kept, sent, stay, away, swapped, mate_swapped, part, mate_part, dinv
     )
-    met = [flipped(piece, "row", flip) if flip else piece for flip, piece in zip(flips, along)]
+    met = lax.all_to_all(terms.reshape(groups_row, tall, span), "row", 0, 0)
+    outward = outward_pieces(kept, got, order, groups_col)
     arrived = [flipped(piece, "col", f) if f else piece for f, piece in enumerate(outward)]
     off_diag, diag_block = close(arrived, met)
     return (off_diag.reshape(block_rows, 1, share, width), diag_block)

time: 32.7 us -> 36.5 us (1.12)
  starting transfers between devices: 18 us -> 19.9 us
  Pallas kernels: 3.53 us -> 4.46 us
  waiting for transfers between devices: 10.3 us -> 11.1 us
    all_to_all x0 -> x1, starting transfers between devices: none -> 3.84 us  [local(): met = lax.all_to_all(terms.reshape(groups_row, tall, span), 'row', 0, 0)]
    ppermute x16 -> x15, starting transfers between devices: 15.6 us -> 13.6 us  [flipped(): lax.ppermute(value, axis, [(i, i ^ flip) for i in range(lax.axis_size(axi...]
    pallas_call x3 -> x4, Pallas kernels: 1.13 us -> 2.02 us  [the longest x1 1.16 us: diagonal_terms(): pl.pallas_call(terms_kernel, out_shape=jax.ShapeDtypeStruct((stay.shape[1...]
    ppermute x16 -> x15, waiting for transfers between devices: 10.3 us -> 11.1 us  [flipped(): lax.ppermute(value, axis, [(i, i ^ flip) for i in range(lax.axis_size(axi...]
  transfers between devices with their start and end apart: 18 -> 18, of which waited for: 6 -> 8; matrix products, arithmetic and copies ran while one was open for 0% -> 0% of each run, Pallas kernels for 2% -> 2%
where the time goes in v25:
time: 36.5 us; the launch traced here: 36.2 us
  starting transfers between devices  19.9 us (55%)
  waiting for transfers between devices  11.1 us (30%)
  Pallas kernels  4.46 us (12%)
  between operations  0.77 us (2%)
    ppermute x15, starting transfers between devices, flipped(): lax.ppermute(value, axis, [(i, i ^ flip) for i in range(lax.axis_size(axi...  13.6 us
    ppermute x15, waiting for transfers between devices, flipped(): lax.ppermute(value, axis, [(i, i ^ flip) for i in range(lax.axis_size(axi...  11.1 us
    all_to_all x1, starting transfers between devices, local(): met = lax.all_to_all(terms.reshape(groups_row, tall, span), 'row', 0, 0)  3.84 us
    ppermute x2, starting transfers between devices, crossed(): return lax.ppermute(swap, ('row', 'col'), cross)  2.41 us
    pallas_call x1, Pallas kernels, prepare(): pl.pallas_call(functools.partial(prepare_kernel, tall), out_shape=(jax.Sh...  1.86 us
    pallas_call x1, Pallas kernels, diagonal_terms(): pl.pallas_call(terms_kernel, out_shape=jax.ShapeDtypeStruct((stay.shape[1...  1.16 us
  transfers between devices with their start and end apart: 18, of which 8 were waited for; matrix products, arithmetic and copies ran while one was open for 0% of the time, Pallas kernels for 2%

profile of v25, /device:TPU:0, one launch (start us, length us, event | category | flops | bytes accessed | tf_op | source)
XLA Modules:
  0.0 36.2 jit_solution(4260604522452669430)
XLA Ops:
  0.6 1.9 %shard_map.59 = (f32[128,128]{1,0:T(8,128)}, f32[128,128]{1,0:T(8,128)}, f32[128,128]{1,0:T(8,128)}) custom-call(s32[1,2]{1,0:T(1,128)} %bitcast.10, f32[256,128]{1,0:T(8,128)} %bitcast.5, f32[128,512]{1,0:T(8,128)} %bitcast.8), custom_call_target="tpu_custom_call" | custom-call | flops 1000 | bytes 1000 | tf_op jit(solution)/shard_map/pallas_call | solution.py:89
  2.5 2.4 %collective-permute-start = (f32[128,128]{1,0:T(8,128)}, f32[128,128]{1,0:T(8,128)S(1)}, u32[]{:S(2)}, u32[]{:S(2)}) collective-permute-start(f32[128,128]{1,0:T(8,128)} %get-tuple-element.16), channel_id=1, source_target_pairs={{0,5},{1,4},{2,7},{3,6},{4,1},{5,0},{6,3},{7,2},{8,13},{9,12},{10,... | collective-permute-start | bytes 196616 | tf_op jit(solution)/shard_map/ppermute | solution.py:311
  4.9 3.4 %collective-permute-start.7 = (f32[128,128]{1,0:T(8,128)}, f32[128,128]{1,0:T(8,128)S(1)}, u32[]{:S(2)}, u32[]{:S(2)}) collective-permute-start(f32[128,128]{1,0:T(8,128)} %get-tuple-element.18.refs_0_), channel_id=1, source_target_pairs={{0,16},{4,20},{8,24},{12,28},{16,0},{20,4},{24,8},{28,12},{1,17},{... | collective-permute-start | bytes 196616 | tf_op jit(solution)/shard_map/ppermute | solution.py:18
  8.3 1.6 %collective-permute-start.8 = (f32[128,128]{1,0:T(8,128)}, f32[128,128]{1,0:T(8,128)S(1)}, u32[]{:S(2)}, u32[]{:S(2)}) collective-permute-start(f32[128,128]{1,0:T(8,128)} %get-tuple-element.18.refs_0_), channel_id=1, source_target_pairs={{0,8},{4,12},{8,0},{12,4},{16,24},{20,28},{24,16},{28,20},{1,9},{5... | collective-permute-start | bytes 196616 | tf_op jit(solution)/shard_map/ppermute | solution.py:18
  10.1 1.6 %collective-permute-start.11 = (f32[128,128]{1,0:T(8,128)S(1)}, f32[128,128]{1,0:T(8,128)S(1)}, u32[]{:S(2)}, u32[]{:S(2)}) collective-permute-start(f32[128,128]{1,0:T(8,128)S(1)} %get-tuple-element.23), channel_id=1, source_target_pairs={{0,4},{4,0},{8,12},{12,8},{16,20},{20,16},{24,28},{28,24},{1,5},{5... | collective-permute-start | bytes 196616 | tf_op jit(solution)/shard_map/ppermute | solution.py:18
  11.7 1.5 %collective-permute-start.3 = (f32[128,128]{1,0:T(8,128)S(1)}, f32[128,128]{1,0:T(8,128)S(1)}, u32[]{:S(2)}, u32[]{:S(2)}) collective-permute-start(f32[128,128]{1,0:T(8,128)S(1)} %shard_map.60.refs_0_), channel_id=1, source_target_pairs={{0,2},{1,3},{2,0},{3,1},{4,6},{5,7},{6,4},{7,5},{8,10},{9,11},{10,... | collective-permute-start | bytes 196616 | tf_op jit(solution)/shard_map/ppermute | solution.py:18
  13.4 0.5 %collective-permute-start.4 = (f32[128,128]{1,0:T(8,128)S(1)}, f32[128,128]{1,0:T(8,128)S(1)}, u32[]{:S(2)}, u32[]{:S(2)}) collective-permute-start(f32[128,128]{1,0:T(8,128)S(1)} %shard_map.61.refs_1_), channel_id=1, source_target_pairs={{0,2},{1,3},{2,0},{3,1},{4,6},{5,7},{6,4},{7,5},{8,10},{9,11},{10,... | collective-permute-start | bytes 196616 | tf_op jit(solution)/shard_map/ppermute | solution.py:18
  13.9 0.5 %collective-permute-start.9 = (f32[128,128]{1,0:T(8,128)S(1)}, f32[128,128]{1,0:T(8,128)S(1)}, u32[]{:S(2)}, u32[]{:S(2)}) collective-permute-start(f32[128,128]{1,0:T(8,128)S(1)} %collective-permute-done.7.refs_1_), channel_id=1, source_target_pairs={{0,8},{4,12},{8,0},{12,4},{16,24},{20,28},{24,16},{28,20},{1,9},{5... | collective-permute-start | bytes 196616 | tf_op jit(solution)/shard_map/ppermute | solution.py:18
  14.5 0.6 %collective-permute-start.10 = (f32[2,128,128]{2,1,0:T(8,128)S(1)}, f32[2,128,128]{2,1,0:T(8,128)S(1)}, u32[]{:S(2)}, u32[]{:S(2)}) collective-permute-start(f32[2,128,128]{2,1,0:T(8,128)S(1)} %shard_map.66.swapped), channel_id=1, source_target_pairs={{0,1},{1,0},{2,3},{3,2},{4,5},{5,4},{6,7},{7,6},{8,9},{9,8},{10,11... | collective-permute-start | bytes 393224 | tf_op jit(solution)/shard_map/ppermute | solution.py:18
  15.0 1.1 %collective-permute-done.3.refs_2_ = f32[128,128]{1,0:T(8,128)S(1)} collective-permute-done((f32[128,128]{1,0:T(8,128)S(1)}, f32[128,128]{1,0:T(8,128)S(1)}, u32[]{:S(2)}, u32[]{:S(2)}) %collective-permute-start.3) | collective-permute-done | bytes 65568 | tf_op jit(solution)/shard_map/ppermute | solution.py:18
  16.1 1.5 %collective-permute-done.4.refs_3_ = f32[128,128]{1,0:T(8,128)S(1)} collective-permute-done((f32[128,128]{1,0:T(8,128)S(1)}, f32[128,128]{1,0:T(8,128)S(1)}, u32[]{:S(2)}, u32[]{:S(2)}) %collective-permute-start.4) | collective-permute-done | bytes 65568 | tf_op jit(solution)/shard_map/ppermute | solution.py:18
  17.7 0.5 %collective-permute-done.9.refs_3_ = f32[128,128]{1,0:T(8,128)S(1)} collective-permute-done((f32[128,128]{1,0:T(8,128)S(1)}, f32[128,128]{1,0:T(8,128)S(1)}, u32[]{:S(2)}, u32[]{:S(2)}) %collective-permute-start.9) | collective-permute-done | bytes 65568 | tf_op jit(solution)/shard_map/ppermute | solution.py:18
  18.2 0.7 %collective-permute-done.5.refs_4_ = f32[128,128]{1,0:T(8,128)S(1)} collective-permute-done((f32[128,128]{1,0:T(8,128)S(1)}, f32[128,128]{1,0:T(8,128)S(1)}, u32[]{:S(2)}, u32[]{:S(2)}) %collective-permute-start.5) | collective-permute-done | bytes 65568 | tf_op jit(solution)/shard_map/ppermute | solution.py:18
  18.9 0.5 %collective-permute-done.6.refs_5_ = f32[128,128]{1,0:T(8,128)S(1)} collective-permute-done((f32[128,128]{1,0:T(8,128)S(1)}, f32[128,128]{1,0:T(8,128)S(1)}, u32[]{:S(2)}, u32[]{:S(2)}) %collective-permute-start.6) | collective-permute-done | bytes 65568 | tf_op jit(solution)/shard_map/ppermute | solution.py:18
  19.4 0.4 %shard_map.64 = (f32[128,128]{1,0:T(8,128)S(1)}, f32[128,128]{1,0:T(8,128)S(1)}) custom-call(f32[2,128,128]{2,1,0:T(8,128)S(1)} %shard_map.62.refs_0_, f32[2,128,128]{2,1,0:T(8,128)S(1)} %collective-permute-done.2.refs_1_, f32[128,128]{1,0:T(8,128)S(1)} %collective-permute-done.3.refs_2_, f32[128,128]{1,0:T(8,128)S(1)} %collective-permute-done.4.refs_3_, ...), custom_call_target="tpu_custom_call" | custom-call | flops 1000 | bytes 1000 | tf_op jit(solution)/shard_map/pallas_call | solution.py:148
  19.8 1.2 %shard_map.67 = f32[4,2,64,128]{3,2,1,0:T(8,128)} custom-call(f32[128,128]{1,0:T(8,128)S(1)} %get-tuple-element.19.kept, f32[128,128]{1,0:T(8,128)S(1)} %get-tuple-element.20.sent, f32[128,256]{1,0:T(8,128)S(1)} %get-tuple-element.21.stay, f32[128,256]{1,0:T(8,128)S(1)} %get-tuple-element.22.away, f32[2,128,128]{2,1,0:T(8,128)S(1)} %shard_map.66.swapped, ...), custom_call_target="tpu_custom_call" | custom-call | flops 1000000000 | bytes 1000 | tf_op jit(solution)/shard_map/pallas_call | solution.py:204
  21.0 3.8 %all-to-all-start = ((f32[8,64,128]{2,1,0:T(8,128)}), f32[8,64,128]{2,1,0:T(8,128)S(1)}, u32[]{:S(2)}, u32[]{:S(2)}) async-start(f32[8,64,128]{2,1,0:T(8,128)} %bitcast.3), calls=%async_computation | async-start | bytes 524288 | tf_op jit(solution)/shard_map/all_to_all | solution.py:355
  24.8 2.0 %collective-permute-start.13 = (f32[128,128]{1,0:T(8,128)S(1)}, f32[128,128]{1,0:T(8,128)S(1)}, u32[]{:S(2)}, u32[]{:S(2)}) collective-permute-start(f32[128,128]{1,0:T(8,128)S(1)} %get-tuple-element.20.sent), channel_id=1, source_target_pairs={{0,4},{4,0},{8,12},{12,8},{16,20},{20,16},{24,28},{28,24},{1,5},{5... | collective-permute-start | bytes 196616 | tf_op jit(solution)/shard_map/ppermute | solution.py:18
  26.8 3.9 %collective-permute-done.13.got = f32[128,128]{1,0:T(8,128)S(1)} collective-permute-done((f32[128,128]{1,0:T(8,128)S(1)}, f32[128,128]{1,0:T(8,128)S(1)}, u32[]{:S(2)}, u32[]{:S(2)}) %collective-permute-start.13) | collective-permute-done | bytes 65568 | tf_op jit(solution)/shard_map/ppermute | solution.py:18
  30.8 1.6 %collective-permute-start.15 = (f32[32,128]{1,0:T(8,128)S(1)}, f32[32,128]{1,0:T(8,128)S(1)}, u32[]{:S(2)}, u32[]{:S(2)}) collective-permute-start(f32[32,128]{1,0:T(8,128)S(1)} %get-tuple-element.26), channel_id=1, source_target_pairs={{0,2},{1,3},{2,0},{3,1},{4,6},{5,7},{6,4},{7,5},{8,10},{9,11},{10,... | collective-permute-start | bytes 49160 | tf_op jit(solution)/shard_map/ppermute | solution.py:18
  32.4 0.3 collective-permute-start.16
  32.7 1.9 %collective-permute-done.15.refs_2_ = f32[32,128]{1,0:T(8,128)S(1)} collective-permute-done((f32[32,128]{1,0:T(8,128)S(1)}, f32[32,128]{1,0:T(8,128)S(1)}, u32[]{:S(2)}, u32[]{:S(2)}) %collective-permute-start.15) | collective-permute-done | bytes 16416 | tf_op jit(solution)/shard_map/ppermute | solution.py:18
  34.6 1.0 %collective-permute-done.16.refs_3_ = f32[32,128]{1,0:T(8,128)S(1)} collective-permute-done((f32[32,128]{1,0:T(8,128)S(1)}, f32[32,128]{1,0:T(8,128)S(1)}, u32[]{:S(2)}, u32[]{:S(2)}) %collective-permute-start.16) | collective-permute-done | bytes 16416 | tf_op jit(solution)/shard_map/ppermute | solution.py:18
  35.6 0.7 %shard_map.69 = (f32[32,512]{1,0:T(8,128)}, f32[64,128]{1,0:T(8,128)}) custom-call(f32[8,64,128]{2,1,0:T(8,128)S(1)} %all-to-all-done.met, f32[32,128]{1,0:T(8,128)S(1)} %get-tuple-element.24.refs_0_, f32[32,128]{1,0:T(8,128)S(1)} %collective-permute-done.14.refs_1_, f32[32,128]{1,0:T(8,128)S(1)} %collective-permute-done.15.refs_2_, ...), custom_call_target="tpu_custom_call" | custom-call | flops 1000 | bytes 1000 | tf_op jit(solution)/shard_map/pallas_call | solution.py:254
  (33 shorter events, 0.7 us)
Async XLA Ops:
  0.6 9.2 %copy-start.1 = (f32[1,1,128,512]{3,2,1,0:T(8,128)S(1)}, f32[1,1,128,512]{3,2,1,0:T(8,128)}, u32[]{:S(2)}) copy-start(f32[1,1,128,512]{3,2,1,0:T(8,128)} %param.6) | copy-start | bytes 786436
  2.5 9.1 %collective-permute-start = (f32[128,128]{1,0:T(8,128)}, f32[128,128]{1,0:T(8,128)S(1)}, u32[]{:S(2)}, u32[]{:S(2)}) collective-permute-start(f32[128,128]{1,0:T(8,128)} %get-tuple-element.16), channel_id=1, source_target_pairs={{0,5},{1,4},{2,7},{3,6},{4,1},{5,0},{6,3},{7,2},{8,13},{9,12},{10,... | collective-permute-start | bytes 196616 | tf_op jit(solution)/shard_map/ppermute | solution.py:311
  4.9 8.4 %collective-permute-start.1 = (f32[128,128]{1,0:T(8,128)}, f32[128,128]{1,0:T(8,128)S(1)}, u32[]{:S(2)}, u32[]{:S(2)}) collective-permute-start(f32[128,128]{1,0:T(8,128)} %get-tuple-element.17), channel_id=1, source_target_pairs={{0,5},{1,4},{2,7},{3,6},{4,1},{5,0},{6,3},{7,2},{8,13},{9,12},{10,... | collective-permute-start | bytes 196616 | tf_op jit(solution)/shard_map/ppermute | solution.py:311
  4.9 6.7 %copy-start = (f32[1,1,128,2,1,128]{5,4,3,2,1,0:T(1,128)S(1)}, f32[1,1,128,2,1,128]{5,4,3,2,1,0:T(1,128)}, u32[]{:S(2)}) copy-start(f32[1,1,128,2,1,128]{5,4,3,2,1,0:T(1,128)} %param.4) | copy-start | bytes 393220
  4.9 9.0 %collective-permute-start.7 = (f32[128,128]{1,0:T(8,128)}, f32[128,128]{1,0:T(8,128)S(1)}, u32[]{:S(2)}, u32[]{:S(2)}) collective-permute-start(f32[128,128]{1,0:T(8,128)} %get-tuple-element.18.refs_0_), channel_id=1, source_target_pairs={{0,16},{4,20},{8,24},{12,28},{16,0},{20,4},{24,8},{28,12},{1,17},{... | collective-permute-start | bytes 196616 | tf_op jit(solution)/shard_map/ppermute | solution.py:18
  8.3 6.1 %collective-permute-start.8 = (f32[128,128]{1,0:T(8,128)}, f32[128,128]{1,0:T(8,128)S(1)}, u32[]{:S(2)}, u32[]{:S(2)}) collective-permute-start(f32[128,128]{1,0:T(8,128)} %get-tuple-element.18.refs_0_), channel_id=1, source_target_pairs={{0,8},{4,12},{8,0},{12,4},{16,24},{20,28},{24,16},{28,20},{1,9},{5... | collective-permute-start | bytes 196616 | tf_op jit(solution)/shard_map/ppermute | solution.py:18
  10.1 1.6 %copy-start.2 = (s32[1,1,2,1]{2,3,1,0:T(1,128)S(1)}, s32[1,1,2,1]{2,3,1,0:T(1,128)}, u32[]{:S(2)}) copy-start(s32[1,1,2,1]{2,3,1,0:T(1,128)} %param.5) | copy-start | bytes 28
  10.1 4.4 %collective-permute-start.11 = (f32[128,128]{1,0:T(8,128)S(1)}, f32[128,128]{1,0:T(8,128)S(1)}, u32[]{:S(2)}, u32[]{:S(2)}) collective-permute-start(f32[128,128]{1,0:T(8,128)S(1)} %get-tuple-element.23), channel_id=1, source_target_pairs={{0,4},{4,0},{8,12},{12,8},{16,20},{20,16},{24,28},{28,24},{1,5},{5... | collective-permute-start | bytes 196616 | tf_op jit(solution)/shard_map/ppermute | solution.py:18
  11.7 4.4 %collective-permute-start.3 = (f32[128,128]{1,0:T(8,128)S(1)}, f32[128,128]{1,0:T(8,128)S(1)}, u32[]{:S(2)}, u32[]{:S(2)}) collective-permute-start(f32[128,128]{1,0:T(8,128)S(1)} %shard_map.60.refs_0_), channel_id=1, source_target_pairs={{0,2},{1,3},{2,0},{3,1},{4,6},{5,7},{6,4},{7,5},{8,10},{9,11},{10,... | collective-permute-start | bytes 196616 | tf_op jit(solution)/shard_map/ppermute | solution.py:18
  13.4 4.3 %collective-permute-start.4 = (f32[128,128]{1,0:T(8,128)S(1)}, f32[128,128]{1,0:T(8,128)S(1)}, u32[]{:S(2)}, u32[]{:S(2)}) collective-permute-start(f32[128,128]{1,0:T(8,128)S(1)} %shard_map.61.refs_1_), channel_id=1, source_target_pairs={{0,2},{1,3},{2,0},{3,1},{4,6},{5,7},{6,4},{7,5},{8,10},{9,11},{10,... | collective-permute-start | bytes 196616 | tf_op jit(solution)/shard_map/ppermute | solution.py:18
  13.9 4.3 %collective-permute-start.9 = (f32[128,128]{1,0:T(8,128)S(1)}, f32[128,128]{1,0:T(8,128)S(1)}, u32[]{:S(2)}, u32[]{:S(2)}) collective-permute-start(f32[128,128]{1,0:T(8,128)S(1)} %collective-permute-done.7.refs_1_), channel_id=1, source_target_pairs={{0,8},{4,12},{8,0},{12,4},{16,24},{20,28},{24,16},{28,20},{1,9},{5... | collective-permute-start | bytes 196616 | tf_op jit(solution)/shard_map/ppermute | solution.py:18
  14.4 3.8 %copy-start.3 = (f32[128,128]{1,0:T(8,128)S(1)}, f32[128,128]{1,0:T(8,128)}, u32[]{:S(2)}) copy-start(f32[128,128]{1,0:T(8,128)} %get-tuple-element.18.refs_0_) | copy-start | bytes 196612
  14.4 5.0 %collective-permute-start.2 = (f32[2,128,128]{2,1,0:T(8,128)S(1)}, f32[2,128,128]{2,1,0:T(8,128)S(1)}, u32[]{:S(2)}, u32[]{:S(2)}) collective-permute-start(f32[2,128,128]{2,1,0:T(8,128)S(1)} %shard_map.62.refs_0_), channel_id=1, source_target_pairs={{0,1},{1,0},{2,3},{3,2},{4,5},{5,4},{6,7},{7,6},{8,9},{9,8},{10,11... | collective-permute-start | bytes 393224 | tf_op jit(solution)/shard_map/ppermute | solution.py:18
  14.5 5.3 %collective-permute-start.10 = (f32[2,128,128]{2,1,0:T(8,128)S(1)}, f32[2,128,128]{2,1,0:T(8,128)S(1)}, u32[]{:S(2)}, u32[]{:S(2)}) collective-permute-start(f32[2,128,128]{2,1,0:T(8,128)S(1)} %shard_map.66.swapped), channel_id=1, source_target_pairs={{0,1},{1,0},{2,3},{3,2},{4,5},{5,4},{6,7},{7,6},{8,9},{9,8},{10,11... | collective-permute-start | bytes 393224 | tf_op jit(solution)/shard_map/ppermute | solution.py:18
  16.1 3.7 %collective-permute-start.12 = (f32[128,128]{1,0:T(8,128)S(1)}, f32[128,128]{1,0:T(8,128)S(1)}, u32[]{:S(2)}, u32[]{:S(2)}) collective-permute-start(f32[128,128]{1,0:T(8,128)S(1)} %collective-permute-done.11.part), channel_id=1, source_target_pairs={{0,1},{1,0},{2,3},{3,2},{4,5},{5,4},{6,7},{7,6},{8,9},{9,8},{10,11... | collective-permute-start | bytes 196616 | tf_op jit(solution)/shard_map/ppermute | solution.py:18
  17.7 1.3 %collective-permute-start.5 = (f32[128,128]{1,0:T(8,128)S(1)}, f32[128,128]{1,0:T(8,128)S(1)}, u32[]{:S(2)}, u32[]{:S(2)}) collective-permute-start(f32[128,128]{1,0:T(8,128)S(1)} %collective-permute-done.3.refs_2_), channel_id=1, source_target_pairs={{0,1},{1,0},{2,3},{3,2},{4,5},{5,4},{6,7},{7,6},{8,9},{9,8},{10,11... | collective-permute-start | bytes 196616 | tf_op jit(solution)/shard_map/ppermute | solution.py:18
  18.2 1.3 %collective-permute-start.6 = (f32[128,128]{1,0:T(8,128)S(1)}, f32[128,128]{1,0:T(8,128)S(1)}, u32[]{:S(2)}, u32[]{:S(2)}) collective-permute-start(f32[128,128]{1,0:T(8,128)S(1)} %collective-permute-done.4.refs_3_), channel_id=1, source_target_pairs={{0,1},{1,0},{2,3},{3,2},{4,5},{5,4},{6,7},{7,6},{8,9},{9,8},{10,11... | collective-permute-start | bytes 196616 | tf_op jit(solution)/shard_map/ppermute | solution.py:18
  18.2 1.6 %copy-start.4 = (f32[64,128]{1,0:T(8,128)S(1)}, f32[64,128]{1,0:T(8,128)}, u32[]{:S(2)}) copy-start(f32[64,128]{1,0:T(8,128)} %dinv.1) | copy-start | bytes 98308
  21.0 14.6 %all-to-all-start = ((f32[8,64,128]{2,1,0:T(8,128)}), f32[8,64,128]{2,1,0:T(8,128)S(1)}, u32[]{:S(2)}, u32[]{:S(2)}) async-start(f32[8,64,128]{2,1,0:T(8,128)} %bitcast.3), calls=%async_computation | async-start | bytes 524288 | tf_op jit(solution)/shard_map/all_to_all | solution.py:355
  24.8 5.9 %collective-permute-start.13 = (f32[128,128]{1,0:T(8,128)S(1)}, f32[128,128]{1,0:T(8,128)S(1)}, u32[]{:S(2)}, u32[]{:S(2)}) collective-permute-start(f32[128,128]{1,0:T(8,128)S(1)} %get-tuple-element.20.sent), channel_id=1, source_target_pairs={{0,4},{4,0},{8,12},{12,8},{16,20},{20,16},{24,28},{28,24},{1,5},{5... | collective-permute-start | bytes 196616 | tf_op jit(solution)/shard_map/ppermute | solution.py:18
  30.7 1.9 %collective-permute-start.14 = (f32[32,128]{1,0:T(8,128)S(1)}, f32[32,128]{1,0:T(8,128)S(1)}, u32[]{:S(2)}, u32[]{:S(2)}) collective-permute-start(f32[32,128]{1,0:T(8,128)S(1)} %get-tuple-element.25), channel_id=1, source_target_pairs={{0,1},{1,0},{2,3},{3,2},{4,5},{5,4},{6,7},{7,6},{8,9},{9,8},{10,11... | collective-permute-start | bytes 49160 | tf_op jit(solution)/shard_map/ppermute | solution.py:18
  30.8 3.8 %collective-permute-start.15 = (f32[32,128]{1,0:T(8,128)S(1)}, f32[32,128]{1,0:T(8,128)S(1)}, u32[]{:S(2)}, u32[]{:S(2)}) collective-permute-start(f32[32,128]{1,0:T(8,128)S(1)} %get-tuple-element.26), channel_id=1, source_target_pairs={{0,2},{1,3},{2,0},{3,1},{4,6},{5,7},{6,4},{7,5},{8,10},{9,11},{10,... | collective-permute-start | bytes 49160 | tf_op jit(solution)/shard_map/ppermute | solution.py:18
  32.4 3.2 %collective-permute-start.16 = (f32[32,128]{1,0:T(8,128)S(1)}, f32[32,128]{1,0:T(8,128)S(1)}, u32[]{:S(2)}, u32[]{:S(2)}) collective-permute-start(f32[32,128]{1,0:T(8,128)S(1)} %get-tuple-element.27), channel_id=1, source_target_pairs={{0,3},{1,2},{2,1},{3,0},{4,7},{5,6},{6,5},{7,4},{8,11},{9,10},{10,... | collective-permute-start | bytes 49160 | tf_op jit(solution)/shard_map/ppermute | solution.py:18

commit v26 on v24

--- a/solution.py
+++ b/solution.py
@@ -10,7 +10,7 @@
 LANES = 128
 WHOLE = pl.BlockSpec(memory_space=pltpu.VMEM)
 ROOM = pltpu.CompilerParams(vmem_limit_bytes=16 * 1024 * 1024)
-HEAVY = 10**9
+HEAVY = 10**8
 LIGHT = pl.CostEstimate(flops=1000, bytes_accessed=1000, transcendentals=0)
 
 
@@ -50,23 +50,23 @@
     return blocks[pl.ds(a * order * block_cols + b, order, stride=block_cols), :] * weight
 
 
-def prepare_kernel(tall, presence, blocks, factor, mine, *swaps):
+def prepare_kernel(tall, presence, blocks, factor, masked, swap, mine):
     rows, span = mine.shape
     mine[...] = factor[:, pl.ds(pl.multiple_of(lax.axis_index("col") * span, LANES), span)]
     row_bit = lax.axis_index("row") & 1
     same = row_bit == (lax.axis_index("col") & 1)
-    order = blocks.shape[1]
-    block_cols = blocks.shape[0] // rows
+    block_cols, _, order = masked.shape
+    for a in range(rows // order):
+        for b in range(block_cols):
+            block = masked_block(presence, blocks, block_cols, a, b)
+            masked[b, pl.ds(a * order, order), :] = block
     half = parity_half(factor[...], tall, 1 - row_bit)
-    for b, swap in enumerate(swaps):
-        for a in range(rows // order):
-            here = pl.ds(a * order, order)
-            part = half[a * order : (a + 1) * order, b * order : (b + 1) * order]
-            if b >= block_cols:
-                swap[here, :] = part
-                continue
-            block = masked_block(presence, blocks, block_cols, a, b)
-            swap[here, :] = jnp.where(same, part, block) if part.shape[1] else block
+    for b in range(swap.shape[0]):
+        part = half[:, b * order : (b + 1) * order]
+        if part.shape[1] and b < block_cols:
+            swap[b] = jnp.where(same, part, masked[b])
+        else:
+            swap[b] = part if part.shape[1] else masked[b]
 
 
 def prepare(presence, blocks, own, span, tall):
@@ -85,16 +85,18 @@
         half = parity_half(own, tall, 1 - row_bit).reshape(rows, -1, order).transpose(1, 0, 2)
         half = jnp.pad(half, ((0, depth - half.shape[0]), (0, 0), (0, 0)))
         padded = jnp.pad(masked, ((0, depth - block_cols), (0, 0), (0, 0)))
-        return mine, list(jnp.where(same, half, padded))
-    mine, *swaps = pl.pallas_call(
+        return masked, jnp.where(same, half, padded), mine
+    return pl.pallas_call(
         functools.partial(prepare_kernel, tall),
-        out_shape=(jax.ShapeDtypeStruct((rows, span), jnp.float32),)
-        + (jax.ShapeDtypeStruct((rows, order), jnp.float32),) * depth,
+        out_shape=(
+            jax.ShapeDtypeStruct((block_cols, rows, order), jnp.float32),
+            jax.ShapeDtypeStruct((depth, rows, order), jnp.float32),
+            jax.ShapeDtypeStruct((rows, span), jnp.float32),
+        ),
         in_specs=[WHOLE] * 3,
-        out_specs=(WHOLE,) * (1 + depth),
+        out_specs=(WHOLE,) * 3,
         cost_estimate=LIGHT,
     )(presence, blocks, own)
-    return mine, swaps
 
 
 def ordered_kernel(flips, *refs):
@@ -119,21 +121,14 @@
 
 
 def partials_kernel(count, *refs):
-    held, mate = refs[:2]
-    block_cols, rows, order = held.shape
-    far = (count - 1) * block_cols
-    ours, theirs, refs = refs[2 : 2 + far], refs[2 + far : 2 + 2 * far], refs[2 + 2 * far :]
-    columns, both = refs
+    pieces = refs[: 2 * count]
+    columns, both = refs[2 * count :]
+    block_cols, rows, _ = pieces[0].shape
     col_index = lax.axis_index("col")
     left, right = [], []
     for t in range(count):
         for b in range(block_cols):
-            if t:
-                at = (t - 1) * block_cols + b
-                pair = [ours[at][...], theirs[at][...]]
-            else:
-                pair = [held[b], mate[b]]
-            left.append(jnp.concatenate(pair, axis=0))
+            left.append(jnp.concatenate([pieces[t][b], pieces[count + t][b]], axis=0))
             right.append(columns[b * count + ((col_index >> 1) ^ t)])
     summed = product(jnp.concatenate(left, axis=1), jnp.concatenate(right, axis=0), ((1,), (0,)))
     here = (col_index & 1) * rows
@@ -141,17 +136,16 @@
     both[pl.ds(pl.multiple_of(rows - here, 8), rows), :] = summed[rows:]
 
 
-def partials(held, mate, ours, theirs, columns):
-    block_cols, rows, _ = held.shape
-    operands = (held, mate, *ours, *theirs, columns)
-    return pl.pallas_call(
-        functools.partial(partials_kernel, 1 + len(ours) // block_cols),
+def partials(pieces, columns):
+    rows = pieces[0].shape[1]
+    return pl.pallas_call(
+        functools.partial(partials_kernel, len(pieces) // 2),
         out_shape=jax.ShapeDtypeStruct((2 * rows, columns.shape[2]), jnp.float32),
-        in_specs=[WHOLE] * len(operands),
+        in_specs=[WHOLE] * (len(pieces) + 1),
         out_specs=WHOLE,
         cost_estimate=LIGHT,
         compiler_params=ROOM,
-    )(*operands)
+    )(*pieces, columns)
 
 
 def stay_kernel(tall, own, stay):
@@ -247,40 +241,26 @@
     )(*met, *arrived)
 
 
-def pick_kernel(block_cols, b, presence, blocks, swapped, held):
+def pick_kernel(presence, blocks, swapped, held):
     same = (lax.axis_index("row") & 1) == (lax.axis_index("col") & 1)
-    rows, order = held.shape
-    for a in range(rows // order):
-        here = pl.ds(a * order, order)
-        block = masked_block(presence, blocks, block_cols, a, b)
-        held[here, :] = jnp.where(same, block, swapped[here, :])
-
-
-def pick(presence, blocks, swapped, b):
-    return pl.pallas_call(
-        functools.partial(pick_kernel, blocks.shape[0] // swapped.shape[0], b),
-        out_shape=jax.ShapeDtypeStruct(swapped.shape, jnp.float32),
+    block_cols, rows, order = held.shape
+    for b in range(block_cols):
+        for a in range(rows // order):
+            here = pl.ds(a * order, order)
+            block = masked_block(presence, blocks, block_cols, a, b)
+            held[b, here, :] = jnp.where(same, block, swapped[b, here, :])
+
+
+def pick(presence, blocks, swapped):
+    rows, order = swapped.shape[1:]
+    return pl.pallas_call(
+        pick_kernel,
+        out_shape=jax.ShapeDtypeStruct((blocks.shape[0] // rows, rows, order), jnp.float32),
         in_specs=[WHOLE] * 3,
         out_specs=WHOLE,
         cost_estimate=LIGHT,
         compiler_params=ROOM,
     )(presence, blocks, swapped)
-
-
-def stacked_kernel(*refs):
-    for at, piece in enumerate(refs[:-1]):
-        refs[-1][at] = piece[...]
-
-
-def stacked(pieces):
-    return pl.pallas_call(
-        stacked_kernel,
-        out_shape=jax.ShapeDtypeStruct((len(pieces),) + pieces[0].shape, jnp.float32),
-        in_specs=[WHOLE] * len(pieces),
-        out_specs=WHOLE,
-        cost_estimate=LIGHT,
-        compiler_params=ROOM,
-    )(*pieces)
 
 
 def crossed(swap):
@@ -294,6 +274,18 @@
     return lax.ppermute(swap, ("row", "col"), cross)
 
 
+def routed(masked, turn, flip):
+    groups_row = lax.axis_size("row")
+    groups_col = lax.axis_size("col")
+    pairs = []
+    for r in range(groups_row):
+        for c in range(groups_col):
+            to_row = (r & ~1) | (c & 1)
+            to_col = (((c >> 1) ^ turn) << 1) | ((r & 1) ^ flip)
+            pairs.append((r * groups_col + c, to_row * groups_col + to_col))
+    return lax.ppermute(masked, ("row", "col"), pairs)
+
+
 def along_line(mine, order):
     strips, flips = [mine], [0]
     bit = lax.axis_size("row") // 2
@@ -317,18 +309,16 @@
     blocks = inverse_set.reshape(rows * block_cols, order)
     marks = presence.reshape(1, -1)
     tall = width // groups_row
-    mine, swaps = prepare(marks, blocks, own, span, tall)
-    swapped = [crossed(swap) for swap in swaps]
+    masked, swap, mine = prepare(marks, blocks, own, span, tall)
+    swapped = crossed(swap)
     stay = stay_half(own, tall)
     columns = along_line(mine, order)
-    held = [pick(marks, blocks, swapped[b], b) for b in range(block_cols)]
-    far = [(flip, piece) for flip in range(2, groups_col, 2) for piece in held]
-    ours = [flipped(piece, "col", flip) for flip, piece in far]
-    theirs = [flipped(piece, "col", 1) for piece in ours]
-    held, swapped = stacked(held), stacked(swapped)
-    mate, mate_swapped = flipped(held, "col", 1), flipped(swapped, "col", 1)
-
-    both = partials(held, mate, ours, theirs, columns)
+    turns = range(groups_col // 2)
+    ours = [routed(masked, turn, 0) for turn in turns if turn]
+    theirs = [routed(masked, turn, 1) for turn in turns]
+    mate_swapped = flipped(swapped, "col", 1)
+
+    both = partials([pick(marks, blocks, swapped), *ours, *theirs], columns)
     got = flipped(both, "row", 1)
     flips = (0, *range(groups_row - 2, 0, -2))
     along, outward = finish(

time: 32.7 us -> 34.4 us (1.052)
  waiting for transfers between devices: 10.3 us -> 14.1 us
  starting transfers between devices: 18 us -> 15.8 us
    ppermute x16 -> x11, starting transfers between devices: 15.6 us -> 11.4 us  [flipped(): lax.ppermute(value, axis, [(i, i ^ flip) for i in range(lax.axis_size(axi...]
    ppermute x16 -> x11, waiting for transfers between devices: 10.3 us -> 14.1 us  [flipped(): lax.ppermute(value, axis, [(i, i ^ flip) for i in range(lax.axis_size(axi...]
    ppermute x0 -> x3, starting transfers between devices: none -> 2 us  [routed(): return lax.ppermute(masked, ('row', 'col'), pairs)]
    ppermute x2 -> x1, starting transfers between devices: 2.43 us -> 2.38 us  [crossed(): return lax.ppermute(swap, ('row', 'col'), cross)]
  transfers between devices with their start and end apart: 18 -> 15, of which waited for: 6 -> 7; matrix products, arithmetic and copies ran while one was open for 0% -> 0% of each run, Pallas kernels for 2% -> 1%
where the time goes in v26:
time: 34.4 us; the launch traced here: 34.2 us
  starting transfers between devices  15.8 us (46%)
  waiting for transfers between devices  14.1 us (41%)
  Pallas kernels  3.49 us (10%)
  between operations  0.73 us (2%)
    ppermute x11, waiting for transfers between devices, flipped(): lax.ppermute(value, axis, [(i, i ^ flip) for i in range(lax.axis_size(axi...  14.1 us
    ppermute x11, starting transfers between devices, flipped(): lax.ppermute(value, axis, [(i, i ^ flip) for i in range(lax.axis_size(axi...  11.4 us
    ppermute x1, starting transfers between devices, crossed(): return lax.ppermute(swap, ('row', 'col'), cross)  2.38 us
    ppermute x3, starting transfers between devices, routed(): return lax.ppermute(masked, ('row', 'col'), pairs)  2 us
    pallas_call x1, Pallas kernels, prepare(): pl.pallas_call(functools.partial(prepare_kernel, tall), out_shape=(jax.Sh...  1.88 us
  transfers between devices with their start and end apart: 15, of which 7 were waited for; matrix products, arithmetic and copies ran while one was open for 0% of the time, Pallas kernels for 1%

profile of v26, /device:TPU:0, one launch (start us, length us, event | category | flops | bytes accessed | tf_op | source)
XLA Modules:
  0.0 34.2 jit_solution(5962196714007165975)
XLA Ops:
  0.6 1.9 %shard_map.59 = (f32[2,128,128]{2,1,0:T(8,128)}, f32[2,128,128]{2,1,0:T(8,128)}, f32[128,128]{1,0:T(8,128)}) custom-call(s32[1,2]{1,0:T(1,128)} %bitcast.8, f32[256,128]{1,0:T(8,128)} %bitcast.6, f32[128,512]{1,0:T(8,128)} %bitcast.4), custom_call_target="tpu_custom_call" | custom-call | flops 1000 | bytes 1000 | tf_op jit(solution)/shard_map/pallas_call | solution.py:89
  2.5 2.4 %collective-permute-start = (f32[2,128,128]{2,1,0:T(8,128)}, f32[2,128,128]{2,1,0:T(8,128)S(1)}, u32[]{:S(2)}, u32[]{:S(2)}) collective-permute-start(f32[2,128,128]{2,1,0:T(8,128)} %get-tuple-element.15), channel_id=1, source_target_pairs={{0,5},{1,4},{2,7},{3,6},{4,1},{5,0},{6,3},{7,2},{8,13},{9,12},{10,... | collective-permute-start | bytes 393224 | tf_op jit(solution)/shard_map/ppermute | solution.py:274
  4.9 2.6 %collective-permute-start.4 = (f32[128,128]{1,0:T(8,128)}, f32[128,128]{1,0:T(8,128)S(1)}, u32[]{:S(2)}, u32[]{:S(2)}) collective-permute-start(f32[128,128]{1,0:T(8,128)} %get-tuple-element.17.refs_0_), channel_id=1, source_target_pairs={{0,16},{4,20},{8,24},{12,28},{16,0},{20,4},{24,8},{28,12},{1,17},{... | collective-permute-start | bytes 196616 | tf_op jit(solution)/shard_map/ppermute | solution.py:18
  7.5 1.5 %collective-permute-start.1 = (f32[2,128,128]{2,1,0:T(8,128)}, f32[2,128,128]{2,1,0:T(8,128)S(1)}, u32[]{:S(2)}, u32[]{:S(2)}) collective-permute-start(f32[2,128,128]{2,1,0:T(8,128)} %get-tuple-element.16), channel_id=1, source_target_pairs={{0,2},{1,6},{2,0},{3,4},{4,3},{5,7},{6,1},{7,5},{8,10},{9,14},{10,... | collective-permute-start | bytes 393224 | tf_op jit(solution)/shard_map/ppermute | solution.py:286
  9.0 0.1 collective-permute-start.2
  9.1 0.3 %collective-permute-start.3 = (f32[2,128,128]{2,1,0:T(8,128)}, f32[2,128,128]{2,1,0:T(8,128)S(1)}, u32[]{:S(2)}, u32[]{:S(2)}) collective-permute-start(f32[2,128,128]{2,1,0:T(8,128)} %get-tuple-element.16), channel_id=1, source_target_pairs={{0,3},{1,7},{2,1},{3,5},{4,2},{5,6},{6,0},{7,4},{8,11},{9,15},{10,... | collective-permute-start | bytes 393224 | tf_op jit(solution)/shard_map/ppermute | solution.py:286
  9.5 2.6 %collective-permute-done.4.refs_1_ = f32[128,128]{1,0:T(8,128)S(1)} collective-permute-done((f32[128,128]{1,0:T(8,128)}, f32[128,128]{1,0:T(8,128)S(1)}, u32[]{:S(2)}, u32[]{:S(2)}) %collective-permute-start.4) | collective-permute-done | bytes 65568 | tf_op jit(solution)/shard_map/ppermute | solution.py:18
  12.1 0.8 %collective-permute-start.5 = (f32[128,128]{1,0:T(8,128)}, f32[128,128]{1,0:T(8,128)S(1)}, u32[]{:S(2)}, u32[]{:S(2)}) collective-permute-start(f32[128,128]{1,0:T(8,128)} %get-tuple-element.17.refs_0_), channel_id=1, source_target_pairs={{0,8},{4,12},{8,0},{12,4},{16,24},{20,28},{24,16},{28,20},{1,9},{5... | collective-permute-start | bytes 196616 | tf_op jit(solution)/shard_map/ppermute | solution.py:18
  12.9 1.2 %collective-permute-start.6 = (f32[128,128]{1,0:T(8,128)S(1)}, f32[128,128]{1,0:T(8,128)S(1)}, u32[]{:S(2)}, u32[]{:S(2)}) collective-permute-start(f32[128,128]{1,0:T(8,128)S(1)} %collective-permute-done.4.refs_1_), channel_id=1, source_target_pairs={{0,8},{4,12},{8,0},{12,4},{16,24},{20,28},{24,16},{28,20},{1,9},{5... | collective-permute-start | bytes 196616 | tf_op jit(solution)/shard_map/ppermute | solution.py:18
  14.2 2.5 %collective-permute-done.5.refs_2_ = f32[128,128]{1,0:T(8,128)S(1)} collective-permute-done((f32[128,128]{1,0:T(8,128)}, f32[128,128]{1,0:T(8,128)S(1)}, u32[]{:S(2)}, u32[]{:S(2)}) %collective-permute-start.5) | collective-permute-done | bytes 65568 | tf_op jit(solution)/shard_map/ppermute | solution.py:18
  16.7 0.7 %collective-permute-done.6.refs_3_ = f32[128,128]{1,0:T(8,128)S(1)} collective-permute-done((f32[128,128]{1,0:T(8,128)S(1)}, f32[128,128]{1,0:T(8,128)S(1)}, u32[]{:S(2)}, u32[]{:S(2)}) %collective-permute-start.6) | collective-permute-done | bytes 65568 | tf_op jit(solution)/shard_map/ppermute | solution.py:18
  17.5 0.4 %shard_map.62.both = f32[256,128]{1,0:T(8,128)S(1)} custom-call(f32[2,128,128]{2,1,0:T(8,128)S(1)} %shard_map.60.refs_0_, f32[2,128,128]{2,1,0:T(8,128)S(1)} %collective-permute-done.1.refs_1_, f32[2,128,128]{2,1,0:T(8,128)S(1)} %collective-permute-done.2.refs_2_, f32[2,128,128]{2,1,0:T(8,128)S(1)} %collective-permute-done.3.refs_3_, ...), custom_call_target="tpu_custom_call" | custom-call | flops 1000 | bytes 1000 | tf_op jit(solution)/shard_map/pallas_call | solution.py:141
  17.8 0.6 %collective-permute-start.7 = (f32[256,128]{1,0:T(8,128)S(1)}, f32[256,128]{1,0:T(8,128)S(1)}, u32[]{:S(2)}, u32[]{:S(2)}) collective-permute-start(f32[256,128]{1,0:T(8,128)S(1)} %shard_map.62.both), channel_id=1, source_target_pairs={{0,4},{4,0},{8,12},{12,8},{16,20},{20,16},{24,28},{28,24},{1,5},{5... | collective-permute-start | bytes 393224 | tf_op jit(solution)/shard_map/ppermute | solution.py:18
  18.4 0.1 shard_map.63.stay
  18.6 4.3 %collective-permute-done.7.got = f32[256,128]{1,0:T(8,128)S(1)} collective-permute-done((f32[256,128]{1,0:T(8,128)S(1)}, f32[256,128]{1,0:T(8,128)S(1)}, u32[]{:S(2)}, u32[]{:S(2)}) %collective-permute-start.7) | collective-permute-done | bytes 131104 | tf_op jit(solution)/shard_map/ppermute | solution.py:18
  22.9 0.3 shard_map.64
  23.3 3.1 %collective-permute-start.10 = (f32[64,128]{1,0:T(8,128)S(1)}, f32[64,128]{1,0:T(8,128)S(1)}, u32[]{:S(2)}, u32[]{:S(2)}) collective-permute-start(f32[64,128]{1,0:T(8,128)S(1)} %get-tuple-element.20), channel_id=1, source_target_pairs={{0,16},{4,20},{8,24},{12,28},{16,0},{20,4},{24,8},{28,12},{1,17},{... | collective-permute-start | bytes 98312 | tf_op jit(solution)/shard_map/ppermute | solution.py:18
  26.4 1.4 %collective-permute-start.11 = (f32[64,128]{1,0:T(8,128)S(1)}, f32[64,128]{1,0:T(8,128)S(1)}, u32[]{:S(2)}, u32[]{:S(2)}) collective-permute-start(f32[64,128]{1,0:T(8,128)S(1)} %get-tuple-element.21), channel_id=1, source_target_pairs={{0,8},{4,12},{8,0},{12,4},{16,24},{20,28},{24,16},{28,20},{1,9},{5... | collective-permute-start | bytes 98312 | tf_op jit(solution)/shard_map/ppermute | solution.py:18
  27.8 0.1 collective-permute-start.9
  27.9 1.5 %collective-permute-start.13 = (f32[32,128]{1,0:T(8,128)S(1)}, f32[32,128]{1,0:T(8,128)S(1)}, u32[]{:S(2)}, u32[]{:S(2)}) collective-permute-start(f32[32,128]{1,0:T(8,128)S(1)} %get-tuple-element.24), channel_id=1, source_target_pairs={{0,2},{1,3},{2,0},{3,1},{4,6},{5,7},{6,4},{7,5},{8,10},{9,11},{10,... | collective-permute-start | bytes 49160 | tf_op jit(solution)/shard_map/ppermute | solution.py:18
  29.5 2.2 %collective-permute-done.13.refs_6_ = f32[32,128]{1,0:T(8,128)S(1)} collective-permute-done((f32[32,128]{1,0:T(8,128)S(1)}, f32[32,128]{1,0:T(8,128)S(1)}, u32[]{:S(2)}, u32[]{:S(2)}) %collective-permute-start.13) | collective-permute-done | bytes 16416 | tf_op jit(solution)/shard_map/ppermute | solution.py:18
  31.7 1.0 %collective-permute-done.14.refs_7_ = f32[32,128]{1,0:T(8,128)S(1)} collective-permute-done((f32[32,128]{1,0:T(8,128)S(1)}, f32[32,128]{1,0:T(8,128)S(1)}, u32[]{:S(2)}, u32[]{:S(2)}) %collective-permute-start.14) | collective-permute-done | bytes 16416 | tf_op jit(solution)/shard_map/ppermute | solution.py:18
  32.6 0.9 %collective-permute-done.9.refs_1_ = f32[64,128]{1,0:T(8,128)S(1)} collective-permute-done((f32[64,128]{1,0:T(8,128)S(1)}, f32[64,128]{1,0:T(8,128)S(1)}, u32[]{:S(2)}, u32[]{:S(2)}) %collective-permute-start.9) | collective-permute-done | bytes 32800 | tf_op jit(solution)/shard_map/ppermute | solution.py:18
  33.6 0.7 %shard_map.65 = (f32[32,512]{1,0:T(8,128)}, f32[64,128]{1,0:T(8,128)}) custom-call(f32[64,128]{1,0:T(8,128)S(1)} %get-tuple-element.18.refs_0_, f32[64,128]{1,0:T(8,128)S(1)} %collective-permute-done.9.refs_1_, f32[64,128]{1,0:T(8,128)S(1)} %collective-permute-done.10.refs_2_, f32[64,128]{1,0:T(8,128)S(1)} %collective-permute-done.11.refs_3_, ...), custom_call_target="tpu_custom_call" | custom-call | flops 1000 | bytes 1000 | tf_op jit(solution)/shard_map/pallas_call | solution.py:231
  (23 shorter events, 0.2 us)
Async XLA Ops:
  0.6 13.5 %copy-start.1 = (f32[1,1,128,2,1,128]{5,4,3,2,1,0:T(1,128)S(1)}, f32[1,1,128,2,1,128]{5,4,3,2,1,0:T(1,128)}, u32[]{:S(2)}) copy-start(f32[1,1,128,2,1,128]{5,4,3,2,1,0:T(1,128)} %param.4) | copy-start | bytes 393220
  2.5 10.3 %collective-permute-start = (f32[2,128,128]{2,1,0:T(8,128)}, f32[2,128,128]{2,1,0:T(8,128)S(1)}, u32[]{:S(2)}, u32[]{:S(2)}) collective-permute-start(f32[2,128,128]{2,1,0:T(8,128)} %get-tuple-element.15), channel_id=1, source_target_pairs={{0,5},{1,4},{2,7},{3,6},{4,1},{5,0},{6,3},{7,2},{8,13},{9,12},{10,... | collective-permute-start | bytes 393224 | tf_op jit(solution)/shard_map/ppermute | solution.py:274
  4.9 9.2 %copy-start.4 = (s32[1,1,2,1]{2,3,1,0:T(1,128)S(1)}, s32[1,1,2,1]{2,3,1,0:T(1,128)}, u32[]{:S(2)}) copy-start(s32[1,1,2,1]{2,3,1,0:T(1,128)} %param.5) | copy-start | bytes 28
  4.9 7.2 %collective-permute-start.4 = (f32[128,128]{1,0:T(8,128)}, f32[128,128]{1,0:T(8,128)S(1)}, u32[]{:S(2)}, u32[]{:S(2)}) collective-permute-start(f32[128,128]{1,0:T(8,128)} %get-tuple-element.17.refs_0_), channel_id=1, source_target_pairs={{0,16},{4,20},{8,24},{12,28},{16,0},{20,4},{24,8},{28,12},{1,17},{... | collective-permute-start | bytes 196616 | tf_op jit(solution)/shard_map/ppermute | solution.py:18
  7.5 9.9 %copy-start.2 = (f32[128,128]{1,0:T(8,128)S(1)}, f32[128,128]{1,0:T(8,128)}, u32[]{:S(2)}) copy-start(f32[128,128]{1,0:T(8,128)} %get-tuple-element.17.refs_0_) | copy-start | bytes 196612
  7.5 9.9 %collective-permute-start.1 = (f32[2,128,128]{2,1,0:T(8,128)}, f32[2,128,128]{2,1,0:T(8,128)S(1)}, u32[]{:S(2)}, u32[]{:S(2)}) collective-permute-start(f32[2,128,128]{2,1,0:T(8,128)} %get-tuple-element.16), channel_id=1, source_target_pairs={{0,2},{1,6},{2,0},{3,4},{4,3},{5,7},{6,1},{7,5},{8,10},{9,14},{10,... | collective-permute-start | bytes 393224 | tf_op jit(solution)/shard_map/ppermute | solution.py:286
  9.0 8.4 %collective-permute-start.2 = (f32[2,128,128]{2,1,0:T(8,128)}, f32[2,128,128]{2,1,0:T(8,128)S(1)}, u32[]{:S(2)}, u32[]{:S(2)}) collective-permute-start(f32[2,128,128]{2,1,0:T(8,128)} %get-tuple-element.16), channel_id=1, source_target_pairs={{0,1},{1,5},{2,3},{3,7},{4,0},{5,4},{6,2},{7,6},{8,9},{9,13},{10,1... | collective-permute-start | bytes 393224 | tf_op jit(solution)/shard_map/ppermute | solution.py:286
  9.1 8.3 %collective-permute-start.3 = (f32[2,128,128]{2,1,0:T(8,128)}, f32[2,128,128]{2,1,0:T(8,128)S(1)}, u32[]{:S(2)}, u32[]{:S(2)}) collective-permute-start(f32[2,128,128]{2,1,0:T(8,128)} %get-tuple-element.16), channel_id=1, source_target_pairs={{0,3},{1,7},{2,1},{3,5},{4,2},{5,6},{6,0},{7,4},{8,11},{9,15},{10,... | collective-permute-start | bytes 393224 | tf_op jit(solution)/shard_map/ppermute | solution.py:286
  12.1 4.6 %collective-permute-start.5 = (f32[128,128]{1,0:T(8,128)}, f32[128,128]{1,0:T(8,128)S(1)}, u32[]{:S(2)}, u32[]{:S(2)}) collective-permute-start(f32[128,128]{1,0:T(8,128)} %get-tuple-element.17.refs_0_), channel_id=1, source_target_pairs={{0,8},{4,12},{8,0},{12,4},{16,24},{20,28},{24,16},{28,20},{1,9},{5... | collective-permute-start | bytes 196616 | tf_op jit(solution)/shard_map/ppermute | solution.py:18
  12.9 4.5 %collective-permute-start.6 = (f32[128,128]{1,0:T(8,128)S(1)}, f32[128,128]{1,0:T(8,128)S(1)}, u32[]{:S(2)}, u32[]{:S(2)}) collective-permute-start(f32[128,128]{1,0:T(8,128)S(1)} %collective-permute-done.4.refs_1_), channel_id=1, source_target_pairs={{0,8},{4,12},{8,0},{12,4},{16,24},{20,28},{24,16},{28,20},{1,9},{5... | collective-permute-start | bytes 196616 | tf_op jit(solution)/shard_map/ppermute | solution.py:18
  17.4 1.0 %copy-start = (f32[1,1,128,512]{3,2,1,0:T(8,128)S(1)}, f32[1,1,128,512]{3,2,1,0:T(8,128)}, u32[]{:S(2)}) copy-start(f32[1,1,128,512]{3,2,1,0:T(8,128)} %param.6) | copy-start | bytes 786436
  17.8 5.1 %copy-start.3 = (f32[64,128]{1,0:T(8,128)S(1)}, f32[64,128]{1,0:T(8,128)}, u32[]{:S(2)}) copy-start(f32[64,128]{1,0:T(8,128)} %dinv.1) | copy-start | bytes 98308
  17.8 5.0 %collective-permute-start.7 = (f32[256,128]{1,0:T(8,128)S(1)}, f32[256,128]{1,0:T(8,128)S(1)}, u32[]{:S(2)}, u32[]{:S(2)}) collective-permute-start(f32[256,128]{1,0:T(8,128)S(1)} %shard_map.62.both), channel_id=1, source_target_pairs={{0,4},{4,0},{8,12},{12,8},{16,20},{20,16},{24,28},{28,24},{1,5},{5... | collective-permute-start | bytes 393224 | tf_op jit(solution)/shard_map/ppermute | solution.py:18
  18.4 4.4 %collective-permute-start.8 = (f32[2,128,128]{2,1,0:T(8,128)S(1)}, f32[2,128,128]{2,1,0:T(8,128)S(1)}, u32[]{:S(2)}, u32[]{:S(2)}) collective-permute-start(f32[2,128,128]{2,1,0:T(8,128)S(1)} %collective-permute-done.swapped), channel_id=1, source_target_pairs={{0,1},{1,0},{2,3},{3,2},{4,5},{5,4},{6,7},{7,6},{8,9},{9,8},{10,11... | collective-permute-start | bytes 393224 | tf_op jit(solution)/shard_map/ppermute | solution.py:18
  23.2 6.2 %collective-permute-start.12 = (f32[32,128]{1,0:T(8,128)S(1)}, f32[32,128]{1,0:T(8,128)S(1)}, u32[]{:S(2)}, u32[]{:S(2)}) collective-permute-start(f32[32,128]{1,0:T(8,128)S(1)} %get-tuple-element.23), channel_id=1, source_target_pairs={{0,1},{1,0},{2,3},{3,2},{4,5},{5,4},{6,7},{7,6},{8,9},{9,8},{10,11... | collective-permute-start | bytes 49160 | tf_op jit(solution)/shard_map/ppermute | solution.py:18
  23.3 9.3 %collective-permute-start.10 = (f32[64,128]{1,0:T(8,128)S(1)}, f32[64,128]{1,0:T(8,128)S(1)}, u32[]{:S(2)}, u32[]{:S(2)}) collective-permute-start(f32[64,128]{1,0:T(8,128)S(1)} %get-tuple-element.20), channel_id=1, source_target_pairs={{0,16},{4,20},{8,24},{12,28},{16,0},{20,4},{24,8},{28,12},{1,17},{... | collective-permute-start | bytes 98312 | tf_op jit(solution)/shard_map/ppermute | solution.py:18
  26.4 6.2 %collective-permute-start.11 = (f32[64,128]{1,0:T(8,128)S(1)}, f32[64,128]{1,0:T(8,128)S(1)}, u32[]{:S(2)}, u32[]{:S(2)}) collective-permute-start(f32[64,128]{1,0:T(8,128)S(1)} %get-tuple-element.21), channel_id=1, source_target_pairs={{0,8},{4,12},{8,0},{12,4},{16,24},{20,28},{24,16},{28,20},{1,9},{5... | collective-permute-start | bytes 98312 | tf_op jit(solution)/shard_map/ppermute | solution.py:18
  27.8 5.7 %collective-permute-start.9 = (f32[64,128]{1,0:T(8,128)S(1)}, f32[64,128]{1,0:T(8,128)S(1)}, u32[]{:S(2)}, u32[]{:S(2)}) collective-permute-start(f32[64,128]{1,0:T(8,128)S(1)} %get-tuple-element.19), channel_id=1, source_target_pairs={{0,24},{4,28},{8,16},{12,20},{16,8},{20,12},{24,0},{28,4},{1,25},{... | collective-permute-start | bytes 98312 | tf_op jit(solution)/shard_map/ppermute | solution.py:18
  27.9 3.7 %collective-permute-start.13 = (f32[32,128]{1,0:T(8,128)S(1)}, f32[32,128]{1,0:T(8,128)S(1)}, u32[]{:S(2)}, u32[]{:S(2)}) collective-permute-start(f32[32,128]{1,0:T(8,128)S(1)} %get-tuple-element.24), channel_id=1, source_target_pairs={{0,2},{1,3},{2,0},{3,1},{4,6},{5,7},{6,4},{7,5},{8,10},{9,11},{10,... | collective-permute-start | bytes 49160 | tf_op jit(solution)/shard_map/ppermute | solution.py:18
  29.5 3.2 %collective-permute-start.14 = (f32[32,128]{1,0:T(8,128)S(1)}, f32[32,128]{1,0:T(8,128)S(1)}, u32[]{:S(2)}, u32[]{:S(2)}) collective-permute-start(f32[32,128]{1,0:T(8,128)S(1)} %get-tuple-element.25), channel_id=1, source_target_pairs={{0,3},{1,2},{2,1},{3,0},{4,7},{5,6},{6,5},{7,4},{8,11},{9,10},{10,... | collective-permute-start | bytes 49160 | tf_op jit(solution)/shard_map/ppermute | solution.py:18

commit v27 on v26

--- a/solution.py
+++ b/solution.py
@@ -320,7 +320,7 @@
 
     both = partials([pick(marks, blocks, swapped), *ours, *theirs], columns)
     got = flipped(both, "row", 1)
-    flips = (0, *range(groups_row - 2, 0, -2))
+    flips = (0, 2, *range(groups_row - 2, 2, -2))
     along, outward = finish(
         both, got, stay, swapped, mate_swapped, dinv, order, flips, groups_col
     )

time: 34.4 us -> 33.4 us (0.971)
  waiting for transfers between devices: 14.1 us -> 13.2 us
    ppermute x11, waiting for transfers between devices: 14.1 us -> 13.2 us  [flipped(): lax.ppermute(value, axis, [(i, i ^ flip) for i in range(lax.axis_size(axi...]
  transfers between devices with their start and end apart: 15 -> 15, of which waited for: 7 -> 6; matrix products, arithmetic and copies ran while one was open for 0% -> 0% of each run, Pallas kernels for 1% -> 1%
where the time goes in v27:
time: 33.4 us; the launch traced here: 33.3 us
  starting transfers between devices  15.8 us (47%)
  waiting for transfers between devices  13.2 us (40%)
  Pallas kernels  3.49 us (10%)
  between operations  0.73 us (2%)
    ppermute x11, waiting for transfers between devices, flipped(): lax.ppermute(value, axis, [(i, i ^ flip) for i in range(lax.axis_size(axi...  13.2 us
    ppermute x11, starting transfers between devices, flipped(): lax.ppermute(value, axis, [(i, i ^ flip) for i in range(lax.axis_size(axi...  11.4 us
    ppermute x1, starting transfers between devices, crossed(): return lax.ppermute(swap, ('row', 'col'), cross)  2.38 us
    ppermute x3, starting transfers between devices, routed(): return lax.ppermute(masked, ('row', 'col'), pairs)  2 us
    pallas_call x1, Pallas kernels, prepare(): pl.pallas_call(functools.partial(prepare_kernel, tall), out_shape=(jax.Sh...  1.88 us
  transfers between devices with their start and end apart: 15, of which 6 were waited for; matrix products, arithmetic and copies ran while one was open for 0% of the time, Pallas kernels for 1%

profile of v27, /device:TPU:0, one launch (start us, length us, event | category | flops | bytes accessed | tf_op | source)
XLA Modules:
  0.0 33.3 jit_solution(11822713583974113359)
XLA Ops:
  0.6 1.9 %shard_map.59 = (f32[2,128,128]{2,1,0:T(8,128)}, f32[2,128,128]{2,1,0:T(8,128)}, f32[128,128]{1,0:T(8,128)}) custom-call(s32[1,2]{1,0:T(1,128)} %bitcast.8, f32[256,128]{1,0:T(8,128)} %bitcast.6, f32[128,512]{1,0:T(8,128)} %bitcast.4), custom_call_target="tpu_custom_call" | custom-call | flops 1000 | bytes 1000 | tf_op jit(solution)/shard_map/pallas_call | solution.py:89
  2.5 2.4 %collective-permute-start = (f32[2,128,128]{2,1,0:T(8,128)}, f32[2,128,128]{2,1,0:T(8,128)S(1)}, u32[]{:S(2)}, u32[]{:S(2)}) collective-permute-start(f32[2,128,128]{2,1,0:T(8,128)} %get-tuple-element.15), channel_id=1, source_target_pairs={{0,5},{1,4},{2,7},{3,6},{4,1},{5,0},{6,3},{7,2},{8,13},{9,12},{10,... | collective-permute-start | bytes 393224 | tf_op jit(solution)/shard_map/ppermute | solution.py:274
  4.9 2.6 %collective-permute-start.4 = (f32[128,128]{1,0:T(8,128)}, f32[128,128]{1,0:T(8,128)S(1)}, u32[]{:S(2)}, u32[]{:S(2)}) collective-permute-start(f32[128,128]{1,0:T(8,128)} %get-tuple-element.17.refs_0_), channel_id=1, source_target_pairs={{0,16},{4,20},{8,24},{12,28},{16,0},{20,4},{24,8},{28,12},{1,17},{... | collective-permute-start | bytes 196616 | tf_op jit(solution)/shard_map/ppermute | solution.py:18
  7.5 1.5 %collective-permute-start.1 = (f32[2,128,128]{2,1,0:T(8,128)}, f32[2,128,128]{2,1,0:T(8,128)S(1)}, u32[]{:S(2)}, u32[]{:S(2)}) collective-permute-start(f32[2,128,128]{2,1,0:T(8,128)} %get-tuple-element.16), channel_id=1, source_target_pairs={{0,2},{1,6},{2,0},{3,4},{4,3},{5,7},{6,1},{7,5},{8,10},{9,14},{10,... | collective-permute-start | bytes 393224 | tf_op jit(solution)/shard_map/ppermute | solution.py:286
  9.0 0.1 collective-permute-start.2
  9.1 0.3 %collective-permute-start.3 = (f32[2,128,128]{2,1,0:T(8,128)}, f32[2,128,128]{2,1,0:T(8,128)S(1)}, u32[]{:S(2)}, u32[]{:S(2)}) collective-permute-start(f32[2,128,128]{2,1,0:T(8,128)} %get-tuple-element.16), channel_id=1, source_target_pairs={{0,3},{1,7},{2,1},{3,5},{4,2},{5,6},{6,0},{7,4},{8,11},{9,15},{10,... | collective-permute-start | bytes 393224 | tf_op jit(solution)/shard_map/ppermute | solution.py:286
  9.5 2.6 %collective-permute-done.4.refs_1_ = f32[128,128]{1,0:T(8,128)S(1)} collective-permute-done((f32[128,128]{1,0:T(8,128)}, f32[128,128]{1,0:T(8,128)S(1)}, u32[]{:S(2)}, u32[]{:S(2)}) %collective-permute-start.4) | collective-permute-done | bytes 65568 | tf_op jit(solution)/shard_map/ppermute | solution.py:18
  12.1 0.8 %collective-permute-start.5 = (f32[128,128]{1,0:T(8,128)}, f32[128,128]{1,0:T(8,128)S(1)}, u32[]{:S(2)}, u32[]{:S(2)}) collective-permute-start(f32[128,128]{1,0:T(8,128)} %get-tuple-element.17.refs_0_), channel_id=1, source_target_pairs={{0,8},{4,12},{8,0},{12,4},{16,24},{20,28},{24,16},{28,20},{1,9},{5... | collective-permute-start | bytes 196616 | tf_op jit(solution)/shard_map/ppermute | solution.py:18
  12.9 1.2 %collective-permute-start.6 = (f32[128,128]{1,0:T(8,128)S(1)}, f32[128,128]{1,0:T(8,128)S(1)}, u32[]{:S(2)}, u32[]{:S(2)}) collective-permute-start(f32[128,128]{1,0:T(8,128)S(1)} %collective-permute-done.4.refs_1_), channel_id=1, source_target_pairs={{0,8},{4,12},{8,0},{12,4},{16,24},{20,28},{24,16},{28,20},{1,9},{5... | collective-permute-start | bytes 196616 | tf_op jit(solution)/shard_map/ppermute | solution.py:18
  14.1 0.1 shard_map.60.refs_0_
  14.2 2.5 %collective-permute-done.5.refs_2_ = f32[128,128]{1,0:T(8,128)S(1)} collective-permute-done((f32[128,128]{1,0:T(8,128)}, f32[128,128]{1,0:T(8,128)S(1)}, u32[]{:S(2)}, u32[]{:S(2)}) %collective-permute-start.5) | collective-permute-done | bytes 65568 | tf_op jit(solution)/shard_map/ppermute | solution.py:18
  16.7 0.7 %collective-permute-done.6.refs_3_ = f32[128,128]{1,0:T(8,128)S(1)} collective-permute-done((f32[128,128]{1,0:T(8,128)S(1)}, f32[128,128]{1,0:T(8,128)S(1)}, u32[]{:S(2)}, u32[]{:S(2)}) %collective-permute-start.6) | collective-permute-done | bytes 65568 | tf_op jit(solution)/shard_map/ppermute | solution.py:18
  17.5 0.4 %shard_map.62.both = f32[256,128]{1,0:T(8,128)S(1)} custom-call(f32[2,128,128]{2,1,0:T(8,128)S(1)} %shard_map.60.refs_0_, f32[2,128,128]{2,1,0:T(8,128)S(1)} %collective-permute-done.1.refs_1_, f32[2,128,128]{2,1,0:T(8,128)S(1)} %collective-permute-done.2.refs_2_, f32[2,128,128]{2,1,0:T(8,128)S(1)} %collective-permute-done.3.refs_3_, ...), custom_call_target="tpu_custom_call" | custom-call | flops 1000 | bytes 1000 | tf_op jit(solution)/shard_map/pallas_call | solution.py:141
  17.8 0.6 %collective-permute-start.7 = (f32[256,128]{1,0:T(8,128)S(1)}, f32[256,128]{1,0:T(8,128)S(1)}, u32[]{:S(2)}, u32[]{:S(2)}) collective-permute-start(f32[256,128]{1,0:T(8,128)S(1)} %shard_map.62.both), channel_id=1, source_target_pairs={{0,4},{4,0},{8,12},{12,8},{16,20},{20,16},{24,28},{28,24},{1,5},{5... | collective-permute-start | bytes 393224 | tf_op jit(solution)/shard_map/ppermute | solution.py:18
  18.4 0.1 shard_map.63.stay
  18.6 4.3 %collective-permute-done.7.got = f32[256,128]{1,0:T(8,128)S(1)} collective-permute-done((f32[256,128]{1,0:T(8,128)S(1)}, f32[256,128]{1,0:T(8,128)S(1)}, u32[]{:S(2)}, u32[]{:S(2)}) %collective-permute-start.7) | collective-permute-done | bytes 131104 | tf_op jit(solution)/shard_map/ppermute | solution.py:18
  22.9 0.3 %shard_map.64 = (f32[64,128]{1,0:T(8,128)S(1)}, f32[64,128]{1,0:T(8,128)S(1)}, f32[64,128]{1,0:T(8,128)S(1)}, f32[64,128]{1,0:T(8,128)S(1)}, f32[32,128]{1,0:T(8...) custom-call(f32[256,128]{1,0:T(8,128)S(1)} %shard_map.62.both, ...), custom_call_target="tpu_custom_call" | custom-call | flops 1000 | bytes 1000 | tf_op jit(solution)/shard_map/pallas_call | solution.py:200
  23.2 0.1 collective-permute-start.12
  23.3 4.0 %collective-permute-start.10 = (f32[64,128]{1,0:T(8,128)S(1)}, f32[64,128]{1,0:T(8,128)S(1)}, u32[]{:S(2)}, u32[]{:S(2)}) collective-permute-start(f32[64,128]{1,0:T(8,128)S(1)} %get-tuple-element.20), channel_id=1, source_target_pairs={{0,24},{4,28},{8,16},{12,20},{16,8},{20,12},{24,0},{28,4},{1,25},{... | collective-permute-start | bytes 98312 | tf_op jit(solution)/shard_map/ppermute | solution.py:18
  27.3 0.6 %collective-permute-start.9 = (f32[64,128]{1,0:T(8,128)S(1)}, f32[64,128]{1,0:T(8,128)S(1)}, u32[]{:S(2)}, u32[]{:S(2)}) collective-permute-start(f32[64,128]{1,0:T(8,128)S(1)} %get-tuple-element.19), channel_id=1, source_target_pairs={{0,8},{4,12},{8,0},{12,4},{16,24},{20,28},{24,16},{28,20},{1,9},{5... | collective-permute-start | bytes 98312 | tf_op jit(solution)/shard_map/ppermute | solution.py:18
  27.9 1.5 %collective-permute-start.13 = (f32[32,128]{1,0:T(8,128)S(1)}, f32[32,128]{1,0:T(8,128)S(1)}, u32[]{:S(2)}, u32[]{:S(2)}) collective-permute-start(f32[32,128]{1,0:T(8,128)S(1)} %get-tuple-element.24), channel_id=1, source_target_pairs={{0,2},{1,3},{2,0},{3,1},{4,6},{5,7},{6,4},{7,5},{8,10},{9,11},{10,... | collective-permute-start | bytes 49160 | tf_op jit(solution)/shard_map/ppermute | solution.py:18
  29.4 2.2 %collective-permute-done.13.refs_6_ = f32[32,128]{1,0:T(8,128)S(1)} collective-permute-done((f32[32,128]{1,0:T(8,128)S(1)}, f32[32,128]{1,0:T(8,128)S(1)}, u32[]{:S(2)}, u32[]{:S(2)}) %collective-permute-start.13) | collective-permute-done | bytes 16416 | tf_op jit(solution)/shard_map/ppermute | solution.py:18
  31.7 0.9 %collective-permute-done.14.refs_7_ = f32[32,128]{1,0:T(8,128)S(1)} collective-permute-done((f32[32,128]{1,0:T(8,128)S(1)}, f32[32,128]{1,0:T(8,128)S(1)}, u32[]{:S(2)}, u32[]{:S(2)}) %collective-permute-start.14) | collective-permute-done | bytes 16416 | tf_op jit(solution)/shard_map/ppermute | solution.py:18
  32.6 0.7 %shard_map.65 = (f32[32,512]{1,0:T(8,128)}, f32[64,128]{1,0:T(8,128)}) custom-call(f32[64,128]{1,0:T(8,128)S(1)} %get-tuple-element.18.refs_0_, f32[64,128]{1,0:T(8,128)S(1)} %collective-permute-done.9.refs_1_, f32[64,128]{1,0:T(8,128)S(1)} %collective-permute-done.10.refs_2_, f32[64,128]{1,0:T(8,128)S(1)} %collective-permute-done.11.refs_3_, ...), custom_call_target="tpu_custom_call" | custom-call | flops 1000 | bytes 1000 | tf_op jit(solution)/shard_map/pallas_call | solution.py:231
  (23 shorter events, 0.1 us)
Async XLA Ops:
  0.6 13.5 %copy-start.1 = (f32[1,1,128,2,1,128]{5,4,3,2,1,0:T(1,128)S(1)}, f32[1,1,128,2,1,128]{5,4,3,2,1,0:T(1,128)}, u32[]{:S(2)}) copy-start(f32[1,1,128,2,1,128]{5,4,3,2,1,0:T(1,128)} %param.4) | copy-start | bytes 393220
  2.5 10.3 %collective-permute-start = (f32[2,128,128]{2,1,0:T(8,128)}, f32[2,128,128]{2,1,0:T(8,128)S(1)}, u32[]{:S(2)}, u32[]{:S(2)}) collective-permute-start(f32[2,128,128]{2,1,0:T(8,128)} %get-tuple-element.15), channel_id=1, source_target_pairs={{0,5},{1,4},{2,7},{3,6},{4,1},{5,0},{6,3},{7,2},{8,13},{9,12},{10,... | collective-permute-start | bytes 393224 | tf_op jit(solution)/shard_map/ppermute | solution.py:274
  4.9 9.2 %copy-start.4 = (s32[1,1,2,1]{2,3,1,0:T(1,128)S(1)}, s32[1,1,2,1]{2,3,1,0:T(1,128)}, u32[]{:S(2)}) copy-start(s32[1,1,2,1]{2,3,1,0:T(1,128)} %param.5) | copy-start | bytes 28
  4.9 7.2 %collective-permute-start.4 = (f32[128,128]{1,0:T(8,128)}, f32[128,128]{1,0:T(8,128)S(1)}, u32[]{:S(2)}, u32[]{:S(2)}) collective-permute-start(f32[128,128]{1,0:T(8,128)} %get-tuple-element.17.refs_0_), channel_id=1, source_target_pairs={{0,16},{4,20},{8,24},{12,28},{16,0},{20,4},{24,8},{28,12},{1,17},{... | collective-permute-start | bytes 196616 | tf_op jit(solution)/shard_map/ppermute | solution.py:18
  7.5 9.9 %copy-start.2 = (f32[128,128]{1,0:T(8,128)S(1)}, f32[128,128]{1,0:T(8,128)}, u32[]{:S(2)}) copy-start(f32[128,128]{1,0:T(8,128)} %get-tuple-element.17.refs_0_) | copy-start | bytes 196612
  7.5 9.9 %collective-permute-start.1 = (f32[2,128,128]{2,1,0:T(8,128)}, f32[2,128,128]{2,1,0:T(8,128)S(1)}, u32[]{:S(2)}, u32[]{:S(2)}) collective-permute-start(f32[2,128,128]{2,1,0:T(8,128)} %get-tuple-element.16), channel_id=1, source_target_pairs={{0,2},{1,6},{2,0},{3,4},{4,3},{5,7},{6,1},{7,5},{8,10},{9,14},{10,... | collective-permute-start | bytes 393224 | tf_op jit(solution)/shard_map/ppermute | solution.py:286
  9.0 8.4 %collective-permute-start.2 = (f32[2,128,128]{2,1,0:T(8,128)}, f32[2,128,128]{2,1,0:T(8,128)S(1)}, u32[]{:S(2)}, u32[]{:S(2)}) collective-permute-start(f32[2,128,128]{2,1,0:T(8,128)} %get-tuple-element.16), channel_id=1, source_target_pairs={{0,1},{1,5},{2,3},{3,7},{4,0},{5,4},{6,2},{7,6},{8,9},{9,13},{10,1... | collective-permute-start | bytes 393224 | tf_op jit(solution)/shard_map/ppermute | solution.py:286
  9.1 8.3 %collective-permute-start.3 = (f32[2,128,128]{2,1,0:T(8,128)}, f32[2,128,128]{2,1,0:T(8,128)S(1)}, u32[]{:S(2)}, u32[]{:S(2)}) collective-permute-start(f32[2,128,128]{2,1,0:T(8,128)} %get-tuple-element.16), channel_id=1, source_target_pairs={{0,3},{1,7},{2,1},{3,5},{4,2},{5,6},{6,0},{7,4},{8,11},{9,15},{10,... | collective-permute-start | bytes 393224 | tf_op jit(solution)/shard_map/ppermute | solution.py:286
  12.1 4.6 %collective-permute-start.5 = (f32[128,128]{1,0:T(8,128)}, f32[128,128]{1,0:T(8,128)S(1)}, u32[]{:S(2)}, u32[]{:S(2)}) collective-permute-start(f32[128,128]{1,0:T(8,128)} %get-tuple-element.17.refs_0_), channel_id=1, source_target_pairs={{0,8},{4,12},{8,0},{12,4},{16,24},{20,28},{24,16},{28,20},{1,9},{5... | collective-permute-start | bytes 196616 | tf_op jit(solution)/shard_map/ppermute | solution.py:18
  12.9 4.5 %collective-permute-start.6 = (f32[128,128]{1,0:T(8,128)S(1)}, f32[128,128]{1,0:T(8,128)S(1)}, u32[]{:S(2)}, u32[]{:S(2)}) collective-permute-start(f32[128,128]{1,0:T(8,128)S(1)} %collective-permute-done.4.refs_1_), channel_id=1, source_target_pairs={{0,8},{4,12},{8,0},{12,4},{16,24},{20,28},{24,16},{28,20},{1,9},{5... | collective-permute-start | bytes 196616 | tf_op jit(solution)/shard_map/ppermute | solution.py:18
  17.4 1.0 %copy-start = (f32[1,1,128,512]{3,2,1,0:T(8,128)S(1)}, f32[1,1,128,512]{3,2,1,0:T(8,128)}, u32[]{:S(2)}) copy-start(f32[1,1,128,512]{3,2,1,0:T(8,128)} %param.6) | copy-start | bytes 786436
  17.8 5.1 %copy-start.3 = (f32[64,128]{1,0:T(8,128)S(1)}, f32[64,128]{1,0:T(8,128)}, u32[]{:S(2)}) copy-start(f32[64,128]{1,0:T(8,128)} %dinv.1) | copy-start | bytes 98308
  17.8 5.0 %collective-permute-start.7 = (f32[256,128]{1,0:T(8,128)S(1)}, f32[256,128]{1,0:T(8,128)S(1)}, u32[]{:S(2)}, u32[]{:S(2)}) collective-permute-start(f32[256,128]{1,0:T(8,128)S(1)} %shard_map.62.both), channel_id=1, source_target_pairs={{0,4},{4,0},{8,12},{12,8},{16,20},{20,16},{24,28},{28,24},{1,5},{5... | collective-permute-start | bytes 393224 | tf_op jit(solution)/shard_map/ppermute | solution.py:18
  18.4 4.4 %collective-permute-start.8 = (f32[2,128,128]{2,1,0:T(8,128)S(1)}, f32[2,128,128]{2,1,0:T(8,128)S(1)}, u32[]{:S(2)}, u32[]{:S(2)}) collective-permute-start(f32[2,128,128]{2,1,0:T(8,128)S(1)} %collective-permute-done.swapped), channel_id=1, source_target_pairs={{0,1},{1,0},{2,3},{3,2},{4,5},{5,4},{6,7},{7,6},{8,9},{9,8},{10,11... | collective-permute-start | bytes 393224 | tf_op jit(solution)/shard_map/ppermute | solution.py:18
  23.2 6.2 %collective-permute-start.12 = (f32[32,128]{1,0:T(8,128)S(1)}, f32[32,128]{1,0:T(8,128)S(1)}, u32[]{:S(2)}, u32[]{:S(2)}) collective-permute-start(f32[32,128]{1,0:T(8,128)S(1)} %get-tuple-element.23), channel_id=1, source_target_pairs={{0,1},{1,0},{2,3},{3,2},{4,5},{5,4},{6,7},{7,6},{8,9},{9,8},{10,11... | collective-permute-start | bytes 49160 | tf_op jit(solution)/shard_map/ppermute | solution.py:18
  23.3 9.3 %collective-permute-start.10 = (f32[64,128]{1,0:T(8,128)S(1)}, f32[64,128]{1,0:T(8,128)S(1)}, u32[]{:S(2)}, u32[]{:S(2)}) collective-permute-start(f32[64,128]{1,0:T(8,128)S(1)} %get-tuple-element.20), channel_id=1, source_target_pairs={{0,24},{4,28},{8,16},{12,20},{16,8},{20,12},{24,0},{28,4},{1,25},{... | collective-permute-start | bytes 98312 | tf_op jit(solution)/shard_map/ppermute | solution.py:18
  27.3 5.3 %collective-permute-start.11 = (f32[64,128]{1,0:T(8,128)S(1)}, f32[64,128]{1,0:T(8,128)S(1)}, u32[]{:S(2)}, u32[]{:S(2)}) collective-permute-start(f32[64,128]{1,0:T(8,128)S(1)} %get-tuple-element.21), channel_id=1, source_target_pairs={{0,16},{4,20},{8,24},{12,28},{16,0},{20,4},{24,8},{28,12},{1,17},{... | collective-permute-start | bytes 98312 | tf_op jit(solution)/shard_map/ppermute | solution.py:18
  27.3 5.3 %collective-permute-start.9 = (f32[64,128]{1,0:T(8,128)S(1)}, f32[64,128]{1,0:T(8,128)S(1)}, u32[]{:S(2)}, u32[]{:S(2)}) collective-permute-start(f32[64,128]{1,0:T(8,128)S(1)} %get-tuple-element.19), channel_id=1, source_target_pairs={{0,8},{4,12},{8,0},{12,4},{16,24},{20,28},{24,16},{28,20},{1,9},{5... | collective-permute-start | bytes 98312 | tf_op jit(solution)/shard_map/ppermute | solution.py:18
  27.9 3.7 %collective-permute-start.13 = (f32[32,128]{1,0:T(8,128)S(1)}, f32[32,128]{1,0:T(8,128)S(1)}, u32[]{:S(2)}, u32[]{:S(2)}) collective-permute-start(f32[32,128]{1,0:T(8,128)S(1)} %get-tuple-element.24), channel_id=1, source_target_pairs={{0,2},{1,3},{2,0},{3,1},{4,6},{5,7},{6,4},{7,5},{8,10},{9,11},{10,... | collective-permute-start | bytes 49160 | tf_op jit(solution)/shard_map/ppermute | solution.py:18
  29.4 3.2 %collective-permute-start.14 = (f32[32,128]{1,0:T(8,128)S(1)}, f32[32,128]{1,0:T(8,128)S(1)}, u32[]{:S(2)}, u32[]{:S(2)}) collective-permute-start(f32[32,128]{1,0:T(8,128)S(1)} %get-tuple-element.25), channel_id=1, source_target_pairs={{0,3},{1,2},{2,1},{3,0},{4,7},{5,6},{6,5},{7,4},{8,11},{9,10},{10,... | collective-permute-start | bytes 49160 | tf_op jit(solution)/shard_map/ppermute | solution.py:18

commit v28 on v24

--- a/solution.py
+++ b/solution.py
@@ -10,7 +10,7 @@
 LANES = 128
 WHOLE = pl.BlockSpec(memory_space=pltpu.VMEM)
 ROOM = pltpu.CompilerParams(vmem_limit_bytes=16 * 1024 * 1024)
-HEAVY = 10**9
+HEAVY = 6 * 10**8
 LIGHT = pl.CostEstimate(flops=1000, bytes_accessed=1000, transcendentals=0)
 
 
@@ -116,6 +116,21 @@
         cost_estimate=pl.CostEstimate(flops=HEAVY, bytes_accessed=1000, transcendentals=0),
         compiler_params=ROOM,
     )(*strips)
+
+
+def passed_kernel(strip, _, out):
+    out[...] = strip[...]
+
+
+def passed(strip, earlier):
+    return pl.pallas_call(
+        passed_kernel,
+        out_shape=jax.ShapeDtypeStruct(strip.shape, strip.dtype),
+        in_specs=[WHOLE, pl.BlockSpec(memory_space=pl.ANY)],
+        out_specs=WHOLE,
+        cost_estimate=LIGHT,
+        compiler_params=ROOM,
+    )(strip, earlier)
 
 
 def partials_kernel(count, *refs):
@@ -294,11 +309,12 @@
     return lax.ppermute(swap, ("row", "col"), cross)
 
 
-def along_line(mine, order):
+def along_line(mine, order, earlier):
     strips, flips = [mine], [0]
     bit = lax.axis_size("row") // 2
     while bit > 1:
         strips = strips + [flipped(strip, "row", bit) for strip in strips]
+        strips[0] = passed(mine, earlier)
         flips = flips + [flip ^ bit for flip in flips]
         bit //= 2
     return ordered(strips, tuple(flips), order)
@@ -320,12 +336,12 @@
     mine, swaps = prepare(marks, blocks, own, span, tall)
     swapped = [crossed(swap) for swap in swaps]
     stay = stay_half(own, tall)
-    columns = along_line(mine, order)
     held = [pick(marks, blocks, swapped[b], b) for b in range(block_cols)]
     far = [(flip, piece) for flip in range(2, groups_col, 2) for piece in held]
     ours = [flipped(piece, "col", flip) for flip, piece in far]
     theirs = [flipped(piece, "col", 1) for piece in ours]
     held, swapped = stacked(held), stacked(swapped)
+    columns = along_line(mine, order, held)
     mate, mate_swapped = flipped(held, "col", 1), flipped(swapped, "col", 1)
 
     both = partials(held, mate, ours, theirs, columns)

time: 32.7 us -> 33.6 us (1.028)
  starting transfers between devices: 18 us -> 18.8 us
    ppermute x16, starting transfers between devices: 15.6 us -> 16.3 us  [flipped(): lax.ppermute(value, axis, [(i, i ^ flip) for i in range(lax.axis_size(axi...]
    ppermute x2, waiting for transfers between devices: 0.01 us -> 0.7 us  [crossed(): return lax.ppermute(swap, ('row', 'col'), cross)]
    ppermute x16, waiting for transfers between devices: 10.3 us -> 9.71 us  [flipped(): lax.ppermute(value, axis, [(i, i ^ flip) for i in range(lax.axis_size(axi...]
  transfers between devices with their start and end apart: 18 -> 18, of which waited for: 6 -> 8; matrix products, arithmetic and copies ran while one was open for 0% -> 0% of each run, Pallas kernels for 2% -> 2%
where the time goes in v28:
time: 33.6 us; the launch traced here: 33.5 us
  starting transfers between devices  18.8 us (56%)
  waiting for transfers between devices  10.4 us (31%)
  Pallas kernels  3.54 us (11%)
  between operations  0.76 us (2%)
    ppermute x16, starting transfers between devices, flipped(): lax.ppermute(value, axis, [(i, i ^ flip) for i in range(lax.axis_size(axi...  16.3 us
    ppermute x16, waiting for transfers between devices, flipped(): lax.ppermute(value, axis, [(i, i ^ flip) for i in range(lax.axis_size(axi...  9.71 us
    ppermute x2, starting transfers between devices, crossed(): return lax.ppermute(swap, ('row', 'col'), cross)  2.43 us
    pallas_call x1, Pallas kernels, prepare(): pl.pallas_call(functools.partial(prepare_kernel, tall), out_shape=(jax.Sh...  1.83 us
    ppermute x2, waiting for transfers between devices, crossed(): return lax.ppermute(swap, ('row', 'col'), cross)  0.7 us
  transfers between devices with their start and end apart: 18, of which 8 were waited for; matrix products, arithmetic and copies ran while one was open for 0% of the time, Pallas kernels for 2%

profile of v28, /device:TPU:0, one launch (start us, length us, event | category | flops | bytes accessed | tf_op | source)
XLA Modules:
  0.0 33.5 jit_solution(7953092287947596775)
XLA Ops:
  0.6 1.8 %shard_map.59 = (f32[128,128]{1,0:T(8,128)}, f32[128,128]{1,0:T(8,128)}, f32[128,128]{1,0:T(8,128)}) custom-call(s32[1,2]{1,0:T(1,128)} %bitcast.9, f32[256,128]{1,0:T(8,128)} %bitcast.4, f32[128,512]{1,0:T(8,128)} %bitcast.7), custom_call_target="tpu_custom_call" | custom-call | flops 1000 | bytes 1000 | tf_op jit(solution)/shard_map/pallas_call | solution.py:89
  2.5 2.4 %collective-permute-start = (f32[128,128]{1,0:T(8,128)}, f32[128,128]{1,0:T(8,128)S(1)}, u32[]{:S(2)}, u32[]{:S(2)}) collective-permute-start(f32[128,128]{1,0:T(8,128)} %get-tuple-element.15), channel_id=1, source_target_pairs={{0,5},{1,4},{2,7},{3,6},{4,1},{5,0},{6,3},{7,2},{8,13},{9,12},{10,... | collective-permute-start | bytes 196616 | tf_op jit(solution)/shard_map/ppermute | solution.py:309
  4.9 3.4 %collective-permute-start.7 = (f32[128,128]{1,0:T(8,128)}, f32[128,128]{1,0:T(8,128)S(1)}, u32[]{:S(2)}, u32[]{:S(2)}) collective-permute-start(f32[128,128]{1,0:T(8,128)} %get-tuple-element.17.strip), channel_id=1, source_target_pairs={{0,16},{4,20},{8,24},{12,28},{16,0},{20,4},{24,8},{28,12},{1,17},{... | collective-permute-start | bytes 196616 | tf_op jit(solution)/shard_map/ppermute | solution.py:18
  8.3 0.1 shard_map.60.refs_0_
  8.3 0.7 %collective-permute-done.1.swapped.refs_1_ = f32[128,128]{1,0:T(8,128)S(1)} collective-permute-done((f32[128,128]{1,0:T(8,128)}, f32[128,128]{1,0:T(8,128)S(1)}, u32[]{:S(2)}, u32[]{:S(2)}) %collective-permute-start.1) | collective-permute-done | bytes 65568 | tf_op jit(solution)/shard_map/ppermute | solution.py:309
  9.1 2.0 %collective-permute-start.3 = (f32[128,128]{1,0:T(8,128)S(1)}, f32[128,128]{1,0:T(8,128)S(1)}, u32[]{:S(2)}, u32[]{:S(2)}) collective-permute-start(f32[128,128]{1,0:T(8,128)S(1)} %shard_map.60.refs_0_), channel_id=1, source_target_pairs={{0,2},{1,3},{2,0},{3,1},{4,6},{5,7},{6,4},{7,5},{8,10},{9,11},{10,... | collective-permute-start | bytes 196616 | tf_op jit(solution)/shard_map/ppermute | solution.py:18
  11.2 0.3 collective-permute-start.4
  11.5 1.9 %collective-permute-start.8 = (f32[128,128]{1,0:T(8,128)S(1)}, f32[128,128]{1,0:T(8,128)S(1)}, u32[]{:S(2)}, u32[]{:S(2)}) collective-permute-start(f32[128,128]{1,0:T(8,128)S(1)} %shard_map.63.refs_0_), channel_id=1, source_target_pairs={{0,8},{4,12},{8,0},{12,4},{16,24},{20,28},{24,16},{28,20},{1,9},{5... | collective-permute-start | bytes 196616 | tf_op jit(solution)/shard_map/ppermute | solution.py:18
  13.5 0.2 collective-permute-start.9
  13.7 2.1 %collective-permute-done.4.refs_3_ = f32[128,128]{1,0:T(8,128)S(1)} collective-permute-done((f32[128,128]{1,0:T(8,128)S(1)}, f32[128,128]{1,0:T(8,128)S(1)}, u32[]{:S(2)}, u32[]{:S(2)}) %collective-permute-start.4) | collective-permute-done | bytes 65568 | tf_op jit(solution)/shard_map/ppermute | solution.py:18
  15.8 0.1 collective-permute-done.8.refs_2_
  15.9 0.5 %collective-permute-start.11 = (f32[2,128,128]{2,1,0:T(8,128)S(1)}, f32[2,128,128]{2,1,0:T(8,128)S(1)}, u32[]{:S(2)}, u32[]{:S(2)}) collective-permute-start(f32[2,128,128]{2,1,0:T(8,128)S(1)} %shard_map.67.swapped), channel_id=1, source_target_pairs={{0,1},{1,0},{2,3},{3,2},{4,5},{5,4},{6,7},{7,6},{8,9},{9,8},{10,11... | collective-permute-start | bytes 393224 | tf_op jit(solution)/shard_map/ppermute | solution.py:18
  16.3 1.4 %collective-permute-done.9.refs_3_ = f32[128,128]{1,0:T(8,128)S(1)} collective-permute-done((f32[128,128]{1,0:T(8,128)S(1)}, f32[128,128]{1,0:T(8,128)S(1)}, u32[]{:S(2)}, u32[]{:S(2)}) %collective-permute-start.9) | collective-permute-done | bytes 65568 | tf_op jit(solution)/shard_map/ppermute | solution.py:18
  17.8 0.4 %shard_map.65.both = f32[256,128]{1,0:T(8,128)S(1)} custom-call(f32[2,128,128]{2,1,0:T(8,128)S(1)} %shard_map.62._.refs_0_, f32[2,128,128]{2,1,0:T(8,128)S(1)} %collective-permute-done.2.refs_1_, f32[128,128]{1,0:T(8,128)S(1)} %collective-permute-done.3.refs_2_, f32[128,128]{1,0:T(8,128)S(1)} %collective-permute-done.4.refs_3_, ...), custom_call_target="tpu_custom_call" | custom-call | flops 1000 | bytes 1000 | tf_op jit(solution)/shard_map/pallas_call | solution.py:162
  18.2 2.0 %collective-permute-start.10 = (f32[256,128]{1,0:T(8,128)S(1)}, f32[256,128]{1,0:T(8,128)S(1)}, u32[]{:S(2)}, u32[]{:S(2)}) collective-permute-start(f32[256,128]{1,0:T(8,128)S(1)} %shard_map.65.both), channel_id=1, source_target_pairs={{0,4},{4,0},{8,12},{12,8},{16,20},{20,16},{24,28},{28,24},{1,5},{5... | collective-permute-start | bytes 393224 | tf_op jit(solution)/shard_map/ppermute | solution.py:18
  20.2 0.1 shard_map.66.stay
  20.3 2.9 %collective-permute-done.10.got = f32[256,128]{1,0:T(8,128)S(1)} collective-permute-done((f32[256,128]{1,0:T(8,128)S(1)}, f32[256,128]{1,0:T(8,128)S(1)}, u32[]{:S(2)}, u32[]{:S(2)}) %collective-permute-start.10) | collective-permute-done | bytes 131104 | tf_op jit(solution)/shard_map/ppermute | solution.py:18
  23.2 0.3 shard_map.68
  23.7 3.8 %collective-permute-start.12 = (f32[64,128]{1,0:T(8,128)S(1)}, f32[64,128]{1,0:T(8,128)S(1)}, u32[]{:S(2)}, u32[]{:S(2)}) collective-permute-start(f32[64,128]{1,0:T(8,128)S(1)} %get-tuple-element.19), channel_id=1, source_target_pairs={{0,24},{4,28},{8,16},{12,20},{16,8},{20,12},{24,0},{28,4},{1,25},{... | collective-permute-start | bytes 98312 | tf_op jit(solution)/shard_map/ppermute | solution.py:18
  27.5 0.6 %collective-permute-start.14 = (f32[64,128]{1,0:T(8,128)S(1)}, f32[64,128]{1,0:T(8,128)S(1)}, u32[]{:S(2)}, u32[]{:S(2)}) collective-permute-start(f32[64,128]{1,0:T(8,128)S(1)} %get-tuple-element.21), channel_id=1, source_target_pairs={{0,8},{4,12},{8,0},{12,4},{16,24},{20,28},{24,16},{28,20},{1,9},{5... | collective-permute-start | bytes 98312 | tf_op jit(solution)/shard_map/ppermute | solution.py:18
  28.1 1.5 %collective-permute-start.16 = (f32[32,128]{1,0:T(8,128)S(1)}, f32[32,128]{1,0:T(8,128)S(1)}, u32[]{:S(2)}, u32[]{:S(2)}) collective-permute-start(f32[32,128]{1,0:T(8,128)S(1)} %get-tuple-element.24), channel_id=1, source_target_pairs={{0,2},{1,3},{2,0},{3,1},{4,6},{5,7},{6,4},{7,5},{8,10},{9,11},{10,... | collective-permute-start | bytes 49160 | tf_op jit(solution)/shard_map/ppermute | solution.py:18
  29.6 2.2 %collective-permute-done.16.refs_6_ = f32[32,128]{1,0:T(8,128)S(1)} collective-permute-done((f32[32,128]{1,0:T(8,128)S(1)}, f32[32,128]{1,0:T(8,128)S(1)}, u32[]{:S(2)}, u32[]{:S(2)}) %collective-permute-start.16) | collective-permute-done | bytes 16416 | tf_op jit(solution)/shard_map/ppermute | solution.py:18
  31.9 0.9 %collective-permute-done.17.refs_7_ = f32[32,128]{1,0:T(8,128)S(1)} collective-permute-done((f32[32,128]{1,0:T(8,128)S(1)}, f32[32,128]{1,0:T(8,128)S(1)}, u32[]{:S(2)}, u32[]{:S(2)}) %collective-permute-start.17) | collective-permute-done | bytes 16416 | tf_op jit(solution)/shard_map/ppermute | solution.py:18
  32.8 0.7 %shard_map.69 = (f32[32,512]{1,0:T(8,128)}, f32[64,128]{1,0:T(8,128)}) custom-call(f32[64,128]{1,0:T(8,128)S(1)} %get-tuple-element.18.refs_0_, f32[64,128]{1,0:T(8,128)S(1)} %collective-permute-done.12.refs_1_, f32[64,128]{1,0:T(8,128)S(1)} %collective-permute-done.13.refs_2_, f32[64,128]{1,0:T(8,128)S(1)} %collective-permute-done.14.refs_3_, ...), custom_call_target="tpu_custom_call" | custom-call | flops 1000 | bytes 1000 | tf_op jit(solution)/shard_map/pallas_call | solution.py:252
  (33 shorter events, 0.4 us)
Async XLA Ops:
  0.6 7.6 %copy-start = (f32[1,1,128,2,1,128]{5,4,3,2,1,0:T(1,128)S(1)}, f32[1,1,128,2,1,128]{5,4,3,2,1,0:T(1,128)}, u32[]{:S(2)}) copy-start(f32[1,1,128,2,1,128]{5,4,3,2,1,0:T(1,128)} %param.4) | copy-start | bytes 393220
  2.5 5.8 %collective-permute-start = (f32[128,128]{1,0:T(8,128)}, f32[128,128]{1,0:T(8,128)S(1)}, u32[]{:S(2)}, u32[]{:S(2)}) collective-permute-start(f32[128,128]{1,0:T(8,128)} %get-tuple-element.15), channel_id=1, source_target_pairs={{0,5},{1,4},{2,7},{3,6},{4,1},{5,0},{6,3},{7,2},{8,13},{9,12},{10,... | collective-permute-start | bytes 196616 | tf_op jit(solution)/shard_map/ppermute | solution.py:309
  4.8 3.4 %copy-start.4 = (s32[1,1,2,1]{2,3,1,0:T(1,128)S(1)}, s32[1,1,2,1]{2,3,1,0:T(1,128)}, u32[]{:S(2)}) copy-start(s32[1,1,2,1]{2,3,1,0:T(1,128)} %param.5) | copy-start | bytes 28
  4.8 4.2 %collective-permute-start.1 = (f32[128,128]{1,0:T(8,128)}, f32[128,128]{1,0:T(8,128)S(1)}, u32[]{:S(2)}, u32[]{:S(2)}) collective-permute-start(f32[128,128]{1,0:T(8,128)} %get-tuple-element.16), channel_id=1, source_target_pairs={{0,5},{1,4},{2,7},{3,6},{4,1},{5,0},{6,3},{7,2},{8,13},{9,12},{10,... | collective-permute-start | bytes 196616 | tf_op jit(solution)/shard_map/ppermute | solution.py:309
  4.9 8.6 %collective-permute-start.7 = (f32[128,128]{1,0:T(8,128)}, f32[128,128]{1,0:T(8,128)S(1)}, u32[]{:S(2)}, u32[]{:S(2)}) collective-permute-start(f32[128,128]{1,0:T(8,128)} %get-tuple-element.17.strip), channel_id=1, source_target_pairs={{0,16},{4,20},{8,24},{12,28},{16,0},{20,4},{24,8},{28,12},{1,17},{... | collective-permute-start | bytes 196616 | tf_op jit(solution)/shard_map/ppermute | solution.py:18
  9.1 2.4 %copy-start.2 = (f32[128,128]{1,0:T(8,128)S(1)}, f32[128,128]{1,0:T(8,128)}, u32[]{:S(2)}) copy-start(f32[128,128]{1,0:T(8,128)} %get-tuple-element.17.strip) | copy-start | bytes 196612
  9.1 4.5 %collective-permute-start.3 = (f32[128,128]{1,0:T(8,128)S(1)}, f32[128,128]{1,0:T(8,128)S(1)}, u32[]{:S(2)}, u32[]{:S(2)}) collective-permute-start(f32[128,128]{1,0:T(8,128)S(1)} %shard_map.60.refs_0_), channel_id=1, source_target_pairs={{0,2},{1,3},{2,0},{3,1},{4,6},{5,7},{6,4},{7,5},{8,10},{9,11},{10,... | collective-permute-start | bytes 196616 | tf_op jit(solution)/shard_map/ppermute | solution.py:18
  11.2 6.6 %collective-permute-start.2 = (f32[2,128,128]{2,1,0:T(8,128)S(1)}, f32[2,128,128]{2,1,0:T(8,128)S(1)}, u32[]{:S(2)}, u32[]{:S(2)}) collective-permute-start(f32[2,128,128]{2,1,0:T(8,128)S(1)} %shard_map.62._.refs_0_), channel_id=1, source_target_pairs={{0,1},{1,0},{2,3},{3,2},{4,5},{5,4},{6,7},{7,6},{8,9},{9,8},{10,11... | collective-permute-start | bytes 393224 | tf_op jit(solution)/shard_map/ppermute | solution.py:18
  11.2 4.5 %collective-permute-start.4 = (f32[128,128]{1,0:T(8,128)S(1)}, f32[128,128]{1,0:T(8,128)S(1)}, u32[]{:S(2)}, u32[]{:S(2)}) collective-permute-start(f32[128,128]{1,0:T(8,128)S(1)} %shard_map.61.refs_1_), channel_id=1, source_target_pairs={{0,2},{1,3},{2,0},{3,1},{4,6},{5,7},{6,4},{7,5},{8,10},{9,11},{10,... | collective-permute-start | bytes 196616 | tf_op jit(solution)/shard_map/ppermute | solution.py:18
  11.5 4.4 %collective-permute-start.8 = (f32[128,128]{1,0:T(8,128)S(1)}, f32[128,128]{1,0:T(8,128)S(1)}, u32[]{:S(2)}, u32[]{:S(2)}) collective-permute-start(f32[128,128]{1,0:T(8,128)S(1)} %shard_map.63.refs_0_), channel_id=1, source_target_pairs={{0,8},{4,12},{8,0},{12,4},{16,24},{20,28},{24,16},{28,20},{1,9},{5... | collective-permute-start | bytes 196616 | tf_op jit(solution)/shard_map/ppermute | solution.py:18
  13.5 4.3 %collective-permute-start.9 = (f32[128,128]{1,0:T(8,128)S(1)}, f32[128,128]{1,0:T(8,128)S(1)}, u32[]{:S(2)}, u32[]{:S(2)}) collective-permute-start(f32[128,128]{1,0:T(8,128)S(1)} %collective-permute-done.7.refs_1_), channel_id=1, source_target_pairs={{0,8},{4,12},{8,0},{12,4},{16,24},{20,28},{24,16},{28,20},{1,9},{5... | collective-permute-start | bytes 196616 | tf_op jit(solution)/shard_map/ppermute | solution.py:18
  13.7 4.1 %collective-permute-start.5 = (f32[128,128]{1,0:T(8,128)S(1)}, f32[128,128]{1,0:T(8,128)S(1)}, u32[]{:S(2)}, u32[]{:S(2)}) collective-permute-start(f32[128,128]{1,0:T(8,128)S(1)} %collective-permute-done.3.refs_2_), channel_id=1, source_target_pairs={{0,1},{1,0},{2,3},{3,2},{4,5},{5,4},{6,7},{7,6},{8,9},{9,8},{10,11... | collective-permute-start | bytes 196616 | tf_op jit(solution)/shard_map/ppermute | solution.py:18
  15.7 2.1 %collective-permute-start.6 = (f32[128,128]{1,0:T(8,128)S(1)}, f32[128,128]{1,0:T(8,128)S(1)}, u32[]{:S(2)}, u32[]{:S(2)}) collective-permute-start(f32[128,128]{1,0:T(8,128)S(1)} %collective-permute-done.4.refs_3_), channel_id=1, source_target_pairs={{0,1},{1,0},{2,3},{3,2},{4,5},{5,4},{6,7},{7,6},{8,9},{9,8},{10,11... | collective-permute-start | bytes 196616 | tf_op jit(solution)/shard_map/ppermute | solution.py:18
  15.9 4.4 %collective-permute-start.11 = (f32[2,128,128]{2,1,0:T(8,128)S(1)}, f32[2,128,128]{2,1,0:T(8,128)S(1)}, u32[]{:S(2)}, u32[]{:S(2)}) collective-permute-start(f32[2,128,128]{2,1,0:T(8,128)S(1)} %shard_map.67.swapped), channel_id=1, source_target_pairs={{0,1},{1,0},{2,3},{3,2},{4,5},{5,4},{6,7},{7,6},{8,9},{9,8},{10,11... | collective-permute-start | bytes 393224 | tf_op jit(solution)/shard_map/ppermute | solution.py:18
  17.8 2.4 %copy-start.1 = (f32[1,1,128,512]{3,2,1,0:T(8,128)S(1)}, f32[1,1,128,512]{3,2,1,0:T(8,128)}, u32[]{:S(2)}) copy-start(f32[1,1,128,512]{3,2,1,0:T(8,128)} %param.6) | copy-start | bytes 786436
  18.2 5.0 %copy-start.3 = (f32[64,128]{1,0:T(8,128)S(1)}, f32[64,128]{1,0:T(8,128)}, u32[]{:S(2)}) copy-start(f32[64,128]{1,0:T(8,128)} %dinv.1) | copy-start | bytes 98308
  18.2 5.0 %collective-permute-start.10 = (f32[256,128]{1,0:T(8,128)S(1)}, f32[256,128]{1,0:T(8,128)S(1)}, u32[]{:S(2)}, u32[]{:S(2)}) collective-permute-start(f32[256,128]{1,0:T(8,128)S(1)} %shard_map.65.both), channel_id=1, source_target_pairs={{0,4},{4,0},{8,12},{12,8},{16,20},{20,16},{24,28},{28,24},{1,5},{5... | collective-permute-start | bytes 393224 | tf_op jit(solution)/shard_map/ppermute | solution.py:18
  23.6 6.1 %collective-permute-start.15 = (f32[32,128]{1,0:T(8,128)S(1)}, f32[32,128]{1,0:T(8,128)S(1)}, u32[]{:S(2)}, u32[]{:S(2)}) collective-permute-start(f32[32,128]{1,0:T(8,128)S(1)} %get-tuple-element.23), channel_id=1, source_target_pairs={{0,1},{1,0},{2,3},{3,2},{4,5},{5,4},{6,7},{7,6},{8,9},{9,8},{10,11... | collective-permute-start | bytes 49160 | tf_op jit(solution)/shard_map/ppermute | solution.py:18
  23.7 9.2 %collective-permute-start.12 = (f32[64,128]{1,0:T(8,128)S(1)}, f32[64,128]{1,0:T(8,128)S(1)}, u32[]{:S(2)}, u32[]{:S(2)}) collective-permute-start(f32[64,128]{1,0:T(8,128)S(1)} %get-tuple-element.19), channel_id=1, source_target_pairs={{0,24},{4,28},{8,16},{12,20},{16,8},{20,12},{24,0},{28,4},{1,25},{... | collective-permute-start | bytes 98312 | tf_op jit(solution)/shard_map/ppermute | solution.py:18
  27.5 5.3 %collective-permute-start.13 = (f32[64,128]{1,0:T(8,128)S(1)}, f32[64,128]{1,0:T(8,128)S(1)}, u32[]{:S(2)}, u32[]{:S(2)}) collective-permute-start(f32[64,128]{1,0:T(8,128)S(1)} %get-tuple-element.20), channel_id=1, source_target_pairs={{0,16},{4,20},{8,24},{12,28},{16,0},{20,4},{24,8},{28,12},{1,17},{... | collective-permute-start | bytes 98312 | tf_op jit(solution)/shard_map/ppermute | solution.py:18
  27.5 5.3 %collective-permute-start.14 = (f32[64,128]{1,0:T(8,128)S(1)}, f32[64,128]{1,0:T(8,128)S(1)}, u32[]{:S(2)}, u32[]{:S(2)}) collective-permute-start(f32[64,128]{1,0:T(8,128)S(1)} %get-tuple-element.21), channel_id=1, source_target_pairs={{0,8},{4,12},{8,0},{12,4},{16,24},{20,28},{24,16},{28,20},{1,9},{5... | collective-permute-start | bytes 98312 | tf_op jit(solution)/shard_map/ppermute | solution.py:18
  28.1 3.7 %collective-permute-start.16 = (f32[32,128]{1,0:T(8,128)S(1)}, f32[32,128]{1,0:T(8,128)S(1)}, u32[]{:S(2)}, u32[]{:S(2)}) collective-permute-start(f32[32,128]{1,0:T(8,128)S(1)} %get-tuple-element.24), channel_id=1, source_target_pairs={{0,2},{1,3},{2,0},{3,1},{4,6},{5,7},{6,4},{7,5},{8,10},{9,11},{10,... | collective-permute-start | bytes 49160 | tf_op jit(solution)/shard_map/ppermute | solution.py:18
  29.6 3.2 %collective-permute-start.17 = (f32[32,128]{1,0:T(8,128)S(1)}, f32[32,128]{1,0:T(8,128)S(1)}, u32[]{:S(2)}, u32[]{:S(2)}) collective-permute-start(f32[32,128]{1,0:T(8,128)S(1)} %get-tuple-element.25), channel_id=1, source_target_pairs={{0,3},{1,2},{2,1},{3,0},{4,7},{5,6},{6,5},{7,4},{8,11},{9,10},{10,... | collective-permute-start | bytes 49160 | tf_op jit(solution)/shard_map/ppermute | solution.py:18

commit v29 on v24

--- a/solution.py
+++ b/solution.py
@@ -50,14 +50,29 @@
     return blocks[pl.ds(a * order * block_cols + b, order, stride=block_cols), :] * weight
 
 
-def prepare_kernel(tall, presence, blocks, factor, mine, *swaps):
+def prepare_kernel(tall, presence_at, blocks_at, factor_at, mine_at, *refs):
+    count = (len(refs) - 5) // 2
+    swaps_at, (presence, blocks, factor, mine) = refs[:count], refs[count : count + 4]
+    swaps, sems = refs[count + 4 : -1], refs[-1]
+    sources = (presence_at, blocks_at, factor_at, mine, *swaps)
+    targets = (presence, blocks, factor, mine_at, *swaps_at)
+    moves = [
+        pltpu.make_async_copy(source, target, sems.at[i])
+        for i, (source, target) in enumerate(zip(sources, targets))
+    ]
+    for move in moves[:3]:
+        move.start()
     rows, span = mine.shape
-    mine[...] = factor[:, pl.ds(pl.multiple_of(lax.axis_index("col") * span, LANES), span)]
     row_bit = lax.axis_index("row") & 1
     same = row_bit == (lax.axis_index("col") & 1)
     order = blocks.shape[1]
     block_cols = blocks.shape[0] // rows
+    moves[2].wait()
+    mine[...] = factor[:, pl.ds(pl.multiple_of(lax.axis_index("col") * span, LANES), span)]
+    moves[3].start()
     half = parity_half(factor[...], tall, 1 - row_bit)
+    moves[0].wait()
+    moves[1].wait()
     for b, swap in enumerate(swaps):
         for a in range(rows // order):
             here = pl.ds(a * order, order)
@@ -67,6 +82,9 @@
                 continue
             block = masked_block(presence, blocks, block_cols, a, b)
             swap[here, :] = jnp.where(same, part, block) if part.shape[1] else block
+        moves[4 + b].start()
+    for move in moves[3:]:
+        move.wait()
 
 
 def prepare(presence, blocks, own, span, tall):
@@ -86,12 +104,22 @@
         half = jnp.pad(half, ((0, depth - half.shape[0]), (0, 0), (0, 0)))
         padded = jnp.pad(masked, ((0, depth - block_cols), (0, 0), (0, 0)))
         return mine, list(jnp.where(same, half, padded))
+    part = pltpu.VMEM((rows, order), jnp.float32)
+    anywhere = pl.BlockSpec(memory_space=pl.ANY)
     mine, *swaps = pl.pallas_call(
         functools.partial(prepare_kernel, tall),
         out_shape=(jax.ShapeDtypeStruct((rows, span), jnp.float32),)
         + (jax.ShapeDtypeStruct((rows, order), jnp.float32),) * depth,
-        in_specs=[WHOLE] * 3,
-        out_specs=(WHOLE,) * (1 + depth),
+        in_specs=[anywhere] * 3,
+        out_specs=(anywhere,) * (1 + depth),
+        scratch_shapes=[
+            pltpu.VMEM(presence.shape, jnp.int32),
+            pltpu.VMEM(blocks.shape, jnp.float32),
+            pltpu.VMEM(own.shape, jnp.float32),
+            pltpu.VMEM((rows, span), jnp.float32),
+            *[part] * depth,
+            pltpu.SemaphoreType.DMA((4 + depth,)),
+        ],
         cost_estimate=LIGHT,
     )(presence, blocks, own)
     return mine, swaps

time: 32.7 us -> 33 us (level)
  no operation moved by 1% of the time
where the time goes in v29:
time: 33 us; the launch traced here: 32.8 us
  starting transfers between devices  18.1 us (55%)
  waiting for transfers between devices  10.3 us (31%)
  Pallas kernels  3.67 us (11%)
  between operations  0.78 us (2%)
    ppermute x16, starting transfers between devices, flipped(): lax.ppermute(value, axis, [(i, i ^ flip) for i in range(lax.axis_size(axi...  15.6 us
    ppermute x16, waiting for transfers between devices, flipped(): lax.ppermute(value, axis, [(i, i ^ flip) for i in range(lax.axis_size(axi...  10.2 us
    ppermute x2, starting transfers between devices, crossed(): return lax.ppermute(swap, ('row', 'col'), cross)  2.53 us
    pallas_call x1, Pallas kernels, prepare(): pl.pallas_call(functools.partial(prepare_kernel, tall), out_shape=(jax.Sh...  1.97 us
  transfers between devices with their start and end apart: 18, of which 6 were waited for; matrix products, arithmetic and copies ran while one was open for 0% of the time, Pallas kernels for 2%

profile of v29, /device:TPU:0, one launch (start us, length us, event | category | flops | bytes accessed | tf_op | source)
XLA Modules:
  0.0 32.8 jit_solution(273323093607704311)
XLA Ops:
  0.6 2.0 %shard_map.59 = (f32[128,128]{1,0:T(8,128)}, f32[128,128]{1,0:T(8,128)}, f32[128,128]{1,0:T(8,128)}) custom-call(s32[1,2]{1,0:T(1,128)} %bitcast.9, f32[256,128]{1,0:T(8,128)} %bitcast.4, f32[128,512]{1,0:T(8,128)} %bitcast.7), custom_call_target="tpu_custom_call" | custom-call | flops 1000 | bytes 1000 | tf_op jit(solution)/shard_map/pallas_call | solution.py:109
  2.6 2.4 %collective-permute-start = (f32[128,128]{1,0:T(8,128)}, f32[128,128]{1,0:T(8,128)S(1)}, u32[]{:S(2)}, u32[]{:S(2)}) collective-permute-start(f32[128,128]{1,0:T(8,128)} %get-tuple-element.15), channel_id=1, source_target_pairs={{0,5},{1,4},{2,7},{3,6},{4,1},{5,0},{6,3},{7,2},{8,13},{9,12},{10,... | collective-permute-start | bytes 196616 | tf_op jit(solution)/shard_map/ppermute | solution.py:322
  5.1 0.1 collective-permute-start.1
  5.1 3.3 %collective-permute-start.7 = (f32[128,128]{1,0:T(8,128)}, f32[128,128]{1,0:T(8,128)S(1)}, u32[]{:S(2)}, u32[]{:S(2)}) collective-permute-start(f32[128,128]{1,0:T(8,128)} %get-tuple-element.17.refs_0_), channel_id=1, source_target_pairs={{0,16},{4,20},{8,24},{12,28},{16,0},{20,4},{24,8},{28,12},{1,17},{... | collective-permute-start | bytes 196616 | tf_op jit(solution)/shard_map/ppermute | solution.py:18
  8.5 1.6 %collective-permute-start.8 = (f32[128,128]{1,0:T(8,128)}, f32[128,128]{1,0:T(8,128)S(1)}, u32[]{:S(2)}, u32[]{:S(2)}) collective-permute-start(f32[128,128]{1,0:T(8,128)} %get-tuple-element.17.refs_0_), channel_id=1, source_target_pairs={{0,8},{4,12},{8,0},{12,4},{16,24},{20,28},{24,16},{28,20},{1,9},{5... | collective-permute-start | bytes 196616 | tf_op jit(solution)/shard_map/ppermute | solution.py:18
  10.1 1.5 %collective-permute-start.3 = (f32[128,128]{1,0:T(8,128)S(1)}, f32[128,128]{1,0:T(8,128)S(1)}, u32[]{:S(2)}, u32[]{:S(2)}) collective-permute-start(f32[128,128]{1,0:T(8,128)S(1)} %shard_map.60.refs_0_), channel_id=1, source_target_pairs={{0,2},{1,3},{2,0},{3,1},{4,6},{5,7},{6,4},{7,5},{8,10},{9,11},{10,... | collective-permute-start | bytes 196616 | tf_op jit(solution)/shard_map/ppermute | solution.py:18
  11.8 0.5 %collective-permute-start.4 = (f32[128,128]{1,0:T(8,128)S(1)}, f32[128,128]{1,0:T(8,128)S(1)}, u32[]{:S(2)}, u32[]{:S(2)}) collective-permute-start(f32[128,128]{1,0:T(8,128)S(1)} %shard_map.61.refs_1_), channel_id=1, source_target_pairs={{0,2},{1,3},{2,0},{3,1},{4,6},{5,7},{6,4},{7,5},{8,10},{9,11},{10,... | collective-permute-start | bytes 196616 | tf_op jit(solution)/shard_map/ppermute | solution.py:18
  12.3 0.9 %collective-permute-start.9 = (f32[128,128]{1,0:T(8,128)S(1)}, f32[128,128]{1,0:T(8,128)S(1)}, u32[]{:S(2)}, u32[]{:S(2)}) collective-permute-start(f32[128,128]{1,0:T(8,128)S(1)} %collective-permute-done.7.refs_1_), channel_id=1, source_target_pairs={{0,8},{4,12},{8,0},{12,4},{16,24},{20,28},{24,16},{28,20},{1,9},{5... | collective-permute-start | bytes 196616 | tf_op jit(solution)/shard_map/ppermute | solution.py:18
  13.3 0.6 %collective-permute-start.11 = (f32[2,128,128]{2,1,0:T(8,128)S(1)}, f32[2,128,128]{2,1,0:T(8,128)S(1)}, u32[]{:S(2)}, u32[]{:S(2)}) collective-permute-start(f32[2,128,128]{2,1,0:T(8,128)S(1)} %shard_map.66.swapped), channel_id=1, source_target_pairs={{0,1},{1,0},{2,3},{3,2},{4,5},{5,4},{6,7},{7,6},{8,9},{9,8},{10,11... | collective-permute-start | bytes 393224 | tf_op jit(solution)/shard_map/ppermute | solution.py:18
  13.9 1.0 %collective-permute-done.3.refs_2_ = f32[128,128]{1,0:T(8,128)S(1)} collective-permute-done((f32[128,128]{1,0:T(8,128)S(1)}, f32[128,128]{1,0:T(8,128)S(1)}, u32[]{:S(2)}, u32[]{:S(2)}) %collective-permute-start.3) | collective-permute-done | bytes 65568 | tf_op jit(solution)/shard_map/ppermute | solution.py:18
  14.9 1.2 %collective-permute-done.4.refs_3_ = f32[128,128]{1,0:T(8,128)S(1)} collective-permute-done((f32[128,128]{1,0:T(8,128)S(1)}, f32[128,128]{1,0:T(8,128)S(1)}, u32[]{:S(2)}, u32[]{:S(2)}) %collective-permute-start.4) | collective-permute-done | bytes 65568 | tf_op jit(solution)/shard_map/ppermute | solution.py:18
  16.1 0.5 %collective-permute-done.9.refs_3_ = f32[128,128]{1,0:T(8,128)S(1)} collective-permute-done((f32[128,128]{1,0:T(8,128)S(1)}, f32[128,128]{1,0:T(8,128)S(1)}, u32[]{:S(2)}, u32[]{:S(2)}) %collective-permute-start.9) | collective-permute-done | bytes 65568 | tf_op jit(solution)/shard_map/ppermute | solution.py:18
  16.6 0.7 %collective-permute-done.6.refs_5_ = f32[128,128]{1,0:T(8,128)S(1)} collective-permute-done((f32[128,128]{1,0:T(8,128)S(1)}, f32[128,128]{1,0:T(8,128)S(1)}, u32[]{:S(2)}, u32[]{:S(2)}) %collective-permute-start.6) | collective-permute-done | bytes 65568 | tf_op jit(solution)/shard_map/ppermute | solution.py:18
  17.3 0.4 %shard_map.64.both = f32[256,128]{1,0:T(8,128)S(1)} custom-call(f32[2,128,128]{2,1,0:T(8,128)S(1)} %shard_map.62.refs_0_, f32[2,128,128]{2,1,0:T(8,128)S(1)} %collective-permute-done.2.refs_1_, f32[128,128]{1,0:T(8,128)S(1)} %collective-permute-done.3.refs_2_, f32[128,128]{1,0:T(8,128)S(1)} %collective-permute-done.4.refs_3_, ...), custom_call_target="tpu_custom_call" | custom-call | flops 1000 | bytes 1000 | tf_op jit(solution)/shard_map/pallas_call | solution.py:175
  17.7 1.6 %collective-permute-start.10 = (f32[256,128]{1,0:T(8,128)S(1)}, f32[256,128]{1,0:T(8,128)S(1)}, u32[]{:S(2)}, u32[]{:S(2)}) collective-permute-start(f32[256,128]{1,0:T(8,128)S(1)} %shard_map.64.both), channel_id=1, source_target_pairs={{0,4},{4,0},{8,12},{12,8},{16,20},{20,16},{24,28},{28,24},{1,5},{5... | collective-permute-start | bytes 393224 | tf_op jit(solution)/shard_map/ppermute | solution.py:18
  19.3 0.1 shard_map.65.stay
  19.4 3.9 %collective-permute-done.10.got = f32[256,128]{1,0:T(8,128)S(1)} collective-permute-done((f32[256,128]{1,0:T(8,128)S(1)}, f32[256,128]{1,0:T(8,128)S(1)}, u32[]{:S(2)}, u32[]{:S(2)}) %collective-permute-start.10) | collective-permute-done | bytes 131104 | tf_op jit(solution)/shard_map/ppermute | solution.py:18
  23.3 0.3 %shard_map.67 = (f32[64,128]{1,0:T(8,128)S(1)}, f32[64,128]{1,0:T(8,128)S(1)}, f32[64,128]{1,0:T(8,128)S(1)}, f32[64,128]{1,0:T(8,128)S(1)}, f32[32,128]{1,0:T(8...) custom-call(f32[256,128]{1,0:T(8,128)S(1)} %shard_map.64.both, ...), custom_call_target="tpu_custom_call" | custom-call | flops 1000 | bytes 1000 | tf_op jit(solution)/shard_map/pallas_call | solution.py:234
  23.7 2.3 %collective-permute-start.12 = (f32[64,128]{1,0:T(8,128)S(1)}, f32[64,128]{1,0:T(8,128)S(1)}, u32[]{:S(2)}, u32[]{:S(2)}) collective-permute-start(f32[64,128]{1,0:T(8,128)S(1)} %get-tuple-element.19), channel_id=1, source_target_pairs={{0,24},{4,28},{8,16},{12,20},{16,8},{20,12},{24,0},{28,4},{1,25},{... | collective-permute-start | bytes 98312 | tf_op jit(solution)/shard_map/ppermute | solution.py:18
  26.1 2.1 %collective-permute-start.14 = (f32[64,128]{1,0:T(8,128)S(1)}, f32[64,128]{1,0:T(8,128)S(1)}, u32[]{:S(2)}, u32[]{:S(2)}) collective-permute-start(f32[64,128]{1,0:T(8,128)S(1)} %get-tuple-element.21), channel_id=1, source_target_pairs={{0,8},{4,12},{8,0},{12,4},{16,24},{20,28},{24,16},{28,20},{1,9},{5... | collective-permute-start | bytes 98312 | tf_op jit(solution)/shard_map/ppermute | solution.py:18
  28.2 0.6 %collective-permute-start.16 = (f32[32,128]{1,0:T(8,128)S(1)}, f32[32,128]{1,0:T(8,128)S(1)}, u32[]{:S(2)}, u32[]{:S(2)}) collective-permute-start(f32[32,128]{1,0:T(8,128)S(1)} %get-tuple-element.24), channel_id=1, source_target_pairs={{0,2},{1,3},{2,0},{3,1},{4,6},{5,7},{6,4},{7,5},{8,10},{9,11},{10,... | collective-permute-start | bytes 49160 | tf_op jit(solution)/shard_map/ppermute | solution.py:18
  28.8 0.4 %collective-permute-start.17 = (f32[32,128]{1,0:T(8,128)S(1)}, f32[32,128]{1,0:T(8,128)S(1)}, u32[]{:S(2)}, u32[]{:S(2)}) collective-permute-start(f32[32,128]{1,0:T(8,128)S(1)} %get-tuple-element.25), channel_id=1, source_target_pairs={{0,3},{1,2},{2,1},{3,0},{4,7},{5,6},{6,5},{7,4},{8,11},{9,10},{10,... | collective-permute-start | bytes 49160 | tf_op jit(solution)/shard_map/ppermute | solution.py:18
  29.2 2.9 %collective-permute-done.16.refs_6_ = f32[32,128]{1,0:T(8,128)S(1)} collective-permute-done((f32[32,128]{1,0:T(8,128)S(1)}, f32[32,128]{1,0:T(8,128)S(1)}, u32[]{:S(2)}, u32[]{:S(2)}) %collective-permute-start.16) | collective-permute-done | bytes 16416 | tf_op jit(solution)/shard_map/ppermute | solution.py:18
  32.1 0.7 %shard_map.68 = (f32[32,512]{1,0:T(8,128)}, f32[64,128]{1,0:T(8,128)}) custom-call(f32[64,128]{1,0:T(8,128)S(1)} %get-tuple-element.18.refs_0_, f32[64,128]{1,0:T(8,128)S(1)} %collective-permute-done.12.refs_1_, f32[64,128]{1,0:T(8,128)S(1)} %collective-permute-done.13.refs_2_, f32[64,128]{1,0:T(8,128)S(1)} %collective-permute-done.14.refs_3_, ...), custom_call_target="tpu_custom_call" | custom-call | flops 1000 | bytes 1000 | tf_op jit(solution)/shard_map/pallas_call | solution.py:265
  (32 shorter events, 0.5 us)
Async XLA Ops:
  0.6 9.4 %copy-start = (f32[1,1,128,2,1,128]{5,4,3,2,1,0:T(1,128)S(1)}, f32[1,1,128,2,1,128]{5,4,3,2,1,0:T(1,128)}, u32[]{:S(2)}) copy-start(f32[1,1,128,2,1,128]{5,4,3,2,1,0:T(1,128)} %param.4) | copy-start | bytes 393220
  2.6 7.4 %collective-permute-start = (f32[128,128]{1,0:T(8,128)}, f32[128,128]{1,0:T(8,128)S(1)}, u32[]{:S(2)}, u32[]{:S(2)}) collective-permute-start(f32[128,128]{1,0:T(8,128)} %get-tuple-element.15), channel_id=1, source_target_pairs={{0,5},{1,4},{2,7},{3,6},{4,1},{5,0},{6,3},{7,2},{8,13},{9,12},{10,... | collective-permute-start | bytes 196616 | tf_op jit(solution)/shard_map/ppermute | solution.py:322
  5.1 5.0 %copy-start.3 = (s32[1,1,2,1]{2,3,1,0:T(1,128)S(1)}, s32[1,1,2,1]{2,3,1,0:T(1,128)}, u32[]{:S(2)}) copy-start(s32[1,1,2,1]{2,3,1,0:T(1,128)} %param.5) | copy-start | bytes 28
  5.1 6.6 %collective-permute-start.1 = (f32[128,128]{1,0:T(8,128)}, f32[128,128]{1,0:T(8,128)S(1)}, u32[]{:S(2)}, u32[]{:S(2)}) collective-permute-start(f32[128,128]{1,0:T(8,128)} %get-tuple-element.16), channel_id=1, source_target_pairs={{0,5},{1,4},{2,7},{3,6},{4,1},{5,0},{6,3},{7,2},{8,13},{9,12},{10,... | collective-permute-start | bytes 196616 | tf_op jit(solution)/shard_map/ppermute | solution.py:322
  5.1 7.1 %collective-permute-start.7 = (f32[128,128]{1,0:T(8,128)}, f32[128,128]{1,0:T(8,128)S(1)}, u32[]{:S(2)}, u32[]{:S(2)}) collective-permute-start(f32[128,128]{1,0:T(8,128)} %get-tuple-element.17.refs_0_), channel_id=1, source_target_pairs={{0,16},{4,20},{8,24},{12,28},{16,0},{20,4},{24,8},{28,12},{1,17},{... | collective-permute-start | bytes 196616 | tf_op jit(solution)/shard_map/ppermute | solution.py:18
  8.5 4.9 %collective-permute-start.8 = (f32[128,128]{1,0:T(8,128)}, f32[128,128]{1,0:T(8,128)S(1)}, u32[]{:S(2)}, u32[]{:S(2)}) collective-permute-start(f32[128,128]{1,0:T(8,128)} %get-tuple-element.17.refs_0_), channel_id=1, source_target_pairs={{0,8},{4,12},{8,0},{12,4},{16,24},{20,28},{24,16},{28,20},{1,9},{5... | collective-permute-start | bytes 196616 | tf_op jit(solution)/shard_map/ppermute | solution.py:18
  10.1 4.8 %collective-permute-start.3 = (f32[128,128]{1,0:T(8,128)S(1)}, f32[128,128]{1,0:T(8,128)S(1)}, u32[]{:S(2)}, u32[]{:S(2)}) collective-permute-start(f32[128,128]{1,0:T(8,128)S(1)} %shard_map.60.refs_0_), channel_id=1, source_target_pairs={{0,2},{1,3},{2,0},{3,1},{4,6},{5,7},{6,4},{7,5},{8,10},{9,11},{10,... | collective-permute-start | bytes 196616 | tf_op jit(solution)/shard_map/ppermute | solution.py:18
  11.8 4.3 %collective-permute-start.4 = (f32[128,128]{1,0:T(8,128)S(1)}, f32[128,128]{1,0:T(8,128)S(1)}, u32[]{:S(2)}, u32[]{:S(2)}) collective-permute-start(f32[128,128]{1,0:T(8,128)S(1)} %shard_map.61.refs_1_), channel_id=1, source_target_pairs={{0,2},{1,3},{2,0},{3,1},{4,6},{5,7},{6,4},{7,5},{8,10},{9,11},{10,... | collective-permute-start | bytes 196616 | tf_op jit(solution)/shard_map/ppermute | solution.py:18
  12.3 4.3 %collective-permute-start.9 = (f32[128,128]{1,0:T(8,128)S(1)}, f32[128,128]{1,0:T(8,128)S(1)}, u32[]{:S(2)}, u32[]{:S(2)}) collective-permute-start(f32[128,128]{1,0:T(8,128)S(1)} %collective-permute-done.7.refs_1_), channel_id=1, source_target_pairs={{0,8},{4,12},{8,0},{12,4},{16,24},{20,28},{24,16},{28,20},{1,9},{5... | collective-permute-start | bytes 196616 | tf_op jit(solution)/shard_map/ppermute | solution.py:18
  13.2 3.3 %copy-start.4 = (f32[128,128]{1,0:T(8,128)S(1)}, f32[128,128]{1,0:T(8,128)}, u32[]{:S(2)}) copy-start(f32[128,128]{1,0:T(8,128)} %get-tuple-element.17.refs_0_) | copy-start | bytes 196612
  13.2 3.4 %collective-permute-start.2 = (f32[2,128,128]{2,1,0:T(8,128)S(1)}, f32[2,128,128]{2,1,0:T(8,128)S(1)}, u32[]{:S(2)}, u32[]{:S(2)}) collective-permute-start(f32[2,128,128]{2,1,0:T(8,128)S(1)} %shard_map.62.refs_0_), channel_id=1, source_target_pairs={{0,1},{1,0},{2,3},{3,2},{4,5},{5,4},{6,7},{7,6},{8,9},{9,8},{10,11... | collective-permute-start | bytes 393224 | tf_op jit(solution)/shard_map/ppermute | solution.py:18
  13.3 6.1 %collective-permute-start.11 = (f32[2,128,128]{2,1,0:T(8,128)S(1)}, f32[2,128,128]{2,1,0:T(8,128)S(1)}, u32[]{:S(2)}, u32[]{:S(2)}) collective-permute-start(f32[2,128,128]{2,1,0:T(8,128)S(1)} %shard_map.66.swapped), channel_id=1, source_target_pairs={{0,1},{1,0},{2,3},{3,2},{4,5},{5,4},{6,7},{7,6},{8,9},{9,8},{10,11... | collective-permute-start | bytes 393224 | tf_op jit(solution)/shard_map/ppermute | solution.py:18
  14.9 1.7 %collective-permute-start.5 = (f32[128,128]{1,0:T(8,128)S(1)}, f32[128,128]{1,0:T(8,128)S(1)}, u32[]{:S(2)}, u32[]{:S(2)}) collective-permute-start(f32[128,128]{1,0:T(8,128)S(1)} %collective-permute-done.3.refs_2_), channel_id=1, source_target_pairs={{0,1},{1,0},{2,3},{3,2},{4,5},{5,4},{6,7},{7,6},{8,9},{9,8},{10,11... | collective-permute-start | bytes 196616 | tf_op jit(solution)/shard_map/ppermute | solution.py:18
  16.1 1.3 %collective-permute-start.6 = (f32[128,128]{1,0:T(8,128)S(1)}, f32[128,128]{1,0:T(8,128)S(1)}, u32[]{:S(2)}, u32[]{:S(2)}) collective-permute-start(f32[128,128]{1,0:T(8,128)S(1)} %collective-permute-done.4.refs_3_), channel_id=1, source_target_pairs={{0,1},{1,0},{2,3},{3,2},{4,5},{5,4},{6,7},{7,6},{8,9},{9,8},{10,11... | collective-permute-start | bytes 196616 | tf_op jit(solution)/shard_map/ppermute | solution.py:18
  16.6 2.7 %copy-start.1 = (f32[1,1,128,512]{3,2,1,0:T(8,128)S(1)}, f32[1,1,128,512]{3,2,1,0:T(8,128)}, u32[]{:S(2)}) copy-start(f32[1,1,128,512]{3,2,1,0:T(8,128)} %param.6) | copy-start | bytes 786436
  17.7 5.6 %copy-start.2 = (f32[64,128]{1,0:T(8,128)S(1)}, f32[64,128]{1,0:T(8,128)}, u32[]{:S(2)}) copy-start(f32[64,128]{1,0:T(8,128)} %dinv.1) | copy-start | bytes 98308
  17.7 5.6 %collective-permute-start.10 = (f32[256,128]{1,0:T(8,128)S(1)}, f32[256,128]{1,0:T(8,128)S(1)}, u32[]{:S(2)}, u32[]{:S(2)}) collective-permute-start(f32[256,128]{1,0:T(8,128)S(1)} %shard_map.64.both), channel_id=1, source_target_pairs={{0,4},{4,0},{8,12},{12,8},{16,20},{20,16},{24,28},{28,24},{1,5},{5... | collective-permute-start | bytes 393224 | tf_op jit(solution)/shard_map/ppermute | solution.py:18
  23.7 5.1 %collective-permute-start.15 = (f32[32,128]{1,0:T(8,128)S(1)}, f32[32,128]{1,0:T(8,128)S(1)}, u32[]{:S(2)}, u32[]{:S(2)}) collective-permute-start(f32[32,128]{1,0:T(8,128)S(1)} %get-tuple-element.23), channel_id=1, source_target_pairs={{0,1},{1,0},{2,3},{3,2},{4,5},{5,4},{6,7},{7,6},{8,9},{9,8},{10,11... | collective-permute-start | bytes 49160 | tf_op jit(solution)/shard_map/ppermute | solution.py:18
  23.7 8.4 %collective-permute-start.12 = (f32[64,128]{1,0:T(8,128)S(1)}, f32[64,128]{1,0:T(8,128)S(1)}, u32[]{:S(2)}, u32[]{:S(2)}) collective-permute-start(f32[64,128]{1,0:T(8,128)S(1)} %get-tuple-element.19), channel_id=1, source_target_pairs={{0,24},{4,28},{8,16},{12,20},{16,8},{20,12},{24,0},{28,4},{1,25},{... | collective-permute-start | bytes 98312 | tf_op jit(solution)/shard_map/ppermute | solution.py:18
  26.1 6.1 %collective-permute-start.13 = (f32[64,128]{1,0:T(8,128)S(1)}, f32[64,128]{1,0:T(8,128)S(1)}, u32[]{:S(2)}, u32[]{:S(2)}) collective-permute-start(f32[64,128]{1,0:T(8,128)S(1)} %get-tuple-element.20), channel_id=1, source_target_pairs={{0,16},{4,20},{8,24},{12,28},{16,0},{20,4},{24,8},{28,12},{1,17},{... | collective-permute-start | bytes 98312 | tf_op jit(solution)/shard_map/ppermute | solution.py:18
  26.1 6.1 %collective-permute-start.14 = (f32[64,128]{1,0:T(8,128)S(1)}, f32[64,128]{1,0:T(8,128)S(1)}, u32[]{:S(2)}, u32[]{:S(2)}) collective-permute-start(f32[64,128]{1,0:T(8,128)S(1)} %get-tuple-element.21), channel_id=1, source_target_pairs={{0,8},{4,12},{8,0},{12,4},{16,24},{20,28},{24,16},{28,20},{1,9},{5... | collective-permute-start | bytes 98312 | tf_op jit(solution)/shard_map/ppermute | solution.py:18
  28.2 3.9 %collective-permute-start.16 = (f32[32,128]{1,0:T(8,128)S(1)}, f32[32,128]{1,0:T(8,128)S(1)}, u32[]{:S(2)}, u32[]{:S(2)}) collective-permute-start(f32[32,128]{1,0:T(8,128)S(1)} %get-tuple-element.24), channel_id=1, source_target_pairs={{0,2},{1,3},{2,0},{3,1},{4,6},{5,7},{6,4},{7,5},{8,10},{9,11},{10,... | collective-permute-start | bytes 49160 | tf_op jit(solution)/shard_map/ppermute | solution.py:18
  28.8 3.3 %collective-permute-start.17 = (f32[32,128]{1,0:T(8,128)S(1)}, f32[32,128]{1,0:T(8,128)S(1)}, u32[]{:S(2)}, u32[]{:S(2)}) collective-permute-start(f32[32,128]{1,0:T(8,128)S(1)} %get-tuple-element.25), channel_id=1, source_target_pairs={{0,3},{1,2},{2,1},{3,0},{4,7},{5,6},{6,5},{7,4},{8,11},{9,10},{10,... | collective-permute-start | bytes 49160 | tf_op jit(solution)/shard_map/ppermute | solution.py:18

commit v30 on v24

--- a/solution.py
+++ b/solution.py
@@ -218,24 +218,58 @@
     return outs[: len(flips)], outs[len(flips) :]
 
 
-def close_kernel(count, *refs):
+def at_place(ref, place):
+    return ref[...] if place is None else ref[place]
+
+
+def joined_kernel(places, *refs):
+    for at, (place, ref) in enumerate(zip(places, refs[:-1])):
+        refs[-1][at] = at_place(ref, place)
+
+
+def joined(pieces):
+    shape = pieces[0][0].shape[-2:]
+    return pl.pallas_call(
+        functools.partial(joined_kernel, [place for _, place in pieces]),
+        out_shape=jax.ShapeDtypeStruct((len(pieces),) + shape, jnp.float32),
+        in_specs=[WHOLE] * len(pieces),
+        out_specs=WHOLE,
+        cost_estimate=LIGHT,
+        compiler_params=ROOM,
+    )(*[array for array, _ in pieces])
+
+
+def swap_over_col(outward):
+    pieces = {(0, flip): (piece, None) for flip, piece in enumerate(outward)}
+    bit = len(outward) // 2
+    while bit:
+        keys = [key for key in sorted(pieces) if key[1] & bit]
+        came = flipped(joined([pieces.pop(key) for key in keys]), "col", bit)
+        for at, (source, flip) in enumerate(keys):
+            pieces[source ^ bit, flip ^ bit] = (came, at)
+        bit //= 2
+    return [pieces[source, 0] for source in range(len(outward))]
+
+
+def close_kernel(count, places, *refs):
     met, arrived = refs[:count], refs[count:-2]
     off_diag, diag_block = refs[-2:]
-    span = arrived[0].shape[1]
-    for flip, piece in enumerate(arrived):
+    span = arrived[0].shape[-1]
+    for flip, (piece, place) in enumerate(zip(arrived, places)):
         first = pl.multiple_of((lax.axis_index("col") ^ flip) * span, LANES)
-        off_diag[:, pl.ds(first, span)] = piece[...]
+        off_diag[:, pl.ds(first, span)] = at_place(piece, place)
     diag_block[...] = sum([piece[...] for piece in met[1:]], met[0][...])
 
 
 def close(arrived, met):
-    share, span = arrived[0].shape
+    share, span = arrived[0][0].shape[-2:]
     if span % LANES:
         me = lax.axis_index("col")
-        laid = [lax.select_n(me ^ j, *arrived) for j in range(len(arrived))]
+        pieces = [array if place is None else array[place] for array, place in arrived]
+        laid = [lax.select_n(me ^ j, *pieces) for j in range(len(pieces))]
         return jnp.concatenate(laid, axis=1), sum(met[1:], met[0])
     return pl.pallas_call(
-        functools.partial(close_kernel, len(met)),
+        functools.partial(close_kernel, len(met), [place for _, place in arrived]),
         out_shape=(
             jax.ShapeDtypeStruct((share, span * len(arrived)), jnp.float32),
             jax.ShapeDtypeStruct(met[0].shape, jnp.float32),
@@ -244,7 +278,7 @@
         out_specs=(WHOLE, WHOLE),
         cost_estimate=LIGHT,
         compiler_params=ROOM,
-    )(*met, *arrived)
+    )(*met, *[array for array, _ in arrived])
 
 
 def pick_kernel(block_cols, b, presence, blocks, swapped, held):
@@ -335,8 +369,7 @@
         both, got, stay, swapped, mate_swapped, dinv, order, flips, groups_col
     )
     met = [flipped(piece, "row", flip) if flip else piece for flip, piece in zip(flips, along)]
-    arrived = [flipped(piece, "col", f) if f else piece for f, piece in enumerate(outward)]
-    off_diag, diag_block = close(arrived, met)
+    off_diag, diag_block = close(swap_over_col(outward), met)
     return (off_diag.reshape(block_rows, 1, share, width), diag_block)
 
 

time: 32.7 us -> 32.9 us (level)
  waiting for transfers between devices: 10.3 us -> 10.9 us
  starting transfers between devices: 18 us -> 17.5 us
    ppermute x16 -> x15, waiting for transfers between devices: 10.3 us -> 10.9 us  [flipped(): lax.ppermute(value, axis, [(i, i ^ flip) for i in range(lax.axis_size(axi...]
    ppermute x16 -> x15, starting transfers between devices: 15.6 us -> 15.1 us  [flipped(): lax.ppermute(value, axis, [(i, i ^ flip) for i in range(lax.axis_size(axi...]
    pallas_call x1 -> x3, Pallas kernels: 0.66 us -> 0.66 us  [the longest x1 0.66 us: close(): pl.pallas_call(functools.partial(close_kernel, len(met), [place for _, pl...]
  transfers between devices with their start and end apart: 18 -> 17, of which waited for: 6 -> 7; matrix products, arithmetic and copies ran while one was open for 0% -> 0% of each run, Pallas kernels for 2% -> 2%
where the time goes in v30:
time: 32.9 us; the launch traced here: 32.8 us
  starting transfers between devices  17.5 us (53%)
  waiting for transfers between devices  10.9 us (33%)
  Pallas kernels  3.55 us (11%)
  between operations  0.77 us (2%)
    ppermute x15, starting transfers between devices, flipped(): lax.ppermute(value, axis, [(i, i ^ flip) for i in range(lax.axis_size(axi...  15.1 us
    ppermute x15, waiting for transfers between devices, flipped(): lax.ppermute(value, axis, [(i, i ^ flip) for i in range(lax.axis_size(axi...  10.9 us
    ppermute x2, starting transfers between devices, crossed(): return lax.ppermute(swap, ('row', 'col'), cross)  2.42 us
    pallas_call x1, Pallas kernels, prepare(): pl.pallas_call(functools.partial(prepare_kernel, tall), out_shape=(jax.Sh...  1.84 us
  transfers between devices with their start and end apart: 17, of which 7 were waited for; matrix products, arithmetic and copies ran while one was open for 0% of the time, Pallas kernels for 2%

profile of v30, /device:TPU:0, one launch (start us, length us, event | category | flops | bytes accessed | tf_op | source)
XLA Modules:
  0.0 32.8 jit_solution(10940547054772353896)
XLA Ops:
  0.6 1.8 %shard_map.59 = (f32[128,128]{1,0:T(8,128)}, f32[128,128]{1,0:T(8,128)}, f32[128,128]{1,0:T(8,128)}) custom-call(s32[1,2]{1,0:T(1,128)} %bitcast.9, f32[256,128]{1,0:T(8,128)} %bitcast.4, f32[128,512]{1,0:T(8,128)} %bitcast.7), custom_call_target="tpu_custom_call" | custom-call | flops 1000 | bytes 1000 | tf_op jit(solution)/shard_map/pallas_call | solution.py:89
  2.5 2.4 %collective-permute-start = (f32[128,128]{1,0:T(8,128)}, f32[128,128]{1,0:T(8,128)S(1)}, u32[]{:S(2)}, u32[]{:S(2)}) collective-permute-start(f32[128,128]{1,0:T(8,128)} %get-tuple-element.15), channel_id=1, source_target_pairs={{0,5},{1,4},{2,7},{3,6},{4,1},{5,0},{6,3},{7,2},{8,13},{9,12},{10,... | collective-permute-start | bytes 196616 | tf_op jit(solution)/shard_map/ppermute | solution.py:328
  4.9 3.4 %collective-permute-start.7 = (f32[128,128]{1,0:T(8,128)}, f32[128,128]{1,0:T(8,128)S(1)}, u32[]{:S(2)}, u32[]{:S(2)}) collective-permute-start(f32[128,128]{1,0:T(8,128)} %get-tuple-element.17.refs_0_), channel_id=1, source_target_pairs={{0,16},{4,20},{8,24},{12,28},{16,0},{20,4},{24,8},{28,12},{1,17},{... | collective-permute-start | bytes 196616 | tf_op jit(solution)/shard_map/ppermute | solution.py:18
  8.3 1.6 %collective-permute-start.8 = (f32[128,128]{1,0:T(8,128)}, f32[128,128]{1,0:T(8,128)S(1)}, u32[]{:S(2)}, u32[]{:S(2)}) collective-permute-start(f32[128,128]{1,0:T(8,128)} %get-tuple-element.17.refs_0_), channel_id=1, source_target_pairs={{0,8},{4,12},{8,0},{12,4},{16,24},{20,28},{24,16},{28,20},{1,9},{5... | collective-permute-start | bytes 196616 | tf_op jit(solution)/shard_map/ppermute | solution.py:18
  9.9 0.1 shard_map.60.refs_0_
  9.9 1.5 %collective-permute-start.3 = (f32[128,128]{1,0:T(8,128)S(1)}, f32[128,128]{1,0:T(8,128)S(1)}, u32[]{:S(2)}, u32[]{:S(2)}) collective-permute-start(f32[128,128]{1,0:T(8,128)S(1)} %shard_map.60.refs_0_), channel_id=1, source_target_pairs={{0,2},{1,3},{2,0},{3,1},{4,6},{5,7},{6,4},{7,5},{8,10},{9,11},{10,... | collective-permute-start | bytes 196616 | tf_op jit(solution)/shard_map/ppermute | solution.py:18
  11.6 0.5 %collective-permute-start.4 = (f32[128,128]{1,0:T(8,128)S(1)}, f32[128,128]{1,0:T(8,128)S(1)}, u32[]{:S(2)}, u32[]{:S(2)}) collective-permute-start(f32[128,128]{1,0:T(8,128)S(1)} %shard_map.61.refs_1_), channel_id=1, source_target_pairs={{0,2},{1,3},{2,0},{3,1},{4,6},{5,7},{6,4},{7,5},{8,10},{9,11},{10,... | collective-permute-start | bytes 196616 | tf_op jit(solution)/shard_map/ppermute | solution.py:18
  12.1 0.9 %collective-permute-start.9 = (f32[128,128]{1,0:T(8,128)S(1)}, f32[128,128]{1,0:T(8,128)S(1)}, u32[]{:S(2)}, u32[]{:S(2)}) collective-permute-start(f32[128,128]{1,0:T(8,128)S(1)} %collective-permute-done.7.refs_1_), channel_id=1, source_target_pairs={{0,8},{4,12},{8,0},{12,4},{16,24},{20,28},{24,16},{28,20},{1,9},{5... | collective-permute-start | bytes 196616 | tf_op jit(solution)/shard_map/ppermute | solution.py:18
  13.1 0.6 %collective-permute-start.11 = (f32[2,128,128]{2,1,0:T(8,128)S(1)}, f32[2,128,128]{2,1,0:T(8,128)S(1)}, u32[]{:S(2)}, u32[]{:S(2)}) collective-permute-start(f32[2,128,128]{2,1,0:T(8,128)S(1)} %shard_map.66.swapped), channel_id=1, source_target_pairs={{0,1},{1,0},{2,3},{3,2},{4,5},{5,4},{6,7},{7,6},{8,9},{9,8},{10,11... | collective-permute-start | bytes 393224 | tf_op jit(solution)/shard_map/ppermute | solution.py:18
  13.7 1.0 %collective-permute-done.3.refs_2_ = f32[128,128]{1,0:T(8,128)S(1)} collective-permute-done((f32[128,128]{1,0:T(8,128)S(1)}, f32[128,128]{1,0:T(8,128)S(1)}, u32[]{:S(2)}, u32[]{:S(2)}) %collective-permute-start.3) | collective-permute-done | bytes 65568 | tf_op jit(solution)/shard_map/ppermute | solution.py:18
  14.7 1.2 %collective-permute-done.4.refs_3_ = f32[128,128]{1,0:T(8,128)S(1)} collective-permute-done((f32[128,128]{1,0:T(8,128)S(1)}, f32[128,128]{1,0:T(8,128)S(1)}, u32[]{:S(2)}, u32[]{:S(2)}) %collective-permute-start.4) | collective-permute-done | bytes 65568 | tf_op jit(solution)/shard_map/ppermute | solution.py:18
  15.9 0.5 %collective-permute-done.9.refs_3_ = f32[128,128]{1,0:T(8,128)S(1)} collective-permute-done((f32[128,128]{1,0:T(8,128)S(1)}, f32[128,128]{1,0:T(8,128)S(1)}, u32[]{:S(2)}, u32[]{:S(2)}) %collective-permute-start.9) | collective-permute-done | bytes 65568 | tf_op jit(solution)/shard_map/ppermute | solution.py:18
  16.4 0.7 %collective-permute-done.6.refs_5_ = f32[128,128]{1,0:T(8,128)S(1)} collective-permute-done((f32[128,128]{1,0:T(8,128)S(1)}, f32[128,128]{1,0:T(8,128)S(1)}, u32[]{:S(2)}, u32[]{:S(2)}) %collective-permute-start.6) | collective-permute-done | bytes 65568 | tf_op jit(solution)/shard_map/ppermute | solution.py:18
  17.1 0.4 %shard_map.64.both = f32[256,128]{1,0:T(8,128)S(1)} custom-call(f32[2,128,128]{2,1,0:T(8,128)S(1)} %shard_map.62.refs_0_, f32[2,128,128]{2,1,0:T(8,128)S(1)} %collective-permute-done.2.refs_1_, f32[128,128]{1,0:T(8,128)S(1)} %collective-permute-done.3.refs_2_, f32[128,128]{1,0:T(8,128)S(1)} %collective-permute-done.4.refs_3_, ...), custom_call_target="tpu_custom_call" | custom-call | flops 1000 | bytes 1000 | tf_op jit(solution)/shard_map/pallas_call | solution.py:147
  17.5 1.6 %collective-permute-start.10 = (f32[256,128]{1,0:T(8,128)S(1)}, f32[256,128]{1,0:T(8,128)S(1)}, u32[]{:S(2)}, u32[]{:S(2)}) collective-permute-start(f32[256,128]{1,0:T(8,128)S(1)} %shard_map.64.both), channel_id=1, source_target_pairs={{0,4},{4,0},{8,12},{12,8},{16,20},{20,16},{24,28},{28,24},{1,5},{5... | collective-permute-start | bytes 393224 | tf_op jit(solution)/shard_map/ppermute | solution.py:18
  19.1 0.1 shard_map.65.stay
  19.2 3.9 %collective-permute-done.10.got = f32[256,128]{1,0:T(8,128)S(1)} collective-permute-done((f32[256,128]{1,0:T(8,128)S(1)}, f32[256,128]{1,0:T(8,128)S(1)}, u32[]{:S(2)}, u32[]{:S(2)}) %collective-permute-start.10) | collective-permute-done | bytes 131104 | tf_op jit(solution)/shard_map/ppermute | solution.py:18
  23.1 0.3 %shard_map.67 = (f32[64,128]{1,0:T(8,128)S(1)}, f32[64,128]{1,0:T(8,128)S(1)}, f32[64,128]{1,0:T(8,128)S(1)}, f32[64,128]{1,0:T(8,128)S(1)}, f32[32,128]{1,0:T(8...) custom-call(f32[256,128]{1,0:T(8,128)S(1)} %shard_map.64.both, ...), custom_call_target="tpu_custom_call" | custom-call | flops 1000 | bytes 1000 | tf_op jit(solution)/shard_map/pallas_call | solution.py:206
  23.5 0.7 %collective-permute-start.15 = (f32[2,32,128]{2,1,0:T(8,128)S(1)}, f32[2,32,128]{2,1,0:T(8,128)S(1)}, u32[]{:S(2)}, u32[]{:S(2)}) collective-permute-start(f32[2,32,128]{2,1,0:T(8,128)S(1)} %shard_map.68), channel_id=1, source_target_pairs={{0,2},{1,3},{2,0},{3,1},{4,6},{5,7},{6,4},{7,5},{8,10},{9,11},{10,... | collective-permute-start | bytes 98312 | tf_op jit(solution)/shard_map/ppermute | solution.py:18
  24.1 3.2 %collective-permute-start.12 = (f32[64,128]{1,0:T(8,128)S(1)}, f32[64,128]{1,0:T(8,128)S(1)}, u32[]{:S(2)}, u32[]{:S(2)}) collective-permute-start(f32[64,128]{1,0:T(8,128)S(1)} %get-tuple-element.19), channel_id=1, source_target_pairs={{0,24},{4,28},{8,16},{12,20},{16,8},{20,12},{24,0},{28,4},{1,25},{... | collective-permute-start | bytes 98312 | tf_op jit(solution)/shard_map/ppermute | solution.py:18
  27.3 1.2 %collective-permute-start.14 = (f32[64,128]{1,0:T(8,128)S(1)}, f32[64,128]{1,0:T(8,128)S(1)}, u32[]{:S(2)}, u32[]{:S(2)}) collective-permute-start(f32[64,128]{1,0:T(8,128)S(1)} %get-tuple-element.21), channel_id=1, source_target_pairs={{0,8},{4,12},{8,0},{12,4},{16,24},{20,28},{24,16},{28,20},{1,9},{5... | collective-permute-start | bytes 98312 | tf_op jit(solution)/shard_map/ppermute | solution.py:18
  28.5 1.5 %collective-permute-done.12.refs_1_ = f32[64,128]{1,0:T(8,128)S(1)} collective-permute-done((f32[64,128]{1,0:T(8,128)S(1)}, f32[64,128]{1,0:T(8,128)S(1)}, u32[]{:S(2)}, u32[]{:S(2)}) %collective-permute-start.12) | collective-permute-done | bytes 32800 | tf_op jit(solution)/shard_map/ppermute | solution.py:18
  30.1 2.0 %collective-permute-done.13.refs_2_ = f32[64,128]{1,0:T(8,128)S(1)} collective-permute-done((f32[64,128]{1,0:T(8,128)S(1)}, f32[64,128]{1,0:T(8,128)S(1)}, u32[]{:S(2)}, u32[]{:S(2)}) %collective-permute-start.13) | collective-permute-done | bytes 32800 | tf_op jit(solution)/shard_map/ppermute | solution.py:18
  32.1 0.7 %shard_map.70 = (f32[32,512]{1,0:T(8,128)}, f32[64,128]{1,0:T(8,128)}) custom-call(f32[64,128]{1,0:T(8,128)S(1)} %get-tuple-element.18.refs_0_, f32[64,128]{1,0:T(8,128)S(1)} %collective-permute-done.12.refs_1_, f32[64,128]{1,0:T(8,128)S(1)} %collective-permute-done.13.refs_2_, f32[64,128]{1,0:T(8,128)S(1)} %collective-permute-done.14.refs_3_, ...), custom_call_target="tpu_custom_call" | custom-call | flops 1000 | bytes 1000 | tf_op jit(solution)/shard_map/pallas_call | solution.py:271
  (32 shorter events, 0.3 us)
Async XLA Ops:
  0.6 9.2 %copy-start = (f32[1,1,128,2,1,128]{5,4,3,2,1,0:T(1,128)S(1)}, f32[1,1,128,2,1,128]{5,4,3,2,1,0:T(1,128)}, u32[]{:S(2)}) copy-start(f32[1,1,128,2,1,128]{5,4,3,2,1,0:T(1,128)} %param.4) | copy-start | bytes 393220
  2.5 7.4 %collective-permute-start = (f32[128,128]{1,0:T(8,128)}, f32[128,128]{1,0:T(8,128)S(1)}, u32[]{:S(2)}, u32[]{:S(2)}) collective-permute-start(f32[128,128]{1,0:T(8,128)} %get-tuple-element.15), channel_id=1, source_target_pairs={{0,5},{1,4},{2,7},{3,6},{4,1},{5,0},{6,3},{7,2},{8,13},{9,12},{10,... | collective-permute-start | bytes 196616 | tf_op jit(solution)/shard_map/ppermute | solution.py:328
  4.9 5.0 %copy-start.3 = (s32[1,1,2,1]{2,3,1,0:T(1,128)S(1)}, s32[1,1,2,1]{2,3,1,0:T(1,128)}, u32[]{:S(2)}) copy-start(s32[1,1,2,1]{2,3,1,0:T(1,128)} %param.5) | copy-start | bytes 28
  4.9 6.6 %collective-permute-start.1 = (f32[128,128]{1,0:T(8,128)}, f32[128,128]{1,0:T(8,128)S(1)}, u32[]{:S(2)}, u32[]{:S(2)}) collective-permute-start(f32[128,128]{1,0:T(8,128)} %get-tuple-element.16), channel_id=1, source_target_pairs={{0,5},{1,4},{2,7},{3,6},{4,1},{5,0},{6,3},{7,2},{8,13},{9,12},{10,... | collective-permute-start | bytes 196616 | tf_op jit(solution)/shard_map/ppermute | solution.py:328
  4.9 7.2 %collective-permute-start.7 = (f32[128,128]{1,0:T(8,128)}, f32[128,128]{1,0:T(8,128)S(1)}, u32[]{:S(2)}, u32[]{:S(2)}) collective-permute-start(f32[128,128]{1,0:T(8,128)} %get-tuple-element.17.refs_0_), channel_id=1, source_target_pairs={{0,16},{4,20},{8,24},{12,28},{16,0},{20,4},{24,8},{28,12},{1,17},{... | collective-permute-start | bytes 196616 | tf_op jit(solution)/shard_map/ppermute | solution.py:18
  8.3 4.8 %collective-permute-start.8 = (f32[128,128]{1,0:T(8,128)}, f32[128,128]{1,0:T(8,128)S(1)}, u32[]{:S(2)}, u32[]{:S(2)}) collective-permute-start(f32[128,128]{1,0:T(8,128)} %get-tuple-element.17.refs_0_), channel_id=1, source_target_pairs={{0,8},{4,12},{8,0},{12,4},{16,24},{20,28},{24,16},{28,20},{1,9},{5... | collective-permute-start | bytes 196616 | tf_op jit(solution)/shard_map/ppermute | solution.py:18
  9.9 4.7 %collective-permute-start.3 = (f32[128,128]{1,0:T(8,128)S(1)}, f32[128,128]{1,0:T(8,128)S(1)}, u32[]{:S(2)}, u32[]{:S(2)}) collective-permute-start(f32[128,128]{1,0:T(8,128)S(1)} %shard_map.60.refs_0_), channel_id=1, source_target_pairs={{0,2},{1,3},{2,0},{3,1},{4,6},{5,7},{6,4},{7,5},{8,10},{9,11},{10,... | collective-permute-start | bytes 196616 | tf_op jit(solution)/shard_map/ppermute | solution.py:18
  11.6 4.3 %collective-permute-start.4 = (f32[128,128]{1,0:T(8,128)S(1)}, f32[128,128]{1,0:T(8,128)S(1)}, u32[]{:S(2)}, u32[]{:S(2)}) collective-permute-start(f32[128,128]{1,0:T(8,128)S(1)} %shard_map.61.refs_1_), channel_id=1, source_target_pairs={{0,2},{1,3},{2,0},{3,1},{4,6},{5,7},{6,4},{7,5},{8,10},{9,11},{10,... | collective-permute-start | bytes 196616 | tf_op jit(solution)/shard_map/ppermute | solution.py:18
  12.1 4.3 %collective-permute-start.9 = (f32[128,128]{1,0:T(8,128)S(1)}, f32[128,128]{1,0:T(8,128)S(1)}, u32[]{:S(2)}, u32[]{:S(2)}) collective-permute-start(f32[128,128]{1,0:T(8,128)S(1)} %collective-permute-done.7.refs_1_), channel_id=1, source_target_pairs={{0,8},{4,12},{8,0},{12,4},{16,24},{20,28},{24,16},{28,20},{1,9},{5... | collective-permute-start | bytes 196616 | tf_op jit(solution)/shard_map/ppermute | solution.py:18
  13.0 3.4 %copy-start.4 = (f32[128,128]{1,0:T(8,128)S(1)}, f32[128,128]{1,0:T(8,128)}, u32[]{:S(2)}) copy-start(f32[128,128]{1,0:T(8,128)} %get-tuple-element.17.refs_0_) | copy-start | bytes 196612
  13.0 3.4 %collective-permute-start.2 = (f32[2,128,128]{2,1,0:T(8,128)S(1)}, f32[2,128,128]{2,1,0:T(8,128)S(1)}, u32[]{:S(2)}, u32[]{:S(2)}) collective-permute-start(f32[2,128,128]{2,1,0:T(8,128)S(1)} %shard_map.62.refs_0_), channel_id=1, source_target_pairs={{0,1},{1,0},{2,3},{3,2},{4,5},{5,4},{6,7},{7,6},{8,9},{9,8},{10,11... | collective-permute-start | bytes 393224 | tf_op jit(solution)/shard_map/ppermute | solution.py:18
  13.1 6.1 %collective-permute-start.11 = (f32[2,128,128]{2,1,0:T(8,128)S(1)}, f32[2,128,128]{2,1,0:T(8,128)S(1)}, u32[]{:S(2)}, u32[]{:S(2)}) collective-permute-start(f32[2,128,128]{2,1,0:T(8,128)S(1)} %shard_map.66.swapped), channel_id=1, source_target_pairs={{0,1},{1,0},{2,3},{3,2},{4,5},{5,4},{6,7},{7,6},{8,9},{9,8},{10,11... | collective-permute-start | bytes 393224 | tf_op jit(solution)/shard_map/ppermute | solution.py:18
  14.6 1.8 %collective-permute-start.5 = (f32[128,128]{1,0:T(8,128)S(1)}, f32[128,128]{1,0:T(8,128)S(1)}, u32[]{:S(2)}, u32[]{:S(2)}) collective-permute-start(f32[128,128]{1,0:T(8,128)S(1)} %collective-permute-done.3.refs_2_), channel_id=1, source_target_pairs={{0,1},{1,0},{2,3},{3,2},{4,5},{5,4},{6,7},{7,6},{8,9},{9,8},{10,11... | collective-permute-start | bytes 196616 | tf_op jit(solution)/shard_map/ppermute | solution.py:18
  15.9 1.3 %collective-permute-start.6 = (f32[128,128]{1,0:T(8,128)S(1)}, f32[128,128]{1,0:T(8,128)S(1)}, u32[]{:S(2)}, u32[]{:S(2)}) collective-permute-start(f32[128,128]{1,0:T(8,128)S(1)} %collective-permute-done.4.refs_3_), channel_id=1, source_target_pairs={{0,1},{1,0},{2,3},{3,2},{4,5},{5,4},{6,7},{7,6},{8,9},{9,8},{10,11... | collective-permute-start | bytes 196616 | tf_op jit(solution)/shard_map/ppermute | solution.py:18
  16.4 2.7 %copy-start.1 = (f32[1,1,128,512]{3,2,1,0:T(8,128)S(1)}, f32[1,1,128,512]{3,2,1,0:T(8,128)}, u32[]{:S(2)}) copy-start(f32[1,1,128,512]{3,2,1,0:T(8,128)} %param.6) | copy-start | bytes 786436
  17.5 5.6 %copy-start.2 = (f32[64,128]{1,0:T(8,128)S(1)}, f32[64,128]{1,0:T(8,128)}, u32[]{:S(2)}) copy-start(f32[64,128]{1,0:T(8,128)} %dinv.1) | copy-start | bytes 98308
  17.5 5.6 %collective-permute-start.10 = (f32[256,128]{1,0:T(8,128)S(1)}, f32[256,128]{1,0:T(8,128)S(1)}, u32[]{:S(2)}, u32[]{:S(2)}) collective-permute-start(f32[256,128]{1,0:T(8,128)S(1)} %shard_map.64.both), channel_id=1, source_target_pairs={{0,4},{4,0},{8,12},{12,8},{16,20},{20,16},{24,28},{28,24},{1,5},{5... | collective-permute-start | bytes 393224 | tf_op jit(solution)/shard_map/ppermute | solution.py:18
  23.5 5.1 %collective-permute-start.15 = (f32[2,32,128]{2,1,0:T(8,128)S(1)}, f32[2,32,128]{2,1,0:T(8,128)S(1)}, u32[]{:S(2)}, u32[]{:S(2)}) collective-permute-start(f32[2,32,128]{2,1,0:T(8,128)S(1)} %shard_map.68), channel_id=1, source_target_pairs={{0,2},{1,3},{2,0},{3,1},{4,6},{5,7},{6,4},{7,5},{8,10},{9,11},{10,... | collective-permute-start | bytes 98312 | tf_op jit(solution)/shard_map/ppermute | solution.py:18
  24.1 5.9 %collective-permute-start.12 = (f32[64,128]{1,0:T(8,128)S(1)}, f32[64,128]{1,0:T(8,128)S(1)}, u32[]{:S(2)}, u32[]{:S(2)}) collective-permute-start(f32[64,128]{1,0:T(8,128)S(1)} %get-tuple-element.19), channel_id=1, source_target_pairs={{0,24},{4,28},{8,16},{12,20},{16,8},{20,12},{24,0},{28,4},{1,25},{... | collective-permute-start | bytes 98312 | tf_op jit(solution)/shard_map/ppermute | solution.py:18
  27.3 4.8 %collective-permute-start.13 = (f32[64,128]{1,0:T(8,128)S(1)}, f32[64,128]{1,0:T(8,128)S(1)}, u32[]{:S(2)}, u32[]{:S(2)}) collective-permute-start(f32[64,128]{1,0:T(8,128)S(1)} %get-tuple-element.20), channel_id=1, source_target_pairs={{0,16},{4,20},{8,24},{12,28},{16,0},{20,4},{24,8},{28,12},{1,17},{... | collective-permute-start | bytes 98312 | tf_op jit(solution)/shard_map/ppermute | solution.py:18
  27.3 4.8 %collective-permute-start.14 = (f32[64,128]{1,0:T(8,128)S(1)}, f32[64,128]{1,0:T(8,128)S(1)}, u32[]{:S(2)}, u32[]{:S(2)}) collective-permute-start(f32[64,128]{1,0:T(8,128)S(1)} %get-tuple-element.21), channel_id=1, source_target_pairs={{0,8},{4,12},{8,0},{12,4},{16,24},{20,28},{24,16},{28,20},{1,9},{5... | collective-permute-start | bytes 98312 | tf_op jit(solution)/shard_map/ppermute | solution.py:18
  28.5 3.6 %collective-permute-start.16 = (f32[2,32,128]{2,1,0:T(8,128)S(1)}, f32[2,32,128]{2,1,0:T(8,128)S(1)}, u32[]{:S(2)}, u32[]{:S(2)}) collective-permute-start(f32[2,32,128]{2,1,0:T(8,128)S(1)} %shard_map.69), channel_id=1, source_target_pairs={{0,1},{1,0},{2,3},{3,2},{4,5},{5,4},{6,7},{7,6},{8,9},{9,8},{10,11... | collective-permute-start | bytes 98312 | tf_op jit(solution)/shard_map/ppermute | solution.py:18

commit v31 on v30

--- a/solution.py
+++ b/solution.py
@@ -364,7 +364,7 @@
 
     both = partials(held, mate, ours, theirs, columns)
     got = flipped(both, "row", 1)
-    flips = (0, *range(groups_row - 2, 0, -2))
+    flips = (0, *range(4, groups_row, 2), 2)
     along, outward = finish(
         both, got, stay, swapped, mate_swapped, dinv, order, flips, groups_col
     )

time: 32.9 us -> 32.9 us (level)
  waiting for transfers between devices: 10.9 us -> 11.6 us
  starting transfers between devices: 17.5 us -> 16.9 us
    ppermute x15, waiting for transfers between devices: 10.9 us -> 11.5 us  [flipped(): lax.ppermute(value, axis, [(i, i ^ flip) for i in range(lax.axis_size(axi...]
    ppermute x15, starting transfers between devices: 15.1 us -> 14.5 us  [flipped(): lax.ppermute(value, axis, [(i, i ^ flip) for i in range(lax.axis_size(axi...]
where the time goes in v31:
time: 32.9 us; the launch traced here: 32.8 us
  starting transfers between devices  16.9 us (51%)
  waiting for transfers between devices  11.6 us (35%)
  Pallas kernels  3.55 us (11%)
  between operations  0.77 us (2%)
    ppermute x15, starting transfers between devices, flipped(): lax.ppermute(value, axis, [(i, i ^ flip) for i in range(lax.axis_size(axi...  14.5 us
    ppermute x15, waiting for transfers between devices, flipped(): lax.ppermute(value, axis, [(i, i ^ flip) for i in range(lax.axis_size(axi...  11.5 us
    ppermute x2, starting transfers between devices, crossed(): return lax.ppermute(swap, ('row', 'col'), cross)  2.42 us
    pallas_call x1, Pallas kernels, prepare(): pl.pallas_call(functools.partial(prepare_kernel, tall), out_shape=(jax.Sh...  1.84 us
  transfers between devices with their start and end apart: 17, of which 7 were waited for; matrix products, arithmetic and copies ran while one was open for 0% of the time, Pallas kernels for 2%

profile of v31, /device:TPU:0, one launch (start us, length us, event | category | flops | bytes accessed | tf_op | source)
XLA Modules:
  0.0 32.8 jit_solution(17859013594325015381)
XLA Ops:
  0.6 1.8 %shard_map.59 = (f32[128,128]{1,0:T(8,128)}, f32[128,128]{1,0:T(8,128)}, f32[128,128]{1,0:T(8,128)}) custom-call(s32[1,2]{1,0:T(1,128)} %bitcast.9, f32[256,128]{1,0:T(8,128)} %bitcast.4, f32[128,512]{1,0:T(8,128)} %bitcast.7), custom_call_target="tpu_custom_call" | custom-call | flops 1000 | bytes 1000 | tf_op jit(solution)/shard_map/pallas_call | solution.py:89
  2.5 2.4 %collective-permute-start = (f32[128,128]{1,0:T(8,128)}, f32[128,128]{1,0:T(8,128)S(1)}, u32[]{:S(2)}, u32[]{:S(2)}) collective-permute-start(f32[128,128]{1,0:T(8,128)} %get-tuple-element.15), channel_id=1, source_target_pairs={{0,5},{1,4},{2,7},{3,6},{4,1},{5,0},{6,3},{7,2},{8,13},{9,12},{10,... | collective-permute-start | bytes 196616 | tf_op jit(solution)/shard_map/ppermute | solution.py:328
  4.9 3.4 %collective-permute-start.7 = (f32[128,128]{1,0:T(8,128)}, f32[128,128]{1,0:T(8,128)S(1)}, u32[]{:S(2)}, u32[]{:S(2)}) collective-permute-start(f32[128,128]{1,0:T(8,128)} %get-tuple-element.17.refs_0_), channel_id=1, source_target_pairs={{0,16},{4,20},{8,24},{12,28},{16,0},{20,4},{24,8},{28,12},{1,17},{... | collective-permute-start | bytes 196616 | tf_op jit(solution)/shard_map/ppermute | solution.py:18
  8.3 1.6 %collective-permute-start.8 = (f32[128,128]{1,0:T(8,128)}, f32[128,128]{1,0:T(8,128)S(1)}, u32[]{:S(2)}, u32[]{:S(2)}) collective-permute-start(f32[128,128]{1,0:T(8,128)} %get-tuple-element.17.refs_0_), channel_id=1, source_target_pairs={{0,8},{4,12},{8,0},{12,4},{16,24},{20,28},{24,16},{28,20},{1,9},{5... | collective-permute-start | bytes 196616 | tf_op jit(solution)/shard_map/ppermute | solution.py:18
  9.9 1.5 %collective-permute-start.3 = (f32[128,128]{1,0:T(8,128)S(1)}, f32[128,128]{1,0:T(8,128)S(1)}, u32[]{:S(2)}, u32[]{:S(2)}) collective-permute-start(f32[128,128]{1,0:T(8,128)S(1)} %shard_map.60.refs_0_), channel_id=1, source_target_pairs={{0,2},{1,3},{2,0},{3,1},{4,6},{5,7},{6,4},{7,5},{8,10},{9,11},{10,... | collective-permute-start | bytes 196616 | tf_op jit(solution)/shard_map/ppermute | solution.py:18
  11.6 0.5 %collective-permute-start.4 = (f32[128,128]{1,0:T(8,128)S(1)}, f32[128,128]{1,0:T(8,128)S(1)}, u32[]{:S(2)}, u32[]{:S(2)}) collective-permute-start(f32[128,128]{1,0:T(8,128)S(1)} %shard_map.61.refs_1_), channel_id=1, source_target_pairs={{0,2},{1,3},{2,0},{3,1},{4,6},{5,7},{6,4},{7,5},{8,10},{9,11},{10,... | collective-permute-start | bytes 196616 | tf_op jit(solution)/shard_map/ppermute | solution.py:18
  12.1 0.9 %collective-permute-start.9 = (f32[128,128]{1,0:T(8,128)S(1)}, f32[128,128]{1,0:T(8,128)S(1)}, u32[]{:S(2)}, u32[]{:S(2)}) collective-permute-start(f32[128,128]{1,0:T(8,128)S(1)} %collective-permute-done.7.refs_1_), channel_id=1, source_target_pairs={{0,8},{4,12},{8,0},{12,4},{16,24},{20,28},{24,16},{28,20},{1,9},{5... | collective-permute-start | bytes 196616 | tf_op jit(solution)/shard_map/ppermute | solution.py:18
  13.1 0.6 %collective-permute-start.11 = (f32[2,128,128]{2,1,0:T(8,128)S(1)}, f32[2,128,128]{2,1,0:T(8,128)S(1)}, u32[]{:S(2)}, u32[]{:S(2)}) collective-permute-start(f32[2,128,128]{2,1,0:T(8,128)S(1)} %shard_map.66.swapped), channel_id=1, source_target_pairs={{0,1},{1,0},{2,3},{3,2},{4,5},{5,4},{6,7},{7,6},{8,9},{9,8},{10,11... | collective-permute-start | bytes 393224 | tf_op jit(solution)/shard_map/ppermute | solution.py:18
  13.7 1.0 %collective-permute-done.3.refs_2_ = f32[128,128]{1,0:T(8,128)S(1)} collective-permute-done((f32[128,128]{1,0:T(8,128)S(1)}, f32[128,128]{1,0:T(8,128)S(1)}, u32[]{:S(2)}, u32[]{:S(2)}) %collective-permute-start.3) | collective-permute-done | bytes 65568 | tf_op jit(solution)/shard_map/ppermute | solution.py:18
  14.7 1.2 %collective-permute-done.4.refs_3_ = f32[128,128]{1,0:T(8,128)S(1)} collective-permute-done((f32[128,128]{1,0:T(8,128)S(1)}, f32[128,128]{1,0:T(8,128)S(1)}, u32[]{:S(2)}, u32[]{:S(2)}) %collective-permute-start.4) | collective-permute-done | bytes 65568 | tf_op jit(solution)/shard_map/ppermute | solution.py:18
  15.9 0.5 %collective-permute-done.9.refs_3_ = f32[128,128]{1,0:T(8,128)S(1)} collective-permute-done((f32[128,128]{1,0:T(8,128)S(1)}, f32[128,128]{1,0:T(8,128)S(1)}, u32[]{:S(2)}, u32[]{:S(2)}) %collective-permute-start.9) | collective-permute-done | bytes 65568 | tf_op jit(solution)/shard_map/ppermute | solution.py:18
  16.4 0.7 %collective-permute-done.6.refs_5_ = f32[128,128]{1,0:T(8,128)S(1)} collective-permute-done((f32[128,128]{1,0:T(8,128)S(1)}, f32[128,128]{1,0:T(8,128)S(1)}, u32[]{:S(2)}, u32[]{:S(2)}) %collective-permute-start.6) | collective-permute-done | bytes 65568 | tf_op jit(solution)/shard_map/ppermute | solution.py:18
  17.1 0.4 %shard_map.64.both = f32[256,128]{1,0:T(8,128)S(1)} custom-call(f32[2,128,128]{2,1,0:T(8,128)S(1)} %shard_map.62.refs_0_, f32[2,128,128]{2,1,0:T(8,128)S(1)} %collective-permute-done.2.refs_1_, f32[128,128]{1,0:T(8,128)S(1)} %collective-permute-done.3.refs_2_, f32[128,128]{1,0:T(8,128)S(1)} %collective-permute-done.4.refs_3_, ...), custom_call_target="tpu_custom_call" | custom-call | flops 1000 | bytes 1000 | tf_op jit(solution)/shard_map/pallas_call | solution.py:147
  17.5 1.6 %collective-permute-start.10 = (f32[256,128]{1,0:T(8,128)S(1)}, f32[256,128]{1,0:T(8,128)S(1)}, u32[]{:S(2)}, u32[]{:S(2)}) collective-permute-start(f32[256,128]{1,0:T(8,128)S(1)} %shard_map.64.both), channel_id=1, source_target_pairs={{0,4},{4,0},{8,12},{12,8},{16,20},{20,16},{24,28},{28,24},{1,5},{5... | collective-permute-start | bytes 393224 | tf_op jit(solution)/shard_map/ppermute | solution.py:18
  19.1 0.1 shard_map.65.stay
  19.2 3.9 %collective-permute-done.10.got = f32[256,128]{1,0:T(8,128)S(1)} collective-permute-done((f32[256,128]{1,0:T(8,128)S(1)}, f32[256,128]{1,0:T(8,128)S(1)}, u32[]{:S(2)}, u32[]{:S(2)}) %collective-permute-start.10) | collective-permute-done | bytes 131104 | tf_op jit(solution)/shard_map/ppermute | solution.py:18
  23.1 0.3 %shard_map.67 = (f32[64,128]{1,0:T(8,128)S(1)}, f32[64,128]{1,0:T(8,128)S(1)}, f32[64,128]{1,0:T(8,128)S(1)}, f32[64,128]{1,0:T(8,128)S(1)}, f32[32,128]{1,0:T(8...) custom-call(f32[256,128]{1,0:T(8,128)S(1)} %shard_map.64.both, ...), custom_call_target="tpu_custom_call" | custom-call | flops 1000 | bytes 1000 | tf_op jit(solution)/shard_map/pallas_call | solution.py:206
  23.5 0.7 %collective-permute-start.15 = (f32[2,32,128]{2,1,0:T(8,128)S(1)}, f32[2,32,128]{2,1,0:T(8,128)S(1)}, u32[]{:S(2)}, u32[]{:S(2)}) collective-permute-start(f32[2,32,128]{2,1,0:T(8,128)S(1)} %shard_map.68), channel_id=1, source_target_pairs={{0,2},{1,3},{2,0},{3,1},{4,6},{5,7},{6,4},{7,5},{8,10},{9,11},{10,... | collective-permute-start | bytes 98312 | tf_op jit(solution)/shard_map/ppermute | solution.py:18
  24.1 2.3 %collective-permute-start.12 = (f32[64,128]{1,0:T(8,128)S(1)}, f32[64,128]{1,0:T(8,128)S(1)}, u32[]{:S(2)}, u32[]{:S(2)}) collective-permute-start(f32[64,128]{1,0:T(8,128)S(1)} %get-tuple-element.19), channel_id=1, source_target_pairs={{0,16},{4,20},{8,24},{12,28},{16,0},{20,4},{24,8},{28,12},{1,17},{... | collective-permute-start | bytes 98312 | tf_op jit(solution)/shard_map/ppermute | solution.py:18
  26.4 1.2 %collective-permute-start.13 = (f32[64,128]{1,0:T(8,128)S(1)}, f32[64,128]{1,0:T(8,128)S(1)}, u32[]{:S(2)}, u32[]{:S(2)}) collective-permute-start(f32[64,128]{1,0:T(8,128)S(1)} %get-tuple-element.20), channel_id=1, source_target_pairs={{0,24},{4,28},{8,16},{12,20},{16,8},{20,12},{24,0},{28,4},{1,25},{... | collective-permute-start | bytes 98312 | tf_op jit(solution)/shard_map/ppermute | solution.py:18
  27.7 0.2 collective-permute-start.14
  27.9 1.1 %collective-permute-done.12.refs_1_ = f32[64,128]{1,0:T(8,128)S(1)} collective-permute-done((f32[64,128]{1,0:T(8,128)S(1)}, f32[64,128]{1,0:T(8,128)S(1)}, u32[]{:S(2)}, u32[]{:S(2)}) %collective-permute-start.12) | collective-permute-done | bytes 32800 | tf_op jit(solution)/shard_map/ppermute | solution.py:18
  29.0 3.1 %collective-permute-done.13.refs_2_ = f32[64,128]{1,0:T(8,128)S(1)} collective-permute-done((f32[64,128]{1,0:T(8,128)S(1)}, f32[64,128]{1,0:T(8,128)S(1)}, u32[]{:S(2)}, u32[]{:S(2)}) %collective-permute-start.13) | collective-permute-done | bytes 32800 | tf_op jit(solution)/shard_map/ppermute | solution.py:18
  32.1 0.7 %shard_map.70 = (f32[32,512]{1,0:T(8,128)}, f32[64,128]{1,0:T(8,128)}) custom-call(f32[64,128]{1,0:T(8,128)S(1)} %get-tuple-element.18.refs_0_, f32[64,128]{1,0:T(8,128)S(1)} %collective-permute-done.12.refs_1_, f32[64,128]{1,0:T(8,128)S(1)} %collective-permute-done.13.refs_2_, f32[64,128]{1,0:T(8,128)S(1)} %collective-permute-done.14.refs_3_, ...), custom_call_target="tpu_custom_call" | custom-call | flops 1000 | bytes 1000 | tf_op jit(solution)/shard_map/pallas_call | solution.py:271
  (32 shorter events, 0.4 us)
Async XLA Ops:
  0.6 9.2 %copy-start = (f32[1,1,128,2,1,128]{5,4,3,2,1,0:T(1,128)S(1)}, f32[1,1,128,2,1,128]{5,4,3,2,1,0:T(1,128)}, u32[]{:S(2)}) copy-start(f32[1,1,128,2,1,128]{5,4,3,2,1,0:T(1,128)} %param.4) | copy-start | bytes 393220
  2.5 7.4 %collective-permute-start = (f32[128,128]{1,0:T(8,128)}, f32[128,128]{1,0:T(8,128)S(1)}, u32[]{:S(2)}, u32[]{:S(2)}) collective-permute-start(f32[128,128]{1,0:T(8,128)} %get-tuple-element.15), channel_id=1, source_target_pairs={{0,5},{1,4},{2,7},{3,6},{4,1},{5,0},{6,3},{7,2},{8,13},{9,12},{10,... | collective-permute-start | bytes 196616 | tf_op jit(solution)/shard_map/ppermute | solution.py:328
  4.9 5.0 %copy-start.3 = (s32[1,1,2,1]{2,3,1,0:T(1,128)S(1)}, s32[1,1,2,1]{2,3,1,0:T(1,128)}, u32[]{:S(2)}) copy-start(s32[1,1,2,1]{2,3,1,0:T(1,128)} %param.5) | copy-start | bytes 28
  4.9 6.6 %collective-permute-start.1 = (f32[128,128]{1,0:T(8,128)}, f32[128,128]{1,0:T(8,128)S(1)}, u32[]{:S(2)}, u32[]{:S(2)}) collective-permute-start(f32[128,128]{1,0:T(8,128)} %get-tuple-element.16), channel_id=1, source_target_pairs={{0,5},{1,4},{2,7},{3,6},{4,1},{5,0},{6,3},{7,2},{8,13},{9,12},{10,... | collective-permute-start | bytes 196616 | tf_op jit(solution)/shard_map/ppermute | solution.py:328
  4.9 7.2 %collective-permute-start.7 = (f32[128,128]{1,0:T(8,128)}, f32[128,128]{1,0:T(8,128)S(1)}, u32[]{:S(2)}, u32[]{:S(2)}) collective-permute-start(f32[128,128]{1,0:T(8,128)} %get-tuple-element.17.refs_0_), channel_id=1, source_target_pairs={{0,16},{4,20},{8,24},{12,28},{16,0},{20,4},{24,8},{28,12},{1,17},{... | collective-permute-start | bytes 196616 | tf_op jit(solution)/shard_map/ppermute | solution.py:18
  8.3 4.8 %collective-permute-start.8 = (f32[128,128]{1,0:T(8,128)}, f32[128,128]{1,0:T(8,128)S(1)}, u32[]{:S(2)}, u32[]{:S(2)}) collective-permute-start(f32[128,128]{1,0:T(8,128)} %get-tuple-element.17.refs_0_), channel_id=1, source_target_pairs={{0,8},{4,12},{8,0},{12,4},{16,24},{20,28},{24,16},{28,20},{1,9},{5... | collective-permute-start | bytes 196616 | tf_op jit(solution)/shard_map/ppermute | solution.py:18
  9.9 4.7 %collective-permute-start.3 = (f32[128,128]{1,0:T(8,128)S(1)}, f32[128,128]{1,0:T(8,128)S(1)}, u32[]{:S(2)}, u32[]{:S(2)}) collective-permute-start(f32[128,128]{1,0:T(8,128)S(1)} %shard_map.60.refs_0_), channel_id=1, source_target_pairs={{0,2},{1,3},{2,0},{3,1},{4,6},{5,7},{6,4},{7,5},{8,10},{9,11},{10,... | collective-permute-start | bytes 196616 | tf_op jit(solution)/shard_map/ppermute | solution.py:18
  11.6 4.3 %collective-permute-start.4 = (f32[128,128]{1,0:T(8,128)S(1)}, f32[128,128]{1,0:T(8,128)S(1)}, u32[]{:S(2)}, u32[]{:S(2)}) collective-permute-start(f32[128,128]{1,0:T(8,128)S(1)} %shard_map.61.refs_1_), channel_id=1, source_target_pairs={{0,2},{1,3},{2,0},{3,1},{4,6},{5,7},{6,4},{7,5},{8,10},{9,11},{10,... | collective-permute-start | bytes 196616 | tf_op jit(solution)/shard_map/ppermute | solution.py:18
  12.1 4.3 %collective-permute-start.9 = (f32[128,128]{1,0:T(8,128)S(1)}, f32[128,128]{1,0:T(8,128)S(1)}, u32[]{:S(2)}, u32[]{:S(2)}) collective-permute-start(f32[128,128]{1,0:T(8,128)S(1)} %collective-permute-done.7.refs_1_), channel_id=1, source_target_pairs={{0,8},{4,12},{8,0},{12,4},{16,24},{20,28},{24,16},{28,20},{1,9},{5... | collective-permute-start | bytes 196616 | tf_op jit(solution)/shard_map/ppermute | solution.py:18
  13.0 3.4 %copy-start.4 = (f32[128,128]{1,0:T(8,128)S(1)}, f32[128,128]{1,0:T(8,128)}, u32[]{:S(2)}) copy-start(f32[128,128]{1,0:T(8,128)} %get-tuple-element.17.refs_0_) | copy-start | bytes 196612
  13.0 3.4 %collective-permute-start.2 = (f32[2,128,128]{2,1,0:T(8,128)S(1)}, f32[2,128,128]{2,1,0:T(8,128)S(1)}, u32[]{:S(2)}, u32[]{:S(2)}) collective-permute-start(f32[2,128,128]{2,1,0:T(8,128)S(1)} %shard_map.62.refs_0_), channel_id=1, source_target_pairs={{0,1},{1,0},{2,3},{3,2},{4,5},{5,4},{6,7},{7,6},{8,9},{9,8},{10,11... | collective-permute-start | bytes 393224 | tf_op jit(solution)/shard_map/ppermute | solution.py:18
  13.1 6.1 %collective-permute-start.11 = (f32[2,128,128]{2,1,0:T(8,128)S(1)}, f32[2,128,128]{2,1,0:T(8,128)S(1)}, u32[]{:S(2)}, u32[]{:S(2)}) collective-permute-start(f32[2,128,128]{2,1,0:T(8,128)S(1)} %shard_map.66.swapped), channel_id=1, source_target_pairs={{0,1},{1,0},{2,3},{3,2},{4,5},{5,4},{6,7},{7,6},{8,9},{9,8},{10,11... | collective-permute-start | bytes 393224 | tf_op jit(solution)/shard_map/ppermute | solution.py:18
  14.6 1.8 %collective-permute-start.5 = (f32[128,128]{1,0:T(8,128)S(1)}, f32[128,128]{1,0:T(8,128)S(1)}, u32[]{:S(2)}, u32[]{:S(2)}) collective-permute-start(f32[128,128]{1,0:T(8,128)S(1)} %collective-permute-done.3.refs_2_), channel_id=1, source_target_pairs={{0,1},{1,0},{2,3},{3,2},{4,5},{5,4},{6,7},{7,6},{8,9},{9,8},{10,11... | collective-permute-start | bytes 196616 | tf_op jit(solution)/shard_map/ppermute | solution.py:18
  15.9 1.3 %collective-permute-start.6 = (f32[128,128]{1,0:T(8,128)S(1)}, f32[128,128]{1,0:T(8,128)S(1)}, u32[]{:S(2)}, u32[]{:S(2)}) collective-permute-start(f32[128,128]{1,0:T(8,128)S(1)} %collective-permute-done.4.refs_3_), channel_id=1, source_target_pairs={{0,1},{1,0},{2,3},{3,2},{4,5},{5,4},{6,7},{7,6},{8,9},{9,8},{10,11... | collective-permute-start | bytes 196616 | tf_op jit(solution)/shard_map/ppermute | solution.py:18
  16.4 2.7 %copy-start.1 = (f32[1,1,128,512]{3,2,1,0:T(8,128)S(1)}, f32[1,1,128,512]{3,2,1,0:T(8,128)}, u32[]{:S(2)}) copy-start(f32[1,1,128,512]{3,2,1,0:T(8,128)} %param.6) | copy-start | bytes 786436
  17.5 5.6 %copy-start.2 = (f32[64,128]{1,0:T(8,128)S(1)}, f32[64,128]{1,0:T(8,128)}, u32[]{:S(2)}) copy-start(f32[64,128]{1,0:T(8,128)} %dinv.1) | copy-start | bytes 98308
  17.5 5.6 %collective-permute-start.10 = (f32[256,128]{1,0:T(8,128)S(1)}, f32[256,128]{1,0:T(8,128)S(1)}, u32[]{:S(2)}, u32[]{:S(2)}) collective-permute-start(f32[256,128]{1,0:T(8,128)S(1)} %shard_map.64.both), channel_id=1, source_target_pairs={{0,4},{4,0},{8,12},{12,8},{16,20},{20,16},{24,28},{28,24},{1,5},{5... | collective-permute-start | bytes 393224 | tf_op jit(solution)/shard_map/ppermute | solution.py:18
  23.5 4.4 %collective-permute-start.15 = (f32[2,32,128]{2,1,0:T(8,128)S(1)}, f32[2,32,128]{2,1,0:T(8,128)S(1)}, u32[]{:S(2)}, u32[]{:S(2)}) collective-permute-start(f32[2,32,128]{2,1,0:T(8,128)S(1)} %shard_map.68), channel_id=1, source_target_pairs={{0,2},{1,3},{2,0},{3,1},{4,6},{5,7},{6,4},{7,5},{8,10},{9,11},{10,... | collective-permute-start | bytes 98312 | tf_op jit(solution)/shard_map/ppermute | solution.py:18
  24.1 4.8 %collective-permute-start.12 = (f32[64,128]{1,0:T(8,128)S(1)}, f32[64,128]{1,0:T(8,128)S(1)}, u32[]{:S(2)}, u32[]{:S(2)}) collective-permute-start(f32[64,128]{1,0:T(8,128)S(1)} %get-tuple-element.19), channel_id=1, source_target_pairs={{0,16},{4,20},{8,24},{12,28},{16,0},{20,4},{24,8},{28,12},{1,17},{... | collective-permute-start | bytes 98312 | tf_op jit(solution)/shard_map/ppermute | solution.py:18
  26.4 5.7 %collective-permute-start.13 = (f32[64,128]{1,0:T(8,128)S(1)}, f32[64,128]{1,0:T(8,128)S(1)}, u32[]{:S(2)}, u32[]{:S(2)}) collective-permute-start(f32[64,128]{1,0:T(8,128)S(1)} %get-tuple-element.20), channel_id=1, source_target_pairs={{0,24},{4,28},{8,16},{12,20},{16,8},{20,12},{24,0},{28,4},{1,25},{... | collective-permute-start | bytes 98312 | tf_op jit(solution)/shard_map/ppermute | solution.py:18
  27.7 4.5 %collective-permute-start.14 = (f32[64,128]{1,0:T(8,128)S(1)}, f32[64,128]{1,0:T(8,128)S(1)}, u32[]{:S(2)}, u32[]{:S(2)}) collective-permute-start(f32[64,128]{1,0:T(8,128)S(1)} %get-tuple-element.21), channel_id=1, source_target_pairs={{0,8},{4,12},{8,0},{12,4},{16,24},{20,28},{24,16},{28,20},{1,9},{5... | collective-permute-start | bytes 98312 | tf_op jit(solution)/shard_map/ppermute | solution.py:18
  27.9 4.3 %collective-permute-start.16 = (f32[2,32,128]{2,1,0:T(8,128)S(1)}, f32[2,32,128]{2,1,0:T(8,128)S(1)}, u32[]{:S(2)}, u32[]{:S(2)}) collective-permute-start(f32[2,32,128]{2,1,0:T(8,128)S(1)} %shard_map.69), channel_id=1, source_target_pairs={{0,1},{1,0},{2,3},{3,2},{4,5},{5,4},{6,7},{7,6},{8,9},{9,8},{10,11... | collective-permute-start | bytes 98312 | tf_op jit(solution)/shard_map/ppermute | solution.py:18

commit v32 on v31

--- a/solution.py
+++ b/solution.py
@@ -364,7 +364,7 @@
 
     both = partials(held, mate, ours, theirs, columns)
     got = flipped(both, "row", 1)
-    flips = (0, *range(4, groups_row, 2), 2)
+    flips = (0, 2, *range(groups_row - 2, 2, -2))
     along, outward = finish(
         both, got, stay, swapped, mate_swapped, dinv, order, flips, groups_col
     )

time: 32.9 us -> 33.8 us (1.027)
  waiting for transfers between devices: 11.6 us -> 12.4 us
    ppermute x15, waiting for transfers between devices: 11.5 us -> 12.4 us  [flipped(): lax.ppermute(value, axis, [(i, i ^ flip) for i in range(lax.axis_size(axi...]
  transfers between devices with their start and end apart: 17 -> 17, of which waited for: 7 -> 8; matrix products, arithmetic and copies ran while one was open for 0% -> 0% of each run, Pallas kernels for 2% -> 2%
where the time goes in v32:
time: 33.8 us; the launch traced here: 33.7 us
  starting transfers between devices  17 us (50%)
  waiting for transfers between devices  12.4 us (37%)
  Pallas kernels  3.55 us (11%)
  between operations  0.78 us (2%)
    ppermute x15, starting transfers between devices, flipped(): lax.ppermute(value, axis, [(i, i ^ flip) for i in range(lax.axis_size(axi...  14.5 us
    ppermute x15, waiting for transfers between devices, flipped(): lax.ppermute(value, axis, [(i, i ^ flip) for i in range(lax.axis_size(axi...  12.4 us
    ppermute x2, starting transfers between devices, crossed(): return lax.ppermute(swap, ('row', 'col'), cross)  2.42 us
    pallas_call x1, Pallas kernels, prepare(): pl.pallas_call(functools.partial(prepare_kernel, tall), out_shape=(jax.Sh...  1.84 us
  transfers between devices with their start and end apart: 17, of which 8 were waited for; matrix products, arithmetic and copies ran while one was open for 0% of the time, Pallas kernels for 2%

profile of v32, /device:TPU:0, one launch (start us, length us, event | category | flops | bytes accessed | tf_op | source)
XLA Modules:
  0.0 33.7 jit_solution(579896229010221182)
XLA Ops:
  0.6 1.8 %shard_map.59 = (f32[128,128]{1,0:T(8,128)}, f32[128,128]{1,0:T(8,128)}, f32[128,128]{1,0:T(8,128)}) custom-call(s32[1,2]{1,0:T(1,128)} %bitcast.9, f32[256,128]{1,0:T(8,128)} %bitcast.4, f32[128,512]{1,0:T(8,128)} %bitcast.7), custom_call_target="tpu_custom_call" | custom-call | flops 1000 | bytes 1000 | tf_op jit(solution)/shard_map/pallas_call | solution.py:89
  2.5 2.4 %collective-permute-start = (f32[128,128]{1,0:T(8,128)}, f32[128,128]{1,0:T(8,128)S(1)}, u32[]{:S(2)}, u32[]{:S(2)}) collective-permute-start(f32[128,128]{1,0:T(8,128)} %get-tuple-element.15), channel_id=1, source_target_pairs={{0,5},{1,4},{2,7},{3,6},{4,1},{5,0},{6,3},{7,2},{8,13},{9,12},{10,... | collective-permute-start | bytes 196616 | tf_op jit(solution)/shard_map/ppermute | solution.py:328
  4.9 3.4 %collective-permute-start.7 = (f32[128,128]{1,0:T(8,128)}, f32[128,128]{1,0:T(8,128)S(1)}, u32[]{:S(2)}, u32[]{:S(2)}) collective-permute-start(f32[128,128]{1,0:T(8,128)} %get-tuple-element.17.refs_0_), channel_id=1, source_target_pairs={{0,16},{4,20},{8,24},{12,28},{16,0},{20,4},{24,8},{28,12},{1,17},{... | collective-permute-start | bytes 196616 | tf_op jit(solution)/shard_map/ppermute | solution.py:18
  8.3 1.6 %collective-permute-start.8 = (f32[128,128]{1,0:T(8,128)}, f32[128,128]{1,0:T(8,128)S(1)}, u32[]{:S(2)}, u32[]{:S(2)}) collective-permute-start(f32[128,128]{1,0:T(8,128)} %get-tuple-element.17.refs_0_), channel_id=1, source_target_pairs={{0,8},{4,12},{8,0},{12,4},{16,24},{20,28},{24,16},{28,20},{1,9},{5... | collective-permute-start | bytes 196616 | tf_op jit(solution)/shard_map/ppermute | solution.py:18
  9.9 1.5 %collective-permute-start.3 = (f32[128,128]{1,0:T(8,128)S(1)}, f32[128,128]{1,0:T(8,128)S(1)}, u32[]{:S(2)}, u32[]{:S(2)}) collective-permute-start(f32[128,128]{1,0:T(8,128)S(1)} %shard_map.60.refs_0_), channel_id=1, source_target_pairs={{0,2},{1,3},{2,0},{3,1},{4,6},{5,7},{6,4},{7,5},{8,10},{9,11},{10,... | collective-permute-start | bytes 196616 | tf_op jit(solution)/shard_map/ppermute | solution.py:18
  11.6 0.5 %collective-permute-start.4 = (f32[128,128]{1,0:T(8,128)S(1)}, f32[128,128]{1,0:T(8,128)S(1)}, u32[]{:S(2)}, u32[]{:S(2)}) collective-permute-start(f32[128,128]{1,0:T(8,128)S(1)} %shard_map.61.refs_1_), channel_id=1, source_target_pairs={{0,2},{1,3},{2,0},{3,1},{4,6},{5,7},{6,4},{7,5},{8,10},{9,11},{10,... | collective-permute-start | bytes 196616 | tf_op jit(solution)/shard_map/ppermute | solution.py:18
  12.1 0.9 %collective-permute-start.9 = (f32[128,128]{1,0:T(8,128)S(1)}, f32[128,128]{1,0:T(8,128)S(1)}, u32[]{:S(2)}, u32[]{:S(2)}) collective-permute-start(f32[128,128]{1,0:T(8,128)S(1)} %collective-permute-done.7.refs_1_), channel_id=1, source_target_pairs={{0,8},{4,12},{8,0},{12,4},{16,24},{20,28},{24,16},{28,20},{1,9},{5... | collective-permute-start | bytes 196616 | tf_op jit(solution)/shard_map/ppermute | solution.py:18
  13.1 0.6 %collective-permute-start.11 = (f32[2,128,128]{2,1,0:T(8,128)S(1)}, f32[2,128,128]{2,1,0:T(8,128)S(1)}, u32[]{:S(2)}, u32[]{:S(2)}) collective-permute-start(f32[2,128,128]{2,1,0:T(8,128)S(1)} %shard_map.66.swapped), channel_id=1, source_target_pairs={{0,1},{1,0},{2,3},{3,2},{4,5},{5,4},{6,7},{7,6},{8,9},{9,8},{10,11... | collective-permute-start | bytes 393224 | tf_op jit(solution)/shard_map/ppermute | solution.py:18
  13.7 1.0 %collective-permute-done.3.refs_2_ = f32[128,128]{1,0:T(8,128)S(1)} collective-permute-done((f32[128,128]{1,0:T(8,128)S(1)}, f32[128,128]{1,0:T(8,128)S(1)}, u32[]{:S(2)}, u32[]{:S(2)}) %collective-permute-start.3) | collective-permute-done | bytes 65568 | tf_op jit(solution)/shard_map/ppermute | solution.py:18
  14.7 1.2 %collective-permute-done.4.refs_3_ = f32[128,128]{1,0:T(8,128)S(1)} collective-permute-done((f32[128,128]{1,0:T(8,128)S(1)}, f32[128,128]{1,0:T(8,128)S(1)}, u32[]{:S(2)}, u32[]{:S(2)}) %collective-permute-start.4) | collective-permute-done | bytes 65568 | tf_op jit(solution)/shard_map/ppermute | solution.py:18
  15.9 0.5 %collective-permute-done.9.refs_3_ = f32[128,128]{1,0:T(8,128)S(1)} collective-permute-done((f32[128,128]{1,0:T(8,128)S(1)}, f32[128,128]{1,0:T(8,128)S(1)}, u32[]{:S(2)}, u32[]{:S(2)}) %collective-permute-start.9) | collective-permute-done | bytes 65568 | tf_op jit(solution)/shard_map/ppermute | solution.py:18
  16.4 0.7 %collective-permute-done.6.refs_5_ = f32[128,128]{1,0:T(8,128)S(1)} collective-permute-done((f32[128,128]{1,0:T(8,128)S(1)}, f32[128,128]{1,0:T(8,128)S(1)}, u32[]{:S(2)}, u32[]{:S(2)}) %collective-permute-start.6) | collective-permute-done | bytes 65568 | tf_op jit(solution)/shard_map/ppermute | solution.py:18
  17.1 0.4 %shard_map.64.both = f32[256,128]{1,0:T(8,128)S(1)} custom-call(f32[2,128,128]{2,1,0:T(8,128)S(1)} %shard_map.62.refs_0_, f32[2,128,128]{2,1,0:T(8,128)S(1)} %collective-permute-done.2.refs_1_, f32[128,128]{1,0:T(8,128)S(1)} %collective-permute-done.3.refs_2_, f32[128,128]{1,0:T(8,128)S(1)} %collective-permute-done.4.refs_3_, ...), custom_call_target="tpu_custom_call" | custom-call | flops 1000 | bytes 1000 | tf_op jit(solution)/shard_map/pallas_call | solution.py:147
  17.5 1.6 %collective-permute-start.10 = (f32[256,128]{1,0:T(8,128)S(1)}, f32[256,128]{1,0:T(8,128)S(1)}, u32[]{:S(2)}, u32[]{:S(2)}) collective-permute-start(f32[256,128]{1,0:T(8,128)S(1)} %shard_map.64.both), channel_id=1, source_target_pairs={{0,4},{4,0},{8,12},{12,8},{16,20},{20,16},{24,28},{28,24},{1,5},{5... | collective-permute-start | bytes 393224 | tf_op jit(solution)/shard_map/ppermute | solution.py:18
  19.1 0.1 shard_map.65.stay
  19.2 3.9 %collective-permute-done.10.got = f32[256,128]{1,0:T(8,128)S(1)} collective-permute-done((f32[256,128]{1,0:T(8,128)S(1)}, f32[256,128]{1,0:T(8,128)S(1)}, u32[]{:S(2)}, u32[]{:S(2)}) %collective-permute-start.10) | collective-permute-done | bytes 131104 | tf_op jit(solution)/shard_map/ppermute | solution.py:18
  23.1 0.3 shard_map.67
  23.5 0.7 %collective-permute-start.15 = (f32[2,32,128]{2,1,0:T(8,128)S(1)}, f32[2,32,128]{2,1,0:T(8,128)S(1)}, u32[]{:S(2)}, u32[]{:S(2)}) collective-permute-start(f32[2,32,128]{2,1,0:T(8,128)S(1)} %shard_map.68), channel_id=1, source_target_pairs={{0,2},{1,3},{2,0},{3,1},{4,6},{5,7},{6,4},{7,5},{8,10},{9,11},{10,... | collective-permute-start | bytes 98312 | tf_op jit(solution)/shard_map/ppermute | solution.py:18
  24.1 1.2 %collective-permute-start.12 = (f32[64,128]{1,0:T(8,128)S(1)}, f32[64,128]{1,0:T(8,128)S(1)}, u32[]{:S(2)}, u32[]{:S(2)}) collective-permute-start(f32[64,128]{1,0:T(8,128)S(1)} %get-tuple-element.19), channel_id=1, source_target_pairs={{0,8},{4,12},{8,0},{12,4},{16,24},{20,28},{24,16},{28,20},{1,9},{5... | collective-permute-start | bytes 98312 | tf_op jit(solution)/shard_map/ppermute | solution.py:18
  25.3 2.6 %collective-permute-start.13 = (f32[64,128]{1,0:T(8,128)S(1)}, f32[64,128]{1,0:T(8,128)S(1)}, u32[]{:S(2)}, u32[]{:S(2)}) collective-permute-start(f32[64,128]{1,0:T(8,128)S(1)} %get-tuple-element.20), channel_id=1, source_target_pairs={{0,24},{4,28},{8,16},{12,20},{16,8},{20,12},{24,0},{28,4},{1,25},{... | collective-permute-start | bytes 98312 | tf_op jit(solution)/shard_map/ppermute | solution.py:18
  28.0 0.1 collective-permute-done.12.refs_1_
  28.1 2.9 %collective-permute-done.13.refs_2_ = f32[64,128]{1,0:T(8,128)S(1)} collective-permute-done((f32[64,128]{1,0:T(8,128)S(1)}, f32[64,128]{1,0:T(8,128)S(1)}, u32[]{:S(2)}, u32[]{:S(2)}) %collective-permute-start.13) | collective-permute-done | bytes 32800 | tf_op jit(solution)/shard_map/ppermute | solution.py:18
  31.0 2.0 %collective-permute-done.14.refs_3_ = f32[64,128]{1,0:T(8,128)S(1)} collective-permute-done((f32[64,128]{1,0:T(8,128)S(1)}, f32[64,128]{1,0:T(8,128)S(1)}, u32[]{:S(2)}, u32[]{:S(2)}) %collective-permute-start.14) | collective-permute-done | bytes 32800 | tf_op jit(solution)/shard_map/ppermute | solution.py:18
  33.0 0.7 %shard_map.70 = (f32[32,512]{1,0:T(8,128)}, f32[64,128]{1,0:T(8,128)}) custom-call(f32[64,128]{1,0:T(8,128)S(1)} %get-tuple-element.18.refs_0_, f32[64,128]{1,0:T(8,128)S(1)} %collective-permute-done.12.refs_1_, f32[64,128]{1,0:T(8,128)S(1)} %collective-permute-done.13.refs_2_, f32[64,128]{1,0:T(8,128)S(1)} %collective-permute-done.14.refs_3_, ...), custom_call_target="tpu_custom_call" | custom-call | flops 1000 | bytes 1000 | tf_op jit(solution)/shard_map/pallas_call | solution.py:271
  (32 shorter events, 0.5 us)
Async XLA Ops:
  0.6 9.2 %copy-start = (f32[1,1,128,2,1,128]{5,4,3,2,1,0:T(1,128)S(1)}, f32[1,1,128,2,1,128]{5,4,3,2,1,0:T(1,128)}, u32[]{:S(2)}) copy-start(f32[1,1,128,2,1,128]{5,4,3,2,1,0:T(1,128)} %param.4) | copy-start | bytes 393220
  2.5 7.4 %collective-permute-start = (f32[128,128]{1,0:T(8,128)}, f32[128,128]{1,0:T(8,128)S(1)}, u32[]{:S(2)}, u32[]{:S(2)}) collective-permute-start(f32[128,128]{1,0:T(8,128)} %get-tuple-element.15), channel_id=1, source_target_pairs={{0,5},{1,4},{2,7},{3,6},{4,1},{5,0},{6,3},{7,2},{8,13},{9,12},{10,... | collective-permute-start | bytes 196616 | tf_op jit(solution)/shard_map/ppermute | solution.py:328
  4.9 5.0 %copy-start.3 = (s32[1,1,2,1]{2,3,1,0:T(1,128)S(1)}, s32[1,1,2,1]{2,3,1,0:T(1,128)}, u32[]{:S(2)}) copy-start(s32[1,1,2,1]{2,3,1,0:T(1,128)} %param.5) | copy-start | bytes 28
  4.9 6.6 %collective-permute-start.1 = (f32[128,128]{1,0:T(8,128)}, f32[128,128]{1,0:T(8,128)S(1)}, u32[]{:S(2)}, u32[]{:S(2)}) collective-permute-start(f32[128,128]{1,0:T(8,128)} %get-tuple-element.16), channel_id=1, source_target_pairs={{0,5},{1,4},{2,7},{3,6},{4,1},{5,0},{6,3},{7,2},{8,13},{9,12},{10,... | collective-permute-start | bytes 196616 | tf_op jit(solution)/shard_map/ppermute | solution.py:328
  4.9 7.2 %collective-permute-start.7 = (f32[128,128]{1,0:T(8,128)}, f32[128,128]{1,0:T(8,128)S(1)}, u32[]{:S(2)}, u32[]{:S(2)}) collective-permute-start(f32[128,128]{1,0:T(8,128)} %get-tuple-element.17.refs_0_), channel_id=1, source_target_pairs={{0,16},{4,20},{8,24},{12,28},{16,0},{20,4},{24,8},{28,12},{1,17},{... | collective-permute-start | bytes 196616 | tf_op jit(solution)/shard_map/ppermute | solution.py:18
  8.3 4.8 %collective-permute-start.8 = (f32[128,128]{1,0:T(8,128)}, f32[128,128]{1,0:T(8,128)S(1)}, u32[]{:S(2)}, u32[]{:S(2)}) collective-permute-start(f32[128,128]{1,0:T(8,128)} %get-tuple-element.17.refs_0_), channel_id=1, source_target_pairs={{0,8},{4,12},{8,0},{12,4},{16,24},{20,28},{24,16},{28,20},{1,9},{5... | collective-permute-start | bytes 196616 | tf_op jit(solution)/shard_map/ppermute | solution.py:18
  9.9 4.7 %collective-permute-start.3 = (f32[128,128]{1,0:T(8,128)S(1)}, f32[128,128]{1,0:T(8,128)S(1)}, u32[]{:S(2)}, u32[]{:S(2)}) collective-permute-start(f32[128,128]{1,0:T(8,128)S(1)} %shard_map.60.refs_0_), channel_id=1, source_target_pairs={{0,2},{1,3},{2,0},{3,1},{4,6},{5,7},{6,4},{7,5},{8,10},{9,11},{10,... | collective-permute-start | bytes 196616 | tf_op jit(solution)/shard_map/ppermute | solution.py:18
  11.6 4.3 %collective-permute-start.4 = (f32[128,128]{1,0:T(8,128)S(1)}, f32[128,128]{1,0:T(8,128)S(1)}, u32[]{:S(2)}, u32[]{:S(2)}) collective-permute-start(f32[128,128]{1,0:T(8,128)S(1)} %shard_map.61.refs_1_), channel_id=1, source_target_pairs={{0,2},{1,3},{2,0},{3,1},{4,6},{5,7},{6,4},{7,5},{8,10},{9,11},{10,... | collective-permute-start | bytes 196616 | tf_op jit(solution)/shard_map/ppermute | solution.py:18
  12.1 4.3 %collective-permute-start.9 = (f32[128,128]{1,0:T(8,128)S(1)}, f32[128,128]{1,0:T(8,128)S(1)}, u32[]{:S(2)}, u32[]{:S(2)}) collective-permute-start(f32[128,128]{1,0:T(8,128)S(1)} %collective-permute-done.7.refs_1_), channel_id=1, source_target_pairs={{0,8},{4,12},{8,0},{12,4},{16,24},{20,28},{24,16},{28,20},{1,9},{5... | collective-permute-start | bytes 196616 | tf_op jit(solution)/shard_map/ppermute | solution.py:18
  13.0 3.4 %copy-start.4 = (f32[128,128]{1,0:T(8,128)S(1)}, f32[128,128]{1,0:T(8,128)}, u32[]{:S(2)}) copy-start(f32[128,128]{1,0:T(8,128)} %get-tuple-element.17.refs_0_) | copy-start | bytes 196612
  13.0 3.4 %collective-permute-start.2 = (f32[2,128,128]{2,1,0:T(8,128)S(1)}, f32[2,128,128]{2,1,0:T(8,128)S(1)}, u32[]{:S(2)}, u32[]{:S(2)}) collective-permute-start(f32[2,128,128]{2,1,0:T(8,128)S(1)} %shard_map.62.refs_0_), channel_id=1, source_target_pairs={{0,1},{1,0},{2,3},{3,2},{4,5},{5,4},{6,7},{7,6},{8,9},{9,8},{10,11... | collective-permute-start | bytes 393224 | tf_op jit(solution)/shard_map/ppermute | solution.py:18
  13.1 6.1 %collective-permute-start.11 = (f32[2,128,128]{2,1,0:T(8,128)S(1)}, f32[2,128,128]{2,1,0:T(8,128)S(1)}, u32[]{:S(2)}, u32[]{:S(2)}) collective-permute-start(f32[2,128,128]{2,1,0:T(8,128)S(1)} %shard_map.66.swapped), channel_id=1, source_target_pairs={{0,1},{1,0},{2,3},{3,2},{4,5},{5,4},{6,7},{7,6},{8,9},{9,8},{10,11... | collective-permute-start | bytes 393224 | tf_op jit(solution)/shard_map/ppermute | solution.py:18
  14.6 1.8 %collective-permute-start.5 = (f32[128,128]{1,0:T(8,128)S(1)}, f32[128,128]{1,0:T(8,128)S(1)}, u32[]{:S(2)}, u32[]{:S(2)}) collective-permute-start(f32[128,128]{1,0:T(8,128)S(1)} %collective-permute-done.3.refs_2_), channel_id=1, source_target_pairs={{0,1},{1,0},{2,3},{3,2},{4,5},{5,4},{6,7},{7,6},{8,9},{9,8},{10,11... | collective-permute-start | bytes 196616 | tf_op jit(solution)/shard_map/ppermute | solution.py:18
  15.9 1.3 %collective-permute-start.6 = (f32[128,128]{1,0:T(8,128)S(1)}, f32[128,128]{1,0:T(8,128)S(1)}, u32[]{:S(2)}, u32[]{:S(2)}) collective-permute-start(f32[128,128]{1,0:T(8,128)S(1)} %collective-permute-done.4.refs_3_), channel_id=1, source_target_pairs={{0,1},{1,0},{2,3},{3,2},{4,5},{5,4},{6,7},{7,6},{8,9},{9,8},{10,11... | collective-permute-start | bytes 196616 | tf_op jit(solution)/shard_map/ppermute | solution.py:18
  16.4 2.7 %copy-start.1 = (f32[1,1,128,512]{3,2,1,0:T(8,128)S(1)}, f32[1,1,128,512]{3,2,1,0:T(8,128)}, u32[]{:S(2)}) copy-start(f32[1,1,128,512]{3,2,1,0:T(8,128)} %param.6) | copy-start | bytes 786436
  17.5 5.6 %copy-start.2 = (f32[64,128]{1,0:T(8,128)S(1)}, f32[64,128]{1,0:T(8,128)}, u32[]{:S(2)}) copy-start(f32[64,128]{1,0:T(8,128)} %dinv.1) | copy-start | bytes 98308
  17.5 5.6 %collective-permute-start.10 = (f32[256,128]{1,0:T(8,128)S(1)}, f32[256,128]{1,0:T(8,128)S(1)}, u32[]{:S(2)}, u32[]{:S(2)}) collective-permute-start(f32[256,128]{1,0:T(8,128)S(1)} %shard_map.64.both), channel_id=1, source_target_pairs={{0,4},{4,0},{8,12},{12,8},{16,20},{20,16},{24,28},{28,24},{1,5},{5... | collective-permute-start | bytes 393224 | tf_op jit(solution)/shard_map/ppermute | solution.py:18
  23.5 4.4 %collective-permute-start.15 = (f32[2,32,128]{2,1,0:T(8,128)S(1)}, f32[2,32,128]{2,1,0:T(8,128)S(1)}, u32[]{:S(2)}, u32[]{:S(2)}) collective-permute-start(f32[2,32,128]{2,1,0:T(8,128)S(1)} %shard_map.68), channel_id=1, source_target_pairs={{0,2},{1,3},{2,0},{3,1},{4,6},{5,7},{6,4},{7,5},{8,10},{9,11},{10,... | collective-permute-start | bytes 98312 | tf_op jit(solution)/shard_map/ppermute | solution.py:18
  24.1 3.9 %collective-permute-start.12 = (f32[64,128]{1,0:T(8,128)S(1)}, f32[64,128]{1,0:T(8,128)S(1)}, u32[]{:S(2)}, u32[]{:S(2)}) collective-permute-start(f32[64,128]{1,0:T(8,128)S(1)} %get-tuple-element.19), channel_id=1, source_target_pairs={{0,8},{4,12},{8,0},{12,4},{16,24},{20,28},{24,16},{28,20},{1,9},{5... | collective-permute-start | bytes 98312 | tf_op jit(solution)/shard_map/ppermute | solution.py:18
  25.3 5.7 %collective-permute-start.13 = (f32[64,128]{1,0:T(8,128)S(1)}, f32[64,128]{1,0:T(8,128)S(1)}, u32[]{:S(2)}, u32[]{:S(2)}) collective-permute-start(f32[64,128]{1,0:T(8,128)S(1)} %get-tuple-element.20), channel_id=1, source_target_pairs={{0,24},{4,28},{8,16},{12,20},{16,8},{20,12},{24,0},{28,4},{1,25},{... | collective-permute-start | bytes 98312 | tf_op jit(solution)/shard_map/ppermute | solution.py:18
  27.9 5.2 %collective-permute-start.14 = (f32[64,128]{1,0:T(8,128)S(1)}, f32[64,128]{1,0:T(8,128)S(1)}, u32[]{:S(2)}, u32[]{:S(2)}) collective-permute-start(f32[64,128]{1,0:T(8,128)S(1)} %get-tuple-element.21), channel_id=1, source_target_pairs={{0,16},{4,20},{8,24},{12,28},{16,0},{20,4},{24,8},{28,12},{1,17},{... | collective-permute-start | bytes 98312 | tf_op jit(solution)/shard_map/ppermute | solution.py:18
  27.9 5.1 %collective-permute-start.16 = (f32[2,32,128]{2,1,0:T(8,128)S(1)}, f32[2,32,128]{2,1,0:T(8,128)S(1)}, u32[]{:S(2)}, u32[]{:S(2)}) collective-permute-start(f32[2,32,128]{2,1,0:T(8,128)S(1)} %shard_map.69), channel_id=1, source_target_pairs={{0,1},{1,0},{2,3},{3,2},{4,5},{5,4},{6,7},{7,6},{8,9},{9,8},{10,11... | collective-permute-start | bytes 98312 | tf_op jit(solution)/shard_map/ppermute | solution.py:18
